TPU v7x, 32 devices: a whole 2x2x4 slice. The times are simulated.
32 devices in a mesh: groups: 2 (over y), px: 4 (over z), py: 4 (over x, core).
Axes of the slice: x: 2, y: 2, z: 4, core: 2. Of those that a mesh axis runs over, the one named last changes fastest.
Arguments:
- nodes: bfloat16 [12288, 256], P(('groups', 'px', 'py')), parts along dimension 0, may hold values from -6 to 6
- edges: bfloat16 [36864, 256], P(('groups', 'px', 'py')), parts along dimension 0, may hold values from -6 to 6
- edge_grads: bfloat16 [36864, 256], P(('groups', 'px', 'py')), parts along dimension 0, may hold values from -6 to 6
- node_grads: bfloat16 [12288, 256], P(('groups', 'px', 'py')), parts along dimension 0, may hold values from -6 to 6
- send_list: int32 [256, 32], P(('groups', 'px', 'py')), parts along dimension 0, may hold values from 0 to 383
- senders: int32 [288, 128], P(('groups', 'px', 'py')), parts along dimension 0, may hold values from 0 to 639
- receivers: int32 [288, 128], P(('groups', 'px', 'py')), parts along dimension 0, may hold values from 0 to 383
- tile_count: int32 [32], P(('groups', 'px', 'py')), parts along dimension 0, may hold values from 2 to 9, as said below
- w_edge_in: bfloat16 [768, 256], replicated, may hold values from -0.21875 to 0.21875
- w_edge_out: bfloat16 [256, 256], replicated, may hold values from -0.375 to 0.375
- gain_edge: bfloat16 [256], replicated, may hold values from 0.099609375 to 1.8984375
- w_node_in: bfloat16 [512, 256], replicated, may hold values from -0.25 to 0.25
- w_node_out: bfloat16 [256, 256], replicated, may hold values from -0.375 to 0.375
- gain_node: bfloat16 [256], replicated, may hold values from 0.099609375 to 1.8984375
Outputs:
- nodes_grad: bfloat16 [12288, 256], P(('groups', 'px', 'py')), parts along dimension 0
- edges_grad: bfloat16 [36864, 256], P(('groups', 'px', 'py')), parts along dimension 0
- w_edge_in_grad: bfloat16 [1536, 256], P('groups'), parts along dimension 0
- w_edge_out_grad: bfloat16 [512, 256], P('groups'), parts along dimension 0
- gain_edge_grad: bfloat16 [512], P('groups'), parts along dimension 0
- w_node_in_grad: bfloat16 [1024, 256], P('groups'), parts along dimension 0
- w_node_out_grad: bfloat16 [512, 256], P('groups'), parts along dimension 0
- gain_node_grad: bfloat16 [512], P('groups'), parts along dimension 0
There are 2 independent parts, one for each index of `groups`. A program takes and returns all parts, laid end to end along the dimension named above; an argument that names none is the same for every part. Nothing has to cross between parts.
Inputs may be any that keep to these rules, and one draw needn't show every extreme that they name: `tile_count`: some patch has all 9 tiles live.
All inputs are finite; a program needn't handle non-finite values.
Results may differ from a plain program's by a relative error of at most 0.0075.
Values may be sent and summed in bfloat16 or wider, within the bound.
No kernel may reach another device: no remote copies, remote signals or barrier semaphores. Data moves between devices by JAX's collectives and lax.ppermute only.
A program may use at most 64 MiB of HBM per device.

v0:
```python
import jax
import jax.numpy as jnp
from jax import lax
from jax.sharding import PartitionSpec as P

EPS = 1e-05


def passed_along(array, axis, by):
    size = lax.axis_size(axis)
    return lax.ppermute(array, axis, [(i, (i + by) % size) for i in range(size)])


def matmul(left, right):
    return jnp.dot(left, right, preferred_element_type=jnp.float32)


def matmul_tn(left, right):
    return lax.dot_general(
        left, right, (((0,), (0,)), ((), ())), preferred_element_type=jnp.float32
    )


def matmul_nt(left, right):
    return lax.dot_general(
        left, right, (((1,), (1,)), ((), ())), preferred_element_type=jnp.float32
    )


def silu_slope(value):
    sigma = jax.nn.sigmoid(value)
    return sigma * (1.0 + value * (1.0 - sigma))


def normalize(value):
    centered = value - jnp.mean(value, axis=-1, keepdims=True)
    scale_inv = lax.rsqrt(jnp.mean(centered * centered, axis=-1, keepdims=True) + EPS)
    return (centered * scale_inv, scale_inv)


def norm_back(normed, scale_inv, gain, upstream):
    scaled = upstream * gain
    inner = (
        scaled
        - jnp.mean(scaled, axis=-1, keepdims=True)
        - normed * jnp.mean(scaled * normed, axis=-1, keepdims=True)
    )
    return (inner * scale_inv, jnp.sum(upstream * normed, axis=0))


def one_hot(ids, count):
    return (ids[:, None] == jnp.arange(count, dtype=jnp.int32)[None, :]).astype(jnp.bfloat16)


def edge_forward(extended, local_nodes, edge_tile, sender_ids, receiver_ids, w_edge_in, w_edge_out):
    inputs = jnp.concatenate(
        [
            edge_tile,
            jnp.take(extended, sender_ids, axis=0),
            jnp.take(local_nodes, receiver_ids, axis=0),
        ],
        axis=1,
    )
    pre_act = matmul(inputs, w_edge_in)
    hidden = jax.nn.silu(pre_act).astype(jnp.bfloat16)
    normed, scale_inv = normalize(matmul(hidden, w_edge_out))
    return (inputs, pre_act, hidden, normed, scale_inv)


def aggregate(
    extended,
    local_nodes,
    edge_tiles,
    sender_tiles,
    receiver_tiles,
    live_tiles,
    w_edge_in,
    w_edge_out,
    gain_edge,
):
    node_count = local_nodes.shape[0]

    def aggregate_visit(total, items):
        edge_tile, sender_ids, receiver_ids, tile_live = items
        kept = edge_forward(
            extended, local_nodes, edge_tile, sender_ids, receiver_ids, w_edge_in, w_edge_out
        )
        message = (tile_live * gain_edge * kept[3]).astype(jnp.bfloat16)
        return (total + matmul_tn(one_hot(receiver_ids, node_count), message), kept)

    start = jnp.zeros((node_count, local_nodes.shape[1]), jnp.float32)
    total, stored = lax.scan(
        aggregate_visit, start, (edge_tiles, sender_tiles, receiver_tiles, live_tiles)
    )
    return (total, stored)


def node_backward(local_nodes, aggregated, node_grads, w_node_in, w_node_out, gain_node):
    width = local_nodes.shape[1]
    node_inputs = jnp.concatenate([local_nodes, aggregated.astype(jnp.bfloat16)], axis=1)
    node_pre = matmul(node_inputs, w_node_in)
    node_hidden = jax.nn.silu(node_pre).astype(jnp.bfloat16)
    normed, scale_inv = normalize(matmul(node_hidden, w_node_out))
    upstream = node_grads.astype(jnp.float32)
    out_pre_grad, gain_grad = norm_back(normed, scale_inv, gain_node, upstream)
    out_pre_grad = out_pre_grad.astype(jnp.bfloat16)
    pre_grad = (matmul_nt(out_pre_grad, w_node_out) * silu_slope(node_pre)).astype(jnp.bfloat16)
    input_grad = matmul_nt(pre_grad, w_node_in)
    node_part = upstream + input_grad[:, :width]
    agg_grad = input_grad[:, width:].astype(jnp.bfloat16)
    return (
        node_part,
        agg_grad,
        matmul_tn(node_inputs, pre_grad),
        matmul_tn(node_hidden, out_pre_grad),
        gain_grad,
    )


def edge_backward(
    stored,
    ext_count,
    node_count,
    grad_tiles,
    sender_tiles,
    receiver_tiles,
    live_tiles,
    agg_grad,
    w_edge_in,
    w_edge_out,
    gain_edge,
):
    width = agg_grad.shape[1]

    def edge_visit(carry, items):
        ext_grad, recv_grad, first_grad, second_grad, gain_grad = carry
        kept, grad_tile, sender_ids, receiver_ids, tile_live = items
        inputs, pre_act, hidden, normed, scale_inv = kept
        message_grad = tile_live * (
            grad_tile.astype(jnp.float32)
            + jnp.take(agg_grad, receiver_ids, axis=0).astype(jnp.float32)
        )
        out_pre_grad, gain_part = norm_back(normed, scale_inv, gain_edge, message_grad)
        out_pre_grad = out_pre_grad.astype(jnp.bfloat16)
        pre_grad = (matmul_nt(out_pre_grad, w_edge_out) * silu_slope(pre_act)).astype(jnp.bfloat16)
        input_grad = matmul_nt(pre_grad, w_edge_in)
        edge_grad = (grad_tile.astype(jnp.float32) + input_grad[:, :width]).astype(jnp.bfloat16)
        sender_grad = input_grad[:, width : 2 * width].astype(jnp.bfloat16)
        receiver_grad = input_grad[:, 2 * width :].astype(jnp.bfloat16)
        carry = (
            ext_grad + matmul_tn(one_hot(sender_ids, ext_count), sender_grad),
            recv_grad + matmul_tn(one_hot(receiver_ids, node_count), receiver_grad),
            first_grad + matmul_tn(inputs, pre_grad),
            second_grad + matmul_tn(hidden, out_pre_grad),
            gain_grad + gain_part,
        )
        return (carry, edge_grad)

    start = (
        jnp.zeros((ext_count, width), jnp.float32),
        jnp.zeros((node_count, width), jnp.float32),
        jnp.zeros((3 * width, width), jnp.float32),
        jnp.zeros((width, width), jnp.float32),
        jnp.zeros((width,), jnp.float32),
    )
    carry, edge_grads_out = lax.scan(
        edge_visit, start, (stored, grad_tiles, sender_tiles, receiver_tiles, live_tiles)
    )
    return (edge_grads_out,) + carry


def along_px(blocks, offset):
    return passed_along(blocks, "px", offset)


def along_py(blocks, offset):
    return passed_along(blocks, "py", offset)


def back_px(blocks, offset):
    return passed_along(blocks, "px", offset)


def back_py(blocks, offset):
    return passed_along(blocks, "py", offset)


def on_device(
    nodes,
    edges,
    edge_grads,
    node_grads,
    send_list,
    senders,
    receivers,
    tile_count,
    w_edge_in,
    w_edge_out,
    gain_edge,
    w_node_in,
    w_node_out,
    gain_node,
):
    node_count = nodes.shape[0]
    width = nodes.shape[1]
    slots = send_list.shape[1]
    tiles = senders.shape[0]
    tile_rows = senders.shape[1]
    outgoing = jnp.take(nodes, send_list, axis=0)
    from_low = along_px(outgoing[5:8], 1)
    from_high = along_px(outgoing[0:3], -1)
    upward = along_py(jnp.stack([from_high[2], outgoing[4], from_low[2]]), 1)
    downward = along_py(jnp.stack([from_high[0], outgoing[3], from_low[0]]), -1)
    halo = jnp.stack(
        [
            downward[0],
            from_high[1],
            upward[0],
            downward[1],
            upward[1],
            downward[2],
            from_low[1],
            upward[2],
        ]
    )
    extended = jnp.concatenate([nodes, halo.reshape(8 * slots, width)], axis=0)
    edge_tiles = edges.reshape(tiles, tile_rows, width)
    grad_tiles = edge_grads.reshape(tiles, tile_rows, width)
    live_tiles = (jnp.arange(tiles, dtype=jnp.int32) < tile_count[0]).astype(jnp.float32)
    aggregated, stored = aggregate(
        extended,
        nodes,
        edge_tiles,
        senders,
        receivers,
        live_tiles,
        w_edge_in,
        w_edge_out,
        gain_edge,
    )
    node_part, agg_grad, node_first, node_second, node_gain = node_backward(
        nodes, aggregated, node_grads, w_node_in, w_node_out, gain_node
    )
    edge_out, ext_grad, recv_grad, edge_first, edge_second, edge_gain = edge_backward(
        stored,
        extended.shape[0],
        node_count,
        grad_tiles,
        senders,
        receivers,
        live_tiles,
        agg_grad,
        w_edge_in,
        w_edge_out,
        gain_edge,
    )
    edge_first, edge_second, edge_gain, node_first, node_second, node_gain = lax.psum(
        (edge_first, edge_second, edge_gain, node_first, node_second, node_gain), ("px", "py")
    )
    local_grad = node_part + ext_grad[:node_count] + recv_grad
    halo_grad = ext_grad[node_count:].reshape(8, slots, width).astype(jnp.bfloat16)
    down_back = back_py(jnp.stack([halo_grad[2], halo_grad[4], halo_grad[7]]), -1)
    up_back = back_py(jnp.stack([halo_grad[0], halo_grad[3], halo_grad[5]]), 1)
    to_high = back_px(jnp.stack([up_back[0], down_back[0], halo_grad[1]]), 1)
    to_low = back_px(jnp.stack([up_back[2], down_back[2], halo_grad[6]]), -1)
    returned = jnp.stack(
        [
            to_high[0],
            to_high[2],
            to_high[1],
            up_back[1],
            down_back[1],
            to_low[0],
            to_low[2],
            to_low[1],
        ]
    )
    list_hot = one_hot(send_list.reshape(8 * slots), node_count)
    nodes_grad = local_grad + matmul_tn(list_hot, returned.reshape(8 * slots, width))
    return (
        nodes_grad.astype(jnp.bfloat16),
        edge_out.reshape(tiles * tile_rows, width),
        edge_first.astype(jnp.bfloat16),
        edge_second.astype(jnp.bfloat16),
        edge_gain.astype(jnp.bfloat16),
        node_first.astype(jnp.bfloat16),
        node_second.astype(jnp.bfloat16),
        node_gain.astype(jnp.bfloat16),
    )


def solution(mesh):
    in_specs = (
        P(("groups", "px", "py"), None),
        P(("groups", "px", "py"), None),
        P(("groups", "px", "py"), None),
        P(("groups", "px", "py"), None),
        P(("groups", "px", "py"), None),
        P(("groups", "px", "py"), None),
        P(("groups", "px", "py"), None),
        P(("groups", "px", "py")),
        P(),
        P(),
        P(),
        P(),
        P(),
        P(),
    )
    out_specs = (
        P(("groups", "px", "py"), None),
        P(("groups", "px", "py"), None),
        P("groups", None),
        P("groups", None),
        P("groups"),
        P("groups", None),
        P("groups", None),
        P("groups"),
    )
    return jax.shard_map(
        on_device, mesh=mesh, in_specs=in_specs, out_specs=out_specs, check_vma=False
    )
```

profile of v0, /device:TPU:0, one launch (start us, length us, event | category | flops | bytes accessed | tf_op | source)
XLA Modules:
  0.0 348.6 jit_solution(9107074265706198253)
XLA Ops:
  2.2 2.0 gather_fusion.3
  4.3 3.1 collective-permute-start.1
  7.4 2.1 collective-permute-start
  9.5 2.1 collective-permute-done.1
  14.5 1.7 collective-permute-start.3
  23.3 105.5 %while.42 = (s32[]{:T(128)}, f32[384,256]{1,0:T(8,128)S(1)}, bf16[9,128,768]{2,1,0:T(8,128)(2,1)}, f32[9,128,256]{2,1,0:T(8,128)}, bf16[9,128,256]{2,1,0:T(8,128...) while((s32[]{:T(128)}, f32[384,256]{1,0:T(8,128)S(1)}, ...), condition=%wide.region_4.6_spmd.clone, body=%wide.region_1.5_spmd.clone.sunk | while | flops 94426240 | bytes 4620831 | solution.py:92
  32.9 1.6 bitcast_dynamic-update-slice_fusion.9
  44.6 1.6 bitcast_dynamic-update-slice_fusion.9
  56.4 1.6 bitcast_dynamic-update-slice_fusion.9
  68.1 1.6 bitcast_dynamic-update-slice_fusion.9
  79.8 1.6 bitcast_dynamic-update-slice_fusion.9
  91.5 1.6 bitcast_dynamic-update-slice_fusion.9
  103.2 1.6 bitcast_dynamic-update-slice_fusion.9
  114.8 1.6 bitcast_dynamic-update-slice_fusion.9
  126.6 1.6 bitcast_dynamic-update-slice_fusion.9
  134.2 125.9 %while.43 = (s32[]{:T(128)}, f32[640,256]{1,0:T(8,128)S(1)}, f32[384,256]{1,0:T(8,128)S(1)}, f32[768,256]{1,0:T(8,128)S(1)}, f32[256,256]{1,0:T(8,128)}, /*index...) while((s32[]{:T(128)}, f32[640,256]{1,0:T(8,128)S(1)}, ...), condition=%wide.region_12.14_spmd.clone, body=%wide.region_8.13_spmd.clone.sunk | while | flops 203721344 | bytes 9789859 | solution.py:166
  136.4 1.8 fusion.125
  138.8 1.7 fusion.126
  140.5 1.2 fusion.127
  143.2 1.5 fusion.129
  145.1 1.3 convolution_add_fusion.14
  150.4 1.8 fusion.125
  152.8 1.7 fusion.126
  154.5 1.2 fusion.127
  157.2 1.5 fusion.129
  159.1 1.3 convolution_add_fusion.14
  164.4 1.8 fusion.125
  166.9 1.7 fusion.126
  171.3 1.5 fusion.129
  173.2 1.3 convolution_add_fusion.14
  178.4 1.8 fusion.125
  180.8 1.7 fusion.126
  182.5 1.2 fusion.127
  185.2 1.5 fusion.129
  187.1 1.3 convolution_add_fusion.14
  192.4 1.8 fusion.125
  194.8 1.7 fusion.126
  196.5 1.2 fusion.127
  199.2 1.5 fusion.129
  201.1 1.3 convolution_add_fusion.14
  206.4 1.8 fusion.125
  208.8 1.7 fusion.126
  210.5 1.2 fusion.127
  213.2 1.5 fusion.129
  215.1 1.3 convolution_add_fusion.14
  220.3 1.8 fusion.125
  222.7 1.7 fusion.126
  227.1 1.5 fusion.129
  229.0 1.3 convolution_add_fusion.14
  234.3 1.8 fusion.125
  236.7 1.7 fusion.126
  238.4 1.2 fusion.127
  241.1 1.5 fusion.129
  243.0 1.3 convolution_add_fusion.14
  248.3 1.8 fusion.125
  250.7 1.7 fusion.126
  252.4 1.2 fusion.127
  255.1 1.5 fusion.129
  257.0 1.3 convolution_add_fusion.14
  260.3 1.8 collective-permute-start.5
  262.5 1.3 collective-permute-done.4
  265.3 5.0 %collective-permute-done.6 = bf16[3,32,256]{2,1,0:T(8,128)(2,1)S(1)} collective-permute-done((bf16[3,32,256]{2,1,0:T(8,128)(2,1)S(1)}, bf16[3,32,256]{2,1,0:T(8,128)(2,1)S(1)}, u32[]{:S(2)}, u32[]{:S(2)}) %collective-permute-start.6) | collective-permute-done | bytes 49184 | tf_op jit(solution)/shard_map/ppermute | solution.py:11
  270.4 1.8 collective-permute-start.7
  272.1 72.0 %all-reduce.2 = (bf16[768,256]{1,0:T(8,128)(2,1)}, bf16[256,256]{1,0:T(8,128)(2,1)}, bf16[256]{0:T(256)(128)(2,1)}, bf16[512,256]{1,0:T(8,128)(2,1)}, bf16[256,256]{1,0:T(8,128)(2,1)}, /*index=5*/bf16[256]{0:T(256)(128)(2,1)}) all-reduce(f32[768,256]{1,0:T(8,128)S(1)} %get-tuple-element.853, ...), channel_id=1, replica_groups=mesh['groups'=2,'px'=4,'py'=4] {'px','py'}, use_global_device_ids=true, to_apply=%region_13.15 | all-reduce | flops 459264 | bytes 2755584 | tf_op jit(solution)/shard_map/psum | solution.py:257
  (670 shorter events, 173.0 us)
Async XLA Ops:
  0.6 128.2 %copy-start = (bf16[512,256]{1,0:T(8,128)(2,1)S(1)}, bf16[512,256]{1,0:T(8,128)(2,1)}, u32[]{:S(2)}) copy-start(bf16[512,256]{1,0:T(8,128)(2,1)} %param.31) | copy-start | bytes 786436
  0.6 16.1 %copy-start.28 = (s32[8,32]{1,0:T(8,128)S(1)}, s32[8,32]{1,0:T(8,128)}, u32[]{:S(2)}) copy-start(s32[8,32]{1,0:T(8,128)} %param.24) | copy-start | bytes 3076
  0.7 16.7 %copy-start.20 = (bf16[384,256]{1,0:T(8,128)(2,1)S(1)}, bf16[384,256]{1,0:T(8,128)(2,1)}, u32[]{:S(2)}) copy-start(bf16[384,256]{1,0:T(8,128)(2,1)} %param.23) | copy-start | bytes 589828
  2.2 16.0 %copy-start.36 = (bf16[256]{0:T(256)(128)(2,1)S(1)}, bf16[256]{0:T(256)(128)(2,1)}, u32[]{:S(2)}) copy-start(bf16[256]{0:T(256)(128)(2,1)} %param.33) | copy-start | bytes 1540
  2.2 20.2 %copy-start.1 = (bf16[384,256]{1,0:T(8,128)(2,1)S(1)}, bf16[384,256]{1,0:T(8,128)(2,1)}, u32[]{:S(2)}) copy-start(bf16[384,256]{1,0:T(8,128)(2,1)} %param.20) | copy-start | bytes 589828
  4.3 19.0 %copy-start.2 = (bf16[768,256]{1,0:T(8,128)(2,1)S(1)}, bf16[768,256]{1,0:T(8,128)(2,1)}, u32[]{:S(2)}) copy-start(bf16[768,256]{1,0:T(8,128)(2,1)} %param.28) | copy-start | bytes 1179652
  4.3 7.3 %collective-permute-start.1 = (bf16[3,32,256]{2,1,0:T(8,128)(2,1)S(1)}, bf16[3,32,256]{2,1,0:T(8,128)(2,1)S(1)}, u32[]{:S(2)}, u32[]{:S(2)}) collective-permute-start(bf16[3,32,256]{2,1,0:T(8,128)(2,1)S(1)} %get-tuple-element.445), channel_id=1, source_target_pairs={{0,4},{4,8},{8,12},{12,0},{1,5},{5,9},{9,13},{13,1},{2,6},{6,10},{... | collective-permute-start | bytes 147464 | tf_op jit(solution)/shard_map/ppermute | solution.py:11
  7.4 4.6 %collective-permute-start = (bf16[3,32,256]{2,1,0:T(8,128)(2,1)S(1)}, bf16[3,32,256]{2,1,0:T(8,128)(2,1)S(1)}, u32[]{:S(2)}, u32[]{:S(2)}) collective-permute-start(bf16[3,32,256]{2,1,0:T(8,128)(2,1)S(1)} %get-tuple-element.444), channel_id=1, source_target_pairs={{0,12},{4,0},{8,4},{12,8},{1,13},{5,1},{9,5},{13,9},{2,14},{6,2},{... | collective-permute-start | bytes 147464 | tf_op jit(solution)/shard_map/ppermute | solution.py:11
  12.0 1.8 collective-permute-start.2
  14.5 4.3 %collective-permute-start.3 = (bf16[3,32,256]{2,1,0:T(8,128)(2,1)S(1)}, bf16[3,32,256]{2,1,0:T(8,128)(2,1)}, u32[]{:S(2)}, u32[]{:S(2)}) collective-permute-start(bf16[3,32,256]{2,1,0:T(8,128)(2,1)S(1)} %pad_maximum_fusion.7), channel_id=1, source_target_pairs={{0,1},{1,2},{2,3},{3,0},{4,5},{5,6},{6,7},{7,4},{8,9},{9,10},{10,1... | collective-permute-start | bytes 147464 | tf_op jit(solution)/shard_map/ppermute | solution.py:11
  25.0 3.5 copy-start.8
  26.7 4.6 %copy-start.37 = (f32[9]{0:T(128)S(1)}, f32[9]{0:T(128)}, u32[]{:S(2)}) copy-start(f32[9]{0:T(128)} %get-tuple-element.754) | copy-start | bytes 112 | tf_op jit(solution)/shard_map/while
  26.7 5.2 %copy-start.31 = (bf16[256]{0:T(256)(128)(2,1)S(1)}, bf16[256]{0:T(256)(128)(2,1)}, u32[]{:S(2)}) copy-start(bf16[256]{0:T(256)(128)(2,1)} %get-tuple-element.755) | copy-start | bytes 1540 | tf_op jit(solution)/shard_map/while
  29.8 2.1 copy-start.29
  36.7 3.5 copy-start.8
  38.4 4.6 %copy-start.37 = (f32[9]{0:T(128)S(1)}, f32[9]{0:T(128)}, u32[]{:S(2)}) copy-start(f32[9]{0:T(128)} %get-tuple-element.754) | copy-start | bytes 112 | tf_op jit(solution)/shard_map/while
  38.4 5.2 %copy-start.31 = (bf16[256]{0:T(256)(128)(2,1)S(1)}, bf16[256]{0:T(256)(128)(2,1)}, u32[]{:S(2)}) copy-start(bf16[256]{0:T(256)(128)(2,1)} %get-tuple-element.755) | copy-start | bytes 1540 | tf_op jit(solution)/shard_map/while
  48.5 3.5 copy-start.8
  50.2 4.6 %copy-start.37 = (f32[9]{0:T(128)S(1)}, f32[9]{0:T(128)}, u32[]{:S(2)}) copy-start(f32[9]{0:T(128)} %get-tuple-element.754) | copy-start | bytes 112 | tf_op jit(solution)/shard_map/while
  50.2 5.2 %copy-start.31 = (bf16[256]{0:T(256)(128)(2,1)S(1)}, bf16[256]{0:T(256)(128)(2,1)}, u32[]{:S(2)}) copy-start(bf16[256]{0:T(256)(128)(2,1)} %get-tuple-element.755) | copy-start | bytes 1540 | tf_op jit(solution)/shard_map/while
  51.1 2.1 copy-start.10
  60.3 3.5 copy-start.8
  62.0 4.6 %copy-start.37 = (f32[9]{0:T(128)S(1)}, f32[9]{0:T(128)}, u32[]{:S(2)}) copy-start(f32[9]{0:T(128)} %get-tuple-element.754) | copy-start | bytes 112 | tf_op jit(solution)/shard_map/while
  62.0 5.2 %copy-start.31 = (bf16[256]{0:T(256)(128)(2,1)S(1)}, bf16[256]{0:T(256)(128)(2,1)}, u32[]{:S(2)}) copy-start(bf16[256]{0:T(256)(128)(2,1)} %get-tuple-element.755) | copy-start | bytes 1540 | tf_op jit(solution)/shard_map/while
  71.9 3.5 copy-start.8
  73.6 4.6 %copy-start.37 = (f32[9]{0:T(128)S(1)}, f32[9]{0:T(128)}, u32[]{:S(2)}) copy-start(f32[9]{0:T(128)} %get-tuple-element.754) | copy-start | bytes 112 | tf_op jit(solution)/shard_map/while
  73.6 5.2 %copy-start.31 = (bf16[256]{0:T(256)(128)(2,1)S(1)}, bf16[256]{0:T(256)(128)(2,1)}, u32[]{:S(2)}) copy-start(bf16[256]{0:T(256)(128)(2,1)} %get-tuple-element.755) | copy-start | bytes 1540 | tf_op jit(solution)/shard_map/while
  83.6 3.5 copy-start.8
  85.3 4.6 %copy-start.37 = (f32[9]{0:T(128)S(1)}, f32[9]{0:T(128)}, u32[]{:S(2)}) copy-start(f32[9]{0:T(128)} %get-tuple-element.754) | copy-start | bytes 112 | tf_op jit(solution)/shard_map/while
  85.4 5.2 %copy-start.31 = (bf16[256]{0:T(256)(128)(2,1)S(1)}, bf16[256]{0:T(256)(128)(2,1)}, u32[]{:S(2)}) copy-start(bf16[256]{0:T(256)(128)(2,1)} %get-tuple-element.755) | copy-start | bytes 1540 | tf_op jit(solution)/shard_map/while
  86.2 2.1 copy-start.10
  95.3 3.5 copy-start.8
  97.0 4.6 %copy-start.37 = (f32[9]{0:T(128)S(1)}, f32[9]{0:T(128)}, u32[]{:S(2)}) copy-start(f32[9]{0:T(128)} %get-tuple-element.754) | copy-start | bytes 112 | tf_op jit(solution)/shard_map/while
  97.0 5.1 %copy-start.31 = (bf16[256]{0:T(256)(128)(2,1)S(1)}, bf16[256]{0:T(256)(128)(2,1)}, u32[]{:S(2)}) copy-start(bf16[256]{0:T(256)(128)(2,1)} %get-tuple-element.755) | copy-start | bytes 1540 | tf_op jit(solution)/shard_map/while
  107.0 3.5 copy-start.8
  108.7 4.6 %copy-start.37 = (f32[9]{0:T(128)S(1)}, f32[9]{0:T(128)}, u32[]{:S(2)}) copy-start(f32[9]{0:T(128)} %get-tuple-element.754) | copy-start | bytes 112 | tf_op jit(solution)/shard_map/while
  108.7 5.2 %copy-start.31 = (bf16[256]{0:T(256)(128)(2,1)S(1)}, bf16[256]{0:T(256)(128)(2,1)}, u32[]{:S(2)}) copy-start(bf16[256]{0:T(256)(128)(2,1)} %get-tuple-element.755) | copy-start | bytes 1540 | tf_op jit(solution)/shard_map/while
  118.7 3.5 copy-start.8
  120.4 4.6 %copy-start.37 = (f32[9]{0:T(128)S(1)}, f32[9]{0:T(128)}, u32[]{:S(2)}) copy-start(f32[9]{0:T(128)} %get-tuple-element.754) | copy-start | bytes 112 | tf_op jit(solution)/shard_map/while
  120.4 5.2 %copy-start.31 = (bf16[256]{0:T(256)(128)(2,1)S(1)}, bf16[256]{0:T(256)(128)(2,1)}, u32[]{:S(2)}) copy-start(bf16[256]{0:T(256)(128)(2,1)} %get-tuple-element.755) | copy-start | bytes 1540 | tf_op jit(solution)/shard_map/while
  121.3 2.1 copy-start.10
  123.5 2.1 copy-start.29
  132.1 2.1 copy-start.27
  132.1 2.1 copy-start.32
  132.1 2.1 copy-start.38
  145.1 3.1 copy-start.39
  159.1 3.1 copy-start.39
  173.1 3.1 copy-start.39
  187.1 3.1 copy-start.39
  201.1 3.1 copy-start.39
  215.0 3.1 copy-start.39
  229.0 3.1 copy-start.39
  243.0 3.1 copy-start.39
  257.0 3.1 copy-start.39
  260.1 4.9 %copy-start.15 = (bf16[384,256]{1,0:T(8,128)(2,1)S(1)}, bf16[384,256]{1,0:T(8,128)(2,1)}, u32[]{:S(2)}) copy-start(bf16[384,256]{1,0:T(8,128)(2,1)} %copy-done.14) | copy-start | bytes 589828
  260.1 4.9 %copy-start.17 = (bf16[384,256]{0,1:T(8,128)(2,1)S(1)}, bf16[384,256]{0,1:T(8,128)(2,1)}, u32[]{:S(2)}) copy-start(bf16[384,256]{0,1:T(8,128)(2,1)} %copy-done.16) | copy-start | bytes 589828
  260.2 3.6 %collective-permute-start.4 = (bf16[3,32,256]{2,1,0:T(8,128)(2,1)S(1)}, bf16[3,32,256]{2,1,0:T(8,128)(2,1)S(1)}, u32[]{:S(2)}, u32[]{:S(2)}) collective-permute-start(bf16[3,32,256]{2,1,0:T(8,128)(2,1)S(1)} %pad_maximum_fusion.8), channel_id=1, source_target_pairs={{0,1},{1,2},{2,3},{3,0},{4,5},{5,6},{6,7},{7,4},{8,9},{9,10},{10,1... | collective-permute-start | bytes 147464 | tf_op jit(solution)/shard_map/ppermute | solution.py:11
  260.3 11.8 %copy-start.5 = (f32[256,256]{1,0:T(8,128)S(1)}, f32[256,256]{1,0:T(8,128)}, u32[]{:S(2)}) copy-start(f32[256,256]{1,0:T(8,128)} %get-tuple-element.854) | copy-start | bytes 786436
  260.3 11.8 %copy-start.33 = (f32[256]{0:T(256)S(1)}, f32[256]{0:T(256)}, u32[]{:S(2)}) copy-start(f32[256]{0:T(256)} %get-tuple-element.340) | copy-start | bytes 3076
  260.3 3.5 %collective-permute-start.5 = (bf16[3,32,256]{2,1,0:T(8,128)(2,1)S(1)}, bf16[3,32,256]{2,1,0:T(8,128)(2,1)S(1)}, u32[]{:S(2)}, u32[]{:S(2)}) collective-permute-start(bf16[3,32,256]{2,1,0:T(8,128)(2,1)S(1)} %pad_maximum_fusion.9), channel_id=1, source_target_pairs={{0,3},{1,0},{2,1},{3,2},{4,7},{5,4},{6,5},{7,6},{8,11},{9,8},{10,9... | collective-permute-start | bytes 147464 | tf_op jit(solution)/shard_map/ppermute | solution.py:11
  263.9 6.4 %collective-permute-start.6 = (bf16[3,32,256]{2,1,0:T(8,128)(2,1)S(1)}, bf16[3,32,256]{2,1,0:T(8,128)(2,1)S(1)}, u32[]{:S(2)}, u32[]{:S(2)}) collective-permute-start(bf16[3,32,256]{2,1,0:T(8,128)(2,1)S(1)} %pad_maximum_fusion.10), channel_id=1, source_target_pairs={{0,4},{4,8},{8,12},{12,0},{1,5},{5,9},{9,13},{13,1},{2,6},{6,10},{... | collective-permute-start | bytes 147464 | tf_op jit(solution)/shard_map/ppermute | solution.py:11
  270.4 74.9 %collective-permute-start.7 = (bf16[3,32,256]{2,1,0:T(8,128)(2,1)S(1)}, bf16[3,32,256]{2,1,0:T(8,128)(2,1)}, u32[]{:S(2)}, u32[]{:S(2)}) collective-permute-start(bf16[3,32,256]{2,1,0:T(8,128)(2,1)S(1)} %pad_maximum_fusion.11), channel_id=1, source_target_pairs={{0,12},{4,0},{8,4},{12,8},{1,13},{5,1},{9,5},{13,9},{2,14},{6,2},{... | collective-permute-start | bytes 147464 | tf_op jit(solution)/shard_map/ppermute | solution.py:11
  344.3 3.1 copy-start.12
  344.4 3.1 copy-start.35
  (81 other events, 126.1 us)
where the time goes:
time: 354 us; the launch traced here: 349 us
  other arithmetic  108 us (31%)
  local copies, waits for them, and re-layouts  76 us (21%)
  blocking collectives  72 us (20%)
  matrix products  66.6 us (19%)
  starting transfers between devices  11.6 us (3%)
  waiting for transfers between devices  10 us (3%)
    psum x1, blocking collectives, on_device(): lax.psum((edge_first, edge_second, edge_gain, node_first, node_second, no...  72 us
    dynamic_update_slice x45, other arithmetic, aggregate(): lax.scan(aggregate_visit, start, (edge_tiles, sender_tiles, receiver_tile...  45.8 us
    dot_general x48, matrix products, matmul_tn(): lax.dot_general(left, right, (((0,), (0,)), ((), ())), preferred_element_...  33.8 us
    dot_general x20, matrix products, matmul(): return jnp.dot(left, right, preferred_element_type=jnp.float32)  18.9 us
    reduce_sum x10, other arithmetic, norm_back(): return (inner * scale_inv, jnp.sum(upstream * normed, axis=0))  16.5 us
    convert_element_type x9, other arithmetic, edge_visit(): out_pre_grad = out_pre_grad.astype(jnp.bfloat16)  15.2 us
    dot_general x20, matrix products, matmul_nt(): lax.dot_general(left, right, (((1,), (1,)), ((), ())), preferred_element_...  13.9 us
    ppermute x8, starting transfers between devices, passed_along(): lax.ppermute(array, axis, [(i, (i + by) % size) for i in range(size)])  11.6 us
  transfers between devices with their start and end apart: 8, of which 6 were waited for; matrix products, arithmetic and copies ran while one was open for 1% of the time, Pallas kernels for 0%

commit v1 on v0

v1 whole, which is shorter than its diff:
```python
import jax
import jax.numpy as jnp
from jax import lax
from jax.experimental import pallas as pl
from jax.experimental.pallas import tpu as pltpu
from jax.sharding import PartitionSpec as P

EPS = 1e-05
BF16 = jnp.bfloat16
F32 = jnp.float32
VMEM_LIMIT = 24 * 1024 * 1024


def passed_along(array, axis, by):
    size = lax.axis_size(axis)
    return lax.ppermute(array, axis, [(i, (i + by) % size) for i in range(size)])


def dot(left, right):
    return jnp.dot(left, right, preferred_element_type=F32)


def dot_tn(left, right):
    return lax.dot_general(left, right, (((0,), (0,)), ((), ())), preferred_element_type=F32)


def dot_nt(left, right):
    return lax.dot_general(left, right, (((1,), (1,)), ((), ())), preferred_element_type=F32)


def sigmoid(value):
    return 1.0 / (1.0 + jnp.exp(-value))


def normalize(value):
    centered = value - jnp.mean(value, axis=-1, keepdims=True)
    scale_inv = lax.rsqrt(jnp.mean(centered * centered, axis=-1, keepdims=True) + EPS)
    return centered * scale_inv, scale_inv


def norm_back(normed, scale_inv, gain, upstream):
    scaled = upstream * gain
    inner = (
        scaled
        - jnp.mean(scaled, axis=-1, keepdims=True)
        - normed * jnp.mean(scaled * normed, axis=-1, keepdims=True)
    )
    return inner * scale_inv


def columns_of(ids):
    rows, lanes = ids.shape
    padded = -(-rows // 8) * 8
    if padded > rows:
        ids = jnp.concatenate([ids, jnp.zeros((padded - rows, lanes), ids.dtype)], axis=0)
    return ids.T


def hot_rows(columns, tiles, base, count):
    parts = []
    for tile in tiles:
        column = columns[:, tile : tile + 1] - base
        lanes = lax.broadcasted_iota(jnp.int32, (columns.shape[0], count), 1)
        parts.append(jnp.where(lanes == column, 1.0, 0.0).astype(BF16))
    return jnp.concatenate(parts, axis=0) if len(parts) > 1 else parts[0]


def hot_columns(ids, tiles, base, count):
    parts = []
    for tile in tiles:
        row = ids[tile : tile + 1, :] - base
        subs = lax.broadcasted_iota(jnp.int32, (count, ids.shape[1]), 0)
        parts.append(jnp.where(subs == row, 1.0, 0.0).astype(BF16))
    return jnp.concatenate(parts, axis=1) if len(parts) > 1 else parts[0]


def list_hot(ids, count):
    directions, slots = ids.shape
    wide = jnp.concatenate([ids, jnp.zeros((directions, 128 - slots), ids.dtype)], axis=1)
    columns = wide.T
    parts = []
    for k in range(directions):
        lanes = lax.broadcasted_iota(jnp.int32, (slots, count), 1)
        parts.append(jnp.where(lanes == columns[:slots, k : k + 1], 1.0, 0.0).astype(BF16))
    return jnp.concatenate(parts, axis=0)


def live_rows(count_ref, first_tile, tiles, tile_rows):
    rows = lax.broadcasted_iota(jnp.int32, (tiles * tile_rows, 1), 0)
    return jnp.where(rows < (count_ref[0] - first_tile) * tile_rows, 1.0, 0.0)


def chunks_of(tiles):
    step = 3 if tiles % 3 == 0 else 1
    return [list(range(first, first + step)) for first in range(0, tiles, step)]


def send_kernel(nodes, send_list, low, mid, high):
    slots = send_list.shape[1]
    rows = dot(list_hot(send_list[...], nodes.shape[0]), nodes[...]).astype(BF16)
    low[...] = rows[: 3 * slots]
    mid[...] = rows[3 * slots : 5 * slots]
    high[...] = rows[5 * slots :]


def local_kernel(nodes, edges, senders, receivers, w_in, pre):
    count, width = nodes.shape
    tile_rows = senders.shape[1]
    x = nodes[...]
    table = jnp.concatenate(
        [
            dot(x, w_in[width : 2 * width]).astype(BF16),
            dot(x, w_in[2 * width :]).astype(BF16),
        ],
        axis=0,
    )
    by_sender = columns_of(senders[...])
    by_receiver = columns_of(receivers[...])
    w_edge = w_in[:width]
    for tiles in chunks_of(senders.shape[0]):
        rows = pl.ds(tiles[0] * tile_rows, len(tiles) * tile_rows)
        hot = jnp.concatenate(
            [hot_rows(by_sender, tiles, 0, count), hot_rows(by_receiver, tiles, 0, count)], axis=1
        )
        pre[rows, :] = dot(edges[rows, :], w_edge) + dot(hot, table)


def forward_kernel(
    count_ref,
    nodes,
    node_grads,
    senders,
    receivers,
    pre_local,
    from_high,
    from_low,
    upward,
    downward,
    w_in,
    w_out,
    gain_edge,
    w_node_in,
    w_node_out,
    gain_node,
    halo_out,
    pre_out,
    normed_out,
    scale_out,
    agg_grad_out,
    node_part_out,
    node_sums,
):
    count, width = nodes.shape
    tile_rows = senders.shape[1]
    slots = from_high.shape[0] // 3
    halo = jnp.concatenate(
        [
            downward[:slots],
            from_high[slots : 2 * slots],
            upward[:slots],
            downward[slots : 2 * slots],
            upward[slots : 2 * slots],
            downward[2 * slots :],
            from_low[slots : 2 * slots],
            upward[2 * slots :],
        ],
        axis=0,
    )
    halo_out[...] = halo
    table = dot(halo, w_in[width : 2 * width]).astype(BF16)
    by_sender = columns_of(senders[...])
    receiver_ids = receivers[...]
    gain = gain_edge[...].astype(F32)
    total = jnp.zeros((count, width), F32)
    for tiles in chunks_of(senders.shape[0]):
        rows = pl.ds(tiles[0] * tile_rows, len(tiles) * tile_rows)
        value = pre_local[rows, :] + dot(hot_rows(by_sender, tiles, count, halo.shape[0]), table)
        pre_out[rows, :] = value
        hidden = (value * sigmoid(value)).astype(BF16)
        normed, scale_inv = normalize(dot(hidden, w_out[...]))
        normed_out[rows, :] = normed
        scale_out[rows, :] = jnp.broadcast_to(scale_inv, (len(tiles) * tile_rows, 128))
        live = live_rows(count_ref, tiles[0], len(tiles), tile_rows)
        message = (live * gain * normed).astype(BF16)
        total = total + dot(hot_columns(receiver_ids, tiles, 0, count), message)
    aggregated = total.astype(BF16)
    x = nodes[...]
    w_first = w_node_in[:width]
    w_second = w_node_in[width:]
    node_pre = dot(x, w_first) + dot(aggregated, w_second)
    sigma = sigmoid(node_pre)
    node_hidden = (node_pre * sigma).astype(BF16)
    normed, scale_inv = normalize(dot(node_hidden, w_node_out[...]))
    upstream = node_grads[...].astype(F32)
    out_grad = norm_back(normed, scale_inv, gain_node[...].astype(F32), upstream).astype(BF16)
    slope = sigma * (1.0 + node_pre * (1.0 - sigma))
    pre_grad = (dot_nt(out_grad, w_node_out[...]) * slope).astype(BF16)
    agg_grad_out[...] = dot_nt(pre_grad, w_second).astype(BF16)
    node_part_out[...] = upstream + dot_nt(pre_grad, w_first)
    node_sums[:width] = dot_tn(x, pre_grad)
    node_sums[width : 2 * width] = dot_tn(aggregated, pre_grad)
    node_sums[2 * width : 3 * width] = dot_tn(node_hidden, out_grad)
    node_sums[3 * width :] = jnp.broadcast_to(
        jnp.sum(upstream * normed, axis=0, keepdims=True), (8, width)
    )


def backward_kernel(
    count_ref,
    nodes,
    halo,
    edges,
    edge_grads,
    senders,
    receivers,
    pre,
    normed,
    scale,
    agg_grad,
    w_in,
    w_out,
    gain_edge,
    pre_grad_out,
    sender_out,
    receiver_out,
    up_out,
    down_out,
    rest_out,
    edge_sums,
):
    count, width = nodes.shape
    tile_rows = senders.shape[1]
    slots = up_out.shape[0] // 3
    by_receiver = columns_of(receivers[...])
    sender_ids = senders[...]
    receiver_ids = receivers[...]
    gain = gain_edge[...].astype(F32)
    extended = count + halo.shape[0]
    sender_total = jnp.zeros((extended, width), F32)
    receiver_total = jnp.zeros((count, width), F32)
    first = jnp.zeros((width, width), F32)
    second = jnp.zeros((width, width), F32)
    gain_total = jnp.zeros((1, width), F32)
    for tiles in chunks_of(senders.shape[0]):
        rows = pl.ds(tiles[0] * tile_rows, len(tiles) * tile_rows)
        live = live_rows(count_ref, tiles[0], len(tiles), tile_rows)
        upstream = live * (
            edge_grads[rows, :].astype(F32)
            + dot(hot_rows(by_receiver, tiles, 0, count), agg_grad[...])
        )
        chunk_normed = normed[rows, :]
        gain_total = gain_total + jnp.sum(upstream * chunk_normed, axis=0, keepdims=True)
        out_grad = norm_back(chunk_normed, scale[rows, :1], gain, upstream).astype(BF16)
        value = pre[rows, :]
        sigma = sigmoid(value)
        hidden = (value * sigma).astype(BF16)
        slope = sigma * (1.0 + value * (1.0 - sigma))
        pre_grad = (dot_nt(out_grad, w_out[...]) * slope).astype(BF16)
        pre_grad_out[rows, :] = pre_grad
        second = second + dot_tn(hidden, out_grad)
        first = first + dot_tn(edges[rows, :], pre_grad)
        sender_total = sender_total + dot(hot_columns(sender_ids, tiles, 0, extended), pre_grad)
        receiver_total = receiver_total + dot(
            hot_columns(receiver_ids, tiles, 0, count), pre_grad
        )
    own = sender_total[:count].astype(BF16)
    away = sender_total[count:].astype(BF16)
    received = receiver_total.astype(BF16)
    sender_out[...] = own
    receiver_out[...] = received
    halo_grad = dot_nt(away, w_in[width : 2 * width]).astype(BF16)
    parts = [halo_grad[k * slots : (k + 1) * slots] for k in range(8)]
    up_out[...] = jnp.concatenate([parts[0], parts[3], parts[5]], axis=0)
    down_out[...] = jnp.concatenate([parts[2], parts[4], parts[7]], axis=0)
    rest_out[...] = jnp.concatenate([parts[1], parts[6]], axis=0)
    x = nodes[...]
    edge_sums[:width] = first
    edge_sums[width : 2 * width] = dot_tn(x, own) + dot_tn(halo[...], away)
    edge_sums[2 * width : 3 * width] = dot_tn(x, received)
    edge_sums[3 * width : 4 * width] = second
    edge_sums[4 * width :] = jnp.broadcast_to(gain_total, (8, width))


def finish_kernel(
    edge_grads, pre_grad, sender_sum, receiver_sum, node_part, w_in, edges_grad, local_grad
):
    width = w_in.shape[1]
    edges_grad[...] = (
        edge_grads[...].astype(F32) + dot_nt(pre_grad[...], w_in[:width])
    ).astype(BF16)
    local_grad[...] = (
        node_part[...]
        + dot_nt(sender_sum[...], w_in[width : 2 * width])
        + dot_nt(receiver_sum[...], w_in[2 * width :])
    )


def return_kernel(send_list, local_grad, up_back, down_back, to_high, to_low, nodes_grad):
    slots = send_list.shape[1]

    def block(ref, k):
        return ref[k * slots : (k + 1) * slots]

    returned = jnp.concatenate(
        [
            block(to_high, 0),
            block(to_high, 2),
            block(to_high, 1),
            block(up_back, 1),
            block(down_back, 1),
            block(to_low, 0),
            block(to_low, 2),
            block(to_low, 1),
        ],
        axis=0,
    )
    hot = list_hot(send_list[...], local_grad.shape[0])
    nodes_grad[...] = (local_grad[...] + dot_tn(hot, returned)).astype(BF16)


def call(body, outs, flops, *operands, scalars=0):
    moved = sum(x.size * x.dtype.itemsize for x in operands)
    moved += sum(x.size * jnp.dtype(x.dtype).itemsize for x in outs)
    smem = pl.BlockSpec(memory_space=pltpu.SMEM)
    vmem = pl.BlockSpec(memory_space=pltpu.VMEM)
    return pl.pallas_call(
        body,
        out_shape=outs,
        in_specs=[smem] * scalars + [vmem] * (len(operands) - scalars),
        out_specs=[vmem] * len(outs),
        compiler_params=pltpu.CompilerParams(vmem_limit_bytes=VMEM_LIMIT),
        cost_estimate=pl.CostEstimate(flops=flops, bytes_accessed=moved, transcendentals=0),
    )(*operands)


def shaped(rows, columns, dtype):
    return jax.ShapeDtypeStruct((rows, columns), dtype)


def on_device(
    nodes,
    edges,
    edge_grads,
    node_grads,
    send_list,
    senders,
    receivers,
    tile_count,
    w_edge_in,
    w_edge_out,
    gain_edge,
    w_node_in,
    w_node_out,
    gain_node,
):
    count, width = nodes.shape
    slots = send_list.shape[1]
    halo_rows = 8 * slots
    edge_rows = edges.shape[0]
    square = 2 * width * width
    gain_edge = gain_edge.reshape(1, width)
    gain_node = gain_node.reshape(1, width)

    low, mid, high = call(
        send_kernel,
        [
            shaped(3 * slots, width, BF16),
            shaped(2 * slots, width, BF16),
            shaped(3 * slots, width, BF16),
        ],
        2 * halo_rows * count * width,
        nodes,
        send_list,
    )
    from_low = passed_along(high, "px", 1)
    from_high = passed_along(low, "px", -1)
    upward = passed_along(
        jnp.concatenate([from_high[2 * slots :], mid[slots:], from_low[2 * slots :]]), "py", 1
    )
    downward = passed_along(
        jnp.concatenate([from_high[:slots], mid[:slots], from_low[:slots]]), "py", -1
    )
    (pre_local,) = call(
        local_kernel,
        [shaped(edge_rows, width, F32)],
        square * (2 * count + edge_rows) + 4 * edge_rows * count * width,
        nodes,
        edges,
        senders,
        receivers,
        w_edge_in,
    )
    halo, pre, normed, scale, agg_grad, node_part, node_sums = call(
        forward_kernel,
        [
            shaped(halo_rows, width, BF16),
            shaped(edge_rows, width, F32),
            shaped(edge_rows, width, F32),
            shaped(edge_rows, 128, F32),
            shaped(count, width, BF16),
            shaped(count, width, F32),
            shaped(3 * width + 8, width, F32),
        ],
        square * (2 * edge_rows + 9 * count) + 2 * edge_rows * count * width,
        tile_count,
        nodes,
        node_grads,
        senders,
        receivers,
        pre_local,
        from_high,
        from_low,
        upward,
        downward,
        w_edge_in,
        w_edge_out,
        gain_edge,
        w_node_in,
        w_node_out,
        gain_node,
        scalars=1,
    )
    node_sums = lax.psum(node_sums, ("px", "py"))
    pre_grad, sender_sum, receiver_sum, up, down, rest, edge_sums = call(
        backward_kernel,
        [
            shaped(edge_rows, width, BF16),
            shaped(count, width, BF16),
            shaped(count, width, BF16),
            shaped(3 * slots, width, BF16),
            shaped(3 * slots, width, BF16),
            shaped(2 * slots, width, BF16),
            shaped(4 * width + 8, width, F32),
        ],
        square * (4 * edge_rows + 2 * count + 2 * halo_rows)
        + 2 * edge_rows * (3 * count + halo_rows) * width,
        tile_count,
        nodes,
        halo,
        edges,
        edge_grads,
        senders,
        receivers,
        pre,
        normed,
        scale,
        agg_grad,
        w_edge_in,
        w_edge_out,
        gain_edge,
        scalars=1,
    )
    edge_sums = lax.psum(edge_sums, ("px", "py"))
    up_back = passed_along(up, "py", 1)
    down_back = passed_along(down, "py", -1)
    to_high = passed_along(
        jnp.concatenate([up_back[:slots], down_back[:slots], rest[:slots]]), "px", 1
    )
    to_low = passed_along(
        jnp.concatenate([up_back[2 * slots :], down_back[2 * slots :], rest[slots:]]), "px", -1
    )
    edges_grad, local_grad = call(
        finish_kernel,
        [shaped(edge_rows, width, BF16), shaped(count, width, F32)],
        square * (edge_rows + 2 * count),
        edge_grads,
        pre_grad,
        sender_sum,
        receiver_sum,
        node_part,
        w_edge_in,
    )
    (nodes_grad,) = call(
        return_kernel,
        [shaped(count, width, BF16)],
        2 * halo_rows * count * width,
        send_list,
        local_grad,
        up_back,
        down_back,
        to_high,
        to_low,
    )
    return (
        nodes_grad,
        edges_grad,
        edge_sums[: 3 * width].astype(BF16),
        edge_sums[3 * width : 4 * width].astype(BF16),
        edge_sums[4 * width].astype(BF16),
        node_sums[: 2 * width].astype(BF16),
        node_sums[2 * width : 3 * width].astype(BF16),
        node_sums[3 * width].astype(BF16),
    )


def solution(mesh):
    in_specs = (
        P(("groups", "px", "py"), None),
        P(("groups", "px", "py"), None),
        P(("groups", "px", "py"), None),
        P(("groups", "px", "py"), None),
        P(("groups", "px", "py"), None),
        P(("groups", "px", "py"), None),
        P(("groups", "px", "py"), None),
        P(("groups", "px", "py")),
        P(),
        P(),
        P(),
        P(),
        P(),
        P(),
    )
    out_specs = (
        P(("groups", "px", "py"), None),
        P(("groups", "px", "py"), None),
        P("groups", None),
        P("groups", None),
        P("groups"),
        P("groups", None),
        P("groups", None),
        P("groups"),
    )
    return jax.shard_map(
        on_device, mesh=mesh, in_specs=in_specs, out_specs=out_specs, check_vma=False
    )
```

time: 354 us -> 117 us (0.33); the launches traced: 349 us -> 116 us
  other arithmetic: 108 us -> 0.02 us
  matrix products: 66.6 us -> 0 us
  local copies, waits for them, and re-layouts: 76 us -> 14.5 us
  Pallas kernels: 0 us -> 10.7 us
  waiting for transfers between devices: 10 us -> 5.64 us
    dot_general x88 -> x0, matrix products: 66.6 us -> none  [the longest x48 33.8 us: matmul_tn(): lax.dot_general(left, right, (((0,), (0,)), ((), ())), preferred_element_...]
    dynamic_update_slice x45 -> x0, other arithmetic: 45.8 us -> none  [aggregate(): lax.scan(aggregate_visit, start, (edge_tiles, sender_tiles, receiver_tile...]
    gather x28 -> x0, local copies, waits for them, and re-layouts: 24.8 us -> none  [the longest x9 7.63 us: edge_forward(): jnp.take(local_nodes, receiver_ids, axis=0)]
    reduce_sum x20 -> x0, other arithmetic: 18.1 us -> none  [the longest x10 16.5 us: norm_back(): return (inner * scale_inv, jnp.sum(upstream * normed, axis=0))]
    convert_element_type x22 -> x0, other arithmetic: 16.5 us -> none  [the longest x9 15.2 us: edge_visit(): out_pre_grad = out_pre_grad.astype(jnp.bfloat16)]
    and x19 -> x0, other arithmetic: 13.4 us -> none  [the longest x9 6.42 us: edge_forward(): jnp.take(local_nodes, receiver_ids, axis=0)]
    pallas_call x0 -> x6, Pallas kernels: none -> 10.7 us  [call(): pl.pallas_call(body, out_shape=outs, in_specs=[smem] * scalars + [vmem] *...]
    dynamic_slice x18 -> x0, local copies, waits for them, and re-layouts: 10.5 us -> none  [aggregate(): lax.scan(aggregate_visit, start, (edge_tiles, sender_tiles, receiver_tile...]
  transfers between devices with their start and end apart: 8 -> 8, of which waited for: 6 -> 2; matrix products, arithmetic and copies ran while one was open for 1% -> 6% of each run, Pallas kernels for 0% -> 2%
where the time goes in v1:
time: 117 us; the launch traced here: 116 us
  blocking collectives  73 us (62%)
  local copies, waits for them, and re-layouts  14.5 us (12%)
  starting transfers between devices  10.8 us (9%)
  Pallas kernels  10.7 us (9%)
  waiting for transfers between devices  5.64 us (5%)
  between operations  1.53 us (1%)
    psum x1, blocking collectives, on_device(): edge_sums = lax.psum(edge_sums, ('px', 'py'))  73 us
    ppermute x8, starting transfers between devices, passed_along(): lax.ppermute(array, axis, [(i, (i + by) % size) for i in range(size)])  10.8 us
    pallas_call x6, Pallas kernels, call(): pl.pallas_call(body, out_shape=outs, in_specs=[smem] * scalars + [vmem] *...  10.7 us
    unnamed x46, local copies, waits for them, and re-layouts  7.21 us
    ppermute x8, waiting for transfers between devices, passed_along(): lax.ppermute(array, axis, [(i, (i + by) % size) for i in range(size)])  5.64 us
  transfers between devices with their start and end apart: 8, of which 2 were waited for; matrix products, arithmetic and copies ran while one was open for 6% of the time, Pallas kernels for 2%

profile of v1, /device:TPU:0, one launch (start us, length us, event | category | flops | bytes accessed | tf_op | source)
XLA Modules:
  0.0 116.2 jit_solution(11106686674411672283)
XLA Ops:
  0.6 0.0 copy-start.9
  0.6 0.9 copy-done.9
  1.6 0.0 copy-start.10
  1.6 0.7 copy-done.10
  2.2 0.3 shard_map.198
  2.6 5.1 %collective-permute-start = (bf16[96,256]{1,0:T(8,128)(2,1)S(1)}, bf16[96,256]{1,0:T(8,128)(2,1)S(1)}, u32[]{:S(2)}, u32[]{:S(2)}) collective-permute-start(bf16[96,256]{1,0:T(8,128)(2,1)S(1)} %get-tuple-element.27), channel_id=1, source_target_pairs={{0,12},{4,0},{8,4},{12,8},{1,13},{5,1},{9,5},{13,9},{2,14},{6,2},{... | collective-permute-start | bytes 147464 | tf_op jit(solution)/shard_map/ppermute | solution.py:16
  7.7 0.0 collective-permute-start.1
  8.4 0.7 reshape.24.gain_edge
  9.0 0.7 reshape.25.gain_node
  9.7 0.0 collective-permute-done.from_high
  9.7 3.9 %collective-permute-done.1.from_low = bf16[96,256]{1,0:T(8,128)(2,1)S(1)} collective-permute-done((bf16[96,256]{1,0:T(8,128)(2,1)S(1)}, bf16[96,256]{1,0:T(8,128)(2,1)S(1)}, u32[]{:S(2)}, u32[]{:S(2)}) %collective-permute-start.1) | collective-permute-done | bytes 49184 | tf_op jit(solution)/shard_map/ppermute | solution.py:16
  13.6 0.1 collective-permute-start.2
  13.7 1.7 %collective-permute-start.3 = (bf16[96,256]{1,0:T(8,128)(2,1)S(1)}, bf16[96,256]{1,0:T(8,128)(2,1)S(1)}, u32[]{:S(2)}, u32[]{:S(2)}) collective-permute-start(bf16[96,256]{1,0:T(8,128)(2,1)S(1)} %pad_maximum_fusion.1), channel_id=1, source_target_pairs={{0,3},{1,0},{2,1},{3,2},{4,7},{5,4},{6,5},{7,6},{8,11},{9,8},{10,9... | collective-permute-start | bytes 147464 | tf_op jit(solution)/shard_map/ppermute | solution.py:16
  15.4 1.0 copy-done.1
  16.4 0.0 copy-start.12
  16.4 1.1 copy-done.12
  17.5 0.0 copy-start.18
  17.5 0.7 copy-done.18
  18.2 0.0 copy-start.20
  18.2 0.7 copy-done.20
  18.9 0.0 copy-start.17
  18.9 0.0 copy-start.19
  18.9 0.0 copy-start.21
  18.9 1.2 shard_map.197.pre_local
  20.1 0.0 copy-start
  20.1 0.0 copy-start.13
  20.1 0.0 collective-permute-done.2.upward
  20.1 0.0 collective-permute-done.3.downward
  20.1 0.0 copy-done.2
  20.1 0.0 copy-done.14
  20.1 0.0 copy-done.15
  20.1 0.0 copy-done.16
  20.1 0.0 copy-done.17
  20.2 0.0 copy-done.19
  20.2 0.0 copy-done.21
  20.2 3.0 %shard_map.199 = (bf16[256,256]{1,0:T(8,128)(2,1)S(1)}, f32[1152,256]{1,0:T(8,128)S(1)}, f32[1152,256]{1,0:T(8,128)S(1)}, f32[1152,128]{1,0:T(8,128)S(1)}, bf16[...) custom-call(s32[1]{0:T(128)S(6)} %copy.26.count_ref, bf16[384,256]{1,0:T(8,128)(2,1)S(1)} %copy-done.9, ...), custom_call_target="tpu_custom_call" | custom-call | flops 981467136 | bytes 7161860 | tf_op jit(solution)/shard_map/pallas_call | solution.py:326
  23.1 0.0 copy-start.3
  23.1 0.7 copy-done.3
  23.9 0.0 copy-done
  23.9 0.0 copy-done.13
  23.9 3.8 %shard_map.200 = (bf16[1152,256]{1,0:T(8,128)(2,1)S(1)}, bf16[384,256]{1,0:T(8,128)(2,1)S(1)}, bf16[384,256]{1,0:T(8,128)(2,1)S(1)}, bf16[96,256]{1,0:T(8,128)(2...) custom-call(s32[1]{0:T(128)S(6)} %copy.26.count_ref, ...), custom_call_target="tpu_custom_call" | custom-call | flops 1602224128 | bytes 7357956 | tf_op jit(solution)/shard_map/pallas_call | solution.py:326
  27.7 0.7 copy-done.5
  28.4 0.7 copy-done.7
  29.1 0.0 collective-permute-start.4
  29.1 73.0 %all-reduce.2 = (bf16[1032,256]{1,0:T(8,128)(2,1)}, bf16[776,256]{1,0:T(8,128)(2,1)}) all-reduce(f32[1032,256]{1,0:T(8,128)S(1)} %get-tuple-element.44, f32[776,256]{1,0:T(8,128)S(1)} %get-tuple-element.45), channel_id=1, replica_groups=mesh['groups'=2,'px'=4,'py'=4] {'px','py'}, use_global_device_ids=true, to_apply=%region_0.0 | all-reduce | flops 462848 | bytes 2777088 | tf_op jit(solution)/shard_map/psum | solution.py:453
  102.1 0.1 collective-permute-start.5
  102.2 0.0 collective-permute-done.4.up_back
  102.2 1.7 %collective-permute-done.5.down_back = bf16[96,256]{1,0:T(8,128)(2,1)S(1)} collective-permute-done((bf16[96,256]{1,0:T(8,128)(2,1)S(1)}, bf16[96,256]{1,0:T(8,128)(2,1)S(1)}, u32[]{:S(2)}, u32[]{:S(2)}) %collective-permute-start.5) | collective-permute-done | bytes 49184 | tf_op jit(solution)/shard_map/ppermute | solution.py:16
  103.9 0.1 collective-permute-start.6
  104.0 3.8 %collective-permute-start.7 = (bf16[96,256]{1,0:T(8,128)(2,1)S(1)}, bf16[96,256]{1,0:T(8,128)(2,1)S(1)}, u32[]{:S(2)}, u32[]{:S(2)}) collective-permute-start(bf16[96,256]{1,0:T(8,128)(2,1)S(1)} %pad_maximum_fusion.3), channel_id=1, source_target_pairs={{0,12},{4,0},{8,4},{12,8},{1,13},{5,1},{9,5},{13,9},{2,14},{6,2},{... | collective-permute-start | bytes 147464 | tf_op jit(solution)/shard_map/ppermute | solution.py:16
  107.8 1.2 %slice_reduce_fusion = (bf16[256]{0:T(256)(128)(2,1)}, bf16[256]{0:T(256)(128)(2,1)}) fusion(bf16[776,256]{1,0:T(8,128)(2,1)} %get-tuple-element.47, bf16[1032,256]{1,0:T(8,128)(2,1)} %get-tuple-element.46), kind=kLoop, calls=%fused_computation.4 | loop fusion | bytes 2048 | tf_op jit(solution)/shard_map/slice | solution.py:492
  109.0 1.6 %slice.87 = bf16[256,256]{1,0:T(8,128)(2,1)} slice(bf16[1032,256]{1,0:T(8,128)(2,1)} %get-tuple-element.46), slice={[768:1024], [0:256]} | slice | bytes 262144 | tf_op jit(solution)/shard_map/slice | solution.py:488
  110.6 1.8 %slice.86 = bf16[768,256]{1,0:T(8,128)(2,1)} slice(bf16[1032,256]{1,0:T(8,128)(2,1)} %get-tuple-element.46), slice={[0:768], [0:256]} | slice | bytes 786432 | tf_op jit(solution)/shard_map/slice | solution.py:487
  112.4 0.0 copy-done.22
  112.4 0.7 slice.90
  113.0 0.7 slice.89
  113.8 0.0 copy-done.4
  113.8 0.0 copy-done.6
  113.8 0.0 copy-done.8
  113.8 1.3 %shard_map.201 = (bf16[1152,256]{1,0:T(8,128)(2,1)}, f32[384,256]{1,0:T(8,128)S(1)}) custom-call(bf16[1152,256]{1,0:T(8,128)(2,1)S(1)} %copy-done, bf16[1152,256]{1,0:T(8,128)(2,1)S(1)} %get-tuple-element.35.pre_grad, bf16[384,256]{1,0:T(8,128)(2,1)S(1)} %copy-done.6, bf16[384,256]{1,0:T(8,128)(2,1)S(1)} %copy-done.8, f32[384,256]{1,0:T(8,128)S(1)} %copy-done.4, ...), custom_call_target="tpu_custom_call" | custom-call | flops 251658240 | bytes 3342336 | tf_op jit(solution)/shard_map/pallas_call | solution.py:326
  115.1 0.0 collective-permute-done.6.to_high
  115.1 0.0 collective-permute-done.7.to_low
  115.1 0.0 copy-done.11
  115.1 1.1 shard_map.202
  (22 shorter events, 0.1 us)
Async XLA Ops:
  0.6 0.9 copy-start.9
  1.6 0.7 copy-start.10
  2.6 7.1 %collective-permute-start = (bf16[96,256]{1,0:T(8,128)(2,1)S(1)}, bf16[96,256]{1,0:T(8,128)(2,1)S(1)}, u32[]{:S(2)}, u32[]{:S(2)}) collective-permute-start(bf16[96,256]{1,0:T(8,128)(2,1)S(1)} %get-tuple-element.27), channel_id=1, source_target_pairs={{0,12},{4,0},{8,4},{12,8},{1,13},{5,1},{9,5},{13,9},{2,14},{6,2},{... | collective-permute-start | bytes 147464 | tf_op jit(solution)/shard_map/ppermute | solution.py:16
  7.7 5.9 %collective-permute-start.1 = (bf16[96,256]{1,0:T(8,128)(2,1)S(1)}, bf16[96,256]{1,0:T(8,128)(2,1)S(1)}, u32[]{:S(2)}, u32[]{:S(2)}) collective-permute-start(bf16[96,256]{1,0:T(8,128)(2,1)S(1)} %get-tuple-element.28), channel_id=1, source_target_pairs={{0,4},{4,8},{8,12},{12,0},{1,5},{5,9},{9,13},{13,1},{2,6},{6,10},{... | collective-permute-start | bytes 147464 | tf_op jit(solution)/shard_map/ppermute | solution.py:16
  13.6 6.5 %collective-permute-start.2 = (bf16[96,256]{1,0:T(8,128)(2,1)S(1)}, bf16[96,256]{1,0:T(8,128)(2,1)S(1)}, u32[]{:S(2)}, u32[]{:S(2)}) collective-permute-start(bf16[96,256]{1,0:T(8,128)(2,1)S(1)} %pad_maximum_fusion), channel_id=1, source_target_pairs={{0,1},{1,2},{2,3},{3,0},{4,5},{5,6},{6,7},{7,4},{8,9},{9,10},{10,1... | collective-permute-start | bytes 147464 | tf_op jit(solution)/shard_map/ppermute | solution.py:16
  13.7 6.4 %collective-permute-start.3 = (bf16[96,256]{1,0:T(8,128)(2,1)S(1)}, bf16[96,256]{1,0:T(8,128)(2,1)S(1)}, u32[]{:S(2)}, u32[]{:S(2)}) collective-permute-start(bf16[96,256]{1,0:T(8,128)(2,1)S(1)} %pad_maximum_fusion.1), channel_id=1, source_target_pairs={{0,3},{1,0},{2,1},{3,2},{4,7},{5,4},{6,5},{7,6},{8,11},{9,8},{10,9... | collective-permute-start | bytes 147464 | tf_op jit(solution)/shard_map/ppermute | solution.py:16
  15.4 1.0 copy-start.1
  16.4 1.1 copy-start.12
  17.5 0.7 copy-start.18
  18.2 0.7 copy-start.20
  18.9 1.3 %copy-start.2 = (bf16[768,256]{1,0:T(8,128)(2,1)S(1)}, bf16[768,256]{1,0:T(8,128)(2,1)}, u32[]{:S(2)}) copy-start(bf16[768,256]{1,0:T(8,128)(2,1)} %w_in.7) | copy-start | bytes 1179652
  18.9 1.3 %copy-start.14 = (bf16[512,256]{1,0:T(8,128)(2,1)S(1)}, bf16[512,256]{1,0:T(8,128)(2,1)}, u32[]{:S(2)}) copy-start(bf16[512,256]{1,0:T(8,128)(2,1)} %w_node_in.1) | copy-start | bytes 786436
  18.9 1.3 %copy-start.15 = (bf16[384,256]{1,0:T(8,128)(2,1)S(1)}, bf16[384,256]{1,0:T(8,128)(2,1)}, u32[]{:S(2)}) copy-start(bf16[384,256]{1,0:T(8,128)(2,1)} %node_grads.1) | copy-start | bytes 589828
  18.9 1.3 %copy-start.16 = (bf16[256,256]{1,0:T(8,128)(2,1)S(1)}, bf16[256,256]{1,0:T(8,128)(2,1)}, u32[]{:S(2)}) copy-start(bf16[256,256]{1,0:T(8,128)(2,1)} %w_node_out.1) | copy-start | bytes 393220
  18.9 1.3 %copy-start.17 = (bf16[256,256]{1,0:T(8,128)(2,1)S(1)}, bf16[256,256]{1,0:T(8,128)(2,1)}, u32[]{:S(2)}) copy-start(bf16[256,256]{1,0:T(8,128)(2,1)} %w_out.3) | copy-start | bytes 393220
  18.9 1.3 %copy-start.19 = (s32[9,128]{1,0:T(8,128)S(1)}, s32[9,128]{1,0:T(8,128)}, u32[]{:S(2)}) copy-start(s32[9,128]{1,0:T(8,128)} %senders.5) | copy-start | bytes 13828
  18.9 1.3 %copy-start.21 = (s32[9,128]{1,0:T(8,128)S(1)}, s32[9,128]{1,0:T(8,128)}, u32[]{:S(2)}) copy-start(s32[9,128]{1,0:T(8,128)} %receivers.5) | copy-start | bytes 13828
  20.1 3.8 %copy-start = (bf16[1152,256]{1,0:T(8,128)(2,1)S(1)}, bf16[1152,256]{1,0:T(8,128)(2,1)}, u32[]{:S(2)}) copy-start(bf16[1152,256]{1,0:T(8,128)(2,1)} %edge_grads.3) | copy-start | bytes 1769476
  20.1 3.8 %copy-start.13 = (bf16[1152,256]{1,0:T(8,128)(2,1)S(1)}, bf16[1152,256]{1,0:T(8,128)(2,1)}, u32[]{:S(2)}) copy-start(bf16[1152,256]{1,0:T(8,128)(2,1)} %edges.3) | copy-start | bytes 1769476
  23.1 0.7 copy-start.3
  27.7 0.7 copy-start.5
  28.4 0.7 copy-start.7
  29.1 73.1 %collective-permute-start.4 = (bf16[96,256]{1,0:T(8,128)(2,1)}, bf16[96,256]{1,0:T(8,128)(2,1)S(1)}, u32[]{:S(2)}, u32[]{:S(2)}) collective-permute-start(bf16[96,256]{1,0:T(8,128)(2,1)} %get-tuple-element.40), channel_id=1, source_target_pairs={{0,1},{1,2},{2,3},{3,0},{4,5},{5,6},{6,7},{7,4},{8,9},{9,10},{10,1... | collective-permute-start | bytes 147464 | tf_op jit(solution)/shard_map/ppermute | solution.py:16
  102.1 10.3 %copy-start.22 = (bf16[776,256]{1,0:T(8,128)(2,1)S(1)}, bf16[776,256]{1,0:T(8,128)(2,1)}, u32[]{:S(2)}) copy-start(bf16[776,256]{1,0:T(8,128)(2,1)} %get-tuple-element.47) | copy-start | bytes 1191940
  102.1 11.7 %copy-start.4 = (f32[384,256]{1,0:T(8,128)S(1)}, f32[384,256]{1,0:T(8,128)}, u32[]{:S(2)}) copy-start(f32[384,256]{1,0:T(8,128)} %copy-done.3) | copy-start | bytes 1179652
  102.1 11.7 %copy-start.6 = (bf16[384,256]{1,0:T(8,128)(2,1)S(1)}, bf16[384,256]{1,0:T(8,128)(2,1)}, u32[]{:S(2)}) copy-start(bf16[384,256]{1,0:T(8,128)(2,1)} %copy-done.5) | copy-start | bytes 589828
  102.1 11.7 %copy-start.8 = (bf16[384,256]{1,0:T(8,128)(2,1)S(1)}, bf16[384,256]{1,0:T(8,128)(2,1)}, u32[]{:S(2)}) copy-start(bf16[384,256]{1,0:T(8,128)(2,1)} %copy-done.7) | copy-start | bytes 589828
  102.1 1.8 %collective-permute-start.5 = (bf16[96,256]{1,0:T(8,128)(2,1)S(1)}, bf16[96,256]{1,0:T(8,128)(2,1)S(1)}, u32[]{:S(2)}, u32[]{:S(2)}) collective-permute-start(bf16[96,256]{1,0:T(8,128)(2,1)S(1)} %get-tuple-element.41), channel_id=1, source_target_pairs={{0,3},{1,0},{2,1},{3,2},{4,7},{5,4},{6,5},{7,6},{8,11},{9,8},{10,9... | collective-permute-start | bytes 147464 | tf_op jit(solution)/shard_map/ppermute | solution.py:16
  103.9 11.2 %collective-permute-start.6 = (bf16[96,256]{1,0:T(8,128)(2,1)S(1)}, bf16[96,256]{1,0:T(8,128)(2,1)S(1)}, u32[]{:S(2)}, u32[]{:S(2)}) collective-permute-start(bf16[96,256]{1,0:T(8,128)(2,1)S(1)} %pad_maximum_fusion.2), channel_id=1, source_target_pairs={{0,4},{4,8},{8,12},{12,0},{1,5},{5,9},{9,13},{13,1},{2,6},{6,10},{... | collective-permute-start | bytes 147464 | tf_op jit(solution)/shard_map/ppermute | solution.py:16
  104.0 11.1 %collective-permute-start.7 = (bf16[96,256]{1,0:T(8,128)(2,1)S(1)}, bf16[96,256]{1,0:T(8,128)(2,1)S(1)}, u32[]{:S(2)}, u32[]{:S(2)}) collective-permute-start(bf16[96,256]{1,0:T(8,128)(2,1)S(1)} %pad_maximum_fusion.3), channel_id=1, source_target_pairs={{0,12},{4,0},{8,4},{12,8},{1,13},{5,1},{9,5},{13,9},{2,14},{6,2},{... | collective-permute-start | bytes 147464 | tf_op jit(solution)/shard_map/ppermute | solution.py:16
  113.8 1.3 %copy-start.11 = (s32[8,32]{1,0:T(8,128)S(1)}, s32[8,32]{1,0:T(8,128)}, u32[]{:S(2)}) copy-start(s32[8,32]{1,0:T(8,128)} %send_list.3) | copy-start | bytes 3076

commit v2 on v1

--- a/solution.py
+++ b/solution.py
@@ -420,7 +420,13 @@
         gain_node,
         scalars=1,
     )
-    node_sums = lax.psum(node_sums, ("px", "py"))
+    devices = lax.axis_size("px") * lax.axis_size("py")
+    node_parts = lax.all_to_all(
+        node_sums[: 3 * width].astype(BF16).reshape(devices, -1, width), ("px", "py"), 0, 0
+    )
+    node_rows = lax.all_gather(
+        jnp.sum(node_parts.astype(F32), axis=0).astype(BF16), ("px", "py"), axis=0, tiled=True
+    )
     pre_grad, sender_sum, receiver_sum, up, down, rest, edge_sums = call(
         backward_kernel,
         [
@@ -450,7 +456,12 @@
         gain_edge,
         scalars=1,
     )
-    edge_sums = lax.psum(edge_sums, ("px", "py"))
+    edge_part = lax.psum_scatter(
+        edge_sums[: 4 * width], ("px", "py"), scatter_dimension=0, tiled=True
+    )
+    edge_rows_all = lax.all_gather(edge_part.astype(BF16), ("px", "py"), axis=0, tiled=True)
+    gains = jnp.concatenate([edge_sums[4 * width :][:1], node_sums[3 * width :][:1]])
+    gains = lax.psum(gains, ("px", "py")).astype(BF16)
     up_back = passed_along(up, "py", 1)
     down_back = passed_along(down, "py", -1)
     to_high = passed_along(
@@ -484,12 +495,12 @@
     return (
         nodes_grad,
         edges_grad,
-        edge_sums[: 3 * width].astype(BF16),
-        edge_sums[3 * width : 4 * width].astype(BF16),
-        edge_sums[4 * width].astype(BF16),
-        node_sums[: 2 * width].astype(BF16),
-        node_sums[2 * width : 3 * width].astype(BF16),
-        node_sums[3 * width].astype(BF16),
+        edge_rows_all[: 3 * width],
+        edge_rows_all[3 * width :],
+        gains[0],
+        node_rows[: 2 * width],
+        node_rows[2 * width :],
+        gains[1],
     )
 
 

time: 117 us -> 134 us (1.15)
  between operations: 1.53 us -> 14.9 us
  starting transfers between devices: 10.8 us -> 16.1 us
  waiting for transfers between devices: 5.64 us -> 4.17 us
    psum x1, blocking collectives: 73 us -> 32.8 us  [on_device(): gains = lax.psum(gains, ('px', 'py')).astype(BF16)]
    all_gather x0 -> x2, blocking collectives: none -> 39.4 us  [the longest x1 20.4 us: on_device(): lax.all_gather(edge_part.astype(BF16), ('px', 'py'), axis=0, tiled=True)]
    all_to_all x0 -> x1, starting transfers between devices: none -> 3.55 us  [on_device(): lax.all_to_all(node_sums[:3 * width].astype(BF16).reshape(devices, -1, wi...]
    ppermute x8, starting transfers between devices: 10.8 us -> 12.5 us  [passed_along(): lax.ppermute(array, axis, [(i, (i + by) % size) for i in range(size)])]
    ppermute x8, waiting for transfers between devices: 5.64 us -> 4.15 us  [passed_along(): lax.ppermute(array, axis, [(i, (i + by) % size) for i in range(size)])]
    unnamed x46 -> x32, local copies, waits for them, and re-layouts: 7.21 us -> 5.99 us
    slice x5 -> x9, local copies, waits for them, and re-layouts: 5.94 us -> 7.04 us  [the longest x1 1.92 us: on_device(): node_sums[:3 * width].astype(BF16).reshape(devices, -1, width)]
  transfers between devices with their start and end apart: 8 -> 10, of which waited for: 2 -> 2; matrix products, arithmetic and copies ran while one was open for 6% -> 4% of each run, Pallas kernels for 2% -> 3%
where the time goes in v2:
time: 134 us; the launch traced here: 133 us
  blocking collectives  72.3 us (54%)
  starting transfers between devices  16.1 us (12%)
  between operations  14.9 us (11%)
  local copies, waits for them, and re-layouts  14.4 us (11%)
  Pallas kernels  10.3 us (8%)
  waiting for transfers between devices  4.17 us (3%)
    psum x1, blocking collectives, on_device(): gains = lax.psum(gains, ('px', 'py')).astype(BF16)  32.8 us
    all_gather x1, blocking collectives, on_device(): lax.all_gather(edge_part.astype(BF16), ('px', 'py'), axis=0, tiled=True)  20.4 us
    all_gather x1, blocking collectives, on_device(): lax.all_gather(jnp.sum(node_parts.astype(F32), axis=0).astype(BF16), ('px...  19 us
    ppermute x8, starting transfers between devices, passed_along(): lax.ppermute(array, axis, [(i, (i + by) % size) for i in range(size)])  12.5 us
    pallas_call x6, Pallas kernels, call(): pl.pallas_call(body, out_shape=outs, in_specs=[smem] * scalars + [vmem] *...  10.3 us
    unnamed x32, local copies, waits for them, and re-layouts  5.99 us
    ppermute x8, waiting for transfers between devices, passed_along(): lax.ppermute(array, axis, [(i, (i + by) % size) for i in range(size)])  4.15 us
    all_to_all x1, starting transfers between devices, on_device(): lax.all_to_all(node_sums[:3 * width].astype(BF16).reshape(devices, -1, wi...  3.55 us
  transfers between devices with their start and end apart: 10, of which 2 were waited for; matrix products, arithmetic and copies ran while one was open for 4% of the time, Pallas kernels for 3%

profile of v2, /device:TPU:0, one launch (start us, length us, event | category | flops | bytes accessed | tf_op | source)
XLA Modules:
  0.0 133.0 jit_solution(1056289491374669466)
XLA Ops:
  7.2 0.0 reduce-scatter.2.cloned.1.call-start
  7.2 0.0 copy-start.3
  7.2 0.9 copy-done.3
  8.1 0.0 copy-start.5
  8.1 0.7 copy-done.5
  8.8 0.3 shard_map.198
  9.2 5.1 %collective-permute-start = (bf16[96,256]{1,0:T(8,128)(2,1)S(1)}, bf16[96,256]{1,0:T(8,128)(2,1)S(1)}, u32[]{:S(2)}, u32[]{:S(2)}) collective-permute-start(bf16[96,256]{1,0:T(8,128)(2,1)S(1)} %get-tuple-element.27), channel_id=1, source_target_pairs={{0,12},{4,0},{8,4},{12,8},{1,13},{5,1},{9,5},{13,9},{2,14},{6,2},{... | collective-permute-start | bytes 147464 | tf_op jit(solution)/shard_map/ppermute | solution.py:16
  14.3 0.0 collective-permute-start.1
  14.9 0.7 reshape.25.gain_edge
  15.6 0.7 reshape.26.gain_node
  16.3 0.0 collective-permute-done.from_high
  16.3 3.9 %collective-permute-done.1.from_low = bf16[96,256]{1,0:T(8,128)(2,1)S(1)} collective-permute-done((bf16[96,256]{1,0:T(8,128)(2,1)S(1)}, bf16[96,256]{1,0:T(8,128)(2,1)S(1)}, u32[]{:S(2)}, u32[]{:S(2)}) %collective-permute-start.1) | collective-permute-done | bytes 49184 | tf_op jit(solution)/shard_map/ppermute | solution.py:16
  20.2 0.1 collective-permute-start.2
  20.3 1.7 %collective-permute-start.3 = (bf16[96,256]{1,0:T(8,128)(2,1)S(1)}, bf16[96,256]{1,0:T(8,128)(2,1)S(1)}, u32[]{:S(2)}, u32[]{:S(2)}) collective-permute-start(bf16[96,256]{1,0:T(8,128)(2,1)S(1)} %pad_maximum_fusion.1), channel_id=1, source_target_pairs={{0,3},{1,0},{2,1},{3,2},{4,7},{5,4},{6,5},{7,6},{8,11},{9,8},{10,9... | collective-permute-start | bytes 147464 | tf_op jit(solution)/shard_map/ppermute | solution.py:16
  22.0 1.0 copy-done.1
  23.0 1.1 copy-done.7
  24.0 0.7 copy-done.13
  24.7 0.7 copy-done.15
  25.4 0.0 copy-start.12
  25.5 0.0 copy-start.14
  25.5 1.2 shard_map.197.pre_local
  26.6 0.0 copy-start
  26.6 0.0 copy-start.8
  26.7 0.0 collective-permute-done.2.upward
  26.7 0.0 collective-permute-done.3.downward
  26.7 0.0 copy-done.2
  26.7 0.0 copy-done.9
  26.7 0.0 copy-done.10
  26.7 0.0 copy-done.11
  26.7 0.0 copy-done.12
  26.7 0.0 copy-done.14
  26.7 2.9 %shard_map.199 = (bf16[256,256]{1,0:T(8,128)(2,1)S(1)}, f32[1152,256]{1,0:T(8,128)S(1)}, f32[1152,256]{1,0:T(8,128)S(1)}, f32[1152,128]{1,0:T(8,128)S(1)}, bf16[...) custom-call(s32[1]{0:T(128)S(6)} %copy.22.count_ref, bf16[384,256]{1,0:T(8,128)(2,1)S(1)} %copy-done.3, ...), custom_call_target="tpu_custom_call" | custom-call | flops 981467136 | bytes 7161860 | tf_op jit(solution)/shard_map/pallas_call | solution.py:326
  29.7 0.0 copy-start.4
  29.7 0.9 copy-done.4
  30.6 0.0 copy-done
  30.6 0.0 copy-done.8
  30.6 3.4 %shard_map.200 = (bf16[1152,256]{1,0:T(8,128)(2,1)S(1)}, bf16[384,256]{1,0:T(8,128)(2,1)S(1)}, bf16[384,256]{1,0:T(8,128)(2,1)S(1)}, bf16[96,256]{1,0:T(8,128)(2...) custom-call(s32[1]{0:T(128)S(6)} %copy.22.count_ref, ...), custom_call_target="tpu_custom_call" | custom-call | flops 1602224128 | bytes 7357956 | tf_op jit(solution)/shard_map/pallas_call | solution.py:326
  34.0 1.1 slice.83
  35.0 0.0 reduce-scatter.2.cloned.1.call-update
  35.1 0.7 slice.87
  35.8 1.9 %slice.111 = bf16[768,256]{1,0:T(8,128)(2,1)} slice(f32[776,256]{1,0:T(8,128)} %copy-done.4), slice={[0:768], [0:256]} | slice | bytes 786432 | tf_op jit(solution)/shard_map/slice | solution.py:425
  37.7 3.6 %all-to-all-start = ((bf16[16,48,256]{2,1,0:T(8,128)(2,1)}), bf16[16,48,256]{2,1,0:T(8,128)(2,1)S(1)}, u32[]{:S(2)}, u32[]{:S(2)}) async-start(bf16[16,48,256]{2,1,0:T(8,128)(2,1)} %bitcast), calls=%async_computation.1 | async-start | bytes 786432 | tf_op jit(solution)/shard_map/all_to_all | solution.py:424
  41.3 0.3 collective-permute-start.4
  41.5 1.5 %collective-permute-start.5 = (bf16[96,256]{1,0:T(8,128)(2,1)S(1)}, bf16[96,256]{1,0:T(8,128)(2,1)S(1)}, u32[]{:S(2)}, u32[]{:S(2)}) collective-permute-start(bf16[96,256]{1,0:T(8,128)(2,1)S(1)} %get-tuple-element.41), channel_id=1, source_target_pairs={{0,3},{1,0},{2,1},{3,2},{4,7},{5,4},{6,5},{7,6},{8,11},{9,8},{10,9... | collective-permute-start | bytes 147464 | tf_op jit(solution)/shard_map/ppermute | solution.py:16
  43.1 32.8 %psum.7 = bf16[2,256]{1,0:T(2,128)(2,1)S(1)} all-reduce(f32[2,256]{1,0:T(2,128)S(1)} %pad_maximum_fusion.4), channel_id=1, replica_groups=mesh['groups'=2,'px'=4,'py'=4] {'px','py'}, use_global_device_ids=true, to_apply=%region_1.0 | all-reduce | flops 512 | bytes 3072 | tf_op jit(solution)/shard_map/psum | solution.py:464
  75.9 0.0 collective-permute-done.4.up_back
  75.9 0.0 collective-permute-done.5.down_back
  75.9 0.1 collective-permute-start.6
  76.0 3.8 %collective-permute-start.7 = (bf16[96,256]{1,0:T(8,128)(2,1)S(1)}, bf16[96,256]{1,0:T(8,128)(2,1)S(1)}, u32[]{:S(2)}, u32[]{:S(2)}) collective-permute-start(bf16[96,256]{1,0:T(8,128)(2,1)S(1)} %pad_maximum_fusion.3), channel_id=1, source_target_pairs={{0,12},{4,0},{8,4},{12,8},{1,13},{5,1},{9,5},{13,9},{2,14},{6,2},{... | collective-permute-start | bytes 147464 | tf_op jit(solution)/shard_map/ppermute | solution.py:16
  79.8 0.5 slice_reduce_fusion
  80.4 1.3 shard_map.201
  81.7 0.2 collective-permute-done.6.to_high
  81.9 0.0 collective-permute-done.7.to_low
  81.9 0.0 copy-done.6
  81.9 1.1 shard_map.202
  83.0 0.0 all-to-all-done
  83.0 0.1 reduce_sum.12
  83.1 19.0 %all_gather.7 = bf16[768,256]{1,0:T(8,128)(2,1)S(1)} all-gather(bf16[48,256]{1,0:T(8,128)(2,1)S(1)} %reduce_sum.12), channel_id=1, replica_groups=mesh['groups'=2,'px'=4,'py'=4] {'px','py'}, dimensions={0}, use_global_device_ids=true | all-gather | bytes 417792 | tf_op jit(solution)/shard_map/all_gather | solution.py:427
  102.1 0.7 slice.106
  102.8 0.7 slice.105
  103.5 0.8 convert_element_type.4
  104.3 20.4 %all_gather.6 = bf16[1024,256]{1,0:T(8,128)(2,1)S(1)} all-gather(bf16[64,256]{1,0:T(8,128)(2,1)S(1)} %convert_element_type.4), channel_id=1, replica_groups=mesh['groups'=2,'px'=4,'py'=4] {'px','py'}, dimensions={0}, use_global_device_ids=true | all-gather | bytes 557056 | tf_op jit(solution)/shard_map/all_gather | solution.py:462
  124.8 0.7 slice.102
  125.4 0.8 slice.101
  (22 shorter events, 0.1 us)
Async XLA Ops:
  7.2 96.3 %reduce-scatter.2.cloned.1.call-start = ((), (), s32[]{:S(2)}) async-start(), calls=%async_computation.2 | async-start | bytes 1114112 | tf_op jit(solution)/shard_map/reduce_scatter | solution.py:459
  7.2 0.9 copy-start.3
  8.1 0.7 copy-start.5
  9.2 7.1 %collective-permute-start = (bf16[96,256]{1,0:T(8,128)(2,1)S(1)}, bf16[96,256]{1,0:T(8,128)(2,1)S(1)}, u32[]{:S(2)}, u32[]{:S(2)}) collective-permute-start(bf16[96,256]{1,0:T(8,128)(2,1)S(1)} %get-tuple-element.27), channel_id=1, source_target_pairs={{0,12},{4,0},{8,4},{12,8},{1,13},{5,1},{9,5},{13,9},{2,14},{6,2},{... | collective-permute-start | bytes 147464 | tf_op jit(solution)/shard_map/ppermute | solution.py:16
  14.3 5.9 %collective-permute-start.1 = (bf16[96,256]{1,0:T(8,128)(2,1)S(1)}, bf16[96,256]{1,0:T(8,128)(2,1)S(1)}, u32[]{:S(2)}, u32[]{:S(2)}) collective-permute-start(bf16[96,256]{1,0:T(8,128)(2,1)S(1)} %get-tuple-element.28), channel_id=1, source_target_pairs={{0,4},{4,8},{8,12},{12,0},{1,5},{5,9},{9,13},{13,1},{2,6},{6,10},{... | collective-permute-start | bytes 147464 | tf_op jit(solution)/shard_map/ppermute | solution.py:16
  20.2 6.5 %collective-permute-start.2 = (bf16[96,256]{1,0:T(8,128)(2,1)S(1)}, bf16[96,256]{1,0:T(8,128)(2,1)S(1)}, u32[]{:S(2)}, u32[]{:S(2)}) collective-permute-start(bf16[96,256]{1,0:T(8,128)(2,1)S(1)} %pad_maximum_fusion), channel_id=1, source_target_pairs={{0,1},{1,2},{2,3},{3,0},{4,5},{5,6},{6,7},{7,4},{8,9},{9,10},{10,1... | collective-permute-start | bytes 147464 | tf_op jit(solution)/shard_map/ppermute | solution.py:16
  20.3 6.4 %collective-permute-start.3 = (bf16[96,256]{1,0:T(8,128)(2,1)S(1)}, bf16[96,256]{1,0:T(8,128)(2,1)S(1)}, u32[]{:S(2)}, u32[]{:S(2)}) collective-permute-start(bf16[96,256]{1,0:T(8,128)(2,1)S(1)} %pad_maximum_fusion.1), channel_id=1, source_target_pairs={{0,3},{1,0},{2,1},{3,2},{4,7},{5,4},{6,5},{7,6},{8,11},{9,8},{10,9... | collective-permute-start | bytes 147464 | tf_op jit(solution)/shard_map/ppermute | solution.py:16
  22.0 1.0 copy-start.1
  23.0 1.1 copy-start.7
  24.0 0.7 copy-start.13
  24.7 0.7 copy-start.15
  25.4 1.2 copy-start.2
  25.4 1.3 copy-start.9
  25.4 1.3 copy-start.10
  25.4 1.3 copy-start.11
  25.4 1.3 copy-start.12
  25.5 1.3 copy-start.14
  26.6 4.0 %copy-start = (bf16[1152,256]{1,0:T(8,128)(2,1)S(1)}, bf16[1152,256]{1,0:T(8,128)(2,1)}, u32[]{:S(2)}) copy-start(bf16[1152,256]{1,0:T(8,128)(2,1)} %edge_grads.3) | copy-start | bytes 1769476
  26.6 3.9 %copy-start.8 = (bf16[1152,256]{1,0:T(8,128)(2,1)S(1)}, bf16[1152,256]{1,0:T(8,128)(2,1)}, u32[]{:S(2)}) copy-start(bf16[1152,256]{1,0:T(8,128)(2,1)} %edges.3) | copy-start | bytes 1769476
  29.7 0.9 copy-start.4
  37.7 45.4 %all-to-all-start = ((bf16[16,48,256]{2,1,0:T(8,128)(2,1)}), bf16[16,48,256]{2,1,0:T(8,128)(2,1)S(1)}, u32[]{:S(2)}, u32[]{:S(2)}) async-start(bf16[16,48,256]{2,1,0:T(8,128)(2,1)} %bitcast), calls=%async_computation.1 | async-start | bytes 786432 | tf_op jit(solution)/shard_map/all_to_all | solution.py:424
  41.3 34.7 %collective-permute-start.4 = (bf16[96,256]{1,0:T(8,128)(2,1)S(1)}, bf16[96,256]{1,0:T(8,128)(2,1)S(1)}, u32[]{:S(2)}, u32[]{:S(2)}) collective-permute-start(bf16[96,256]{1,0:T(8,128)(2,1)S(1)} %get-tuple-element.40), channel_id=1, source_target_pairs={{0,1},{1,2},{2,3},{3,0},{4,5},{5,6},{6,7},{7,4},{8,9},{9,10},{10,1... | collective-permute-start | bytes 147464 | tf_op jit(solution)/shard_map/ppermute | solution.py:16
  41.5 34.4 %collective-permute-start.5 = (bf16[96,256]{1,0:T(8,128)(2,1)S(1)}, bf16[96,256]{1,0:T(8,128)(2,1)S(1)}, u32[]{:S(2)}, u32[]{:S(2)}) collective-permute-start(bf16[96,256]{1,0:T(8,128)(2,1)S(1)} %get-tuple-element.41), channel_id=1, source_target_pairs={{0,3},{1,0},{2,1},{3,2},{4,7},{5,4},{6,5},{7,6},{8,11},{9,8},{10,9... | collective-permute-start | bytes 147464 | tf_op jit(solution)/shard_map/ppermute | solution.py:16
  75.9 6.0 %collective-permute-start.6 = (bf16[96,256]{1,0:T(8,128)(2,1)S(1)}, bf16[96,256]{1,0:T(8,128)(2,1)S(1)}, u32[]{:S(2)}, u32[]{:S(2)}) collective-permute-start(bf16[96,256]{1,0:T(8,128)(2,1)S(1)} %pad_maximum_fusion.2), channel_id=1, source_target_pairs={{0,4},{4,8},{8,12},{12,0},{1,5},{5,9},{9,13},{13,1},{2,6},{6,10},{... | collective-permute-start | bytes 147464 | tf_op jit(solution)/shard_map/ppermute | solution.py:16
  76.0 5.9 %collective-permute-start.7 = (bf16[96,256]{1,0:T(8,128)(2,1)S(1)}, bf16[96,256]{1,0:T(8,128)(2,1)S(1)}, u32[]{:S(2)}, u32[]{:S(2)}) collective-permute-start(bf16[96,256]{1,0:T(8,128)(2,1)S(1)} %pad_maximum_fusion.3), channel_id=1, source_target_pairs={{0,12},{4,0},{8,4},{12,8},{1,13},{5,1},{9,5},{13,9},{2,14},{6,2},{... | collective-permute-start | bytes 147464 | tf_op jit(solution)/shard_map/ppermute | solution.py:16
  80.4 1.6 %copy-start.6 = (s32[8,32]{1,0:T(8,128)S(1)}, s32[8,32]{1,0:T(8,128)}, u32[]{:S(2)}) copy-start(s32[8,32]{1,0:T(8,128)} %send_list.3) | copy-start | bytes 3076
Sparse Core Ops, SparseCore 0:
  35.2 55.8 reduce-scatter.1

commit v3 on v1

--- a/solution.py
+++ b/solution.py
@@ -11,9 +11,18 @@
 VMEM_LIMIT = 24 * 1024 * 1024
 
 
+CORE = "core"
+PY = ("side", "core")
+CHIPS = ("px", "side")
+
+
 def passed_along(array, axis, by):
     size = lax.axis_size(axis)
     return lax.ppermute(array, axis, [(i, (i + by) % size) for i in range(size)])
+
+
+def across_cores(array):
+    return lax.ppermute(array, CORE, [(0, 1), (1, 0)])
 
 
 def dot(left, right):
@@ -95,18 +104,37 @@
     return [list(range(first, first + step)) for first in range(0, tiles, step)]
 
 
-def send_kernel(nodes, send_list, low, mid, high):
+def fetch_all(sources, targets, sems):
+    copies = [
+        pltpu.make_async_copy(source, target, sems.at[i])
+        for i, (source, target) in enumerate(zip(sources, targets))
+    ]
+    for copy in copies:
+        copy.start()
+    return copies
+
+
+def send_kernel(nodes_hbm, list_hbm, low, mid, high, nodes, send_list, sems):
     slots = send_list.shape[1]
+    for copy in fetch_all([list_hbm, nodes_hbm], [send_list, nodes], sems):
+        copy.wait()
     rows = dot(list_hot(send_list[...], nodes.shape[0]), nodes[...]).astype(BF16)
     low[...] = rows[: 3 * slots]
     mid[...] = rows[3 * slots : 5 * slots]
     high[...] = rows[5 * slots :]
 
 
-def local_kernel(nodes, edges, senders, receivers, w_in, pre):
+def local_kernel(nodes, *refs):
+    fetched = (len(refs) - 2) // 2
+    pre, sems = refs[fetched], refs[-1]
+    targets = refs[fetched + 1 : -1]
+    w_in, senders, receivers, edges = targets[:4]
+    copies = fetch_all(refs[:fetched], targets, sems)
     count, width = nodes.shape
     tile_rows = senders.shape[1]
     x = nodes[...]
+    for copy in copies[:4]:
+        copy.wait()
     table = jnp.concatenate(
         [
             dot(x, w_in[width : 2 * width]).astype(BF16),
@@ -123,6 +151,27 @@
             [hot_rows(by_sender, tiles, 0, count), hot_rows(by_receiver, tiles, 0, count)], axis=1
         )
         pre[rows, :] = dot(edges[rows, :], w_edge) + dot(hot, table)
+    for copy in copies[4:]:
+        copy.wait()
+
+
+def split_by_core(sums, keep_out, away_out):
+    half = keep_out.shape[0]
+    core = lax.axis_index(CORE)
+    keep_out[...] = sums[pl.ds(pl.multiple_of(core * half, half), half), :]
+    away = sums[pl.ds(pl.multiple_of((1 - core) * half, half), half), :]
+    away_out[:half] = away.astype(BF16)
+
+
+def pack_gains(edge_gain, node_gain):
+    edge_high = edge_gain.astype(BF16).astype(F32)
+    node_high = node_gain.astype(BF16).astype(F32)
+    row = lax.broadcasted_iota(jnp.int32, (16, edge_gain.shape[1]), 0)
+    packed = jnp.where(row == 0, edge_high, 0.0)
+    packed = jnp.where(row == 1, edge_gain - edge_high, packed)
+    packed = jnp.where(row == 2, node_high, packed)
+    packed = jnp.where(row == 3, node_gain - node_high, packed)
+    return packed.astype(BF16)
 
 
 def forward_kernel(
@@ -148,6 +197,9 @@
     scale_out,
     agg_grad_out,
     node_part_out,
+    keep_out,
+    away_out,
+    node_gain_out,
     node_sums,
 ):
     count, width = nodes.shape
@@ -200,7 +252,8 @@
     node_sums[:width] = dot_tn(x, pre_grad)
     node_sums[width : 2 * width] = dot_tn(aggregated, pre_grad)
     node_sums[2 * width : 3 * width] = dot_tn(node_hidden, out_grad)
-    node_sums[3 * width :] = jnp.broadcast_to(
+    split_by_core(node_sums, keep_out, away_out)
+    node_gain_out[...] = jnp.broadcast_to(
         jnp.sum(upstream * normed, axis=0, keepdims=True), (8, width)
     )
 
@@ -220,12 +273,16 @@
     w_in,
     w_out,
     gain_edge,
+    node_gain,
     pre_grad_out,
     sender_out,
     receiver_out,
     up_out,
     down_out,
     rest_out,
+    keep_out,
+    away_out,
+    gains_out,
     edge_sums,
 ):
     count, width = nodes.shape
@@ -278,7 +335,46 @@
     edge_sums[width : 2 * width] = dot_tn(x, own) + dot_tn(halo[...], away)
     edge_sums[2 * width : 3 * width] = dot_tn(x, received)
     edge_sums[3 * width : 4 * width] = second
-    edge_sums[4 * width :] = jnp.broadcast_to(gain_total, (8, width))
+    split_by_core(edge_sums, keep_out, away_out)
+    gains = pack_gains(gain_total, node_gain[:1])
+    away_out[keep_out.shape[0] :] = gains
+    gains_out[...] = gains
+
+
+def edge_pair_kernel(keep, gains, other, rows_out, gains_out):
+    half = keep.shape[0]
+    rows_out[...] = (keep[...] + other[:half].astype(F32)).astype(BF16)
+    both = gains[...].astype(F32) + other[half:].astype(F32)
+    gains_out[...] = pack_gains(both[0:1] + both[1:2], both[2:3] + both[3:4])
+
+
+def node_pair_kernel(keep, other, rows_out):
+    rows_out[...] = (keep[...] + other[...].astype(F32)).astype(BF16)
+
+
+def place_kernel(own, other, first, second, sems):
+    half = own.shape[0]
+    rest = first.shape[0] - half
+    core = lax.axis_index(CORE)
+
+    def place(low, high):
+        copies = [
+            pltpu.make_async_copy(low, first.at[:half], sems.at[0]),
+            pltpu.make_async_copy(high.at[:rest], first.at[half:], sems.at[1]),
+            pltpu.make_async_copy(high.at[rest:], second, sems.at[2]),
+        ]
+        for copy in copies:
+            copy.start()
+        for copy in copies:
+            copy.wait()
+
+    @pl.when(core == 0)
+    def _():
+        place(own, other)
+
+    @pl.when(core == 1)
+    def _():
+        place(other, own)
 
 
 def finish_kernel(
@@ -318,23 +414,51 @@
     nodes_grad[...] = (local_grad[...] + dot_tn(hot, returned)).astype(BF16)
 
 
-def call(body, outs, flops, *operands, scalars=0):
+SMEM = pltpu.SMEM
+VMEM = pltpu.VMEM
+HBM = pltpu.HBM
+
+
+def call(body, outs, flops, *operands, spaces=(), out_space=VMEM, scratch=()):
     moved = sum(x.size * x.dtype.itemsize for x in operands)
     moved += sum(x.size * jnp.dtype(x.dtype).itemsize for x in outs)
-    smem = pl.BlockSpec(memory_space=pltpu.SMEM)
-    vmem = pl.BlockSpec(memory_space=pltpu.VMEM)
+    spaces = list(spaces) + [VMEM] * (len(operands) - len(spaces))
     return pl.pallas_call(
         body,
         out_shape=outs,
-        in_specs=[smem] * scalars + [vmem] * (len(operands) - scalars),
-        out_specs=[vmem] * len(outs),
+        in_specs=[pl.BlockSpec(memory_space=space) for space in spaces],
+        out_specs=[pl.BlockSpec(memory_space=out_space) for _ in outs],
+        scratch_shapes=list(scratch),
         compiler_params=pltpu.CompilerParams(vmem_limit_bytes=VMEM_LIMIT),
         cost_estimate=pl.CostEstimate(flops=flops, bytes_accessed=moved, transcendentals=0),
     )(*operands)
 
 
+def like(array):
+    return jax.ShapeDtypeStruct(array.shape, array.dtype)
+
+
+def spread(rows):
+    chips = lax.axis_size(CHIPS)
+    copies = jnp.broadcast_to(rows[None], (chips,) + rows.shape)
+    return lax.all_to_all(copies, CHIPS, 0, 0).reshape(chips * rows.shape[0], rows.shape[1])
+
+
 def shaped(rows, columns, dtype):
     return jax.ShapeDtypeStruct((rows, columns), dtype)
+
+
+def placed(own, first_rows, second_rows):
+    width = own.shape[1]
+    return call(
+        place_kernel,
+        [shaped(first_rows, width, BF16), shaped(second_rows, width, BF16)],
+        0,
+        own,
+        across_cores(own),
+        out_space=HBM,
+        scratch=[pltpu.SemaphoreType.DMA((3,))],
+    )
 
 
 def on_device(
@@ -361,36 +485,61 @@
     gain_edge = gain_edge.reshape(1, width)
     gain_node = gain_node.reshape(1, width)
 
-    low, mid, high = call(
+    low, mid, high, nodes, send_list = call(
         send_kernel,
         [
             shaped(3 * slots, width, BF16),
             shaped(2 * slots, width, BF16),
             shaped(3 * slots, width, BF16),
+            like(nodes),
+            like(send_list),
         ],
         2 * halo_rows * count * width,
         nodes,
         send_list,
+        spaces=[HBM, HBM],
+        scratch=[pltpu.SemaphoreType.DMA((2,))],
     )
     from_low = passed_along(high, "px", 1)
     from_high = passed_along(low, "px", -1)
     upward = passed_along(
-        jnp.concatenate([from_high[2 * slots :], mid[slots:], from_low[2 * slots :]]), "py", 1
+        jnp.concatenate([from_high[2 * slots :], mid[slots:], from_low[2 * slots :]]), PY, 1
     )
     downward = passed_along(
-        jnp.concatenate([from_high[:slots], mid[:slots], from_low[:slots]]), "py", -1
-    )
-    (pre_local,) = call(
+        jnp.concatenate([from_high[:slots], mid[:slots], from_low[:slots]]), PY, -1
+    )
+    fetched = [
+        w_edge_in,
+        senders,
+        receivers,
+        edges,
+        w_edge_out,
+        w_node_in,
+        w_node_out,
+        node_grads,
+        edge_grads,
+    ]
+    pre_local, *fetched = call(
         local_kernel,
-        [shaped(edge_rows, width, F32)],
+        [shaped(edge_rows, width, F32)] + [like(x) for x in fetched],
         square * (2 * count + edge_rows) + 4 * edge_rows * count * width,
         nodes,
-        edges,
+        *fetched,
+        spaces=[VMEM] + [HBM] * len(fetched),
+        scratch=[pltpu.SemaphoreType.DMA((len(fetched),))],
+    )
+    (
+        w_edge_in,
         senders,
         receivers,
-        w_edge_in,
-    )
-    halo, pre, normed, scale, agg_grad, node_part, node_sums = call(
+        edges,
+        w_edge_out,
+        w_node_in,
+        w_node_out,
+        node_grads,
+        edge_grads,
+    ) = fetched
+    halo, pre, normed, scale, agg_grad, node_part, node_keep, node_away, node_gain = call(
         forward_kernel,
         [
             shaped(halo_rows, width, BF16),
@@ -399,7 +548,9 @@
             shaped(edge_rows, 128, F32),
             shaped(count, width, BF16),
             shaped(count, width, F32),
-            shaped(3 * width + 8, width, F32),
+            shaped(3 * width // 2, width, F32),
+            shaped(3 * width // 2, width, BF16),
+            shaped(8, width, F32),
         ],
         square * (2 * edge_rows + 9 * count) + 2 * edge_rows * count * width,
         tile_count,
@@ -418,10 +569,11 @@
         w_node_in,
         w_node_out,
         gain_node,
-        scalars=1,
-    )
-    node_sums = lax.psum(node_sums, ("px", "py"))
-    pre_grad, sender_sum, receiver_sum, up, down, rest, edge_sums = call(
+        spaces=[SMEM],
+        scratch=[pltpu.VMEM((3 * width, width), F32)],
+    )
+    node_other = across_cores(node_away)
+    pre_grad, sender_sum, receiver_sum, up, down, rest, edge_keep, edge_away, gains = call(
         backward_kernel,
         [
             shaped(edge_rows, width, BF16),
@@ -430,7 +582,9 @@
             shaped(3 * slots, width, BF16),
             shaped(3 * slots, width, BF16),
             shaped(2 * slots, width, BF16),
-            shaped(4 * width + 8, width, F32),
+            shaped(2 * width, width, F32),
+            shaped(2 * width + 16, width, BF16),
+            shaped(16, width, BF16),
         ],
         square * (4 * edge_rows + 2 * count + 2 * halo_rows)
         + 2 * edge_rows * (3 * count + halo_rows) * width,
@@ -448,11 +602,39 @@
         w_edge_in,
         w_edge_out,
         gain_edge,
-        scalars=1,
-    )
-    edge_sums = lax.psum(edge_sums, ("px", "py"))
-    up_back = passed_along(up, "py", 1)
-    down_back = passed_along(down, "py", -1)
+        node_gain,
+        spaces=[SMEM],
+        scratch=[pltpu.VMEM((4 * width, width), F32)],
+    )
+    edge_other = across_cores(edge_away)
+    (node_pair,) = call(
+        node_pair_kernel, [shaped(3 * width // 2, width, BF16)], 0, node_keep, node_other
+    )
+    edge_pair, gains = call(
+        edge_pair_kernel,
+        [shaped(2 * width, width, BF16), like(gains)],
+        0,
+        edge_keep,
+        gains,
+        edge_other,
+    )
+    chips = lax.axis_size(CHIPS)
+    blocks = jnp.concatenate(
+        [
+            edge_pair.reshape(chips, -1, width),
+            jnp.broadcast_to(gains[None], (chips,) + gains.shape),
+        ],
+        axis=1,
+    )
+    edge_part = jnp.sum(lax.all_to_all(blocks, CHIPS, 0, 0).astype(F32), axis=0)
+    node_part_sum = jnp.sum(
+        lax.all_to_all(node_pair.reshape(chips, -1, width), CHIPS, 0, 0).astype(F32), axis=0
+    )
+    gains = edge_part[2 * width // chips :]
+    edge_half = spread(edge_part[: 2 * width // chips].astype(BF16))
+    node_half = spread(node_part_sum.astype(BF16))
+    up_back = passed_along(up, PY, 1)
+    down_back = passed_along(down, PY, -1)
     to_high = passed_along(
         jnp.concatenate([up_back[:slots], down_back[:slots], rest[:slots]]), "px", 1
     )
@@ -481,28 +663,30 @@
         to_high,
         to_low,
     )
+    w_edge_in_grad, w_edge_out_grad = placed(edge_half, 3 * width, width)
+    w_node_in_grad, w_node_out_grad = placed(node_half, 2 * width, width)
     return (
         nodes_grad,
         edges_grad,
-        edge_sums[: 3 * width].astype(BF16),
-        edge_sums[3 * width : 4 * width].astype(BF16),
-        edge_sums[4 * width].astype(BF16),
-        node_sums[: 2 * width].astype(BF16),
-        node_sums[2 * width : 3 * width].astype(BF16),
-        node_sums[3 * width].astype(BF16),
+        w_edge_in_grad,
+        w_edge_out_grad,
+        (gains[0] + gains[1]).astype(BF16),
+        w_node_in_grad,
+        w_node_out_grad,
+        (gains[2] + gains[3]).astype(BF16),
     )
 
 
 def solution(mesh):
     in_specs = (
-        P(("groups", "px", "py"), None),
-        P(("groups", "px", "py"), None),
-        P(("groups", "px", "py"), None),
-        P(("groups", "px", "py"), None),
-        P(("groups", "px", "py"), None),
-        P(("groups", "px", "py"), None),
-        P(("groups", "px", "py"), None),
-        P(("groups", "px", "py")),
+        P(("groups", "px") + PY, None),
+        P(("groups", "px") + PY, None),
+        P(("groups", "px") + PY, None),
+        P(("groups", "px") + PY, None),
+        P(("groups", "px") + PY, None),
+        P(("groups", "px") + PY, None),
+        P(("groups", "px") + PY, None),
+        P(("groups", "px") + PY),
         P(),
         P(),
         P(),
@@ -511,8 +695,8 @@
         P(),
     )
     out_specs = (
-        P(("groups", "px", "py"), None),
-        P(("groups", "px", "py"), None),
+        P(("groups", "px") + PY, None),
+        P(("groups", "px") + PY, None),
         P("groups", None),
         P("groups", None),
         P("groups"),
@@ -520,6 +704,10 @@
         P("groups", None),
         P("groups"),
     )
+    groups, px, py = mesh.devices.shape
+    by_core = jax.sharding.Mesh(
+        mesh.devices.reshape(groups, px, py // 2, 2), ("groups", "px") + PY
+    )
     return jax.shard_map(
-        on_device, mesh=mesh, in_specs=in_specs, out_specs=out_specs, check_vma=False
-    )
+        on_device, mesh=by_core, in_specs=in_specs, out_specs=out_specs, check_vma=False
+    )

time: 117 us -> 94.5 us (0.81)
  blocking collectives: 73 us -> 0 us
  waiting for transfers between devices: 5.64 us -> 34.4 us
  starting transfers between devices: 10.8 us -> 26.3 us
  Pallas kernels: 10.7 us -> 15.1 us
  other arithmetic: 0.02 us -> 3.77 us
  local copies, waits for them, and re-layouts: 14.5 us -> 12.6 us
    psum x1 -> x0, blocking collectives: 73 us -> none  [on_device(): edge_sums = lax.psum(edge_sums, ('px', 'py'))]
    all_to_all x0 -> x4, waiting for transfers between devices: none -> 28.2 us  [the longest x2 13.6 us: spread(): lax.all_to_all(copies, CHIPS, 0, 0)]
    all_to_all x0 -> x4, starting transfers between devices: none -> 14.5 us  [the longest x2 7.05 us: spread(): lax.all_to_all(copies, CHIPS, 0, 0)]
    slice x5 -> x1, local copies, waits for them, and re-layouts: 5.94 us -> 0.01 us  [on_device(): edge_half = spread(edge_part[:2 * width // chips].astype(BF16))]
    pallas_call x6 -> x10, Pallas kernels: 10.7 us -> 15.1 us  [call(): pl.pallas_call(body, out_shape=outs, in_specs=[pl.BlockSpec(memory_space=...]
    unnamed x46 -> x24, local copies, waits for them, and re-layouts: 7.21 us -> 9.81 us
    broadcast_in_dim x0 -> x3, local copies, waits for them, and re-layouts: none -> 1.42 us  [the longest x2 1.41 us: spread(): copies = jnp.broadcast_to(rows[None], (chips,) + rows.shape)]
    convert_element_type x0 -> x1, other arithmetic: none -> 1.37 us  [on_device(): (gains[2] + gains[3]).astype(BF16)]
  transfers between devices with their start and end apart: 8 -> 16, of which waited for: 2 -> 6; matrix products, arithmetic and copies ran while one was open for 6% -> 7% of each run, Pallas kernels for 2% -> 11%
where the time goes in v3:
time: 94.5 us; the launch traced here: 93.6 us
  waiting for transfers between devices  34.4 us (36%)
  starting transfers between devices  26.3 us (28%)
  Pallas kernels  15.1 us (16%)
  local copies, waits for them, and re-layouts  12.6 us (13%)
  other arithmetic  3.77 us (4%)
  between operations  1.51 us (2%)
    pallas_call x10, Pallas kernels, call(): pl.pallas_call(body, out_shape=outs, in_specs=[pl.BlockSpec(memory_space=...  15.1 us
    all_to_all x2, waiting for transfers between devices, spread(): lax.all_to_all(copies, CHIPS, 0, 0)  13.6 us
    ppermute x8, starting transfers between devices, passed_along(): lax.ppermute(array, axis, [(i, (i + by) % size) for i in range(size)])  11.2 us
    unnamed x24, local copies, waits for them, and re-layouts  9.81 us
    all_to_all x1, waiting for transfers between devices, on_device(): lax.all_to_all(node_pair.reshape(chips, -1, width), CHIPS, 0, 0).astype(F32)  7.61 us
    all_to_all x2, starting transfers between devices, spread(): lax.all_to_all(copies, CHIPS, 0, 0)  7.05 us
    all_to_all x1, waiting for transfers between devices, on_device(): edge_part = jnp.sum(lax.all_to_all(blocks, CHIPS, 0, 0).astype(F32), axis=0)  6.98 us
    ppermute x8, waiting for transfers between devices, passed_along(): lax.ppermute(array, axis, [(i, (i + by) % size) for i in range(size)])  6.12 us
  transfers between devices with their start and end apart: 16, of which 6 were waited for; matrix products, arithmetic and copies ran while one was open for 7% of the time, Pallas kernels for 11%

profile of v3, /device:TPU:0, one launch (start us, length us, event | category | flops | bytes accessed | tf_op | source)
XLA Modules:
  0.0 93.6 jit_solution(5464374479071963320)
XLA Ops:
  0.6 0.0 copy-start
  0.6 0.9 copy-done
  1.6 0.7 copy-done.1
  2.2 0.6 shard_map.197
  2.8 5.1 %collective-permute-start = (bf16[96,256]{1,0:T(8,128)(2,1)S(1)}, bf16[96,256]{1,0:T(8,128)(2,1)S(1)}, u32[]{:S(2)}, u32[]{:S(2)}) collective-permute-start(bf16[96,256]{1,0:T(8,128)(2,1)S(1)} %get-tuple-element.56), channel_id=1, source_target_pairs={{0,12},{4,0},{8,4},{12,8},{1,13},{5,1},{9,5},{13,9},{2,14},{6,2},{... | collective-permute-start | bytes 147464 | tf_op jit(solution)/shard_map/ppermute | solution.py:21
  8.0 0.0 collective-permute-start.1
  8.6 0.7 reshape.41.gain_edge
  9.3 0.7 reshape.42.gain_node
  9.9 0.0 collective-permute-done.from_high
  9.9 3.9 %collective-permute-done.1.from_low = bf16[96,256]{1,0:T(8,128)(2,1)S(1)} collective-permute-done((bf16[96,256]{1,0:T(8,128)(2,1)S(1)}, bf16[96,256]{1,0:T(8,128)(2,1)S(1)}, u32[]{:S(2)}, u32[]{:S(2)}) %collective-permute-start.1) | collective-permute-done | bytes 49184 | tf_op jit(solution)/shard_map/ppermute | solution.py:21
  13.9 0.1 collective-permute-start.2
  13.9 1.7 %collective-permute-start.3 = (bf16[96,256]{1,0:T(8,128)(2,1)S(1)}, bf16[96,256]{1,0:T(8,128)(2,1)S(1)}, u32[]{:S(2)}, u32[]{:S(2)}) collective-permute-start(bf16[96,256]{1,0:T(8,128)(2,1)S(1)} %pad_maximum_fusion.2), channel_id=1, source_target_pairs={{0,3},{1,0},{2,1},{3,2},{4,7},{5,4},{6,5},{7,6},{8,11},{9,8},{10,9... | collective-permute-start | bytes 147464 | tf_op jit(solution)/shard_map/ppermute | solution.py:21
  15.7 1.1 %copy-done.2 = bf16[1152,256]{1,0:T(8,128)(2,1)S(1)} copy-done((bf16[1152,256]{1,0:T(8,128)(2,1)S(1)}, bf16[1152,256]{1,0:T(8,128)(2,1)}, u32[]{:S(2)}) %copy-start.2) | copy-done | bytes 589848
  16.7 1.1 %copy-done.3 = bf16[1152,256]{1,0:T(8,128)(2,1)S(1)} copy-done((bf16[1152,256]{1,0:T(8,128)(2,1)S(1)}, bf16[1152,256]{1,0:T(8,128)(2,1)}, u32[]{:S(2)}) %copy-start.3) | copy-done | bytes 589848
  17.8 1.0 %copy-done.4 = bf16[768,256]{1,0:T(8,128)(2,1)S(1)} copy-done((bf16[768,256]{1,0:T(8,128)(2,1)S(1)}, bf16[768,256]{1,0:T(8,128)(2,1)}, u32[]{:S(2)}) %copy-start.4) | copy-done | bytes 393240
  18.8 0.9 %copy-done.5 = bf16[512,256]{1,0:T(8,128)(2,1)S(1)} copy-done((bf16[512,256]{1,0:T(8,128)(2,1)S(1)}, bf16[512,256]{1,0:T(8,128)(2,1)}, u32[]{:S(2)}) %copy-start.5) | copy-done | bytes 262168
  19.7 0.9 copy-done.6
  20.7 0.9 copy-done.7
  21.6 0.9 copy-done.8
  22.5 0.7 copy-done.9
  23.2 0.7 copy-done.10
  23.9 2.4 %shard_map.198 = (f32[1152,256]{1,0:T(8,128)S(1)}, bf16[768,256]{1,0:T(8,128)(2,1)S(1)}, s32[9,128]{1,0:T(8,128)S(1)}, s32[9,128]{1,0:T(8,128)S(1)}, bf16[1152,2...) custom-call(bf16[384,256]{1,0:T(8,128)(2,1)S(1)} %get-tuple-element., ...), custom_call_target="tpu_custom_call" | custom-call | flops 704643072 | bytes 5982208 | tf_op jit(solution)/shard_map/pallas_call | solution.py:426
  26.2 0.0 collective-permute-done.2.upward
  26.2 0.0 collective-permute-done.3.downward
  26.3 3.0 %shard_map.199 = (bf16[256,256]{1,0:T(8,128)(2,1)S(1)}, f32[1152,256]{1,0:T(8,128)S(1)}, f32[1152,256]{1,0:T(8,128)S(1)}, f32[1152,128]{1,0:T(8,128)S(1)}, bf16[...) custom-call(s32[1]{0:T(128)S(6)} %copy.22.count_ref, ...), custom_call_target="tpu_custom_call" | custom-call | flops 981467136 | bytes 6965252 | tf_op jit(solution)/shard_map/pallas_call | solution.py:426
  29.3 0.1 collective-permute-start.10
  29.4 4.3 %shard_map.200 = (bf16[1152,256]{1,0:T(8,128)(2,1)S(1)}, bf16[384,256]{1,0:T(8,128)(2,1)S(1)}, bf16[384,256]{1,0:T(8,128)(2,1)S(1)}, bf16[96,256]{1,0:T(8,128)(2...) custom-call(s32[1]{0:T(128)S(6)} %copy.22.count_ref, ...), custom_call_target="tpu_custom_call" | custom-call | flops 1602224128 | bytes 7112196 | tf_op jit(solution)/shard_map/pallas_call | solution.py:426
  33.7 0.5 collective-permute-start.8
  34.1 0.0 collective-permute-done.10.other
  34.1 0.7 shard_map.205
  34.9 4.0 %all-to-all-start.2 = ((bf16[8,48,256]{2,1,0:T(8,128)(2,1)}), bf16[8,48,256]{2,1,0:T(8,128)(2,1)}, u32[]{:S(2)}, u32[]{:S(2)}) async-start(bf16[8,48,256]{2,1,0:T(8,128)(2,1)} %bitcast.2), calls=%async_computation.2 | async-start | bytes 393216 | tf_op jit(solution)/shard_map/all_to_all | solution.py:631
  38.9 0.0 collective-permute-done.8.other
  38.9 0.1 shard_map.203
  39.0 0.7 pad_maximum_fusion
  39.7 7.6 %all-to-all-done.2 = bf16[8,48,256]{2,1,0:T(8,128)(2,1)} async-done(((bf16[8,48,256]{2,1,0:T(8,128)(2,1)}), bf16[8,48,256]{2,1,0:T(8,128)(2,1)}, u32[]{:S(2)}, u32[]{:S(2)}) %all-to-all-start.2) | async-done | bytes 196640 | tf_op jit(solution)/shard_map/all_to_all | solution.py:631
  47.3 3.4 %all-to-all-start = ((bf16[8,80,256]{2,1,0:T(8,128)(2,1)}), bf16[8,80,256]{2,1,0:T(8,128)(2,1)S(1)}, u32[]{:S(2)}, u32[]{:S(2)}) async-start(bf16[8,80,256]{2,1,0:T(8,128)(2,1)} %pad_maximum_fusion), calls=%async_computation | async-start | bytes 655360 | tf_op jit(solution)/shard_map/all_to_all | solution.py:629
  50.8 0.1 collective-permute-start.4
  50.8 1.7 %collective-permute-start.5 = (bf16[96,256]{1,0:T(8,128)(2,1)S(1)}, bf16[96,256]{1,0:T(8,128)(2,1)S(1)}, u32[]{:S(2)}, u32[]{:S(2)}) collective-permute-start(bf16[96,256]{1,0:T(8,128)(2,1)S(1)} %get-tuple-element.76), channel_id=1, source_target_pairs={{0,3},{1,0},{2,1},{3,2},{4,7},{5,4},{6,5},{7,6},{8,11},{9,8},{10,9... | collective-permute-start | bytes 147464 | tf_op jit(solution)/shard_map/ppermute | solution.py:21
  52.6 1.0 %reduce_sum.22 = bf16[48,256]{1,0:T(8,128)(2,1)S(1)} reduce(bf16[8,48,256]{2,1,0:T(8,128)(2,1)} %all-to-all-done.2, bf16[]{:T(256)} %constant.3.clone.1), dimensions={0}, to_apply=%region_1.0 | reduce | flops 86016 | bytes 221186 | tf_op jit(solution)/shard_map/reduce_sum | solution.py:630
  53.5 7.0 %all-to-all-done = bf16[8,80,256]{2,1,0:T(8,128)(2,1)S(1)} async-done(((bf16[8,80,256]{2,1,0:T(8,128)(2,1)}), bf16[8,80,256]{2,1,0:T(8,128)(2,1)S(1)}, u32[]{:S(2)}, u32[]{:S(2)}) %all-to-all-start) | async-done | bytes 327712 | tf_op jit(solution)/shard_map/all_to_all | solution.py:629
  60.5 0.7 broadcast_in_dim.8
  61.2 3.6 %all-to-all-start.3 = ((bf16[8,48,256]{2,1,0:T(8,128)(2,1)}), bf16[8,48,256]{2,1,0:T(8,128)(2,1)S(1)}, u32[]{:S(2)}, u32[]{:S(2)}) async-start(bf16[8,48,256]{2,1,0:T(8,128)(2,1)} %broadcast_in_dim.8), calls=%async_computation.3 | async-start | bytes 393216 | tf_op jit(solution)/shard_map/all_to_all | solution.py:444
  64.9 0.0 copy-start.11
  64.9 7.7 %all-to-all-done.3 = bf16[8,48,256]{2,1,0:T(8,128)(2,1)S(1)} async-done(((bf16[8,48,256]{2,1,0:T(8,128)(2,1)}), bf16[8,48,256]{2,1,0:T(8,128)(2,1)S(1)}, u32[]{:S(2)}, u32[]{:S(2)}) %all-to-all-start.3) | async-done | bytes 196640 | tf_op jit(solution)/shard_map/all_to_all | solution.py:444
  72.6 0.7 broadcast_in_dim.7
  73.3 3.4 %all-to-all-start.1 = ((bf16[8,64,256]{2,1,0:T(8,128)(2,1)}), bf16[8,64,256]{2,1,0:T(8,128)(2,1)S(1)}, u32[]{:S(2)}, u32[]{:S(2)}) async-start(bf16[8,64,256]{2,1,0:T(8,128)(2,1)} %broadcast_in_dim.7), calls=%async_computation.1 | async-start | bytes 524288 | tf_op jit(solution)/shard_map/all_to_all | solution.py:444
  76.8 0.0 collective-permute-done.4.up_back
  76.8 0.0 collective-permute-done.5.down_back
  76.8 0.6 pad_maximum_fusion.3
  77.4 1.9 %collective-permute-start.6 = (bf16[96,256]{1,0:T(8,128)(2,1)}, bf16[96,256]{1,0:T(8,128)(2,1)S(1)}, u32[]{:S(2)}, u32[]{:S(2)}) collective-permute-start(bf16[96,256]{1,0:T(8,128)(2,1)} %pad_maximum_fusion.3), channel_id=1, source_target_pairs={{0,4},{4,8},{8,12},{12,0},{1,5},{5,9},{9,13},{13,1},{2,6},{6,10},{... | collective-permute-start | bytes 147464 | tf_op jit(solution)/shard_map/ppermute | solution.py:21
  79.3 0.0 copy-done.11
  79.3 0.0 collective-permute-start.11
  79.3 5.9 %all-to-all-done.1 = bf16[8,64,256]{2,1,0:T(8,128)(2,1)S(1)} async-done(((bf16[8,64,256]{2,1,0:T(8,128)(2,1)}), bf16[8,64,256]{2,1,0:T(8,128)(2,1)S(1)}, u32[]{:S(2)}, u32[]{:S(2)}) %all-to-all-start.1) | async-done | bytes 262176 | tf_op jit(solution)/shard_map/all_to_all | solution.py:444
  85.3 0.0 collective-permute-start.9
  85.3 0.6 collective-permute-start.7
  85.9 1.3 %shard_map.201 = (bf16[1152,256]{1,0:T(8,128)(2,1)}, f32[384,256]{1,0:T(8,128)S(1)}) custom-call(bf16[1152,256]{1,0:T(8,128)(2,1)S(1)} %get-tuple-element.51.edge_grads, bf16[1152,256]{1,0:T(8,128)(2,1)S(1)} %get-tuple-element.70.pre_grad, bf16[384,256]{1,0:T(8,128)(2,1)S(1)} %get-tuple-element.71.sender_sum, ...), custom_call_target="tpu_custom_call" | custom-call | flops 251658240 | bytes 3342336 | tf_op jit(solution)/shard_map/pallas_call | solution.py:426
  87.2 0.0 collective-permute-done.6.to_high
  87.2 2.2 %collective-permute-done.7.to_low = bf16[96,256]{1,0:T(8,128)(2,1)S(1)} collective-permute-done((bf16[96,256]{1,0:T(8,128)(2,1)S(1)}, bf16[96,256]{1,0:T(8,128)(2,1)S(1)}, u32[]{:S(2)}, u32[]{:S(2)}) %collective-permute-start.7) | collective-permute-done | bytes 49184 | tf_op jit(solution)/shard_map/ppermute | solution.py:21
  89.5 1.1 %shard_map.202 = bf16[384,256]{1,0:T(8,128)(2,1)} custom-call(s32[8,32]{1,0:T(8,128)S(1)} %get-tuple-element.49.send_list, f32[384,256]{1,0:T(8,128)S(1)} %get-tuple-element.74.local_grad, bf16[96,256]{1,0:T(8,128)(2,1)S(1)} %collective-permute-done.4.up_back, bf16[96,256]{1,0:T(8,128)(2,1)S(1)} %collective-permute-done.5.down_back, ...), custom_call_target="tpu_custom_call" | custom-call | flops 50331648 | bytes 787456 | tf_op jit(solution)/shard_map/pallas_call | solution.py:426
  90.6 1.4 %fusion.3 = (bf16[256]{0:T(256)(128)(2,1)}, bf16[256]{0:T(256)(128)(2,1)}) fusion(f32[80,256]{1,0:T(8,128)} %copy-done.11), kind=kLoop, calls=%fused_computation.12 | loop fusion | flops 1024 | bytes 5120 | tf_op jit(solution)/shard_map/convert_element_type | solution.py:676
  91.9 0.0 collective-permute-done.11.other
  91.9 0.8 shard_map.206
  92.7 0.0 collective-permute-done.9.other
  92.7 0.8 shard_map.204
  (22 shorter events, 0.1 us)
Async XLA Ops:
  0.6 0.9 copy-start
  1.6 0.7 copy-start.1
  2.8 7.1 %collective-permute-start = (bf16[96,256]{1,0:T(8,128)(2,1)S(1)}, bf16[96,256]{1,0:T(8,128)(2,1)S(1)}, u32[]{:S(2)}, u32[]{:S(2)}) collective-permute-start(bf16[96,256]{1,0:T(8,128)(2,1)S(1)} %get-tuple-element.56), channel_id=1, source_target_pairs={{0,12},{4,0},{8,4},{12,8},{1,13},{5,1},{9,5},{13,9},{2,14},{6,2},{... | collective-permute-start | bytes 147464 | tf_op jit(solution)/shard_map/ppermute | solution.py:21
  8.0 5.9 %collective-permute-start.1 = (bf16[96,256]{1,0:T(8,128)(2,1)S(1)}, bf16[96,256]{1,0:T(8,128)(2,1)S(1)}, u32[]{:S(2)}, u32[]{:S(2)}) collective-permute-start(bf16[96,256]{1,0:T(8,128)(2,1)S(1)} %get-tuple-element.57), channel_id=1, source_target_pairs={{0,4},{4,8},{8,12},{12,0},{1,5},{5,9},{9,13},{13,1},{2,6},{6,10},{... | collective-permute-start | bytes 147464 | tf_op jit(solution)/shard_map/ppermute | solution.py:21
  13.9 12.4 %collective-permute-start.2 = (bf16[96,256]{1,0:T(8,128)(2,1)S(1)}, bf16[96,256]{1,0:T(8,128)(2,1)S(1)}, u32[]{:S(2)}, u32[]{:S(2)}) collective-permute-start(bf16[96,256]{1,0:T(8,128)(2,1)S(1)} %pad_maximum_fusion.1), channel_id=1, source_target_pairs={{0,1},{1,2},{2,3},{3,0},{4,5},{5,6},{6,7},{7,4},{8,9},{9,10},{10,1... | collective-permute-start | bytes 147464 | tf_op jit(solution)/shard_map/ppermute | solution.py:21
  13.9 12.3 %collective-permute-start.3 = (bf16[96,256]{1,0:T(8,128)(2,1)S(1)}, bf16[96,256]{1,0:T(8,128)(2,1)S(1)}, u32[]{:S(2)}, u32[]{:S(2)}) collective-permute-start(bf16[96,256]{1,0:T(8,128)(2,1)S(1)} %pad_maximum_fusion.2), channel_id=1, source_target_pairs={{0,3},{1,0},{2,1},{3,2},{4,7},{5,4},{6,5},{7,6},{8,11},{9,8},{10,9... | collective-permute-start | bytes 147464 | tf_op jit(solution)/shard_map/ppermute | solution.py:21
  15.7 1.1 %copy-start.2 = (bf16[1152,256]{1,0:T(8,128)(2,1)S(1)}, bf16[1152,256]{1,0:T(8,128)(2,1)}, u32[]{:S(2)}) copy-start(bf16[1152,256]{1,0:T(8,128)(2,1)} %refs_3_.1) | copy-start | bytes 1769476
  16.7 1.1 %copy-start.3 = (bf16[1152,256]{1,0:T(8,128)(2,1)S(1)}, bf16[1152,256]{1,0:T(8,128)(2,1)}, u32[]{:S(2)}) copy-start(bf16[1152,256]{1,0:T(8,128)(2,1)} %refs_8_.1) | copy-start | bytes 1769476
  17.8 1.0 %copy-start.4 = (bf16[768,256]{1,0:T(8,128)(2,1)S(1)}, bf16[768,256]{1,0:T(8,128)(2,1)}, u32[]{:S(2)}) copy-start(bf16[768,256]{1,0:T(8,128)(2,1)} %refs_0_.1) | copy-start | bytes 1179652
  18.8 0.9 %copy-start.5 = (bf16[512,256]{1,0:T(8,128)(2,1)S(1)}, bf16[512,256]{1,0:T(8,128)(2,1)}, u32[]{:S(2)}) copy-start(bf16[512,256]{1,0:T(8,128)(2,1)} %refs_5_.1) | copy-start | bytes 786436
  19.7 0.9 copy-start.6
  20.7 0.9 copy-start.7
  21.6 0.9 copy-start.8
  22.5 0.7 copy-start.9
  23.2 0.7 copy-start.10
  29.3 4.9 %collective-permute-start.10 = (bf16[384,256]{1,0:T(8,128)(2,1)S(1)}, bf16[384,256]{1,0:T(8,128)(2,1)S(1)}, u32[]{:S(2)}, u32[]{:S(2)}) collective-permute-start(bf16[384,256]{1,0:T(8,128)(2,1)S(1)} %get-tuple-element.87), channel_id=1, source_target_pairs={{0,1},{1,0},{2,3},{3,2},{4,5},{5,4},{6,7},{7,6},{8,9},{9,8},{10,11... | collective-permute-start | bytes 589832 | tf_op jit(solution)/shard_map/ppermute | solution.py:25
  33.7 5.2 %collective-permute-start.8 = (bf16[528,256]{1,0:T(8,128)(2,1)}, bf16[528,256]{1,0:T(8,128)(2,1)S(1)}, u32[]{:S(2)}, u32[]{:S(2)}) collective-permute-start(bf16[528,256]{1,0:T(8,128)(2,1)} %get-tuple-element.81), channel_id=1, source_target_pairs={{0,1},{1,0},{2,3},{3,2},{4,5},{5,4},{6,7},{7,6},{8,9},{9,8},{10,11... | collective-permute-start | bytes 811016 | tf_op jit(solution)/shard_map/ppermute | solution.py:25
  34.9 12.5 %all-to-all-start.2 = ((bf16[8,48,256]{2,1,0:T(8,128)(2,1)}), bf16[8,48,256]{2,1,0:T(8,128)(2,1)}, u32[]{:S(2)}, u32[]{:S(2)}) async-start(bf16[8,48,256]{2,1,0:T(8,128)(2,1)} %bitcast.2), calls=%async_computation.2 | async-start | bytes 393216 | tf_op jit(solution)/shard_map/all_to_all | solution.py:631
  47.3 13.2 %all-to-all-start = ((bf16[8,80,256]{2,1,0:T(8,128)(2,1)}), bf16[8,80,256]{2,1,0:T(8,128)(2,1)S(1)}, u32[]{:S(2)}, u32[]{:S(2)}) async-start(bf16[8,80,256]{2,1,0:T(8,128)(2,1)} %pad_maximum_fusion), calls=%async_computation | async-start | bytes 655360 | tf_op jit(solution)/shard_map/all_to_all | solution.py:629
  50.8 26.0 %collective-permute-start.4 = (bf16[96,256]{1,0:T(8,128)(2,1)S(1)}, bf16[96,256]{1,0:T(8,128)(2,1)S(1)}, u32[]{:S(2)}, u32[]{:S(2)}) collective-permute-start(bf16[96,256]{1,0:T(8,128)(2,1)S(1)} %get-tuple-element.75), channel_id=1, source_target_pairs={{0,1},{1,2},{2,3},{3,0},{4,5},{5,6},{6,7},{7,4},{8,9},{9,10},{10,1... | collective-permute-start | bytes 147464 | tf_op jit(solution)/shard_map/ppermute | solution.py:21
  50.8 26.0 %collective-permute-start.5 = (bf16[96,256]{1,0:T(8,128)(2,1)S(1)}, bf16[96,256]{1,0:T(8,128)(2,1)S(1)}, u32[]{:S(2)}, u32[]{:S(2)}) collective-permute-start(bf16[96,256]{1,0:T(8,128)(2,1)S(1)} %get-tuple-element.76), channel_id=1, source_target_pairs={{0,3},{1,0},{2,1},{3,2},{4,7},{5,4},{6,5},{7,6},{8,11},{9,8},{10,9... | collective-permute-start | bytes 147464 | tf_op jit(solution)/shard_map/ppermute | solution.py:21
  61.2 11.4 %all-to-all-start.3 = ((bf16[8,48,256]{2,1,0:T(8,128)(2,1)}), bf16[8,48,256]{2,1,0:T(8,128)(2,1)S(1)}, u32[]{:S(2)}, u32[]{:S(2)}) async-start(bf16[8,48,256]{2,1,0:T(8,128)(2,1)} %broadcast_in_dim.8), calls=%async_computation.3 | async-start | bytes 393216 | tf_op jit(solution)/shard_map/all_to_all | solution.py:444
  64.9 14.5 %copy-start.11 = (f32[80,256]{1,0:T(8,128)}, f32[80,256]{1,0:T(8,128)S(1)}, u32[]{:S(2)}) copy-start(f32[80,256]{1,0:T(8,128)S(1)} %convert_reduce_fusion) | copy-start | bytes 245764
  73.3 12.0 %all-to-all-start.1 = ((bf16[8,64,256]{2,1,0:T(8,128)(2,1)}), bf16[8,64,256]{2,1,0:T(8,128)(2,1)S(1)}, u32[]{:S(2)}, u32[]{:S(2)}) async-start(bf16[8,64,256]{2,1,0:T(8,128)(2,1)} %broadcast_in_dim.7), calls=%async_computation.1 | async-start | bytes 524288 | tf_op jit(solution)/shard_map/all_to_all | solution.py:444
  77.4 9.8 %collective-permute-start.6 = (bf16[96,256]{1,0:T(8,128)(2,1)}, bf16[96,256]{1,0:T(8,128)(2,1)S(1)}, u32[]{:S(2)}, u32[]{:S(2)}) collective-permute-start(bf16[96,256]{1,0:T(8,128)(2,1)} %pad_maximum_fusion.3), channel_id=1, source_target_pairs={{0,4},{4,8},{8,12},{12,0},{1,5},{5,9},{9,13},{13,1},{2,6},{6,10},{... | collective-permute-start | bytes 147464 | tf_op jit(solution)/shard_map/ppermute | solution.py:21
  79.3 12.6 %collective-permute-start.11 = (bf16[384,256]{1,0:T(8,128)(2,1)S(1)}, bf16[384,256]{1,0:T(8,128)(2,1)S(1)}, u32[]{:S(2)}, u32[]{:S(2)}) collective-permute-start(bf16[384,256]{1,0:T(8,128)(2,1)S(1)} %bitcast.6), channel_id=1, source_target_pairs={{0,1},{1,0},{2,3},{3,2},{4,5},{5,4},{6,7},{7,6},{8,9},{9,8},{10,11... | collective-permute-start | bytes 589832 | tf_op jit(solution)/shard_map/ppermute | solution.py:25
  85.3 7.4 %collective-permute-start.9 = (bf16[512,256]{1,0:T(8,128)(2,1)S(1)}, bf16[512,256]{1,0:T(8,128)(2,1)S(1)}, u32[]{:S(2)}, u32[]{:S(2)}) collective-permute-start(bf16[512,256]{1,0:T(8,128)(2,1)S(1)} %bitcast.4), channel_id=1, source_target_pairs={{0,1},{1,0},{2,3},{3,2},{4,5},{5,4},{6,7},{7,6},{8,9},{9,8},{10,11... | collective-permute-start | bytes 786440 | tf_op jit(solution)/shard_map/ppermute | solution.py:25
  85.3 4.2 %collective-permute-start.7 = (bf16[96,256]{1,0:T(8,128)(2,1)S(1)}, bf16[96,256]{1,0:T(8,128)(2,1)S(1)}, u32[]{:S(2)}, u32[]{:S(2)}) collective-permute-start(bf16[96,256]{1,0:T(8,128)(2,1)S(1)} %pad_maximum_fusion.4), channel_id=1, source_target_pairs={{0,12},{4,0},{8,4},{12,8},{1,13},{5,1},{9,5},{13,9},{2,14},{6,2},{... | collective-permute-start | bytes 147464 | tf_op jit(solution)/shard_map/ppermute | solution.py:21

commit v4 on v3

--- a/solution.py
+++ b/solution.py
@@ -1,3 +1,5 @@
+import functools
+
 import jax
 import jax.numpy as jnp
 from jax import lax
@@ -155,12 +157,12 @@
         copy.wait()
 
 
-def split_by_core(sums, keep_out, away_out):
-    half = keep_out.shape[0]
+def split_by_core(sums, first, keep_out, away_out):
+    half = sums.shape[0] // 2
     core = lax.axis_index(CORE)
-    keep_out[...] = sums[pl.ds(pl.multiple_of(core * half, half), half), :]
+    keep_out[first : first + half] = sums[pl.ds(pl.multiple_of(core * half, half), half), :]
     away = sums[pl.ds(pl.multiple_of((1 - core) * half, half), half), :]
-    away_out[:half] = away.astype(BF16)
+    away_out[first : first + half] = away.astype(BF16)
 
 
 def pack_gains(edge_gain, node_gain):
@@ -174,10 +176,12 @@
     return packed.astype(BF16)
 
 
-def forward_kernel(
+def layer_kernel(
     count_ref,
     nodes,
     node_grads,
+    edges,
+    edge_grads,
     senders,
     receivers,
     pre_local,
@@ -191,16 +195,21 @@
     w_node_in,
     w_node_out,
     gain_node,
-    halo_out,
-    pre_out,
-    normed_out,
-    scale_out,
-    agg_grad_out,
+    pre_grad_out,
+    sender_out,
+    receiver_out,
     node_part_out,
+    up_out,
+    down_out,
+    rest_out,
     keep_out,
     away_out,
-    node_gain_out,
+    gains_out,
+    pre_kept,
+    normed_kept,
+    scale_kept,
     node_sums,
+    edge_sums,
 ):
     count, width = nodes.shape
     tile_rows = senders.shape[1]
@@ -218,7 +227,6 @@
         ],
         axis=0,
     )
-    halo_out[...] = halo
     table = dot(halo, w_in[width : 2 * width]).astype(BF16)
     by_sender = columns_of(senders[...])
     receiver_ids = receivers[...]
@@ -227,11 +235,11 @@
     for tiles in chunks_of(senders.shape[0]):
         rows = pl.ds(tiles[0] * tile_rows, len(tiles) * tile_rows)
         value = pre_local[rows, :] + dot(hot_rows(by_sender, tiles, count, halo.shape[0]), table)
-        pre_out[rows, :] = value
+        pre_kept[rows, :] = value
         hidden = (value * sigmoid(value)).astype(BF16)
         normed, scale_inv = normalize(dot(hidden, w_out[...]))
-        normed_out[rows, :] = normed
-        scale_out[rows, :] = jnp.broadcast_to(scale_inv, (len(tiles) * tile_rows, 128))
+        normed_kept[rows, :] = normed
+        scale_kept[rows, :] = jnp.broadcast_to(scale_inv, (len(tiles) * tile_rows, 128))
         live = live_rows(count_ref, tiles[0], len(tiles), tile_rows)
         message = (live * gain * normed).astype(BF16)
         total = total + dot(hot_columns(receiver_ids, tiles, 0, count), message)
@@ -247,51 +255,14 @@
     out_grad = norm_back(normed, scale_inv, gain_node[...].astype(F32), upstream).astype(BF16)
     slope = sigma * (1.0 + node_pre * (1.0 - sigma))
     pre_grad = (dot_nt(out_grad, w_node_out[...]) * slope).astype(BF16)
-    agg_grad_out[...] = dot_nt(pre_grad, w_second).astype(BF16)
+    agg_grad = dot_nt(pre_grad, w_second).astype(BF16)
     node_part_out[...] = upstream + dot_nt(pre_grad, w_first)
     node_sums[:width] = dot_tn(x, pre_grad)
     node_sums[width : 2 * width] = dot_tn(aggregated, pre_grad)
     node_sums[2 * width : 3 * width] = dot_tn(node_hidden, out_grad)
-    split_by_core(node_sums, keep_out, away_out)
-    node_gain_out[...] = jnp.broadcast_to(
-        jnp.sum(upstream * normed, axis=0, keepdims=True), (8, width)
-    )
-
-
-def backward_kernel(
-    count_ref,
-    nodes,
-    halo,
-    edges,
-    edge_grads,
-    senders,
-    receivers,
-    pre,
-    normed,
-    scale,
-    agg_grad,
-    w_in,
-    w_out,
-    gain_edge,
-    node_gain,
-    pre_grad_out,
-    sender_out,
-    receiver_out,
-    up_out,
-    down_out,
-    rest_out,
-    keep_out,
-    away_out,
-    gains_out,
-    edge_sums,
-):
-    count, width = nodes.shape
-    tile_rows = senders.shape[1]
-    slots = up_out.shape[0] // 3
+    node_gain = jnp.sum(upstream * normed, axis=0, keepdims=True)
     by_receiver = columns_of(receivers[...])
     sender_ids = senders[...]
-    receiver_ids = receivers[...]
-    gain = gain_edge[...].astype(F32)
     extended = count + halo.shape[0]
     sender_total = jnp.zeros((extended, width), F32)
     receiver_total = jnp.zeros((count, width), F32)
@@ -303,12 +274,12 @@
         live = live_rows(count_ref, tiles[0], len(tiles), tile_rows)
         upstream = live * (
             edge_grads[rows, :].astype(F32)
-            + dot(hot_rows(by_receiver, tiles, 0, count), agg_grad[...])
+            + dot(hot_rows(by_receiver, tiles, 0, count), agg_grad)
         )
-        chunk_normed = normed[rows, :]
+        chunk_normed = normed_kept[rows, :]
         gain_total = gain_total + jnp.sum(upstream * chunk_normed, axis=0, keepdims=True)
-        out_grad = norm_back(chunk_normed, scale[rows, :1], gain, upstream).astype(BF16)
-        value = pre[rows, :]
+        out_grad = norm_back(chunk_normed, scale_kept[rows, :1], gain, upstream).astype(BF16)
+        value = pre_kept[rows, :]
         sigma = sigmoid(value)
         hidden = (value * sigma).astype(BF16)
         slope = sigma * (1.0 + value * (1.0 - sigma))
@@ -330,51 +301,79 @@
     up_out[...] = jnp.concatenate([parts[0], parts[3], parts[5]], axis=0)
     down_out[...] = jnp.concatenate([parts[2], parts[4], parts[7]], axis=0)
     rest_out[...] = jnp.concatenate([parts[1], parts[6]], axis=0)
-    x = nodes[...]
     edge_sums[:width] = first
-    edge_sums[width : 2 * width] = dot_tn(x, own) + dot_tn(halo[...], away)
+    edge_sums[width : 2 * width] = dot_tn(x, own) + dot_tn(halo, away)
     edge_sums[2 * width : 3 * width] = dot_tn(x, received)
     edge_sums[3 * width : 4 * width] = second
-    split_by_core(edge_sums, keep_out, away_out)
-    gains = pack_gains(gain_total, node_gain[:1])
+    split_by_core(edge_sums, 0, keep_out, away_out)
+    split_by_core(node_sums, edge_sums.shape[0] // 2, keep_out, away_out)
+    gains = pack_gains(gain_total, node_gain)
     away_out[keep_out.shape[0] :] = gains
     gains_out[...] = gains
 
 
-def edge_pair_kernel(keep, gains, other, rows_out, gains_out):
-    half = keep.shape[0]
-    rows_out[...] = (keep[...] + other[:half].astype(F32)).astype(BF16)
-    both = gains[...].astype(F32) + other[half:].astype(F32)
-    gains_out[...] = pack_gains(both[0:1] + both[1:2], both[2:3] + both[3:4])
-
-
-def node_pair_kernel(keep, other, rows_out):
-    rows_out[...] = (keep[...] + other[...].astype(F32)).astype(BF16)
-
-
-def place_kernel(own, other, first, second, sems):
-    half = own.shape[0]
-    rest = first.shape[0] - half
+def pair_kernel(parts, keep, gains, other, blocks_out, total, staged, sems):
+    rows = keep.shape[0]
+    chips = blocks_out.shape[0]
+    packed = gains.shape[0]
+    both = gains[...].astype(F32) + other[rows:].astype(F32)
+    summed = pack_gains(both[0:1] + both[1:2], both[2:3] + both[3:4])
+    total[...] = (keep[...] + other[:rows].astype(F32)).astype(BF16)
+    copies = []
+    for chip in range(chips):
+        staged[chip, :packed, :] = summed
+        first, at = 0, packed
+        for part in parts:
+            step = part // chips
+            staged[chip, at : at + step, :] = total[first + chip * step : first + (chip + 1) * step]
+            first, at = first + part, at + step
+        copies.append(
+            pltpu.make_async_copy(staged.at[chip], blocks_out.at[chip], sems.at[chip])
+        )
+        copies[-1].start()
+    for copy in copies:
+        copy.wait()
+
+
+def place_kernel(parts, own, other, *refs):
+    outs, sems = refs[:-1], refs[-1]
+    chips = own.shape[0]
     core = lax.axis_index(CORE)
 
-    def place(low, high):
-        copies = [
-            pltpu.make_async_copy(low, first.at[:half], sems.at[0]),
-            pltpu.make_async_copy(high.at[:rest], first.at[half:], sems.at[1]),
-            pltpu.make_async_copy(high.at[rest:], second, sems.at[2]),
-        ]
-        for copy in copies:
-            copy.start()
+    def place(halves):
+        copies = []
+
+        def put(source, target):
+            copies.append(pltpu.make_async_copy(source, target, sems.at[len(copies)]))
+            copies[-1].start()
+
+        for half, blocks in enumerate(halves):
+            for chip in range(chips):
+                at = 0
+                for i, part in enumerate(parts):
+                    step = part // chips
+                    row = half * part + chip * step
+                    cut = outs[2 * i].shape[0]
+                    split = min(max(cut - row, 0), step)
+                    if split > 0:
+                        put(blocks.at[chip, at : at + split], outs[2 * i].at[row : row + split])
+                    if split < step:
+                        rest = row + split - cut
+                        put(
+                            blocks.at[chip, at + split : at + step],
+                            outs[2 * i + 1].at[rest : rest + step - split],
+                        )
+                    at += step
         for copy in copies:
             copy.wait()
 
     @pl.when(core == 0)
     def _():
-        place(own, other)
+        place([own, other])
 
     @pl.when(core == 1)
     def _():
-        place(other, own)
+        place([other, own])
 
 
 def finish_kernel(
@@ -423,6 +422,10 @@
     moved = sum(x.size * x.dtype.itemsize for x in operands)
     moved += sum(x.size * jnp.dtype(x.dtype).itemsize for x in outs)
     spaces = list(spaces) + [VMEM] * (len(operands) - len(spaces))
+    operands = [
+        pltpu.with_memory_space_constraint(x, HBM) if space is HBM else x
+        for x, space in zip(operands, spaces)
+    ]
     return pl.pallas_call(
         body,
         out_shape=outs,
@@ -438,27 +441,82 @@
     return jax.ShapeDtypeStruct(array.shape, array.dtype)
 
 
-def spread(rows):
-    chips = lax.axis_size(CHIPS)
-    copies = jnp.broadcast_to(rows[None], (chips,) + rows.shape)
-    return lax.all_to_all(copies, CHIPS, 0, 0).reshape(chips * rows.shape[0], rows.shape[1])
-
-
 def shaped(rows, columns, dtype):
     return jax.ShapeDtypeStruct((rows, columns), dtype)
 
 
-def placed(own, first_rows, second_rows):
-    width = own.shape[1]
-    return call(
-        place_kernel,
-        [shaped(first_rows, width, BF16), shaped(second_rows, width, BF16)],
-        0,
-        own,
-        across_cores(own),
-        out_space=HBM,
-        scratch=[pltpu.SemaphoreType.DMA((3,))],
-    )
+def placed(parts, own, other, width):
+    chips = own.shape[0]
+    outs = [
+        shaped(3 * width, width, BF16),
+        shaped(width, width, BF16),
+        shaped(2 * width, width, BF16),
+        shaped(width, width, BF16),
+    ]
+    steps = [part // chips for part in parts]
+    cuts = [x.shape[0] for x in outs[::2]]
+    if all(x % 16 == 0 for x in steps + cuts):
+        return call(
+            functools.partial(place_kernel, parts),
+            outs,
+            0,
+            own,
+            other,
+            out_space=HBM,
+            scratch=[pltpu.SemaphoreType.DMA((2 * len(parts) * chips + len(parts),))],
+        )
+    core = lax.axis_index(CORE)
+    low = jnp.where(core == 0, own, other)
+    high = jnp.where(core == 0, other, own)
+    results = []
+    at = 0
+    for step, cut in zip(steps, cuts):
+        whole = jnp.concatenate(
+            [x[:, at : at + step].reshape(chips * step, width) for x in (low, high)]
+        )
+        results += [whole[:cut], whole[cut:]]
+        at += step
+    return results
+
+
+def blocks_of(parts, keep, gains, other):
+    chips = lax.axis_size(CHIPS)
+    rows, width = keep.shape
+    packed = gains.shape[0]
+    steps = [part // chips for part in parts]
+    shape = (chips, packed + sum(steps), width)
+    body = functools.partial(pair_kernel, parts)
+    if all(x % 16 == 0 for x in steps):
+        (blocks,) = call(
+            body,
+            [jax.ShapeDtypeStruct(shape, BF16)],
+            0,
+            keep,
+            gains,
+            other,
+            out_space=HBM,
+            scratch=[
+                pltpu.VMEM((rows, width), BF16),
+                pltpu.VMEM(shape, BF16),
+                pltpu.SemaphoreType.DMA((chips,)),
+            ],
+        )
+        return blocks
+    both = gains.astype(F32) + other[rows:].astype(F32)
+    summed = jnp.where(
+        jnp.arange(packed)[:, None] % 2 == 0,
+        both + jnp.roll(both, -1, axis=0),
+        0.0,
+    )
+    high = summed.astype(BF16).astype(F32)
+    summed = (high + jnp.roll(summed - high, 1, axis=0)).astype(BF16)
+    total = (keep + other[:rows].astype(F32)).astype(BF16)
+    pieces = [jnp.broadcast_to(summed[None], (chips, packed, width))]
+    first = 0
+    for part, step in zip(parts, steps):
+        pieces.append(total[first : first + part].reshape(chips, step, width))
+        first += part
+    return jnp.concatenate(pieces, axis=1)
 
 
 def on_device(
@@ -539,23 +597,29 @@
         node_grads,
         edge_grads,
     ) = fetched
-    halo, pre, normed, scale, agg_grad, node_part, node_keep, node_away, node_gain = call(
-        forward_kernel,
+    parts = (2 * width, 3 * width // 2)
+    halves = sum(parts)
+    pre_grad, sender_sum, receiver_sum, node_part, up, down, rest, keep, away, gains = call(
+        layer_kernel,
         [
-            shaped(halo_rows, width, BF16),
-            shaped(edge_rows, width, F32),
-            shaped(edge_rows, width, F32),
-            shaped(edge_rows, 128, F32),
+            shaped(edge_rows, width, BF16),
+            shaped(count, width, BF16),
             shaped(count, width, BF16),
             shaped(count, width, F32),
-            shaped(3 * width // 2, width, F32),
-            shaped(3 * width // 2, width, BF16),
-            shaped(8, width, F32),
+            shaped(3 * slots, width, BF16),
+            shaped(3 * slots, width, BF16),
+            shaped(2 * slots, width, BF16),
+            shaped(halves, width, F32),
+            shaped(halves + 16, width, BF16),
+            shaped(16, width, BF16),
         ],
-        square * (2 * edge_rows + 9 * count) + 2 * edge_rows * count * width,
+        square * (6 * edge_rows + 11 * count + 2 * halo_rows)
+        + 2 * edge_rows * (4 * count + halo_rows) * width,
         tile_count,
         nodes,
         node_grads,
+        edges,
+        edge_grads,
         senders,
         receivers,
         pre_local,
@@ -570,69 +634,21 @@
         w_node_out,
         gain_node,
         spaces=[SMEM],
-        scratch=[pltpu.VMEM((3 * width, width), F32)],
-    )
-    node_other = across_cores(node_away)
-    pre_grad, sender_sum, receiver_sum, up, down, rest, edge_keep, edge_away, gains = call(
-        backward_kernel,
-        [
-            shaped(edge_rows, width, BF16),
-            shaped(count, width, BF16),
-            shaped(count, width, BF16),
-            shaped(3 * slots, width, BF16),
-            shaped(3 * slots, width, BF16),
-            shaped(2 * slots, width, BF16),
-            shaped(2 * width, width, F32),
-            shaped(2 * width + 16, width, BF16),
-            shaped(16, width, BF16),
+        scratch=[
+            pltpu.VMEM((edge_rows, width), F32),
+            pltpu.VMEM((edge_rows, width), F32),
+            pltpu.VMEM((edge_rows, 128), F32),
+            pltpu.VMEM((3 * width, width), F32),
+            pltpu.VMEM((4 * width, width), F32),
         ],
-        square * (4 * edge_rows + 2 * count + 2 * halo_rows)
-        + 2 * edge_rows * (3 * count + halo_rows) * width,
-        tile_count,
-        nodes,
-        halo,
-        edges,
-        edge_grads,
-        senders,
-        receivers,
-        pre,
-        normed,
-        scale,
-        agg_grad,
-        w_edge_in,
-        w_edge_out,
-        gain_edge,
-        node_gain,
-        spaces=[SMEM],
-        scratch=[pltpu.VMEM((4 * width, width), F32)],
-    )
-    edge_other = across_cores(edge_away)
-    (node_pair,) = call(
-        node_pair_kernel, [shaped(3 * width // 2, width, BF16)], 0, node_keep, node_other
-    )
-    edge_pair, gains = call(
-        edge_pair_kernel,
-        [shaped(2 * width, width, BF16), like(gains)],
-        0,
-        edge_keep,
-        gains,
-        edge_other,
-    )
-    chips = lax.axis_size(CHIPS)
-    blocks = jnp.concatenate(
-        [
-            edge_pair.reshape(chips, -1, width),
-            jnp.broadcast_to(gains[None], (chips,) + gains.shape),
-        ],
-        axis=1,
-    )
-    edge_part = jnp.sum(lax.all_to_all(blocks, CHIPS, 0, 0).astype(F32), axis=0)
-    node_part_sum = jnp.sum(
-        lax.all_to_all(node_pair.reshape(chips, -1, width), CHIPS, 0, 0).astype(F32), axis=0
-    )
-    gains = edge_part[2 * width // chips :]
-    edge_half = spread(edge_part[: 2 * width // chips].astype(BF16))
-    node_half = spread(node_part_sum.astype(BF16))
+    )
+    blocks = blocks_of(parts, keep, gains, across_cores(away))
+    received = lax.all_to_all(blocks, CHIPS, 0, 0)
+    sums = jnp.sum(received.astype(F32), axis=0)
+    gains = sums[:16]
+    mine = sums[16:].astype(BF16)
+    spread = jnp.broadcast_to(mine[None], (blocks.shape[0],) + mine.shape)
+    own = lax.all_to_all(spread, CHIPS, 0, 0)
     up_back = passed_along(up, PY, 1)
     down_back = passed_along(down, PY, -1)
     to_high = passed_along(
@@ -663,8 +679,10 @@
         to_high,
         to_low,
     )
-    w_edge_in_grad, w_edge_out_grad = placed(edge_half, 3 * width, width)
-    w_node_in_grad, w_node_out_grad = placed(node_half, 2 * width, width)
+    own, nodes_grad, edges_grad = lax.optimization_barrier((own, nodes_grad, edges_grad))
+    w_edge_in_grad, w_edge_out_grad, w_node_in_grad, w_node_out_grad = placed(
+        parts, own, across_cores(own), width
+    )
     return (
         nodes_grad,
         edges_grad,

time: 94.5 us -> 68.9 us (0.73)
  local copies, waits for them, and re-layouts: 12.6 us -> 2.8 us
  waiting for transfers between devices: 34.4 us -> 27 us
  starting transfers between devices: 26.3 us -> 21.4 us
  other arithmetic: 3.77 us -> 1.47 us
    all_to_all x4 -> x2, waiting for transfers between devices: 28.2 us -> 15.5 us  [the longest x1 14.8 us: on_device(): received = lax.all_to_all(blocks, CHIPS, 0, 0)]
    unnamed x24 -> x2, local copies, waits for them, and re-layouts: 9.81 us -> 0.65 us
    all_to_all x4 -> x2, starting transfers between devices: 14.5 us -> 7.12 us  [the longest x1 3.62 us: on_device(): own = lax.all_to_all(spread, CHIPS, 0, 0)]
    ppermute x8, waiting for transfers between devices: 6.12 us -> 9.61 us  [passed_along(): lax.ppermute(array, axis, [(i, (i + by) % size) for i in range(size)])]
    ppermute x8, starting transfers between devices: 11.2 us -> 13.3 us  [passed_along(): lax.ppermute(array, axis, [(i, (i + by) % size) for i in range(size)])]
    ppermute x4 -> x2, waiting for transfers between devices: 0.01 us -> 1.89 us  [across_cores(): return lax.ppermute(array, CORE, [(0, 1), (1, 0)])]
    pallas_call x10 -> x7, Pallas kernels: 15.1 us -> 14.4 us  [call(): pl.pallas_call(body, out_shape=outs, in_specs=[pl.BlockSpec(memory_space=...]
  transfers between devices with their start and end apart: 16 -> 12, of which waited for: 6 -> 7; matrix products, arithmetic and copies ran while one was open for 7% -> 5% of each run, Pallas kernels for 11% -> 7%
where the time goes in v4:
time: 68.9 us; the launch traced here: 68.5 us
  waiting for transfers between devices  27 us (39%)
  starting transfers between devices  21.4 us (31%)
  Pallas kernels  14.4 us (21%)
  local copies, waits for them, and re-layouts  2.8 us (4%)
  other arithmetic  1.47 us (2%)
  between operations  1.39 us (2%)
    all_to_all x1, waiting for transfers between devices, on_device(): received = lax.all_to_all(blocks, CHIPS, 0, 0)  14.8 us
    pallas_call x7, Pallas kernels, call(): pl.pallas_call(body, out_shape=outs, in_specs=[pl.BlockSpec(memory_space=...  14.4 us
    ppermute x8, starting transfers between devices, passed_along(): lax.ppermute(array, axis, [(i, (i + by) % size) for i in range(size)])  13.3 us
    ppermute x8, waiting for transfers between devices, passed_along(): lax.ppermute(array, axis, [(i, (i + by) % size) for i in range(size)])  9.61 us
    all_to_all x1, starting transfers between devices, on_device(): own = lax.all_to_all(spread, CHIPS, 0, 0)  3.62 us
    all_to_all x1, starting transfers between devices, on_device(): received = lax.all_to_all(blocks, CHIPS, 0, 0)  3.51 us
    ppermute x2, waiting for transfers between devices, across_cores(): return lax.ppermute(array, CORE, [(0, 1), (1, 0)])  1.89 us
  transfers between devices with their start and end apart: 12, of which 7 were waited for; matrix products, arithmetic and copies ran while one was open for 5% of the time, Pallas kernels for 7%

profile of v4, /device:TPU:0, one launch (start us, length us, event | category | flops | bytes accessed | tf_op | source)
XLA Modules:
  0.0 68.5 jit_solution(8969850763382201944)
XLA Ops:
  0.6 1.3 %shard_map.197 = (bf16[96,256]{1,0:T(8,128)(2,1)S(1)}, bf16[64,256]{1,0:T(8,128)(2,1)S(1)}, bf16[96,256]{1,0:T(8,128)(2,1)S(1)}, bf16[384,256]{1,0:T(8,128)(2,1)S(1)}, s32[8,32]{1,0:T(8,128)S(1)}) custom-call(bf16[384,256]{1,0:T(8,128)(2,1)} %nodes_hbm.1, s32[8,32]{1,0:T(8,128)} %list_hbm.1), custom_call_target="tpu_custom_call" | custom-call | flops 50331648 | bytes 526336 | tf_op jit(solution)/shard_map/pallas_call | solution.py:429
  1.9 5.1 %collective-permute-start = (bf16[96,256]{1,0:T(8,128)(2,1)S(1)}, bf16[96,256]{1,0:T(8,128)(2,1)S(1)}, u32[]{:S(2)}, u32[]{:S(2)}) collective-permute-start(bf16[96,256]{1,0:T(8,128)(2,1)S(1)} %get-tuple-element.49), channel_id=1, source_target_pairs={{0,12},{4,0},{8,4},{12,8},{1,13},{5,1},{9,5},{13,9},{2,14},{6,2},{... | collective-permute-start | bytes 147464 | tf_op jit(solution)/shard_map/ppermute | solution.py:23
  7.0 0.0 collective-permute-start.1
  7.7 0.7 reshape.27.gain_edge
  8.4 0.7 reshape.28.gain_node
  9.0 0.0 collective-permute-done.from_high
  9.0 3.9 %collective-permute-done.1.from_low = bf16[96,256]{1,0:T(8,128)(2,1)S(1)} collective-permute-done((bf16[96,256]{1,0:T(8,128)(2,1)S(1)}, bf16[96,256]{1,0:T(8,128)(2,1)S(1)}, u32[]{:S(2)}, u32[]{:S(2)}) %collective-permute-start.1) | collective-permute-done | bytes 49184 | tf_op jit(solution)/shard_map/ppermute | solution.py:23
  12.9 0.1 collective-permute-start.2
  13.0 1.7 %collective-permute-start.3 = (bf16[96,256]{1,0:T(8,128)(2,1)S(1)}, bf16[96,256]{1,0:T(8,128)(2,1)S(1)}, u32[]{:S(2)}, u32[]{:S(2)}) collective-permute-start(bf16[96,256]{1,0:T(8,128)(2,1)S(1)} %pad_maximum_fusion.1), channel_id=1, source_target_pairs={{0,3},{1,0},{2,1},{3,2},{4,7},{5,4},{6,5},{7,6},{8,11},{9,8},{10,9... | collective-permute-start | bytes 147464 | tf_op jit(solution)/shard_map/ppermute | solution.py:23
  14.8 2.5 %shard_map.198 = (f32[1152,256]{1,0:T(8,128)S(1)}, bf16[768,256]{1,0:T(8,128)(2,1)S(1)}, s32[9,128]{1,0:T(8,128)S(1)}, s32[9,128]{1,0:T(8,128)S(1)}, bf16[1152,2...) custom-call(bf16[384,256]{1,0:T(8,128)(2,1)S(1)} %get-tuple-element., ...), custom_call_target="tpu_custom_call" | custom-call | flops 704643072 | bytes 5982208 | tf_op jit(solution)/shard_map/pallas_call | solution.py:429
  17.2 0.0 collective-permute-done.2.upward
  17.2 0.0 collective-permute-done.3.downward
  17.2 6.1 %shard_map.199 = (bf16[1152,256]{1,0:T(8,128)(2,1)S(1)}, bf16[384,256]{1,0:T(8,128)(2,1)S(1)}, bf16[384,256]{1,0:T(8,128)(2,1)S(1)}, f32[384,256]{1,0:T(8,128)S(...) custom-call(s32[1]{0:T(128)S(6)} %copy.22.count_ref, ...), custom_call_target="tpu_custom_call" | custom-call | flops 2583691264 | bytes 6776836 | tf_op jit(solution)/shard_map/pallas_call | solution.py:429
  23.4 0.9 %collective-permute-start.4 = (bf16[912,256]{1,0:T(8,128)(2,1)S(1)}, bf16[912,256]{1,0:T(8,128)(2,1)S(1)}, u32[]{:S(2)}, u32[]{:S(2)}) collective-permute-start(bf16[912,256]{1,0:T(8,128)(2,1)S(1)} %get-tuple-element.58), channel_id=1, source_target_pairs={{0,1},{1,0},{2,3},{3,2},{4,5},{5,4},{6,7},{7,6},{8,9},{9,8},{10,11... | collective-permute-start | bytes 1400840 | tf_op jit(solution)/shard_map/ppermute | solution.py:27
  24.3 1.5 %collective-permute-done.4.other = bf16[912,256]{1,0:T(8,128)(2,1)S(1)} collective-permute-done((bf16[912,256]{1,0:T(8,128)(2,1)S(1)}, bf16[912,256]{1,0:T(8,128)(2,1)S(1)}, u32[]{:S(2)}, u32[]{:S(2)}) %collective-permute-start.4) | collective-permute-done | bytes 466976 | tf_op jit(solution)/shard_map/ppermute | solution.py:27
  25.8 0.9 %shard_map.200 = bf16[8,128,256]{2,1,0:T(8,128)(2,1)} custom-call(f32[896,256]{1,0:T(8,128)S(1)} %get-tuple-element.56.keep, bf16[16,256]{1,0:T(8,128)(2,1)S(1)} %get-tuple-element.57.gains, bf16[912,256]{1,0:T(8,128)(2,1)S(1)} %collective-permute-done.4.other), custom_call_target="tpu_custom_call" | custom-call | bytes 1916928 | tf_op jit(solution)/shard_map/pallas_call | solution.py:429
  26.7 3.5 %all-to-all-start = ((bf16[8,128,256]{2,1,0:T(8,128)(2,1)}), bf16[8,128,256]{2,1,0:T(8,128)(2,1)S(1)}, u32[]{:S(2)}, u32[]{:S(2)}) async-start(bf16[8,128,256]{2,1,0:T(8,128)(2,1)} %shard_map.200), calls=%async_computation | async-start | bytes 1048576 | tf_op jit(solution)/shard_map/all_to_all | solution.py:646
  30.2 0.4 collective-permute-start.5
  30.6 14.8 %all-to-all-done = bf16[8,128,256]{2,1,0:T(8,128)(2,1)S(1)} async-done(((bf16[8,128,256]{2,1,0:T(8,128)(2,1)}), bf16[8,128,256]{2,1,0:T(8,128)(2,1)S(1)}, u32[]{:S(2)}, u32[]{:S(2)}) %all-to-all-start) | async-done | bytes 524320 | tf_op jit(solution)/shard_map/all_to_all | solution.py:646
  45.4 0.1 convert_reduce_fusion
  45.5 0.0 copy-start
  45.5 0.6 copy-done
  46.1 0.8 %broadcast_in_dim.2 = bf16[8,112,256]{2,1,0:T(8,128)(2,1)} broadcast(bf16[112,256]{1,0:T(8,128)(2,1)S(1)} %slice.104), dimensions={1,2} | broadcast | bytes 516096 | tf_op jit(solution)/shard_map/broadcast_in_dim | solution.py:650
  46.9 3.6 %all-to-all-start.1 = ((bf16[8,112,256]{2,1,0:T(8,128)(2,1)}), bf16[8,112,256]{2,1,0:T(8,128)(2,1)S(1)}, u32[]{:S(2)}, u32[]{:S(2)}) async-start(bf16[8,112,256]{2,1,0:T(8,128)(2,1)} %broadcast_in_dim.2), calls=%async_computation.1 | async-start | bytes 917504 | tf_op jit(solution)/shard_map/all_to_all | solution.py:651
  50.6 1.1 %collective-permute-start.6 = (bf16[96,256]{1,0:T(8,128)(2,1)S(1)}, bf16[96,256]{1,0:T(8,128)(2,1)S(1)}, u32[]{:S(2)}, u32[]{:S(2)}) collective-permute-start(bf16[96,256]{1,0:T(8,128)(2,1)S(1)} %get-tuple-element.66), channel_id=1, source_target_pairs={{0,3},{1,0},{2,1},{3,2},{4,7},{5,4},{6,5},{7,6},{8,11},{9,8},{10,9... | collective-permute-start | bytes 147464 | tf_op jit(solution)/shard_map/ppermute | solution.py:23
  51.7 0.0 collective-permute-done.5.up_back
  51.7 2.0 %collective-permute-done.6.down_back = bf16[96,256]{1,0:T(8,128)(2,1)S(1)} collective-permute-done((bf16[96,256]{1,0:T(8,128)(2,1)S(1)}, bf16[96,256]{1,0:T(8,128)(2,1)S(1)}, u32[]{:S(2)}, u32[]{:S(2)}) %collective-permute-start.6) | collective-permute-done | bytes 49184 | tf_op jit(solution)/shard_map/ppermute | solution.py:23
  53.7 3.3 %collective-permute-start.7 = (bf16[96,256]{1,0:T(8,128)(2,1)S(1)}, bf16[96,256]{1,0:T(8,128)(2,1)S(1)}, u32[]{:S(2)}, u32[]{:S(2)}) collective-permute-start(bf16[96,256]{1,0:T(8,128)(2,1)S(1)} %pad_maximum_fusion.2), channel_id=1, source_target_pairs={{0,4},{4,8},{8,12},{12,0},{1,5},{5,9},{9,13},{13,1},{2,6},{6,10},{... | collective-permute-start | bytes 147464 | tf_op jit(solution)/shard_map/ppermute | solution.py:23
  57.0 1.6 %collective-permute-start.8 = (bf16[96,256]{1,0:T(8,128)(2,1)S(1)}, bf16[96,256]{1,0:T(8,128)(2,1)S(1)}, u32[]{:S(2)}, u32[]{:S(2)}) collective-permute-start(bf16[96,256]{1,0:T(8,128)(2,1)S(1)} %pad_maximum_fusion.3), channel_id=1, source_target_pairs={{0,12},{4,0},{8,4},{12,8},{1,13},{5,1},{9,5},{13,9},{2,14},{6,2},{... | collective-permute-start | bytes 147464 | tf_op jit(solution)/shard_map/ppermute | solution.py:23
  58.6 1.3 %shard_map.201 = (bf16[1152,256]{1,0:T(8,128)(2,1)}, f32[384,256]{1,0:T(8,128)S(1)}) custom-call(bf16[1152,256]{1,0:T(8,128)(2,1)S(1)} %get-tuple-element.45.edge_grads, bf16[1152,256]{1,0:T(8,128)(2,1)S(1)} %get-tuple-element.60.pre_grad, bf16[384,256]{1,0:T(8,128)(2,1)S(1)} %get-tuple-element.61.sender_sum, ...), custom_call_target="tpu_custom_call" | custom-call | flops 251658240 | bytes 3342336 | tf_op jit(solution)/shard_map/pallas_call | solution.py:429
  59.9 3.7 %collective-permute-done.7.to_high = bf16[96,256]{1,0:T(8,128)(2,1)S(1)} collective-permute-done((bf16[96,256]{1,0:T(8,128)(2,1)S(1)}, bf16[96,256]{1,0:T(8,128)(2,1)S(1)}, u32[]{:S(2)}, u32[]{:S(2)}) %collective-permute-start.7) | collective-permute-done | bytes 49184 | tf_op jit(solution)/shard_map/ppermute | solution.py:23
  63.6 0.0 collective-permute-done.8.to_low
  63.6 1.1 %shard_map.202 = bf16[384,256]{1,0:T(8,128)(2,1)} custom-call(s32[8,32]{1,0:T(8,128)S(1)} %get-tuple-element.59.send_list, f32[384,256]{1,0:T(8,128)S(1)} %get-tuple-element.64.local_grad, bf16[96,256]{1,0:T(8,128)(2,1)S(1)} %collective-permute-done.5.up_back, bf16[96,256]{1,0:T(8,128)(2,1)S(1)} %collective-permute-done.6.down_back, ...), custom_call_target="tpu_custom_call" | custom-call | flops 50331648 | bytes 787456 | tf_op jit(solution)/shard_map/pallas_call | solution.py:429
  64.7 0.7 %all-to-all-done.1.own = bf16[8,112,256]{2,1,0:T(8,128)(2,1)S(1)} async-done(((bf16[8,112,256]{2,1,0:T(8,128)(2,1)}), bf16[8,112,256]{2,1,0:T(8,128)(2,1)S(1)}, u32[]{:S(2)}, u32[]{:S(2)}) %all-to-all-start.1) | async-done | bytes 458784 | tf_op jit(solution)/shard_map/all_to_all | solution.py:651
  65.4 0.0 collective-permute-start.9
  65.4 1.4 %fusion.3 = (bf16[256]{0:T(256)(128)(2,1)}, bf16[256]{0:T(256)(128)(2,1)}) fusion(f32[128,256]{1,0:T(8,128)} %copy-done), kind=kLoop, calls=%fused_computation.11 | loop fusion | flops 1024 | bytes 5120 | tf_op jit(solution)/shard_map/convert_element_type | solution.py:694
  66.8 0.4 collective-permute-done.9.other
  67.3 1.2 %shard_map.203 = (bf16[768,256]{1,0:T(8,128)(2,1)}, bf16[256,256]{1,0:T(8,128)(2,1)}, bf16[512,256]{1,0:T(8,128)(2,1)}, bf16[256,256]{1,0:T(8,128)(2,1)}) custom-call(bf16[8,112,256]{2,1,0:T(8,128)(2,1)S(1)} %all-to-all-done.1.own, bf16[8,112,256]{2,1,0:T(8,128)(2,1)S(1)} %collective-permute-done.9.other), custom_call_target="tpu_custom_call" | custom-call | bytes 1835008 | tf_op jit(solution)/shard_map/pallas_call | solution.py:429
  (11 shorter events, 0.0 us)
Async XLA Ops:
  1.9 7.1 %collective-permute-start = (bf16[96,256]{1,0:T(8,128)(2,1)S(1)}, bf16[96,256]{1,0:T(8,128)(2,1)S(1)}, u32[]{:S(2)}, u32[]{:S(2)}) collective-permute-start(bf16[96,256]{1,0:T(8,128)(2,1)S(1)} %get-tuple-element.49), channel_id=1, source_target_pairs={{0,12},{4,0},{8,4},{12,8},{1,13},{5,1},{9,5},{13,9},{2,14},{6,2},{... | collective-permute-start | bytes 147464 | tf_op jit(solution)/shard_map/ppermute | solution.py:23
  7.0 5.9 %collective-permute-start.1 = (bf16[96,256]{1,0:T(8,128)(2,1)S(1)}, bf16[96,256]{1,0:T(8,128)(2,1)S(1)}, u32[]{:S(2)}, u32[]{:S(2)}) collective-permute-start(bf16[96,256]{1,0:T(8,128)(2,1)S(1)} %get-tuple-element.50), channel_id=1, source_target_pairs={{0,4},{4,8},{8,12},{12,0},{1,5},{5,9},{9,13},{13,1},{2,6},{6,10},{... | collective-permute-start | bytes 147464 | tf_op jit(solution)/shard_map/ppermute | solution.py:23
  12.9 4.3 %collective-permute-start.2 = (bf16[96,256]{1,0:T(8,128)(2,1)S(1)}, bf16[96,256]{1,0:T(8,128)(2,1)S(1)}, u32[]{:S(2)}, u32[]{:S(2)}) collective-permute-start(bf16[96,256]{1,0:T(8,128)(2,1)S(1)} %pad_maximum_fusion), channel_id=1, source_target_pairs={{0,1},{1,2},{2,3},{3,0},{4,5},{5,6},{6,7},{7,4},{8,9},{9,10},{10,1... | collective-permute-start | bytes 147464 | tf_op jit(solution)/shard_map/ppermute | solution.py:23
  13.0 4.2 %collective-permute-start.3 = (bf16[96,256]{1,0:T(8,128)(2,1)S(1)}, bf16[96,256]{1,0:T(8,128)(2,1)S(1)}, u32[]{:S(2)}, u32[]{:S(2)}) collective-permute-start(bf16[96,256]{1,0:T(8,128)(2,1)S(1)} %pad_maximum_fusion.1), channel_id=1, source_target_pairs={{0,3},{1,0},{2,1},{3,2},{4,7},{5,4},{6,5},{7,6},{8,11},{9,8},{10,9... | collective-permute-start | bytes 147464 | tf_op jit(solution)/shard_map/ppermute | solution.py:23
  23.4 2.4 %collective-permute-start.4 = (bf16[912,256]{1,0:T(8,128)(2,1)S(1)}, bf16[912,256]{1,0:T(8,128)(2,1)S(1)}, u32[]{:S(2)}, u32[]{:S(2)}) collective-permute-start(bf16[912,256]{1,0:T(8,128)(2,1)S(1)} %get-tuple-element.58), channel_id=1, source_target_pairs={{0,1},{1,0},{2,3},{3,2},{4,5},{5,4},{6,7},{7,6},{8,9},{9,8},{10,11... | collective-permute-start | bytes 1400840 | tf_op jit(solution)/shard_map/ppermute | solution.py:27
  26.7 18.7 %all-to-all-start = ((bf16[8,128,256]{2,1,0:T(8,128)(2,1)}), bf16[8,128,256]{2,1,0:T(8,128)(2,1)S(1)}, u32[]{:S(2)}, u32[]{:S(2)}) async-start(bf16[8,128,256]{2,1,0:T(8,128)(2,1)} %shard_map.200), calls=%async_computation | async-start | bytes 1048576 | tf_op jit(solution)/shard_map/all_to_all | solution.py:646
  30.2 21.5 %collective-permute-start.5 = (bf16[96,256]{1,0:T(8,128)(2,1)S(1)}, bf16[96,256]{1,0:T(8,128)(2,1)S(1)}, u32[]{:S(2)}, u32[]{:S(2)}) collective-permute-start(bf16[96,256]{1,0:T(8,128)(2,1)S(1)} %get-tuple-element.65), channel_id=1, source_target_pairs={{0,1},{1,2},{2,3},{3,0},{4,5},{5,6},{6,7},{7,4},{8,9},{9,10},{10,1... | collective-permute-start | bytes 147464 | tf_op jit(solution)/shard_map/ppermute | solution.py:23
  45.5 0.7 copy-start
  46.9 18.5 %all-to-all-start.1 = ((bf16[8,112,256]{2,1,0:T(8,128)(2,1)}), bf16[8,112,256]{2,1,0:T(8,128)(2,1)S(1)}, u32[]{:S(2)}, u32[]{:S(2)}) async-start(bf16[8,112,256]{2,1,0:T(8,128)(2,1)} %broadcast_in_dim.2), calls=%async_computation.1 | async-start | bytes 917504 | tf_op jit(solution)/shard_map/all_to_all | solution.py:651
  50.6 3.1 %collective-permute-start.6 = (bf16[96,256]{1,0:T(8,128)(2,1)S(1)}, bf16[96,256]{1,0:T(8,128)(2,1)S(1)}, u32[]{:S(2)}, u32[]{:S(2)}) collective-permute-start(bf16[96,256]{1,0:T(8,128)(2,1)S(1)} %get-tuple-element.66), channel_id=1, source_target_pairs={{0,3},{1,0},{2,1},{3,2},{4,7},{5,4},{6,5},{7,6},{8,11},{9,8},{10,9... | collective-permute-start | bytes 147464 | tf_op jit(solution)/shard_map/ppermute | solution.py:23
  53.7 10.0 %collective-permute-start.7 = (bf16[96,256]{1,0:T(8,128)(2,1)S(1)}, bf16[96,256]{1,0:T(8,128)(2,1)S(1)}, u32[]{:S(2)}, u32[]{:S(2)}) collective-permute-start(bf16[96,256]{1,0:T(8,128)(2,1)S(1)} %pad_maximum_fusion.2), channel_id=1, source_target_pairs={{0,4},{4,8},{8,12},{12,0},{1,5},{5,9},{9,13},{13,1},{2,6},{6,10},{... | collective-permute-start | bytes 147464 | tf_op jit(solution)/shard_map/ppermute | solution.py:23
  57.0 6.6 %collective-permute-start.8 = (bf16[96,256]{1,0:T(8,128)(2,1)S(1)}, bf16[96,256]{1,0:T(8,128)(2,1)S(1)}, u32[]{:S(2)}, u32[]{:S(2)}) collective-permute-start(bf16[96,256]{1,0:T(8,128)(2,1)S(1)} %pad_maximum_fusion.3), channel_id=1, source_target_pairs={{0,12},{4,0},{8,4},{12,8},{1,13},{5,1},{9,5},{13,9},{2,14},{6,2},{... | collective-permute-start | bytes 147464 | tf_op jit(solution)/shard_map/ppermute | solution.py:23
  65.4 1.8 %collective-permute-start.9 = (bf16[8,112,256]{2,1,0:T(8,128)(2,1)S(1)}, bf16[8,112,256]{2,1,0:T(8,128)(2,1)S(1)}, u32[]{:S(2)}, u32[]{:S(2)}) collective-permute-start(bf16[8,112,256]{2,1,0:T(8,128)(2,1)S(1)} %all-to-all-done.1.own), channel_id=1, source_target_pairs={{0,1},{1,0},{2,3},{3,2},{4,5},{5,4},{6,7},{7,6},{8,9},{9,8},{10,11... | collective-permute-start | bytes 1376264 | tf_op jit(solution)/shard_map/ppermute | solution.py:27

commit v5 on v4

--- a/solution.py
+++ b/solution.py
@@ -40,7 +40,7 @@
 
 
 def sigmoid(value):
-    return 1.0 / (1.0 + jnp.exp(-value))
+    return 0.5 + 0.5 * jnp.tanh(0.5 * value)
 
 
 def normalize(value):
@@ -96,9 +96,9 @@
     return jnp.concatenate(parts, axis=0)
 
 
-def live_rows(count_ref, first_tile, tiles, tile_rows):
-    rows = lax.broadcasted_iota(jnp.int32, (tiles * tile_rows, 1), 0)
-    return jnp.where(rows < (count_ref[0] - first_tile) * tile_rows, 1.0, 0.0)
+def live_rows(count_ref, tile_rows, rows):
+    index = lax.broadcasted_iota(jnp.int32, (rows.stop - rows.start, 1), 0)
+    return jnp.where(index < count_ref[0] * tile_rows - rows.start, 1.0, 0.0)
 
 
 def chunks_of(tiles):
@@ -127,9 +127,9 @@
 
 
 def local_kernel(nodes, *refs):
-    fetched = (len(refs) - 2) // 2
-    pre, sems = refs[fetched], refs[-1]
-    targets = refs[fetched + 1 : -1]
+    fetched = (len(refs) - 3) // 2
+    pre, receiver_rows, sems = refs[fetched], refs[fetched + 1], refs[-1]
+    targets = refs[fetched + 2 : -1]
     w_in, senders, receivers, edges = targets[:4]
     copies = fetch_all(refs[:fetched], targets, sems)
     count, width = nodes.shape
@@ -149,12 +149,26 @@
     w_edge = w_in[:width]
     for tiles in chunks_of(senders.shape[0]):
         rows = pl.ds(tiles[0] * tile_rows, len(tiles) * tile_rows)
-        hot = jnp.concatenate(
-            [hot_rows(by_sender, tiles, 0, count), hot_rows(by_receiver, tiles, 0, count)], axis=1
-        )
+        by_receiver_hot = hot_rows(by_receiver, tiles, 0, count)
+        receiver_rows[rows, :] = by_receiver_hot
+        hot = jnp.concatenate([hot_rows(by_sender, tiles, 0, count), by_receiver_hot], axis=1)
         pre[rows, :] = dot(edges[rows, :], w_edge) + dot(hot, table)
     for copy in copies[4:]:
         copy.wait()
+
+
+def index_kernel(senders, receivers, halo_rows, sender_columns, receiver_columns):
+    tile_rows = senders.shape[1]
+    extended = sender_columns.shape[0]
+    count = receiver_columns.shape[0]
+    sender_ids = senders[...]
+    receiver_ids = receivers[...]
+    by_sender = columns_of(sender_ids)
+    for tile in range(senders.shape[0]):
+        rows = slice(tile * tile_rows, (tile + 1) * tile_rows)
+        halo_rows[rows, :] = hot_rows(by_sender, [tile], count, halo_rows.shape[1])
+        sender_columns[:, rows] = hot_columns(sender_ids, [tile], 0, extended)
+        receiver_columns[:, rows] = hot_columns(receiver_ids, [tile], 0, count)
 
 
 def split_by_core(sums, first, keep_out, away_out):
@@ -177,14 +191,17 @@
 
 
 def layer_kernel(
+    tile_rows,
     count_ref,
     nodes,
     node_grads,
     edges,
     edge_grads,
-    senders,
-    receivers,
     pre_local,
+    halo_rows,
+    receiver_rows,
+    sender_columns,
+    receiver_columns,
     from_high,
     from_low,
     upward,
@@ -205,14 +222,17 @@
     keep_out,
     away_out,
     gains_out,
-    pre_kept,
+    slope_kept,
+    hidden_kept,
     normed_kept,
     scale_kept,
     node_sums,
     edge_sums,
 ):
     count, width = nodes.shape
-    tile_rows = senders.shape[1]
+    edge_rows = edges.shape[0]
+    step = edge_rows // 3 if edge_rows % 48 == 0 else edge_rows
+    chunks = [slice(first, first + step) for first in range(0, edge_rows, step)]
     slots = from_high.shape[0] // 3
     halo = jnp.concatenate(
         [
@@ -228,21 +248,19 @@
         axis=0,
     )
     table = dot(halo, w_in[width : 2 * width]).astype(BF16)
-    by_sender = columns_of(senders[...])
-    receiver_ids = receivers[...]
     gain = gain_edge[...].astype(F32)
     total = jnp.zeros((count, width), F32)
-    for tiles in chunks_of(senders.shape[0]):
-        rows = pl.ds(tiles[0] * tile_rows, len(tiles) * tile_rows)
-        value = pre_local[rows, :] + dot(hot_rows(by_sender, tiles, count, halo.shape[0]), table)
-        pre_kept[rows, :] = value
-        hidden = (value * sigmoid(value)).astype(BF16)
+    for rows in chunks:
+        value = pre_local[rows, :] + dot(halo_rows[rows, :], table)
+        sigma = sigmoid(value)
+        hidden = (value * sigma).astype(BF16)
+        hidden_kept[rows, :] = hidden
+        slope_kept[rows, :] = sigma * (1.0 + value * (1.0 - sigma))
         normed, scale_inv = normalize(dot(hidden, w_out[...]))
         normed_kept[rows, :] = normed
-        scale_kept[rows, :] = jnp.broadcast_to(scale_inv, (len(tiles) * tile_rows, 128))
-        live = live_rows(count_ref, tiles[0], len(tiles), tile_rows)
-        message = (live * gain * normed).astype(BF16)
-        total = total + dot(hot_columns(receiver_ids, tiles, 0, count), message)
+        scale_kept[rows, :] = jnp.broadcast_to(scale_inv, (step, 128))
+        message = (live_rows(count_ref, tile_rows, rows) * gain * normed).astype(BF16)
+        total = total + dot(receiver_columns[:, rows], message)
     aggregated = total.astype(BF16)
     x = nodes[...]
     w_first = w_node_in[:width]
@@ -261,36 +279,25 @@
     node_sums[width : 2 * width] = dot_tn(aggregated, pre_grad)
     node_sums[2 * width : 3 * width] = dot_tn(node_hidden, out_grad)
     node_gain = jnp.sum(upstream * normed, axis=0, keepdims=True)
-    by_receiver = columns_of(receivers[...])
-    sender_ids = senders[...]
     extended = count + halo.shape[0]
     sender_total = jnp.zeros((extended, width), F32)
     receiver_total = jnp.zeros((count, width), F32)
     first = jnp.zeros((width, width), F32)
     second = jnp.zeros((width, width), F32)
     gain_total = jnp.zeros((1, width), F32)
-    for tiles in chunks_of(senders.shape[0]):
-        rows = pl.ds(tiles[0] * tile_rows, len(tiles) * tile_rows)
-        live = live_rows(count_ref, tiles[0], len(tiles), tile_rows)
-        upstream = live * (
-            edge_grads[rows, :].astype(F32)
-            + dot(hot_rows(by_receiver, tiles, 0, count), agg_grad)
+    for rows in chunks:
+        upstream = live_rows(count_ref, tile_rows, rows) * (
+            edge_grads[rows, :].astype(F32) + dot(receiver_rows[rows, :], agg_grad)
         )
         chunk_normed = normed_kept[rows, :]
         gain_total = gain_total + jnp.sum(upstream * chunk_normed, axis=0, keepdims=True)
         out_grad = norm_back(chunk_normed, scale_kept[rows, :1], gain, upstream).astype(BF16)
-        value = pre_kept[rows, :]
-        sigma = sigmoid(value)
-        hidden = (value * sigma).astype(BF16)
-        slope = sigma * (1.0 + value * (1.0 - sigma))
-        pre_grad = (dot_nt(out_grad, w_out[...]) * slope).astype(BF16)
+        pre_grad = (dot_nt(out_grad, w_out[...]) * slope_kept[rows, :]).astype(BF16)
         pre_grad_out[rows, :] = pre_grad
-        second = second + dot_tn(hidden, out_grad)
+        second = second + dot_tn(hidden_kept[rows, :], out_grad)
         first = first + dot_tn(edges[rows, :], pre_grad)
-        sender_total = sender_total + dot(hot_columns(sender_ids, tiles, 0, extended), pre_grad)
-        receiver_total = receiver_total + dot(
-            hot_columns(receiver_ids, tiles, 0, count), pre_grad
-        )
+        sender_total = sender_total + dot(sender_columns[:, rows], pre_grad)
+        receiver_total = receiver_total + dot(receiver_columns[:, rows], pre_grad)
     own = sender_total[:count].astype(BF16)
     away = sender_total[count:].astype(BF16)
     received = receiver_total.astype(BF16)
@@ -335,6 +342,22 @@
         copy.wait()
 
 
+def spread_kernel(packed, received, gains_out, spread_out, mine, sems):
+    sums = received[0].astype(F32)
+    for chip in range(1, received.shape[0]):
+        sums = sums + received[chip].astype(F32)
+    gains_out[...] = sums[:packed]
+    mine[...] = sums[packed:].astype(BF16)
+    copies = [
+        pltpu.make_async_copy(mine, spread_out.at[chip], sems.at[chip])
+        for chip in range(received.shape[0])
+    ]
+    for copy in copies:
+        copy.start()
+    for copy in copies:
+        copy.wait()
+
+
 def place_kernel(parts, own, other, *refs):
     outs, sems = refs[:-1], refs[-1]
     chips = own.shape[0]
@@ -422,6 +445,7 @@
     moved = sum(x.size * x.dtype.itemsize for x in operands)
     moved += sum(x.size * jnp.dtype(x.dtype).itemsize for x in outs)
     spaces = list(spaces) + [VMEM] * (len(operands) - len(spaces))
+    out_spaces = out_space if isinstance(out_space, list) else [out_space] * len(outs)
     operands = [
         pltpu.with_memory_space_constraint(x, HBM) if space is HBM else x
         for x, space in zip(operands, spaces)
@@ -430,7 +454,7 @@
         body,
         out_shape=outs,
         in_specs=[pl.BlockSpec(memory_space=space) for space in spaces],
-        out_specs=[pl.BlockSpec(memory_space=out_space) for _ in outs],
+        out_specs=[pl.BlockSpec(memory_space=space) for space in out_spaces],
         scratch_shapes=list(scratch),
         compiler_params=pltpu.CompilerParams(vmem_limit_bytes=VMEM_LIMIT),
         cost_estimate=pl.CostEstimate(flops=flops, bytes_accessed=moved, transcendentals=0),
@@ -479,6 +503,22 @@
     return results
 
 
+def spread_of(received, packed):
+    chips, rows, width = received.shape
+    mine = rows - packed
+    if mine % 16 == 0:
+        return call(
+            functools.partial(spread_kernel, packed),
+            [shaped(packed, width, F32), jax.ShapeDtypeStruct((chips, mine, width), BF16)],
+            0,
+            received,
+            out_space=[VMEM, HBM],
+            scratch=[pltpu.VMEM((mine, width), BF16), pltpu.SemaphoreType.DMA((chips,))],
+        )
+    sums = jnp.sum(received.astype(F32), axis=0)
+    return sums[:packed], jnp.broadcast_to(sums[packed:].astype(BF16)[None], (chips, mine, width))
+
+
 def blocks_of(parts, keep, gains, other):
     chips = lax.axis_size(CHIPS)
     rows, width = keep.shape
@@ -539,6 +579,7 @@
     slots = send_list.shape[1]
     halo_rows = 8 * slots
     edge_rows = edges.shape[0]
+    tile_rows = senders.shape[1]
     square = 2 * width * width
     gain_edge = gain_edge.reshape(1, width)
     gain_node = gain_node.reshape(1, width)
@@ -560,12 +601,6 @@
     )
     from_low = passed_along(high, "px", 1)
     from_high = passed_along(low, "px", -1)
-    upward = passed_along(
-        jnp.concatenate([from_high[2 * slots :], mid[slots:], from_low[2 * slots :]]), PY, 1
-    )
-    downward = passed_along(
-        jnp.concatenate([from_high[:slots], mid[:slots], from_low[:slots]]), PY, -1
-    )
     fetched = [
         w_edge_in,
         senders,
@@ -577,9 +612,10 @@
         node_grads,
         edge_grads,
     ]
-    pre_local, *fetched = call(
+    pre_local, receiver_rows, *fetched = call(
         local_kernel,
-        [shaped(edge_rows, width, F32)] + [like(x) for x in fetched],
+        [shaped(edge_rows, width, F32), shaped(edge_rows, count, BF16)]
+        + [like(x) for x in fetched],
         square * (2 * count + edge_rows) + 4 * edge_rows * count * width,
         nodes,
         *fetched,
@@ -597,10 +633,28 @@
         node_grads,
         edge_grads,
     ) = fetched
+    from_low, from_high, pre_local = lax.optimization_barrier((from_low, from_high, pre_local))
+    upward = passed_along(
+        jnp.concatenate([from_high[2 * slots :], mid[slots:], from_low[2 * slots :]]), PY, 1
+    )
+    downward = passed_along(
+        jnp.concatenate([from_high[:slots], mid[:slots], from_low[:slots]]), PY, -1
+    )
+    halo_hot, sender_columns, receiver_columns = call(
+        index_kernel,
+        [
+            shaped(edge_rows, halo_rows, BF16),
+            shaped(count + halo_rows, edge_rows, BF16),
+            shaped(count, edge_rows, BF16),
+        ],
+        0,
+        senders,
+        receivers,
+    )
     parts = (2 * width, 3 * width // 2)
     halves = sum(parts)
     pre_grad, sender_sum, receiver_sum, node_part, up, down, rest, keep, away, gains = call(
-        layer_kernel,
+        functools.partial(layer_kernel, tile_rows),
         [
             shaped(edge_rows, width, BF16),
             shaped(count, width, BF16),
@@ -620,9 +674,11 @@
         node_grads,
         edges,
         edge_grads,
-        senders,
-        receivers,
         pre_local,
+        halo_hot,
+        receiver_rows,
+        sender_columns,
+        receiver_columns,
         from_high,
         from_low,
         upward,
@@ -636,6 +692,7 @@
         spaces=[SMEM],
         scratch=[
             pltpu.VMEM((edge_rows, width), F32),
+            pltpu.VMEM((edge_rows, width), BF16),
             pltpu.VMEM((edge_rows, width), F32),
             pltpu.VMEM((edge_rows, 128), F32),
             pltpu.VMEM((3 * width, width), F32),
@@ -644,10 +701,7 @@
     )
     blocks = blocks_of(parts, keep, gains, across_cores(away))
     received = lax.all_to_all(blocks, CHIPS, 0, 0)
-    sums = jnp.sum(received.astype(F32), axis=0)
-    gains = sums[:16]
-    mine = sums[16:].astype(BF16)
-    spread = jnp.broadcast_to(mine[None], (blocks.shape[0],) + mine.shape)
+    gains, spread = spread_of(received, gains.shape[0])
     own = lax.all_to_all(spread, CHIPS, 0, 0)
     up_back = passed_along(up, PY, 1)
     down_back = passed_along(down, PY, -1)

time: 68.9 us -> 65.7 us (0.954)
  local copies, waits for them, and re-layouts: 2.8 us -> 0.04 us
  waiting for transfers between devices: 27 us -> 24.7 us
  Pallas kernels: 14.4 us -> 16.4 us
  other arithmetic: 1.47 us -> 0.56 us
  starting transfers between devices: 21.4 us -> 22.3 us
    ppermute x8, waiting for transfers between devices: 9.61 us -> 6.16 us  [passed_along(): lax.ppermute(array, axis, [(i, (i + by) % size) for i in range(size)])]
    pallas_call x7 -> x9, Pallas kernels: 14.4 us -> 16.4 us  [call(): pl.pallas_call(body, out_shape=outs, in_specs=[pl.BlockSpec(memory_space=...]
    all_to_all x1, starting transfers between devices: 3.51 us -> 4.59 us  [on_device(): received = lax.all_to_all(blocks, CHIPS, 0, 0)]
    ppermute x8, starting transfers between devices: 13.3 us -> 12.4 us  [passed_along(): lax.ppermute(array, axis, [(i, (i + by) % size) for i in range(size)])]
    ppermute x2, waiting for transfers between devices: 1.89 us -> 2.73 us  [across_cores(): return lax.ppermute(array, CORE, [(0, 1), (1, 0)])]
    convert_element_type x1, other arithmetic: 1.38 us -> 0.54 us  [on_device(): (gains[2] + gains[3]).astype(BF16)]
    broadcast_in_dim x1 -> x0, local copies, waits for them, and re-layouts: 0.8 us -> none  [on_device(): spread = jnp.broadcast_to(mine[None], (blocks.shape[0],) + mine.shape)]
  transfers between devices with their start and end apart: 12 -> 12, of which waited for: 7 -> 6; matrix products, arithmetic and copies ran while one was open for 5% -> 1% of each run, Pallas kernels for 7% -> 11%
where the time goes in v5:
time: 65.7 us; the launch traced here: 65.4 us
  waiting for transfers between devices  24.7 us (38%)
  starting transfers between devices  22.3 us (34%)
  Pallas kernels  16.4 us (25%)
  between operations  1.44 us (2%)
    pallas_call x9, Pallas kernels, call(): pl.pallas_call(body, out_shape=outs, in_specs=[pl.BlockSpec(memory_space=...  16.4 us
    all_to_all x1, waiting for transfers between devices, on_device(): received = lax.all_to_all(blocks, CHIPS, 0, 0)  14.9 us
    ppermute x8, starting transfers between devices, passed_along(): lax.ppermute(array, axis, [(i, (i + by) % size) for i in range(size)])  12.4 us
    ppermute x8, waiting for transfers between devices, passed_along(): lax.ppermute(array, axis, [(i, (i + by) % size) for i in range(size)])  6.16 us
    all_to_all x1, starting transfers between devices, on_device(): received = lax.all_to_all(blocks, CHIPS, 0, 0)  4.59 us
    all_to_all x1, starting transfers between devices, on_device(): own = lax.all_to_all(spread, CHIPS, 0, 0)  3.65 us
    ppermute x2, waiting for transfers between devices, across_cores(): return lax.ppermute(array, CORE, [(0, 1), (1, 0)])  2.73 us
    ppermute x2, starting transfers between devices, across_cores(): return lax.ppermute(array, CORE, [(0, 1), (1, 0)])  1.63 us
  transfers between devices with their start and end apart: 12, of which 6 were waited for; matrix products, arithmetic and copies ran while one was open for 1% of the time, Pallas kernels for 11%

profile of v5, /device:TPU:0, one launch (start us, length us, event | category | flops | bytes accessed | tf_op | source)
XLA Modules:
  0.0 65.4 jit_solution(3998392375426685166)
XLA Ops:
  0.6 1.3 %shard_map.197 = (bf16[96,256]{1,0:T(8,128)(2,1)S(1)}, bf16[64,256]{1,0:T(8,128)(2,1)S(1)}, bf16[96,256]{1,0:T(8,128)(2,1)S(1)}, bf16[384,256]{1,0:T(8,128)(2,1)S(1)}, s32[8,32]{1,0:T(8,128)S(1)}) custom-call(bf16[384,256]{1,0:T(8,128)(2,1)} %nodes_hbm.1, s32[8,32]{1,0:T(8,128)} %list_hbm.1), custom_call_target="tpu_custom_call" | custom-call | flops 50331648 | bytes 526336 | tf_op jit(solution)/shard_map/pallas_call | solution.py:453
  1.9 3.1 %collective-permute-start = (bf16[96,256]{1,0:T(8,128)(2,1)S(1)}, bf16[96,256]{1,0:T(8,128)(2,1)S(1)}, u32[]{:S(2)}, u32[]{:S(2)}) collective-permute-start(bf16[96,256]{1,0:T(8,128)(2,1)S(1)} %get-tuple-element.55), channel_id=1, source_target_pairs={{0,4},{4,8},{8,12},{12,0},{1,5},{5,9},{9,13},{13,1},{2,6},{6,10},{... | collective-permute-start | bytes 147464 | tf_op jit(solution)/shard_map/ppermute | solution.py:23
  5.0 2.1 %collective-permute-start.1 = (bf16[96,256]{1,0:T(8,128)(2,1)S(1)}, bf16[96,256]{1,0:T(8,128)(2,1)S(1)}, u32[]{:S(2)}, u32[]{:S(2)}) collective-permute-start(bf16[96,256]{1,0:T(8,128)(2,1)S(1)} %get-tuple-element.56), channel_id=1, source_target_pairs={{0,12},{4,0},{8,4},{12,8},{1,13},{5,1},{9,5},{13,9},{2,14},{6,2},{... | collective-permute-start | bytes 147464 | tf_op jit(solution)/shard_map/ppermute | solution.py:23
  7.1 0.0 copy-start
  7.1 0.0 copy-start.1
  7.1 2.6 %shard_map.198 = (f32[1152,256]{1,0:T(8,128)S(1)}, bf16[1152,384]{1,0:T(8,128)(2,1)S(1)}, bf16[768,256]{1,0:T(8,128)(2,1)S(1)}, s32[9,128]{1,0:T(8,128)S(1)}, s3...) custom-call(bf16[384,256]{1,0:T(8,128)(2,1)S(1)} %get-tuple-element., ...), custom_call_target="tpu_custom_call" | custom-call | flops 704643072 | bytes 6866944 | tf_op jit(solution)/shard_map/pallas_call | solution.py:453
  9.7 0.0 collective-permute-done.from_low
  9.7 0.0 collective-permute-done.1.from_high
  9.7 0.1 collective-permute-start.2
  9.8 1.7 %collective-permute-start.3 = (bf16[96,256]{1,0:T(8,128)(2,1)S(1)}, bf16[96,256]{1,0:T(8,128)(2,1)S(1)}, u32[]{:S(2)}, u32[]{:S(2)}) collective-permute-start(bf16[96,256]{1,0:T(8,128)(2,1)S(1)} %pad_maximum_fusion.1), channel_id=1, source_target_pairs={{0,3},{1,0},{2,1},{3,2},{4,7},{5,4},{6,5},{7,6},{8,11},{9,8},{10,9... | collective-permute-start | bytes 147464 | tf_op jit(solution)/shard_map/ppermute | solution.py:23
  12.2 0.0 copy-done
  12.2 0.0 copy-done.1
  12.2 1.2 %shard_map.199 = (bf16[1152,256]{1,0:T(8,128)(2,1)S(1)}, bf16[640,1152]{1,0:T(8,128)(2,1)S(1)}, bf16[384,1152]{1,0:T(8,128)(2,1)S(1)}) custom-call(s32[9,128]{1,0:T(8,128)S(1)} %get-tuple-element.59.senders, s32[9,128]{1,0:T(8,128)S(1)} %get-tuple-element.60.receivers), custom_call_target="tpu_custom_call" | custom-call | bytes 2958336 | tf_op jit(solution)/shard_map/pallas_call | solution.py:453
  13.5 0.0 collective-permute-done.2.upward
  13.5 0.0 collective-permute-done.3.downward
  13.5 5.9 %shard_map.200 = (bf16[1152,256]{1,0:T(8,128)(2,1)S(1)}, bf16[384,256]{1,0:T(8,128)(2,1)S(1)}, bf16[384,256]{1,0:T(8,128)(2,1)S(1)}, f32[384,256]{1,0:T(8,128)S(...) custom-call(s32[1]{0:T(128)S(6)} %copy.22.count_ref, ...), custom_call_target="tpu_custom_call" | custom-call | flops 2583691264 | bytes 10601476 | tf_op jit(solution)/shard_map/pallas_call | solution.py:453
  19.4 1.6 %collective-permute-start.4 = (bf16[912,256]{1,0:T(8,128)(2,1)S(1)}, bf16[912,256]{1,0:T(8,128)(2,1)S(1)}, u32[]{:S(2)}, u32[]{:S(2)}) collective-permute-start(bf16[912,256]{1,0:T(8,128)(2,1)S(1)} %get-tuple-element.74), channel_id=1, source_target_pairs={{0,1},{1,0},{2,3},{3,2},{4,5},{5,4},{6,7},{7,6},{8,9},{9,8},{10,11... | collective-permute-start | bytes 1400840 | tf_op jit(solution)/shard_map/ppermute | solution.py:27
  21.0 1.5 %collective-permute-done.4.other = bf16[912,256]{1,0:T(8,128)(2,1)S(1)} collective-permute-done((bf16[912,256]{1,0:T(8,128)(2,1)S(1)}, bf16[912,256]{1,0:T(8,128)(2,1)S(1)}, u32[]{:S(2)}, u32[]{:S(2)}) %collective-permute-start.4) | collective-permute-done | bytes 466976 | tf_op jit(solution)/shard_map/ppermute | solution.py:27
  22.5 0.9 %shard_map.201 = bf16[8,128,256]{2,1,0:T(8,128)(2,1)} custom-call(f32[896,256]{1,0:T(8,128)S(1)} %get-tuple-element.72.keep, bf16[16,256]{1,0:T(8,128)(2,1)S(1)} %get-tuple-element.73.gains, bf16[912,256]{1,0:T(8,128)(2,1)S(1)} %collective-permute-done.4.other), custom_call_target="tpu_custom_call" | custom-call | bytes 1916928 | tf_op jit(solution)/shard_map/pallas_call | solution.py:453
  23.4 4.6 %all-to-all-start = ((bf16[8,128,256]{2,1,0:T(8,128)(2,1)}), bf16[8,128,256]{2,1,0:T(8,128)(2,1)S(1)}, u32[]{:S(2)}, u32[]{:S(2)}) async-start(bf16[8,128,256]{2,1,0:T(8,128)(2,1)} %shard_map.201), calls=%async_computation | async-start | bytes 1048576 | tf_op jit(solution)/shard_map/all_to_all | solution.py:703
  28.0 0.1 collective-permute-start.5
  28.0 14.9 %all-to-all-done.received = bf16[8,128,256]{2,1,0:T(8,128)(2,1)S(1)} async-done(((bf16[8,128,256]{2,1,0:T(8,128)(2,1)}), bf16[8,128,256]{2,1,0:T(8,128)(2,1)S(1)}, u32[]{:S(2)}, u32[]{:S(2)}) %all-to-all-start) | async-done | bytes 524320 | tf_op jit(solution)/shard_map/all_to_all | solution.py:703
  43.0 0.9 %shard_map.202 = (f32[16,256]{1,0:T(8,128)S(1)}, bf16[8,112,256]{2,1,0:T(8,128)(2,1)}) custom-call(bf16[8,128,256]{2,1,0:T(8,128)(2,1)S(1)} %all-to-all-done.received), custom_call_target="tpu_custom_call" | custom-call | bytes 999424 | tf_op jit(solution)/shard_map/pallas_call | solution.py:453
  43.9 3.6 %all-to-all-start.1 = ((bf16[8,112,256]{2,1,0:T(8,128)(2,1)}), bf16[8,112,256]{2,1,0:T(8,128)(2,1)S(1)}, u32[]{:S(2)}, u32[]{:S(2)}) async-start(bf16[8,112,256]{2,1,0:T(8,128)(2,1)} %get-tuple-element.75), calls=%async_computation.1 | async-start | bytes 917504 | tf_op jit(solution)/shard_map/all_to_all | solution.py:705
  47.5 1.1 %collective-permute-start.6 = (bf16[96,256]{1,0:T(8,128)(2,1)S(1)}, bf16[96,256]{1,0:T(8,128)(2,1)S(1)}, u32[]{:S(2)}, u32[]{:S(2)}) collective-permute-start(bf16[96,256]{1,0:T(8,128)(2,1)S(1)} %get-tuple-element.83), channel_id=1, source_target_pairs={{0,3},{1,0},{2,1},{3,2},{4,7},{5,4},{6,5},{7,6},{8,11},{9,8},{10,9... | collective-permute-start | bytes 147464 | tf_op jit(solution)/shard_map/ppermute | solution.py:23
  48.6 0.0 collective-permute-done.5.up_back
  48.6 2.6 %collective-permute-done.6.down_back = bf16[96,256]{1,0:T(8,128)(2,1)S(1)} collective-permute-done((bf16[96,256]{1,0:T(8,128)(2,1)S(1)}, bf16[96,256]{1,0:T(8,128)(2,1)S(1)}, u32[]{:S(2)}, u32[]{:S(2)}) %collective-permute-start.6) | collective-permute-done | bytes 49184 | tf_op jit(solution)/shard_map/ppermute | solution.py:23
  51.2 2.7 %collective-permute-start.7 = (bf16[96,256]{1,0:T(8,128)(2,1)S(1)}, bf16[96,256]{1,0:T(8,128)(2,1)S(1)}, u32[]{:S(2)}, u32[]{:S(2)}) collective-permute-start(bf16[96,256]{1,0:T(8,128)(2,1)S(1)} %pad_maximum_fusion.2), channel_id=1, source_target_pairs={{0,4},{4,8},{8,12},{12,0},{1,5},{5,9},{9,13},{13,1},{2,6},{6,10},{... | collective-permute-start | bytes 147464 | tf_op jit(solution)/shard_map/ppermute | solution.py:23
  53.9 1.6 %collective-permute-start.8 = (bf16[96,256]{1,0:T(8,128)(2,1)S(1)}, bf16[96,256]{1,0:T(8,128)(2,1)S(1)}, u32[]{:S(2)}, u32[]{:S(2)}) collective-permute-start(bf16[96,256]{1,0:T(8,128)(2,1)S(1)} %pad_maximum_fusion.3), channel_id=1, source_target_pairs={{0,12},{4,0},{8,4},{12,8},{1,13},{5,1},{9,5},{13,9},{2,14},{6,2},{... | collective-permute-start | bytes 147464 | tf_op jit(solution)/shard_map/ppermute | solution.py:23
  55.5 1.3 %shard_map.203 = (bf16[1152,256]{1,0:T(8,128)(2,1)}, f32[384,256]{1,0:T(8,128)S(1)}) custom-call(bf16[1152,256]{1,0:T(8,128)(2,1)S(1)} %get-tuple-element.54.edge_grads, bf16[1152,256]{1,0:T(8,128)(2,1)S(1)} %get-tuple-element.77.pre_grad, bf16[384,256]{1,0:T(8,128)(2,1)S(1)} %get-tuple-element.78.sender_sum, ...), custom_call_target="tpu_custom_call" | custom-call | flops 251658240 | bytes 3342336 | tf_op jit(solution)/shard_map/pallas_call | solution.py:453
  56.8 3.6 %collective-permute-done.7.to_high = bf16[96,256]{1,0:T(8,128)(2,1)S(1)} collective-permute-done((bf16[96,256]{1,0:T(8,128)(2,1)S(1)}, bf16[96,256]{1,0:T(8,128)(2,1)S(1)}, u32[]{:S(2)}, u32[]{:S(2)}) %collective-permute-start.7) | collective-permute-done | bytes 49184 | tf_op jit(solution)/shard_map/ppermute | solution.py:23
  60.4 0.0 collective-permute-done.8.to_low
  60.4 1.1 %shard_map.204 = bf16[384,256]{1,0:T(8,128)(2,1)} custom-call(s32[8,32]{1,0:T(8,128)S(1)} %get-tuple-element.76.send_list, f32[384,256]{1,0:T(8,128)S(1)} %get-tuple-element.81.local_grad, bf16[96,256]{1,0:T(8,128)(2,1)S(1)} %collective-permute-done.5.up_back, bf16[96,256]{1,0:T(8,128)(2,1)S(1)} %collective-permute-done.6.down_back, ...), custom_call_target="tpu_custom_call" | custom-call | flops 50331648 | bytes 787456 | tf_op jit(solution)/shard_map/pallas_call | solution.py:453
  61.5 0.9 %all-to-all-done.1.own = bf16[8,112,256]{2,1,0:T(8,128)(2,1)S(1)} async-done(((bf16[8,112,256]{2,1,0:T(8,128)(2,1)}), bf16[8,112,256]{2,1,0:T(8,128)(2,1)S(1)}, u32[]{:S(2)}, u32[]{:S(2)}) %all-to-all-start.1) | async-done | bytes 458784 | tf_op jit(solution)/shard_map/all_to_all | solution.py:705
  62.4 0.0 collective-permute-start.9
  62.4 0.5 convert_reduce_fusion
  62.9 1.3 %collective-permute-done.9.other = bf16[8,112,256]{2,1,0:T(8,128)(2,1)S(1)} collective-permute-done((bf16[8,112,256]{2,1,0:T(8,128)(2,1)S(1)}, bf16[8,112,256]{2,1,0:T(8,128)(2,1)S(1)}, u32[]{:S(2)}, u32[]{:S(2)}) %collective-permute-start.9) | collective-permute-done | bytes 458784 | tf_op jit(solution)/shard_map/ppermute | solution.py:27
  64.2 1.2 %shard_map.205 = (bf16[768,256]{1,0:T(8,128)(2,1)}, bf16[256,256]{1,0:T(8,128)(2,1)}, bf16[512,256]{1,0:T(8,128)(2,1)}, bf16[256,256]{1,0:T(8,128)(2,1)}) custom-call(bf16[8,112,256]{2,1,0:T(8,128)(2,1)S(1)} %all-to-all-done.1.own, bf16[8,112,256]{2,1,0:T(8,128)(2,1)S(1)} %collective-permute-done.9.other), custom_call_target="tpu_custom_call" | custom-call | bytes 1835008 | tf_op jit(solution)/shard_map/pallas_call | solution.py:453
  (11 shorter events, 0.1 us)
Async XLA Ops:
  1.9 7.7 %collective-permute-start = (bf16[96,256]{1,0:T(8,128)(2,1)S(1)}, bf16[96,256]{1,0:T(8,128)(2,1)S(1)}, u32[]{:S(2)}, u32[]{:S(2)}) collective-permute-start(bf16[96,256]{1,0:T(8,128)(2,1)S(1)} %get-tuple-element.55), channel_id=1, source_target_pairs={{0,4},{4,8},{8,12},{12,0},{1,5},{5,9},{9,13},{13,1},{2,6},{6,10},{... | collective-permute-start | bytes 147464 | tf_op jit(solution)/shard_map/ppermute | solution.py:23
  5.0 4.7 %collective-permute-start.1 = (bf16[96,256]{1,0:T(8,128)(2,1)S(1)}, bf16[96,256]{1,0:T(8,128)(2,1)S(1)}, u32[]{:S(2)}, u32[]{:S(2)}) collective-permute-start(bf16[96,256]{1,0:T(8,128)(2,1)S(1)} %get-tuple-element.56), channel_id=1, source_target_pairs={{0,12},{4,0},{8,4},{12,8},{1,13},{5,1},{9,5},{13,9},{2,14},{6,2},{... | collective-permute-start | bytes 147464 | tf_op jit(solution)/shard_map/ppermute | solution.py:23
  7.1 5.1 %copy-start = (bf16[256]{0:T(256)(128)(2,1)S(1)}, bf16[256]{0:T(256)(128)(2,1)}, u32[]{:S(2)}) copy-start(bf16[256]{0:T(256)(128)(2,1)} %param.24) | copy-start | bytes 1540
  7.1 5.1 %copy-start.1 = (bf16[256]{0:T(256)(128)(2,1)S(1)}, bf16[256]{0:T(256)(128)(2,1)}, u32[]{:S(2)}) copy-start(bf16[256]{0:T(256)(128)(2,1)} %param.27) | copy-start | bytes 1540
  9.7 3.7 %collective-permute-start.2 = (bf16[96,256]{1,0:T(8,128)(2,1)S(1)}, bf16[96,256]{1,0:T(8,128)(2,1)S(1)}, u32[]{:S(2)}, u32[]{:S(2)}) collective-permute-start(bf16[96,256]{1,0:T(8,128)(2,1)S(1)} %pad_maximum_fusion), channel_id=1, source_target_pairs={{0,1},{1,2},{2,3},{3,0},{4,5},{5,6},{6,7},{7,4},{8,9},{9,10},{10,1... | collective-permute-start | bytes 147464 | tf_op jit(solution)/shard_map/ppermute | solution.py:23
  9.8 3.7 %collective-permute-start.3 = (bf16[96,256]{1,0:T(8,128)(2,1)S(1)}, bf16[96,256]{1,0:T(8,128)(2,1)S(1)}, u32[]{:S(2)}, u32[]{:S(2)}) collective-permute-start(bf16[96,256]{1,0:T(8,128)(2,1)S(1)} %pad_maximum_fusion.1), channel_id=1, source_target_pairs={{0,3},{1,0},{2,1},{3,2},{4,7},{5,4},{6,5},{7,6},{8,11},{9,8},{10,9... | collective-permute-start | bytes 147464 | tf_op jit(solution)/shard_map/ppermute | solution.py:23
  19.4 3.1 %collective-permute-start.4 = (bf16[912,256]{1,0:T(8,128)(2,1)S(1)}, bf16[912,256]{1,0:T(8,128)(2,1)S(1)}, u32[]{:S(2)}, u32[]{:S(2)}) collective-permute-start(bf16[912,256]{1,0:T(8,128)(2,1)S(1)} %get-tuple-element.74), channel_id=1, source_target_pairs={{0,1},{1,0},{2,3},{3,2},{4,5},{5,4},{6,7},{7,6},{8,9},{9,8},{10,11... | collective-permute-start | bytes 1400840 | tf_op jit(solution)/shard_map/ppermute | solution.py:27
  23.4 19.6 %all-to-all-start = ((bf16[8,128,256]{2,1,0:T(8,128)(2,1)}), bf16[8,128,256]{2,1,0:T(8,128)(2,1)S(1)}, u32[]{:S(2)}, u32[]{:S(2)}) async-start(bf16[8,128,256]{2,1,0:T(8,128)(2,1)} %shard_map.201), calls=%async_computation | async-start | bytes 1048576 | tf_op jit(solution)/shard_map/all_to_all | solution.py:703
  28.0 20.7 %collective-permute-start.5 = (bf16[96,256]{1,0:T(8,128)(2,1)S(1)}, bf16[96,256]{1,0:T(8,128)(2,1)S(1)}, u32[]{:S(2)}, u32[]{:S(2)}) collective-permute-start(bf16[96,256]{1,0:T(8,128)(2,1)S(1)} %get-tuple-element.82), channel_id=1, source_target_pairs={{0,1},{1,2},{2,3},{3,0},{4,5},{5,6},{6,7},{7,4},{8,9},{9,10},{10,1... | collective-permute-start | bytes 147464 | tf_op jit(solution)/shard_map/ppermute | solution.py:23
  43.9 18.5 %all-to-all-start.1 = ((bf16[8,112,256]{2,1,0:T(8,128)(2,1)}), bf16[8,112,256]{2,1,0:T(8,128)(2,1)S(1)}, u32[]{:S(2)}, u32[]{:S(2)}) async-start(bf16[8,112,256]{2,1,0:T(8,128)(2,1)} %get-tuple-element.75), calls=%async_computation.1 | async-start | bytes 917504 | tf_op jit(solution)/shard_map/all_to_all | solution.py:705
  47.5 3.7 %collective-permute-start.6 = (bf16[96,256]{1,0:T(8,128)(2,1)S(1)}, bf16[96,256]{1,0:T(8,128)(2,1)S(1)}, u32[]{:S(2)}, u32[]{:S(2)}) collective-permute-start(bf16[96,256]{1,0:T(8,128)(2,1)S(1)} %get-tuple-element.83), channel_id=1, source_target_pairs={{0,3},{1,0},{2,1},{3,2},{4,7},{5,4},{6,5},{7,6},{8,11},{9,8},{10,9... | collective-permute-start | bytes 147464 | tf_op jit(solution)/shard_map/ppermute | solution.py:23
  51.2 9.2 %collective-permute-start.7 = (bf16[96,256]{1,0:T(8,128)(2,1)S(1)}, bf16[96,256]{1,0:T(8,128)(2,1)S(1)}, u32[]{:S(2)}, u32[]{:S(2)}) collective-permute-start(bf16[96,256]{1,0:T(8,128)(2,1)S(1)} %pad_maximum_fusion.2), channel_id=1, source_target_pairs={{0,4},{4,8},{8,12},{12,0},{1,5},{5,9},{9,13},{13,1},{2,6},{6,10},{... | collective-permute-start | bytes 147464 | tf_op jit(solution)/shard_map/ppermute | solution.py:23
  53.9 6.5 %collective-permute-start.8 = (bf16[96,256]{1,0:T(8,128)(2,1)S(1)}, bf16[96,256]{1,0:T(8,128)(2,1)S(1)}, u32[]{:S(2)}, u32[]{:S(2)}) collective-permute-start(bf16[96,256]{1,0:T(8,128)(2,1)S(1)} %pad_maximum_fusion.3), channel_id=1, source_target_pairs={{0,12},{4,0},{8,4},{12,8},{1,13},{5,1},{9,5},{13,9},{2,14},{6,2},{... | collective-permute-start | bytes 147464 | tf_op jit(solution)/shard_map/ppermute | solution.py:23
  62.4 1.8 %collective-permute-start.9 = (bf16[8,112,256]{2,1,0:T(8,128)(2,1)S(1)}, bf16[8,112,256]{2,1,0:T(8,128)(2,1)S(1)}, u32[]{:S(2)}, u32[]{:S(2)}) collective-permute-start(bf16[8,112,256]{2,1,0:T(8,128)(2,1)S(1)} %all-to-all-done.1.own), channel_id=1, source_target_pairs={{0,1},{1,0},{2,3},{3,2},{4,5},{5,4},{6,7},{7,6},{8,9},{9,8},{10,11... | collective-permute-start | bytes 1376264 | tf_op jit(solution)/shard_map/ppermute | solution.py:27

commit v6 on v5

--- a/solution.py
+++ b/solution.py
@@ -97,13 +97,8 @@
 
 
 def live_rows(count_ref, tile_rows, rows):
-    index = lax.broadcasted_iota(jnp.int32, (rows.stop - rows.start, 1), 0)
-    return jnp.where(index < count_ref[0] * tile_rows - rows.start, 1.0, 0.0)
-
-
-def chunks_of(tiles):
-    step = 3 if tiles % 3 == 0 else 1
-    return [list(range(first, first + step)) for first in range(0, tiles, step)]
+    index = lax.broadcasted_iota(jnp.int32, (rows, 1), 0)
+    return jnp.where(index < count_ref[0] * tile_rows, 1.0, 0.0)
 
 
 def fetch_all(sources, targets, sems):
@@ -126,17 +121,35 @@
     high[...] = rows[5 * slots :]
 
 
-def local_kernel(nodes, *refs):
-    fetched = (len(refs) - 3) // 2
-    pre, receiver_rows, sems = refs[fetched], refs[fetched + 1], refs[-1]
-    targets = refs[fetched + 2 : -1]
-    w_in, senders, receivers, edges = targets[:4]
-    copies = fetch_all(refs[:fetched], targets, sems)
-    count, width = nodes.shape
+def index_kernel(sources, *refs):
+    fetched, refs = refs[:sources], refs[sources:]
+    near_rows, halo_rows, sender_columns, receiver_columns = refs[:4]
+    targets, sems = refs[4:-1], refs[-1]
+    senders, receivers = targets[:2]
+    copies = fetch_all(fetched, targets, sems)
+    for copy in copies[:2]:
+        copy.wait()
     tile_rows = senders.shape[1]
+    extended = sender_columns.shape[0]
+    count = receiver_columns.shape[0]
+    sender_ids = senders[...]
+    receiver_ids = receivers[...]
+    by_sender = columns_of(sender_ids)
+    by_receiver = columns_of(receiver_ids)
+    for tile in range(senders.shape[0]):
+        rows = slice(tile * tile_rows, (tile + 1) * tile_rows)
+        near_rows[rows, :count] = hot_rows(by_sender, [tile], 0, count)
+        near_rows[rows, count:] = hot_rows(by_receiver, [tile], 0, count)
+        halo_rows[rows, :] = hot_rows(by_sender, [tile], count, halo_rows.shape[1])
+        sender_columns[:, rows] = hot_columns(sender_ids, [tile], 0, extended)
+        receiver_columns[:, rows] = hot_columns(receiver_ids, [tile], 0, count)
+    for copy in copies[2:]:
+        copy.wait()
+
+
+def local_kernel(nodes, edges, near_rows, w_in, pre):
+    width = nodes.shape[1]
     x = nodes[...]
-    for copy in copies[:4]:
-        copy.wait()
     table = jnp.concatenate(
         [
             dot(x, w_in[width : 2 * width]).astype(BF16),
@@ -144,31 +157,7 @@
         ],
         axis=0,
     )
-    by_sender = columns_of(senders[...])
-    by_receiver = columns_of(receivers[...])
-    w_edge = w_in[:width]
-    for tiles in chunks_of(senders.shape[0]):
-        rows = pl.ds(tiles[0] * tile_rows, len(tiles) * tile_rows)
-        by_receiver_hot = hot_rows(by_receiver, tiles, 0, count)
-        receiver_rows[rows, :] = by_receiver_hot
-        hot = jnp.concatenate([hot_rows(by_sender, tiles, 0, count), by_receiver_hot], axis=1)
-        pre[rows, :] = dot(edges[rows, :], w_edge) + dot(hot, table)
-    for copy in copies[4:]:
-        copy.wait()
-
-
-def index_kernel(senders, receivers, halo_rows, sender_columns, receiver_columns):
-    tile_rows = senders.shape[1]
-    extended = sender_columns.shape[0]
-    count = receiver_columns.shape[0]
-    sender_ids = senders[...]
-    receiver_ids = receivers[...]
-    by_sender = columns_of(sender_ids)
-    for tile in range(senders.shape[0]):
-        rows = slice(tile * tile_rows, (tile + 1) * tile_rows)
-        halo_rows[rows, :] = hot_rows(by_sender, [tile], count, halo_rows.shape[1])
-        sender_columns[:, rows] = hot_columns(sender_ids, [tile], 0, extended)
-        receiver_columns[:, rows] = hot_columns(receiver_ids, [tile], 0, count)
+    pre[...] = dot(edges[...], w_in[:width]) + dot(near_rows[...], table)
 
 
 def split_by_core(sums, first, keep_out, away_out):
@@ -199,7 +188,7 @@
     edge_grads,
     pre_local,
     halo_rows,
-    receiver_rows,
+    near_rows,
     sender_columns,
     receiver_columns,
     from_high,
@@ -231,8 +220,7 @@
 ):
     count, width = nodes.shape
     edge_rows = edges.shape[0]
-    step = edge_rows // 3 if edge_rows % 48 == 0 else edge_rows
-    chunks = [slice(first, first + step) for first in range(0, edge_rows, step)]
+    live = live_rows(count_ref, tile_rows, edge_rows)
     slots = from_high.shape[0] // 3
     halo = jnp.concatenate(
         [
@@ -248,19 +236,17 @@
         axis=0,
     )
     table = dot(halo, w_in[width : 2 * width]).astype(BF16)
-    gain = gain_edge[...].astype(F32)
-    total = jnp.zeros((count, width), F32)
-    for rows in chunks:
-        value = pre_local[rows, :] + dot(halo_rows[rows, :], table)
-        sigma = sigmoid(value)
-        hidden = (value * sigma).astype(BF16)
-        hidden_kept[rows, :] = hidden
-        slope_kept[rows, :] = sigma * (1.0 + value * (1.0 - sigma))
-        normed, scale_inv = normalize(dot(hidden, w_out[...]))
-        normed_kept[rows, :] = normed
-        scale_kept[rows, :] = jnp.broadcast_to(scale_inv, (step, 128))
-        message = (live_rows(count_ref, tile_rows, rows) * gain * normed).astype(BF16)
-        total = total + dot(receiver_columns[:, rows], message)
+    gain = gain_edge[...].astype(F32)[None, :]
+    value = pre_local[...] + dot(halo_rows[...], table)
+    sigma = sigmoid(value)
+    hidden = (value * sigma).astype(BF16)
+    hidden_kept[...] = hidden
+    slope_kept[...] = sigma * (1.0 + value * (1.0 - sigma))
+    edge_normed, edge_scale = normalize(dot(hidden, w_out[...]))
+    normed_kept[...] = edge_normed
+    scale_kept[...] = jnp.broadcast_to(edge_scale, (edge_rows, 128))
+    message = (live * gain * edge_normed).astype(BF16)
+    total = dot(receiver_columns[...], message)
     aggregated = total.astype(BF16)
     x = nodes[...]
     w_first = w_node_in[:width]
@@ -270,7 +256,7 @@
     node_hidden = (node_pre * sigma).astype(BF16)
     normed, scale_inv = normalize(dot(node_hidden, w_node_out[...]))
     upstream = node_grads[...].astype(F32)
-    out_grad = norm_back(normed, scale_inv, gain_node[...].astype(F32), upstream).astype(BF16)
+    out_grad = norm_back(normed, scale_inv, gain_node[...].astype(F32)[None, :], upstream).astype(BF16)
     slope = sigma * (1.0 + node_pre * (1.0 - sigma))
     pre_grad = (dot_nt(out_grad, w_node_out[...]) * slope).astype(BF16)
     agg_grad = dot_nt(pre_grad, w_second).astype(BF16)
@@ -279,25 +265,16 @@
     node_sums[width : 2 * width] = dot_tn(aggregated, pre_grad)
     node_sums[2 * width : 3 * width] = dot_tn(node_hidden, out_grad)
     node_gain = jnp.sum(upstream * normed, axis=0, keepdims=True)
-    extended = count + halo.shape[0]
-    sender_total = jnp.zeros((extended, width), F32)
-    receiver_total = jnp.zeros((count, width), F32)
-    first = jnp.zeros((width, width), F32)
-    second = jnp.zeros((width, width), F32)
-    gain_total = jnp.zeros((1, width), F32)
-    for rows in chunks:
-        upstream = live_rows(count_ref, tile_rows, rows) * (
-            edge_grads[rows, :].astype(F32) + dot(receiver_rows[rows, :], agg_grad)
-        )
-        chunk_normed = normed_kept[rows, :]
-        gain_total = gain_total + jnp.sum(upstream * chunk_normed, axis=0, keepdims=True)
-        out_grad = norm_back(chunk_normed, scale_kept[rows, :1], gain, upstream).astype(BF16)
-        pre_grad = (dot_nt(out_grad, w_out[...]) * slope_kept[rows, :]).astype(BF16)
-        pre_grad_out[rows, :] = pre_grad
-        second = second + dot_tn(hidden_kept[rows, :], out_grad)
-        first = first + dot_tn(edges[rows, :], pre_grad)
-        sender_total = sender_total + dot(sender_columns[:, rows], pre_grad)
-        receiver_total = receiver_total + dot(receiver_columns[:, rows], pre_grad)
+    upstream = live * (
+        edge_grads[...].astype(F32) + dot(near_rows[:, count:], agg_grad)
+    )
+    edge_normed = normed_kept[...]
+    edge_gain = jnp.sum(upstream * edge_normed, axis=0, keepdims=True)
+    out_grad = norm_back(edge_normed, scale_kept[:, :1], gain, upstream).astype(BF16)
+    pre_grad = (dot_nt(out_grad, w_out[...]) * slope_kept[...]).astype(BF16)
+    pre_grad_out[...] = pre_grad
+    sender_total = dot(sender_columns[...], pre_grad)
+    receiver_total = dot(receiver_columns[...], pre_grad)
     own = sender_total[:count].astype(BF16)
     away = sender_total[count:].astype(BF16)
     received = receiver_total.astype(BF16)
@@ -308,28 +285,33 @@
     up_out[...] = jnp.concatenate([parts[0], parts[3], parts[5]], axis=0)
     down_out[...] = jnp.concatenate([parts[2], parts[4], parts[7]], axis=0)
     rest_out[...] = jnp.concatenate([parts[1], parts[6]], axis=0)
-    edge_sums[:width] = first
+    edge_sums[:width] = dot_tn(edges[...], pre_grad)
     edge_sums[width : 2 * width] = dot_tn(x, own) + dot_tn(halo, away)
     edge_sums[2 * width : 3 * width] = dot_tn(x, received)
-    edge_sums[3 * width : 4 * width] = second
+    edge_sums[3 * width : 4 * width] = dot_tn(hidden_kept[...], out_grad)
     split_by_core(edge_sums, 0, keep_out, away_out)
     split_by_core(node_sums, edge_sums.shape[0] // 2, keep_out, away_out)
-    gains = pack_gains(gain_total, node_gain)
+    gains = pack_gains(edge_gain, node_gain)
     away_out[keep_out.shape[0] :] = gains
     gains_out[...] = gains
 
 
-def pair_kernel(parts, keep, gains, other, blocks_out, total, staged, sems):
+def add_gains(own, other):
+    both = own.astype(F32) + other.astype(F32)
+    return pack_gains(both[0:1] + both[1:2], both[2:3] + both[3:4])
+
+
+def gains_kernel(own, other, gains_out):
+    gains_out[...] = add_gains(own[...], other[...])
+
+
+def pair_kernel(parts, keep, gains, other, blocks_out, gains_out, total, staged, sems):
     rows = keep.shape[0]
     chips = blocks_out.shape[0]
-    packed = gains.shape[0]
-    both = gains[...].astype(F32) + other[rows:].astype(F32)
-    summed = pack_gains(both[0:1] + both[1:2], both[2:3] + both[3:4])
     total[...] = (keep[...] + other[:rows].astype(F32)).astype(BF16)
     copies = []
     for chip in range(chips):
-        staged[chip, :packed, :] = summed
-        first, at = 0, packed
+        first, at = 0, 0
         for part in parts:
             step = part // chips
             staged[chip, at : at + step, :] = total[first + chip * step : first + (chip + 1) * step]
@@ -338,16 +320,16 @@
             pltpu.make_async_copy(staged.at[chip], blocks_out.at[chip], sems.at[chip])
         )
         copies[-1].start()
+    gains_out[...] = add_gains(gains[...], other[rows:])
     for copy in copies:
         copy.wait()
 
 
-def spread_kernel(packed, received, gains_out, spread_out, mine, sems):
+def spread_kernel(received, spread_out, mine, sems):
     sums = received[0].astype(F32)
     for chip in range(1, received.shape[0]):
         sums = sums + received[chip].astype(F32)
-    gains_out[...] = sums[:packed]
-    mine[...] = sums[packed:].astype(BF16)
+    mine[...] = sums.astype(BF16)
     copies = [
         pltpu.make_async_copy(mine, spread_out.at[chip], sems.at[chip])
         for chip in range(received.shape[0])
@@ -503,60 +485,60 @@
     return results
 
 
-def spread_of(received, packed):
+def spread_of(received):
     chips, rows, width = received.shape
-    mine = rows - packed
-    if mine % 16 == 0:
+    if rows % 16 == 0:
         return call(
-            functools.partial(spread_kernel, packed),
-            [shaped(packed, width, F32), jax.ShapeDtypeStruct((chips, mine, width), BF16)],
+            spread_kernel,
+            [like(received)],
             0,
             received,
-            out_space=[VMEM, HBM],
-            scratch=[pltpu.VMEM((mine, width), BF16), pltpu.SemaphoreType.DMA((chips,))],
-        )
+            out_space=HBM,
+            scratch=[pltpu.VMEM((rows, width), BF16), pltpu.SemaphoreType.DMA((chips,))],
+        )[0]
     sums = jnp.sum(received.astype(F32), axis=0)
-    return sums[:packed], jnp.broadcast_to(sums[packed:].astype(BF16)[None], (chips, mine, width))
+    return jnp.broadcast_to(sums.astype(BF16)[None], received.shape)
+
+
+def summed_gains(gains):
+    for axis in ("side", "px"):
+        size = lax.axis_size(axis)
+        distance = 1
+        while distance < size:
+            other = lax.ppermute(gains, axis, [(i, i ^ distance) for i in range(size)])
+            (gains,) = call(gains_kernel, [like(gains)], 0, gains, other)
+            distance *= 2
+    return gains
 
 
 def blocks_of(parts, keep, gains, other):
     chips = lax.axis_size(CHIPS)
     rows, width = keep.shape
-    packed = gains.shape[0]
     steps = [part // chips for part in parts]
-    shape = (chips, packed + sum(steps), width)
-    body = functools.partial(pair_kernel, parts)
+    shape = (chips, sum(steps), width)
     if all(x % 16 == 0 for x in steps):
-        (blocks,) = call(
-            body,
-            [jax.ShapeDtypeStruct(shape, BF16)],
+        return call(
+            functools.partial(pair_kernel, parts),
+            [jax.ShapeDtypeStruct(shape, BF16), like(gains)],
             0,
             keep,
             gains,
             other,
-            out_space=HBM,
+            out_space=[HBM, VMEM],
             scratch=[
                 pltpu.VMEM((rows, width), BF16),
                 pltpu.VMEM(shape, BF16),
                 pltpu.SemaphoreType.DMA((chips,)),
             ],
         )
-        return blocks
-    both = gains.astype(F32) + other[rows:].astype(F32)
-    summed = jnp.where(
-        jnp.arange(packed)[:, None] % 2 == 0,
-        both + jnp.roll(both, -1, axis=0),
-        0.0,
-    )
-    high = summed.astype(BF16).astype(F32)
-    summed = (high + jnp.roll(summed - high, 1, axis=0)).astype(BF16)
     total = (keep + other[:rows].astype(F32)).astype(BF16)
-    pieces = [jnp.broadcast_to(summed[None], (chips, packed, width))]
+    pieces = []
     first = 0
     for part, step in zip(parts, steps):
         pieces.append(total[first : first + part].reshape(chips, step, width))
         first += part
-    return jnp.concatenate(pieces, axis=1)
+    (gains,) = call(gains_kernel, [like(gains)], 0, gains, other[rows:])
+    return jnp.concatenate(pieces, axis=1), gains
 
 
 def on_device(
@@ -581,9 +563,6 @@
     edge_rows = edges.shape[0]
     tile_rows = senders.shape[1]
     square = 2 * width * width
-    gain_edge = gain_edge.reshape(1, width)
-    gain_node = gain_node.reshape(1, width)
-
     low, mid, high, nodes, send_list = call(
         send_kernel,
         [
@@ -602,54 +581,60 @@
     from_low = passed_along(high, "px", 1)
     from_high = passed_along(low, "px", -1)
     fetched = [
-        w_edge_in,
         senders,
         receivers,
         edges,
+        w_edge_in,
         w_edge_out,
+        gain_edge,
         w_node_in,
         w_node_out,
+        gain_node,
         node_grads,
         edge_grads,
     ]
-    pre_local, receiver_rows, *fetched = call(
-        local_kernel,
-        [shaped(edge_rows, width, F32), shaped(edge_rows, count, BF16)]
+    near_hot, halo_hot, sender_columns, receiver_columns, *fetched = call(
+        functools.partial(index_kernel, len(fetched)),
+        [
+            shaped(edge_rows, 2 * count, BF16),
+            shaped(edge_rows, halo_rows, BF16),
+            shaped(count + halo_rows, edge_rows, BF16),
+            shaped(count, edge_rows, BF16),
+        ]
         + [like(x) for x in fetched],
-        square * (2 * count + edge_rows) + 4 * edge_rows * count * width,
-        nodes,
+        0,
         *fetched,
-        spaces=[VMEM] + [HBM] * len(fetched),
+        spaces=[HBM] * len(fetched),
         scratch=[pltpu.SemaphoreType.DMA((len(fetched),))],
     )
     (
-        w_edge_in,
         senders,
         receivers,
         edges,
+        w_edge_in,
         w_edge_out,
+        gain_edge,
         w_node_in,
         w_node_out,
+        gain_node,
         node_grads,
         edge_grads,
     ) = fetched
-    from_low, from_high, pre_local = lax.optimization_barrier((from_low, from_high, pre_local))
+    from_low, from_high, near_hot = lax.optimization_barrier((from_low, from_high, near_hot))
     upward = passed_along(
         jnp.concatenate([from_high[2 * slots :], mid[slots:], from_low[2 * slots :]]), PY, 1
     )
     downward = passed_along(
         jnp.concatenate([from_high[:slots], mid[:slots], from_low[:slots]]), PY, -1
     )
-    halo_hot, sender_columns, receiver_columns = call(
-        index_kernel,
-        [
-            shaped(edge_rows, halo_rows, BF16),
-            shaped(count + halo_rows, edge_rows, BF16),
-            shaped(count, edge_rows, BF16),
-        ],
-        0,
-        senders,
-        receivers,
+    (pre_local,) = call(
+        local_kernel,
+        [shaped(edge_rows, width, F32)],
+        square * (2 * count + edge_rows) + 4 * edge_rows * count * width,
+        nodes,
+        edges,
+        near_hot,
+        w_edge_in,
     )
     parts = (2 * width, 3 * width // 2)
     halves = sum(parts)
@@ -676,7 +661,7 @@
         edge_grads,
         pre_local,
         halo_hot,
-        receiver_rows,
+        near_hot,
         sender_columns,
         receiver_columns,
         from_high,
@@ -699,12 +684,15 @@
             pltpu.VMEM((4 * width, width), F32),
         ],
     )
-    blocks = blocks_of(parts, keep, gains, across_cores(away))
+    blocks, gains = blocks_of(parts, keep, gains, across_cores(away))
     received = lax.all_to_all(blocks, CHIPS, 0, 0)
-    gains, spread = spread_of(received, gains.shape[0])
-    own = lax.all_to_all(spread, CHIPS, 0, 0)
+    gains = summed_gains(gains)
     up_back = passed_along(up, PY, 1)
     down_back = passed_along(down, PY, -1)
+    received, gains, up_back, down_back = lax.optimization_barrier(
+        (received, gains, up_back, down_back)
+    )
+    own = lax.all_to_all(spread_of(received), CHIPS, 0, 0)
     to_high = passed_along(
         jnp.concatenate([up_back[:slots], down_back[:slots], rest[:slots]]), "px", 1
     )
@@ -742,10 +730,10 @@
         edges_grad,
         w_edge_in_grad,
         w_edge_out_grad,
-        (gains[0] + gains[1]).astype(BF16),
+        (gains[0].astype(F32) + gains[1].astype(F32)).astype(BF16),
         w_node_in_grad,
         w_node_out_grad,
-        (gains[2] + gains[3]).astype(BF16),
+        (gains[2].astype(F32) + gains[3].astype(F32)).astype(BF16),
     )
 
 

time: 65.7 us -> 65.4 us (level)
  waiting for transfers between devices: 24.7 us -> 18 us
  starting transfers between devices: 22.3 us -> 28.8 us
    all_to_all x1, waiting for transfers between devices: 14.9 us -> 0.01 us  [on_device(): received = lax.all_to_all(blocks, CHIPS, 0, 0)]
    ppermute x0 -> x3, waiting for transfers between devices: none -> 8.92 us  [summed_gains(): other = lax.ppermute(gains, axis, [(i, i ^ distance) for i in range(size)])]
    ppermute x0 -> x3, starting transfers between devices: none -> 5.3 us  [summed_gains(): other = lax.ppermute(gains, axis, [(i, i ^ distance) for i in range(size)])]
    all_to_all x1, starting transfers between devices: 3.65 us -> 5.37 us  [on_device(): own = lax.all_to_all(spread_of(received), CHIPS, 0, 0)]
    all_to_all x1, starting transfers between devices: 4.59 us -> 3.59 us  [on_device(): received = lax.all_to_all(blocks, CHIPS, 0, 0)]
    pallas_call x9 -> x12, Pallas kernels: 16.4 us -> 16.2 us  [call(): pl.pallas_call(body, out_shape=outs, in_specs=[pl.BlockSpec(memory_space=...]
  transfers between devices with their start and end apart: 12 -> 15, of which waited for: 6 -> 8; matrix products, arithmetic and copies ran while one was open for 1% -> 1% of each run, Pallas kernels for 11% -> 10%
where the time goes in v6:
time: 65.4 us; the launch traced here: 65 us
  starting transfers between devices  28.8 us (44%)
  waiting for transfers between devices  18 us (28%)
  Pallas kernels  16.2 us (25%)
  between operations  1.44 us (2%)
    pallas_call x12, Pallas kernels, call(): pl.pallas_call(body, out_shape=outs, in_specs=[pl.BlockSpec(memory_space=...  16.2 us
    ppermute x8, starting transfers between devices, passed_along(): lax.ppermute(array, axis, [(i, (i + by) % size) for i in range(size)])  12.7 us
    ppermute x3, waiting for transfers between devices, summed_gains(): other = lax.ppermute(gains, axis, [(i, i ^ distance) for i in range(size)])  8.92 us
    ppermute x8, waiting for transfers between devices, passed_along(): lax.ppermute(array, axis, [(i, (i + by) % size) for i in range(size)])  6.1 us
    all_to_all x1, starting transfers between devices, on_device(): own = lax.all_to_all(spread_of(received), CHIPS, 0, 0)  5.37 us
    ppermute x3, starting transfers between devices, summed_gains(): other = lax.ppermute(gains, axis, [(i, i ^ distance) for i in range(size)])  5.3 us
    all_to_all x1, starting transfers between devices, on_device(): received = lax.all_to_all(blocks, CHIPS, 0, 0)  3.59 us
    ppermute x2, waiting for transfers between devices, across_cores(): return lax.ppermute(array, CORE, [(0, 1), (1, 0)])  2.73 us
  transfers between devices with their start and end apart: 15, of which 8 were waited for; matrix products, arithmetic and copies ran while one was open for 1% of the time, Pallas kernels for 10%

profile of v6, /device:TPU:0, one launch (start us, length us, event | category | flops | bytes accessed | tf_op | source)
XLA Modules:
  0.0 65.0 jit_solution(17084543060244309411)
XLA Ops:
  0.6 1.3 %shard_map.197 = (bf16[96,256]{1,0:T(8,128)(2,1)S(1)}, bf16[64,256]{1,0:T(8,128)(2,1)S(1)}, bf16[96,256]{1,0:T(8,128)(2,1)S(1)}, bf16[384,256]{1,0:T(8,128)(2,1)S(1)}, s32[8,32]{1,0:T(8,128)S(1)}) custom-call(bf16[384,256]{1,0:T(8,128)(2,1)} %nodes_hbm.1, s32[8,32]{1,0:T(8,128)} %list_hbm.1), custom_call_target="tpu_custom_call" | custom-call | flops 50331648 | bytes 526336 | tf_op jit(solution)/shard_map/pallas_call | solution.py:435
  1.9 3.1 %collective-permute-start = (bf16[96,256]{1,0:T(8,128)(2,1)S(1)}, bf16[96,256]{1,0:T(8,128)(2,1)S(1)}, u32[]{:S(2)}, u32[]{:S(2)}) collective-permute-start(bf16[96,256]{1,0:T(8,128)(2,1)S(1)} %get-tuple-element.58), channel_id=1, source_target_pairs={{0,4},{4,8},{8,12},{12,0},{1,5},{5,9},{9,13},{13,1},{2,6},{6,10},{... | collective-permute-start | bytes 147464 | tf_op jit(solution)/shard_map/ppermute | solution.py:23
  5.0 2.1 %collective-permute-start.1 = (bf16[96,256]{1,0:T(8,128)(2,1)S(1)}, bf16[96,256]{1,0:T(8,128)(2,1)S(1)}, u32[]{:S(2)}, u32[]{:S(2)}) collective-permute-start(bf16[96,256]{1,0:T(8,128)(2,1)S(1)} %get-tuple-element.59), channel_id=1, source_target_pairs={{0,12},{4,0},{8,4},{12,8},{1,13},{5,1},{9,5},{13,9},{2,14},{6,2},{... | collective-permute-start | bytes 147464 | tf_op jit(solution)/shard_map/ppermute | solution.py:23
  7.8 2.9 %shard_map.198 = (bf16[1152,768]{1,0:T(8,128)(2,1)S(1)}, bf16[1152,256]{1,0:T(8,128)(2,1)S(1)}, bf16[640,1152]{1,0:T(8,128)(2,1)S(1)}, bf16[384,1152]{1,0:T(8,12...) custom-call(s32[9,128]{1,0:T(8,128)} %refs_0_.1, ...), custom_call_target="tpu_custom_call" | custom-call | bytes 9326592 | tf_op jit(solution)/shard_map/pallas_call | solution.py:435
  10.7 0.0 collective-permute-done.from_low
  10.7 0.0 collective-permute-done.1.from_high
  10.7 0.1 collective-permute-start.2
  10.8 1.7 %collective-permute-start.3 = (bf16[96,256]{1,0:T(8,128)(2,1)S(1)}, bf16[96,256]{1,0:T(8,128)(2,1)S(1)}, u32[]{:S(2)}, u32[]{:S(2)}) collective-permute-start(bf16[96,256]{1,0:T(8,128)(2,1)S(1)} %pad_maximum_fusion.1), channel_id=1, source_target_pairs={{0,3},{1,0},{2,1},{3,2},{4,7},{5,4},{6,5},{7,6},{8,11},{9,8},{10,9... | collective-permute-start | bytes 147464 | tf_op jit(solution)/shard_map/ppermute | solution.py:23
  12.5 1.0 %shard_map.199.pre_local = f32[1152,256]{1,0:T(8,128)S(1)} custom-call(bf16[384,256]{1,0:T(8,128)(2,1)S(1)} %get-tuple-element.54.nodes, bf16[1152,256]{1,0:T(8,128)(2,1)S(1)} %get-tuple-element.56.edges, bf16[1152,768]{1,0:T(8,128)(2,1)S(1)} %get-tuple-element.61.near_rows, bf16[768,256]{1,0:T(8,128)(2,1)S(1)} %get-tuple-element.62.w_in), custom_call_target="tpu_custom_call" | custom-call | flops 704643072 | bytes 4128768 | tf_op jit(solution)/shard_map/pallas_call | solution.py:435
  13.5 0.8 %collective-permute-done.2.upward = bf16[96,256]{1,0:T(8,128)(2,1)S(1)} collective-permute-done((bf16[96,256]{1,0:T(8,128)(2,1)S(1)}, bf16[96,256]{1,0:T(8,128)(2,1)S(1)}, u32[]{:S(2)}, u32[]{:S(2)}) %collective-permute-start.2) | collective-permute-done | bytes 49184 | tf_op jit(solution)/shard_map/ppermute | solution.py:23
  14.3 0.0 collective-permute-done.3.downward
  14.3 5.6 %shard_map.200 = (bf16[1152,256]{1,0:T(8,128)(2,1)S(1)}, bf16[384,256]{1,0:T(8,128)(2,1)S(1)}, bf16[384,256]{1,0:T(8,128)(2,1)S(1)}, f32[384,256]{1,0:T(8,128)S(...) custom-call(s32[1]{0:T(128)S(6)} %copy.22.count_ref, ...), custom_call_target="tpu_custom_call" | custom-call | flops 2583691264 | bytes 11486212 | tf_op jit(solution)/shard_map/pallas_call | solution.py:435
  19.9 1.8 %collective-permute-start.4 = (bf16[912,256]{1,0:T(8,128)(2,1)S(1)}, bf16[912,256]{1,0:T(8,128)(2,1)S(1)}, u32[]{:S(2)}, u32[]{:S(2)}) collective-permute-start(bf16[912,256]{1,0:T(8,128)(2,1)S(1)} %get-tuple-element.76), channel_id=1, source_target_pairs={{0,1},{1,0},{2,3},{3,2},{4,5},{5,4},{6,7},{7,6},{8,9},{9,8},{10,11... | collective-permute-start | bytes 1400840 | tf_op jit(solution)/shard_map/ppermute | solution.py:27
  21.7 1.5 %collective-permute-done.4.other = bf16[912,256]{1,0:T(8,128)(2,1)S(1)} collective-permute-done((bf16[912,256]{1,0:T(8,128)(2,1)S(1)}, bf16[912,256]{1,0:T(8,128)(2,1)S(1)}, u32[]{:S(2)}, u32[]{:S(2)}) %collective-permute-start.4) | collective-permute-done | bytes 466976 | tf_op jit(solution)/shard_map/ppermute | solution.py:27
  23.2 0.8 %shard_map.201 = (bf16[8,112,256]{2,1,0:T(8,128)(2,1)}, bf16[16,256]{1,0:T(8,128)(2,1)S(1)}) custom-call(f32[896,256]{1,0:T(8,128)S(1)} %get-tuple-element.74.keep, bf16[16,256]{1,0:T(8,128)(2,1)S(1)} %get-tuple-element.75.gains, bf16[912,256]{1,0:T(8,128)(2,1)S(1)} %collective-permute-done.4.other), custom_call_target="tpu_custom_call" | custom-call | bytes 1859584 | tf_op jit(solution)/shard_map/pallas_call | solution.py:435
  24.0 3.6 %all-to-all-start = ((bf16[8,112,256]{2,1,0:T(8,128)(2,1)}), bf16[8,112,256]{2,1,0:T(8,128)(2,1)S(1)}, u32[]{:S(2)}, u32[]{:S(2)}) async-start(bf16[8,112,256]{2,1,0:T(8,128)(2,1)} %get-tuple-element.77), calls=%async_computation | async-start | bytes 917504 | tf_op jit(solution)/shard_map/all_to_all | solution.py:688
  27.6 0.3 collective-permute-start.8
  27.9 1.4 %collective-permute-start.9 = (bf16[96,256]{1,0:T(8,128)(2,1)S(1)}, bf16[96,256]{1,0:T(8,128)(2,1)S(1)}, u32[]{:S(2)}, u32[]{:S(2)}) collective-permute-start(bf16[96,256]{1,0:T(8,128)(2,1)S(1)} %get-tuple-element.80), channel_id=1, source_target_pairs={{0,3},{1,0},{2,1},{3,2},{4,7},{5,4},{6,5},{7,6},{8,11},{9,8},{10,9... | collective-permute-start | bytes 147464 | tf_op jit(solution)/shard_map/ppermute | solution.py:23
  29.4 2.0 %collective-permute-start.5 = (bf16[16,256]{1,0:T(8,128)(2,1)S(1)}, bf16[16,256]{1,0:T(8,128)(2,1)S(1)}, u32[]{:S(2)}, u32[]{:S(2)}) collective-permute-start(bf16[16,256]{1,0:T(8,128)(2,1)S(1)} %get-tuple-element.78.own), channel_id=1, source_target_pairs={{0,2},{2,0},{1,3},{3,1},{4,6},{6,4},{5,7},{7,5},{8,10},{10,8},{9,1... | collective-permute-start | bytes 24584 | tf_op jit(solution)/shard_map/ppermute | solution.py:508
  31.4 3.9 %collective-permute-done.5.other = bf16[16,256]{1,0:T(8,128)(2,1)S(1)} collective-permute-done((bf16[16,256]{1,0:T(8,128)(2,1)S(1)}, bf16[16,256]{1,0:T(8,128)(2,1)S(1)}, u32[]{:S(2)}, u32[]{:S(2)}) %collective-permute-start.5) | collective-permute-done | bytes 8224 | tf_op jit(solution)/shard_map/ppermute | solution.py:508
  35.3 0.6 collective-permute-start.6
  35.9 3.1 %collective-permute-done.6.other = bf16[16,256]{1,0:T(8,128)(2,1)S(1)} collective-permute-done((bf16[16,256]{1,0:T(8,128)(2,1)S(1)}, bf16[16,256]{1,0:T(8,128)(2,1)S(1)}, u32[]{:S(2)}, u32[]{:S(2)}) %collective-permute-start.6) | collective-permute-done | bytes 8224 | tf_op jit(solution)/shard_map/ppermute | solution.py:508
  39.0 2.7 %collective-permute-start.7 = (bf16[16,256]{1,0:T(8,128)(2,1)S(1)}, bf16[16,256]{1,0:T(8,128)(2,1)S(1)}, u32[]{:S(2)}, u32[]{:S(2)}) collective-permute-start(bf16[16,256]{1,0:T(8,128)(2,1)S(1)} %shard_map.203.own), channel_id=1, source_target_pairs={{0,8},{4,12},{8,0},{12,4},{1,9},{5,13},{9,1},{13,5},{2,10},{6,14},... | collective-permute-start | bytes 24584 | tf_op jit(solution)/shard_map/ppermute | solution.py:508
  41.7 1.9 %collective-permute-done.7.other = bf16[16,256]{1,0:T(8,128)(2,1)S(1)} collective-permute-done((bf16[16,256]{1,0:T(8,128)(2,1)S(1)}, bf16[16,256]{1,0:T(8,128)(2,1)S(1)}, u32[]{:S(2)}, u32[]{:S(2)}) %collective-permute-start.7) | collective-permute-done | bytes 8224 | tf_op jit(solution)/shard_map/ppermute | solution.py:508
  43.7 0.0 collective-permute-done.8.up_back
  43.7 0.0 collective-permute-done.9.down_back
  43.7 0.0 all-to-all-done.received
  43.7 0.9 %shard_map.205 = bf16[8,112,256]{2,1,0:T(8,128)(2,1)} custom-call(bf16[8,112,256]{2,1,0:T(8,128)(2,1)S(1)} %all-to-all-done.received), custom_call_target="tpu_custom_call" | custom-call | bytes 917504 | tf_op jit(solution)/shard_map/pallas_call | solution.py:435
  44.6 5.4 %all-to-all-start.1 = ((bf16[8,112,256]{2,1,0:T(8,128)(2,1)}), bf16[8,112,256]{2,1,0:T(8,128)(2,1)S(1)}, u32[]{:S(2)}, u32[]{:S(2)}) async-start(bf16[8,112,256]{2,1,0:T(8,128)(2,1)} %shard_map.205), calls=%async_computation.1 | async-start | bytes 917504 | tf_op jit(solution)/shard_map/all_to_all | solution.py:695
  50.0 2.1 %collective-permute-start.10 = (bf16[96,256]{1,0:T(8,128)(2,1)S(1)}, bf16[96,256]{1,0:T(8,128)(2,1)S(1)}, u32[]{:S(2)}, u32[]{:S(2)}) collective-permute-start(bf16[96,256]{1,0:T(8,128)(2,1)S(1)} %pad_maximum_fusion.2), channel_id=1, source_target_pairs={{0,4},{4,8},{8,12},{12,0},{1,5},{5,9},{9,13},{13,1},{2,6},{6,10},{... | collective-permute-start | bytes 147464 | tf_op jit(solution)/shard_map/ppermute | solution.py:23
  52.1 1.9 %collective-permute-start.11 = (bf16[96,256]{1,0:T(8,128)(2,1)S(1)}, bf16[96,256]{1,0:T(8,128)(2,1)S(1)}, u32[]{:S(2)}, u32[]{:S(2)}) collective-permute-start(bf16[96,256]{1,0:T(8,128)(2,1)S(1)} %pad_maximum_fusion.3), channel_id=1, source_target_pairs={{0,12},{4,0},{8,4},{12,8},{1,13},{5,1},{9,5},{13,9},{2,14},{6,2},{... | collective-permute-start | bytes 147464 | tf_op jit(solution)/shard_map/ppermute | solution.py:23
  54.0 1.3 %shard_map.206 = (bf16[1152,256]{1,0:T(8,128)(2,1)}, f32[384,256]{1,0:T(8,128)S(1)}) custom-call(bf16[1152,256]{1,0:T(8,128)(2,1)S(1)} %get-tuple-element.57.edge_grads, bf16[1152,256]{1,0:T(8,128)(2,1)S(1)} %get-tuple-element.83.pre_grad, bf16[384,256]{1,0:T(8,128)(2,1)S(1)} %get-tuple-element.84.sender_sum, ...), custom_call_target="tpu_custom_call" | custom-call | flops 251658240 | bytes 3342336 | tf_op jit(solution)/shard_map/pallas_call | solution.py:435
  55.3 5.3 %collective-permute-done.10.to_high = bf16[96,256]{1,0:T(8,128)(2,1)S(1)} collective-permute-done((bf16[96,256]{1,0:T(8,128)(2,1)S(1)}, bf16[96,256]{1,0:T(8,128)(2,1)S(1)}, u32[]{:S(2)}, u32[]{:S(2)}) %collective-permute-start.10) | collective-permute-done | bytes 49184 | tf_op jit(solution)/shard_map/ppermute | solution.py:23
  60.6 0.0 collective-permute-done.11.to_low
  60.6 1.1 %shard_map.207 = bf16[384,256]{1,0:T(8,128)(2,1)} custom-call(s32[8,32]{1,0:T(8,128)S(1)} %get-tuple-element.82.send_list, f32[384,256]{1,0:T(8,128)S(1)} %get-tuple-element.87.local_grad, bf16[96,256]{1,0:T(8,128)(2,1)S(1)} %collective-permute-done.8.up_back, bf16[96,256]{1,0:T(8,128)(2,1)S(1)} %collective-permute-done.9.down_back, ...), custom_call_target="tpu_custom_call" | custom-call | flops 50331648 | bytes 787456 | tf_op jit(solution)/shard_map/pallas_call | solution.py:435
  61.7 0.3 all-to-all-done.1.own
  62.0 0.0 collective-permute-start.12
  62.0 0.5 convert_reduce_fusion
  62.6 1.3 %collective-permute-done.12.other = bf16[8,112,256]{2,1,0:T(8,128)(2,1)S(1)} collective-permute-done((bf16[8,112,256]{2,1,0:T(8,128)(2,1)S(1)}, bf16[8,112,256]{2,1,0:T(8,128)(2,1)S(1)}, u32[]{:S(2)}, u32[]{:S(2)}) %collective-permute-start.12) | collective-permute-done | bytes 458784 | tf_op jit(solution)/shard_map/ppermute | solution.py:27
  63.8 1.2 %shard_map.208 = (bf16[768,256]{1,0:T(8,128)(2,1)}, bf16[256,256]{1,0:T(8,128)(2,1)}, bf16[512,256]{1,0:T(8,128)(2,1)}, bf16[256,256]{1,0:T(8,128)(2,1)}) custom-call(bf16[8,112,256]{2,1,0:T(8,128)(2,1)S(1)} %all-to-all-done.1.own, bf16[8,112,256]{2,1,0:T(8,128)(2,1)S(1)} %collective-permute-done.12.other), custom_call_target="tpu_custom_call" | custom-call | bytes 1835008 | tf_op jit(solution)/shard_map/pallas_call | solution.py:435
  (12 shorter events, 0.1 us)
Async XLA Ops:
  1.9 8.7 %collective-permute-start = (bf16[96,256]{1,0:T(8,128)(2,1)S(1)}, bf16[96,256]{1,0:T(8,128)(2,1)S(1)}, u32[]{:S(2)}, u32[]{:S(2)}) collective-permute-start(bf16[96,256]{1,0:T(8,128)(2,1)S(1)} %get-tuple-element.58), channel_id=1, source_target_pairs={{0,4},{4,8},{8,12},{12,0},{1,5},{5,9},{9,13},{13,1},{2,6},{6,10},{... | collective-permute-start | bytes 147464 | tf_op jit(solution)/shard_map/ppermute | solution.py:23
  5.0 5.7 %collective-permute-start.1 = (bf16[96,256]{1,0:T(8,128)(2,1)S(1)}, bf16[96,256]{1,0:T(8,128)(2,1)S(1)}, u32[]{:S(2)}, u32[]{:S(2)}) collective-permute-start(bf16[96,256]{1,0:T(8,128)(2,1)S(1)} %get-tuple-element.59), channel_id=1, source_target_pairs={{0,12},{4,0},{8,4},{12,8},{1,13},{5,1},{9,5},{13,9},{2,14},{6,2},{... | collective-permute-start | bytes 147464 | tf_op jit(solution)/shard_map/ppermute | solution.py:23
  10.7 3.6 %collective-permute-start.2 = (bf16[96,256]{1,0:T(8,128)(2,1)S(1)}, bf16[96,256]{1,0:T(8,128)(2,1)S(1)}, u32[]{:S(2)}, u32[]{:S(2)}) collective-permute-start(bf16[96,256]{1,0:T(8,128)(2,1)S(1)} %pad_maximum_fusion), channel_id=1, source_target_pairs={{0,1},{1,2},{2,3},{3,0},{4,5},{5,6},{6,7},{7,4},{8,9},{9,10},{10,1... | collective-permute-start | bytes 147464 | tf_op jit(solution)/shard_map/ppermute | solution.py:23
  10.8 3.5 %collective-permute-start.3 = (bf16[96,256]{1,0:T(8,128)(2,1)S(1)}, bf16[96,256]{1,0:T(8,128)(2,1)S(1)}, u32[]{:S(2)}, u32[]{:S(2)}) collective-permute-start(bf16[96,256]{1,0:T(8,128)(2,1)S(1)} %pad_maximum_fusion.1), channel_id=1, source_target_pairs={{0,3},{1,0},{2,1},{3,2},{4,7},{5,4},{6,5},{7,6},{8,11},{9,8},{10,9... | collective-permute-start | bytes 147464 | tf_op jit(solution)/shard_map/ppermute | solution.py:23
  19.9 3.3 %collective-permute-start.4 = (bf16[912,256]{1,0:T(8,128)(2,1)S(1)}, bf16[912,256]{1,0:T(8,128)(2,1)S(1)}, u32[]{:S(2)}, u32[]{:S(2)}) collective-permute-start(bf16[912,256]{1,0:T(8,128)(2,1)S(1)} %get-tuple-element.76), channel_id=1, source_target_pairs={{0,1},{1,0},{2,3},{3,2},{4,5},{5,4},{6,7},{7,6},{8,9},{9,8},{10,11... | collective-permute-start | bytes 1400840 | tf_op jit(solution)/shard_map/ppermute | solution.py:27
  24.0 19.7 %all-to-all-start = ((bf16[8,112,256]{2,1,0:T(8,128)(2,1)}), bf16[8,112,256]{2,1,0:T(8,128)(2,1)S(1)}, u32[]{:S(2)}, u32[]{:S(2)}) async-start(bf16[8,112,256]{2,1,0:T(8,128)(2,1)} %get-tuple-element.77), calls=%async_computation | async-start | bytes 917504 | tf_op jit(solution)/shard_map/all_to_all | solution.py:688
  27.6 16.0 %collective-permute-start.8 = (bf16[96,256]{1,0:T(8,128)(2,1)S(1)}, bf16[96,256]{1,0:T(8,128)(2,1)S(1)}, u32[]{:S(2)}, u32[]{:S(2)}) collective-permute-start(bf16[96,256]{1,0:T(8,128)(2,1)S(1)} %get-tuple-element.79), channel_id=1, source_target_pairs={{0,1},{1,2},{2,3},{3,0},{4,5},{5,6},{6,7},{7,4},{8,9},{9,10},{10,1... | collective-permute-start | bytes 147464 | tf_op jit(solution)/shard_map/ppermute | solution.py:23
  27.9 15.7 %collective-permute-start.9 = (bf16[96,256]{1,0:T(8,128)(2,1)S(1)}, bf16[96,256]{1,0:T(8,128)(2,1)S(1)}, u32[]{:S(2)}, u32[]{:S(2)}) collective-permute-start(bf16[96,256]{1,0:T(8,128)(2,1)S(1)} %get-tuple-element.80), channel_id=1, source_target_pairs={{0,3},{1,0},{2,1},{3,2},{4,7},{5,4},{6,5},{7,6},{8,11},{9,8},{10,9... | collective-permute-start | bytes 147464 | tf_op jit(solution)/shard_map/ppermute | solution.py:23
  29.4 5.9 %collective-permute-start.5 = (bf16[16,256]{1,0:T(8,128)(2,1)S(1)}, bf16[16,256]{1,0:T(8,128)(2,1)S(1)}, u32[]{:S(2)}, u32[]{:S(2)}) collective-permute-start(bf16[16,256]{1,0:T(8,128)(2,1)S(1)} %get-tuple-element.78.own), channel_id=1, source_target_pairs={{0,2},{2,0},{1,3},{3,1},{4,6},{6,4},{5,7},{7,5},{8,10},{10,8},{9,1... | collective-permute-start | bytes 24584 | tf_op jit(solution)/shard_map/ppermute | solution.py:508
  35.3 3.7 %collective-permute-start.6 = (bf16[16,256]{1,0:T(8,128)(2,1)S(1)}, bf16[16,256]{1,0:T(8,128)(2,1)S(1)}, u32[]{:S(2)}, u32[]{:S(2)}) collective-permute-start(bf16[16,256]{1,0:T(8,128)(2,1)S(1)} %shard_map.202.own), channel_id=1, source_target_pairs={{0,4},{4,0},{8,12},{12,8},{1,5},{5,1},{9,13},{13,9},{2,6},{6,2},{1... | collective-permute-start | bytes 24584 | tf_op jit(solution)/shard_map/ppermute | solution.py:508
  39.0 4.6 %collective-permute-start.7 = (bf16[16,256]{1,0:T(8,128)(2,1)S(1)}, bf16[16,256]{1,0:T(8,128)(2,1)S(1)}, u32[]{:S(2)}, u32[]{:S(2)}) collective-permute-start(bf16[16,256]{1,0:T(8,128)(2,1)S(1)} %shard_map.203.own), channel_id=1, source_target_pairs={{0,8},{4,12},{8,0},{12,4},{1,9},{5,13},{9,1},{13,5},{2,10},{6,14},... | collective-permute-start | bytes 24584 | tf_op jit(solution)/shard_map/ppermute | solution.py:508
  44.6 17.4 %all-to-all-start.1 = ((bf16[8,112,256]{2,1,0:T(8,128)(2,1)}), bf16[8,112,256]{2,1,0:T(8,128)(2,1)S(1)}, u32[]{:S(2)}, u32[]{:S(2)}) async-start(bf16[8,112,256]{2,1,0:T(8,128)(2,1)} %shard_map.205), calls=%async_computation.1 | async-start | bytes 917504 | tf_op jit(solution)/shard_map/all_to_all | solution.py:695
  50.0 10.6 %collective-permute-start.10 = (bf16[96,256]{1,0:T(8,128)(2,1)S(1)}, bf16[96,256]{1,0:T(8,128)(2,1)S(1)}, u32[]{:S(2)}, u32[]{:S(2)}) collective-permute-start(bf16[96,256]{1,0:T(8,128)(2,1)S(1)} %pad_maximum_fusion.2), channel_id=1, source_target_pairs={{0,4},{4,8},{8,12},{12,0},{1,5},{5,9},{9,13},{13,1},{2,6},{6,10},{... | collective-permute-start | bytes 147464 | tf_op jit(solution)/shard_map/ppermute | solution.py:23
  52.1 8.5 %collective-permute-start.11 = (bf16[96,256]{1,0:T(8,128)(2,1)S(1)}, bf16[96,256]{1,0:T(8,128)(2,1)S(1)}, u32[]{:S(2)}, u32[]{:S(2)}) collective-permute-start(bf16[96,256]{1,0:T(8,128)(2,1)S(1)} %pad_maximum_fusion.3), channel_id=1, source_target_pairs={{0,12},{4,0},{8,4},{12,8},{1,13},{5,1},{9,5},{13,9},{2,14},{6,2},{... | collective-permute-start | bytes 147464 | tf_op jit(solution)/shard_map/ppermute | solution.py:23
  62.0 1.8 %collective-permute-start.12 = (bf16[8,112,256]{2,1,0:T(8,128)(2,1)S(1)}, bf16[8,112,256]{2,1,0:T(8,128)(2,1)S(1)}, u32[]{:S(2)}, u32[]{:S(2)}) collective-permute-start(bf16[8,112,256]{2,1,0:T(8,128)(2,1)S(1)} %all-to-all-done.1.own), channel_id=1, source_target_pairs={{0,1},{1,0},{2,3},{3,2},{4,5},{5,4},{6,7},{7,6},{8,9},{9,8},{10,11... | collective-permute-start | bytes 1376264 | tf_op jit(solution)/shard_map/ppermute | solution.py:27

commit v7 on v6

--- a/solution.py
+++ b/solution.py
@@ -47,6 +47,26 @@
     centered = value - jnp.mean(value, axis=-1, keepdims=True)
     scale_inv = lax.rsqrt(jnp.mean(centered * centered, axis=-1, keepdims=True) + EPS)
     return centered * scale_inv, scale_inv
+
+
+def row_mean(value, split):
+    width = value.shape[1]
+    high = value.astype(BF16)
+    if split:
+        high = jnp.concatenate([high, (value - high.astype(F32)).astype(BF16)], axis=1)
+    return dot(high, jnp.full((high.shape[1], width), 1.0 / width, BF16))
+
+
+def normalize_wide(value):
+    centered = value - row_mean(value, True)
+    scale_inv = lax.rsqrt(row_mean(centered * centered, False) + EPS)
+    return centered * scale_inv, scale_inv
+
+
+def norm_back_wide(normed, scale_inv, gain, upstream):
+    scaled = upstream * gain
+    inner = scaled - row_mean(scaled, True) - normed * row_mean(scaled * normed, False)
+    return inner * scale_inv
 
 
 def norm_back(normed, scale_inv, gain, upstream):
@@ -242,9 +262,9 @@
     hidden = (value * sigma).astype(BF16)
     hidden_kept[...] = hidden
     slope_kept[...] = sigma * (1.0 + value * (1.0 - sigma))
-    edge_normed, edge_scale = normalize(dot(hidden, w_out[...]))
+    edge_normed, edge_scale = normalize_wide(dot(hidden, w_out[...]))
     normed_kept[...] = edge_normed
-    scale_kept[...] = jnp.broadcast_to(edge_scale, (edge_rows, 128))
+    scale_kept[...] = edge_scale
     message = (live * gain * edge_normed).astype(BF16)
     total = dot(receiver_columns[...], message)
     aggregated = total.astype(BF16)
@@ -270,7 +290,7 @@
     )
     edge_normed = normed_kept[...]
     edge_gain = jnp.sum(upstream * edge_normed, axis=0, keepdims=True)
-    out_grad = norm_back(edge_normed, scale_kept[:, :1], gain, upstream).astype(BF16)
+    out_grad = norm_back_wide(edge_normed, scale_kept[...], gain, upstream).astype(BF16)
     pre_grad = (dot_nt(out_grad, w_out[...]) * slope_kept[...]).astype(BF16)
     pre_grad_out[...] = pre_grad
     sender_total = dot(sender_columns[...], pre_grad)
@@ -296,22 +316,17 @@
     gains_out[...] = gains
 
 
-def add_gains(own, other):
-    both = own.astype(F32) + other.astype(F32)
-    return pack_gains(both[0:1] + both[1:2], both[2:3] + both[3:4])
-
-
-def gains_kernel(own, other, gains_out):
-    gains_out[...] = add_gains(own[...], other[...])
-
-
-def pair_kernel(parts, keep, gains, other, blocks_out, gains_out, total, staged, sems):
+def pair_kernel(parts, keep, gains, other, blocks_out, total, staged, sems):
     rows = keep.shape[0]
     chips = blocks_out.shape[0]
+    packed = gains.shape[0]
+    both = gains[...].astype(F32) + other[rows:].astype(F32)
+    summed = pack_gains(both[0:1] + both[1:2], both[2:3] + both[3:4])
     total[...] = (keep[...] + other[:rows].astype(F32)).astype(BF16)
     copies = []
     for chip in range(chips):
-        first, at = 0, 0
+        staged[chip, :packed, :] = summed
+        first, at = 0, packed
         for part in parts:
             step = part // chips
             staged[chip, at : at + step, :] = total[first + chip * step : first + (chip + 1) * step]
@@ -320,16 +335,16 @@
             pltpu.make_async_copy(staged.at[chip], blocks_out.at[chip], sems.at[chip])
         )
         copies[-1].start()
-    gains_out[...] = add_gains(gains[...], other[rows:])
     for copy in copies:
         copy.wait()
 
 
-def spread_kernel(received, spread_out, mine, sems):
+def spread_kernel(packed, received, gains_out, spread_out, mine, sems):
     sums = received[0].astype(F32)
     for chip in range(1, received.shape[0]):
         sums = sums + received[chip].astype(F32)
-    mine[...] = sums.astype(BF16)
+    gains_out[...] = sums[:packed]
+    mine[...] = sums[packed:].astype(BF16)
     copies = [
         pltpu.make_async_copy(mine, spread_out.at[chip], sems.at[chip])
         for chip in range(received.shape[0])
@@ -485,60 +500,60 @@
     return results
 
 
-def spread_of(received):
+def spread_of(received, packed):
     chips, rows, width = received.shape
-    if rows % 16 == 0:
+    mine = rows - packed
+    if mine % 16 == 0:
         return call(
-            spread_kernel,
-            [like(received)],
+            functools.partial(spread_kernel, packed),
+            [shaped(packed, width, F32), jax.ShapeDtypeStruct((chips, mine, width), BF16)],
             0,
             received,
-            out_space=HBM,
-            scratch=[pltpu.VMEM((rows, width), BF16), pltpu.SemaphoreType.DMA((chips,))],
-        )[0]
+            out_space=[VMEM, HBM],
+            scratch=[pltpu.VMEM((mine, width), BF16), pltpu.SemaphoreType.DMA((chips,))],
+        )
     sums = jnp.sum(received.astype(F32), axis=0)
-    return jnp.broadcast_to(sums.astype(BF16)[None], received.shape)
-
-
-def summed_gains(gains):
-    for axis in ("side", "px"):
-        size = lax.axis_size(axis)
-        distance = 1
-        while distance < size:
-            other = lax.ppermute(gains, axis, [(i, i ^ distance) for i in range(size)])
-            (gains,) = call(gains_kernel, [like(gains)], 0, gains, other)
-            distance *= 2
-    return gains
+    return sums[:packed], jnp.broadcast_to(sums[packed:].astype(BF16)[None], (chips, mine, width))
 
 
 def blocks_of(parts, keep, gains, other):
     chips = lax.axis_size(CHIPS)
     rows, width = keep.shape
+    packed = gains.shape[0]
     steps = [part // chips for part in parts]
-    shape = (chips, sum(steps), width)
+    shape = (chips, packed + sum(steps), width)
+    body = functools.partial(pair_kernel, parts)
     if all(x % 16 == 0 for x in steps):
-        return call(
-            functools.partial(pair_kernel, parts),
-            [jax.ShapeDtypeStruct(shape, BF16), like(gains)],
+        (blocks,) = call(
+            body,
+            [jax.ShapeDtypeStruct(shape, BF16)],
             0,
             keep,
             gains,
             other,
-            out_space=[HBM, VMEM],
+            out_space=HBM,
             scratch=[
                 pltpu.VMEM((rows, width), BF16),
                 pltpu.VMEM(shape, BF16),
                 pltpu.SemaphoreType.DMA((chips,)),
             ],
         )
+        return blocks
+    both = gains.astype(F32) + other[rows:].astype(F32)
+    summed = jnp.where(
+        jnp.arange(packed)[:, None] % 2 == 0,
+        both + jnp.roll(both, -1, axis=0),
+        0.0,
+    )
+    high = summed.astype(BF16).astype(F32)
+    summed = (high + jnp.roll(summed - high, 1, axis=0)).astype(BF16)
     total = (keep + other[:rows].astype(F32)).astype(BF16)
-    pieces = []
+    pieces = [jnp.broadcast_to(summed[None], (chips, packed, width))]
     first = 0
     for part, step in zip(parts, steps):
         pieces.append(total[first : first + part].reshape(chips, step, width))
         first += part
-    (gains,) = call(gains_kernel, [like(gains)], 0, gains, other[rows:])
-    return jnp.concatenate(pieces, axis=1), gains
+    return jnp.concatenate(pieces, axis=1)
 
 
 def on_device(
@@ -679,26 +694,24 @@
             pltpu.VMEM((edge_rows, width), F32),
             pltpu.VMEM((edge_rows, width), BF16),
             pltpu.VMEM((edge_rows, width), F32),
-            pltpu.VMEM((edge_rows, 128), F32),
+            pltpu.VMEM((edge_rows, width), F32),
             pltpu.VMEM((3 * width, width), F32),
             pltpu.VMEM((4 * width, width), F32),
         ],
     )
-    blocks, gains = blocks_of(parts, keep, gains, across_cores(away))
+    blocks = blocks_of(parts, keep, gains, across_cores(away))
     received = lax.all_to_all(blocks, CHIPS, 0, 0)
-    gains = summed_gains(gains)
     up_back = passed_along(up, PY, 1)
     down_back = passed_along(down, PY, -1)
-    received, gains, up_back, down_back = lax.optimization_barrier(
-        (received, gains, up_back, down_back)
-    )
-    own = lax.all_to_all(spread_of(received), CHIPS, 0, 0)
     to_high = passed_along(
         jnp.concatenate([up_back[:slots], down_back[:slots], rest[:slots]]), "px", 1
     )
     to_low = passed_along(
         jnp.concatenate([up_back[2 * slots :], down_back[2 * slots :], rest[slots:]]), "px", -1
     )
+    received, to_high, to_low = lax.optimization_barrier((received, to_high, to_low))
+    gains, spread = spread_of(received, gains.shape[0])
+    own = lax.all_to_all(spread, CHIPS, 0, 0)
     edges_grad, local_grad = call(
         finish_kernel,
         [shaped(edge_rows, width, BF16), shaped(count, width, F32)],
@@ -730,10 +743,10 @@
         edges_grad,
         w_edge_in_grad,
         w_edge_out_grad,
-        (gains[0].astype(F32) + gains[1].astype(F32)).astype(BF16),
+        (gains[0] + gains[1]).astype(BF16),
         w_node_in_grad,
         w_node_out_grad,
-        (gains[2].astype(F32) + gains[3].astype(F32)).astype(BF16),
+        (gains[2] + gains[3]).astype(BF16),
     )
 
 

time: 65.4 us -> 65.9 us (level)
  starting transfers between devices: 28.8 us -> 22.3 us
  waiting for transfers between devices: 18 us -> 24.4 us
  Pallas kernels: 16.2 us -> 16.9 us
    all_to_all x1, waiting for transfers between devices: 0.28 us -> 10.6 us  [on_device(): own = lax.all_to_all(spread, CHIPS, 0, 0)]
    ppermute x3 -> x0, waiting for transfers between devices: 8.92 us -> none  [summed_gains(): other = lax.ppermute(gains, axis, [(i, i ^ distance) for i in range(size)])]
    ppermute x3 -> x0, starting transfers between devices: 5.3 us -> none  [summed_gains(): other = lax.ppermute(gains, axis, [(i, i ^ distance) for i in range(size)])]
    ppermute x8, waiting for transfers between devices: 6.1 us -> 9.24 us  [passed_along(): lax.ppermute(array, axis, [(i, (i + by) % size) for i in range(size)])]
    all_to_all x1, starting transfers between devices: 5.37 us -> 3.48 us  [on_device(): own = lax.all_to_all(spread, CHIPS, 0, 0)]
    all_to_all x1, waiting for transfers between devices: 0.01 us -> 1.89 us  [on_device(): received = lax.all_to_all(blocks, CHIPS, 0, 0)]
    ppermute x8, starting transfers between devices: 12.7 us -> 13.3 us  [passed_along(): lax.ppermute(array, axis, [(i, (i + by) % size) for i in range(size)])]
    pallas_call x12 -> x9, Pallas kernels: 16.2 us -> 16.9 us  [call(): pl.pallas_call(body, out_shape=outs, in_specs=[pl.BlockSpec(memory_space=...]
  transfers between devices with their start and end apart: 15 -> 12, of which waited for: 8 -> 7; matrix products, arithmetic and copies ran while one was open for 1% -> 1% of each run, Pallas kernels for 10% -> 11%
where the time goes in v7:
time: 65.9 us; the launch traced here: 65.5 us
  waiting for transfers between devices  24.4 us (37%)
  starting transfers between devices  22.3 us (34%)
  Pallas kernels  16.9 us (26%)
  between operations  1.4 us (2%)
    pallas_call x9, Pallas kernels, call(): pl.pallas_call(body, out_shape=outs, in_specs=[pl.BlockSpec(memory_space=...  16.9 us
    ppermute x8, starting transfers between devices, passed_along(): lax.ppermute(array, axis, [(i, (i + by) % size) for i in range(size)])  13.3 us
    all_to_all x1, waiting for transfers between devices, on_device(): own = lax.all_to_all(spread, CHIPS, 0, 0)  10.6 us
    ppermute x8, waiting for transfers between devices, passed_along(): lax.ppermute(array, axis, [(i, (i + by) % size) for i in range(size)])  9.24 us
    all_to_all x1, starting transfers between devices, on_device(): received = lax.all_to_all(blocks, CHIPS, 0, 0)  3.59 us
    all_to_all x1, starting transfers between devices, on_device(): own = lax.all_to_all(spread, CHIPS, 0, 0)  3.48 us
    ppermute x2, waiting for transfers between devices, across_cores(): return lax.ppermute(array, CORE, [(0, 1), (1, 0)])  2.67 us
    all_to_all x1, waiting for transfers between devices, on_device(): received = lax.all_to_all(blocks, CHIPS, 0, 0)  1.89 us
  transfers between devices with their start and end apart: 12, of which 7 were waited for; matrix products, arithmetic and copies ran while one was open for 1% of the time, Pallas kernels for 11%

profile of v7, /device:TPU:0, one launch (start us, length us, event | category | flops | bytes accessed | tf_op | source)
XLA Modules:
  0.0 65.5 jit_solution(12902143282260650201)
XLA Ops:
  0.6 1.3 %shard_map.197 = (bf16[96,256]{1,0:T(8,128)(2,1)S(1)}, bf16[64,256]{1,0:T(8,128)(2,1)S(1)}, bf16[96,256]{1,0:T(8,128)(2,1)S(1)}, bf16[384,256]{1,0:T(8,128)(2,1)S(1)}, s32[8,32]{1,0:T(8,128)S(1)}) custom-call(bf16[384,256]{1,0:T(8,128)(2,1)} %nodes_hbm.1, s32[8,32]{1,0:T(8,128)} %list_hbm.1), custom_call_target="tpu_custom_call" | custom-call | flops 50331648 | bytes 526336 | tf_op jit(solution)/shard_map/pallas_call | solution.py:450
  1.9 3.1 %collective-permute-start = (bf16[96,256]{1,0:T(8,128)(2,1)S(1)}, bf16[96,256]{1,0:T(8,128)(2,1)S(1)}, u32[]{:S(2)}, u32[]{:S(2)}) collective-permute-start(bf16[96,256]{1,0:T(8,128)(2,1)S(1)} %get-tuple-element.57), channel_id=1, source_target_pairs={{0,4},{4,8},{8,12},{12,0},{1,5},{5,9},{9,13},{13,1},{2,6},{6,10},{... | collective-permute-start | bytes 147464 | tf_op jit(solution)/shard_map/ppermute | solution.py:23
  5.0 2.1 %collective-permute-start.1 = (bf16[96,256]{1,0:T(8,128)(2,1)S(1)}, bf16[96,256]{1,0:T(8,128)(2,1)S(1)}, u32[]{:S(2)}, u32[]{:S(2)}) collective-permute-start(bf16[96,256]{1,0:T(8,128)(2,1)S(1)} %get-tuple-element.58), channel_id=1, source_target_pairs={{0,12},{4,0},{8,4},{12,8},{1,13},{5,1},{9,5},{13,9},{2,14},{6,2},{... | collective-permute-start | bytes 147464 | tf_op jit(solution)/shard_map/ppermute | solution.py:23
  7.8 2.9 %shard_map.198 = (bf16[1152,768]{1,0:T(8,128)(2,1)S(1)}, bf16[1152,256]{1,0:T(8,128)(2,1)S(1)}, bf16[640,1152]{1,0:T(8,128)(2,1)S(1)}, bf16[384,1152]{1,0:T(8,12...) custom-call(s32[9,128]{1,0:T(8,128)} %refs_0_.1, ...), custom_call_target="tpu_custom_call" | custom-call | bytes 9326592 | tf_op jit(solution)/shard_map/pallas_call | solution.py:450
  10.7 0.0 collective-permute-done.from_low
  10.7 0.0 collective-permute-done.1.from_high
  10.7 0.1 collective-permute-start.2
  10.8 1.7 %collective-permute-start.3 = (bf16[96,256]{1,0:T(8,128)(2,1)S(1)}, bf16[96,256]{1,0:T(8,128)(2,1)S(1)}, u32[]{:S(2)}, u32[]{:S(2)}) collective-permute-start(bf16[96,256]{1,0:T(8,128)(2,1)S(1)} %pad_maximum_fusion.1), channel_id=1, source_target_pairs={{0,3},{1,0},{2,1},{3,2},{4,7},{5,4},{6,5},{7,6},{8,11},{9,8},{10,9... | collective-permute-start | bytes 147464 | tf_op jit(solution)/shard_map/ppermute | solution.py:23
  12.5 1.0 %shard_map.199.pre_local = f32[1152,256]{1,0:T(8,128)S(1)} custom-call(bf16[384,256]{1,0:T(8,128)(2,1)S(1)} %get-tuple-element.53.nodes, bf16[1152,256]{1,0:T(8,128)(2,1)S(1)} %get-tuple-element.55.edges, bf16[1152,768]{1,0:T(8,128)(2,1)S(1)} %get-tuple-element.60.near_rows, bf16[768,256]{1,0:T(8,128)(2,1)S(1)} %get-tuple-element.61.w_in), custom_call_target="tpu_custom_call" | custom-call | flops 704643072 | bytes 4128768 | tf_op jit(solution)/shard_map/pallas_call | solution.py:450
  13.5 0.8 %collective-permute-done.2.upward = bf16[96,256]{1,0:T(8,128)(2,1)S(1)} collective-permute-done((bf16[96,256]{1,0:T(8,128)(2,1)S(1)}, bf16[96,256]{1,0:T(8,128)(2,1)S(1)}, u32[]{:S(2)}, u32[]{:S(2)}) %collective-permute-start.2) | collective-permute-done | bytes 49184 | tf_op jit(solution)/shard_map/ppermute | solution.py:23
  14.3 0.0 collective-permute-done.3.downward
  14.3 6.2 %shard_map.200 = (bf16[1152,256]{1,0:T(8,128)(2,1)S(1)}, bf16[384,256]{1,0:T(8,128)(2,1)S(1)}, bf16[384,256]{1,0:T(8,128)(2,1)S(1)}, f32[384,256]{1,0:T(8,128)S(...) custom-call(s32[1]{0:T(128)S(6)} %copy.22.count_ref, ...), custom_call_target="tpu_custom_call" | custom-call | flops 2583691264 | bytes 11486212 | tf_op jit(solution)/shard_map/pallas_call | solution.py:450
  20.5 1.8 %collective-permute-start.4 = (bf16[912,256]{1,0:T(8,128)(2,1)S(1)}, bf16[912,256]{1,0:T(8,128)(2,1)S(1)}, u32[]{:S(2)}, u32[]{:S(2)}) collective-permute-start(bf16[912,256]{1,0:T(8,128)(2,1)S(1)} %get-tuple-element.75), channel_id=1, source_target_pairs={{0,1},{1,0},{2,3},{3,2},{4,5},{5,4},{6,7},{7,6},{8,9},{9,8},{10,11... | collective-permute-start | bytes 1400840 | tf_op jit(solution)/shard_map/ppermute | solution.py:27
  22.4 0.1 collective-permute-start.5
  22.5 1.4 %collective-permute-done.4.other = bf16[912,256]{1,0:T(8,128)(2,1)S(1)} collective-permute-done((bf16[912,256]{1,0:T(8,128)(2,1)S(1)}, bf16[912,256]{1,0:T(8,128)(2,1)S(1)}, u32[]{:S(2)}, u32[]{:S(2)}) %collective-permute-start.4) | collective-permute-done | bytes 466976 | tf_op jit(solution)/shard_map/ppermute | solution.py:27
  23.8 0.9 %shard_map.201 = bf16[8,128,256]{2,1,0:T(8,128)(2,1)} custom-call(f32[896,256]{1,0:T(8,128)S(1)} %get-tuple-element.73.keep, bf16[16,256]{1,0:T(8,128)(2,1)S(1)} %get-tuple-element.74.gains, bf16[912,256]{1,0:T(8,128)(2,1)S(1)} %collective-permute-done.4.other), custom_call_target="tpu_custom_call" | custom-call | bytes 1916928 | tf_op jit(solution)/shard_map/pallas_call | solution.py:450
  24.7 3.6 %all-to-all-start = ((bf16[8,128,256]{2,1,0:T(8,128)(2,1)}), bf16[8,128,256]{2,1,0:T(8,128)(2,1)S(1)}, u32[]{:S(2)}, u32[]{:S(2)}) async-start(bf16[8,128,256]{2,1,0:T(8,128)(2,1)} %shard_map.201), calls=%async_computation | async-start | bytes 1048576 | tf_op jit(solution)/shard_map/all_to_all | solution.py:703
  28.3 1.5 %collective-permute-start.6 = (bf16[96,256]{1,0:T(8,128)(2,1)S(1)}, bf16[96,256]{1,0:T(8,128)(2,1)S(1)}, u32[]{:S(2)}, u32[]{:S(2)}) collective-permute-start(bf16[96,256]{1,0:T(8,128)(2,1)S(1)} %get-tuple-element.77), channel_id=1, source_target_pairs={{0,3},{1,0},{2,1},{3,2},{4,7},{5,4},{6,5},{7,6},{8,11},{9,8},{10,9... | collective-permute-start | bytes 147464 | tf_op jit(solution)/shard_map/ppermute | solution.py:23
  29.9 0.0 collective-permute-done.5.up_back
  29.9 2.6 %collective-permute-done.6.down_back = bf16[96,256]{1,0:T(8,128)(2,1)S(1)} collective-permute-done((bf16[96,256]{1,0:T(8,128)(2,1)S(1)}, bf16[96,256]{1,0:T(8,128)(2,1)S(1)}, u32[]{:S(2)}, u32[]{:S(2)}) %collective-permute-start.6) | collective-permute-done | bytes 49184 | tf_op jit(solution)/shard_map/ppermute | solution.py:23
  32.5 3.2 %collective-permute-start.7 = (bf16[96,256]{1,0:T(8,128)(2,1)S(1)}, bf16[96,256]{1,0:T(8,128)(2,1)S(1)}, u32[]{:S(2)}, u32[]{:S(2)}) collective-permute-start(bf16[96,256]{1,0:T(8,128)(2,1)S(1)} %pad_maximum_fusion.2), channel_id=1, source_target_pairs={{0,4},{4,8},{8,12},{12,0},{1,5},{5,9},{9,13},{13,1},{2,6},{6,10},{... | collective-permute-start | bytes 147464 | tf_op jit(solution)/shard_map/ppermute | solution.py:23
  35.7 1.6 %collective-permute-start.8 = (bf16[96,256]{1,0:T(8,128)(2,1)S(1)}, bf16[96,256]{1,0:T(8,128)(2,1)S(1)}, u32[]{:S(2)}, u32[]{:S(2)}) collective-permute-start(bf16[96,256]{1,0:T(8,128)(2,1)S(1)} %pad_maximum_fusion.3), channel_id=1, source_target_pairs={{0,12},{4,0},{8,4},{12,8},{1,13},{5,1},{9,5},{13,9},{2,14},{6,2},{... | collective-permute-start | bytes 147464 | tf_op jit(solution)/shard_map/ppermute | solution.py:23
  37.3 5.9 %collective-permute-done.7.to_high = bf16[96,256]{1,0:T(8,128)(2,1)S(1)} collective-permute-done((bf16[96,256]{1,0:T(8,128)(2,1)S(1)}, bf16[96,256]{1,0:T(8,128)(2,1)S(1)}, u32[]{:S(2)}, u32[]{:S(2)}) %collective-permute-start.7) | collective-permute-done | bytes 49184 | tf_op jit(solution)/shard_map/ppermute | solution.py:23
  43.1 0.0 collective-permute-done.8.to_low
  43.1 1.9 %all-to-all-done.received = bf16[8,128,256]{2,1,0:T(8,128)(2,1)S(1)} async-done(((bf16[8,128,256]{2,1,0:T(8,128)(2,1)}), bf16[8,128,256]{2,1,0:T(8,128)(2,1)S(1)}, u32[]{:S(2)}, u32[]{:S(2)}) %all-to-all-start) | async-done | bytes 524320 | tf_op jit(solution)/shard_map/all_to_all | solution.py:703
  45.0 0.9 %shard_map.202 = (f32[16,256]{1,0:T(8,128)S(1)}, bf16[8,112,256]{2,1,0:T(8,128)(2,1)}) custom-call(bf16[8,128,256]{2,1,0:T(8,128)(2,1)S(1)} %all-to-all-done.received), custom_call_target="tpu_custom_call" | custom-call | bytes 999424 | tf_op jit(solution)/shard_map/pallas_call | solution.py:450
  46.0 3.5 %all-to-all-start.1 = ((bf16[8,112,256]{2,1,0:T(8,128)(2,1)}), bf16[8,112,256]{2,1,0:T(8,128)(2,1)S(1)}, u32[]{:S(2)}, u32[]{:S(2)}) async-start(bf16[8,112,256]{2,1,0:T(8,128)(2,1)} %get-tuple-element.80), calls=%async_computation.1 | async-start | bytes 917504 | tf_op jit(solution)/shard_map/all_to_all | solution.py:714
  49.4 1.3 %shard_map.203 = (bf16[1152,256]{1,0:T(8,128)(2,1)}, f32[384,256]{1,0:T(8,128)S(1)}) custom-call(bf16[1152,256]{1,0:T(8,128)(2,1)S(1)} %get-tuple-element.56.edge_grads, bf16[1152,256]{1,0:T(8,128)(2,1)S(1)} %get-tuple-element.82.pre_grad, bf16[384,256]{1,0:T(8,128)(2,1)S(1)} %get-tuple-element.83.sender_sum, ...), custom_call_target="tpu_custom_call" | custom-call | flops 251658240 | bytes 3342336 | tf_op jit(solution)/shard_map/pallas_call | solution.py:450
  50.8 1.1 %shard_map.204 = bf16[384,256]{1,0:T(8,128)(2,1)} custom-call(s32[8,32]{1,0:T(8,128)S(1)} %get-tuple-element.81.send_list, f32[384,256]{1,0:T(8,128)S(1)} %get-tuple-element.86.local_grad, bf16[96,256]{1,0:T(8,128)(2,1)S(1)} %collective-permute-done.5.up_back, bf16[96,256]{1,0:T(8,128)(2,1)S(1)} %collective-permute-done.6.down_back, ...), custom_call_target="tpu_custom_call" | custom-call | flops 50331648 | bytes 787456 | tf_op jit(solution)/shard_map/pallas_call | solution.py:450
  51.9 10.6 %all-to-all-done.1.own = bf16[8,112,256]{2,1,0:T(8,128)(2,1)S(1)} async-done(((bf16[8,112,256]{2,1,0:T(8,128)(2,1)}), bf16[8,112,256]{2,1,0:T(8,128)(2,1)S(1)}, u32[]{:S(2)}, u32[]{:S(2)}) %all-to-all-start.1) | async-done | bytes 458784 | tf_op jit(solution)/shard_map/all_to_all | solution.py:714
  62.5 0.0 collective-permute-start.9
  62.5 0.5 convert_reduce_fusion
  63.0 1.3 %collective-permute-done.9.other = bf16[8,112,256]{2,1,0:T(8,128)(2,1)S(1)} collective-permute-done((bf16[8,112,256]{2,1,0:T(8,128)(2,1)S(1)}, bf16[8,112,256]{2,1,0:T(8,128)(2,1)S(1)}, u32[]{:S(2)}, u32[]{:S(2)}) %collective-permute-start.9) | collective-permute-done | bytes 458784 | tf_op jit(solution)/shard_map/ppermute | solution.py:27
  64.3 1.2 %shard_map.205 = (bf16[768,256]{1,0:T(8,128)(2,1)}, bf16[256,256]{1,0:T(8,128)(2,1)}, bf16[512,256]{1,0:T(8,128)(2,1)}, bf16[256,256]{1,0:T(8,128)(2,1)}) custom-call(bf16[8,112,256]{2,1,0:T(8,128)(2,1)S(1)} %all-to-all-done.1.own, bf16[8,112,256]{2,1,0:T(8,128)(2,1)S(1)} %collective-permute-done.9.other), custom_call_target="tpu_custom_call" | custom-call | bytes 1835008 | tf_op jit(solution)/shard_map/pallas_call | solution.py:450
  (9 shorter events, 0.0 us)
Async XLA Ops:
  1.9 8.7 %collective-permute-start = (bf16[96,256]{1,0:T(8,128)(2,1)S(1)}, bf16[96,256]{1,0:T(8,128)(2,1)S(1)}, u32[]{:S(2)}, u32[]{:S(2)}) collective-permute-start(bf16[96,256]{1,0:T(8,128)(2,1)S(1)} %get-tuple-element.57), channel_id=1, source_target_pairs={{0,4},{4,8},{8,12},{12,0},{1,5},{5,9},{9,13},{13,1},{2,6},{6,10},{... | collective-permute-start | bytes 147464 | tf_op jit(solution)/shard_map/ppermute | solution.py:23
  5.0 5.7 %collective-permute-start.1 = (bf16[96,256]{1,0:T(8,128)(2,1)S(1)}, bf16[96,256]{1,0:T(8,128)(2,1)S(1)}, u32[]{:S(2)}, u32[]{:S(2)}) collective-permute-start(bf16[96,256]{1,0:T(8,128)(2,1)S(1)} %get-tuple-element.58), channel_id=1, source_target_pairs={{0,12},{4,0},{8,4},{12,8},{1,13},{5,1},{9,5},{13,9},{2,14},{6,2},{... | collective-permute-start | bytes 147464 | tf_op jit(solution)/shard_map/ppermute | solution.py:23
  10.7 3.6 %collective-permute-start.2 = (bf16[96,256]{1,0:T(8,128)(2,1)S(1)}, bf16[96,256]{1,0:T(8,128)(2,1)S(1)}, u32[]{:S(2)}, u32[]{:S(2)}) collective-permute-start(bf16[96,256]{1,0:T(8,128)(2,1)S(1)} %pad_maximum_fusion), channel_id=1, source_target_pairs={{0,1},{1,2},{2,3},{3,0},{4,5},{5,6},{6,7},{7,4},{8,9},{9,10},{10,1... | collective-permute-start | bytes 147464 | tf_op jit(solution)/shard_map/ppermute | solution.py:23
  10.8 3.5 %collective-permute-start.3 = (bf16[96,256]{1,0:T(8,128)(2,1)S(1)}, bf16[96,256]{1,0:T(8,128)(2,1)S(1)}, u32[]{:S(2)}, u32[]{:S(2)}) collective-permute-start(bf16[96,256]{1,0:T(8,128)(2,1)S(1)} %pad_maximum_fusion.1), channel_id=1, source_target_pairs={{0,3},{1,0},{2,1},{3,2},{4,7},{5,4},{6,5},{7,6},{8,11},{9,8},{10,9... | collective-permute-start | bytes 147464 | tf_op jit(solution)/shard_map/ppermute | solution.py:23
  20.5 3.3 %collective-permute-start.4 = (bf16[912,256]{1,0:T(8,128)(2,1)S(1)}, bf16[912,256]{1,0:T(8,128)(2,1)S(1)}, u32[]{:S(2)}, u32[]{:S(2)}) collective-permute-start(bf16[912,256]{1,0:T(8,128)(2,1)S(1)} %get-tuple-element.75), channel_id=1, source_target_pairs={{0,1},{1,0},{2,3},{3,2},{4,5},{5,4},{6,7},{7,6},{8,9},{9,8},{10,11... | collective-permute-start | bytes 1400840 | tf_op jit(solution)/shard_map/ppermute | solution.py:27
  22.4 7.5 %collective-permute-start.5 = (bf16[96,256]{1,0:T(8,128)(2,1)S(1)}, bf16[96,256]{1,0:T(8,128)(2,1)S(1)}, u32[]{:S(2)}, u32[]{:S(2)}) collective-permute-start(bf16[96,256]{1,0:T(8,128)(2,1)S(1)} %get-tuple-element.76), channel_id=1, source_target_pairs={{0,1},{1,2},{2,3},{3,0},{4,5},{5,6},{6,7},{7,4},{8,9},{9,10},{10,1... | collective-permute-start | bytes 147464 | tf_op jit(solution)/shard_map/ppermute | solution.py:23
  24.7 20.3 %all-to-all-start = ((bf16[8,128,256]{2,1,0:T(8,128)(2,1)}), bf16[8,128,256]{2,1,0:T(8,128)(2,1)S(1)}, u32[]{:S(2)}, u32[]{:S(2)}) async-start(bf16[8,128,256]{2,1,0:T(8,128)(2,1)} %shard_map.201), calls=%async_computation | async-start | bytes 1048576 | tf_op jit(solution)/shard_map/all_to_all | solution.py:703
  28.3 4.2 %collective-permute-start.6 = (bf16[96,256]{1,0:T(8,128)(2,1)S(1)}, bf16[96,256]{1,0:T(8,128)(2,1)S(1)}, u32[]{:S(2)}, u32[]{:S(2)}) collective-permute-start(bf16[96,256]{1,0:T(8,128)(2,1)S(1)} %get-tuple-element.77), channel_id=1, source_target_pairs={{0,3},{1,0},{2,1},{3,2},{4,7},{5,4},{6,5},{7,6},{8,11},{9,8},{10,9... | collective-permute-start | bytes 147464 | tf_op jit(solution)/shard_map/ppermute | solution.py:23
  32.5 10.7 %collective-permute-start.7 = (bf16[96,256]{1,0:T(8,128)(2,1)S(1)}, bf16[96,256]{1,0:T(8,128)(2,1)S(1)}, u32[]{:S(2)}, u32[]{:S(2)}) collective-permute-start(bf16[96,256]{1,0:T(8,128)(2,1)S(1)} %pad_maximum_fusion.2), channel_id=1, source_target_pairs={{0,4},{4,8},{8,12},{12,0},{1,5},{5,9},{9,13},{13,1},{2,6},{6,10},{... | collective-permute-start | bytes 147464 | tf_op jit(solution)/shard_map/ppermute | solution.py:23
  35.7 7.4 %collective-permute-start.8 = (bf16[96,256]{1,0:T(8,128)(2,1)S(1)}, bf16[96,256]{1,0:T(8,128)(2,1)S(1)}, u32[]{:S(2)}, u32[]{:S(2)}) collective-permute-start(bf16[96,256]{1,0:T(8,128)(2,1)S(1)} %pad_maximum_fusion.3), channel_id=1, source_target_pairs={{0,12},{4,0},{8,4},{12,8},{1,13},{5,1},{9,5},{13,9},{2,14},{6,2},{... | collective-permute-start | bytes 147464 | tf_op jit(solution)/shard_map/ppermute | solution.py:23
  46.0 16.6 %all-to-all-start.1 = ((bf16[8,112,256]{2,1,0:T(8,128)(2,1)}), bf16[8,112,256]{2,1,0:T(8,128)(2,1)S(1)}, u32[]{:S(2)}, u32[]{:S(2)}) async-start(bf16[8,112,256]{2,1,0:T(8,128)(2,1)} %get-tuple-element.80), calls=%async_computation.1 | async-start | bytes 917504 | tf_op jit(solution)/shard_map/all_to_all | solution.py:714
  62.5 1.8 %collective-permute-start.9 = (bf16[8,112,256]{2,1,0:T(8,128)(2,1)S(1)}, bf16[8,112,256]{2,1,0:T(8,128)(2,1)S(1)}, u32[]{:S(2)}, u32[]{:S(2)}) collective-permute-start(bf16[8,112,256]{2,1,0:T(8,128)(2,1)S(1)} %all-to-all-done.1.own), channel_id=1, source_target_pairs={{0,1},{1,0},{2,3},{3,2},{4,5},{5,4},{6,7},{7,6},{8,9},{9,8},{10,11... | collective-permute-start | bytes 1376264 | tf_op jit(solution)/shard_map/ppermute | solution.py:27

commit v8 on v6

--- a/solution.py
+++ b/solution.py
@@ -123,32 +123,38 @@
 
 def index_kernel(sources, *refs):
     fetched, refs = refs[:sources], refs[sources:]
-    near_rows, halo_rows, sender_columns, receiver_columns = refs[:4]
-    targets, sems = refs[4:-1], refs[-1]
+    near_rows, halo_rows = refs[:2]
+    targets, sems = refs[2:-1], refs[-1]
     senders, receivers = targets[:2]
     copies = fetch_all(fetched, targets, sems)
     for copy in copies[:2]:
         copy.wait()
     tile_rows = senders.shape[1]
-    extended = sender_columns.shape[0]
-    count = receiver_columns.shape[0]
-    sender_ids = senders[...]
-    receiver_ids = receivers[...]
-    by_sender = columns_of(sender_ids)
-    by_receiver = columns_of(receiver_ids)
+    count = near_rows.shape[1] // 2
+    by_sender = columns_of(senders[...])
+    by_receiver = columns_of(receivers[...])
     for tile in range(senders.shape[0]):
         rows = slice(tile * tile_rows, (tile + 1) * tile_rows)
         near_rows[rows, :count] = hot_rows(by_sender, [tile], 0, count)
         near_rows[rows, count:] = hot_rows(by_receiver, [tile], 0, count)
         halo_rows[rows, :] = hot_rows(by_sender, [tile], count, halo_rows.shape[1])
+    for copy in copies[2:]:
+        copy.wait()
+
+
+def local_kernel(
+    nodes, edges, senders, receivers, near_rows, w_in, pre, sender_columns, receiver_columns
+):
+    width = nodes.shape[1]
+    tile_rows = senders.shape[1]
+    extended = sender_columns.shape[0]
+    count = receiver_columns.shape[0]
+    sender_ids = senders[...]
+    receiver_ids = receivers[...]
+    for tile in range(senders.shape[0]):
+        rows = slice(tile * tile_rows, (tile + 1) * tile_rows)
         sender_columns[:, rows] = hot_columns(sender_ids, [tile], 0, extended)
         receiver_columns[:, rows] = hot_columns(receiver_ids, [tile], 0, count)
-    for copy in copies[2:]:
-        copy.wait()
-
-
-def local_kernel(nodes, edges, near_rows, w_in, pre):
-    width = nodes.shape[1]
     x = nodes[...]
     table = jnp.concatenate(
         [
@@ -296,48 +302,11 @@
     gains_out[...] = gains
 
 
-def add_gains(own, other):
-    both = own.astype(F32) + other.astype(F32)
-    return pack_gains(both[0:1] + both[1:2], both[2:3] + both[3:4])
-
-
-def gains_kernel(own, other, gains_out):
-    gains_out[...] = add_gains(own[...], other[...])
-
-
-def pair_kernel(parts, keep, gains, other, blocks_out, gains_out, total, staged, sems):
+def pair_kernel(keep, gains, other, sums_out):
     rows = keep.shape[0]
-    chips = blocks_out.shape[0]
-    total[...] = (keep[...] + other[:rows].astype(F32)).astype(BF16)
-    copies = []
-    for chip in range(chips):
-        first, at = 0, 0
-        for part in parts:
-            step = part // chips
-            staged[chip, at : at + step, :] = total[first + chip * step : first + (chip + 1) * step]
-            first, at = first + part, at + step
-        copies.append(
-            pltpu.make_async_copy(staged.at[chip], blocks_out.at[chip], sems.at[chip])
-        )
-        copies[-1].start()
-    gains_out[...] = add_gains(gains[...], other[rows:])
-    for copy in copies:
-        copy.wait()
-
-
-def spread_kernel(received, spread_out, mine, sems):
-    sums = received[0].astype(F32)
-    for chip in range(1, received.shape[0]):
-        sums = sums + received[chip].astype(F32)
-    mine[...] = sums.astype(BF16)
-    copies = [
-        pltpu.make_async_copy(mine, spread_out.at[chip], sems.at[chip])
-        for chip in range(received.shape[0])
-    ]
-    for copy in copies:
-        copy.start()
-    for copy in copies:
-        copy.wait()
+    sums_out[:rows] = (keep[...] + other[:rows].astype(F32)).astype(BF16)
+    both = gains[...].astype(F32) + other[rows:].astype(F32)
+    sums_out[rows:] = pack_gains(both[0:1] + both[1:2], both[2:3] + both[3:4])
 
 
 def place_kernel(parts, own, other, *refs):
@@ -483,62 +452,6 @@
         results += [whole[:cut], whole[cut:]]
         at += step
     return results
-
-
-def spread_of(received):
-    chips, rows, width = received.shape
-    if rows % 16 == 0:
-        return call(
-            spread_kernel,
-            [like(received)],
-            0,
-            received,
-            out_space=HBM,
-            scratch=[pltpu.VMEM((rows, width), BF16), pltpu.SemaphoreType.DMA((chips,))],
-        )[0]
-    sums = jnp.sum(received.astype(F32), axis=0)
-    return jnp.broadcast_to(sums.astype(BF16)[None], received.shape)
-
-
-def summed_gains(gains):
-    for axis in ("side", "px"):
-        size = lax.axis_size(axis)
-        distance = 1
-        while distance < size:
-            other = lax.ppermute(gains, axis, [(i, i ^ distance) for i in range(size)])
-            (gains,) = call(gains_kernel, [like(gains)], 0, gains, other)
-            distance *= 2
-    return gains
-
-
-def blocks_of(parts, keep, gains, other):
-    chips = lax.axis_size(CHIPS)
-    rows, width = keep.shape
-    steps = [part // chips for part in parts]
-    shape = (chips, sum(steps), width)
-    if all(x % 16 == 0 for x in steps):
-        return call(
-            functools.partial(pair_kernel, parts),
-            [jax.ShapeDtypeStruct(shape, BF16), like(gains)],
-            0,
-            keep,
-            gains,
-            other,
-            out_space=[HBM, VMEM],
-            scratch=[
-                pltpu.VMEM((rows, width), BF16),
-                pltpu.VMEM(shape, BF16),
-                pltpu.SemaphoreType.DMA((chips,)),
-            ],
-        )
-    total = (keep + other[:rows].astype(F32)).astype(BF16)
-    pieces = []
-    first = 0
-    for part, step in zip(parts, steps):
-        pieces.append(total[first : first + part].reshape(chips, step, width))
-        first += part
-    (gains,) = call(gains_kernel, [like(gains)], 0, gains, other[rows:])
-    return jnp.concatenate(pieces, axis=1), gains
 
 
 def on_device(
@@ -593,13 +506,11 @@
         node_grads,
         edge_grads,
     ]
-    near_hot, halo_hot, sender_columns, receiver_columns, *fetched = call(
+    near_hot, halo_hot, *fetched = call(
         functools.partial(index_kernel, len(fetched)),
         [
             shaped(edge_rows, 2 * count, BF16),
             shaped(edge_rows, halo_rows, BF16),
-            shaped(count + halo_rows, edge_rows, BF16),
-            shaped(count, edge_rows, BF16),
         ]
         + [like(x) for x in fetched],
         0,
@@ -627,12 +538,18 @@
     downward = passed_along(
         jnp.concatenate([from_high[:slots], mid[:slots], from_low[:slots]]), PY, -1
     )
-    (pre_local,) = call(
+    pre_local, sender_columns, receiver_columns = call(
         local_kernel,
-        [shaped(edge_rows, width, F32)],
+        [
+            shaped(edge_rows, width, F32),
+            shaped(count + halo_rows, edge_rows, BF16),
+            shaped(count, edge_rows, BF16),
+        ],
         square * (2 * count + edge_rows) + 4 * edge_rows * count * width,
         nodes,
         edges,
+        senders,
+        receivers,
         near_hot,
         w_edge_in,
     )
@@ -684,15 +601,12 @@
             pltpu.VMEM((4 * width, width), F32),
         ],
     )
-    blocks, gains = blocks_of(parts, keep, gains, across_cores(away))
-    received = lax.all_to_all(blocks, CHIPS, 0, 0)
-    gains = summed_gains(gains)
+    (sums,) = call(pair_kernel, [like(away)], 0, keep, gains, across_cores(away))
+    sums = lax.psum(sums, CHIPS)
+    gains = sums[halves:].astype(F32)
+    own = sums[None, :halves]
     up_back = passed_along(up, PY, 1)
     down_back = passed_along(down, PY, -1)
-    received, gains, up_back, down_back = lax.optimization_barrier(
-        (received, gains, up_back, down_back)
-    )
-    own = lax.all_to_all(spread_of(received), CHIPS, 0, 0)
     to_high = passed_along(
         jnp.concatenate([up_back[:slots], down_back[:slots], rest[:slots]]), "px", 1
     )
@@ -730,10 +644,10 @@
         edges_grad,
         w_edge_in_grad,
         w_edge_out_grad,
-        (gains[0].astype(F32) + gains[1].astype(F32)).astype(BF16),
+        (gains[0] + gains[1]).astype(BF16),
         w_node_in_grad,
         w_node_out_grad,
-        (gains[2].astype(F32) + gains[3].astype(F32)).astype(BF16),
+        (gains[2] + gains[3]).astype(BF16),
     )
 
 

time: 65.4 us -> 115 us (1.76)
  waiting for transfers between devices: 18 us -> 68.3 us
  starting transfers between devices: 28.8 us -> 14.3 us
  between operations: 1.44 us -> 14.8 us
  Pallas kernels: 16.2 us -> 14.8 us
    psum x0 -> x1, waiting for transfers between devices: none -> 64.5 us  [on_device(): sums = lax.psum(sums, CHIPS)]
    all_to_all x2 -> x0, starting transfers between devices: 8.97 us -> none  [the longest x1 5.37 us: on_device(): own = lax.all_to_all(spread_of(received), CHIPS, 0, 0)]
    ppermute x3 -> x0, waiting for transfers between devices: 8.92 us -> none  [summed_gains(): other = lax.ppermute(gains, axis, [(i, i ^ distance) for i in range(size)])]
    ppermute x3 -> x0, starting transfers between devices: 5.3 us -> none  [summed_gains(): other = lax.ppermute(gains, axis, [(i, i ^ distance) for i in range(size)])]
    ppermute x8, waiting for transfers between devices: 6.1 us -> 3.24 us  [passed_along(): lax.ppermute(array, axis, [(i, (i + by) % size) for i in range(size)])]
    ppermute x2, waiting for transfers between devices: 2.73 us -> 0.57 us  [across_cores(): return lax.ppermute(array, CORE, [(0, 1), (1, 0)])]
    pallas_call x12 -> x8, Pallas kernels: 16.2 us -> 14.8 us  [call(): pl.pallas_call(body, out_shape=outs, in_specs=[pl.BlockSpec(memory_space=...]
  transfers between devices with their start and end apart: 15 -> 11, of which waited for: 8 -> 5; matrix products, arithmetic and copies ran while one was open for 1% -> 1% of each run, Pallas kernels for 10% -> 6%
where the time goes in v8:
time: 115 us
  waiting for transfers between devices  68.3 us (59%)
  Pallas kernels  14.8 us (13%)
  between operations  14.8 us (13%)
  starting transfers between devices  14.3 us (12%)
  other arithmetic  1.26 us (1%)
    psum x1, waiting for transfers between devices, on_device(): sums = lax.psum(sums, CHIPS)  64.5 us
    pallas_call x8, Pallas kernels, call(): pl.pallas_call(body, out_shape=outs, in_specs=[pl.BlockSpec(memory_space=...  14.8 us
    ppermute x8, starting transfers between devices, passed_along(): lax.ppermute(array, axis, [(i, (i + by) % size) for i in range(size)])  12.6 us
    ppermute x8, waiting for transfers between devices, passed_along(): lax.ppermute(array, axis, [(i, (i + by) % size) for i in range(size)])  3.24 us
  transfers between devices with their start and end apart: 11, of which 5 were waited for; matrix products, arithmetic and copies ran while one was open for 1% of the time, Pallas kernels for 6%

profile of v8, /device:TPU:0, one launch (start us, length us, event | category | flops | bytes accessed | tf_op | source)
XLA Modules:
  0.0 114.6 jit_solution(16807245666176833189)
XLA Ops:
  7.2 0.0 all-reduce.2.cloned.1.call-start
  7.2 1.3 %shard_map.197 = (bf16[96,256]{1,0:T(8,128)(2,1)S(1)}, bf16[64,256]{1,0:T(8,128)(2,1)S(1)}, bf16[96,256]{1,0:T(8,128)(2,1)S(1)}, bf16[384,256]{1,0:T(8,128)(2,1)S(1)}, s32[8,32]{1,0:T(8,128)S(1)}) custom-call(bf16[384,256]{1,0:T(8,128)(2,1)} %nodes_hbm.1, s32[8,32]{1,0:T(8,128)} %list_hbm.1), custom_call_target="tpu_custom_call" | custom-call | flops 50331648 | bytes 526336 | tf_op jit(solution)/shard_map/pallas_call | solution.py:404
  8.5 3.1 %collective-permute-start = (bf16[96,256]{1,0:T(8,128)(2,1)S(1)}, bf16[96,256]{1,0:T(8,128)(2,1)S(1)}, u32[]{:S(2)}, u32[]{:S(2)}) collective-permute-start(bf16[96,256]{1,0:T(8,128)(2,1)S(1)} %get-tuple-element.57), channel_id=1, source_target_pairs={{0,4},{4,8},{8,12},{12,0},{1,5},{5,9},{9,13},{13,1},{2,6},{6,10},{... | collective-permute-start | bytes 147464 | tf_op jit(solution)/shard_map/ppermute | solution.py:23
  11.6 2.1 %collective-permute-start.1 = (bf16[96,256]{1,0:T(8,128)(2,1)S(1)}, bf16[96,256]{1,0:T(8,128)(2,1)S(1)}, u32[]{:S(2)}, u32[]{:S(2)}) collective-permute-start(bf16[96,256]{1,0:T(8,128)(2,1)S(1)} %get-tuple-element.58), channel_id=1, source_target_pairs={{0,12},{4,0},{8,4},{12,8},{1,13},{5,1},{9,5},{13,9},{2,14},{6,2},{... | collective-permute-start | bytes 147464 | tf_op jit(solution)/shard_map/ppermute | solution.py:23
  14.3 1.7 %shard_map.198 = (bf16[1152,768]{1,0:T(8,128)(2,1)S(1)}, bf16[1152,256]{1,0:T(8,128)(2,1)S(1)}, s32[9,128]{1,0:T(8,128)S(1)}, s32[9,128]{1,0:T(8,128)S(1)}, bf16...) custom-call(s32[9,128]{1,0:T(8,128)} %refs_0_.1, ...), custom_call_target="tpu_custom_call" | custom-call | bytes 6967296 | tf_op jit(solution)/shard_map/pallas_call | solution.py:404
  16.1 0.0 collective-permute-done.from_low
  16.1 0.1 collective-permute-done.1.from_high
  16.2 0.1 collective-permute-start.2
  16.3 1.7 %collective-permute-start.3 = (bf16[96,256]{1,0:T(8,128)(2,1)S(1)}, bf16[96,256]{1,0:T(8,128)(2,1)S(1)}, u32[]{:S(2)}, u32[]{:S(2)}) collective-permute-start(bf16[96,256]{1,0:T(8,128)(2,1)S(1)} %pad_maximum_fusion.1), channel_id=1, source_target_pairs={{0,3},{1,0},{2,1},{3,2},{4,7},{5,4},{6,5},{7,6},{8,11},{9,8},{10,9... | collective-permute-start | bytes 147464 | tf_op jit(solution)/shard_map/ppermute | solution.py:23
  18.0 1.8 %shard_map.199 = (f32[1152,256]{1,0:T(8,128)S(1)}, bf16[640,1152]{1,0:T(8,128)(2,1)S(1)}, bf16[384,1152]{1,0:T(8,128)(2,1)S(1)}) custom-call(bf16[384,256]{1,0:T(8,128)(2,1)S(1)} %get-tuple-element.51.nodes, bf16[1152,256]{1,0:T(8,128)(2,1)S(1)} %get-tuple-element.53.edges, s32[9,128]{1,0:T(8,128)S(1)} %get-tuple-element.55.senders, ...), custom_call_target="tpu_custom_call" | custom-call | flops 704643072 | bytes 6497280 | tf_op jit(solution)/shard_map/pallas_call | solution.py:404
  19.9 0.0 collective-permute-done.2.upward
  19.9 0.0 collective-permute-done.3.downward
  19.9 5.6 %shard_map.200 = (bf16[1152,256]{1,0:T(8,128)(2,1)S(1)}, bf16[384,256]{1,0:T(8,128)(2,1)S(1)}, bf16[384,256]{1,0:T(8,128)(2,1)S(1)}, f32[384,256]{1,0:T(8,128)S(...) custom-call(s32[1]{0:T(128)S(6)} %copy.23.count_ref, ...), custom_call_target="tpu_custom_call" | custom-call | flops 2583691264 | bytes 11486212 | tf_op jit(solution)/shard_map/pallas_call | solution.py:404
  25.5 1.6 %collective-permute-start.4 = (bf16[912,256]{1,0:T(8,128)(2,1)S(1)}, bf16[912,256]{1,0:T(8,128)(2,1)S(1)}, u32[]{:S(2)}, u32[]{:S(2)}) collective-permute-start(bf16[912,256]{1,0:T(8,128)(2,1)S(1)} %get-tuple-element.76), channel_id=1, source_target_pairs={{0,1},{1,0},{2,3},{3,2},{4,5},{5,4},{6,7},{7,6},{8,9},{9,8},{10,11... | collective-permute-start | bytes 1400840 | tf_op jit(solution)/shard_map/ppermute | solution.py:27
  27.1 0.1 collective-permute-start.5
  27.2 1.7 %collective-permute-start.6 = (bf16[96,256]{1,0:T(8,128)(2,1)S(1)}, bf16[96,256]{1,0:T(8,128)(2,1)S(1)}, u32[]{:S(2)}, u32[]{:S(2)}) collective-permute-start(bf16[96,256]{1,0:T(8,128)(2,1)S(1)} %get-tuple-element.84), channel_id=1, source_target_pairs={{0,3},{1,0},{2,1},{3,2},{4,7},{5,4},{6,5},{7,6},{8,11},{9,8},{10,9... | collective-permute-start | bytes 147464 | tf_op jit(solution)/shard_map/ppermute | solution.py:23
  28.9 1.8 %collective-permute-done.5.up_back = bf16[96,256]{1,0:T(8,128)(2,1)S(1)} collective-permute-done((bf16[96,256]{1,0:T(8,128)(2,1)S(1)}, bf16[96,256]{1,0:T(8,128)(2,1)S(1)}, u32[]{:S(2)}, u32[]{:S(2)}) %collective-permute-start.5) | collective-permute-done | bytes 49184 | tf_op jit(solution)/shard_map/ppermute | solution.py:23
  30.7 0.0 collective-permute-done.4.other
  30.7 0.9 shard_map.201
  31.5 0.0 all-reduce.2.cloned.1.call-update
  31.6 0.0 collective-permute-done.6.down_back
  31.6 1.0 collective-permute-start.7
  32.6 2.8 %collective-permute-start.8 = (bf16[96,256]{1,0:T(8,128)(2,1)S(1)}, bf16[96,256]{1,0:T(8,128)(2,1)S(1)}, u32[]{:S(2)}, u32[]{:S(2)}) collective-permute-start(bf16[96,256]{1,0:T(8,128)(2,1)S(1)} %pad_maximum_fusion.3), channel_id=1, source_target_pairs={{0,12},{4,0},{8,4},{12,8},{1,13},{5,1},{9,5},{13,9},{2,14},{6,2},{... | collective-permute-start | bytes 147464 | tf_op jit(solution)/shard_map/ppermute | solution.py:23
  35.5 1.3 %shard_map.202 = (bf16[1152,256]{1,0:T(8,128)(2,1)}, f32[384,256]{1,0:T(8,128)S(1)}) custom-call(bf16[1152,256]{1,0:T(8,128)(2,1)S(1)} %get-tuple-element.54.edge_grads, bf16[1152,256]{1,0:T(8,128)(2,1)S(1)} %get-tuple-element.78.pre_grad, bf16[384,256]{1,0:T(8,128)(2,1)S(1)} %get-tuple-element.79.sender_sum, ...), custom_call_target="tpu_custom_call" | custom-call | flops 251658240 | bytes 3342336 | tf_op jit(solution)/shard_map/pallas_call | solution.py:404
  36.8 1.3 %collective-permute-done.7.to_high = bf16[96,256]{1,0:T(8,128)(2,1)S(1)} collective-permute-done((bf16[96,256]{1,0:T(8,128)(2,1)S(1)}, bf16[96,256]{1,0:T(8,128)(2,1)S(1)}, u32[]{:S(2)}, u32[]{:S(2)}) %collective-permute-start.7) | collective-permute-done | bytes 49184 | tf_op jit(solution)/shard_map/ppermute | solution.py:23
  38.2 0.0 collective-permute-done.8.to_low
  38.2 1.1 shard_map.203
  39.3 64.5 %all-reduce.2.cloned.1.call-done = bf16[912,256]{1,0:T(8,128)(2,1)} async-done(((bf16[912,256]{1,0:T(8,128)(2,1)}), bf16[912,256]{1,0:T(8,128)(2,1)}) %all-reduce.2.cloned.1.call-update) | async-done | bytes 466960 | tf_op jit(solution)/shard_map/psum | solution.py:605
  103.8 1.0 slice_bitcast_fusion.own
  104.8 0.1 collective-permute-start.9
  104.9 0.7 slice_convert_fusion
  105.6 0.5 fusion.3
  106.2 0.6 collective-permute-done.9.other
  106.7 1.0 shard_map.204
  (9 shorter events, 0.0 us)
Async XLA Ops:
  7.2 96.6 %all-reduce.2.cloned.1.call-start = ((), (), s32[]{:S(2)}) async-start(), calls=%async_computation | async-start | bytes 933888 | tf_op jit(solution)/shard_map/psum | solution.py:605
  8.5 7.6 %collective-permute-start = (bf16[96,256]{1,0:T(8,128)(2,1)S(1)}, bf16[96,256]{1,0:T(8,128)(2,1)S(1)}, u32[]{:S(2)}, u32[]{:S(2)}) collective-permute-start(bf16[96,256]{1,0:T(8,128)(2,1)S(1)} %get-tuple-element.57), channel_id=1, source_target_pairs={{0,4},{4,8},{8,12},{12,0},{1,5},{5,9},{9,13},{13,1},{2,6},{6,10},{... | collective-permute-start | bytes 147464 | tf_op jit(solution)/shard_map/ppermute | solution.py:23
  11.6 4.6 %collective-permute-start.1 = (bf16[96,256]{1,0:T(8,128)(2,1)S(1)}, bf16[96,256]{1,0:T(8,128)(2,1)S(1)}, u32[]{:S(2)}, u32[]{:S(2)}) collective-permute-start(bf16[96,256]{1,0:T(8,128)(2,1)S(1)} %get-tuple-element.58), channel_id=1, source_target_pairs={{0,12},{4,0},{8,4},{12,8},{1,13},{5,1},{9,5},{13,9},{2,14},{6,2},{... | collective-permute-start | bytes 147464 | tf_op jit(solution)/shard_map/ppermute | solution.py:23
  16.2 3.6 %collective-permute-start.2 = (bf16[96,256]{1,0:T(8,128)(2,1)S(1)}, bf16[96,256]{1,0:T(8,128)(2,1)S(1)}, u32[]{:S(2)}, u32[]{:S(2)}) collective-permute-start(bf16[96,256]{1,0:T(8,128)(2,1)S(1)} %pad_maximum_fusion), channel_id=1, source_target_pairs={{0,1},{1,2},{2,3},{3,0},{4,5},{5,6},{6,7},{7,4},{8,9},{9,10},{10,1... | collective-permute-start | bytes 147464 | tf_op jit(solution)/shard_map/ppermute | solution.py:23
  16.3 3.6 %collective-permute-start.3 = (bf16[96,256]{1,0:T(8,128)(2,1)S(1)}, bf16[96,256]{1,0:T(8,128)(2,1)S(1)}, u32[]{:S(2)}, u32[]{:S(2)}) collective-permute-start(bf16[96,256]{1,0:T(8,128)(2,1)S(1)} %pad_maximum_fusion.1), channel_id=1, source_target_pairs={{0,3},{1,0},{2,1},{3,2},{4,7},{5,4},{6,5},{7,6},{8,11},{9,8},{10,9... | collective-permute-start | bytes 147464 | tf_op jit(solution)/shard_map/ppermute | solution.py:23
  25.5 5.2 %collective-permute-start.4 = (bf16[912,256]{1,0:T(8,128)(2,1)S(1)}, bf16[912,256]{1,0:T(8,128)(2,1)S(1)}, u32[]{:S(2)}, u32[]{:S(2)}) collective-permute-start(bf16[912,256]{1,0:T(8,128)(2,1)S(1)} %get-tuple-element.76), channel_id=1, source_target_pairs={{0,1},{1,0},{2,3},{3,2},{4,5},{5,4},{6,7},{7,6},{8,9},{9,8},{10,11... | collective-permute-start | bytes 1400840 | tf_op jit(solution)/shard_map/ppermute | solution.py:27
  27.1 3.5 %collective-permute-start.5 = (bf16[96,256]{1,0:T(8,128)(2,1)S(1)}, bf16[96,256]{1,0:T(8,128)(2,1)S(1)}, u32[]{:S(2)}, u32[]{:S(2)}) collective-permute-start(bf16[96,256]{1,0:T(8,128)(2,1)S(1)} %get-tuple-element.83), channel_id=1, source_target_pairs={{0,1},{1,2},{2,3},{3,0},{4,5},{5,6},{6,7},{7,4},{8,9},{9,10},{10,1... | collective-permute-start | bytes 147464 | tf_op jit(solution)/shard_map/ppermute | solution.py:23
  27.2 4.4 %collective-permute-start.6 = (bf16[96,256]{1,0:T(8,128)(2,1)S(1)}, bf16[96,256]{1,0:T(8,128)(2,1)S(1)}, u32[]{:S(2)}, u32[]{:S(2)}) collective-permute-start(bf16[96,256]{1,0:T(8,128)(2,1)S(1)} %get-tuple-element.84), channel_id=1, source_target_pairs={{0,3},{1,0},{2,1},{3,2},{4,7},{5,4},{6,5},{7,6},{8,11},{9,8},{10,9... | collective-permute-start | bytes 147464 | tf_op jit(solution)/shard_map/ppermute | solution.py:23
  31.6 6.5 %collective-permute-start.7 = (bf16[96,256]{1,0:T(8,128)(2,1)S(1)}, bf16[96,256]{1,0:T(8,128)(2,1)S(1)}, u32[]{:S(2)}, u32[]{:S(2)}) collective-permute-start(bf16[96,256]{1,0:T(8,128)(2,1)S(1)} %pad_maximum_fusion.2), channel_id=1, source_target_pairs={{0,4},{4,8},{8,12},{12,0},{1,5},{5,9},{9,13},{13,1},{2,6},{6,10},{... | collective-permute-start | bytes 147464 | tf_op jit(solution)/shard_map/ppermute | solution.py:23
  32.6 5.5 %collective-permute-start.8 = (bf16[96,256]{1,0:T(8,128)(2,1)S(1)}, bf16[96,256]{1,0:T(8,128)(2,1)S(1)}, u32[]{:S(2)}, u32[]{:S(2)}) collective-permute-start(bf16[96,256]{1,0:T(8,128)(2,1)S(1)} %pad_maximum_fusion.3), channel_id=1, source_target_pairs={{0,12},{4,0},{8,4},{12,8},{1,13},{5,1},{9,5},{13,9},{2,14},{6,2},{... | collective-permute-start | bytes 147464 | tf_op jit(solution)/shard_map/ppermute | solution.py:23
  104.8 1.9 %collective-permute-start.9 = (bf16[1,896,256]{2,1,0:T(8,128)(2,1)S(1)}, bf16[1,896,256]{2,1,0:T(8,128)(2,1)S(1)}, u32[]{:S(2)}, u32[]{:S(2)}) collective-permute-start(bf16[1,896,256]{2,1,0:T(8,128)(2,1)S(1)} %slice_bitcast_fusion.own), channel_id=1, source_target_pairs={{0,1},{1,0},{2,3},{3,2},{4,5},{5,4},{6,7},{7,6},{8,9},{9,8},{10,11... | collective-permute-start | bytes 1376264 | tf_op jit(solution)/shard_map/ppermute | solution.py:27
Sparse Core Ops, SparseCore 0:
  31.7 72.0 all-reduce.1

commit v9 on v8

--- a/solution.py
+++ b/solution.py
@@ -14,8 +14,10 @@
 
 
 CORE = "core"
-PY = ("side", "core")
-CHIPS = ("px", "side")
+FAR = "far"
+PX = (FAR, "near")
+PY = ("side", CORE)
+SQUARE = ("near", "side")
 
 
 def passed_along(array, axis, by):
@@ -302,11 +304,62 @@
     gains_out[...] = gains
 
 
-def pair_kernel(keep, gains, other, sums_out):
+def pair_kernel(parts, keep, gains, other, blocks_out, total, staged, sems):
     rows = keep.shape[0]
-    sums_out[:rows] = (keep[...] + other[:rows].astype(F32)).astype(BF16)
+    chips = blocks_out.shape[0]
+    packed = gains.shape[0]
     both = gains[...].astype(F32) + other[rows:].astype(F32)
-    sums_out[rows:] = pack_gains(both[0:1] + both[1:2], both[2:3] + both[3:4])
+    summed = pack_gains(both[0:1] + both[1:2], both[2:3] + both[3:4])
+    total[...] = (keep[...] + other[:rows].astype(F32)).astype(BF16)
+    copies = []
+    for chip in range(chips):
+        staged[chip, :packed, :] = summed
+        first, at = 0, packed
+        for part in parts:
+            step = part // chips
+            staged[chip, at : at + step, :] = total[first + chip * step : first + (chip + 1) * step]
+            first, at = first + part, at + step
+        copies.append(
+            pltpu.make_async_copy(staged.at[chip], blocks_out.at[chip], sems.at[chip])
+        )
+        copies[-1].start()
+    for copy in copies:
+        copy.wait()
+
+
+def add_packed(values):
+    packed = 16
+    gains = values[:packed]
+    return pack_gains(gains[0:1] + gains[1:2], gains[2:3] + gains[3:4])
+
+
+def sum_kernel(received, sums_out):
+    sums = received[0].astype(F32)
+    for chip in range(1, received.shape[0]):
+        sums = sums + received[chip].astype(F32)
+    sums_out[...] = sums.astype(BF16)
+    sums_out[:16] = add_packed(sums)
+
+
+def join_kernel(own, other, sums_out):
+    sums = own[...].astype(F32) + other[...].astype(F32)
+    sums_out[...] = sums.astype(BF16)
+    sums_out[:16] = add_packed(sums)
+
+
+def spread_kernel(own, other, gains_out, spread_out, mine, sems):
+    packed = gains_out.shape[0]
+    sums = own[...].astype(F32) + other[...].astype(F32)
+    mine[...] = sums[packed:].astype(BF16)
+    copies = [
+        pltpu.make_async_copy(mine, spread_out.at[chip], sems.at[chip])
+        for chip in range(spread_out.shape[0])
+    ]
+    for copy in copies:
+        copy.start()
+    gains_out[...] = sums[:packed]
+    for copy in copies:
+        copy.wait()
 
 
 def place_kernel(parts, own, other, *refs):
@@ -428,30 +481,59 @@
         shaped(2 * width, width, BF16),
         shaped(width, width, BF16),
     ]
-    steps = [part // chips for part in parts]
-    cuts = [x.shape[0] for x in outs[::2]]
-    if all(x % 16 == 0 for x in steps + cuts):
-        return call(
-            functools.partial(place_kernel, parts),
-            outs,
-            0,
-            own,
-            other,
-            out_space=HBM,
-            scratch=[pltpu.SemaphoreType.DMA((2 * len(parts) * chips + len(parts),))],
-        )
-    core = lax.axis_index(CORE)
-    low = jnp.where(core == 0, own, other)
-    high = jnp.where(core == 0, other, own)
-    results = []
-    at = 0
-    for step, cut in zip(steps, cuts):
-        whole = jnp.concatenate(
-            [x[:, at : at + step].reshape(chips * step, width) for x in (low, high)]
-        )
-        results += [whole[:cut], whole[cut:]]
-        at += step
-    return results
+    return call(
+        functools.partial(place_kernel, parts),
+        outs,
+        0,
+        own,
+        other,
+        out_space=HBM,
+        scratch=[pltpu.SemaphoreType.DMA((2 * len(parts) * chips + len(parts),))],
+    )
+
+
+def spread_of(received, packed):
+    chips, rows, width = received.shape
+    (sums,) = call(sum_kernel, [shaped(rows, width, BF16)], 0, received)
+    size = lax.axis_size(FAR)
+    distance = 1
+    while True:
+        other = lax.ppermute(sums, FAR, [(i, i ^ distance) for i in range(size)])
+        distance *= 2
+        if distance == size:
+            break
+        (sums,) = call(join_kernel, [like(sums)], 0, sums, other)
+    mine = rows - packed
+    return call(
+        spread_kernel,
+        [shaped(packed, width, F32), jax.ShapeDtypeStruct((chips, mine, width), BF16)],
+        0,
+        sums,
+        other,
+        out_space=[VMEM, HBM],
+        scratch=[pltpu.VMEM((mine, width), BF16), pltpu.SemaphoreType.DMA((chips,))],
+    )
+
+
+def blocks_of(parts, keep, gains, other):
+    chips = lax.axis_size(SQUARE)
+    rows, width = keep.shape
+    shape = (chips, gains.shape[0] + rows // chips, width)
+    (blocks,) = call(
+        functools.partial(pair_kernel, parts),
+        [jax.ShapeDtypeStruct(shape, BF16)],
+        0,
+        keep,
+        gains,
+        other,
+        out_space=HBM,
+        scratch=[
+            pltpu.VMEM((rows, width), BF16),
+            pltpu.VMEM(shape, BF16),
+            pltpu.SemaphoreType.DMA((chips,)),
+        ],
+    )
+    return blocks
 
 
 def on_device(
@@ -491,8 +573,8 @@
         spaces=[HBM, HBM],
         scratch=[pltpu.SemaphoreType.DMA((2,))],
     )
-    from_low = passed_along(high, "px", 1)
-    from_high = passed_along(low, "px", -1)
+    from_low = passed_along(high, PX, 1)
+    from_high = passed_along(low, PX, -1)
     fetched = [
         senders,
         receivers,
@@ -601,18 +683,19 @@
             pltpu.VMEM((4 * width, width), F32),
         ],
     )
-    (sums,) = call(pair_kernel, [like(away)], 0, keep, gains, across_cores(away))
-    sums = lax.psum(sums, CHIPS)
-    gains = sums[halves:].astype(F32)
-    own = sums[None, :halves]
+    blocks = blocks_of(parts, keep, gains, across_cores(away))
+    received = lax.all_to_all(blocks, SQUARE, 0, 0)
     up_back = passed_along(up, PY, 1)
     down_back = passed_along(down, PY, -1)
+    received, up_back, down_back = lax.optimization_barrier((received, up_back, down_back))
     to_high = passed_along(
-        jnp.concatenate([up_back[:slots], down_back[:slots], rest[:slots]]), "px", 1
+        jnp.concatenate([up_back[:slots], down_back[:slots], rest[:slots]]), PX, 1
     )
     to_low = passed_along(
-        jnp.concatenate([up_back[2 * slots :], down_back[2 * slots :], rest[slots:]]), "px", -1
-    )
+        jnp.concatenate([up_back[2 * slots :], down_back[2 * slots :], rest[slots:]]), PX, -1
+    )
+    gains, spread = spread_of(received, gains.shape[0])
+    own = lax.all_to_all(spread, SQUARE, 0, 0)
     edges_grad, local_grad = call(
         finish_kernel,
         [shaped(edge_rows, width, BF16), shaped(count, width, F32)],
@@ -653,14 +736,14 @@
 
 def solution(mesh):
     in_specs = (
-        P(("groups", "px") + PY, None),
-        P(("groups", "px") + PY, None),
-        P(("groups", "px") + PY, None),
-        P(("groups", "px") + PY, None),
-        P(("groups", "px") + PY, None),
-        P(("groups", "px") + PY, None),
-        P(("groups", "px") + PY, None),
-        P(("groups", "px") + PY),
+        P(("groups",) + PX + PY, None),
+        P(("groups",) + PX + PY, None),
+        P(("groups",) + PX + PY, None),
+        P(("groups",) + PX + PY, None),
+        P(("groups",) + PX + PY, None),
+        P(("groups",) + PX + PY, None),
+        P(("groups",) + PX + PY, None),
+        P(("groups",) + PX + PY),
         P(),
         P(),
         P(),
@@ -669,8 +752,8 @@
         P(),
     )
     out_specs = (
-        P(("groups", "px") + PY, None),
-        P(("groups", "px") + PY, None),
+        P(("groups",) + PX + PY, None),
+        P(("groups",) + PX + PY, None),
         P("groups", None),
         P("groups", None),
         P("groups"),
@@ -680,7 +763,7 @@
     )
     groups, px, py = mesh.devices.shape
     by_core = jax.sharding.Mesh(
-        mesh.devices.reshape(groups, px, py // 2, 2), ("groups", "px") + PY
+        mesh.devices.reshape(groups, px // 2, 2, py // 2, 2), ("groups",) + PX + PY
     )
     return jax.shard_map(
         on_device, mesh=by_core, in_specs=in_specs, out_specs=out_specs, check_vma=False

time: 115 us -> 63.7 us (0.55)
  waiting for transfers between devices: 68.3 us -> 22.4 us
  between operations: 14.8 us -> 1.42 us
  starting transfers between devices: 14.3 us -> 23.3 us
    psum x1 -> x0, waiting for transfers between devices: 64.5 us -> none  [on_device(): sums = lax.psum(sums, CHIPS)]
    ppermute x8, waiting for transfers between devices: 3.24 us -> 12.5 us  [passed_along(): lax.ppermute(array, axis, [(i, (i + by) % size) for i in range(size)])]
    ppermute x0 -> x1, waiting for transfers between devices: none -> 7.11 us  [spread_of(): other = lax.ppermute(sums, FAR, [(i, i ^ distance) for i in range(size)])]
    all_to_all x0 -> x2, starting transfers between devices: none -> 6.96 us  [the longest x1 3.48 us: on_device(): received = lax.all_to_all(blocks, SQUARE, 0, 0)]
    ppermute x2, waiting for transfers between devices: 0.57 us -> 2.73 us  [across_cores(): return lax.ppermute(array, CORE, [(0, 1), (1, 0)])]
    ppermute x0 -> x1, starting transfers between devices: none -> 2.06 us  [spread_of(): other = lax.ppermute(sums, FAR, [(i, i ^ distance) for i in range(size)])]
    pallas_call x8 -> x10, Pallas kernels: 14.8 us -> 15.7 us  [call(): pl.pallas_call(body, out_shape=outs, in_specs=[pl.BlockSpec(memory_space=...]
  transfers between devices with their start and end apart: 11 -> 13, of which waited for: 5 -> 6; matrix products, arithmetic and copies ran while one was open for 1% -> 1% of each run, Pallas kernels for 6% -> 9%
where the time goes in v9:
time: 63.7 us; the launch traced here: 63.4 us
  starting transfers between devices  23.3 us (37%)
  waiting for transfers between devices  22.4 us (35%)
  Pallas kernels  15.7 us (25%)
  between operations  1.42 us (2%)
    pallas_call x10, Pallas kernels, call(): pl.pallas_call(body, out_shape=outs, in_specs=[pl.BlockSpec(memory_space=...  15.7 us
    ppermute x8, starting transfers between devices, passed_along(): lax.ppermute(array, axis, [(i, (i + by) % size) for i in range(size)])  12.6 us
    ppermute x8, waiting for transfers between devices, passed_along(): lax.ppermute(array, axis, [(i, (i + by) % size) for i in range(size)])  12.5 us
    ppermute x1, waiting for transfers between devices, spread_of(): other = lax.ppermute(sums, FAR, [(i, i ^ distance) for i in range(size)])  7.11 us
    all_to_all x1, starting transfers between devices, on_device(): received = lax.all_to_all(blocks, SQUARE, 0, 0)  3.48 us
    all_to_all x1, starting transfers between devices, on_device(): own = lax.all_to_all(spread, SQUARE, 0, 0)  3.48 us
    ppermute x2, waiting for transfers between devices, across_cores(): return lax.ppermute(array, CORE, [(0, 1), (1, 0)])  2.73 us
    ppermute x1, starting transfers between devices, spread_of(): other = lax.ppermute(sums, FAR, [(i, i ^ distance) for i in range(size)])  2.06 us
  transfers between devices with their start and end apart: 13, of which 6 were waited for; matrix products, arithmetic and copies ran while one was open for 1% of the time, Pallas kernels for 9%

profile of v9, /device:TPU:0, one launch (start us, length us, event | category | flops | bytes accessed | tf_op | source)
XLA Modules:
  0.0 63.4 jit_solution(12318842166570433731)
XLA Ops:
  0.6 1.3 %shard_map.197 = (bf16[96,256]{1,0:T(8,128)(2,1)S(1)}, bf16[64,256]{1,0:T(8,128)(2,1)S(1)}, bf16[96,256]{1,0:T(8,128)(2,1)S(1)}, bf16[384,256]{1,0:T(8,128)(2,1)S(1)}, s32[8,32]{1,0:T(8,128)S(1)}) custom-call(bf16[384,256]{1,0:T(8,128)(2,1)} %nodes_hbm.1, s32[8,32]{1,0:T(8,128)} %list_hbm.1), custom_call_target="tpu_custom_call" | custom-call | flops 50331648 | bytes 526336 | tf_op jit(solution)/shard_map/pallas_call | solution.py:457
  1.9 3.1 %collective-permute-start = (bf16[96,256]{1,0:T(8,128)(2,1)S(1)}, bf16[96,256]{1,0:T(8,128)(2,1)S(1)}, u32[]{:S(2)}, u32[]{:S(2)}) collective-permute-start(bf16[96,256]{1,0:T(8,128)(2,1)S(1)} %get-tuple-element.62), channel_id=1, source_target_pairs={{0,4},{4,8},{8,12},{12,0},{1,5},{5,9},{9,13},{13,1},{2,6},{6,10},{... | collective-permute-start | bytes 147464 | tf_op jit(solution)/shard_map/ppermute | solution.py:25
  5.0 2.1 %collective-permute-start.1 = (bf16[96,256]{1,0:T(8,128)(2,1)S(1)}, bf16[96,256]{1,0:T(8,128)(2,1)S(1)}, u32[]{:S(2)}, u32[]{:S(2)}) collective-permute-start(bf16[96,256]{1,0:T(8,128)(2,1)S(1)} %get-tuple-element.63), channel_id=1, source_target_pairs={{0,12},{4,0},{8,4},{12,8},{1,13},{5,1},{9,5},{13,9},{2,14},{6,2},{... | collective-permute-start | bytes 147464 | tf_op jit(solution)/shard_map/ppermute | solution.py:25
  7.8 1.7 %shard_map.198 = (bf16[1152,768]{1,0:T(8,128)(2,1)S(1)}, bf16[1152,256]{1,0:T(8,128)(2,1)S(1)}, s32[9,128]{1,0:T(8,128)S(1)}, s32[9,128]{1,0:T(8,128)S(1)}, bf16...) custom-call(s32[9,128]{1,0:T(8,128)} %refs_0_.1, ...), custom_call_target="tpu_custom_call" | custom-call | bytes 6967296 | tf_op jit(solution)/shard_map/pallas_call | solution.py:457
  9.5 0.0 collective-permute-done.from_low
  9.5 0.1 collective-permute-done.1.from_high
  9.7 0.1 collective-permute-start.2
  9.7 1.7 %collective-permute-start.3 = (bf16[96,256]{1,0:T(8,128)(2,1)S(1)}, bf16[96,256]{1,0:T(8,128)(2,1)S(1)}, u32[]{:S(2)}, u32[]{:S(2)}) collective-permute-start(bf16[96,256]{1,0:T(8,128)(2,1)S(1)} %pad_maximum_fusion.1), channel_id=1, source_target_pairs={{0,3},{1,0},{2,1},{3,2},{4,7},{5,4},{6,5},{7,6},{8,11},{9,8},{10,9... | collective-permute-start | bytes 147464 | tf_op jit(solution)/shard_map/ppermute | solution.py:25
  11.5 1.8 %shard_map.199 = (f32[1152,256]{1,0:T(8,128)S(1)}, bf16[640,1152]{1,0:T(8,128)(2,1)S(1)}, bf16[384,1152]{1,0:T(8,128)(2,1)S(1)}) custom-call(bf16[384,256]{1,0:T(8,128)(2,1)S(1)} %get-tuple-element.56.nodes, bf16[1152,256]{1,0:T(8,128)(2,1)S(1)} %get-tuple-element.58.edges, s32[9,128]{1,0:T(8,128)S(1)} %get-tuple-element.60.senders, ...), custom_call_target="tpu_custom_call" | custom-call | flops 704643072 | bytes 6497280 | tf_op jit(solution)/shard_map/pallas_call | solution.py:457
  13.3 0.0 collective-permute-done.2.upward
  13.3 0.0 collective-permute-done.3.downward
  13.3 5.6 %shard_map.200 = (bf16[1152,256]{1,0:T(8,128)(2,1)S(1)}, bf16[384,256]{1,0:T(8,128)(2,1)S(1)}, bf16[384,256]{1,0:T(8,128)(2,1)S(1)}, f32[384,256]{1,0:T(8,128)S(...) custom-call(s32[1]{0:T(128)S(6)} %copy.22.count_ref, ...), custom_call_target="tpu_custom_call" | custom-call | flops 2583691264 | bytes 11486212 | tf_op jit(solution)/shard_map/pallas_call | solution.py:457
  18.9 1.6 %collective-permute-start.4 = (bf16[912,256]{1,0:T(8,128)(2,1)S(1)}, bf16[912,256]{1,0:T(8,128)(2,1)S(1)}, u32[]{:S(2)}, u32[]{:S(2)}) collective-permute-start(bf16[912,256]{1,0:T(8,128)(2,1)S(1)} %get-tuple-element.81), channel_id=1, source_target_pairs={{0,1},{1,0},{2,3},{3,2},{4,5},{5,4},{6,7},{7,6},{8,9},{9,8},{10,11... | collective-permute-start | bytes 1400840 | tf_op jit(solution)/shard_map/ppermute | solution.py:29
  20.6 1.5 %collective-permute-done.4.other = bf16[912,256]{1,0:T(8,128)(2,1)S(1)} collective-permute-done((bf16[912,256]{1,0:T(8,128)(2,1)S(1)}, bf16[912,256]{1,0:T(8,128)(2,1)S(1)}, u32[]{:S(2)}, u32[]{:S(2)}) %collective-permute-start.4) | collective-permute-done | bytes 466976 | tf_op jit(solution)/shard_map/ppermute | solution.py:29
  22.0 0.8 %shard_map.201 = bf16[4,240,256]{2,1,0:T(8,128)(2,1)} custom-call(f32[896,256]{1,0:T(8,128)S(1)} %get-tuple-element.79.keep, bf16[16,256]{1,0:T(8,128)(2,1)S(1)} %get-tuple-element.80.gains, bf16[912,256]{1,0:T(8,128)(2,1)S(1)} %collective-permute-done.4.other), custom_call_target="tpu_custom_call" | custom-call | bytes 1884160 | tf_op jit(solution)/shard_map/pallas_call | solution.py:457
  22.9 3.5 %all-to-all-start = ((bf16[4,240,256]{2,1,0:T(8,128)(2,1)}), bf16[4,240,256]{2,1,0:T(8,128)(2,1)S(1)}, u32[]{:S(2)}, u32[]{:S(2)}) async-start(bf16[4,240,256]{2,1,0:T(8,128)(2,1)} %shard_map.201), calls=%async_computation | async-start | bytes 983040 | tf_op jit(solution)/shard_map/all_to_all | solution.py:687
  26.4 0.4 collective-permute-start.5
  26.8 1.4 %collective-permute-start.6 = (bf16[96,256]{1,0:T(8,128)(2,1)S(1)}, bf16[96,256]{1,0:T(8,128)(2,1)S(1)}, u32[]{:S(2)}, u32[]{:S(2)}) collective-permute-start(bf16[96,256]{1,0:T(8,128)(2,1)S(1)} %get-tuple-element.83), channel_id=1, source_target_pairs={{0,3},{1,0},{2,1},{3,2},{4,7},{5,4},{6,5},{7,6},{8,11},{9,8},{10,9... | collective-permute-start | bytes 147464 | tf_op jit(solution)/shard_map/ppermute | solution.py:25
  28.1 7.1 %collective-permute-done.5.up_back = bf16[96,256]{1,0:T(8,128)(2,1)S(1)} collective-permute-done((bf16[96,256]{1,0:T(8,128)(2,1)S(1)}, bf16[96,256]{1,0:T(8,128)(2,1)S(1)}, u32[]{:S(2)}, u32[]{:S(2)}) %collective-permute-start.5) | collective-permute-done | bytes 49184 | tf_op jit(solution)/shard_map/ppermute | solution.py:25
  35.2 0.0 collective-permute-done.6.down_back
  35.3 0.0 all-to-all-done.received
  35.3 0.1 shard_map.202.own
  35.4 2.1 %collective-permute-start.7 = (bf16[240,256]{1,0:T(8,128)(2,1)S(1)}, bf16[240,256]{1,0:T(8,128)(2,1)S(1)}, u32[]{:S(2)}, u32[]{:S(2)}) collective-permute-start(bf16[240,256]{1,0:T(8,128)(2,1)S(1)} %shard_map.202.own), channel_id=1, source_target_pairs={{0,8},{8,0},{1,9},{9,1},{2,10},{10,2},{3,11},{11,3},{4,12},{12,4},... | collective-permute-start | bytes 368648 | tf_op jit(solution)/shard_map/ppermute | solution.py:501
  37.4 7.1 %collective-permute-done.7.other = bf16[240,256]{1,0:T(8,128)(2,1)S(1)} collective-permute-done((bf16[240,256]{1,0:T(8,128)(2,1)S(1)}, bf16[240,256]{1,0:T(8,128)(2,1)S(1)}, u32[]{:S(2)}, u32[]{:S(2)}) %collective-permute-start.7) | collective-permute-done | bytes 122912 | tf_op jit(solution)/shard_map/ppermute | solution.py:501
  44.5 0.8 %shard_map.203 = (f32[16,256]{1,0:T(8,128)S(1)}, bf16[4,224,256]{2,1,0:T(8,128)(2,1)}) custom-call(bf16[240,256]{1,0:T(8,128)(2,1)S(1)} %shard_map.202.own, bf16[240,256]{1,0:T(8,128)(2,1)S(1)} %collective-permute-done.7.other), custom_call_target="tpu_custom_call" | custom-call | bytes 720896 | tf_op jit(solution)/shard_map/pallas_call | solution.py:457
  45.4 3.5 %all-to-all-start.1 = ((bf16[4,224,256]{2,1,0:T(8,128)(2,1)}), bf16[4,224,256]{2,1,0:T(8,128)(2,1)S(1)}, u32[]{:S(2)}, u32[]{:S(2)}) async-start(bf16[4,224,256]{2,1,0:T(8,128)(2,1)} %get-tuple-element.85), calls=%async_computation.1 | async-start | bytes 917504 | tf_op jit(solution)/shard_map/all_to_all | solution.py:698
  48.9 2.0 %collective-permute-start.8 = (bf16[96,256]{1,0:T(8,128)(2,1)S(1)}, bf16[96,256]{1,0:T(8,128)(2,1)S(1)}, u32[]{:S(2)}, u32[]{:S(2)}) collective-permute-start(bf16[96,256]{1,0:T(8,128)(2,1)S(1)} %pad_maximum_fusion.2), channel_id=1, source_target_pairs={{0,4},{4,8},{8,12},{12,0},{1,5},{5,9},{9,13},{13,1},{2,6},{6,10},{... | collective-permute-start | bytes 147464 | tf_op jit(solution)/shard_map/ppermute | solution.py:25
  50.9 1.9 %collective-permute-start.9 = (bf16[96,256]{1,0:T(8,128)(2,1)S(1)}, bf16[96,256]{1,0:T(8,128)(2,1)S(1)}, u32[]{:S(2)}, u32[]{:S(2)}) collective-permute-start(bf16[96,256]{1,0:T(8,128)(2,1)S(1)} %pad_maximum_fusion.3), channel_id=1, source_target_pairs={{0,12},{4,0},{8,4},{12,8},{1,13},{5,1},{9,5},{13,9},{2,14},{6,2},{... | collective-permute-start | bytes 147464 | tf_op jit(solution)/shard_map/ppermute | solution.py:25
  52.8 1.3 %shard_map.204 = (bf16[1152,256]{1,0:T(8,128)(2,1)}, f32[384,256]{1,0:T(8,128)S(1)}) custom-call(bf16[1152,256]{1,0:T(8,128)(2,1)S(1)} %get-tuple-element.59.edge_grads, bf16[1152,256]{1,0:T(8,128)(2,1)S(1)} %get-tuple-element.87.pre_grad, bf16[384,256]{1,0:T(8,128)(2,1)S(1)} %get-tuple-element.88.sender_sum, ...), custom_call_target="tpu_custom_call" | custom-call | flops 251658240 | bytes 3342336 | tf_op jit(solution)/shard_map/pallas_call | solution.py:457
  54.1 5.3 %collective-permute-done.8.to_high = bf16[96,256]{1,0:T(8,128)(2,1)S(1)} collective-permute-done((bf16[96,256]{1,0:T(8,128)(2,1)S(1)}, bf16[96,256]{1,0:T(8,128)(2,1)S(1)}, u32[]{:S(2)}, u32[]{:S(2)}) %collective-permute-start.8) | collective-permute-done | bytes 49184 | tf_op jit(solution)/shard_map/ppermute | solution.py:25
  59.4 0.0 collective-permute-done.9.to_low
  59.4 1.1 %shard_map.205 = bf16[384,256]{1,0:T(8,128)(2,1)} custom-call(s32[8,32]{1,0:T(8,128)S(1)} %get-tuple-element.86.send_list, f32[384,256]{1,0:T(8,128)S(1)} %get-tuple-element.91.local_grad, bf16[96,256]{1,0:T(8,128)(2,1)S(1)} %collective-permute-done.5.up_back, bf16[96,256]{1,0:T(8,128)(2,1)S(1)} %collective-permute-done.6.down_back, ...), custom_call_target="tpu_custom_call" | custom-call | flops 50331648 | bytes 787456 | tf_op jit(solution)/shard_map/pallas_call | solution.py:457
  60.5 0.0 all-to-all-done.1.own
  60.5 0.0 collective-permute-start.10
  60.5 0.5 convert_reduce_fusion
  61.0 1.3 %collective-permute-done.10.other = bf16[4,224,256]{2,1,0:T(8,128)(2,1)S(1)} collective-permute-done((bf16[4,224,256]{2,1,0:T(8,128)(2,1)S(1)}, bf16[4,224,256]{2,1,0:T(8,128)(2,1)S(1)}, u32[]{:S(2)}, u32[]{:S(2)}) %collective-permute-start.10) | collective-permute-done | bytes 458784 | tf_op jit(solution)/shard_map/ppermute | solution.py:29
  62.3 1.1 %shard_map.206 = (bf16[768,256]{1,0:T(8,128)(2,1)}, bf16[256,256]{1,0:T(8,128)(2,1)}, bf16[512,256]{1,0:T(8,128)(2,1)}, bf16[256,256]{1,0:T(8,128)(2,1)}) custom-call(bf16[4,224,256]{2,1,0:T(8,128)(2,1)S(1)} %all-to-all-done.1.own, bf16[4,224,256]{2,1,0:T(8,128)(2,1)S(1)} %collective-permute-done.10.other), custom_call_target="tpu_custom_call" | custom-call | bytes 1835008 | tf_op jit(solution)/shard_map/pallas_call | solution.py:457
  (9 shorter events, 0.0 us)
Async XLA Ops:
  1.9 7.6 %collective-permute-start = (bf16[96,256]{1,0:T(8,128)(2,1)S(1)}, bf16[96,256]{1,0:T(8,128)(2,1)S(1)}, u32[]{:S(2)}, u32[]{:S(2)}) collective-permute-start(bf16[96,256]{1,0:T(8,128)(2,1)S(1)} %get-tuple-element.62), channel_id=1, source_target_pairs={{0,4},{4,8},{8,12},{12,0},{1,5},{5,9},{9,13},{13,1},{2,6},{6,10},{... | collective-permute-start | bytes 147464 | tf_op jit(solution)/shard_map/ppermute | solution.py:25
  5.0 4.6 %collective-permute-start.1 = (bf16[96,256]{1,0:T(8,128)(2,1)S(1)}, bf16[96,256]{1,0:T(8,128)(2,1)S(1)}, u32[]{:S(2)}, u32[]{:S(2)}) collective-permute-start(bf16[96,256]{1,0:T(8,128)(2,1)S(1)} %get-tuple-element.63), channel_id=1, source_target_pairs={{0,12},{4,0},{8,4},{12,8},{1,13},{5,1},{9,5},{13,9},{2,14},{6,2},{... | collective-permute-start | bytes 147464 | tf_op jit(solution)/shard_map/ppermute | solution.py:25
  9.7 3.6 %collective-permute-start.2 = (bf16[96,256]{1,0:T(8,128)(2,1)S(1)}, bf16[96,256]{1,0:T(8,128)(2,1)S(1)}, u32[]{:S(2)}, u32[]{:S(2)}) collective-permute-start(bf16[96,256]{1,0:T(8,128)(2,1)S(1)} %pad_maximum_fusion), channel_id=1, source_target_pairs={{0,1},{1,2},{2,3},{3,0},{4,5},{5,6},{6,7},{7,4},{8,9},{9,10},{10,1... | collective-permute-start | bytes 147464 | tf_op jit(solution)/shard_map/ppermute | solution.py:25
  9.7 3.6 %collective-permute-start.3 = (bf16[96,256]{1,0:T(8,128)(2,1)S(1)}, bf16[96,256]{1,0:T(8,128)(2,1)S(1)}, u32[]{:S(2)}, u32[]{:S(2)}) collective-permute-start(bf16[96,256]{1,0:T(8,128)(2,1)S(1)} %pad_maximum_fusion.1), channel_id=1, source_target_pairs={{0,3},{1,0},{2,1},{3,2},{4,7},{5,4},{6,5},{7,6},{8,11},{9,8},{10,9... | collective-permute-start | bytes 147464 | tf_op jit(solution)/shard_map/ppermute | solution.py:25
  18.9 3.1 %collective-permute-start.4 = (bf16[912,256]{1,0:T(8,128)(2,1)S(1)}, bf16[912,256]{1,0:T(8,128)(2,1)S(1)}, u32[]{:S(2)}, u32[]{:S(2)}) collective-permute-start(bf16[912,256]{1,0:T(8,128)(2,1)S(1)} %get-tuple-element.81), channel_id=1, source_target_pairs={{0,1},{1,0},{2,3},{3,2},{4,5},{5,4},{6,7},{7,6},{8,9},{9,8},{10,11... | collective-permute-start | bytes 1400840 | tf_op jit(solution)/shard_map/ppermute | solution.py:29
  22.9 12.4 %all-to-all-start = ((bf16[4,240,256]{2,1,0:T(8,128)(2,1)}), bf16[4,240,256]{2,1,0:T(8,128)(2,1)S(1)}, u32[]{:S(2)}, u32[]{:S(2)}) async-start(bf16[4,240,256]{2,1,0:T(8,128)(2,1)} %shard_map.201), calls=%async_computation | async-start | bytes 983040 | tf_op jit(solution)/shard_map/all_to_all | solution.py:687
  26.4 8.9 %collective-permute-start.5 = (bf16[96,256]{1,0:T(8,128)(2,1)S(1)}, bf16[96,256]{1,0:T(8,128)(2,1)S(1)}, u32[]{:S(2)}, u32[]{:S(2)}) collective-permute-start(bf16[96,256]{1,0:T(8,128)(2,1)S(1)} %get-tuple-element.82), channel_id=1, source_target_pairs={{0,1},{1,2},{2,3},{3,0},{4,5},{5,6},{6,7},{7,4},{8,9},{9,10},{10,1... | collective-permute-start | bytes 147464 | tf_op jit(solution)/shard_map/ppermute | solution.py:25
  26.8 8.5 %collective-permute-start.6 = (bf16[96,256]{1,0:T(8,128)(2,1)S(1)}, bf16[96,256]{1,0:T(8,128)(2,1)S(1)}, u32[]{:S(2)}, u32[]{:S(2)}) collective-permute-start(bf16[96,256]{1,0:T(8,128)(2,1)S(1)} %get-tuple-element.83), channel_id=1, source_target_pairs={{0,3},{1,0},{2,1},{3,2},{4,7},{5,4},{6,5},{7,6},{8,11},{9,8},{10,9... | collective-permute-start | bytes 147464 | tf_op jit(solution)/shard_map/ppermute | solution.py:25
  35.4 9.2 %collective-permute-start.7 = (bf16[240,256]{1,0:T(8,128)(2,1)S(1)}, bf16[240,256]{1,0:T(8,128)(2,1)S(1)}, u32[]{:S(2)}, u32[]{:S(2)}) collective-permute-start(bf16[240,256]{1,0:T(8,128)(2,1)S(1)} %shard_map.202.own), channel_id=1, source_target_pairs={{0,8},{8,0},{1,9},{9,1},{2,10},{10,2},{3,11},{11,3},{4,12},{12,4},... | collective-permute-start | bytes 368648 | tf_op jit(solution)/shard_map/ppermute | solution.py:501
  45.4 15.1 %all-to-all-start.1 = ((bf16[4,224,256]{2,1,0:T(8,128)(2,1)}), bf16[4,224,256]{2,1,0:T(8,128)(2,1)S(1)}, u32[]{:S(2)}, u32[]{:S(2)}) async-start(bf16[4,224,256]{2,1,0:T(8,128)(2,1)} %get-tuple-element.85), calls=%async_computation.1 | async-start | bytes 917504 | tf_op jit(solution)/shard_map/all_to_all | solution.py:698
  48.9 10.5 %collective-permute-start.8 = (bf16[96,256]{1,0:T(8,128)(2,1)S(1)}, bf16[96,256]{1,0:T(8,128)(2,1)S(1)}, u32[]{:S(2)}, u32[]{:S(2)}) collective-permute-start(bf16[96,256]{1,0:T(8,128)(2,1)S(1)} %pad_maximum_fusion.2), channel_id=1, source_target_pairs={{0,4},{4,8},{8,12},{12,0},{1,5},{5,9},{9,13},{13,1},{2,6},{6,10},{... | collective-permute-start | bytes 147464 | tf_op jit(solution)/shard_map/ppermute | solution.py:25
  50.9 8.4 %collective-permute-start.9 = (bf16[96,256]{1,0:T(8,128)(2,1)S(1)}, bf16[96,256]{1,0:T(8,128)(2,1)S(1)}, u32[]{:S(2)}, u32[]{:S(2)}) collective-permute-start(bf16[96,256]{1,0:T(8,128)(2,1)S(1)} %pad_maximum_fusion.3), channel_id=1, source_target_pairs={{0,12},{4,0},{8,4},{12,8},{1,13},{5,1},{9,5},{13,9},{2,14},{6,2},{... | collective-permute-start | bytes 147464 | tf_op jit(solution)/shard_map/ppermute | solution.py:25
  60.5 1.8 %collective-permute-start.10 = (bf16[4,224,256]{2,1,0:T(8,128)(2,1)S(1)}, bf16[4,224,256]{2,1,0:T(8,128)(2,1)S(1)}, u32[]{:S(2)}, u32[]{:S(2)}) collective-permute-start(bf16[4,224,256]{2,1,0:T(8,128)(2,1)S(1)} %all-to-all-done.1.own), channel_id=1, source_target_pairs={{0,1},{1,0},{2,3},{3,2},{4,5},{5,4},{6,7},{7,6},{8,9},{9,8},{10,11... | collective-permute-start | bytes 1376264 | tf_op jit(solution)/shard_map/ppermute | solution.py:29

commit v10 on v9

--- a/solution.py
+++ b/solution.py
@@ -23,6 +23,12 @@
 def passed_along(array, axis, by):
     size = lax.axis_size(axis)
     return lax.ppermute(array, axis, [(i, (i + by) % size) for i in range(size)])
+
+
+def across_chips(array):
+    size = lax.axis_size(PY)
+    pairs = [(i, (i + 1 if i % 2 else i - 1) % size) for i in range(size)]
+    return lax.ppermute(array, PY, pairs)
 
 
 def across_cores(array):
@@ -213,8 +219,7 @@
     sender_out,
     receiver_out,
     node_part_out,
-    up_out,
-    down_out,
+    across_out,
     rest_out,
     keep_out,
     away_out,
@@ -290,8 +295,21 @@
     receiver_out[...] = received
     halo_grad = dot_nt(away, w_in[width : 2 * width]).astype(BF16)
     parts = [halo_grad[k * slots : (k + 1) * slots] for k in range(8)]
-    up_out[...] = jnp.concatenate([parts[0], parts[3], parts[5]], axis=0)
-    down_out[...] = jnp.concatenate([parts[2], parts[4], parts[7]], axis=0)
+    up = jnp.concatenate([parts[0], parts[3], parts[5]], axis=0)
+    down = jnp.concatenate([parts[2], parts[4], parts[7]], axis=0)
+    core = lax.axis_index(CORE)
+    sums_rows = gains_out.shape[0] + keep_out.shape[0]
+
+    @pl.when(core == 0)
+    def _():
+        away_out[sums_rows:] = up
+        across_out[...] = down
+
+    @pl.when(core == 1)
+    def _():
+        away_out[sums_rows:] = down
+        across_out[...] = up
+
     rest_out[...] = jnp.concatenate([parts[1], parts[6]], axis=0)
     edge_sums[:width] = dot_tn(edges[...], pre_grad)
     edge_sums[width : 2 * width] = dot_tn(x, own) + dot_tn(halo, away)
@@ -300,7 +318,7 @@
     split_by_core(edge_sums, 0, keep_out, away_out)
     split_by_core(node_sums, edge_sums.shape[0] // 2, keep_out, away_out)
     gains = pack_gains(edge_gain, node_gain)
-    away_out[keep_out.shape[0] :] = gains
+    away_out[keep_out.shape[0] : sums_rows] = gains
     gains_out[...] = gains
 
 
@@ -308,7 +326,7 @@
     rows = keep.shape[0]
     chips = blocks_out.shape[0]
     packed = gains.shape[0]
-    both = gains[...].astype(F32) + other[rows:].astype(F32)
+    both = gains[...].astype(F32) + other[rows : rows + packed].astype(F32)
     summed = pack_gains(both[0:1] + both[1:2], both[2:3] + both[3:4])
     total[...] = (keep[...] + other[:rows].astype(F32)).astype(BF16)
     copies = []
@@ -417,7 +435,32 @@
     )
 
 
-def return_kernel(send_list, local_grad, up_back, down_back, to_high, to_low, nodes_grad):
+def turn_kernel(other, across, rest, high, low, middle):
+    slots = rest.shape[0] // 2
+    first = other.shape[0] - 3 * slots
+
+    def turn(up_back, down_back):
+        high[:slots] = up_back[:slots]
+        high[slots : 2 * slots] = down_back[:slots]
+        high[2 * slots :] = rest[:slots]
+        low[:slots] = up_back[2 * slots :]
+        low[slots : 2 * slots] = down_back[2 * slots :]
+        low[2 * slots :] = rest[slots:]
+        middle[:slots] = up_back[slots : 2 * slots]
+        middle[slots:] = down_back[slots : 2 * slots]
+
+    core = lax.axis_index(CORE)
+
+    @pl.when(core == 0)
+    def _():
+        turn(across, other.at[first:])
+
+    @pl.when(core == 1)
+    def _():
+        turn(other.at[first:], across)
+
+
+def return_kernel(send_list, local_grad, middle, to_high, to_low, nodes_grad):
     slots = send_list.shape[1]
 
     def block(ref, k):
@@ -428,8 +471,8 @@
             block(to_high, 0),
             block(to_high, 2),
             block(to_high, 1),
-            block(up_back, 1),
-            block(down_back, 1),
+            block(middle, 0),
+            block(middle, 1),
             block(to_low, 0),
             block(to_low, 2),
             block(to_low, 1),
@@ -492,7 +535,7 @@
     )
 
 
-def spread_of(received, packed):
+def spread_of(received, packed, *beside):
     chips, rows, width = received.shape
     (sums,) = call(sum_kernel, [shaped(rows, width, BF16)], 0, received)
     size = lax.axis_size(FAR)
@@ -504,7 +547,8 @@
             break
         (sums,) = call(join_kernel, [like(sums)], 0, sums, other)
     mine = rows - packed
-    return call(
+    other, *beside = lax.optimization_barrier((other, *beside))
+    gains, spread = call(
         spread_kernel,
         [shaped(packed, width, F32), jax.ShapeDtypeStruct((chips, mine, width), BF16)],
         0,
@@ -513,6 +557,7 @@
         out_space=[VMEM, HBM],
         scratch=[pltpu.VMEM((mine, width), BF16), pltpu.SemaphoreType.DMA((chips,))],
     )
+    return gains, spread, *beside
 
 
 def blocks_of(parts, keep, gains, other):
@@ -637,7 +682,7 @@
     )
     parts = (2 * width, 3 * width // 2)
     halves = sum(parts)
-    pre_grad, sender_sum, receiver_sum, node_part, up, down, rest, keep, away, gains = call(
+    pre_grad, sender_sum, receiver_sum, node_part, across, rest, keep, away, gains = call(
         functools.partial(layer_kernel, tile_rows),
         [
             shaped(edge_rows, width, BF16),
@@ -645,10 +690,9 @@
             shaped(count, width, BF16),
             shaped(count, width, F32),
             shaped(3 * slots, width, BF16),
-            shaped(3 * slots, width, BF16),
             shaped(2 * slots, width, BF16),
             shaped(halves, width, F32),
-            shaped(halves + 16, width, BF16),
+            shaped(halves + 16 + 3 * slots, width, BF16),
             shaped(16, width, BF16),
         ],
         square * (6 * edge_rows + 11 * count + 2 * halo_rows)
@@ -683,18 +727,25 @@
             pltpu.VMEM((4 * width, width), F32),
         ],
     )
-    blocks = blocks_of(parts, keep, gains, across_cores(away))
+    other = across_cores(away)
+    blocks = blocks_of(parts, keep, gains, other)
     received = lax.all_to_all(blocks, SQUARE, 0, 0)
-    up_back = passed_along(up, PY, 1)
-    down_back = passed_along(down, PY, -1)
-    received, up_back, down_back = lax.optimization_barrier((received, up_back, down_back))
-    to_high = passed_along(
-        jnp.concatenate([up_back[:slots], down_back[:slots], rest[:slots]]), PX, 1
-    )
-    to_low = passed_along(
-        jnp.concatenate([up_back[2 * slots :], down_back[2 * slots :], rest[slots:]]), PX, -1
-    )
-    gains, spread = spread_of(received, gains.shape[0])
+    high, low, middle = call(
+        turn_kernel,
+        [
+            shaped(3 * slots, width, BF16),
+            shaped(3 * slots, width, BF16),
+            shaped(2 * slots, width, BF16),
+        ],
+        0,
+        other,
+        across_chips(across),
+        rest,
+    )
+    received, high, low = lax.optimization_barrier((received, high, low))
+    gains, spread, to_high, to_low = spread_of(
+        received, gains.shape[0], passed_along(high, PX, 1), passed_along(low, PX, -1)
+    )
     own = lax.all_to_all(spread, SQUARE, 0, 0)
     edges_grad, local_grad = call(
         finish_kernel,
@@ -713,8 +764,7 @@
         2 * halo_rows * count * width,
         send_list,
         local_grad,
-        up_back,
-        down_back,
+        middle,
         to_high,
         to_low,
     )

time: 63.7 us -> 60.5 us (0.950)
  waiting for transfers between devices: 22.4 us -> 19.3 us
    ppermute x8 -> x6, waiting for transfers between devices: 12.5 us -> 3.55 us  [passed_along(): lax.ppermute(array, axis, [(i, (i + by) % size) for i in range(size)])]
    ppermute x0 -> x1, waiting for transfers between devices: none -> 7.21 us  [across_chips(): return lax.ppermute(array, PY, pairs)]
    ppermute x1, waiting for transfers between devices: 7.11 us -> 1.45 us  [spread_of(): other = lax.ppermute(sums, FAR, [(i, i ^ distance) for i in range(size)])]
    all_to_all x1, waiting for transfers between devices: 0.01 us -> 4.27 us  [on_device(): own = lax.all_to_all(spread, SQUARE, 0, 0)]
    ppermute x8 -> x6, starting transfers between devices: 12.6 us -> 10.8 us  [passed_along(): lax.ppermute(array, axis, [(i, (i + by) % size) for i in range(size)])]
    ppermute x0 -> x1, starting transfers between devices: none -> 1.68 us  [across_chips(): return lax.ppermute(array, PY, pairs)]
    pallas_call x10 -> x11, Pallas kernels: 15.7 us -> 15.8 us  [call(): pl.pallas_call(body, out_shape=outs, in_specs=[pl.BlockSpec(memory_space=...]
  transfers between devices with their start and end apart: 13 -> 12, of which waited for: 6 -> 7; matrix products, arithmetic and copies ran while one was open for 1% -> 1% of each run, Pallas kernels for 9% -> 10%
where the time goes in v10:
time: 60.5 us; the launch traced here: 60.2 us
  starting transfers between devices  23.1 us (38%)
  waiting for transfers between devices  19.3 us (32%)
  Pallas kernels  15.8 us (26%)
  between operations  1.4 us (2%)
    pallas_call x11, Pallas kernels, call(): pl.pallas_call(body, out_shape=outs, in_specs=[pl.BlockSpec(memory_space=...  15.8 us
    ppermute x6, starting transfers between devices, passed_along(): lax.ppermute(array, axis, [(i, (i + by) % size) for i in range(size)])  10.8 us
    ppermute x1, waiting for transfers between devices, across_chips(): return lax.ppermute(array, PY, pairs)  7.21 us
    all_to_all x1, waiting for transfers between devices, on_device(): own = lax.all_to_all(spread, SQUARE, 0, 0)  4.27 us
    ppermute x6, waiting for transfers between devices, passed_along(): lax.ppermute(array, axis, [(i, (i + by) % size) for i in range(size)])  3.55 us
    all_to_all x1, starting transfers between devices, on_device(): received = lax.all_to_all(blocks, SQUARE, 0, 0)  3.48 us
    all_to_all x1, starting transfers between devices, on_device(): own = lax.all_to_all(spread, SQUARE, 0, 0)  3.48 us
    ppermute x2, waiting for transfers between devices, across_cores(): return lax.ppermute(array, CORE, [(0, 1), (1, 0)])  2.8 us
  transfers between devices with their start and end apart: 12, of which 7 were waited for; matrix products, arithmetic and copies ran while one was open for 1% of the time, Pallas kernels for 10%

profile of v10, /device:TPU:0, one launch (start us, length us, event | category | flops | bytes accessed | tf_op | source)
XLA Modules:
  0.0 60.2 jit_solution(4435242838329393863)
XLA Ops:
  0.6 1.3 %shard_map.197 = (bf16[96,256]{1,0:T(8,128)(2,1)S(1)}, bf16[64,256]{1,0:T(8,128)(2,1)S(1)}, bf16[96,256]{1,0:T(8,128)(2,1)S(1)}, bf16[384,256]{1,0:T(8,128)(2,1)S(1)}, s32[8,32]{1,0:T(8,128)S(1)}) custom-call(bf16[384,256]{1,0:T(8,128)(2,1)} %nodes_hbm.1, s32[8,32]{1,0:T(8,128)} %list_hbm.1), custom_call_target="tpu_custom_call" | custom-call | flops 50331648 | bytes 526336 | tf_op jit(solution)/shard_map/pallas_call | solution.py:500
  1.9 3.1 %collective-permute-start = (bf16[96,256]{1,0:T(8,128)(2,1)S(1)}, bf16[96,256]{1,0:T(8,128)(2,1)S(1)}, u32[]{:S(2)}, u32[]{:S(2)}) collective-permute-start(bf16[96,256]{1,0:T(8,128)(2,1)S(1)} %get-tuple-element.67), channel_id=1, source_target_pairs={{0,4},{4,8},{8,12},{12,0},{1,5},{5,9},{9,13},{13,1},{2,6},{6,10},{... | collective-permute-start | bytes 147464 | tf_op jit(solution)/shard_map/ppermute | solution.py:25
  5.0 2.1 %collective-permute-start.1 = (bf16[96,256]{1,0:T(8,128)(2,1)S(1)}, bf16[96,256]{1,0:T(8,128)(2,1)S(1)}, u32[]{:S(2)}, u32[]{:S(2)}) collective-permute-start(bf16[96,256]{1,0:T(8,128)(2,1)S(1)} %get-tuple-element.68), channel_id=1, source_target_pairs={{0,12},{4,0},{8,4},{12,8},{1,13},{5,1},{9,5},{13,9},{2,14},{6,2},{... | collective-permute-start | bytes 147464 | tf_op jit(solution)/shard_map/ppermute | solution.py:25
  7.8 1.7 %shard_map.198 = (bf16[1152,768]{1,0:T(8,128)(2,1)S(1)}, bf16[1152,256]{1,0:T(8,128)(2,1)S(1)}, s32[9,128]{1,0:T(8,128)S(1)}, s32[9,128]{1,0:T(8,128)S(1)}, bf16...) custom-call(s32[9,128]{1,0:T(8,128)} %refs_0_.1, ...), custom_call_target="tpu_custom_call" | custom-call | bytes 6967296 | tf_op jit(solution)/shard_map/pallas_call | solution.py:500
  9.5 0.0 collective-permute-done.from_low
  9.5 0.1 collective-permute-done.1.from_high
  9.7 0.1 collective-permute-start.2
  9.7 1.7 %collective-permute-start.3 = (bf16[96,256]{1,0:T(8,128)(2,1)S(1)}, bf16[96,256]{1,0:T(8,128)(2,1)S(1)}, u32[]{:S(2)}, u32[]{:S(2)}) collective-permute-start(bf16[96,256]{1,0:T(8,128)(2,1)S(1)} %pad_maximum_fusion.1), channel_id=1, source_target_pairs={{0,3},{1,0},{2,1},{3,2},{4,7},{5,4},{6,5},{7,6},{8,11},{9,8},{10,9... | collective-permute-start | bytes 147464 | tf_op jit(solution)/shard_map/ppermute | solution.py:25
  11.5 1.8 %shard_map.199 = (f32[1152,256]{1,0:T(8,128)S(1)}, bf16[640,1152]{1,0:T(8,128)(2,1)S(1)}, bf16[384,1152]{1,0:T(8,128)(2,1)S(1)}) custom-call(bf16[384,256]{1,0:T(8,128)(2,1)S(1)} %get-tuple-element.61.nodes, bf16[1152,256]{1,0:T(8,128)(2,1)S(1)} %get-tuple-element.63.edges, s32[9,128]{1,0:T(8,128)S(1)} %get-tuple-element.65.senders, ...), custom_call_target="tpu_custom_call" | custom-call | flops 704643072 | bytes 6497280 | tf_op jit(solution)/shard_map/pallas_call | solution.py:500
  13.3 0.0 collective-permute-done.2.upward
  13.3 0.0 collective-permute-done.3.downward
  13.3 5.6 %shard_map.200 = (bf16[1152,256]{1,0:T(8,128)(2,1)S(1)}, bf16[384,256]{1,0:T(8,128)(2,1)S(1)}, bf16[384,256]{1,0:T(8,128)(2,1)S(1)}, f32[384,256]{1,0:T(8,128)S(...) custom-call(s32[1]{0:T(128)S(6)} %copy.22.count_ref, ...), custom_call_target="tpu_custom_call" | custom-call | flops 2583691264 | bytes 11486212 | tf_op jit(solution)/shard_map/pallas_call | solution.py:500
  18.9 1.7 %collective-permute-start.4 = (bf16[1008,256]{1,0:T(8,128)(2,1)S(1)}, bf16[1008,256]{1,0:T(8,128)(2,1)S(1)}, u32[]{:S(2)}, u32[]{:S(2)}) collective-permute-start(bf16[1008,256]{1,0:T(8,128)(2,1)S(1)} %get-tuple-element.86), channel_id=1, source_target_pairs={{0,1},{1,0},{2,3},{3,2},{4,5},{5,4},{6,7},{7,6},{8,9},{9,8},{10,11... | collective-permute-start | bytes 1548296 | tf_op jit(solution)/shard_map/ppermute | solution.py:35
  20.6 1.5 %collective-permute-done.4.other = bf16[1008,256]{1,0:T(8,128)(2,1)S(1)} collective-permute-done((bf16[1008,256]{1,0:T(8,128)(2,1)S(1)}, bf16[1008,256]{1,0:T(8,128)(2,1)S(1)}, u32[]{:S(2)}, u32[]{:S(2)}) %collective-permute-start.4) | collective-permute-done | bytes 516128 | tf_op jit(solution)/shard_map/ppermute | solution.py:35
  22.1 0.8 %shard_map.201 = bf16[4,240,256]{2,1,0:T(8,128)(2,1)} custom-call(f32[896,256]{1,0:T(8,128)S(1)} %get-tuple-element.84.keep, bf16[16,256]{1,0:T(8,128)(2,1)S(1)} %get-tuple-element.85.gains, bf16[1008,256]{1,0:T(8,128)(2,1)S(1)} %collective-permute-done.4.other), custom_call_target="tpu_custom_call" | custom-call | bytes 1933312 | tf_op jit(solution)/shard_map/pallas_call | solution.py:500
  23.0 3.5 %all-to-all-start = ((bf16[4,240,256]{2,1,0:T(8,128)(2,1)}), bf16[4,240,256]{2,1,0:T(8,128)(2,1)S(1)}, u32[]{:S(2)}, u32[]{:S(2)}) async-start(bf16[4,240,256]{2,1,0:T(8,128)(2,1)} %shard_map.201), calls=%async_computation | async-start | bytes 983040 | tf_op jit(solution)/shard_map/all_to_all | solution.py:732
  26.5 1.7 %collective-permute-start.5 = (bf16[96,256]{1,0:T(8,128)(2,1)S(1)}, bf16[96,256]{1,0:T(8,128)(2,1)S(1)}, u32[]{:S(2)}, u32[]{:S(2)}) collective-permute-start(bf16[96,256]{1,0:T(8,128)(2,1)S(1)} %get-tuple-element.87), channel_id=1, source_target_pairs={{0,3},{1,2},{2,1},{3,0},{4,7},{5,6},{6,5},{7,4},{8,11},{9,10},{10,... | collective-permute-start | bytes 147464 | tf_op jit(solution)/shard_map/ppermute | solution.py:31
  28.2 7.2 %collective-permute-done.5.across = bf16[96,256]{1,0:T(8,128)(2,1)S(1)} collective-permute-done((bf16[96,256]{1,0:T(8,128)(2,1)S(1)}, bf16[96,256]{1,0:T(8,128)(2,1)S(1)}, u32[]{:S(2)}, u32[]{:S(2)}) %collective-permute-start.5) | collective-permute-done | bytes 49184 | tf_op jit(solution)/shard_map/ppermute | solution.py:31
  35.4 0.0 all-to-all-done.received
  35.4 0.1 shard_map.203.own
  35.5 2.1 %collective-permute-start.6 = (bf16[240,256]{1,0:T(8,128)(2,1)S(1)}, bf16[240,256]{1,0:T(8,128)(2,1)S(1)}, u32[]{:S(2)}, u32[]{:S(2)}) collective-permute-start(bf16[240,256]{1,0:T(8,128)(2,1)S(1)} %shard_map.203.own), channel_id=1, source_target_pairs={{0,8},{8,0},{1,9},{9,1},{2,10},{10,2},{3,11},{11,3},{4,12},{12,4},... | collective-permute-start | bytes 368648 | tf_op jit(solution)/shard_map/ppermute | solution.py:544
  37.5 1.9 %collective-permute-start.7 = (bf16[96,256]{1,0:T(8,128)(2,1)S(1)}, bf16[96,256]{1,0:T(8,128)(2,1)S(1)}, u32[]{:S(2)}, u32[]{:S(2)}) collective-permute-start(bf16[96,256]{1,0:T(8,128)(2,1)S(1)} %get-tuple-element.92), channel_id=1, source_target_pairs={{0,4},{4,8},{8,12},{12,0},{1,5},{5,9},{9,13},{13,1},{2,6},{6,10},{... | collective-permute-start | bytes 147464 | tf_op jit(solution)/shard_map/ppermute | solution.py:25
  39.5 1.9 %collective-permute-start.8 = (bf16[96,256]{1,0:T(8,128)(2,1)S(1)}, bf16[96,256]{1,0:T(8,128)(2,1)S(1)}, u32[]{:S(2)}, u32[]{:S(2)}) collective-permute-start(bf16[96,256]{1,0:T(8,128)(2,1)S(1)} %get-tuple-element.93), channel_id=1, source_target_pairs={{0,12},{4,0},{8,4},{12,8},{1,13},{5,1},{9,5},{13,9},{2,14},{6,2},{... | collective-permute-start | bytes 147464 | tf_op jit(solution)/shard_map/ppermute | solution.py:25
  41.4 3.4 %collective-permute-done.7.to_high = bf16[96,256]{1,0:T(8,128)(2,1)S(1)} collective-permute-done((bf16[96,256]{1,0:T(8,128)(2,1)S(1)}, bf16[96,256]{1,0:T(8,128)(2,1)S(1)}, u32[]{:S(2)}, u32[]{:S(2)}) %collective-permute-start.7) | collective-permute-done | bytes 49184 | tf_op jit(solution)/shard_map/ppermute | solution.py:25
  44.8 0.0 collective-permute-done.8.to_low
  44.8 1.4 %collective-permute-done.6.other = bf16[240,256]{1,0:T(8,128)(2,1)S(1)} collective-permute-done((bf16[240,256]{1,0:T(8,128)(2,1)S(1)}, bf16[240,256]{1,0:T(8,128)(2,1)S(1)}, u32[]{:S(2)}, u32[]{:S(2)}) %collective-permute-start.6) | collective-permute-done | bytes 122912 | tf_op jit(solution)/shard_map/ppermute | solution.py:544
  46.2 0.8 %shard_map.204 = (f32[16,256]{1,0:T(8,128)S(1)}, bf16[4,224,256]{2,1,0:T(8,128)(2,1)}) custom-call(bf16[240,256]{1,0:T(8,128)(2,1)S(1)} %shard_map.203.own, bf16[240,256]{1,0:T(8,128)(2,1)S(1)} %collective-permute-done.6.other), custom_call_target="tpu_custom_call" | custom-call | bytes 720896 | tf_op jit(solution)/shard_map/pallas_call | solution.py:500
  47.1 3.5 %all-to-all-start.1 = ((bf16[4,224,256]{2,1,0:T(8,128)(2,1)}), bf16[4,224,256]{2,1,0:T(8,128)(2,1)S(1)}, u32[]{:S(2)}, u32[]{:S(2)}) async-start(bf16[4,224,256]{2,1,0:T(8,128)(2,1)} %get-tuple-element.95), calls=%async_computation.1 | async-start | bytes 917504 | tf_op jit(solution)/shard_map/all_to_all | solution.py:749
  50.6 1.3 %shard_map.205 = (bf16[1152,256]{1,0:T(8,128)(2,1)}, f32[384,256]{1,0:T(8,128)S(1)}) custom-call(bf16[1152,256]{1,0:T(8,128)(2,1)S(1)} %get-tuple-element.64.edge_grads, bf16[1152,256]{1,0:T(8,128)(2,1)S(1)} %get-tuple-element.97.pre_grad, bf16[384,256]{1,0:T(8,128)(2,1)S(1)} %get-tuple-element.98.sender_sum, ...), custom_call_target="tpu_custom_call" | custom-call | flops 251658240 | bytes 3342336 | tf_op jit(solution)/shard_map/pallas_call | solution.py:500
  51.9 1.1 %shard_map.206 = bf16[384,256]{1,0:T(8,128)(2,1)} custom-call(s32[8,32]{1,0:T(8,128)S(1)} %get-tuple-element.96.send_list, f32[384,256]{1,0:T(8,128)S(1)} %get-tuple-element.101.local_grad, bf16[64,256]{1,0:T(8,128)(2,1)S(1)} %get-tuple-element.102.middle, bf16[96,256]{1,0:T(8,128)(2,1)S(1)} %collective-permute-done.7.to_high, ...), custom_call_target="tpu_custom_call" | custom-call | flops 50331648 | bytes 721920 | tf_op jit(solution)/shard_map/pallas_call | solution.py:500
  53.0 4.3 %all-to-all-done.1.own = bf16[4,224,256]{2,1,0:T(8,128)(2,1)S(1)} async-done(((bf16[4,224,256]{2,1,0:T(8,128)(2,1)}), bf16[4,224,256]{2,1,0:T(8,128)(2,1)S(1)}, u32[]{:S(2)}, u32[]{:S(2)}) %all-to-all-start.1) | async-done | bytes 458784 | tf_op jit(solution)/shard_map/all_to_all | solution.py:749
  57.3 0.0 collective-permute-start.9
  57.3 0.5 convert_reduce_fusion
  57.8 1.3 %collective-permute-done.9.other = bf16[4,224,256]{2,1,0:T(8,128)(2,1)S(1)} collective-permute-done((bf16[4,224,256]{2,1,0:T(8,128)(2,1)S(1)}, bf16[4,224,256]{2,1,0:T(8,128)(2,1)S(1)}, u32[]{:S(2)}, u32[]{:S(2)}) %collective-permute-start.9) | collective-permute-done | bytes 458784 | tf_op jit(solution)/shard_map/ppermute | solution.py:35
  59.1 1.1 %shard_map.207 = (bf16[768,256]{1,0:T(8,128)(2,1)}, bf16[256,256]{1,0:T(8,128)(2,1)}, bf16[512,256]{1,0:T(8,128)(2,1)}, bf16[256,256]{1,0:T(8,128)(2,1)}) custom-call(bf16[4,224,256]{2,1,0:T(8,128)(2,1)S(1)} %all-to-all-done.1.own, bf16[4,224,256]{2,1,0:T(8,128)(2,1)S(1)} %collective-permute-done.9.other), custom_call_target="tpu_custom_call" | custom-call | bytes 1835008 | tf_op jit(solution)/shard_map/pallas_call | solution.py:500
  (5 shorter events, 0.0 us)
Async XLA Ops:
  1.9 7.6 %collective-permute-start = (bf16[96,256]{1,0:T(8,128)(2,1)S(1)}, bf16[96,256]{1,0:T(8,128)(2,1)S(1)}, u32[]{:S(2)}, u32[]{:S(2)}) collective-permute-start(bf16[96,256]{1,0:T(8,128)(2,1)S(1)} %get-tuple-element.67), channel_id=1, source_target_pairs={{0,4},{4,8},{8,12},{12,0},{1,5},{5,9},{9,13},{13,1},{2,6},{6,10},{... | collective-permute-start | bytes 147464 | tf_op jit(solution)/shard_map/ppermute | solution.py:25
  5.0 4.6 %collective-permute-start.1 = (bf16[96,256]{1,0:T(8,128)(2,1)S(1)}, bf16[96,256]{1,0:T(8,128)(2,1)S(1)}, u32[]{:S(2)}, u32[]{:S(2)}) collective-permute-start(bf16[96,256]{1,0:T(8,128)(2,1)S(1)} %get-tuple-element.68), channel_id=1, source_target_pairs={{0,12},{4,0},{8,4},{12,8},{1,13},{5,1},{9,5},{13,9},{2,14},{6,2},{... | collective-permute-start | bytes 147464 | tf_op jit(solution)/shard_map/ppermute | solution.py:25
  9.7 3.6 %collective-permute-start.2 = (bf16[96,256]{1,0:T(8,128)(2,1)S(1)}, bf16[96,256]{1,0:T(8,128)(2,1)S(1)}, u32[]{:S(2)}, u32[]{:S(2)}) collective-permute-start(bf16[96,256]{1,0:T(8,128)(2,1)S(1)} %pad_maximum_fusion), channel_id=1, source_target_pairs={{0,1},{1,2},{2,3},{3,0},{4,5},{5,6},{6,7},{7,4},{8,9},{9,10},{10,1... | collective-permute-start | bytes 147464 | tf_op jit(solution)/shard_map/ppermute | solution.py:25
  9.7 3.6 %collective-permute-start.3 = (bf16[96,256]{1,0:T(8,128)(2,1)S(1)}, bf16[96,256]{1,0:T(8,128)(2,1)S(1)}, u32[]{:S(2)}, u32[]{:S(2)}) collective-permute-start(bf16[96,256]{1,0:T(8,128)(2,1)S(1)} %pad_maximum_fusion.1), channel_id=1, source_target_pairs={{0,3},{1,0},{2,1},{3,2},{4,7},{5,4},{6,5},{7,6},{8,11},{9,8},{10,9... | collective-permute-start | bytes 147464 | tf_op jit(solution)/shard_map/ppermute | solution.py:25
  18.9 3.2 %collective-permute-start.4 = (bf16[1008,256]{1,0:T(8,128)(2,1)S(1)}, bf16[1008,256]{1,0:T(8,128)(2,1)S(1)}, u32[]{:S(2)}, u32[]{:S(2)}) collective-permute-start(bf16[1008,256]{1,0:T(8,128)(2,1)S(1)} %get-tuple-element.86), channel_id=1, source_target_pairs={{0,1},{1,0},{2,3},{3,2},{4,5},{5,4},{6,7},{7,6},{8,9},{9,8},{10,11... | collective-permute-start | bytes 1548296 | tf_op jit(solution)/shard_map/ppermute | solution.py:35
  23.0 12.4 %all-to-all-start = ((bf16[4,240,256]{2,1,0:T(8,128)(2,1)}), bf16[4,240,256]{2,1,0:T(8,128)(2,1)S(1)}, u32[]{:S(2)}, u32[]{:S(2)}) async-start(bf16[4,240,256]{2,1,0:T(8,128)(2,1)} %shard_map.201), calls=%async_computation | async-start | bytes 983040 | tf_op jit(solution)/shard_map/all_to_all | solution.py:732
  26.5 8.9 %collective-permute-start.5 = (bf16[96,256]{1,0:T(8,128)(2,1)S(1)}, bf16[96,256]{1,0:T(8,128)(2,1)S(1)}, u32[]{:S(2)}, u32[]{:S(2)}) collective-permute-start(bf16[96,256]{1,0:T(8,128)(2,1)S(1)} %get-tuple-element.87), channel_id=1, source_target_pairs={{0,3},{1,2},{2,1},{3,0},{4,7},{5,6},{6,5},{7,4},{8,11},{9,10},{10,... | collective-permute-start | bytes 147464 | tf_op jit(solution)/shard_map/ppermute | solution.py:31
  35.5 10.8 %collective-permute-start.6 = (bf16[240,256]{1,0:T(8,128)(2,1)S(1)}, bf16[240,256]{1,0:T(8,128)(2,1)S(1)}, u32[]{:S(2)}, u32[]{:S(2)}) collective-permute-start(bf16[240,256]{1,0:T(8,128)(2,1)S(1)} %shard_map.203.own), channel_id=1, source_target_pairs={{0,8},{8,0},{1,9},{9,1},{2,10},{10,2},{3,11},{11,3},{4,12},{12,4},... | collective-permute-start | bytes 368648 | tf_op jit(solution)/shard_map/ppermute | solution.py:544
  37.5 7.3 %collective-permute-start.7 = (bf16[96,256]{1,0:T(8,128)(2,1)S(1)}, bf16[96,256]{1,0:T(8,128)(2,1)S(1)}, u32[]{:S(2)}, u32[]{:S(2)}) collective-permute-start(bf16[96,256]{1,0:T(8,128)(2,1)S(1)} %get-tuple-element.92), channel_id=1, source_target_pairs={{0,4},{4,8},{8,12},{12,0},{1,5},{5,9},{9,13},{13,1},{2,6},{6,10},{... | collective-permute-start | bytes 147464 | tf_op jit(solution)/shard_map/ppermute | solution.py:25
  39.5 5.3 %collective-permute-start.8 = (bf16[96,256]{1,0:T(8,128)(2,1)S(1)}, bf16[96,256]{1,0:T(8,128)(2,1)S(1)}, u32[]{:S(2)}, u32[]{:S(2)}) collective-permute-start(bf16[96,256]{1,0:T(8,128)(2,1)S(1)} %get-tuple-element.93), channel_id=1, source_target_pairs={{0,12},{4,0},{8,4},{12,8},{1,13},{5,1},{9,5},{13,9},{2,14},{6,2},{... | collective-permute-start | bytes 147464 | tf_op jit(solution)/shard_map/ppermute | solution.py:25
  47.1 10.2 %all-to-all-start.1 = ((bf16[4,224,256]{2,1,0:T(8,128)(2,1)}), bf16[4,224,256]{2,1,0:T(8,128)(2,1)S(1)}, u32[]{:S(2)}, u32[]{:S(2)}) async-start(bf16[4,224,256]{2,1,0:T(8,128)(2,1)} %get-tuple-element.95), calls=%async_computation.1 | async-start | bytes 917504 | tf_op jit(solution)/shard_map/all_to_all | solution.py:749
  57.3 1.8 %collective-permute-start.9 = (bf16[4,224,256]{2,1,0:T(8,128)(2,1)S(1)}, bf16[4,224,256]{2,1,0:T(8,128)(2,1)S(1)}, u32[]{:S(2)}, u32[]{:S(2)}) collective-permute-start(bf16[4,224,256]{2,1,0:T(8,128)(2,1)S(1)} %all-to-all-done.1.own), channel_id=1, source_target_pairs={{0,1},{1,0},{2,3},{3,2},{4,5},{5,4},{6,7},{7,6},{8,9},{9,8},{10,11... | collective-permute-start | bytes 1376264 | tf_op jit(solution)/shard_map/ppermute | solution.py:35

commit v11 on v10

--- a/solution.py
+++ b/solution.py
@@ -151,7 +151,17 @@
 
 
 def local_kernel(
-    nodes, edges, senders, receivers, near_rows, w_in, pre, sender_columns, receiver_columns
+    nodes,
+    edges,
+    senders,
+    receivers,
+    near_rows,
+    w_in,
+    pre,
+    sender_columns,
+    receiver_columns,
+    nodes_turned,
+    edges_turned,
 ):
     width = nodes.shape[1]
     tile_rows = senders.shape[1]
@@ -172,6 +182,8 @@
         axis=0,
     )
     pre[...] = dot(edges[...], w_in[:width]) + dot(near_rows[...], table)
+    nodes_turned[...] = x.T
+    edges_turned[...] = edges[...].T
 
 
 def split_by_core(sums, first, keep_out, away_out):
@@ -198,7 +210,8 @@
     count_ref,
     nodes,
     node_grads,
-    edges,
+    nodes_turned,
+    edges_turned,
     edge_grads,
     pre_local,
     halo_rows,
@@ -218,7 +231,7 @@
     pre_grad_out,
     sender_out,
     receiver_out,
-    node_part_out,
+    node_grad_out,
     across_out,
     rest_out,
     keep_out,
@@ -232,7 +245,7 @@
     edge_sums,
 ):
     count, width = nodes.shape
-    edge_rows = edges.shape[0]
+    edge_rows = edge_grads.shape[0]
     live = live_rows(count_ref, tile_rows, edge_rows)
     slots = from_high.shape[0] // 3
     halo = jnp.concatenate(
@@ -273,8 +286,8 @@
     slope = sigma * (1.0 + node_pre * (1.0 - sigma))
     pre_grad = (dot_nt(out_grad, w_node_out[...]) * slope).astype(BF16)
     agg_grad = dot_nt(pre_grad, w_second).astype(BF16)
-    node_part_out[...] = upstream + dot_nt(pre_grad, w_first)
-    node_sums[:width] = dot_tn(x, pre_grad)
+    node_grad_out[...] = pre_grad
+    node_sums[:width] = dot(nodes_turned[...], pre_grad)
     node_sums[width : 2 * width] = dot_tn(aggregated, pre_grad)
     node_sums[2 * width : 3 * width] = dot_tn(node_hidden, out_grad)
     node_gain = jnp.sum(upstream * normed, axis=0, keepdims=True)
@@ -311,9 +324,9 @@
         across_out[...] = up
 
     rest_out[...] = jnp.concatenate([parts[1], parts[6]], axis=0)
-    edge_sums[:width] = dot_tn(edges[...], pre_grad)
-    edge_sums[width : 2 * width] = dot_tn(x, own) + dot_tn(halo, away)
-    edge_sums[2 * width : 3 * width] = dot_tn(x, received)
+    edge_sums[:width] = dot(edges_turned[...], pre_grad)
+    edge_sums[width : 2 * width] = dot(nodes_turned[...], own) + dot_tn(halo, away)
+    edge_sums[2 * width : 3 * width] = dot(nodes_turned[...], received)
     edge_sums[3 * width : 4 * width] = dot_tn(hidden_kept[...], out_grad)
     split_by_core(edge_sums, 0, keep_out, away_out)
     split_by_core(node_sums, edge_sums.shape[0] // 2, keep_out, away_out)
@@ -322,27 +335,22 @@
     gains_out[...] = gains
 
 
-def pair_kernel(parts, keep, gains, other, blocks_out, total, staged, sems):
+def pair_kernel(parts, keep, gains, other, blocks_out):
     rows = keep.shape[0]
     chips = blocks_out.shape[0]
     packed = gains.shape[0]
     both = gains[...].astype(F32) + other[rows : rows + packed].astype(F32)
     summed = pack_gains(both[0:1] + both[1:2], both[2:3] + both[3:4])
-    total[...] = (keep[...] + other[:rows].astype(F32)).astype(BF16)
-    copies = []
     for chip in range(chips):
-        staged[chip, :packed, :] = summed
+        blocks_out[chip, :packed, :] = summed
         first, at = 0, packed
         for part in parts:
             step = part // chips
-            staged[chip, at : at + step, :] = total[first + chip * step : first + (chip + 1) * step]
+            rows_in = slice(first + chip * step, first + (chip + 1) * step)
+            blocks_out[chip, at : at + step, :] = (
+                keep[rows_in] + other[rows_in].astype(F32)
+            ).astype(BF16)
             first, at = first + part, at + step
-        copies.append(
-            pltpu.make_async_copy(staged.at[chip], blocks_out.at[chip], sems.at[chip])
-        )
-        copies[-1].start()
-    for copy in copies:
-        copy.wait()
 
 
 def add_packed(values):
@@ -365,19 +373,13 @@
     sums_out[:16] = add_packed(sums)
 
 
-def spread_kernel(own, other, gains_out, spread_out, mine, sems):
+def spread_kernel(own, other, gains_out, spread_out):
     packed = gains_out.shape[0]
     sums = own[...].astype(F32) + other[...].astype(F32)
-    mine[...] = sums[packed:].astype(BF16)
-    copies = [
-        pltpu.make_async_copy(mine, spread_out.at[chip], sems.at[chip])
-        for chip in range(spread_out.shape[0])
-    ]
-    for copy in copies:
-        copy.start()
     gains_out[...] = sums[:packed]
-    for copy in copies:
-        copy.wait()
+    mine = sums[packed:].astype(BF16)
+    for chip in range(spread_out.shape[0]):
+        spread_out[chip] = mine
 
 
 def place_kernel(parts, own, other, *refs):
@@ -422,14 +424,24 @@
 
 
 def finish_kernel(
-    edge_grads, pre_grad, sender_sum, receiver_sum, node_part, w_in, edges_grad, local_grad
+    edge_grads,
+    node_grads,
+    pre_grad,
+    sender_sum,
+    receiver_sum,
+    node_pre_grad,
+    w_in,
+    w_node_in,
+    edges_grad,
+    local_grad,
 ):
     width = w_in.shape[1]
     edges_grad[...] = (
         edge_grads[...].astype(F32) + dot_nt(pre_grad[...], w_in[:width])
     ).astype(BF16)
     local_grad[...] = (
-        node_part[...]
+        node_grads[...].astype(F32)
+        + dot_nt(node_pre_grad[...], w_node_in[:width])
         + dot_nt(sender_sum[...], w_in[width : 2 * width])
         + dot_nt(receiver_sum[...], w_in[2 * width :])
     )
@@ -554,8 +566,6 @@
         0,
         sums,
         other,
-        out_space=[VMEM, HBM],
-        scratch=[pltpu.VMEM((mine, width), BF16), pltpu.SemaphoreType.DMA((chips,))],
     )
     return gains, spread, *beside
 
@@ -571,12 +581,6 @@
         keep,
         gains,
         other,
-        out_space=HBM,
-        scratch=[
-            pltpu.VMEM((rows, width), BF16),
-            pltpu.VMEM(shape, BF16),
-            pltpu.SemaphoreType.DMA((chips,)),
-        ],
     )
     return blocks
 
@@ -665,12 +669,14 @@
     downward = passed_along(
         jnp.concatenate([from_high[:slots], mid[:slots], from_low[:slots]]), PY, -1
     )
-    pre_local, sender_columns, receiver_columns = call(
+    pre_local, sender_columns, receiver_columns, nodes_turned, edges_turned = call(
         local_kernel,
         [
             shaped(edge_rows, width, F32),
             shaped(count + halo_rows, edge_rows, BF16),
             shaped(count, edge_rows, BF16),
+            shaped(width, count, BF16),
+            shaped(width, edge_rows, BF16),
         ],
         square * (2 * count + edge_rows) + 4 * edge_rows * count * width,
         nodes,
@@ -682,13 +688,13 @@
     )
     parts = (2 * width, 3 * width // 2)
     halves = sum(parts)
-    pre_grad, sender_sum, receiver_sum, node_part, across, rest, keep, away, gains = call(
+    pre_grad, sender_sum, receiver_sum, node_pre_grad, across, rest, keep, away, gains = call(
         functools.partial(layer_kernel, tile_rows),
         [
             shaped(edge_rows, width, BF16),
             shaped(count, width, BF16),
             shaped(count, width, BF16),
-            shaped(count, width, F32),
+            shaped(count, width, BF16),
             shaped(3 * slots, width, BF16),
             shaped(2 * slots, width, BF16),
             shaped(halves, width, F32),
@@ -700,7 +706,8 @@
         tile_count,
         nodes,
         node_grads,
-        edges,
+        nodes_turned,
+        edges_turned,
         edge_grads,
         pre_local,
         halo_hot,
@@ -737,7 +744,7 @@
             shaped(3 * slots, width, BF16),
             shaped(2 * slots, width, BF16),
         ],
-        0,
+        10**10,
         other,
         across_chips(across),
         rest,
@@ -750,13 +757,15 @@
     edges_grad, local_grad = call(
         finish_kernel,
         [shaped(edge_rows, width, BF16), shaped(count, width, F32)],
-        square * (edge_rows + 2 * count),
+        square * (edge_rows + 3 * count),
         edge_grads,
+        node_grads,
         pre_grad,
         sender_sum,
         receiver_sum,
-        node_part,
+        node_pre_grad,
         w_edge_in,
+        w_node_in,
     )
     (nodes_grad,) = call(
         return_kernel,

time: 60.5 us -> 60.2 us (level)
  starting transfers between devices: 23.1 us -> 21.7 us
  local copies, waits for them, and re-layouts: 0.01 us -> 1.3 us
  waiting for transfers between devices: 19.3 us -> 18.3 us
  Pallas kernels: 15.8 us -> 16.6 us
    ppermute x1, waiting for transfers between devices: 7.21 us -> 0.01 us  [across_chips(): return lax.ppermute(array, PY, pairs)]
    all_to_all x1, waiting for transfers between devices: 0.01 us -> 7 us  [on_device(): received = lax.all_to_all(blocks, SQUARE, 0, 0)]
    ppermute x1, starting transfers between devices: 1.68 us -> 0.07 us  [across_chips(): return lax.ppermute(array, PY, pairs)]
    unnamed x0 -> x6, local copies, waits for them, and re-layouts: none -> 1.29 us
    ppermute x6, waiting for transfers between devices: 3.55 us -> 2.67 us  [passed_along(): lax.ppermute(array, axis, [(i, (i + by) % size) for i in range(size)])]
    pallas_call x11, Pallas kernels: 15.8 us -> 16.6 us  [call(): pl.pallas_call(body, out_shape=outs, in_specs=[pl.BlockSpec(memory_space=...]
  transfers between devices with their start and end apart: 12 -> 12, of which waited for: 7 -> 7; matrix products, arithmetic and copies ran while one was open for 1% -> 1% of each run, Pallas kernels for 10% -> 13%
where the time goes in v11:
time: 60.2 us; the launch traced here: 59.9 us
  starting transfers between devices  21.7 us (36%)
  waiting for transfers between devices  18.3 us (30%)
  Pallas kernels  16.6 us (28%)
  between operations  1.42 us (2%)
  local copies, waits for them, and re-layouts  1.3 us (2%)
    pallas_call x11, Pallas kernels, call(): pl.pallas_call(body, out_shape=outs, in_specs=[pl.BlockSpec(memory_space=...  16.6 us
    ppermute x6, starting transfers between devices, passed_along(): lax.ppermute(array, axis, [(i, (i + by) % size) for i in range(size)])  10.8 us
    all_to_all x1, waiting for transfers between devices, on_device(): received = lax.all_to_all(blocks, SQUARE, 0, 0)  7 us
    all_to_all x1, waiting for transfers between devices, on_device(): own = lax.all_to_all(spread, SQUARE, 0, 0)  4.62 us
    all_to_all x1, starting transfers between devices, on_device(): received = lax.all_to_all(blocks, SQUARE, 0, 0)  3.47 us
    all_to_all x1, starting transfers between devices, on_device(): own = lax.all_to_all(spread, SQUARE, 0, 0)  3.46 us
    ppermute x2, waiting for transfers between devices, across_cores(): return lax.ppermute(array, CORE, [(0, 1), (1, 0)])  2.73 us
    ppermute x6, waiting for transfers between devices, passed_along(): lax.ppermute(array, axis, [(i, (i + by) % size) for i in range(size)])  2.67 us
  transfers between devices with their start and end apart: 12, of which 7 were waited for; matrix products, arithmetic and copies ran while one was open for 1% of the time, Pallas kernels for 13%

profile of v11, /device:TPU:0, one launch (start us, length us, event | category | flops | bytes accessed | tf_op | source)
XLA Modules:
  0.0 59.9 jit_solution(14982256077550640658)
XLA Ops:
  0.6 1.3 %shard_map.197 = (bf16[96,256]{1,0:T(8,128)(2,1)S(1)}, bf16[64,256]{1,0:T(8,128)(2,1)S(1)}, bf16[96,256]{1,0:T(8,128)(2,1)S(1)}, bf16[384,256]{1,0:T(8,128)(2,1)S(1)}, s32[8,32]{1,0:T(8,128)S(1)}) custom-call(bf16[384,256]{1,0:T(8,128)(2,1)} %nodes_hbm.1, s32[8,32]{1,0:T(8,128)} %list_hbm.1), custom_call_target="tpu_custom_call" | custom-call | flops 50331648 | bytes 526336 | tf_op jit(solution)/shard_map/pallas_call | solution.py:512
  1.9 3.1 %collective-permute-start = (bf16[96,256]{1,0:T(8,128)(2,1)S(1)}, bf16[96,256]{1,0:T(8,128)(2,1)S(1)}, u32[]{:S(2)}, u32[]{:S(2)}) collective-permute-start(bf16[96,256]{1,0:T(8,128)(2,1)S(1)} %get-tuple-element.68), channel_id=1, source_target_pairs={{0,4},{4,8},{8,12},{12,0},{1,5},{5,9},{9,13},{13,1},{2,6},{6,10},{... | collective-permute-start | bytes 147464 | tf_op jit(solution)/shard_map/ppermute | solution.py:25
  5.0 2.1 %collective-permute-start.1 = (bf16[96,256]{1,0:T(8,128)(2,1)S(1)}, bf16[96,256]{1,0:T(8,128)(2,1)S(1)}, u32[]{:S(2)}, u32[]{:S(2)}) collective-permute-start(bf16[96,256]{1,0:T(8,128)(2,1)S(1)} %get-tuple-element.69), channel_id=1, source_target_pairs={{0,12},{4,0},{8,4},{12,8},{1,13},{5,1},{9,5},{13,9},{2,14},{6,2},{... | collective-permute-start | bytes 147464 | tf_op jit(solution)/shard_map/ppermute | solution.py:25
  7.8 1.7 %shard_map.198 = (bf16[1152,768]{1,0:T(8,128)(2,1)S(1)}, bf16[1152,256]{1,0:T(8,128)(2,1)S(1)}, s32[9,128]{1,0:T(8,128)S(1)}, s32[9,128]{1,0:T(8,128)S(1)}, bf16...) custom-call(s32[9,128]{1,0:T(8,128)} %refs_0_.1, ...), custom_call_target="tpu_custom_call" | custom-call | bytes 6967296 | tf_op jit(solution)/shard_map/pallas_call | solution.py:512
  9.5 0.0 collective-permute-done.from_low
  9.5 0.1 collective-permute-done.1.from_high
  9.7 0.1 collective-permute-start.2
  9.7 1.7 %collective-permute-start.3 = (bf16[96,256]{1,0:T(8,128)(2,1)S(1)}, bf16[96,256]{1,0:T(8,128)(2,1)S(1)}, u32[]{:S(2)}, u32[]{:S(2)}) collective-permute-start(bf16[96,256]{1,0:T(8,128)(2,1)S(1)} %pad_maximum_fusion.1), channel_id=1, source_target_pairs={{0,3},{1,0},{2,1},{3,2},{4,7},{5,4},{6,5},{7,6},{8,11},{9,8},{10,9... | collective-permute-start | bytes 147464 | tf_op jit(solution)/shard_map/ppermute | solution.py:25
  11.5 1.8 %shard_map.199 = (f32[1152,256]{1,0:T(8,128)S(1)}, bf16[640,1152]{1,0:T(8,128)(2,1)S(1)}, bf16[384,1152]{1,0:T(8,128)(2,1)S(1)}, bf16[256,384]{1,0:T(8,128)(2,1)S(1)}, bf16[256,1152]{1,0:T(8,128)(2,1)S(1)}) custom-call(bf16[384,256]{1,0:T(8,128)(2,1)S(1)} %get-tuple-element.63.nodes, bf16[1152,256]{1,0:T(8,128)(2,1)S(1)} %get-tuple-element.65.edges, ...), custom_call_target="tpu_custom_call" | custom-call | flops 704643072 | bytes 7283712 | tf_op jit(solution)/shard_map/pallas_call | solution.py:512
  13.3 0.0 collective-permute-done.2.upward
  13.3 0.0 collective-permute-done.3.downward
  13.3 5.7 %shard_map.200 = (bf16[1152,256]{1,0:T(8,128)(2,1)S(1)}, bf16[384,256]{1,0:T(8,128)(2,1)S(1)}, bf16[384,256]{1,0:T(8,128)(2,1)S(1)}, bf16[384,256]{1,0:T(8,128)(...) custom-call(s32[1]{0:T(128)S(6)} %copy.22.count_ref, ...), custom_call_target="tpu_custom_call" | custom-call | flops 2583691264 | bytes 11486212 | tf_op jit(solution)/shard_map/pallas_call | solution.py:512
  19.0 0.0 copy-start
  19.0 0.7 %copy-done = bf16[384,256]{1,0:T(8,128)(2,1)} copy-done((bf16[384,256]{1,0:T(8,128)(2,1)}, bf16[384,256]{1,0:T(8,128)(2,1)S(1)}, u32[]{:S(2)}) %copy-start) | copy-done | bytes 196632
  19.7 1.6 %collective-permute-start.4 = (bf16[1008,256]{1,0:T(8,128)(2,1)S(1)}, bf16[1008,256]{1,0:T(8,128)(2,1)S(1)}, u32[]{:S(2)}, u32[]{:S(2)}) collective-permute-start(bf16[1008,256]{1,0:T(8,128)(2,1)S(1)} %get-tuple-element.90), channel_id=1, source_target_pairs={{0,1},{1,0},{2,3},{3,2},{4,5},{5,4},{6,7},{7,6},{8,9},{9,8},{10,11... | collective-permute-start | bytes 1548296 | tf_op jit(solution)/shard_map/ppermute | solution.py:35
  21.3 0.1 collective-permute-start.5
  21.3 1.5 %collective-permute-done.4.other = bf16[1008,256]{1,0:T(8,128)(2,1)S(1)} collective-permute-done((bf16[1008,256]{1,0:T(8,128)(2,1)S(1)}, bf16[1008,256]{1,0:T(8,128)(2,1)S(1)}, u32[]{:S(2)}, u32[]{:S(2)}) %collective-permute-start.4) | collective-permute-done | bytes 516128 | tf_op jit(solution)/shard_map/ppermute | solution.py:35
  22.8 0.9 %shard_map.201 = bf16[4,240,256]{2,1,0:T(8,128)(2,1)} custom-call(f32[896,256]{1,0:T(8,128)S(1)} %get-tuple-element.88.keep, bf16[16,256]{1,0:T(8,128)(2,1)S(1)} %get-tuple-element.89.gains, bf16[1008,256]{1,0:T(8,128)(2,1)S(1)} %collective-permute-done.4.other), custom_call_target="tpu_custom_call" | custom-call | bytes 1933312 | tf_op jit(solution)/shard_map/pallas_call | solution.py:512
  23.7 3.5 %all-to-all-start = ((bf16[4,240,256]{2,1,0:T(8,128)(2,1)}), bf16[4,240,256]{2,1,0:T(8,128)(2,1)S(1)}, u32[]{:S(2)}, u32[]{:S(2)}) async-start(bf16[4,240,256]{2,1,0:T(8,128)(2,1)} %shard_map.201), calls=%async_computation | async-start | bytes 983040 | tf_op jit(solution)/shard_map/all_to_all | solution.py:739
  27.1 0.0 collective-permute-done.5.across
  27.2 0.8 %shard_map.202 = (bf16[96,256]{1,0:T(8,128)(2,1)S(1)}, bf16[96,256]{1,0:T(8,128)(2,1)S(1)}, bf16[64,256]{1,0:T(8,128)(2,1)S(1)}) custom-call(bf16[1008,256]{1,0:T(8,128)(2,1)S(1)} %collective-permute-done.4.other, bf16[96,256]{1,0:T(8,128)(2,1)} %collective-permute-done.5.across, bf16[64,256]{1,0:T(8,128)(2,1)S(1)} %get-tuple-element.92.rest), custom_call_target="tpu_custom_call" | custom-call | flops 10000000000 | bytes 729088 | tf_op jit(solution)/shard_map/pallas_call | solution.py:512
  28.0 0.0 copy-start.2
  28.0 0.6 %copy-done.2 = bf16[96,256]{1,0:T(8,128)(2,1)} copy-done((bf16[96,256]{1,0:T(8,128)(2,1)}, bf16[96,256]{1,0:T(8,128)(2,1)S(1)}, u32[]{:S(2)}) %copy-start.2) | copy-done | bytes 49176
  28.6 0.0 copy-start.1
  28.6 7.0 %all-to-all-done.received = bf16[4,240,256]{2,1,0:T(8,128)(2,1)S(1)} async-done(((bf16[4,240,256]{2,1,0:T(8,128)(2,1)}), bf16[4,240,256]{2,1,0:T(8,128)(2,1)S(1)}, u32[]{:S(2)}, u32[]{:S(2)}) %all-to-all-start) | async-done | bytes 491552 | tf_op jit(solution)/shard_map/all_to_all | solution.py:739
  35.6 0.1 shard_map.203.own
  35.7 2.3 %collective-permute-start.6 = (bf16[240,256]{1,0:T(8,128)(2,1)S(1)}, bf16[240,256]{1,0:T(8,128)(2,1)S(1)}, u32[]{:S(2)}, u32[]{:S(2)}) collective-permute-start(bf16[240,256]{1,0:T(8,128)(2,1)S(1)} %shard_map.203.own), channel_id=1, source_target_pairs={{0,8},{8,0},{1,9},{9,1},{2,10},{10,2},{3,11},{11,3},{4,12},{12,4},... | collective-permute-start | bytes 368648 | tf_op jit(solution)/shard_map/ppermute | solution.py:556
  38.0 1.1 %collective-permute-start.7 = (bf16[96,256]{1,0:T(8,128)(2,1)}, bf16[96,256]{1,0:T(8,128)(2,1)S(1)}, u32[]{:S(2)}, u32[]{:S(2)}) collective-permute-start(bf16[96,256]{1,0:T(8,128)(2,1)} %copy-done.2), channel_id=1, source_target_pairs={{0,4},{4,8},{8,12},{12,0},{1,5},{5,9},{9,13},{13,1},{2,6},{6,10},{... | collective-permute-start | bytes 147464 | tf_op jit(solution)/shard_map/ppermute | solution.py:25
  39.1 2.7 %collective-permute-start.8 = (bf16[96,256]{1,0:T(8,128)(2,1)S(1)}, bf16[96,256]{1,0:T(8,128)(2,1)S(1)}, u32[]{:S(2)}, u32[]{:S(2)}) collective-permute-start(bf16[96,256]{1,0:T(8,128)(2,1)S(1)} %get-tuple-element.97), channel_id=1, source_target_pairs={{0,12},{4,0},{8,4},{12,8},{1,13},{5,1},{9,5},{13,9},{2,14},{6,2},{... | collective-permute-start | bytes 147464 | tf_op jit(solution)/shard_map/ppermute | solution.py:25
  41.8 2.6 %collective-permute-done.7.to_high = bf16[96,256]{1,0:T(8,128)(2,1)S(1)} collective-permute-done((bf16[96,256]{1,0:T(8,128)(2,1)}, bf16[96,256]{1,0:T(8,128)(2,1)S(1)}, u32[]{:S(2)}, u32[]{:S(2)}) %collective-permute-start.7) | collective-permute-done | bytes 49184 | tf_op jit(solution)/shard_map/ppermute | solution.py:25
  44.4 0.0 collective-permute-done.8.to_low
  44.4 1.3 %collective-permute-done.6.other = bf16[240,256]{1,0:T(8,128)(2,1)S(1)} collective-permute-done((bf16[240,256]{1,0:T(8,128)(2,1)S(1)}, bf16[240,256]{1,0:T(8,128)(2,1)S(1)}, u32[]{:S(2)}, u32[]{:S(2)}) %collective-permute-start.6) | collective-permute-done | bytes 122912 | tf_op jit(solution)/shard_map/ppermute | solution.py:556
  45.7 0.8 %shard_map.204 = (f32[16,256]{1,0:T(8,128)S(1)}, bf16[4,224,256]{2,1,0:T(8,128)(2,1)}) custom-call(bf16[240,256]{1,0:T(8,128)(2,1)S(1)} %shard_map.203.own, bf16[240,256]{1,0:T(8,128)(2,1)S(1)} %collective-permute-done.6.other), custom_call_target="tpu_custom_call" | custom-call | bytes 720896 | tf_op jit(solution)/shard_map/pallas_call | solution.py:512
  46.5 3.5 %all-to-all-start.1 = ((bf16[4,224,256]{2,1,0:T(8,128)(2,1)}), bf16[4,224,256]{2,1,0:T(8,128)(2,1)S(1)}, u32[]{:S(2)}, u32[]{:S(2)}) async-start(bf16[4,224,256]{2,1,0:T(8,128)(2,1)} %get-tuple-element.99), calls=%async_computation.1 | async-start | bytes 917504 | tf_op jit(solution)/shard_map/all_to_all | solution.py:756
  49.9 0.0 copy-done.1
  49.9 1.3 %shard_map.205 = (bf16[1152,256]{1,0:T(8,128)(2,1)}, f32[384,256]{1,0:T(8,128)S(1)}) custom-call(bf16[1152,256]{1,0:T(8,128)(2,1)S(1)} %get-tuple-element.75.edge_grads, bf16[384,256]{1,0:T(8,128)(2,1)S(1)} %get-tuple-element.64.node_grads, bf16[1152,256]{1,0:T(8,128)(2,1)S(1)} %get-tuple-element.101.pre_grad, ...), custom_call_target="tpu_custom_call" | custom-call | flops 301989888 | bytes 3604480 | tf_op jit(solution)/shard_map/pallas_call | solution.py:512
  51.3 1.1 %shard_map.206 = bf16[384,256]{1,0:T(8,128)(2,1)} custom-call(s32[8,32]{1,0:T(8,128)S(1)} %get-tuple-element.100.send_list, f32[384,256]{1,0:T(8,128)S(1)} %get-tuple-element.105.local_grad, bf16[64,256]{1,0:T(8,128)(2,1)S(1)} %get-tuple-element.106.middle, bf16[96,256]{1,0:T(8,128)(2,1)S(1)} %collective-permute-done.7.to_high, ...), custom_call_target="tpu_custom_call" | custom-call | flops 50331648 | bytes 721920 | tf_op jit(solution)/shard_map/pallas_call | solution.py:512
  52.4 4.6 %all-to-all-done.1.own = bf16[4,224,256]{2,1,0:T(8,128)(2,1)S(1)} async-done(((bf16[4,224,256]{2,1,0:T(8,128)(2,1)}), bf16[4,224,256]{2,1,0:T(8,128)(2,1)S(1)}, u32[]{:S(2)}, u32[]{:S(2)}) %all-to-all-start.1) | async-done | bytes 458784 | tf_op jit(solution)/shard_map/all_to_all | solution.py:756
  57.0 0.0 collective-permute-start.9
  57.0 0.5 convert_reduce_fusion
  57.6 1.3 %collective-permute-done.9.other = bf16[4,224,256]{2,1,0:T(8,128)(2,1)S(1)} collective-permute-done((bf16[4,224,256]{2,1,0:T(8,128)(2,1)S(1)}, bf16[4,224,256]{2,1,0:T(8,128)(2,1)S(1)}, u32[]{:S(2)}, u32[]{:S(2)}) %collective-permute-start.9) | collective-permute-done | bytes 458784 | tf_op jit(solution)/shard_map/ppermute | solution.py:35
  58.8 1.1 %shard_map.207 = (bf16[768,256]{1,0:T(8,128)(2,1)}, bf16[256,256]{1,0:T(8,128)(2,1)}, bf16[512,256]{1,0:T(8,128)(2,1)}, bf16[256,256]{1,0:T(8,128)(2,1)}) custom-call(bf16[4,224,256]{2,1,0:T(8,128)(2,1)S(1)} %all-to-all-done.1.own, bf16[4,224,256]{2,1,0:T(8,128)(2,1)S(1)} %collective-permute-done.9.other), custom_call_target="tpu_custom_call" | custom-call | bytes 1835008 | tf_op jit(solution)/shard_map/pallas_call | solution.py:512
  (4 shorter events, 0.0 us)
Async XLA Ops:
  1.9 7.6 %collective-permute-start = (bf16[96,256]{1,0:T(8,128)(2,1)S(1)}, bf16[96,256]{1,0:T(8,128)(2,1)S(1)}, u32[]{:S(2)}, u32[]{:S(2)}) collective-permute-start(bf16[96,256]{1,0:T(8,128)(2,1)S(1)} %get-tuple-element.68), channel_id=1, source_target_pairs={{0,4},{4,8},{8,12},{12,0},{1,5},{5,9},{9,13},{13,1},{2,6},{6,10},{... | collective-permute-start | bytes 147464 | tf_op jit(solution)/shard_map/ppermute | solution.py:25
  5.0 4.6 %collective-permute-start.1 = (bf16[96,256]{1,0:T(8,128)(2,1)S(1)}, bf16[96,256]{1,0:T(8,128)(2,1)S(1)}, u32[]{:S(2)}, u32[]{:S(2)}) collective-permute-start(bf16[96,256]{1,0:T(8,128)(2,1)S(1)} %get-tuple-element.69), channel_id=1, source_target_pairs={{0,12},{4,0},{8,4},{12,8},{1,13},{5,1},{9,5},{13,9},{2,14},{6,2},{... | collective-permute-start | bytes 147464 | tf_op jit(solution)/shard_map/ppermute | solution.py:25
  9.7 3.6 %collective-permute-start.2 = (bf16[96,256]{1,0:T(8,128)(2,1)S(1)}, bf16[96,256]{1,0:T(8,128)(2,1)S(1)}, u32[]{:S(2)}, u32[]{:S(2)}) collective-permute-start(bf16[96,256]{1,0:T(8,128)(2,1)S(1)} %pad_maximum_fusion), channel_id=1, source_target_pairs={{0,1},{1,2},{2,3},{3,0},{4,5},{5,6},{6,7},{7,4},{8,9},{9,10},{10,1... | collective-permute-start | bytes 147464 | tf_op jit(solution)/shard_map/ppermute | solution.py:25
  9.7 3.6 %collective-permute-start.3 = (bf16[96,256]{1,0:T(8,128)(2,1)S(1)}, bf16[96,256]{1,0:T(8,128)(2,1)S(1)}, u32[]{:S(2)}, u32[]{:S(2)}) collective-permute-start(bf16[96,256]{1,0:T(8,128)(2,1)S(1)} %pad_maximum_fusion.1), channel_id=1, source_target_pairs={{0,3},{1,0},{2,1},{3,2},{4,7},{5,4},{6,5},{7,6},{8,11},{9,8},{10,9... | collective-permute-start | bytes 147464 | tf_op jit(solution)/shard_map/ppermute | solution.py:25
  19.0 0.7 %copy-start = (bf16[384,256]{1,0:T(8,128)(2,1)}, bf16[384,256]{1,0:T(8,128)(2,1)S(1)}, u32[]{:S(2)}) copy-start(bf16[384,256]{1,0:T(8,128)(2,1)S(1)} %get-tuple-element.104.node_pre_grad) | copy-start | bytes 589828
  19.7 3.1 %collective-permute-start.4 = (bf16[1008,256]{1,0:T(8,128)(2,1)S(1)}, bf16[1008,256]{1,0:T(8,128)(2,1)S(1)}, u32[]{:S(2)}, u32[]{:S(2)}) collective-permute-start(bf16[1008,256]{1,0:T(8,128)(2,1)S(1)} %get-tuple-element.90), channel_id=1, source_target_pairs={{0,1},{1,0},{2,3},{3,2},{4,5},{5,4},{6,7},{7,6},{8,9},{9,8},{10,11... | collective-permute-start | bytes 1548296 | tf_op jit(solution)/shard_map/ppermute | solution.py:35
  21.3 5.9 %collective-permute-start.5 = (bf16[96,256]{1,0:T(8,128)(2,1)S(1)}, bf16[96,256]{1,0:T(8,128)(2,1)}, u32[]{:S(2)}, u32[]{:S(2)}) collective-permute-start(bf16[96,256]{1,0:T(8,128)(2,1)S(1)} %get-tuple-element.91), channel_id=1, source_target_pairs={{0,3},{1,2},{2,1},{3,0},{4,7},{5,6},{6,5},{7,4},{8,11},{9,10},{10,... | collective-permute-start | bytes 147464 | tf_op jit(solution)/shard_map/ppermute | solution.py:31
  23.7 11.9 %all-to-all-start = ((bf16[4,240,256]{2,1,0:T(8,128)(2,1)}), bf16[4,240,256]{2,1,0:T(8,128)(2,1)S(1)}, u32[]{:S(2)}, u32[]{:S(2)}) async-start(bf16[4,240,256]{2,1,0:T(8,128)(2,1)} %shard_map.201), calls=%async_computation | async-start | bytes 983040 | tf_op jit(solution)/shard_map/all_to_all | solution.py:739
  28.0 0.6 %copy-start.2 = (bf16[96,256]{1,0:T(8,128)(2,1)}, bf16[96,256]{1,0:T(8,128)(2,1)S(1)}, u32[]{:S(2)}) copy-start(bf16[96,256]{1,0:T(8,128)(2,1)S(1)} %get-tuple-element.96) | copy-start | bytes 147460
  28.6 21.4 %copy-start.1 = (bf16[384,256]{1,0:T(8,128)(2,1)S(1)}, bf16[384,256]{1,0:T(8,128)(2,1)}, u32[]{:S(2)}) copy-start(bf16[384,256]{1,0:T(8,128)(2,1)} %copy-done) | copy-start | bytes 589828
  35.7 10.0 %collective-permute-start.6 = (bf16[240,256]{1,0:T(8,128)(2,1)S(1)}, bf16[240,256]{1,0:T(8,128)(2,1)S(1)}, u32[]{:S(2)}, u32[]{:S(2)}) collective-permute-start(bf16[240,256]{1,0:T(8,128)(2,1)S(1)} %shard_map.203.own), channel_id=1, source_target_pairs={{0,8},{8,0},{1,9},{9,1},{2,10},{10,2},{3,11},{11,3},{4,12},{12,4},... | collective-permute-start | bytes 368648 | tf_op jit(solution)/shard_map/ppermute | solution.py:556
  38.0 6.4 %collective-permute-start.7 = (bf16[96,256]{1,0:T(8,128)(2,1)}, bf16[96,256]{1,0:T(8,128)(2,1)S(1)}, u32[]{:S(2)}, u32[]{:S(2)}) collective-permute-start(bf16[96,256]{1,0:T(8,128)(2,1)} %copy-done.2), channel_id=1, source_target_pairs={{0,4},{4,8},{8,12},{12,0},{1,5},{5,9},{9,13},{13,1},{2,6},{6,10},{... | collective-permute-start | bytes 147464 | tf_op jit(solution)/shard_map/ppermute | solution.py:25
  39.1 5.2 %collective-permute-start.8 = (bf16[96,256]{1,0:T(8,128)(2,1)S(1)}, bf16[96,256]{1,0:T(8,128)(2,1)S(1)}, u32[]{:S(2)}, u32[]{:S(2)}) collective-permute-start(bf16[96,256]{1,0:T(8,128)(2,1)S(1)} %get-tuple-element.97), channel_id=1, source_target_pairs={{0,12},{4,0},{8,4},{12,8},{1,13},{5,1},{9,5},{13,9},{2,14},{6,2},{... | collective-permute-start | bytes 147464 | tf_op jit(solution)/shard_map/ppermute | solution.py:25
  46.5 10.5 %all-to-all-start.1 = ((bf16[4,224,256]{2,1,0:T(8,128)(2,1)}), bf16[4,224,256]{2,1,0:T(8,128)(2,1)S(1)}, u32[]{:S(2)}, u32[]{:S(2)}) async-start(bf16[4,224,256]{2,1,0:T(8,128)(2,1)} %get-tuple-element.99), calls=%async_computation.1 | async-start | bytes 917504 | tf_op jit(solution)/shard_map/all_to_all | solution.py:756
  57.0 1.8 %collective-permute-start.9 = (bf16[4,224,256]{2,1,0:T(8,128)(2,1)S(1)}, bf16[4,224,256]{2,1,0:T(8,128)(2,1)S(1)}, u32[]{:S(2)}, u32[]{:S(2)}) collective-permute-start(bf16[4,224,256]{2,1,0:T(8,128)(2,1)S(1)} %all-to-all-done.1.own), channel_id=1, source_target_pairs={{0,1},{1,0},{2,3},{3,2},{4,5},{5,4},{6,7},{7,6},{8,9},{9,8},{10,11... | collective-permute-start | bytes 1376264 | tf_op jit(solution)/shard_map/ppermute | solution.py:35

commit v12 on v10

--- a/solution.py
+++ b/solution.py
@@ -29,6 +29,25 @@
     size = lax.axis_size(PY)
     pairs = [(i, (i + 1 if i % 2 else i - 1) % size) for i in range(size)]
     return lax.ppermute(array, PY, pairs)
+
+
+def square_members():
+    return lax.axis_size(SQUARE)
+
+
+def place_in_square():
+    near, side = SQUARE
+    return lax.axis_index(near) * lax.axis_size(side) + lax.axis_index(side)
+
+
+def in_square(array, offset):
+    return lax.ppermute(array, SQUARE, [(i, i ^ offset) for i in range(square_members())])
+
+
+def tree_sum(terms):
+    while len(terms) > 1:
+        terms = [terms[i] + terms[i + 1] for i in range(0, len(terms), 2)]
+    return terms[0]
 
 
 def across_cores(array):
@@ -322,27 +341,22 @@
     gains_out[...] = gains
 
 
-def pair_kernel(parts, keep, gains, other, blocks_out, total, staged, sems):
+def pair_kernel(parts, keep, gains, other, *outs):
     rows = keep.shape[0]
-    chips = blocks_out.shape[0]
     packed = gains.shape[0]
+    members = len(outs)
     both = gains[...].astype(F32) + other[rows : rows + packed].astype(F32)
     summed = pack_gains(both[0:1] + both[1:2], both[2:3] + both[3:4])
-    total[...] = (keep[...] + other[:rows].astype(F32)).astype(BF16)
-    copies = []
-    for chip in range(chips):
-        staged[chip, :packed, :] = summed
+    me = place_in_square()
+    for offset, out in enumerate(outs):
+        owner = me ^ offset
+        out[:packed] = summed
         first, at = 0, packed
         for part in parts:
-            step = part // chips
-            staged[chip, at : at + step, :] = total[first + chip * step : first + (chip + 1) * step]
+            step = part // members
+            source = pl.ds(pl.multiple_of(first + owner * step, 16), step)
+            out[at : at + step] = (keep[source, :] + other[source, :].astype(F32)).astype(BF16)
             first, at = first + part, at + step
-        copies.append(
-            pltpu.make_async_copy(staged.at[chip], blocks_out.at[chip], sems.at[chip])
-        )
-        copies[-1].start()
-    for copy in copies:
-        copy.wait()
 
 
 def add_packed(values):
@@ -351,10 +365,9 @@
     return pack_gains(gains[0:1] + gains[1:2], gains[2:3] + gains[3:4])
 
 
-def sum_kernel(received, sums_out):
-    sums = received[0].astype(F32)
-    for chip in range(1, received.shape[0]):
-        sums = sums + received[chip].astype(F32)
+def sum_kernel(*refs):
+    sums_out = refs[-1]
+    sums = tree_sum([block[...].astype(F32) for block in refs[:-1]])
     sums_out[...] = sums.astype(BF16)
     sums_out[:16] = add_packed(sums)
 
@@ -365,60 +378,39 @@
     sums_out[:16] = add_packed(sums)
 
 
-def spread_kernel(own, other, gains_out, spread_out, mine, sems):
+def whole_kernel(own, other, gains_out, mine):
     packed = gains_out.shape[0]
     sums = own[...].astype(F32) + other[...].astype(F32)
+    gains_out[...] = sums[:packed]
     mine[...] = sums[packed:].astype(BF16)
-    copies = [
-        pltpu.make_async_copy(mine, spread_out.at[chip], sems.at[chip])
-        for chip in range(spread_out.shape[0])
-    ]
+
+
+def place_kernel(parts, *refs):
+    count = 2 * len(parts)
+    sems, wholes = refs[-1], refs[-1 - len(parts) : -1]
+    outs = refs[-1 - len(parts) - count : -1 - len(parts)]
+    blocks = refs[: -1 - len(parts) - count]
+    members = len(blocks) // 2
+    core = lax.axis_index(CORE)
+    me = place_in_square()
+    for position, block in enumerate(blocks):
+        half = core if position < members else 1 - core
+        owner = me ^ (position % members)
+        at = 0
+        for part, whole in zip(parts, wholes):
+            step = part // members
+            row = pl.multiple_of(half * part + owner * step, 16)
+            whole[pl.ds(row, step), :] = block[at : at + step]
+            at += step
+    copies = []
+    for i, whole in enumerate(wholes):
+        cut = outs[2 * i].shape[0]
+        copies.append(pltpu.make_async_copy(whole.at[:cut], outs[2 * i], sems.at[2 * i]))
+        copies.append(pltpu.make_async_copy(whole.at[cut:], outs[2 * i + 1], sems.at[2 * i + 1]))
     for copy in copies:
         copy.start()
-    gains_out[...] = sums[:packed]
     for copy in copies:
         copy.wait()
-
-
-def place_kernel(parts, own, other, *refs):
-    outs, sems = refs[:-1], refs[-1]
-    chips = own.shape[0]
-    core = lax.axis_index(CORE)
-
-    def place(halves):
-        copies = []
-
-        def put(source, target):
-            copies.append(pltpu.make_async_copy(source, target, sems.at[len(copies)]))
-            copies[-1].start()
-
-        for half, blocks in enumerate(halves):
-            for chip in range(chips):
-                at = 0
-                for i, part in enumerate(parts):
-                    step = part // chips
-                    row = half * part + chip * step
-                    cut = outs[2 * i].shape[0]
-                    split = min(max(cut - row, 0), step)
-                    if split > 0:
-                        put(blocks.at[chip, at : at + split], outs[2 * i].at[row : row + split])
-                    if split < step:
-                        rest = row + split - cut
-                        put(
-                            blocks.at[chip, at + split : at + step],
-                            outs[2 * i + 1].at[rest : rest + step - split],
-                        )
-                    at += step
-        for copy in copies:
-            copy.wait()
-
-    @pl.when(core == 0)
-    def _():
-        place([own, other])
-
-    @pl.when(core == 1)
-    def _():
-        place([other, own])
 
 
 def finish_kernel(
@@ -516,28 +508,25 @@
     return jax.ShapeDtypeStruct((rows, columns), dtype)
 
 
-def placed(parts, own, other, width):
-    chips = own.shape[0]
-    outs = [
-        shaped(3 * width, width, BF16),
-        shaped(width, width, BF16),
-        shaped(2 * width, width, BF16),
-        shaped(width, width, BF16),
-    ]
+def placed(parts, blocks, width):
     return call(
         functools.partial(place_kernel, parts),
-        outs,
+        [
+            shaped(3 * width, width, BF16),
+            shaped(width, width, BF16),
+            shaped(2 * width, width, BF16),
+            shaped(width, width, BF16),
+        ],
         0,
-        own,
-        other,
+        *blocks,
         out_space=HBM,
-        scratch=[pltpu.SemaphoreType.DMA((2 * len(parts) * chips + len(parts),))],
-    )
-
-
-def spread_of(received, packed, *beside):
-    chips, rows, width = received.shape
-    (sums,) = call(sum_kernel, [shaped(rows, width, BF16)], 0, received)
+        scratch=[pltpu.VMEM((2 * part, width), BF16) for part in parts]
+        + [pltpu.SemaphoreType.DMA((2 * len(parts),))],
+    )
+
+
+def joined(sums, packed, *beside):
+    rows, width = sums.shape
     size = lax.axis_size(FAR)
     distance = 1
     while True:
@@ -546,39 +535,15 @@
         if distance == size:
             break
         (sums,) = call(join_kernel, [like(sums)], 0, sums, other)
-    mine = rows - packed
     other, *beside = lax.optimization_barrier((other, *beside))
-    gains, spread = call(
-        spread_kernel,
-        [shaped(packed, width, F32), jax.ShapeDtypeStruct((chips, mine, width), BF16)],
+    gains, mine = call(
+        whole_kernel,
+        [shaped(packed, width, F32), shaped(rows - packed, width, BF16)],
         0,
         sums,
         other,
-        out_space=[VMEM, HBM],
-        scratch=[pltpu.VMEM((mine, width), BF16), pltpu.SemaphoreType.DMA((chips,))],
-    )
-    return gains, spread, *beside
-
-
-def blocks_of(parts, keep, gains, other):
-    chips = lax.axis_size(SQUARE)
-    rows, width = keep.shape
-    shape = (chips, gains.shape[0] + rows // chips, width)
-    (blocks,) = call(
-        functools.partial(pair_kernel, parts),
-        [jax.ShapeDtypeStruct(shape, BF16)],
-        0,
-        keep,
-        gains,
-        other,
-        out_space=HBM,
-        scratch=[
-            pltpu.VMEM((rows, width), BF16),
-            pltpu.VMEM(shape, BF16),
-            pltpu.SemaphoreType.DMA((chips,)),
-        ],
-    )
-    return blocks
+    )
+    return gains, mine, *beside
 
 
 def on_device(
@@ -728,8 +693,16 @@
         ],
     )
     other = across_cores(away)
-    blocks = blocks_of(parts, keep, gains, other)
-    received = lax.all_to_all(blocks, SQUARE, 0, 0)
+    members = square_members()
+    own, *blocks = call(
+        functools.partial(pair_kernel, parts),
+        [shaped(16 + halves // members, width, BF16)] * members,
+        0,
+        keep,
+        gains,
+        other,
+    )
+    received = [in_square(block, offset) for offset, block in enumerate(blocks, 1)]
     high, low, middle = call(
         turn_kernel,
         [
@@ -737,16 +710,18 @@
             shaped(3 * slots, width, BF16),
             shaped(2 * slots, width, BF16),
         ],
-        0,
+        10**10,
         other,
         across_chips(across),
         rest,
     )
-    received, high, low = lax.optimization_barrier((received, high, low))
-    gains, spread, to_high, to_low = spread_of(
-        received, gains.shape[0], passed_along(high, PX, 1), passed_along(low, PX, -1)
-    )
-    own = lax.all_to_all(spread, SQUARE, 0, 0)
+    *received, high, low = lax.optimization_barrier((*received, high, low))
+    (sums,) = call(sum_kernel, [like(own)], 0, own, *received)
+    gains, mine, to_high, to_low = joined(
+        sums, gains.shape[0], passed_along(high, PX, 1), passed_along(low, PX, -1)
+    )
+    blocks = [mine] + [in_square(mine, offset) for offset in range(1, members)]
+    blocks += [across_cores(block) for block in blocks]
     edges_grad, local_grad = call(
         finish_kernel,
         [shaped(edge_rows, width, BF16), shaped(count, width, F32)],
@@ -768,9 +743,9 @@
         to_high,
         to_low,
     )
-    own, nodes_grad, edges_grad = lax.optimization_barrier((own, nodes_grad, edges_grad))
+    *blocks, nodes_grad, edges_grad = lax.optimization_barrier((*blocks, nodes_grad, edges_grad))
     w_edge_in_grad, w_edge_out_grad, w_node_in_grad, w_node_out_grad = placed(
-        parts, own, across_cores(own), width
+        parts, blocks, width
     )
     return (
         nodes_grad,

time: 60.5 us -> 52.4 us (0.87)
  waiting for transfers between devices: 19.3 us -> 13 us
  Pallas kernels: 15.8 us -> 14.1 us
    ppermute x1 -> x7, starting transfers between devices: 2.07 us -> 9.45 us  [the longest x6 7.12 us: in_square(): lax.ppermute(array, SQUARE, [(i, i ^ offset) for i in range(square_member...]
    ppermute x1, waiting for transfers between devices: 7.21 us -> 0.01 us  [across_chips(): return lax.ppermute(array, PY, pairs)]
    all_to_all x2 -> x0, starting transfers between devices: 6.96 us -> none  [the longest x1 3.48 us: on_device(): received = lax.all_to_all(blocks, SQUARE, 0, 0)]
    ppermute x1 -> x7, waiting for transfers between devices: 1.45 us -> 8.34 us  [the longest x6 7.99 us: in_square(): lax.ppermute(array, SQUARE, [(i, i ^ offset) for i in range(square_member...]
    all_to_all x2 -> x0, waiting for transfers between devices: 4.29 us -> none  [the longest x1 4.27 us: on_device(): own = lax.all_to_all(spread, SQUARE, 0, 0)]
    pallas_call x11, Pallas kernels: 15.8 us -> 14.1 us  [call(): pl.pallas_call(body, out_shape=outs, in_specs=[pl.BlockSpec(memory_space=...]
    ppermute x1, starting transfers between devices: 1.68 us -> 0.14 us  [across_chips(): return lax.ppermute(array, PY, pairs)]
    ppermute x2 -> x5, waiting for transfers between devices: 2.8 us -> 1.39 us  [across_cores(): return lax.ppermute(array, CORE, [(0, 1), (1, 0)])]
  transfers between devices with their start and end apart: 12 -> 19, of which waited for: 7 -> 10; matrix products, arithmetic and copies ran while one was open for 1% -> 1% of each run, Pallas kernels for 10% -> 12%
where the time goes in v12:
time: 52.4 us; the launch traced here: 51.6 us
  starting transfers between devices  22.5 us (43%)
  Pallas kernels  14.1 us (27%)
  waiting for transfers between devices  13 us (25%)
  between operations  1.4 us (3%)
  other arithmetic  0.55 us (1%)
    pallas_call x11, Pallas kernels, call(): pl.pallas_call(body, out_shape=outs, in_specs=[pl.BlockSpec(memory_space=...  14.1 us
    ppermute x6, starting transfers between devices, passed_along(): lax.ppermute(array, axis, [(i, (i + by) % size) for i in range(size)])  10.8 us
    ppermute x6, waiting for transfers between devices, in_square(): lax.ppermute(array, SQUARE, [(i, i ^ offset) for i in range(square_member...  7.99 us
    ppermute x6, starting transfers between devices, in_square(): lax.ppermute(array, SQUARE, [(i, i ^ offset) for i in range(square_member...  7.12 us
    ppermute x6, waiting for transfers between devices, passed_along(): lax.ppermute(array, axis, [(i, (i + by) % size) for i in range(size)])  3.26 us
    ppermute x1, starting transfers between devices, joined(): other = lax.ppermute(sums, FAR, [(i, i ^ distance) for i in range(size)])  2.33 us
    ppermute x5, starting transfers between devices, across_cores(): return lax.ppermute(array, CORE, [(0, 1), (1, 0)])  2.18 us
    ppermute x5, waiting for transfers between devices, across_cores(): return lax.ppermute(array, CORE, [(0, 1), (1, 0)])  1.39 us
  transfers between devices with their start and end apart: 19, of which 10 were waited for; matrix products, arithmetic and copies ran while one was open for 1% of the time, Pallas kernels for 12%

profile of v12, /device:TPU:0, one launch (start us, length us, event | category | flops | bytes accessed | tf_op | source)
XLA Modules:
  0.0 51.6 jit_solution(629337490104274858)
XLA Ops:
  0.6 1.3 %shard_map.197 = (bf16[96,256]{1,0:T(8,128)(2,1)S(1)}, bf16[64,256]{1,0:T(8,128)(2,1)S(1)}, bf16[96,256]{1,0:T(8,128)(2,1)S(1)}, bf16[384,256]{1,0:T(8,128)(2,1)S(1)}, s32[8,32]{1,0:T(8,128)S(1)}) custom-call(bf16[384,256]{1,0:T(8,128)(2,1)} %nodes_hbm.1, s32[8,32]{1,0:T(8,128)} %list_hbm.1), custom_call_target="tpu_custom_call" | custom-call | flops 50331648 | bytes 526336 | tf_op jit(solution)/shard_map/pallas_call | solution.py:492
  1.9 3.1 %collective-permute-start = (bf16[96,256]{1,0:T(8,128)(2,1)S(1)}, bf16[96,256]{1,0:T(8,128)(2,1)S(1)}, u32[]{:S(2)}, u32[]{:S(2)}) collective-permute-start(bf16[96,256]{1,0:T(8,128)(2,1)S(1)} %get-tuple-element.80), channel_id=1, source_target_pairs={{0,4},{4,8},{8,12},{12,0},{1,5},{5,9},{9,13},{13,1},{2,6},{6,10},{... | collective-permute-start | bytes 147464 | tf_op jit(solution)/shard_map/ppermute | solution.py:25
  5.0 2.1 %collective-permute-start.1 = (bf16[96,256]{1,0:T(8,128)(2,1)S(1)}, bf16[96,256]{1,0:T(8,128)(2,1)S(1)}, u32[]{:S(2)}, u32[]{:S(2)}) collective-permute-start(bf16[96,256]{1,0:T(8,128)(2,1)S(1)} %get-tuple-element.81), channel_id=1, source_target_pairs={{0,12},{4,0},{8,4},{12,8},{1,13},{5,1},{9,5},{13,9},{2,14},{6,2},{... | collective-permute-start | bytes 147464 | tf_op jit(solution)/shard_map/ppermute | solution.py:25
  7.8 1.7 %shard_map.198 = (bf16[1152,768]{1,0:T(8,128)(2,1)S(1)}, bf16[1152,256]{1,0:T(8,128)(2,1)S(1)}, s32[9,128]{1,0:T(8,128)S(1)}, s32[9,128]{1,0:T(8,128)S(1)}, bf16...) custom-call(s32[9,128]{1,0:T(8,128)} %refs_0_.1, ...), custom_call_target="tpu_custom_call" | custom-call | bytes 6967296 | tf_op jit(solution)/shard_map/pallas_call | solution.py:492
  9.5 0.0 collective-permute-done.from_low
  9.5 0.1 collective-permute-done.1.from_high
  9.7 0.1 collective-permute-start.2
  9.7 1.7 %collective-permute-start.3 = (bf16[96,256]{1,0:T(8,128)(2,1)S(1)}, bf16[96,256]{1,0:T(8,128)(2,1)S(1)}, u32[]{:S(2)}, u32[]{:S(2)}) collective-permute-start(bf16[96,256]{1,0:T(8,128)(2,1)S(1)} %pad_maximum_fusion.1), channel_id=1, source_target_pairs={{0,3},{1,0},{2,1},{3,2},{4,7},{5,4},{6,5},{7,6},{8,11},{9,8},{10,9... | collective-permute-start | bytes 147464 | tf_op jit(solution)/shard_map/ppermute | solution.py:25
  11.5 1.8 %shard_map.199 = (f32[1152,256]{1,0:T(8,128)S(1)}, bf16[640,1152]{1,0:T(8,128)(2,1)S(1)}, bf16[384,1152]{1,0:T(8,128)(2,1)S(1)}) custom-call(bf16[384,256]{1,0:T(8,128)(2,1)S(1)} %get-tuple-element.74.nodes, bf16[1152,256]{1,0:T(8,128)(2,1)S(1)} %get-tuple-element.76.edges, s32[9,128]{1,0:T(8,128)S(1)} %get-tuple-element.78.senders, ...), custom_call_target="tpu_custom_call" | custom-call | flops 704643072 | bytes 6497280 | tf_op jit(solution)/shard_map/pallas_call | solution.py:492
  13.3 0.0 collective-permute-done.2.upward
  13.3 0.0 collective-permute-done.3.downward
  13.3 5.6 %shard_map.200 = (bf16[1152,256]{1,0:T(8,128)(2,1)S(1)}, bf16[384,256]{1,0:T(8,128)(2,1)S(1)}, bf16[384,256]{1,0:T(8,128)(2,1)S(1)}, f32[384,256]{1,0:T(8,128)S(...) custom-call(s32[1]{0:T(128)S(6)} %copy.22.count_ref, ...), custom_call_target="tpu_custom_call" | custom-call | flops 2583691264 | bytes 11486212 | tf_op jit(solution)/shard_map/pallas_call | solution.py:492
  18.9 1.7 %collective-permute-start.4 = (bf16[1008,256]{1,0:T(8,128)(2,1)S(1)}, bf16[1008,256]{1,0:T(8,128)(2,1)S(1)}, u32[]{:S(2)}, u32[]{:S(2)}) collective-permute-start(bf16[1008,256]{1,0:T(8,128)(2,1)S(1)} %get-tuple-element.99), channel_id=1, source_target_pairs={{0,1},{1,0},{2,3},{3,2},{4,5},{5,4},{6,7},{7,6},{8,9},{9,8},{10,11... | collective-permute-start | bytes 1548296 | tf_op jit(solution)/shard_map/ppermute | solution.py:54
  20.6 0.1 collective-permute-start.8
  20.7 1.4 %collective-permute-done.4.other = bf16[1008,256]{1,0:T(8,128)(2,1)S(1)} collective-permute-done((bf16[1008,256]{1,0:T(8,128)(2,1)S(1)}, bf16[1008,256]{1,0:T(8,128)(2,1)S(1)}, u32[]{:S(2)}, u32[]{:S(2)}) %collective-permute-start.4) | collective-permute-done | bytes 516128 | tf_op jit(solution)/shard_map/ppermute | solution.py:54
  22.1 0.1 shard_map.201
  22.2 0.5 %collective-permute-start.5 = (bf16[240,256]{1,0:T(8,128)(2,1)S(1)}, bf16[240,256]{1,0:T(8,128)(2,1)S(1)}, u32[]{:S(2)}, u32[]{:S(2)}) collective-permute-start(bf16[240,256]{1,0:T(8,128)(2,1)S(1)} %get-tuple-element.101), channel_id=1, source_target_pairs={{0,2},{2,0},{4,6},{6,4},{1,3},{3,1},{5,7},{7,5},{8,10},{10,8},{12,... | collective-permute-start | bytes 368648 | tf_op jit(solution)/shard_map/ppermute | solution.py:44
  22.8 1.1 %collective-permute-start.6 = (bf16[240,256]{1,0:T(8,128)(2,1)S(1)}, bf16[240,256]{1,0:T(8,128)(2,1)S(1)}, u32[]{:S(2)}, u32[]{:S(2)}) collective-permute-start(bf16[240,256]{1,0:T(8,128)(2,1)S(1)} %get-tuple-element.102), channel_id=1, source_target_pairs={{0,4},{2,6},{4,0},{6,2},{1,5},{3,7},{5,1},{7,3},{8,12},{10,14},{12... | collective-permute-start | bytes 368648 | tf_op jit(solution)/shard_map/ppermute | solution.py:44
  23.8 2.0 %collective-permute-start.7 = (bf16[240,256]{1,0:T(8,128)(2,1)S(1)}, bf16[240,256]{1,0:T(8,128)(2,1)S(1)}, u32[]{:S(2)}, u32[]{:S(2)}) collective-permute-start(bf16[240,256]{1,0:T(8,128)(2,1)S(1)} %get-tuple-element.103), channel_id=1, source_target_pairs={{0,6},{2,4},{4,2},{6,0},{1,7},{3,5},{5,3},{7,1},{8,14},{10,12},{12... | collective-permute-start | bytes 368648 | tf_op jit(solution)/shard_map/ppermute | solution.py:44
  25.8 0.0 collective-permute-done.8.across
  25.8 2.1 %collective-permute-done.5.refs_1_ = bf16[240,256]{1,0:T(8,128)(2,1)S(1)} collective-permute-done((bf16[240,256]{1,0:T(8,128)(2,1)S(1)}, bf16[240,256]{1,0:T(8,128)(2,1)S(1)}, u32[]{:S(2)}, u32[]{:S(2)}) %collective-permute-start.5) | collective-permute-done | bytes 122912 | tf_op jit(solution)/shard_map/ppermute | solution.py:44
  27.9 1.1 %collective-permute-done.6.refs_2_ = bf16[240,256]{1,0:T(8,128)(2,1)S(1)} collective-permute-done((bf16[240,256]{1,0:T(8,128)(2,1)S(1)}, bf16[240,256]{1,0:T(8,128)(2,1)S(1)}, u32[]{:S(2)}, u32[]{:S(2)}) %collective-permute-start.6) | collective-permute-done | bytes 122912 | tf_op jit(solution)/shard_map/ppermute | solution.py:44
  28.9 2.8 %collective-permute-done.7.refs_3_ = bf16[240,256]{1,0:T(8,128)(2,1)S(1)} collective-permute-done((bf16[240,256]{1,0:T(8,128)(2,1)S(1)}, bf16[240,256]{1,0:T(8,128)(2,1)S(1)}, u32[]{:S(2)}, u32[]{:S(2)}) %collective-permute-start.7) | collective-permute-done | bytes 122912 | tf_op jit(solution)/shard_map/ppermute | solution.py:44
  31.7 0.1 shard_map.203.own
  31.8 2.3 %collective-permute-start.9 = (bf16[240,256]{1,0:T(8,128)(2,1)S(1)}, bf16[240,256]{1,0:T(8,128)(2,1)S(1)}, u32[]{:S(2)}, u32[]{:S(2)}) collective-permute-start(bf16[240,256]{1,0:T(8,128)(2,1)S(1)} %shard_map.203.own), channel_id=1, source_target_pairs={{0,8},{8,0},{1,9},{9,1},{2,10},{10,2},{3,11},{11,3},{4,12},{12,4},... | collective-permute-start | bytes 368648 | tf_op jit(solution)/shard_map/ppermute | solution.py:533
  34.1 1.7 %collective-permute-start.10 = (bf16[96,256]{1,0:T(8,128)(2,1)S(1)}, bf16[96,256]{1,0:T(8,128)(2,1)S(1)}, u32[]{:S(2)}, u32[]{:S(2)}) collective-permute-start(bf16[96,256]{1,0:T(8,128)(2,1)S(1)} %get-tuple-element.111), channel_id=1, source_target_pairs={{0,4},{4,8},{8,12},{12,0},{1,5},{5,9},{9,13},{13,1},{2,6},{6,10},{... | collective-permute-start | bytes 147464 | tf_op jit(solution)/shard_map/ppermute | solution.py:25
  35.8 2.1 %collective-permute-start.11 = (bf16[96,256]{1,0:T(8,128)(2,1)S(1)}, bf16[96,256]{1,0:T(8,128)(2,1)S(1)}, u32[]{:S(2)}, u32[]{:S(2)}) collective-permute-start(bf16[96,256]{1,0:T(8,128)(2,1)S(1)} %get-tuple-element.112), channel_id=1, source_target_pairs={{0,12},{4,0},{8,4},{12,8},{1,13},{5,1},{9,5},{13,9},{2,14},{6,2},{... | collective-permute-start | bytes 147464 | tf_op jit(solution)/shard_map/ppermute | solution.py:25
  37.9 2.2 %collective-permute-done.10.to_high = bf16[96,256]{1,0:T(8,128)(2,1)S(1)} collective-permute-done((bf16[96,256]{1,0:T(8,128)(2,1)S(1)}, bf16[96,256]{1,0:T(8,128)(2,1)S(1)}, u32[]{:S(2)}, u32[]{:S(2)}) %collective-permute-start.10) | collective-permute-done | bytes 49184 | tf_op jit(solution)/shard_map/ppermute | solution.py:25
  40.1 0.9 %collective-permute-done.11.to_low = bf16[96,256]{1,0:T(8,128)(2,1)S(1)} collective-permute-done((bf16[96,256]{1,0:T(8,128)(2,1)S(1)}, bf16[96,256]{1,0:T(8,128)(2,1)S(1)}, u32[]{:S(2)}, u32[]{:S(2)}) %collective-permute-start.11) | collective-permute-done | bytes 49184 | tf_op jit(solution)/shard_map/ppermute | solution.py:25
  41.1 0.4 collective-permute-done.9.other
  41.5 1.0 %collective-permute-start.14 = (bf16[224,256]{1,0:T(8,128)(2,1)S(1)}, bf16[224,256]{1,0:T(8,128)(2,1)S(1)}, u32[]{:S(2)}, u32[]{:S(2)}) collective-permute-start(bf16[224,256]{1,0:T(8,128)(2,1)S(1)} %get-tuple-element.127.refs_0_), channel_id=1, source_target_pairs={{0,6},{2,4},{4,2},{6,0},{1,7},{3,5},{5,3},{7,1},{8,14},{10,12},{12... | collective-permute-start | bytes 344072 | tf_op jit(solution)/shard_map/ppermute | solution.py:44
  42.5 0.9 %collective-permute-start.13 = (bf16[224,256]{1,0:T(8,128)(2,1)S(1)}, bf16[224,256]{1,0:T(8,128)(2,1)S(1)}, u32[]{:S(2)}, u32[]{:S(2)}) collective-permute-start(bf16[224,256]{1,0:T(8,128)(2,1)S(1)} %get-tuple-element.127.refs_0_), channel_id=1, source_target_pairs={{0,4},{2,6},{4,0},{6,2},{1,5},{3,7},{5,1},{7,3},{8,12},{10,14},{12... | collective-permute-start | bytes 344072 | tf_op jit(solution)/shard_map/ppermute | solution.py:44
  43.4 1.6 %collective-permute-start.12 = (bf16[224,256]{1,0:T(8,128)(2,1)S(1)}, bf16[224,256]{1,0:T(8,128)(2,1)S(1)}, u32[]{:S(2)}, u32[]{:S(2)}) collective-permute-start(bf16[224,256]{1,0:T(8,128)(2,1)S(1)} %get-tuple-element.127.refs_0_), channel_id=1, source_target_pairs={{0,2},{2,0},{4,6},{6,4},{1,3},{3,1},{5,7},{7,5},{8,10},{10,8},{12,... | collective-permute-start | bytes 344072 | tf_op jit(solution)/shard_map/ppermute | solution.py:44
  45.0 1.3 %shard_map.205 = (bf16[1152,256]{1,0:T(8,128)(2,1)}, f32[384,256]{1,0:T(8,128)S(1)}) custom-call(bf16[1152,256]{1,0:T(8,128)(2,1)S(1)} %get-tuple-element.77.edge_grads, bf16[1152,256]{1,0:T(8,128)(2,1)S(1)} %get-tuple-element.116.pre_grad, bf16[384,256]{1,0:T(8,128)(2,1)S(1)} %get-tuple-element.117.sender_sum, ...), custom_call_target="tpu_custom_call" | custom-call | flops 251658240 | bytes 3342336 | tf_op jit(solution)/shard_map/pallas_call | solution.py:492
  46.3 0.0 collective-permute-start.15
  46.3 1.9 %collective-permute-done.14.refs_3_ = bf16[224,256]{1,0:T(8,128)(2,1)S(1)} collective-permute-done((bf16[224,256]{1,0:T(8,128)(2,1)S(1)}, bf16[224,256]{1,0:T(8,128)(2,1)S(1)}, u32[]{:S(2)}, u32[]{:S(2)}) %collective-permute-start.14) | collective-permute-done | bytes 114720 | tf_op jit(solution)/shard_map/ppermute | solution.py:44
  48.3 0.0 collective-permute-start.18
  48.3 0.0 collective-permute-done.13.refs_2_
  48.3 0.5 collective-permute-start.17
  48.8 0.2 collective-permute-done.12.refs_1_
  49.0 0.0 collective-permute-start.16
  49.0 1.1 %shard_map.206 = bf16[384,256]{1,0:T(8,128)(2,1)} custom-call(s32[8,32]{1,0:T(8,128)S(1)} %get-tuple-element.115.send_list, f32[384,256]{1,0:T(8,128)S(1)} %get-tuple-element.120.local_grad, bf16[64,256]{1,0:T(8,128)(2,1)S(1)} %get-tuple-element.121.middle, bf16[96,256]{1,0:T(8,128)(2,1)S(1)} %collective-permute-done.10.to_high, ...), custom_call_target="tpu_custom_call" | custom-call | flops 50331648 | bytes 721920 | tf_op jit(solution)/shard_map/pallas_call | solution.py:492
  50.1 0.5 %convert_reduce_fusion = (bf16[256]{0:T(256)(128)(2,1)}, bf16[256]{0:T(256)(128)(2,1)}) fusion(f32[16,256]{1,0:T(8,128)S(1)} %get-tuple-element.137), kind=kLoop, calls=%fused_computation.2 | loop fusion | flops 1024 | bytes 5120 | tf_op jit(solution)/shard_map/convert_element_type | solution.py:758
  50.6 0.0 collective-permute-done.15.refs_4_
  50.6 0.0 collective-permute-done.18.refs_7_
  50.6 0.0 collective-permute-done.17.refs_6_
  50.6 0.0 collective-permute-done.16.refs_5_
  50.6 1.0 %shard_map.207 = (bf16[768,256]{1,0:T(8,128)(2,1)}, bf16[256,256]{1,0:T(8,128)(2,1)}, bf16[512,256]{1,0:T(8,128)(2,1)}, bf16[256,256]{1,0:T(8,128)(2,1)}) custom-call(bf16[224,256]{1,0:T(8,128)(2,1)S(1)} %get-tuple-element.127.refs_0_, bf16[224,256]{1,0:T(8,128)(2,1)S(1)} %collective-permute-done.12.refs_1_, ...), custom_call_target="tpu_custom_call" | custom-call | bytes 1835008 | tf_op jit(solution)/shard_map/pallas_call | solution.py:492
  (6 shorter events, 0.1 us)
Async XLA Ops:
  1.9 7.6 %collective-permute-start = (bf16[96,256]{1,0:T(8,128)(2,1)S(1)}, bf16[96,256]{1,0:T(8,128)(2,1)S(1)}, u32[]{:S(2)}, u32[]{:S(2)}) collective-permute-start(bf16[96,256]{1,0:T(8,128)(2,1)S(1)} %get-tuple-element.80), channel_id=1, source_target_pairs={{0,4},{4,8},{8,12},{12,0},{1,5},{5,9},{9,13},{13,1},{2,6},{6,10},{... | collective-permute-start | bytes 147464 | tf_op jit(solution)/shard_map/ppermute | solution.py:25
  5.0 4.6 %collective-permute-start.1 = (bf16[96,256]{1,0:T(8,128)(2,1)S(1)}, bf16[96,256]{1,0:T(8,128)(2,1)S(1)}, u32[]{:S(2)}, u32[]{:S(2)}) collective-permute-start(bf16[96,256]{1,0:T(8,128)(2,1)S(1)} %get-tuple-element.81), channel_id=1, source_target_pairs={{0,12},{4,0},{8,4},{12,8},{1,13},{5,1},{9,5},{13,9},{2,14},{6,2},{... | collective-permute-start | bytes 147464 | tf_op jit(solution)/shard_map/ppermute | solution.py:25
  9.7 3.6 %collective-permute-start.2 = (bf16[96,256]{1,0:T(8,128)(2,1)S(1)}, bf16[96,256]{1,0:T(8,128)(2,1)S(1)}, u32[]{:S(2)}, u32[]{:S(2)}) collective-permute-start(bf16[96,256]{1,0:T(8,128)(2,1)S(1)} %pad_maximum_fusion), channel_id=1, source_target_pairs={{0,1},{1,2},{2,3},{3,0},{4,5},{5,6},{6,7},{7,4},{8,9},{9,10},{10,1... | collective-permute-start | bytes 147464 | tf_op jit(solution)/shard_map/ppermute | solution.py:25
  9.7 3.6 %collective-permute-start.3 = (bf16[96,256]{1,0:T(8,128)(2,1)S(1)}, bf16[96,256]{1,0:T(8,128)(2,1)S(1)}, u32[]{:S(2)}, u32[]{:S(2)}) collective-permute-start(bf16[96,256]{1,0:T(8,128)(2,1)S(1)} %pad_maximum_fusion.1), channel_id=1, source_target_pairs={{0,3},{1,0},{2,1},{3,2},{4,7},{5,4},{6,5},{7,6},{8,11},{9,8},{10,9... | collective-permute-start | bytes 147464 | tf_op jit(solution)/shard_map/ppermute | solution.py:25
  18.9 3.2 %collective-permute-start.4 = (bf16[1008,256]{1,0:T(8,128)(2,1)S(1)}, bf16[1008,256]{1,0:T(8,128)(2,1)S(1)}, u32[]{:S(2)}, u32[]{:S(2)}) collective-permute-start(bf16[1008,256]{1,0:T(8,128)(2,1)S(1)} %get-tuple-element.99), channel_id=1, source_target_pairs={{0,1},{1,0},{2,3},{3,2},{4,5},{5,4},{6,7},{7,6},{8,9},{9,8},{10,11... | collective-permute-start | bytes 1548296 | tf_op jit(solution)/shard_map/ppermute | solution.py:54
  20.6 5.2 %collective-permute-start.8 = (bf16[96,256]{1,0:T(8,128)(2,1)S(1)}, bf16[96,256]{1,0:T(8,128)(2,1)S(1)}, u32[]{:S(2)}, u32[]{:S(2)}) collective-permute-start(bf16[96,256]{1,0:T(8,128)(2,1)S(1)} %get-tuple-element.104), channel_id=1, source_target_pairs={{0,3},{1,2},{2,1},{3,0},{4,7},{5,6},{6,5},{7,4},{8,11},{9,10},{10,... | collective-permute-start | bytes 147464 | tf_op jit(solution)/shard_map/ppermute | solution.py:31
  22.2 5.7 %collective-permute-start.5 = (bf16[240,256]{1,0:T(8,128)(2,1)S(1)}, bf16[240,256]{1,0:T(8,128)(2,1)S(1)}, u32[]{:S(2)}, u32[]{:S(2)}) collective-permute-start(bf16[240,256]{1,0:T(8,128)(2,1)S(1)} %get-tuple-element.101), channel_id=1, source_target_pairs={{0,2},{2,0},{4,6},{6,4},{1,3},{3,1},{5,7},{7,5},{8,10},{10,8},{12,... | collective-permute-start | bytes 368648 | tf_op jit(solution)/shard_map/ppermute | solution.py:44
  22.8 6.2 %collective-permute-start.6 = (bf16[240,256]{1,0:T(8,128)(2,1)S(1)}, bf16[240,256]{1,0:T(8,128)(2,1)S(1)}, u32[]{:S(2)}, u32[]{:S(2)}) collective-permute-start(bf16[240,256]{1,0:T(8,128)(2,1)S(1)} %get-tuple-element.102), channel_id=1, source_target_pairs={{0,4},{2,6},{4,0},{6,2},{1,5},{3,7},{5,1},{7,3},{8,12},{10,14},{12... | collective-permute-start | bytes 368648 | tf_op jit(solution)/shard_map/ppermute | solution.py:44
  23.8 7.9 %collective-permute-start.7 = (bf16[240,256]{1,0:T(8,128)(2,1)S(1)}, bf16[240,256]{1,0:T(8,128)(2,1)S(1)}, u32[]{:S(2)}, u32[]{:S(2)}) collective-permute-start(bf16[240,256]{1,0:T(8,128)(2,1)S(1)} %get-tuple-element.103), channel_id=1, source_target_pairs={{0,6},{2,4},{4,2},{6,0},{1,7},{3,5},{5,3},{7,1},{8,14},{10,12},{12... | collective-permute-start | bytes 368648 | tf_op jit(solution)/shard_map/ppermute | solution.py:44
  31.8 9.7 %collective-permute-start.9 = (bf16[240,256]{1,0:T(8,128)(2,1)S(1)}, bf16[240,256]{1,0:T(8,128)(2,1)S(1)}, u32[]{:S(2)}, u32[]{:S(2)}) collective-permute-start(bf16[240,256]{1,0:T(8,128)(2,1)S(1)} %shard_map.203.own), channel_id=1, source_target_pairs={{0,8},{8,0},{1,9},{9,1},{2,10},{10,2},{3,11},{11,3},{4,12},{12,4},... | collective-permute-start | bytes 368648 | tf_op jit(solution)/shard_map/ppermute | solution.py:533
  34.1 6.0 %collective-permute-start.10 = (bf16[96,256]{1,0:T(8,128)(2,1)S(1)}, bf16[96,256]{1,0:T(8,128)(2,1)S(1)}, u32[]{:S(2)}, u32[]{:S(2)}) collective-permute-start(bf16[96,256]{1,0:T(8,128)(2,1)S(1)} %get-tuple-element.111), channel_id=1, source_target_pairs={{0,4},{4,8},{8,12},{12,0},{1,5},{5,9},{9,13},{13,1},{2,6},{6,10},{... | collective-permute-start | bytes 147464 | tf_op jit(solution)/shard_map/ppermute | solution.py:25
  35.8 5.2 %collective-permute-start.11 = (bf16[96,256]{1,0:T(8,128)(2,1)S(1)}, bf16[96,256]{1,0:T(8,128)(2,1)S(1)}, u32[]{:S(2)}, u32[]{:S(2)}) collective-permute-start(bf16[96,256]{1,0:T(8,128)(2,1)S(1)} %get-tuple-element.112), channel_id=1, source_target_pairs={{0,12},{4,0},{8,4},{12,8},{1,13},{5,1},{9,5},{13,9},{2,14},{6,2},{... | collective-permute-start | bytes 147464 | tf_op jit(solution)/shard_map/ppermute | solution.py:25
  41.5 6.8 %collective-permute-start.14 = (bf16[224,256]{1,0:T(8,128)(2,1)S(1)}, bf16[224,256]{1,0:T(8,128)(2,1)S(1)}, u32[]{:S(2)}, u32[]{:S(2)}) collective-permute-start(bf16[224,256]{1,0:T(8,128)(2,1)S(1)} %get-tuple-element.127.refs_0_), channel_id=1, source_target_pairs={{0,6},{2,4},{4,2},{6,0},{1,7},{3,5},{5,3},{7,1},{8,14},{10,12},{12... | collective-permute-start | bytes 344072 | tf_op jit(solution)/shard_map/ppermute | solution.py:44
  42.5 5.8 %collective-permute-start.13 = (bf16[224,256]{1,0:T(8,128)(2,1)S(1)}, bf16[224,256]{1,0:T(8,128)(2,1)S(1)}, u32[]{:S(2)}, u32[]{:S(2)}) collective-permute-start(bf16[224,256]{1,0:T(8,128)(2,1)S(1)} %get-tuple-element.127.refs_0_), channel_id=1, source_target_pairs={{0,4},{2,6},{4,0},{6,2},{1,5},{3,7},{5,1},{7,3},{8,12},{10,14},{12... | collective-permute-start | bytes 344072 | tf_op jit(solution)/shard_map/ppermute | solution.py:44
  43.4 5.5 %collective-permute-start.12 = (bf16[224,256]{1,0:T(8,128)(2,1)S(1)}, bf16[224,256]{1,0:T(8,128)(2,1)S(1)}, u32[]{:S(2)}, u32[]{:S(2)}) collective-permute-start(bf16[224,256]{1,0:T(8,128)(2,1)S(1)} %get-tuple-element.127.refs_0_), channel_id=1, source_target_pairs={{0,2},{2,0},{4,6},{6,4},{1,3},{3,1},{5,7},{7,5},{8,10},{10,8},{12,... | collective-permute-start | bytes 344072 | tf_op jit(solution)/shard_map/ppermute | solution.py:44
  46.3 4.3 %collective-permute-start.15 = (bf16[224,256]{1,0:T(8,128)(2,1)S(1)}, bf16[224,256]{1,0:T(8,128)(2,1)S(1)}, u32[]{:S(2)}, u32[]{:S(2)}) collective-permute-start(bf16[224,256]{1,0:T(8,128)(2,1)S(1)} %get-tuple-element.127.refs_0_), channel_id=1, source_target_pairs={{0,1},{1,0},{2,3},{3,2},{4,5},{5,4},{6,7},{7,6},{8,9},{9,8},{10,11... | collective-permute-start | bytes 344072 | tf_op jit(solution)/shard_map/ppermute | solution.py:54
  48.3 2.3 %collective-permute-start.18 = (bf16[224,256]{1,0:T(8,128)(2,1)S(1)}, bf16[224,256]{1,0:T(8,128)(2,1)S(1)}, u32[]{:S(2)}, u32[]{:S(2)}) collective-permute-start(bf16[224,256]{1,0:T(8,128)(2,1)S(1)} %collective-permute-done.14.refs_3_), channel_id=1, source_target_pairs={{0,1},{1,0},{2,3},{3,2},{4,5},{5,4},{6,7},{7,6},{8,9},{9,8},{10,11... | collective-permute-start | bytes 344072 | tf_op jit(solution)/shard_map/ppermute | solution.py:54
  48.3 2.3 %collective-permute-start.17 = (bf16[224,256]{1,0:T(8,128)(2,1)S(1)}, bf16[224,256]{1,0:T(8,128)(2,1)S(1)}, u32[]{:S(2)}, u32[]{:S(2)}) collective-permute-start(bf16[224,256]{1,0:T(8,128)(2,1)S(1)} %collective-permute-done.13.refs_2_), channel_id=1, source_target_pairs={{0,1},{1,0},{2,3},{3,2},{4,5},{5,4},{6,7},{7,6},{8,9},{9,8},{10,11... | collective-permute-start | bytes 344072 | tf_op jit(solution)/shard_map/ppermute | solution.py:54
  49.0 1.7 %collective-permute-start.16 = (bf16[224,256]{1,0:T(8,128)(2,1)S(1)}, bf16[224,256]{1,0:T(8,128)(2,1)S(1)}, u32[]{:S(2)}, u32[]{:S(2)}) collective-permute-start(bf16[224,256]{1,0:T(8,128)(2,1)S(1)} %collective-permute-done.12.refs_1_), channel_id=1, source_target_pairs={{0,1},{1,0},{2,3},{3,2},{4,5},{5,4},{6,7},{7,6},{8,9},{9,8},{10,11... | collective-permute-start | bytes 344072 | tf_op jit(solution)/shard_map/ppermute | solution.py:54

commit v13 on v12

--- a/solution.py
+++ b/solution.py
@@ -193,12 +193,12 @@
     pre[...] = dot(edges[...], w_in[:width]) + dot(near_rows[...], table)
 
 
-def split_by_core(sums, first, keep_out, away_out):
+def split_by_core(sums, keep_out, away_out):
     half = sums.shape[0] // 2
     core = lax.axis_index(CORE)
-    keep_out[first : first + half] = sums[pl.ds(pl.multiple_of(core * half, half), half), :]
+    keep_out[...] = sums[pl.ds(pl.multiple_of(core * half, half), half), :]
     away = sums[pl.ds(pl.multiple_of((1 - core) * half, half), half), :]
-    away_out[first : first + half] = away.astype(BF16)
+    away_out[:half] = away.astype(BF16)
 
 
 def pack_gains(edge_gain, node_gain):
@@ -238,10 +238,13 @@
     sender_out,
     receiver_out,
     node_part_out,
-    across_out,
-    rest_out,
-    keep_out,
-    away_out,
+    top_out,
+    middle_out,
+    bottom_out,
+    edge_keep,
+    edge_away,
+    node_keep,
+    node_away,
     gains_out,
     slope_kept,
     hidden_kept,
@@ -313,100 +316,68 @@
     sender_out[...] = own
     receiver_out[...] = received
     halo_grad = dot_nt(away, w_in[width : 2 * width]).astype(BF16)
-    parts = [halo_grad[k * slots : (k + 1) * slots] for k in range(8)]
-    up = jnp.concatenate([parts[0], parts[3], parts[5]], axis=0)
-    down = jnp.concatenate([parts[2], parts[4], parts[7]], axis=0)
-    core = lax.axis_index(CORE)
-    sums_rows = gains_out.shape[0] + keep_out.shape[0]
-
-    @pl.when(core == 0)
-    def _():
-        away_out[sums_rows:] = up
-        across_out[...] = down
-
-    @pl.when(core == 1)
-    def _():
-        away_out[sums_rows:] = down
-        across_out[...] = up
-
-    rest_out[...] = jnp.concatenate([parts[1], parts[6]], axis=0)
+    top_out[...] = halo_grad[: 3 * slots]
+    middle_out[...] = halo_grad[3 * slots : 5 * slots]
+    bottom_out[...] = halo_grad[5 * slots :]
     edge_sums[:width] = dot_tn(edges[...], pre_grad)
     edge_sums[width : 2 * width] = dot_tn(x, own) + dot_tn(halo, away)
     edge_sums[2 * width : 3 * width] = dot_tn(x, received)
     edge_sums[3 * width : 4 * width] = dot_tn(hidden_kept[...], out_grad)
-    split_by_core(edge_sums, 0, keep_out, away_out)
-    split_by_core(node_sums, edge_sums.shape[0] // 2, keep_out, away_out)
+    split_by_core(edge_sums, edge_keep, edge_away)
+    split_by_core(node_sums, node_keep, node_away)
     gains = pack_gains(edge_gain, node_gain)
-    away_out[keep_out.shape[0] : sums_rows] = gains
+    edge_away[edge_keep.shape[0] :] = gains
     gains_out[...] = gains
 
 
-def pair_kernel(parts, keep, gains, other, *outs):
+def pair_kernel(packed, keep, *refs):
+    gains, other, outs = (refs[0], refs[1], refs[2:]) if packed else (None, refs[0], refs[1:])
     rows = keep.shape[0]
-    packed = gains.shape[0]
-    members = len(outs)
-    both = gains[...].astype(F32) + other[rows : rows + packed].astype(F32)
-    summed = pack_gains(both[0:1] + both[1:2], both[2:3] + both[3:4])
+    step = rows // len(outs)
     me = place_in_square()
     for offset, out in enumerate(outs):
-        owner = me ^ offset
-        out[:packed] = summed
-        first, at = 0, packed
-        for part in parts:
-            step = part // members
-            source = pl.ds(pl.multiple_of(first + owner * step, 16), step)
-            out[at : at + step] = (keep[source, :] + other[source, :].astype(F32)).astype(BF16)
-            first, at = first + part, at + step
-
-
-def add_packed(values):
-    packed = 16
-    gains = values[:packed]
-    return pack_gains(gains[0:1] + gains[1:2], gains[2:3] + gains[3:4])
-
-
-def sum_kernel(*refs):
-    sums_out = refs[-1]
-    sums = tree_sum([block[...].astype(F32) for block in refs[:-1]])
+        source = pl.ds(pl.multiple_of((me ^ offset) * step, 16), step)
+        out[packed:] = (keep[source, :] + other[source, :].astype(F32)).astype(BF16)
+    if packed:
+        both = gains[...].astype(F32) + other[rows:].astype(F32)
+        summed = pack_gains(both[0:1] + both[1:2], both[2:3] + both[3:4])
+        for out in outs:
+            out[:packed] = summed
+
+
+def store_sums(packed, sums, sums_out):
     sums_out[...] = sums.astype(BF16)
-    sums_out[:16] = add_packed(sums)
-
-
-def join_kernel(own, other, sums_out):
+    if packed:
+        sums_out[:packed] = pack_gains(sums[0:1] + sums[1:2], sums[2:3] + sums[3:4])
+
+
+def sum_kernel(packed, *refs):
+    store_sums(packed, tree_sum([block[...].astype(F32) for block in refs[:-1]]), refs[-1])
+
+
+def whole_kernel(packed, own, other, mine, *gains_out):
     sums = own[...].astype(F32) + other[...].astype(F32)
-    sums_out[...] = sums.astype(BF16)
-    sums_out[:16] = add_packed(sums)
-
-
-def whole_kernel(own, other, gains_out, mine):
-    packed = gains_out.shape[0]
-    sums = own[...].astype(F32) + other[...].astype(F32)
-    gains_out[...] = sums[:packed]
     mine[...] = sums[packed:].astype(BF16)
-
-
-def place_kernel(parts, *refs):
-    count = 2 * len(parts)
-    sems, wholes = refs[-1], refs[-1 - len(parts) : -1]
-    outs = refs[-1 - len(parts) - count : -1 - len(parts)]
-    blocks = refs[: -1 - len(parts) - count]
+    for out in gains_out:
+        out[...] = sums[:packed]
+
+
+def place_kernel(*refs):
+    blocks, first, second, whole, sems = refs[:-4], *refs[-4:]
     members = len(blocks) // 2
     core = lax.axis_index(CORE)
     me = place_in_square()
     for position, block in enumerate(blocks):
         half = core if position < members else 1 - core
         owner = me ^ (position % members)
-        at = 0
-        for part, whole in zip(parts, wholes):
-            step = part // members
-            row = pl.multiple_of(half * part + owner * step, 16)
-            whole[pl.ds(row, step), :] = block[at : at + step]
-            at += step
-    copies = []
-    for i, whole in enumerate(wholes):
-        cut = outs[2 * i].shape[0]
-        copies.append(pltpu.make_async_copy(whole.at[:cut], outs[2 * i], sems.at[2 * i]))
-        copies.append(pltpu.make_async_copy(whole.at[cut:], outs[2 * i + 1], sems.at[2 * i + 1]))
+        step = block.shape[0]
+        row = pl.multiple_of((half * members + owner) * step, 16)
+        whole[pl.ds(row, step), :] = block[...]
+    cut = first.shape[0]
+    copies = [
+        pltpu.make_async_copy(whole.at[:cut], first, sems.at[0]),
+        pltpu.make_async_copy(whole.at[cut:], second, sems.at[1]),
+    ]
     for copy in copies:
         copy.start()
     for copy in copies:
@@ -427,52 +398,61 @@
     )
 
 
-def turn_kernel(other, across, rest, high, low, middle):
-    slots = rest.shape[0] // 2
-    first = other.shape[0] - 3 * slots
-
-    def turn(up_back, down_back):
-        high[:slots] = up_back[:slots]
-        high[slots : 2 * slots] = down_back[:slots]
-        high[2 * slots :] = rest[:slots]
-        low[:slots] = up_back[2 * slots :]
-        low[slots : 2 * slots] = down_back[2 * slots :]
-        low[2 * slots :] = rest[slots:]
-        middle[:slots] = up_back[slots : 2 * slots]
-        middle[slots:] = down_back[slots : 2 * slots]
+def turn_kernel(top, middle, bottom, along_core, along_chip, center):
+    slots = middle.shape[0] // 2
+
+    def turn(up, down):
+        up[:slots] = top[:slots]
+        up[slots : 2 * slots] = middle[:slots]
+        up[2 * slots :] = bottom[:slots]
+        down[:slots] = top[2 * slots :]
+        down[slots : 2 * slots] = middle[slots:]
+        down[2 * slots :] = bottom[2 * slots :]
 
     core = lax.axis_index(CORE)
 
     @pl.when(core == 0)
     def _():
-        turn(across, other.at[first:])
+        turn(along_core, along_chip)
 
     @pl.when(core == 1)
     def _():
-        turn(other.at[first:], across)
-
-
-def return_kernel(send_list, local_grad, middle, to_high, to_low, nodes_grad):
+        turn(along_chip, along_core)
+
+    center[:slots] = top[slots : 2 * slots]
+    center[slots:] = bottom[slots : 2 * slots]
+
+
+def return_kernel(send_list, local_grad, center, along_core, along_chip, nodes_grad, returned):
     slots = send_list.shape[1]
 
-    def block(ref, k):
-        return ref[k * slots : (k + 1) * slots]
-
-    returned = jnp.concatenate(
-        [
-            block(to_high, 0),
-            block(to_high, 2),
-            block(to_high, 1),
-            block(middle, 0),
-            block(middle, 1),
-            block(to_low, 0),
-            block(to_low, 2),
-            block(to_low, 1),
-        ],
-        axis=0,
-    )
+    def fill(up, down):
+        for k, (source, i) in enumerate(
+            [
+                (up, 0),
+                (center, 0),
+                (down, 0),
+                (up, 1),
+                (down, 1),
+                (up, 2),
+                (center, 1),
+                (down, 2),
+            ]
+        ):
+            returned[k * slots : (k + 1) * slots] = source[i * slots : (i + 1) * slots]
+
+    core = lax.axis_index(CORE)
+
+    @pl.when(core == 0)
+    def _():
+        fill(along_chip, along_core)
+
+    @pl.when(core == 1)
+    def _():
+        fill(along_core, along_chip)
+
     hot = list_hot(send_list[...], local_grad.shape[0])
-    nodes_grad[...] = (local_grad[...] + dot_tn(hot, returned)).astype(BF16)
+    nodes_grad[...] = (local_grad[...] + dot_tn(hot, returned[...])).astype(BF16)
 
 
 SMEM = pltpu.SMEM
@@ -480,7 +460,15 @@
 HBM = pltpu.HBM
 
 
-def call(body, outs, flops, *operands, spaces=(), out_space=VMEM, scratch=()):
+def call(body, outs, flops, *operands, spaces=(), out_space=VMEM, scratch=(), after=()):
+    if after:
+        first, rest = len(operands), len(operands) + len(after)
+        inner = body
+
+        def body(*refs):
+            inner(*refs[:first], *refs[rest:])
+
+        operands = operands + tuple(after)
     moved = sum(x.size * x.dtype.itemsize for x in operands)
     moved += sum(x.size * jnp.dtype(x.dtype).itemsize for x in outs)
     spaces = list(spaces) + [VMEM] * (len(operands) - len(spaces))
@@ -508,42 +496,60 @@
     return jax.ShapeDtypeStruct((rows, columns), dtype)
 
 
-def placed(parts, blocks, width):
-    return call(
-        functools.partial(place_kernel, parts),
-        [
-            shaped(3 * width, width, BF16),
-            shaped(width, width, BF16),
-            shaped(2 * width, width, BF16),
-            shaped(width, width, BF16),
-        ],
-        0,
-        *blocks,
-        out_space=HBM,
-        scratch=[pltpu.VMEM((2 * part, width), BF16) for part in parts]
-        + [pltpu.SemaphoreType.DMA((2 * len(parts),))],
-    )
-
-
-def joined(sums, packed, *beside):
-    rows, width = sums.shape
+def cut_in_blocks(keep, gains, other, after=()):
+    packed = 0 if gains is None else gains.shape[0]
+    members = square_members()
+    block = shaped(packed + keep.shape[0] // members, keep.shape[1], BF16)
+    operands = [keep, other] if gains is None else [keep, gains, other]
+    return call(functools.partial(pair_kernel, packed), [block] * members, 0, *operands, after=after)
+
+
+def exchanged(blocks):
+    return [blocks[0]] + [in_square(x, offset) for offset, x in enumerate(blocks[1:], 1)]
+
+
+def summed(packed, blocks, after=()):
+    body = functools.partial(sum_kernel, packed)
+    return call(body, [like(blocks[0])], 0, *blocks, after=after)[0]
+
+
+def over_squares(packed, sums):
     size = lax.axis_size(FAR)
     distance = 1
     while True:
         other = lax.ppermute(sums, FAR, [(i, i ^ distance) for i in range(size)])
         distance *= 2
         if distance == size:
-            break
-        (sums,) = call(join_kernel, [like(sums)], 0, sums, other)
-    other, *beside = lax.optimization_barrier((other, *beside))
-    gains, mine = call(
-        whole_kernel,
-        [shaped(packed, width, F32), shaped(rows - packed, width, BF16)],
+            return sums, other
+        sums = summed(packed, [sums, other])
+
+
+def whole_sum(packed, sums, other, after=()):
+    rows, width = sums.shape
+    outs = [shaped(rows - packed, width, BF16)]
+    if packed:
+        outs.append(shaped(packed, width, F32))
+    return call(functools.partial(whole_kernel, packed), outs, 0, sums, other, after=after)
+
+
+def gathered(mine):
+    blocks = [mine] + [in_square(mine, offset) for offset in range(1, square_members())]
+    return blocks + [across_cores(block) for block in blocks]
+
+
+def placed(blocks, first_rows, second_rows):
+    width = blocks[0].shape[1]
+    return call(
+        place_kernel,
+        [shaped(first_rows, width, BF16), shaped(second_rows, width, BF16)],
         0,
-        sums,
-        other,
-    )
-    return gains, mine, *beside
+        *blocks,
+        out_space=HBM,
+        scratch=[
+            pltpu.VMEM((first_rows + second_rows, width), BF16),
+            pltpu.SemaphoreType.DMA((2,)),
+        ],
+    )
 
 
 def on_device(
@@ -645,9 +651,20 @@
         near_hot,
         w_edge_in,
     )
-    parts = (2 * width, 3 * width // 2)
-    halves = sum(parts)
-    pre_grad, sender_sum, receiver_sum, node_part, across, rest, keep, away, gains = call(
+    (
+        pre_grad,
+        sender_sum,
+        receiver_sum,
+        node_part,
+        top,
+        middle,
+        bottom,
+        edge_keep,
+        edge_away,
+        node_keep,
+        node_away,
+        gains,
+    ) = call(
         functools.partial(layer_kernel, tile_rows),
         [
             shaped(edge_rows, width, BF16),
@@ -656,8 +673,11 @@
             shaped(count, width, F32),
             shaped(3 * slots, width, BF16),
             shaped(2 * slots, width, BF16),
-            shaped(halves, width, F32),
-            shaped(halves + 16 + 3 * slots, width, BF16),
+            shaped(3 * slots, width, BF16),
+            shaped(2 * width, width, F32),
+            shaped(2 * width + 16, width, BF16),
+            shaped(3 * width // 2, width, F32),
+            shaped(3 * width // 2, width, BF16),
             shaped(16, width, BF16),
         ],
         square * (6 * edge_rows + 11 * count + 2 * halo_rows)
@@ -692,18 +712,16 @@
             pltpu.VMEM((4 * width, width), F32),
         ],
     )
-    other = across_cores(away)
-    members = square_members()
-    own, *blocks = call(
-        functools.partial(pair_kernel, parts),
-        [shaped(16 + halves // members, width, BF16)] * members,
-        0,
-        keep,
-        gains,
-        other,
-    )
-    received = [in_square(block, offset) for offset, block in enumerate(blocks, 1)]
-    high, low, middle = call(
+    packed = gains.shape[0]
+    edge_other = across_cores(edge_away)
+    node_other = across_cores(node_away)
+    top = passed_along(top, PX, 1)
+    bottom = passed_along(bottom, PX, -1)
+    edge_cut = cut_in_blocks(edge_keep, gains, edge_other)
+    node_cut = cut_in_blocks(node_keep, None, node_other, after=edge_cut[:1])
+    edge_blocks = exchanged(edge_cut)
+    node_blocks = exchanged(node_cut)
+    along_core, along_chip, center = call(
         turn_kernel,
         [
             shaped(3 * slots, width, BF16),
@@ -711,17 +729,26 @@
             shaped(2 * slots, width, BF16),
         ],
         10**10,
-        other,
-        across_chips(across),
-        rest,
-    )
-    *received, high, low = lax.optimization_barrier((*received, high, low))
-    (sums,) = call(sum_kernel, [like(own)], 0, own, *received)
-    gains, mine, to_high, to_low = joined(
-        sums, gains.shape[0], passed_along(high, PX, 1), passed_along(low, PX, -1)
-    )
-    blocks = [mine] + [in_square(mine, offset) for offset in range(1, members)]
-    blocks += [across_cores(block) for block in blocks]
+        top,
+        middle,
+        bottom,
+    )
+    edge_sum = summed(packed, edge_blocks, after=node_cut[:1])
+    *node_blocks, along_core, along_chip = lax.optimization_barrier(
+        (*node_blocks, along_core, along_chip)
+    )
+    node_sum = summed(0, node_blocks, after=[edge_sum])
+    edge_pair = over_squares(packed, edge_sum)
+    node_pair = over_squares(0, node_sum)
+    along_core = across_cores(along_core)
+    along_chip = across_chips(along_chip)
+    edge_mine, gains = whole_sum(packed, *edge_pair, after=[node_sum])
+    *node_pair, along_core, along_chip = lax.optimization_barrier(
+        (*node_pair, along_core, along_chip)
+    )
+    (node_mine,) = whole_sum(0, *node_pair, after=[edge_mine])
+    edge_blocks = gathered(edge_mine)
+    node_blocks = gathered(node_mine)
     edges_grad, local_grad = call(
         finish_kernel,
         [shaped(edge_rows, width, BF16), shaped(count, width, F32)],
@@ -739,14 +766,16 @@
         2 * halo_rows * count * width,
         send_list,
         local_grad,
-        middle,
-        to_high,
-        to_low,
-    )
-    *blocks, nodes_grad, edges_grad = lax.optimization_barrier((*blocks, nodes_grad, edges_grad))
-    w_edge_in_grad, w_edge_out_grad, w_node_in_grad, w_node_out_grad = placed(
-        parts, blocks, width
-    )
+        center,
+        along_core,
+        along_chip,
+        scratch=[pltpu.VMEM((halo_rows, width), BF16)],
+    )
+    *node_blocks, nodes_grad, edges_grad = lax.optimization_barrier(
+        (*node_blocks, nodes_grad, edges_grad)
+    )
+    w_edge_in_grad, w_edge_out_grad = placed(edge_blocks, 3 * width, width)
+    w_node_in_grad, w_node_out_grad = placed(node_blocks, 2 * width, width)
     return (
         nodes_grad,
         edges_grad,

time: 52.4 us -> 56.8 us (1.084)
  starting transfers between devices: 22.5 us -> 32.3 us
  waiting for transfers between devices: 13 us -> 7.44 us
  Pallas kernels: 14.1 us -> 14.8 us
    ppermute x6 -> x12, starting transfers between devices: 7.12 us -> 14.5 us  [in_square(): lax.ppermute(array, SQUARE, [(i, i ^ offset) for i in range(square_member...]
    ppermute x6 -> x12, waiting for transfers between devices: 7.99 us -> 3.07 us  [in_square(): lax.ppermute(array, SQUARE, [(i, i ^ offset) for i in range(square_member...]
    ppermute x6, waiting for transfers between devices: 3.26 us -> 0.23 us  [passed_along(): lax.ppermute(array, axis, [(i, (i + by) % size) for i in range(size)])]
    ppermute x1 -> x2, waiting for transfers between devices: 0.35 us -> 2.47 us  [over_squares(): other = lax.ppermute(sums, FAR, [(i, i ^ distance) for i in range(size)])]
    ppermute x1 -> x2, starting transfers between devices: 2.33 us -> 3.44 us  [over_squares(): other = lax.ppermute(sums, FAR, [(i, i ^ distance) for i in range(size)])]
    ppermute x5 -> x11, starting transfers between devices: 2.18 us -> 3.22 us  [across_cores(): return lax.ppermute(array, CORE, [(0, 1), (1, 0)])]
    pallas_call x11 -> x15, Pallas kernels: 14.1 us -> 14.8 us  [call(): pl.pallas_call(body, out_shape=outs, in_specs=[pl.BlockSpec(memory_space=...]
    ppermute x5 -> x11, waiting for transfers between devices: 1.39 us -> 1.12 us  [across_cores(): return lax.ppermute(array, CORE, [(0, 1), (1, 0)])]
  transfers between devices with their start and end apart: 19 -> 32, of which waited for: 10 -> 9; matrix products, arithmetic and copies ran while one was open for 1% -> 1% of each run, Pallas kernels for 12% -> 12%
where the time goes in v13:
time: 56.8 us; the launch traced here: 56.6 us
  starting transfers between devices  32.3 us (57%)
  Pallas kernels  14.8 us (26%)
  waiting for transfers between devices  7.44 us (13%)
  between operations  1.47 us (3%)
    pallas_call x15, Pallas kernels, call(): pl.pallas_call(body, out_shape=outs, in_specs=[pl.BlockSpec(memory_space=...  14.8 us
    ppermute x12, starting transfers between devices, in_square(): lax.ppermute(array, SQUARE, [(i, i ^ offset) for i in range(square_member...  14.5 us
    ppermute x6, starting transfers between devices, passed_along(): lax.ppermute(array, axis, [(i, (i + by) % size) for i in range(size)])  10.8 us
    ppermute x2, starting transfers between devices, over_squares(): other = lax.ppermute(sums, FAR, [(i, i ^ distance) for i in range(size)])  3.44 us
    ppermute x11, starting transfers between devices, across_cores(): return lax.ppermute(array, CORE, [(0, 1), (1, 0)])  3.22 us
    ppermute x12, waiting for transfers between devices, in_square(): lax.ppermute(array, SQUARE, [(i, i ^ offset) for i in range(square_member...  3.07 us
    ppermute x2, waiting for transfers between devices, over_squares(): other = lax.ppermute(sums, FAR, [(i, i ^ distance) for i in range(size)])  2.47 us
  transfers between devices with their start and end apart: 32, of which 9 were waited for; matrix products, arithmetic and copies ran while one was open for 1% of the time, Pallas kernels for 12%

profile of v13, /device:TPU:0, one launch (start us, length us, event | category | flops | bytes accessed | tf_op | source)
XLA Modules:
  0.0 56.6 jit_solution(7098020299883039484)
XLA Ops:
  0.6 1.3 %shard_map.197 = (bf16[96,256]{1,0:T(8,128)(2,1)S(1)}, bf16[64,256]{1,0:T(8,128)(2,1)S(1)}, bf16[96,256]{1,0:T(8,128)(2,1)S(1)}, bf16[384,256]{1,0:T(8,128)(2,1)S(1)}, s32[8,32]{1,0:T(8,128)S(1)}) custom-call(bf16[384,256]{1,0:T(8,128)(2,1)} %nodes_hbm.1, s32[8,32]{1,0:T(8,128)} %list_hbm.1), custom_call_target="tpu_custom_call" | custom-call | flops 50331648 | bytes 526336 | tf_op jit(solution)/shard_map/pallas_call | solution.py:480
  1.9 3.1 %collective-permute-start = (bf16[96,256]{1,0:T(8,128)(2,1)S(1)}, bf16[96,256]{1,0:T(8,128)(2,1)S(1)}, u32[]{:S(2)}, u32[]{:S(2)}) collective-permute-start(bf16[96,256]{1,0:T(8,128)(2,1)S(1)} %get-tuple-element.89), channel_id=1, source_target_pairs={{0,4},{4,8},{8,12},{12,0},{1,5},{5,9},{9,13},{13,1},{2,6},{6,10},{... | collective-permute-start | bytes 147464 | tf_op jit(solution)/shard_map/ppermute | solution.py:25
  5.0 2.1 %collective-permute-start.1 = (bf16[96,256]{1,0:T(8,128)(2,1)S(1)}, bf16[96,256]{1,0:T(8,128)(2,1)S(1)}, u32[]{:S(2)}, u32[]{:S(2)}) collective-permute-start(bf16[96,256]{1,0:T(8,128)(2,1)S(1)} %get-tuple-element.90), channel_id=1, source_target_pairs={{0,12},{4,0},{8,4},{12,8},{1,13},{5,1},{9,5},{13,9},{2,14},{6,2},{... | collective-permute-start | bytes 147464 | tf_op jit(solution)/shard_map/ppermute | solution.py:25
  7.8 1.7 %shard_map.198 = (bf16[1152,768]{1,0:T(8,128)(2,1)S(1)}, bf16[1152,256]{1,0:T(8,128)(2,1)S(1)}, s32[9,128]{1,0:T(8,128)S(1)}, s32[9,128]{1,0:T(8,128)S(1)}, bf16...) custom-call(s32[9,128]{1,0:T(8,128)} %refs_0_.1, ...), custom_call_target="tpu_custom_call" | custom-call | bytes 6967296 | tf_op jit(solution)/shard_map/pallas_call | solution.py:480
  9.5 0.0 collective-permute-done.from_low
  9.5 0.1 collective-permute-done.1.from_high
  9.7 0.1 collective-permute-start.2
  9.7 1.7 %collective-permute-start.3 = (bf16[96,256]{1,0:T(8,128)(2,1)S(1)}, bf16[96,256]{1,0:T(8,128)(2,1)S(1)}, u32[]{:S(2)}, u32[]{:S(2)}) collective-permute-start(bf16[96,256]{1,0:T(8,128)(2,1)S(1)} %pad_maximum_fusion.1), channel_id=1, source_target_pairs={{0,3},{1,0},{2,1},{3,2},{4,7},{5,4},{6,5},{7,6},{8,11},{9,8},{10,9... | collective-permute-start | bytes 147464 | tf_op jit(solution)/shard_map/ppermute | solution.py:25
  11.5 1.8 %shard_map.199 = (f32[1152,256]{1,0:T(8,128)S(1)}, bf16[640,1152]{1,0:T(8,128)(2,1)S(1)}, bf16[384,1152]{1,0:T(8,128)(2,1)S(1)}) custom-call(bf16[384,256]{1,0:T(8,128)(2,1)S(1)} %get-tuple-element.83.nodes, bf16[1152,256]{1,0:T(8,128)(2,1)S(1)} %get-tuple-element.85.edges, s32[9,128]{1,0:T(8,128)S(1)} %get-tuple-element.87.senders, ...), custom_call_target="tpu_custom_call" | custom-call | flops 704643072 | bytes 6497280 | tf_op jit(solution)/shard_map/pallas_call | solution.py:480
  13.3 0.0 collective-permute-done.2.upward
  13.3 0.0 collective-permute-done.3.downward
  13.3 5.6 %shard_map.200 = (bf16[1152,256]{1,0:T(8,128)(2,1)S(1)}, bf16[384,256]{1,0:T(8,128)(2,1)S(1)}, bf16[384,256]{1,0:T(8,128)(2,1)S(1)}, f32[384,256]{1,0:T(8,128)S(...) custom-call(s32[1]{0:T(128)S(6)} %copy.22.count_ref, ...), custom_call_target="tpu_custom_call" | custom-call | flops 2583691264 | bytes 11486212 | tf_op jit(solution)/shard_map/pallas_call | solution.py:480
  18.9 1.6 %collective-permute-start.5 = (bf16[528,256]{1,0:T(8,128)(2,1)S(1)}, bf16[528,256]{1,0:T(8,128)(2,1)S(1)}, u32[]{:S(2)}, u32[]{:S(2)}) collective-permute-start(bf16[528,256]{1,0:T(8,128)(2,1)S(1)} %get-tuple-element.110), channel_id=1, source_target_pairs={{0,1},{1,0},{2,3},{3,2},{4,5},{5,4},{6,7},{7,6},{8,9},{9,8},{10,11... | collective-permute-start | bytes 811016 | tf_op jit(solution)/shard_map/ppermute | solution.py:54
  20.6 0.1 collective-permute-start.4
  20.7 1.1 %collective-permute-done.5.refs_1_ = bf16[528,256]{1,0:T(8,128)(2,1)S(1)} collective-permute-done((bf16[528,256]{1,0:T(8,128)(2,1)S(1)}, bf16[528,256]{1,0:T(8,128)(2,1)S(1)}, u32[]{:S(2)}, u32[]{:S(2)}) %collective-permute-start.5) | collective-permute-done | bytes 270368 | tf_op jit(solution)/shard_map/ppermute | solution.py:54
  21.8 0.1 shard_map.201
  21.8 0.5 collective-permute-start.11
  22.4 1.0 %collective-permute-start.12 = (bf16[144,256]{1,0:T(8,128)(2,1)S(1)}, bf16[144,256]{1,0:T(8,128)(2,1)S(1)}, u32[]{:S(2)}, u32[]{:S(2)}) collective-permute-start(bf16[144,256]{1,0:T(8,128)(2,1)S(1)} %get-tuple-element.126), channel_id=1, source_target_pairs={{0,4},{2,6},{4,0},{6,2},{1,5},{3,7},{5,1},{7,3},{8,12},{10,14},{12... | collective-permute-start | bytes 221192 | tf_op jit(solution)/shard_map/ppermute | solution.py:44
  23.4 2.0 %collective-permute-start.13 = (bf16[144,256]{1,0:T(8,128)(2,1)S(1)}, bf16[144,256]{1,0:T(8,128)(2,1)S(1)}, u32[]{:S(2)}, u32[]{:S(2)}) collective-permute-start(bf16[144,256]{1,0:T(8,128)(2,1)S(1)} %get-tuple-element.127), channel_id=1, source_target_pairs={{0,6},{2,4},{4,2},{6,0},{1,7},{3,5},{5,3},{7,1},{8,14},{10,12},{12... | collective-permute-start | bytes 221192 | tf_op jit(solution)/shard_map/ppermute | solution.py:44
  25.4 1.0 %collective-permute-start.9 = (bf16[96,256]{1,0:T(8,128)(2,1)S(1)}, bf16[96,256]{1,0:T(8,128)(2,1)S(1)}, u32[]{:S(2)}, u32[]{:S(2)}) collective-permute-start(bf16[96,256]{1,0:T(8,128)(2,1)S(1)} %get-tuple-element.116), channel_id=1, source_target_pairs={{0,4},{4,8},{8,12},{12,0},{1,5},{5,9},{9,13},{13,1},{2,6},{6,10},{... | collective-permute-start | bytes 147464 | tf_op jit(solution)/shard_map/ppermute | solution.py:25
  26.4 2.8 %collective-permute-start.10 = (bf16[96,256]{1,0:T(8,128)(2,1)S(1)}, bf16[96,256]{1,0:T(8,128)(2,1)S(1)}, u32[]{:S(2)}, u32[]{:S(2)}) collective-permute-start(bf16[96,256]{1,0:T(8,128)(2,1)S(1)} %get-tuple-element.118), channel_id=1, source_target_pairs={{0,12},{4,0},{8,4},{12,8},{1,13},{5,1},{9,5},{13,9},{2,14},{6,2},{... | collective-permute-start | bytes 147464 | tf_op jit(solution)/shard_map/ppermute | solution.py:25
  29.3 0.0 collective-permute-done.11.refs_1_
  29.3 0.5 collective-permute-start.6
  29.8 0.0 collective-permute-done.12.refs_2_
  29.8 0.0 collective-permute-start.7
  29.8 3.0 %collective-permute-start.8 = (bf16[96,256]{1,0:T(8,128)(2,1)S(1)}, bf16[96,256]{1,0:T(8,128)(2,1)S(1)}, u32[]{:S(2)}, u32[]{:S(2)}) collective-permute-start(bf16[96,256]{1,0:T(8,128)(2,1)S(1)} %get-tuple-element.115), channel_id=1, source_target_pairs={{0,6},{2,4},{4,2},{6,0},{1,7},{3,5},{5,3},{7,1},{8,14},{10,12},{12... | collective-permute-start | bytes 147464 | tf_op jit(solution)/shard_map/ppermute | solution.py:44
  32.9 0.1 collective-permute-done.9.top
  33.0 0.9 %collective-permute-start.17 = (bf16[144,256]{1,0:T(8,128)(2,1)S(1)}, bf16[144,256]{1,0:T(8,128)(2,1)S(1)}, u32[]{:S(2)}, u32[]{:S(2)}) collective-permute-start(bf16[144,256]{1,0:T(8,128)(2,1)S(1)} %shard_map.204.refs_4_.refs_0_), channel_id=1, source_target_pairs={{0,8},{8,0},{1,9},{9,1},{2,10},{10,2},{3,11},{11,3},{4,12},{12,4},... | collective-permute-start | bytes 221192 | tf_op jit(solution)/shard_map/ppermute | solution.py:520
  33.9 0.1 collective-permute-done.6.refs_1_
  34.0 0.0 collective-permute-done.7.refs_2_
  34.0 2.3 %collective-permute-done.8.refs_3_ = bf16[96,256]{1,0:T(8,128)(2,1)S(1)} collective-permute-done((bf16[96,256]{1,0:T(8,128)(2,1)S(1)}, bf16[96,256]{1,0:T(8,128)(2,1)S(1)}, u32[]{:S(2)}, u32[]{:S(2)}) %collective-permute-start.8) | collective-permute-done | bytes 49184 | tf_op jit(solution)/shard_map/ppermute | solution.py:44
  36.2 0.0 collective-permute-start.15
  36.2 0.4 collective-permute-start.16
  36.6 2.6 %collective-permute-start.14 = (bf16[96,256]{1,0:T(8,128)(2,1)S(1)}, bf16[96,256]{1,0:T(8,128)(2,1)S(1)}, u32[]{:S(2)}, u32[]{:S(2)}) collective-permute-start(bf16[96,256]{1,0:T(8,128)(2,1)S(1)} %shard_map.205.refs_2_.refs_0_), channel_id=1, source_target_pairs={{0,8},{8,0},{1,9},{9,1},{2,10},{10,2},{3,11},{11,3},{4,12},{12,4},... | collective-permute-start | bytes 147464 | tf_op jit(solution)/shard_map/ppermute | solution.py:520
  39.2 0.0 collective-permute-done.15.along_core
  39.2 0.6 collective-permute-done.16.along_chip
  39.7 2.5 %collective-permute-done.14.refs_1_ = bf16[96,256]{1,0:T(8,128)(2,1)S(1)} collective-permute-done((bf16[96,256]{1,0:T(8,128)(2,1)S(1)}, bf16[96,256]{1,0:T(8,128)(2,1)S(1)}, u32[]{:S(2)}, u32[]{:S(2)}) %collective-permute-start.14) | collective-permute-done | bytes 49184 | tf_op jit(solution)/shard_map/ppermute | solution.py:520
  42.2 0.1 collective-permute-start.21
  42.3 1.4 %collective-permute-start.20 = (bf16[96,256]{1,0:T(8,128)(2,1)S(1)}, bf16[96,256]{1,0:T(8,128)(2,1)S(1)}, u32[]{:S(2)}, u32[]{:S(2)}) collective-permute-start(bf16[96,256]{1,0:T(8,128)(2,1)S(1)} %shard_map.207.refs_0_), channel_id=1, source_target_pairs={{0,6},{2,4},{4,2},{6,0},{1,7},{3,5},{5,3},{7,1},{8,14},{10,12},{12... | collective-permute-start | bytes 147464 | tf_op jit(solution)/shard_map/ppermute | solution.py:44
  43.7 2.0 %collective-permute-start.19 = (bf16[96,256]{1,0:T(8,128)(2,1)S(1)}, bf16[96,256]{1,0:T(8,128)(2,1)S(1)}, u32[]{:S(2)}, u32[]{:S(2)}) collective-permute-start(bf16[96,256]{1,0:T(8,128)(2,1)S(1)} %shard_map.207.refs_0_), channel_id=1, source_target_pairs={{0,4},{2,6},{4,0},{6,2},{1,5},{3,7},{5,1},{7,3},{8,12},{10,14},{12... | collective-permute-start | bytes 147464 | tf_op jit(solution)/shard_map/ppermute | solution.py:44
  45.7 0.2 collective-permute-start.18
  45.9 1.3 %collective-permute-start.27 = (bf16[128,256]{1,0:T(8,128)(2,1)S(1)}, bf16[128,256]{1,0:T(8,128)(2,1)S(1)}, u32[]{:S(2)}, u32[]{:S(2)}) collective-permute-start(bf16[128,256]{1,0:T(8,128)(2,1)S(1)} %get-tuple-element.132.refs_2_.refs_0_), channel_id=1, source_target_pairs={{0,6},{2,4},{4,2},{6,0},{1,7},{3,5},{5,3},{7,1},{8,14},{10,12},{12... | collective-permute-start | bytes 196616 | tf_op jit(solution)/shard_map/ppermute | solution.py:44
  47.2 2.0 %collective-permute-start.26 = (bf16[128,256]{1,0:T(8,128)(2,1)S(1)}, bf16[128,256]{1,0:T(8,128)(2,1)S(1)}, u32[]{:S(2)}, u32[]{:S(2)}) collective-permute-start(bf16[128,256]{1,0:T(8,128)(2,1)S(1)} %get-tuple-element.132.refs_2_.refs_0_), channel_id=1, source_target_pairs={{0,4},{2,6},{4,0},{6,2},{1,5},{3,7},{5,1},{7,3},{8,12},{10,14},{12... | collective-permute-start | bytes 196616 | tf_op jit(solution)/shard_map/ppermute | solution.py:44
  49.2 0.0 collective-permute-done.20.refs_3_
  49.2 0.5 collective-permute-start.25
  49.7 0.6 %collective-permute-done.18.refs_1_ = bf16[96,256]{1,0:T(8,128)(2,1)S(1)} collective-permute-done((bf16[96,256]{1,0:T(8,128)(2,1)S(1)}, bf16[96,256]{1,0:T(8,128)(2,1)S(1)}, u32[]{:S(2)}, u32[]{:S(2)}) %collective-permute-start.18) | collective-permute-done | bytes 49184 | tf_op jit(solution)/shard_map/ppermute | solution.py:44
  50.3 0.0 collective-permute-start.23
  50.3 1.3 %shard_map.208 = (bf16[1152,256]{1,0:T(8,128)(2,1)}, f32[384,256]{1,0:T(8,128)S(1)}) custom-call(bf16[1152,256]{1,0:T(8,128)(2,1)S(1)} %get-tuple-element.86.edge_grads, bf16[1152,256]{1,0:T(8,128)(2,1)S(1)} %get-tuple-element.134.pre_grad, bf16[384,256]{1,0:T(8,128)(2,1)S(1)} %get-tuple-element.135.sender_sum, ...), custom_call_target="tpu_custom_call" | custom-call | flops 251658240 | bytes 3342336 | tf_op jit(solution)/shard_map/pallas_call | solution.py:480
  51.6 1.1 %shard_map.209 = bf16[384,256]{1,0:T(8,128)(2,1)} custom-call(s32[8,32]{1,0:T(8,128)S(1)} %get-tuple-element.133.send_list, f32[384,256]{1,0:T(8,128)S(1)} %get-tuple-element.138.local_grad, bf16[64,256]{1,0:T(8,128)(2,1)S(1)} %get-tuple-element.139.center, bf16[96,256]{1,0:T(8,128)(2,1)S(1)} %collective-permute-done.15.along_core, ...), custom_call_target="tpu_custom_call" | custom-call | flops 50331648 | bytes 721920 | tf_op jit(solution)/shard_map/pallas_call | solution.py:480
  52.8 0.5 collective-permute-start.28
  53.3 0.0 collective-permute-done.26.refs_2_
  53.3 0.1 collective-permute-start.22
  53.4 0.1 collective-permute-done.25.refs_1_
  53.5 0.3 collective-permute-start.31
  53.8 0.0 collective-permute-done.24.refs_7_
  53.8 0.2 collective-permute-start.30
  54.0 0.3 collective-permute-start.29
  54.3 0.5 convert_reduce_fusion
  54.9 0.0 collective-permute-done.22.refs_5_
  54.9 0.8 %shard_map.211 = (bf16[512,256]{1,0:T(8,128)(2,1)}, bf16[256,256]{1,0:T(8,128)(2,1)}) custom-call(bf16[96,256]{1,0:T(8,128)(2,1)S(1)} %shard_map.207.refs_0_, bf16[96,256]{1,0:T(8,128)(2,1)S(1)} %collective-permute-done.18.refs_1_, bf16[96,256]{1,0:T(8,128)(2,1)S(1)} %collective-permute-done.19.refs_2_, bf16[96,256]{1,0:T(8,128)(2,1)S(1)} %collective-permute-done.20.refs_3_, ...), custom_call_target="tpu_custom_call" | custom-call | bytes 786432 | tf_op jit(solution)/shard_map/pallas_call | solution.py:480
  55.7 0.0 collective-permute-done.28.refs_4_
  55.7 0.0 collective-permute-done.30.refs_6_
  55.7 0.0 collective-permute-done.29.refs_5_
  55.7 0.9 %shard_map.210 = (bf16[768,256]{1,0:T(8,128)(2,1)}, bf16[256,256]{1,0:T(8,128)(2,1)}) custom-call(bf16[128,256]{1,0:T(8,128)(2,1)S(1)} %get-tuple-element.132.refs_2_.refs_0_, bf16[128,256]{1,0:T(8,128)(2,1)S(1)} %collective-permute-done.25.refs_1_, bf16[128,256]{1,0:T(8,128)(2,1)S(1)} %collective-permute-done.26.refs_2_, ...), custom_call_target="tpu_custom_call" | custom-call | bytes 1048576 | tf_op jit(solution)/shard_map/pallas_call | solution.py:480
  (20 shorter events, 0.2 us)
Async XLA Ops:
  1.9 7.6 %collective-permute-start = (bf16[96,256]{1,0:T(8,128)(2,1)S(1)}, bf16[96,256]{1,0:T(8,128)(2,1)S(1)}, u32[]{:S(2)}, u32[]{:S(2)}) collective-permute-start(bf16[96,256]{1,0:T(8,128)(2,1)S(1)} %get-tuple-element.89), channel_id=1, source_target_pairs={{0,4},{4,8},{8,12},{12,0},{1,5},{5,9},{9,13},{13,1},{2,6},{6,10},{... | collective-permute-start | bytes 147464 | tf_op jit(solution)/shard_map/ppermute | solution.py:25
  5.0 4.6 %collective-permute-start.1 = (bf16[96,256]{1,0:T(8,128)(2,1)S(1)}, bf16[96,256]{1,0:T(8,128)(2,1)S(1)}, u32[]{:S(2)}, u32[]{:S(2)}) collective-permute-start(bf16[96,256]{1,0:T(8,128)(2,1)S(1)} %get-tuple-element.90), channel_id=1, source_target_pairs={{0,12},{4,0},{8,4},{12,8},{1,13},{5,1},{9,5},{13,9},{2,14},{6,2},{... | collective-permute-start | bytes 147464 | tf_op jit(solution)/shard_map/ppermute | solution.py:25
  9.7 3.6 %collective-permute-start.2 = (bf16[96,256]{1,0:T(8,128)(2,1)S(1)}, bf16[96,256]{1,0:T(8,128)(2,1)S(1)}, u32[]{:S(2)}, u32[]{:S(2)}) collective-permute-start(bf16[96,256]{1,0:T(8,128)(2,1)S(1)} %pad_maximum_fusion), channel_id=1, source_target_pairs={{0,1},{1,2},{2,3},{3,0},{4,5},{5,6},{6,7},{7,4},{8,9},{9,10},{10,1... | collective-permute-start | bytes 147464 | tf_op jit(solution)/shard_map/ppermute | solution.py:25
  9.7 3.6 %collective-permute-start.3 = (bf16[96,256]{1,0:T(8,128)(2,1)S(1)}, bf16[96,256]{1,0:T(8,128)(2,1)S(1)}, u32[]{:S(2)}, u32[]{:S(2)}) collective-permute-start(bf16[96,256]{1,0:T(8,128)(2,1)S(1)} %pad_maximum_fusion.1), channel_id=1, source_target_pairs={{0,3},{1,0},{2,1},{3,2},{4,7},{5,4},{6,5},{7,6},{8,11},{9,8},{10,9... | collective-permute-start | bytes 147464 | tf_op jit(solution)/shard_map/ppermute | solution.py:25
  18.9 2.8 %collective-permute-start.5 = (bf16[528,256]{1,0:T(8,128)(2,1)S(1)}, bf16[528,256]{1,0:T(8,128)(2,1)S(1)}, u32[]{:S(2)}, u32[]{:S(2)}) collective-permute-start(bf16[528,256]{1,0:T(8,128)(2,1)S(1)} %get-tuple-element.110), channel_id=1, source_target_pairs={{0,1},{1,0},{2,3},{3,2},{4,5},{5,4},{6,7},{7,6},{8,9},{9,8},{10,11... | collective-permute-start | bytes 811016 | tf_op jit(solution)/shard_map/ppermute | solution.py:54
  20.6 5.8 %collective-permute-start.4 = (bf16[384,256]{1,0:T(8,128)(2,1)S(1)}, bf16[384,256]{1,0:T(8,128)(2,1)S(1)}, u32[]{:S(2)}, u32[]{:S(2)}) collective-permute-start(bf16[384,256]{1,0:T(8,128)(2,1)S(1)} %get-tuple-element.107), channel_id=1, source_target_pairs={{0,1},{1,0},{2,3},{3,2},{4,5},{5,4},{6,7},{7,6},{8,9},{9,8},{10,11... | collective-permute-start | bytes 589832 | tf_op jit(solution)/shard_map/ppermute | solution.py:54
  21.8 7.4 %collective-permute-start.11 = (bf16[144,256]{1,0:T(8,128)(2,1)S(1)}, bf16[144,256]{1,0:T(8,128)(2,1)S(1)}, u32[]{:S(2)}, u32[]{:S(2)}) collective-permute-start(bf16[144,256]{1,0:T(8,128)(2,1)S(1)} %get-tuple-element.125), channel_id=1, source_target_pairs={{0,2},{2,0},{4,6},{6,4},{1,3},{3,1},{5,7},{7,5},{8,10},{10,8},{12,... | collective-permute-start | bytes 221192 | tf_op jit(solution)/shard_map/ppermute | solution.py:44
  22.4 7.4 %collective-permute-start.12 = (bf16[144,256]{1,0:T(8,128)(2,1)S(1)}, bf16[144,256]{1,0:T(8,128)(2,1)S(1)}, u32[]{:S(2)}, u32[]{:S(2)}) collective-permute-start(bf16[144,256]{1,0:T(8,128)(2,1)S(1)} %get-tuple-element.126), channel_id=1, source_target_pairs={{0,4},{2,6},{4,0},{6,2},{1,5},{3,7},{5,1},{7,3},{8,12},{10,14},{12... | collective-permute-start | bytes 221192 | tf_op jit(solution)/shard_map/ppermute | solution.py:44
  23.4 6.4 %collective-permute-start.13 = (bf16[144,256]{1,0:T(8,128)(2,1)S(1)}, bf16[144,256]{1,0:T(8,128)(2,1)S(1)}, u32[]{:S(2)}, u32[]{:S(2)}) collective-permute-start(bf16[144,256]{1,0:T(8,128)(2,1)S(1)} %get-tuple-element.127), channel_id=1, source_target_pairs={{0,6},{2,4},{4,2},{6,0},{1,7},{3,5},{5,3},{7,1},{8,14},{10,12},{12... | collective-permute-start | bytes 221192 | tf_op jit(solution)/shard_map/ppermute | solution.py:44
  25.4 7.6 %collective-permute-start.9 = (bf16[96,256]{1,0:T(8,128)(2,1)S(1)}, bf16[96,256]{1,0:T(8,128)(2,1)S(1)}, u32[]{:S(2)}, u32[]{:S(2)}) collective-permute-start(bf16[96,256]{1,0:T(8,128)(2,1)S(1)} %get-tuple-element.116), channel_id=1, source_target_pairs={{0,4},{4,8},{8,12},{12,0},{1,5},{5,9},{9,13},{13,1},{2,6},{6,10},{... | collective-permute-start | bytes 147464 | tf_op jit(solution)/shard_map/ppermute | solution.py:25
  26.4 7.5 %collective-permute-start.10 = (bf16[96,256]{1,0:T(8,128)(2,1)S(1)}, bf16[96,256]{1,0:T(8,128)(2,1)S(1)}, u32[]{:S(2)}, u32[]{:S(2)}) collective-permute-start(bf16[96,256]{1,0:T(8,128)(2,1)S(1)} %get-tuple-element.118), channel_id=1, source_target_pairs={{0,12},{4,0},{8,4},{12,8},{1,13},{5,1},{9,5},{13,9},{2,14},{6,2},{... | collective-permute-start | bytes 147464 | tf_op jit(solution)/shard_map/ppermute | solution.py:25
  29.3 4.7 %collective-permute-start.6 = (bf16[96,256]{1,0:T(8,128)(2,1)S(1)}, bf16[96,256]{1,0:T(8,128)(2,1)S(1)}, u32[]{:S(2)}, u32[]{:S(2)}) collective-permute-start(bf16[96,256]{1,0:T(8,128)(2,1)S(1)} %get-tuple-element.113), channel_id=1, source_target_pairs={{0,2},{2,0},{4,6},{6,4},{1,3},{3,1},{5,7},{7,5},{8,10},{10,8},{12,... | collective-permute-start | bytes 147464 | tf_op jit(solution)/shard_map/ppermute | solution.py:44
  29.8 4.2 %collective-permute-start.7 = (bf16[96,256]{1,0:T(8,128)(2,1)S(1)}, bf16[96,256]{1,0:T(8,128)(2,1)S(1)}, u32[]{:S(2)}, u32[]{:S(2)}) collective-permute-start(bf16[96,256]{1,0:T(8,128)(2,1)S(1)} %get-tuple-element.114), channel_id=1, source_target_pairs={{0,4},{2,6},{4,0},{6,2},{1,5},{3,7},{5,1},{7,3},{8,12},{10,14},{12... | collective-permute-start | bytes 147464 | tf_op jit(solution)/shard_map/ppermute | solution.py:44
  29.8 6.4 %collective-permute-start.8 = (bf16[96,256]{1,0:T(8,128)(2,1)S(1)}, bf16[96,256]{1,0:T(8,128)(2,1)S(1)}, u32[]{:S(2)}, u32[]{:S(2)}) collective-permute-start(bf16[96,256]{1,0:T(8,128)(2,1)S(1)} %get-tuple-element.115), channel_id=1, source_target_pairs={{0,6},{2,4},{4,2},{6,0},{1,7},{3,5},{5,3},{7,1},{8,14},{10,12},{12... | collective-permute-start | bytes 147464 | tf_op jit(solution)/shard_map/ppermute | solution.py:44
  33.0 9.2 %collective-permute-start.17 = (bf16[144,256]{1,0:T(8,128)(2,1)S(1)}, bf16[144,256]{1,0:T(8,128)(2,1)S(1)}, u32[]{:S(2)}, u32[]{:S(2)}) collective-permute-start(bf16[144,256]{1,0:T(8,128)(2,1)S(1)} %shard_map.204.refs_4_.refs_0_), channel_id=1, source_target_pairs={{0,8},{8,0},{1,9},{9,1},{2,10},{10,2},{3,11},{11,3},{4,12},{12,4},... | collective-permute-start | bytes 221192 | tf_op jit(solution)/shard_map/ppermute | solution.py:520
  36.2 3.0 %collective-permute-start.15 = (bf16[96,256]{1,0:T(8,128)(2,1)S(1)}, bf16[96,256]{1,0:T(8,128)(2,1)S(1)}, u32[]{:S(2)}, u32[]{:S(2)}) collective-permute-start(bf16[96,256]{1,0:T(8,128)(2,1)S(1)} %get-tuple-element.128), channel_id=1, source_target_pairs={{0,1},{1,0},{2,3},{3,2},{4,5},{5,4},{6,7},{7,6},{8,9},{9,8},{10,11... | collective-permute-start | bytes 147464 | tf_op jit(solution)/shard_map/ppermute | solution.py:54
  36.2 3.5 %collective-permute-start.16 = (bf16[96,256]{1,0:T(8,128)(2,1)S(1)}, bf16[96,256]{1,0:T(8,128)(2,1)S(1)}, u32[]{:S(2)}, u32[]{:S(2)}) collective-permute-start(bf16[96,256]{1,0:T(8,128)(2,1)S(1)} %get-tuple-element.129), channel_id=1, source_target_pairs={{0,3},{1,2},{2,1},{3,0},{4,7},{5,6},{6,5},{7,4},{8,11},{9,10},{10,... | collective-permute-start | bytes 147464 | tf_op jit(solution)/shard_map/ppermute | solution.py:31
  36.6 5.6 %collective-permute-start.14 = (bf16[96,256]{1,0:T(8,128)(2,1)S(1)}, bf16[96,256]{1,0:T(8,128)(2,1)S(1)}, u32[]{:S(2)}, u32[]{:S(2)}) collective-permute-start(bf16[96,256]{1,0:T(8,128)(2,1)S(1)} %shard_map.205.refs_2_.refs_0_), channel_id=1, source_target_pairs={{0,8},{8,0},{1,9},{9,1},{2,10},{10,2},{3,11},{11,3},{4,12},{12,4},... | collective-permute-start | bytes 147464 | tf_op jit(solution)/shard_map/ppermute | solution.py:520
  42.2 4.9 %collective-permute-start.21 = (bf16[96,256]{1,0:T(8,128)(2,1)S(1)}, bf16[96,256]{1,0:T(8,128)(2,1)S(1)}, u32[]{:S(2)}, u32[]{:S(2)}) collective-permute-start(bf16[96,256]{1,0:T(8,128)(2,1)S(1)} %shard_map.207.refs_0_), channel_id=1, source_target_pairs={{0,1},{1,0},{2,3},{3,2},{4,5},{5,4},{6,7},{7,6},{8,9},{9,8},{10,11... | collective-permute-start | bytes 147464 | tf_op jit(solution)/shard_map/ppermute | solution.py:54
  42.3 6.9 %collective-permute-start.20 = (bf16[96,256]{1,0:T(8,128)(2,1)S(1)}, bf16[96,256]{1,0:T(8,128)(2,1)S(1)}, u32[]{:S(2)}, u32[]{:S(2)}) collective-permute-start(bf16[96,256]{1,0:T(8,128)(2,1)S(1)} %shard_map.207.refs_0_), channel_id=1, source_target_pairs={{0,6},{2,4},{4,2},{6,0},{1,7},{3,5},{5,3},{7,1},{8,14},{10,12},{12... | collective-permute-start | bytes 147464 | tf_op jit(solution)/shard_map/ppermute | solution.py:44
  43.7 6.0 %collective-permute-start.19 = (bf16[96,256]{1,0:T(8,128)(2,1)S(1)}, bf16[96,256]{1,0:T(8,128)(2,1)S(1)}, u32[]{:S(2)}, u32[]{:S(2)}) collective-permute-start(bf16[96,256]{1,0:T(8,128)(2,1)S(1)} %shard_map.207.refs_0_), channel_id=1, source_target_pairs={{0,4},{2,6},{4,0},{6,2},{1,5},{3,7},{5,1},{7,3},{8,12},{10,14},{12... | collective-permute-start | bytes 147464 | tf_op jit(solution)/shard_map/ppermute | solution.py:44
  45.7 4.6 %collective-permute-start.18 = (bf16[96,256]{1,0:T(8,128)(2,1)S(1)}, bf16[96,256]{1,0:T(8,128)(2,1)S(1)}, u32[]{:S(2)}, u32[]{:S(2)}) collective-permute-start(bf16[96,256]{1,0:T(8,128)(2,1)S(1)} %shard_map.207.refs_0_), channel_id=1, source_target_pairs={{0,2},{2,0},{4,6},{6,4},{1,3},{3,1},{5,7},{7,5},{8,10},{10,8},{12,... | collective-permute-start | bytes 147464 | tf_op jit(solution)/shard_map/ppermute | solution.py:44
  45.9 6.9 %collective-permute-start.27 = (bf16[128,256]{1,0:T(8,128)(2,1)S(1)}, bf16[128,256]{1,0:T(8,128)(2,1)S(1)}, u32[]{:S(2)}, u32[]{:S(2)}) collective-permute-start(bf16[128,256]{1,0:T(8,128)(2,1)S(1)} %get-tuple-element.132.refs_2_.refs_0_), channel_id=1, source_target_pairs={{0,6},{2,4},{4,2},{6,0},{1,7},{3,5},{5,3},{7,1},{8,14},{10,12},{12... | collective-permute-start | bytes 196616 | tf_op jit(solution)/shard_map/ppermute | solution.py:44
  47.2 6.1 %collective-permute-start.26 = (bf16[128,256]{1,0:T(8,128)(2,1)S(1)}, bf16[128,256]{1,0:T(8,128)(2,1)S(1)}, u32[]{:S(2)}, u32[]{:S(2)}) collective-permute-start(bf16[128,256]{1,0:T(8,128)(2,1)S(1)} %get-tuple-element.132.refs_2_.refs_0_), channel_id=1, source_target_pairs={{0,4},{2,6},{4,0},{6,2},{1,5},{3,7},{5,1},{7,3},{8,12},{10,14},{12... | collective-permute-start | bytes 196616 | tf_op jit(solution)/shard_map/ppermute | solution.py:44
  49.2 4.3 %collective-permute-start.25 = (bf16[128,256]{1,0:T(8,128)(2,1)S(1)}, bf16[128,256]{1,0:T(8,128)(2,1)S(1)}, u32[]{:S(2)}, u32[]{:S(2)}) collective-permute-start(bf16[128,256]{1,0:T(8,128)(2,1)S(1)} %get-tuple-element.132.refs_2_.refs_0_), channel_id=1, source_target_pairs={{0,2},{2,0},{4,6},{6,4},{1,3},{3,1},{5,7},{7,5},{8,10},{10,8},{12,... | collective-permute-start | bytes 196616 | tf_op jit(solution)/shard_map/ppermute | solution.py:44
  49.7 4.1 %collective-permute-start.24 = (bf16[96,256]{1,0:T(8,128)(2,1)S(1)}, bf16[96,256]{1,0:T(8,128)(2,1)S(1)}, u32[]{:S(2)}, u32[]{:S(2)}) collective-permute-start(bf16[96,256]{1,0:T(8,128)(2,1)S(1)} %collective-permute-done.20.refs_3_), channel_id=1, source_target_pairs={{0,1},{1,0},{2,3},{3,2},{4,5},{5,4},{6,7},{7,6},{8,9},{9,8},{10,11... | collective-permute-start | bytes 147464 | tf_op jit(solution)/shard_map/ppermute | solution.py:54
  50.3 3.7 %collective-permute-start.23 = (bf16[96,256]{1,0:T(8,128)(2,1)S(1)}, bf16[96,256]{1,0:T(8,128)(2,1)S(1)}, u32[]{:S(2)}, u32[]{:S(2)}) collective-permute-start(bf16[96,256]{1,0:T(8,128)(2,1)S(1)} %collective-permute-done.19.refs_2_), channel_id=1, source_target_pairs={{0,1},{1,0},{2,3},{3,2},{4,5},{5,4},{6,7},{7,6},{8,9},{9,8},{10,11... | collective-permute-start | bytes 147464 | tf_op jit(solution)/shard_map/ppermute | solution.py:54
  52.8 2.9 %collective-permute-start.28 = (bf16[128,256]{1,0:T(8,128)(2,1)S(1)}, bf16[128,256]{1,0:T(8,128)(2,1)S(1)}, u32[]{:S(2)}, u32[]{:S(2)}) collective-permute-start(bf16[128,256]{1,0:T(8,128)(2,1)S(1)} %get-tuple-element.132.refs_2_.refs_0_), channel_id=1, source_target_pairs={{0,1},{1,0},{2,3},{3,2},{4,5},{5,4},{6,7},{7,6},{8,9},{9,8},{10,11... | collective-permute-start | bytes 196616 | tf_op jit(solution)/shard_map/ppermute | solution.py:54
  53.3 1.6 %collective-permute-start.22 = (bf16[96,256]{1,0:T(8,128)(2,1)S(1)}, bf16[96,256]{1,0:T(8,128)(2,1)S(1)}, u32[]{:S(2)}, u32[]{:S(2)}) collective-permute-start(bf16[96,256]{1,0:T(8,128)(2,1)S(1)} %collective-permute-done.18.refs_1_), channel_id=1, source_target_pairs={{0,1},{1,0},{2,3},{3,2},{4,5},{5,4},{6,7},{7,6},{8,9},{9,8},{10,11... | collective-permute-start | bytes 147464 | tf_op jit(solution)/shard_map/ppermute | solution.py:54
  53.5 2.2 %collective-permute-start.31 = (bf16[128,256]{1,0:T(8,128)(2,1)S(1)}, bf16[128,256]{1,0:T(8,128)(2,1)S(1)}, u32[]{:S(2)}, u32[]{:S(2)}) collective-permute-start(bf16[128,256]{1,0:T(8,128)(2,1)S(1)} %collective-permute-done.27.refs_3_), channel_id=1, source_target_pairs={{0,1},{1,0},{2,3},{3,2},{4,5},{5,4},{6,7},{7,6},{8,9},{9,8},{10,11... | collective-permute-start | bytes 196616 | tf_op jit(solution)/shard_map/ppermute | solution.py:54
  53.8 1.9 %collective-permute-start.30 = (bf16[128,256]{1,0:T(8,128)(2,1)S(1)}, bf16[128,256]{1,0:T(8,128)(2,1)S(1)}, u32[]{:S(2)}, u32[]{:S(2)}) collective-permute-start(bf16[128,256]{1,0:T(8,128)(2,1)S(1)} %collective-permute-done.26.refs_2_), channel_id=1, source_target_pairs={{0,1},{1,0},{2,3},{3,2},{4,5},{5,4},{6,7},{7,6},{8,9},{9,8},{10,11... | collective-permute-start | bytes 196616 | tf_op jit(solution)/shard_map/ppermute | solution.py:54
  54.0 1.7 %collective-permute-start.29 = (bf16[128,256]{1,0:T(8,128)(2,1)S(1)}, bf16[128,256]{1,0:T(8,128)(2,1)S(1)}, u32[]{:S(2)}, u32[]{:S(2)}) collective-permute-start(bf16[128,256]{1,0:T(8,128)(2,1)S(1)} %collective-permute-done.25.refs_1_), channel_id=1, source_target_pairs={{0,1},{1,0},{2,3},{3,2},{4,5},{5,4},{6,7},{7,6},{8,9},{9,8},{10,11... | collective-permute-start | bytes 196616 | tf_op jit(solution)/shard_map/ppermute | solution.py:54

commit v14 on v12

--- a/solution.py
+++ b/solution.py
@@ -238,8 +238,9 @@
     sender_out,
     receiver_out,
     node_part_out,
-    across_out,
-    rest_out,
+    top_out,
+    middle_out,
+    bottom_out,
     keep_out,
     away_out,
     gains_out,
@@ -313,23 +314,9 @@
     sender_out[...] = own
     receiver_out[...] = received
     halo_grad = dot_nt(away, w_in[width : 2 * width]).astype(BF16)
-    parts = [halo_grad[k * slots : (k + 1) * slots] for k in range(8)]
-    up = jnp.concatenate([parts[0], parts[3], parts[5]], axis=0)
-    down = jnp.concatenate([parts[2], parts[4], parts[7]], axis=0)
-    core = lax.axis_index(CORE)
-    sums_rows = gains_out.shape[0] + keep_out.shape[0]
-
-    @pl.when(core == 0)
-    def _():
-        away_out[sums_rows:] = up
-        across_out[...] = down
-
-    @pl.when(core == 1)
-    def _():
-        away_out[sums_rows:] = down
-        across_out[...] = up
-
-    rest_out[...] = jnp.concatenate([parts[1], parts[6]], axis=0)
+    top_out[...] = halo_grad[: 3 * slots]
+    middle_out[...] = halo_grad[3 * slots : 5 * slots]
+    bottom_out[...] = halo_grad[5 * slots :]
     edge_sums[:width] = dot_tn(edges[...], pre_grad)
     edge_sums[width : 2 * width] = dot_tn(x, own) + dot_tn(halo, away)
     edge_sums[2 * width : 3 * width] = dot_tn(x, received)
@@ -337,7 +324,7 @@
     split_by_core(edge_sums, 0, keep_out, away_out)
     split_by_core(node_sums, edge_sums.shape[0] // 2, keep_out, away_out)
     gains = pack_gains(edge_gain, node_gain)
-    away_out[keep_out.shape[0] : sums_rows] = gains
+    away_out[keep_out.shape[0] :] = gains
     gains_out[...] = gains
 
 
@@ -427,52 +414,61 @@
     )
 
 
-def turn_kernel(other, across, rest, high, low, middle):
-    slots = rest.shape[0] // 2
-    first = other.shape[0] - 3 * slots
-
-    def turn(up_back, down_back):
-        high[:slots] = up_back[:slots]
-        high[slots : 2 * slots] = down_back[:slots]
-        high[2 * slots :] = rest[:slots]
-        low[:slots] = up_back[2 * slots :]
-        low[slots : 2 * slots] = down_back[2 * slots :]
-        low[2 * slots :] = rest[slots:]
-        middle[:slots] = up_back[slots : 2 * slots]
-        middle[slots:] = down_back[slots : 2 * slots]
+def turn_kernel(top, middle, bottom, along_core, along_chip, center):
+    slots = middle.shape[0] // 2
+
+    def turn(up, down):
+        up[:slots] = top[:slots]
+        up[slots : 2 * slots] = middle[:slots]
+        up[2 * slots :] = bottom[:slots]
+        down[:slots] = top[2 * slots :]
+        down[slots : 2 * slots] = middle[slots:]
+        down[2 * slots :] = bottom[2 * slots :]
 
     core = lax.axis_index(CORE)
 
     @pl.when(core == 0)
     def _():
-        turn(across, other.at[first:])
+        turn(along_core, along_chip)
 
     @pl.when(core == 1)
     def _():
-        turn(other.at[first:], across)
-
-
-def return_kernel(send_list, local_grad, middle, to_high, to_low, nodes_grad):
+        turn(along_chip, along_core)
+
+    center[:slots] = top[slots : 2 * slots]
+    center[slots:] = bottom[slots : 2 * slots]
+
+
+def return_kernel(send_list, local_grad, center, along_core, along_chip, nodes_grad, returned):
     slots = send_list.shape[1]
 
-    def block(ref, k):
-        return ref[k * slots : (k + 1) * slots]
-
-    returned = jnp.concatenate(
-        [
-            block(to_high, 0),
-            block(to_high, 2),
-            block(to_high, 1),
-            block(middle, 0),
-            block(middle, 1),
-            block(to_low, 0),
-            block(to_low, 2),
-            block(to_low, 1),
-        ],
-        axis=0,
-    )
+    def fill(up, down):
+        for k, (source, i) in enumerate(
+            [
+                (up, 0),
+                (center, 0),
+                (down, 0),
+                (up, 1),
+                (down, 1),
+                (up, 2),
+                (center, 1),
+                (down, 2),
+            ]
+        ):
+            returned[k * slots : (k + 1) * slots] = source[i * slots : (i + 1) * slots]
+
+    core = lax.axis_index(CORE)
+
+    @pl.when(core == 0)
+    def _():
+        fill(along_chip, along_core)
+
+    @pl.when(core == 1)
+    def _():
+        fill(along_core, along_chip)
+
     hot = list_hot(send_list[...], local_grad.shape[0])
-    nodes_grad[...] = (local_grad[...] + dot_tn(hot, returned)).astype(BF16)
+    nodes_grad[...] = (local_grad[...] + dot_tn(hot, returned[...])).astype(BF16)
 
 
 SMEM = pltpu.SMEM
@@ -647,7 +643,7 @@
     )
     parts = (2 * width, 3 * width // 2)
     halves = sum(parts)
-    pre_grad, sender_sum, receiver_sum, node_part, across, rest, keep, away, gains = call(
+    pre_grad, sender_sum, receiver_sum, node_part, top, middle, bottom, keep, away, gains = call(
         functools.partial(layer_kernel, tile_rows),
         [
             shaped(edge_rows, width, BF16),
@@ -656,8 +652,9 @@
             shaped(count, width, F32),
             shaped(3 * slots, width, BF16),
             shaped(2 * slots, width, BF16),
+            shaped(3 * slots, width, BF16),
             shaped(halves, width, F32),
-            shaped(halves + 16 + 3 * slots, width, BF16),
+            shaped(halves + 16, width, BF16),
             shaped(16, width, BF16),
         ],
         square * (6 * edge_rows + 11 * count + 2 * halo_rows)
@@ -703,7 +700,7 @@
         other,
     )
     received = [in_square(block, offset) for offset, block in enumerate(blocks, 1)]
-    high, low, middle = call(
+    along_core, along_chip, center = call(
         turn_kernel,
         [
             shaped(3 * slots, width, BF16),
@@ -711,17 +708,20 @@
             shaped(2 * slots, width, BF16),
         ],
         10**10,
-        other,
-        across_chips(across),
-        rest,
-    )
-    *received, high, low = lax.optimization_barrier((*received, high, low))
+        passed_along(top, PX, 1),
+        middle,
+        passed_along(bottom, PX, -1),
+    )
+    *received, along_core, along_chip = lax.optimization_barrier(
+        (*received, along_core, along_chip)
+    )
     (sums,) = call(sum_kernel, [like(own)], 0, own, *received)
-    gains, mine, to_high, to_low = joined(
-        sums, gains.shape[0], passed_along(high, PX, 1), passed_along(low, PX, -1)
+    gains, mine, along_core, along_chip = joined(
+        sums, gains.shape[0], across_cores(along_core), across_chips(along_chip)
     )
     blocks = [mine] + [in_square(mine, offset) for offset in range(1, members)]
-    blocks += [across_cores(block) for block in blocks]
+    gain_edge_grad = (gains[0] + gains[1]).astype(BF16)
+    gain_node_grad = (gains[2] + gains[3]).astype(BF16)
     edges_grad, local_grad = call(
         finish_kernel,
         [shaped(edge_rows, width, BF16), shaped(count, width, F32)],
@@ -739,11 +739,16 @@
         2 * halo_rows * count * width,
         send_list,
         local_grad,
-        middle,
-        to_high,
-        to_low,
-    )
-    *blocks, nodes_grad, edges_grad = lax.optimization_barrier((*blocks, nodes_grad, edges_grad))
+        center,
+        along_core,
+        along_chip,
+        scratch=[pltpu.VMEM((halo_rows, width), BF16)],
+    )
+    done = (nodes_grad, edges_grad, gain_edge_grad, gain_node_grad)
+    for i in range(members):
+        blocks[i], *done = lax.optimization_barrier((blocks[i], *done))
+    nodes_grad, edges_grad, gain_edge_grad, gain_node_grad = done
+    blocks += [across_cores(block) for block in blocks]
     w_edge_in_grad, w_edge_out_grad, w_node_in_grad, w_node_out_grad = placed(
         parts, blocks, width
     )
@@ -752,10 +757,10 @@
         edges_grad,
         w_edge_in_grad,
         w_edge_out_grad,
-        (gains[0] + gains[1]).astype(BF16),
+        gain_edge_grad,
         w_node_in_grad,
         w_node_out_grad,
-        (gains[2] + gains[3]).astype(BF16),
+        gain_node_grad,
     )
 
 

time: 52.4 us -> 50.5 us (0.964)
  waiting for transfers between devices: 13 us -> 12.2 us
  starting transfers between devices: 22.5 us -> 21.9 us
    ppermute x6, waiting for transfers between devices: 3.26 us -> 0.12 us  [passed_along(): lax.ppermute(array, axis, [(i, (i + by) % size) for i in range(size)])]
    ppermute x1, waiting for transfers between devices: 0.35 us -> 2.76 us  [joined(): other = lax.ppermute(sums, FAR, [(i, i ^ distance) for i in range(size)])]
    ppermute x1, starting transfers between devices: 2.33 us -> 0.83 us  [joined(): other = lax.ppermute(sums, FAR, [(i, i ^ distance) for i in range(size)])]
    ppermute x1, waiting for transfers between devices: 0.01 us -> 1.18 us  [across_chips(): return lax.ppermute(array, PY, pairs)]
    ppermute x6, waiting for transfers between devices: 7.99 us -> 6.84 us  [in_square(): lax.ppermute(array, SQUARE, [(i, i ^ offset) for i in range(square_member...]
    ppermute x1, starting transfers between devices: 0.14 us -> 1.02 us  [across_chips(): return lax.ppermute(array, PY, pairs)]
    ppermute x5 -> x6, waiting for transfers between devices: 1.39 us -> 1.32 us  [across_cores(): return lax.ppermute(array, CORE, [(0, 1), (1, 0)])]
    ppermute x5 -> x6, starting transfers between devices: 2.18 us -> 2.16 us  [across_cores(): return lax.ppermute(array, CORE, [(0, 1), (1, 0)])]
  transfers between devices with their start and end apart: 19 -> 20, of which waited for: 10 -> 9; matrix products, arithmetic and copies ran while one was open for 1% -> 1% of each run, Pallas kernels for 12% -> 12%
where the time goes in v14:
time: 50.5 us; the launch traced here: 50.3 us
  starting transfers between devices  21.9 us (43%)
  Pallas kernels  14.2 us (28%)
  waiting for transfers between devices  12.2 us (24%)
  between operations  1.39 us (3%)
  other arithmetic  0.55 us (1%)
    pallas_call x11, Pallas kernels, call(): pl.pallas_call(body, out_shape=outs, in_specs=[pl.BlockSpec(memory_space=...  14.2 us
    ppermute x6, starting transfers between devices, passed_along(): lax.ppermute(array, axis, [(i, (i + by) % size) for i in range(size)])  10.8 us
    ppermute x6, starting transfers between devices, in_square(): lax.ppermute(array, SQUARE, [(i, i ^ offset) for i in range(square_member...  7.11 us
    ppermute x6, waiting for transfers between devices, in_square(): lax.ppermute(array, SQUARE, [(i, i ^ offset) for i in range(square_member...  6.84 us
    ppermute x1, waiting for transfers between devices, joined(): other = lax.ppermute(sums, FAR, [(i, i ^ distance) for i in range(size)])  2.76 us
    ppermute x6, starting transfers between devices, across_cores(): return lax.ppermute(array, CORE, [(0, 1), (1, 0)])  2.16 us
    ppermute x6, waiting for transfers between devices, across_cores(): return lax.ppermute(array, CORE, [(0, 1), (1, 0)])  1.32 us
    ppermute x1, waiting for transfers between devices, across_chips(): return lax.ppermute(array, PY, pairs)  1.18 us
  transfers between devices with their start and end apart: 20, of which 9 were waited for; matrix products, arithmetic and copies ran while one was open for 1% of the time, Pallas kernels for 12%

profile of v14, /device:TPU:0, one launch (start us, length us, event | category | flops | bytes accessed | tf_op | source)
XLA Modules:
  0.0 50.3 jit_solution(2777985710625776726)
XLA Ops:
  0.6 1.3 %shard_map.197 = (bf16[96,256]{1,0:T(8,128)(2,1)S(1)}, bf16[64,256]{1,0:T(8,128)(2,1)S(1)}, bf16[96,256]{1,0:T(8,128)(2,1)S(1)}, bf16[384,256]{1,0:T(8,128)(2,1)S(1)}, s32[8,32]{1,0:T(8,128)S(1)}) custom-call(bf16[384,256]{1,0:T(8,128)(2,1)} %nodes_hbm.1, s32[8,32]{1,0:T(8,128)} %list_hbm.1), custom_call_target="tpu_custom_call" | custom-call | flops 50331648 | bytes 526336 | tf_op jit(solution)/shard_map/pallas_call | solution.py:488
  1.9 3.1 %collective-permute-start = (bf16[96,256]{1,0:T(8,128)(2,1)S(1)}, bf16[96,256]{1,0:T(8,128)(2,1)S(1)}, u32[]{:S(2)}, u32[]{:S(2)}) collective-permute-start(bf16[96,256]{1,0:T(8,128)(2,1)S(1)} %get-tuple-element.91), channel_id=1, source_target_pairs={{0,4},{4,8},{8,12},{12,0},{1,5},{5,9},{9,13},{13,1},{2,6},{6,10},{... | collective-permute-start | bytes 147464 | tf_op jit(solution)/shard_map/ppermute | solution.py:25
  5.0 2.1 %collective-permute-start.1 = (bf16[96,256]{1,0:T(8,128)(2,1)S(1)}, bf16[96,256]{1,0:T(8,128)(2,1)S(1)}, u32[]{:S(2)}, u32[]{:S(2)}) collective-permute-start(bf16[96,256]{1,0:T(8,128)(2,1)S(1)} %get-tuple-element.92), channel_id=1, source_target_pairs={{0,12},{4,0},{8,4},{12,8},{1,13},{5,1},{9,5},{13,9},{2,14},{6,2},{... | collective-permute-start | bytes 147464 | tf_op jit(solution)/shard_map/ppermute | solution.py:25
  7.8 1.7 %shard_map.198 = (bf16[1152,768]{1,0:T(8,128)(2,1)S(1)}, bf16[1152,256]{1,0:T(8,128)(2,1)S(1)}, s32[9,128]{1,0:T(8,128)S(1)}, s32[9,128]{1,0:T(8,128)S(1)}, bf16...) custom-call(s32[9,128]{1,0:T(8,128)} %refs_0_.1, ...), custom_call_target="tpu_custom_call" | custom-call | bytes 6967296 | tf_op jit(solution)/shard_map/pallas_call | solution.py:488
  9.5 0.0 collective-permute-done.from_low
  9.5 0.1 collective-permute-done.1.from_high
  9.7 0.1 collective-permute-start.2
  9.7 1.7 %collective-permute-start.3 = (bf16[96,256]{1,0:T(8,128)(2,1)S(1)}, bf16[96,256]{1,0:T(8,128)(2,1)S(1)}, u32[]{:S(2)}, u32[]{:S(2)}) collective-permute-start(bf16[96,256]{1,0:T(8,128)(2,1)S(1)} %pad_maximum_fusion.1), channel_id=1, source_target_pairs={{0,3},{1,0},{2,1},{3,2},{4,7},{5,4},{6,5},{7,6},{8,11},{9,8},{10,9... | collective-permute-start | bytes 147464 | tf_op jit(solution)/shard_map/ppermute | solution.py:25
  11.5 1.8 %shard_map.199 = (f32[1152,256]{1,0:T(8,128)S(1)}, bf16[640,1152]{1,0:T(8,128)(2,1)S(1)}, bf16[384,1152]{1,0:T(8,128)(2,1)S(1)}) custom-call(bf16[384,256]{1,0:T(8,128)(2,1)S(1)} %get-tuple-element.85.nodes, bf16[1152,256]{1,0:T(8,128)(2,1)S(1)} %get-tuple-element.87.edges, s32[9,128]{1,0:T(8,128)S(1)} %get-tuple-element.89.senders, ...), custom_call_target="tpu_custom_call" | custom-call | flops 704643072 | bytes 6497280 | tf_op jit(solution)/shard_map/pallas_call | solution.py:488
  13.3 0.0 collective-permute-done.2.upward
  13.3 0.0 collective-permute-done.3.downward
  13.3 5.6 %shard_map.200 = (bf16[1152,256]{1,0:T(8,128)(2,1)S(1)}, bf16[384,256]{1,0:T(8,128)(2,1)S(1)}, bf16[384,256]{1,0:T(8,128)(2,1)S(1)}, f32[384,256]{1,0:T(8,128)S(...) custom-call(s32[1]{0:T(128)S(6)} %copy.22.count_ref, ...), custom_call_target="tpu_custom_call" | custom-call | flops 2583691264 | bytes 11486212 | tf_op jit(solution)/shard_map/pallas_call | solution.py:488
  19.0 1.6 %collective-permute-start.4 = (bf16[912,256]{1,0:T(8,128)(2,1)S(1)}, bf16[912,256]{1,0:T(8,128)(2,1)S(1)}, u32[]{:S(2)}, u32[]{:S(2)}) collective-permute-start(bf16[912,256]{1,0:T(8,128)(2,1)S(1)} %get-tuple-element.110), channel_id=1, source_target_pairs={{0,1},{1,0},{2,3},{3,2},{4,5},{5,4},{6,7},{7,6},{8,9},{9,8},{10,11... | collective-permute-start | bytes 1400840 | tf_op jit(solution)/shard_map/ppermute | solution.py:54
  20.6 1.0 %collective-permute-start.8 = (bf16[96,256]{1,0:T(8,128)(2,1)S(1)}, bf16[96,256]{1,0:T(8,128)(2,1)S(1)}, u32[]{:S(2)}, u32[]{:S(2)}) collective-permute-start(bf16[96,256]{1,0:T(8,128)(2,1)S(1)} %get-tuple-element.115), channel_id=1, source_target_pairs={{0,4},{4,8},{8,12},{12,0},{1,5},{5,9},{9,13},{13,1},{2,6},{6,10},{... | collective-permute-start | bytes 147464 | tf_op jit(solution)/shard_map/ppermute | solution.py:25
  21.6 2.8 %collective-permute-start.9 = (bf16[96,256]{1,0:T(8,128)(2,1)S(1)}, bf16[96,256]{1,0:T(8,128)(2,1)S(1)}, u32[]{:S(2)}, u32[]{:S(2)}) collective-permute-start(bf16[96,256]{1,0:T(8,128)(2,1)S(1)} %get-tuple-element.117), channel_id=1, source_target_pairs={{0,12},{4,0},{8,4},{12,8},{1,13},{5,1},{9,5},{13,9},{2,14},{6,2},{... | collective-permute-start | bytes 147464 | tf_op jit(solution)/shard_map/ppermute | solution.py:25
  24.4 0.0 collective-permute-done.4.other
  24.4 0.1 shard_map.201
  24.5 0.5 %collective-permute-start.5 = (bf16[240,256]{1,0:T(8,128)(2,1)S(1)}, bf16[240,256]{1,0:T(8,128)(2,1)S(1)}, u32[]{:S(2)}, u32[]{:S(2)}) collective-permute-start(bf16[240,256]{1,0:T(8,128)(2,1)S(1)} %get-tuple-element.112), channel_id=1, source_target_pairs={{0,2},{2,0},{4,6},{6,4},{1,3},{3,1},{5,7},{7,5},{8,10},{10,8},{12,... | collective-permute-start | bytes 368648 | tf_op jit(solution)/shard_map/ppermute | solution.py:44
  25.1 0.0 collective-permute-start.6
  25.1 3.0 %collective-permute-start.7 = (bf16[240,256]{1,0:T(8,128)(2,1)S(1)}, bf16[240,256]{1,0:T(8,128)(2,1)S(1)}, u32[]{:S(2)}, u32[]{:S(2)}) collective-permute-start(bf16[240,256]{1,0:T(8,128)(2,1)S(1)} %get-tuple-element.114), channel_id=1, source_target_pairs={{0,6},{2,4},{4,2},{6,0},{1,7},{3,5},{5,3},{7,1},{8,14},{10,12},{12... | collective-permute-start | bytes 368648 | tf_op jit(solution)/shard_map/ppermute | solution.py:44
  28.1 0.0 collective-permute-done.8.top
  28.1 0.0 collective-permute-done.9.bottom
  28.1 2.1 %collective-permute-done.5.refs_1_ = bf16[240,256]{1,0:T(8,128)(2,1)S(1)} collective-permute-done((bf16[240,256]{1,0:T(8,128)(2,1)S(1)}, bf16[240,256]{1,0:T(8,128)(2,1)S(1)}, u32[]{:S(2)}, u32[]{:S(2)}) %collective-permute-start.5) | collective-permute-done | bytes 122912 | tf_op jit(solution)/shard_map/ppermute | solution.py:44
  30.3 0.6 %collective-permute-done.6.refs_2_ = bf16[240,256]{1,0:T(8,128)(2,1)S(1)} collective-permute-done((bf16[240,256]{1,0:T(8,128)(2,1)S(1)}, bf16[240,256]{1,0:T(8,128)(2,1)S(1)}, u32[]{:S(2)}, u32[]{:S(2)}) %collective-permute-start.6) | collective-permute-done | bytes 122912 | tf_op jit(solution)/shard_map/ppermute | solution.py:44
  30.8 2.3 %collective-permute-done.7.refs_3_ = bf16[240,256]{1,0:T(8,128)(2,1)S(1)} collective-permute-done((bf16[240,256]{1,0:T(8,128)(2,1)S(1)}, bf16[240,256]{1,0:T(8,128)(2,1)S(1)}, u32[]{:S(2)}, u32[]{:S(2)}) %collective-permute-start.7) | collective-permute-done | bytes 122912 | tf_op jit(solution)/shard_map/ppermute | solution.py:44
  33.2 0.1 shard_map.203.own
  33.2 0.8 %collective-permute-start.10 = (bf16[240,256]{1,0:T(8,128)(2,1)S(1)}, bf16[240,256]{1,0:T(8,128)(2,1)S(1)}, u32[]{:S(2)}, u32[]{:S(2)}) collective-permute-start(bf16[240,256]{1,0:T(8,128)(2,1)S(1)} %shard_map.203.own), channel_id=1, source_target_pairs={{0,8},{8,0},{1,9},{9,1},{2,10},{10,2},{3,11},{11,3},{4,12},{12,4},... | collective-permute-start | bytes 368648 | tf_op jit(solution)/shard_map/ppermute | solution.py:529
  34.1 0.0 collective-permute-start.11
  34.1 1.0 %collective-permute-start.12 = (bf16[96,256]{1,0:T(8,128)(2,1)S(1)}, bf16[96,256]{1,0:T(8,128)(2,1)S(1)}, u32[]{:S(2)}, u32[]{:S(2)}) collective-permute-start(bf16[96,256]{1,0:T(8,128)(2,1)S(1)} %get-tuple-element.124), channel_id=1, source_target_pairs={{0,3},{1,2},{2,1},{3,0},{4,7},{5,6},{6,5},{7,4},{8,11},{9,10},{10,... | collective-permute-start | bytes 147464 | tf_op jit(solution)/shard_map/ppermute | solution.py:31
  35.1 1.3 %shard_map.205 = (bf16[1152,256]{1,0:T(8,128)(2,1)}, f32[384,256]{1,0:T(8,128)S(1)}) custom-call(bf16[1152,256]{1,0:T(8,128)(2,1)S(1)} %get-tuple-element.88.edge_grads, bf16[1152,256]{1,0:T(8,128)(2,1)S(1)} %get-tuple-element.128.pre_grad, bf16[384,256]{1,0:T(8,128)(2,1)S(1)} %get-tuple-element.129.sender_sum, ...), custom_call_target="tpu_custom_call" | custom-call | flops 251658240 | bytes 3342336 | tf_op jit(solution)/shard_map/pallas_call | solution.py:488
  36.4 0.0 collective-permute-done.11.along_core
  36.4 1.2 %collective-permute-done.12.along_chip = bf16[96,256]{1,0:T(8,128)(2,1)S(1)} collective-permute-done((bf16[96,256]{1,0:T(8,128)(2,1)S(1)}, bf16[96,256]{1,0:T(8,128)(2,1)S(1)}, u32[]{:S(2)}, u32[]{:S(2)}) %collective-permute-start.12) | collective-permute-done | bytes 49184 | tf_op jit(solution)/shard_map/ppermute | solution.py:31
  37.6 2.8 %collective-permute-done.10.other = bf16[240,256]{1,0:T(8,128)(2,1)S(1)} collective-permute-done((bf16[240,256]{1,0:T(8,128)(2,1)S(1)}, bf16[240,256]{1,0:T(8,128)(2,1)S(1)}, u32[]{:S(2)}, u32[]{:S(2)}) %collective-permute-start.10) | collective-permute-done | bytes 122912 | tf_op jit(solution)/shard_map/ppermute | solution.py:529
  40.4 0.6 %collective-permute-start.15 = (bf16[224,256]{1,0:T(8,128)(2,1)S(1)}, bf16[224,256]{1,0:T(8,128)(2,1)S(1)}, u32[]{:S(2)}, u32[]{:S(2)}) collective-permute-start(bf16[224,256]{1,0:T(8,128)(2,1)S(1)} %get-tuple-element.152.refs_0_), channel_id=1, source_target_pairs={{0,2},{2,0},{4,6},{6,4},{1,3},{3,1},{5,7},{7,5},{8,10},{10,8},{12,... | collective-permute-start | bytes 344072 | tf_op jit(solution)/shard_map/ppermute | solution.py:44
  41.0 0.0 collective-permute-start.14
  41.0 3.0 %collective-permute-start.13 = (bf16[224,256]{1,0:T(8,128)(2,1)S(1)}, bf16[224,256]{1,0:T(8,128)(2,1)S(1)}, u32[]{:S(2)}, u32[]{:S(2)}) collective-permute-start(bf16[224,256]{1,0:T(8,128)(2,1)S(1)} %get-tuple-element.152.refs_0_), channel_id=1, source_target_pairs={{0,6},{2,4},{4,2},{6,0},{1,7},{3,5},{5,3},{7,1},{8,14},{10,12},{12... | collective-permute-start | bytes 344072 | tf_op jit(solution)/shard_map/ppermute | solution.py:44
  43.9 1.1 %shard_map.206 = bf16[384,256]{1,0:T(8,128)(2,1)} custom-call(s32[8,32]{1,0:T(8,128)S(1)} %get-tuple-element.127.send_list, f32[384,256]{1,0:T(8,128)S(1)} %get-tuple-element.132.local_grad, bf16[64,256]{1,0:T(8,128)(2,1)S(1)} %get-tuple-element.133.center, bf16[96,256]{1,0:T(8,128)(2,1)S(1)} %collective-permute-done.11.along_core, ...), custom_call_target="tpu_custom_call" | custom-call | flops 50331648 | bytes 721920 | tf_op jit(solution)/shard_map/pallas_call | solution.py:488
  45.1 0.5 %convert_reduce_fusion = (bf16[256]{0:T(256)(128)(2,1)}, bf16[256]{0:T(256)(128)(2,1)}) fusion(f32[16,256]{1,0:T(8,128)S(1)} %get-tuple-element.137), kind=kLoop, calls=%fused_computation.2 | loop fusion | flops 1024 | bytes 5120 | tf_op jit(solution)/shard_map/convert_element_type | solution.py:724
  45.6 0.0 collective-permute-start.16
  45.6 0.9 %collective-permute-done.15.refs_1_ = bf16[224,256]{1,0:T(8,128)(2,1)S(1)} collective-permute-done((bf16[224,256]{1,0:T(8,128)(2,1)S(1)}, bf16[224,256]{1,0:T(8,128)(2,1)S(1)}, u32[]{:S(2)}, u32[]{:S(2)}) %collective-permute-start.15) | collective-permute-done | bytes 114720 | tf_op jit(solution)/shard_map/ppermute | solution.py:44
  46.5 0.0 collective-permute-start.17
  46.5 0.0 collective-permute-done.14.refs_2_
  46.5 0.5 %collective-permute-start.18 = (bf16[224,256]{1,0:T(8,128)(2,1)S(1)}, bf16[224,256]{1,0:T(8,128)(2,1)S(1)}, u32[]{:S(2)}, u32[]{:S(2)}) collective-permute-start(bf16[224,256]{1,0:T(8,128)(2,1)S(1)} %collective-permute-done.14.refs_2_), channel_id=1, source_target_pairs={{0,1},{1,0},{2,3},{3,2},{4,5},{5,4},{6,7},{7,6},{8,9},{9,8},{10,11... | collective-permute-start | bytes 344072 | tf_op jit(solution)/shard_map/ppermute | solution.py:54
  47.0 0.9 %collective-permute-done.13.refs_3_ = bf16[224,256]{1,0:T(8,128)(2,1)S(1)} collective-permute-done((bf16[224,256]{1,0:T(8,128)(2,1)S(1)}, bf16[224,256]{1,0:T(8,128)(2,1)S(1)}, u32[]{:S(2)}, u32[]{:S(2)}) %collective-permute-start.13) | collective-permute-done | bytes 114720 | tf_op jit(solution)/shard_map/ppermute | solution.py:44
  47.9 0.0 collective-permute-start.19
  47.9 0.0 collective-permute-done.16.refs_4_
  47.9 0.0 collective-permute-done.17.refs_5_
  47.9 0.0 collective-permute-done.18.refs_6_
  48.0 1.3 %collective-permute-done.19.refs_7_ = bf16[224,256]{1,0:T(8,128)(2,1)S(1)} collective-permute-done((bf16[224,256]{1,0:T(8,128)(2,1)S(1)}, bf16[224,256]{1,0:T(8,128)(2,1)S(1)}, u32[]{:S(2)}, u32[]{:S(2)}) %collective-permute-start.19) | collective-permute-done | bytes 114720 | tf_op jit(solution)/shard_map/ppermute | solution.py:54
  49.3 1.0 %shard_map.207 = (bf16[768,256]{1,0:T(8,128)(2,1)}, bf16[256,256]{1,0:T(8,128)(2,1)}, bf16[512,256]{1,0:T(8,128)(2,1)}, bf16[256,256]{1,0:T(8,128)(2,1)}) custom-call(bf16[224,256]{1,0:T(8,128)(2,1)S(1)} %get-tuple-element.152.refs_0_, bf16[224,256]{1,0:T(8,128)(2,1)S(1)} %collective-permute-done.15.refs_1_, ...), custom_call_target="tpu_custom_call" | custom-call | bytes 1835008 | tf_op jit(solution)/shard_map/pallas_call | solution.py:488
  (6 shorter events, 0.1 us)
Async XLA Ops:
  1.9 7.6 %collective-permute-start = (bf16[96,256]{1,0:T(8,128)(2,1)S(1)}, bf16[96,256]{1,0:T(8,128)(2,1)S(1)}, u32[]{:S(2)}, u32[]{:S(2)}) collective-permute-start(bf16[96,256]{1,0:T(8,128)(2,1)S(1)} %get-tuple-element.91), channel_id=1, source_target_pairs={{0,4},{4,8},{8,12},{12,0},{1,5},{5,9},{9,13},{13,1},{2,6},{6,10},{... | collective-permute-start | bytes 147464 | tf_op jit(solution)/shard_map/ppermute | solution.py:25
  5.0 4.6 %collective-permute-start.1 = (bf16[96,256]{1,0:T(8,128)(2,1)S(1)}, bf16[96,256]{1,0:T(8,128)(2,1)S(1)}, u32[]{:S(2)}, u32[]{:S(2)}) collective-permute-start(bf16[96,256]{1,0:T(8,128)(2,1)S(1)} %get-tuple-element.92), channel_id=1, source_target_pairs={{0,12},{4,0},{8,4},{12,8},{1,13},{5,1},{9,5},{13,9},{2,14},{6,2},{... | collective-permute-start | bytes 147464 | tf_op jit(solution)/shard_map/ppermute | solution.py:25
  9.7 3.6 %collective-permute-start.2 = (bf16[96,256]{1,0:T(8,128)(2,1)S(1)}, bf16[96,256]{1,0:T(8,128)(2,1)S(1)}, u32[]{:S(2)}, u32[]{:S(2)}) collective-permute-start(bf16[96,256]{1,0:T(8,128)(2,1)S(1)} %pad_maximum_fusion), channel_id=1, source_target_pairs={{0,1},{1,2},{2,3},{3,0},{4,5},{5,6},{6,7},{7,4},{8,9},{9,10},{10,1... | collective-permute-start | bytes 147464 | tf_op jit(solution)/shard_map/ppermute | solution.py:25
  9.7 3.6 %collective-permute-start.3 = (bf16[96,256]{1,0:T(8,128)(2,1)S(1)}, bf16[96,256]{1,0:T(8,128)(2,1)S(1)}, u32[]{:S(2)}, u32[]{:S(2)}) collective-permute-start(bf16[96,256]{1,0:T(8,128)(2,1)S(1)} %pad_maximum_fusion.1), channel_id=1, source_target_pairs={{0,3},{1,0},{2,1},{3,2},{4,7},{5,4},{6,5},{7,6},{8,11},{9,8},{10,9... | collective-permute-start | bytes 147464 | tf_op jit(solution)/shard_map/ppermute | solution.py:25
  19.0 5.5 %collective-permute-start.4 = (bf16[912,256]{1,0:T(8,128)(2,1)S(1)}, bf16[912,256]{1,0:T(8,128)(2,1)S(1)}, u32[]{:S(2)}, u32[]{:S(2)}) collective-permute-start(bf16[912,256]{1,0:T(8,128)(2,1)S(1)} %get-tuple-element.110), channel_id=1, source_target_pairs={{0,1},{1,0},{2,3},{3,2},{4,5},{5,4},{6,7},{7,6},{8,9},{9,8},{10,11... | collective-permute-start | bytes 1400840 | tf_op jit(solution)/shard_map/ppermute | solution.py:54
  20.6 7.5 %collective-permute-start.8 = (bf16[96,256]{1,0:T(8,128)(2,1)S(1)}, bf16[96,256]{1,0:T(8,128)(2,1)S(1)}, u32[]{:S(2)}, u32[]{:S(2)}) collective-permute-start(bf16[96,256]{1,0:T(8,128)(2,1)S(1)} %get-tuple-element.115), channel_id=1, source_target_pairs={{0,4},{4,8},{8,12},{12,0},{1,5},{5,9},{9,13},{13,1},{2,6},{6,10},{... | collective-permute-start | bytes 147464 | tf_op jit(solution)/shard_map/ppermute | solution.py:25
  21.6 6.5 %collective-permute-start.9 = (bf16[96,256]{1,0:T(8,128)(2,1)S(1)}, bf16[96,256]{1,0:T(8,128)(2,1)S(1)}, u32[]{:S(2)}, u32[]{:S(2)}) collective-permute-start(bf16[96,256]{1,0:T(8,128)(2,1)S(1)} %get-tuple-element.117), channel_id=1, source_target_pairs={{0,12},{4,0},{8,4},{12,8},{1,13},{5,1},{9,5},{13,9},{2,14},{6,2},{... | collective-permute-start | bytes 147464 | tf_op jit(solution)/shard_map/ppermute | solution.py:25
  24.5 5.7 %collective-permute-start.5 = (bf16[240,256]{1,0:T(8,128)(2,1)S(1)}, bf16[240,256]{1,0:T(8,128)(2,1)S(1)}, u32[]{:S(2)}, u32[]{:S(2)}) collective-permute-start(bf16[240,256]{1,0:T(8,128)(2,1)S(1)} %get-tuple-element.112), channel_id=1, source_target_pairs={{0,2},{2,0},{4,6},{6,4},{1,3},{3,1},{5,7},{7,5},{8,10},{10,8},{12,... | collective-permute-start | bytes 368648 | tf_op jit(solution)/shard_map/ppermute | solution.py:44
  25.1 5.8 %collective-permute-start.6 = (bf16[240,256]{1,0:T(8,128)(2,1)S(1)}, bf16[240,256]{1,0:T(8,128)(2,1)S(1)}, u32[]{:S(2)}, u32[]{:S(2)}) collective-permute-start(bf16[240,256]{1,0:T(8,128)(2,1)S(1)} %get-tuple-element.113), channel_id=1, source_target_pairs={{0,4},{2,6},{4,0},{6,2},{1,5},{3,7},{5,1},{7,3},{8,12},{10,14},{12... | collective-permute-start | bytes 368648 | tf_op jit(solution)/shard_map/ppermute | solution.py:44
  25.1 8.1 %collective-permute-start.7 = (bf16[240,256]{1,0:T(8,128)(2,1)S(1)}, bf16[240,256]{1,0:T(8,128)(2,1)S(1)}, u32[]{:S(2)}, u32[]{:S(2)}) collective-permute-start(bf16[240,256]{1,0:T(8,128)(2,1)S(1)} %get-tuple-element.114), channel_id=1, source_target_pairs={{0,6},{2,4},{4,2},{6,0},{1,7},{3,5},{5,3},{7,1},{8,14},{10,12},{12... | collective-permute-start | bytes 368648 | tf_op jit(solution)/shard_map/ppermute | solution.py:44
  33.2 7.1 %collective-permute-start.10 = (bf16[240,256]{1,0:T(8,128)(2,1)S(1)}, bf16[240,256]{1,0:T(8,128)(2,1)S(1)}, u32[]{:S(2)}, u32[]{:S(2)}) collective-permute-start(bf16[240,256]{1,0:T(8,128)(2,1)S(1)} %shard_map.203.own), channel_id=1, source_target_pairs={{0,8},{8,0},{1,9},{9,1},{2,10},{10,2},{3,11},{11,3},{4,12},{12,4},... | collective-permute-start | bytes 368648 | tf_op jit(solution)/shard_map/ppermute | solution.py:529
  34.1 2.3 %collective-permute-start.11 = (bf16[96,256]{1,0:T(8,128)(2,1)S(1)}, bf16[96,256]{1,0:T(8,128)(2,1)S(1)}, u32[]{:S(2)}, u32[]{:S(2)}) collective-permute-start(bf16[96,256]{1,0:T(8,128)(2,1)S(1)} %get-tuple-element.123), channel_id=1, source_target_pairs={{0,1},{1,0},{2,3},{3,2},{4,5},{5,4},{6,7},{7,6},{8,9},{9,8},{10,11... | collective-permute-start | bytes 147464 | tf_op jit(solution)/shard_map/ppermute | solution.py:54
  34.1 3.5 %collective-permute-start.12 = (bf16[96,256]{1,0:T(8,128)(2,1)S(1)}, bf16[96,256]{1,0:T(8,128)(2,1)S(1)}, u32[]{:S(2)}, u32[]{:S(2)}) collective-permute-start(bf16[96,256]{1,0:T(8,128)(2,1)S(1)} %get-tuple-element.124), channel_id=1, source_target_pairs={{0,3},{1,2},{2,1},{3,0},{4,7},{5,6},{6,5},{7,4},{8,11},{9,10},{10,... | collective-permute-start | bytes 147464 | tf_op jit(solution)/shard_map/ppermute | solution.py:31
  40.4 6.1 %collective-permute-start.15 = (bf16[224,256]{1,0:T(8,128)(2,1)S(1)}, bf16[224,256]{1,0:T(8,128)(2,1)S(1)}, u32[]{:S(2)}, u32[]{:S(2)}) collective-permute-start(bf16[224,256]{1,0:T(8,128)(2,1)S(1)} %get-tuple-element.152.refs_0_), channel_id=1, source_target_pairs={{0,2},{2,0},{4,6},{6,4},{1,3},{3,1},{5,7},{7,5},{8,10},{10,8},{12,... | collective-permute-start | bytes 344072 | tf_op jit(solution)/shard_map/ppermute | solution.py:44
  41.0 5.5 %collective-permute-start.14 = (bf16[224,256]{1,0:T(8,128)(2,1)S(1)}, bf16[224,256]{1,0:T(8,128)(2,1)S(1)}, u32[]{:S(2)}, u32[]{:S(2)}) collective-permute-start(bf16[224,256]{1,0:T(8,128)(2,1)S(1)} %get-tuple-element.152.refs_0_), channel_id=1, source_target_pairs={{0,4},{2,6},{4,0},{6,2},{1,5},{3,7},{5,1},{7,3},{8,12},{10,14},{12... | collective-permute-start | bytes 344072 | tf_op jit(solution)/shard_map/ppermute | solution.py:44
  41.0 7.0 %collective-permute-start.13 = (bf16[224,256]{1,0:T(8,128)(2,1)S(1)}, bf16[224,256]{1,0:T(8,128)(2,1)S(1)}, u32[]{:S(2)}, u32[]{:S(2)}) collective-permute-start(bf16[224,256]{1,0:T(8,128)(2,1)S(1)} %get-tuple-element.152.refs_0_), channel_id=1, source_target_pairs={{0,6},{2,4},{4,2},{6,0},{1,7},{3,5},{5,3},{7,1},{8,14},{10,12},{12... | collective-permute-start | bytes 344072 | tf_op jit(solution)/shard_map/ppermute | solution.py:44
  45.6 2.3 %collective-permute-start.16 = (bf16[224,256]{1,0:T(8,128)(2,1)S(1)}, bf16[224,256]{1,0:T(8,128)(2,1)S(1)}, u32[]{:S(2)}, u32[]{:S(2)}) collective-permute-start(bf16[224,256]{1,0:T(8,128)(2,1)S(1)} %get-tuple-element.152.refs_0_), channel_id=1, source_target_pairs={{0,1},{1,0},{2,3},{3,2},{4,5},{5,4},{6,7},{7,6},{8,9},{9,8},{10,11... | collective-permute-start | bytes 344072 | tf_op jit(solution)/shard_map/ppermute | solution.py:54
  46.5 1.5 %collective-permute-start.17 = (bf16[224,256]{1,0:T(8,128)(2,1)S(1)}, bf16[224,256]{1,0:T(8,128)(2,1)S(1)}, u32[]{:S(2)}, u32[]{:S(2)}) collective-permute-start(bf16[224,256]{1,0:T(8,128)(2,1)S(1)} %collective-permute-done.15.refs_1_), channel_id=1, source_target_pairs={{0,1},{1,0},{2,3},{3,2},{4,5},{5,4},{6,7},{7,6},{8,9},{9,8},{10,11... | collective-permute-start | bytes 344072 | tf_op jit(solution)/shard_map/ppermute | solution.py:54
  46.5 1.5 %collective-permute-start.18 = (bf16[224,256]{1,0:T(8,128)(2,1)S(1)}, bf16[224,256]{1,0:T(8,128)(2,1)S(1)}, u32[]{:S(2)}, u32[]{:S(2)}) collective-permute-start(bf16[224,256]{1,0:T(8,128)(2,1)S(1)} %collective-permute-done.14.refs_2_), channel_id=1, source_target_pairs={{0,1},{1,0},{2,3},{3,2},{4,5},{5,4},{6,7},{7,6},{8,9},{9,8},{10,11... | collective-permute-start | bytes 344072 | tf_op jit(solution)/shard_map/ppermute | solution.py:54
  47.9 1.3 %collective-permute-start.19 = (bf16[224,256]{1,0:T(8,128)(2,1)S(1)}, bf16[224,256]{1,0:T(8,128)(2,1)S(1)}, u32[]{:S(2)}, u32[]{:S(2)}) collective-permute-start(bf16[224,256]{1,0:T(8,128)(2,1)S(1)} %collective-permute-done.13.refs_3_), channel_id=1, source_target_pairs={{0,1},{1,0},{2,3},{3,2},{4,5},{5,4},{6,7},{7,6},{8,9},{9,8},{10,11... | collective-permute-start | bytes 344072 | tf_op jit(solution)/shard_map/ppermute | solution.py:54

commit v15 on v14

--- a/solution.py
+++ b/solution.py
@@ -10,6 +10,7 @@
 EPS = 1e-05
 BF16 = jnp.bfloat16
 F32 = jnp.float32
+PACKED = 8
 VMEM_LIMIT = 24 * 1024 * 1024
 
 
@@ -25,10 +26,23 @@
     return lax.ppermute(array, axis, [(i, (i + by) % size) for i in range(size)])
 
 
+def chip_neighbour(i, size):
+    return (i + 1 if i % 2 else i - 1) % size
+
+
 def across_chips(array):
     size = lax.axis_size(PY)
-    pairs = [(i, (i + 1 if i % 2 else i - 1) % size) for i in range(size)]
-    return lax.ppermute(array, PY, pairs)
+    return lax.ppermute(array, PY, [(i, chip_neighbour(i, size)) for i in range(size)])
+
+
+def to_corner(array, by):
+    rows, columns = lax.axis_size(PX), lax.axis_size(PY)
+    pairs = [
+        (i * columns + j, (i + by) % rows * columns + chip_neighbour(j, columns))
+        for i in range(rows)
+        for j in range(columns)
+    ]
+    return lax.ppermute(array, PX + PY, pairs)
 
 
 def square_members():
@@ -138,14 +152,37 @@
     return copies
 
 
-def send_kernel(nodes_hbm, list_hbm, low, mid, high, nodes, send_list, sems):
-    slots = send_list.shape[1]
-    for copy in fetch_all([list_hbm, nodes_hbm], [send_list, nodes], sems):
+def send_kernel(
+    nodes_hbm, list_hbm, up, down, self_out, straight, corner_up, corner_down, nodes, ids, sems
+):
+    slots = ids.shape[1]
+    for copy in fetch_all([list_hbm, nodes_hbm], [ids, nodes], sems):
         copy.wait()
-    rows = dot(list_hot(send_list[...], nodes.shape[0]), nodes[...]).astype(BF16)
-    low[...] = rows[: 3 * slots]
-    mid[...] = rows[3 * slots : 5 * slots]
-    high[...] = rows[5 * slots :]
+    rows = dot(list_hot(ids[...], nodes.shape[0]), nodes[...]).astype(BF16)
+
+    def block(k):
+        return rows[k * slots : (k + 1) * slots]
+
+    up[:slots] = block(6)
+    down[:slots] = block(1)
+
+    def store(up_k, down_k, self_k, straight_k, corner_up_k, corner_down_k):
+        up[slots:] = block(up_k)
+        down[slots:] = block(down_k)
+        self_out[...] = block(self_k)
+        straight[...] = block(straight_k)
+        corner_up[...] = block(corner_up_k)
+        corner_down[...] = block(corner_down_k)
+
+    core = lax.axis_index(CORE)
+
+    @pl.when(core == 0)
+    def _():
+        store(7, 2, 4, 3, 5, 0)
+
+    @pl.when(core == 1)
+    def _():
+        store(5, 0, 3, 4, 7, 2)
 
 
 def index_kernel(sources, *refs):
@@ -204,7 +241,7 @@
 def pack_gains(edge_gain, node_gain):
     edge_high = edge_gain.astype(BF16).astype(F32)
     node_high = node_gain.astype(BF16).astype(F32)
-    row = lax.broadcasted_iota(jnp.int32, (16, edge_gain.shape[1]), 0)
+    row = lax.broadcasted_iota(jnp.int32, (PACKED, edge_gain.shape[1]), 0)
     packed = jnp.where(row == 0, edge_high, 0.0)
     packed = jnp.where(row == 1, edge_gain - edge_high, packed)
     packed = jnp.where(row == 2, node_high, packed)
@@ -224,10 +261,12 @@
     near_rows,
     sender_columns,
     receiver_columns,
+    from_low,
     from_high,
-    from_low,
-    upward,
-    downward,
+    from_core,
+    straight,
+    corner_low,
+    corner_high,
     w_in,
     w_out,
     gain_edge,
@@ -254,17 +293,20 @@
     count, width = nodes.shape
     edge_rows = edges.shape[0]
     live = live_rows(count_ref, tile_rows, edge_rows)
-    slots = from_high.shape[0] // 3
+    slots = straight.shape[0]
+    first_core = lax.axis_index(CORE) == 0
+    parts = [from_core[i * slots : (i + 1) * slots] for i in range(3)]
+    other = [straight[...], corner_low[...], corner_high[...]]
     halo = jnp.concatenate(
         [
-            downward[:slots],
-            from_high[slots : 2 * slots],
-            upward[:slots],
-            downward[slots : 2 * slots],
-            upward[slots : 2 * slots],
-            downward[2 * slots :],
-            from_low[slots : 2 * slots],
-            upward[2 * slots :],
+            jnp.where(first_core, parts[2], other[2]),
+            from_high[:slots],
+            jnp.where(first_core, other[2], parts[2]),
+            jnp.where(first_core, parts[0], other[0]),
+            jnp.where(first_core, other[0], parts[0]),
+            jnp.where(first_core, parts[1], other[1]),
+            from_low[:slots],
+            jnp.where(first_core, other[1], parts[1]),
         ],
         axis=0,
     )
@@ -347,7 +389,7 @@
 
 
 def add_packed(values):
-    packed = 16
+    packed = PACKED
     gains = values[:packed]
     return pack_gains(gains[0:1] + gains[1:2], gains[2:3] + gains[3:4])
 
@@ -356,13 +398,13 @@
     sums_out = refs[-1]
     sums = tree_sum([block[...].astype(F32) for block in refs[:-1]])
     sums_out[...] = sums.astype(BF16)
-    sums_out[:16] = add_packed(sums)
+    sums_out[:PACKED] = add_packed(sums)
 
 
 def join_kernel(own, other, sums_out):
     sums = own[...].astype(F32) + other[...].astype(F32)
     sums_out[...] = sums.astype(BF16)
-    sums_out[:16] = add_packed(sums)
+    sums_out[:PACKED] = add_packed(sums)
 
 
 def whole_kernel(own, other, gains_out, mine):
@@ -564,23 +606,22 @@
     edge_rows = edges.shape[0]
     tile_rows = senders.shape[1]
     square = 2 * width * width
-    low, mid, high, nodes, send_list = call(
+    up, down, own_rows, straight, corner_up, corner_down, nodes, send_list = call(
         send_kernel,
-        [
-            shaped(3 * slots, width, BF16),
-            shaped(2 * slots, width, BF16),
-            shaped(3 * slots, width, BF16),
-            like(nodes),
-            like(send_list),
-        ],
+        [shaped(2 * slots, width, BF16)] * 2
+        + [shaped(slots, width, BF16)] * 4
+        + [like(nodes), like(send_list)],
         2 * halo_rows * count * width,
         nodes,
         send_list,
         spaces=[HBM, HBM],
         scratch=[pltpu.SemaphoreType.DMA((2,))],
     )
-    from_low = passed_along(high, PX, 1)
-    from_high = passed_along(low, PX, -1)
+    from_low = passed_along(up, PX, 1)
+    from_high = passed_along(down, PX, -1)
+    straight = across_chips(straight)
+    corner_low = to_corner(corner_up, 1)
+    corner_high = to_corner(corner_down, -1)
     fetched = [
         senders,
         receivers,
@@ -620,11 +661,8 @@
         edge_grads,
     ) = fetched
     from_low, from_high, near_hot = lax.optimization_barrier((from_low, from_high, near_hot))
-    upward = passed_along(
-        jnp.concatenate([from_high[2 * slots :], mid[slots:], from_low[2 * slots :]]), PY, 1
-    )
-    downward = passed_along(
-        jnp.concatenate([from_high[:slots], mid[:slots], from_low[:slots]]), PY, -1
+    from_core = across_cores(
+        jnp.concatenate([own_rows, from_low[slots:], from_high[slots:]])
     )
     pre_local, sender_columns, receiver_columns = call(
         local_kernel,
@@ -654,8 +692,8 @@
             shaped(2 * slots, width, BF16),
             shaped(3 * slots, width, BF16),
             shaped(halves, width, F32),
-            shaped(halves + 16, width, BF16),
-            shaped(16, width, BF16),
+            shaped(halves + PACKED, width, BF16),
+            shaped(PACKED, width, BF16),
         ],
         square * (6 * edge_rows + 11 * count + 2 * halo_rows)
         + 2 * edge_rows * (4 * count + halo_rows) * width,
@@ -669,10 +707,12 @@
         near_hot,
         sender_columns,
         receiver_columns,
+        from_low,
         from_high,
-        from_low,
-        upward,
-        downward,
+        from_core,
+        straight,
+        corner_low,
+        corner_high,
         w_edge_in,
         w_edge_out,
         gain_edge,
@@ -693,7 +733,7 @@
     members = square_members()
     own, *blocks = call(
         functools.partial(pair_kernel, parts),
-        [shaped(16 + halves // members, width, BF16)] * members,
+        [shaped(PACKED + halves // members, width, BF16)] * members,
         0,
         keep,
         gains,

time: 50.5 us -> 53.6 us (1.061)
  starting transfers between devices: 21.9 us -> 24.5 us
  waiting for transfers between devices: 12.2 us -> 12.8 us
    ppermute x1 -> x4, starting transfers between devices: 1.02 us -> 6.42 us  [the longest x2 4.44 us: to_corner(): return lax.ppermute(array, PX + PY, pairs)]
    ppermute x6 -> x4, starting transfers between devices: 10.8 us -> 9.04 us  [passed_along(): lax.ppermute(array, axis, [(i, (i + by) % size) for i in range(size)])]
    ppermute x1, starting transfers between devices: 0.83 us -> 0.07 us  [joined(): other = lax.ppermute(sums, FAR, [(i, i ^ distance) for i in range(size)])]
    ppermute x1, waiting for transfers between devices: 2.76 us -> 3.31 us  [joined(): other = lax.ppermute(sums, FAR, [(i, i ^ distance) for i in range(size)])]
    ppermute x6 -> x7, starting transfers between devices: 2.16 us -> 1.84 us  [across_cores(): return lax.ppermute(array, CORE, [(0, 1), (1, 0)])]
    ppermute x1 -> x4, waiting for transfers between devices: 1.18 us -> 0.93 us  [the longest x2 0.92 us: across_chips(): lax.ppermute(array, PY, [(i, chip_neighbour(i, size)) for i in range(size)])]
    ppermute x6 -> x7, waiting for transfers between devices: 1.32 us -> 1.32 us  [across_cores(): return lax.ppermute(array, CORE, [(0, 1), (1, 0)])]
  transfers between devices with their start and end apart: 20 -> 22, of which waited for: 9 -> 8; matrix products, arithmetic and copies ran while one was open for 1% -> 1% of each run, Pallas kernels for 12% -> 12%
where the time goes in v15:
time: 53.6 us; the launch traced here: 53.4 us
  starting transfers between devices  24.5 us (46%)
  Pallas kernels  14.2 us (26%)
  waiting for transfers between devices  12.8 us (24%)
  between operations  1.45 us (3%)
  other arithmetic  0.54 us (1%)
    pallas_call x11, Pallas kernels, call(): pl.pallas_call(body, out_shape=outs, in_specs=[pl.BlockSpec(memory_space=...  14.2 us
    ppermute x4, starting transfers between devices, passed_along(): lax.ppermute(array, axis, [(i, (i + by) % size) for i in range(size)])  9.04 us
    ppermute x6, waiting for transfers between devices, in_square(): lax.ppermute(array, SQUARE, [(i, i ^ offset) for i in range(square_member...  7.24 us
    ppermute x6, starting transfers between devices, in_square(): lax.ppermute(array, SQUARE, [(i, i ^ offset) for i in range(square_member...  7.11 us
    ppermute x2, starting transfers between devices, to_corner(): return lax.ppermute(array, PX + PY, pairs)  4.44 us
    ppermute x1, waiting for transfers between devices, joined(): other = lax.ppermute(sums, FAR, [(i, i ^ distance) for i in range(size)])  3.31 us
    ppermute x2, starting transfers between devices, across_chips(): lax.ppermute(array, PY, [(i, chip_neighbour(i, size)) for i in range(size)])  1.97 us
    ppermute x7, starting transfers between devices, across_cores(): return lax.ppermute(array, CORE, [(0, 1), (1, 0)])  1.84 us
  transfers between devices with their start and end apart: 22, of which 8 were waited for; matrix products, arithmetic and copies ran while one was open for 1% of the time, Pallas kernels for 12%

profile of v15, /device:TPU:0, one launch (start us, length us, event | category | flops | bytes accessed | tf_op | source)
XLA Modules:
  0.0 53.4 jit_solution(16560148201555328565)
XLA Ops:
  0.6 1.3 %shard_map.197 = (bf16[64,256]{1,0:T(8,128)(2,1)S(1)}, bf16[64,256]{1,0:T(8,128)(2,1)S(1)}, bf16[32,256]{1,0:T(8,128)(2,1)S(1)}, bf16[32,256]{1,0:T(8,128)(2,1)S...) custom-call(bf16[384,256]{1,0:T(8,128)(2,1)} %nodes_hbm.1, ...), custom_call_target="tpu_custom_call" | custom-call | flops 50331648 | bytes 526336 | tf_op jit(solution)/shard_map/pallas_call | solution.py:530
  1.9 3.1 %collective-permute-start = (bf16[64,256]{1,0:T(8,128)(2,1)S(1)}, bf16[64,256]{1,0:T(8,128)(2,1)S(1)}, u32[]{:S(2)}, u32[]{:S(2)}) collective-permute-start(bf16[64,256]{1,0:T(8,128)(2,1)S(1)} %get-tuple-element.94), channel_id=1, source_target_pairs={{0,4},{4,8},{8,12},{12,0},{1,5},{5,9},{9,13},{13,1},{2,6},{6,10},{... | collective-permute-start | bytes 98312 | tf_op jit(solution)/shard_map/ppermute | solution.py:26
  5.0 2.1 %collective-permute-start.1 = (bf16[64,256]{1,0:T(8,128)(2,1)S(1)}, bf16[64,256]{1,0:T(8,128)(2,1)S(1)}, u32[]{:S(2)}, u32[]{:S(2)}) collective-permute-start(bf16[64,256]{1,0:T(8,128)(2,1)S(1)} %get-tuple-element.95), channel_id=1, source_target_pairs={{0,12},{4,0},{8,4},{12,8},{1,13},{5,1},{9,5},{13,9},{2,14},{6,2},{... | collective-permute-start | bytes 98312 | tf_op jit(solution)/shard_map/ppermute | solution.py:26
  7.1 0.7 %collective-permute-start.3 = (bf16[32,256]{1,0:T(8,128)(2,1)S(1)}, bf16[32,256]{1,0:T(8,128)(2,1)S(1)}, u32[]{:S(2)}, u32[]{:S(2)}) collective-permute-start(bf16[32,256]{1,0:T(8,128)(2,1)S(1)} %get-tuple-element.106), channel_id=1, source_target_pairs={{0,3},{1,2},{2,1},{3,0},{4,7},{5,6},{6,5},{7,4},{8,11},{9,10},{10,... | collective-permute-start | bytes 49160 | tf_op jit(solution)/shard_map/ppermute | solution.py:35
  7.8 0.5 collective-permute-start.4
  8.2 4.0 %collective-permute-start.5 = (bf16[32,256]{1,0:T(8,128)(2,1)S(1)}, bf16[32,256]{1,0:T(8,128)(2,1)S(1)}, u32[]{:S(2)}, u32[]{:S(2)}) collective-permute-start(bf16[32,256]{1,0:T(8,128)(2,1)S(1)} %get-tuple-element.108), channel_id=1, source_target_pairs={{0,15},{1,14},{2,13},{3,12},{4,3},{5,2},{6,1},{7,0},{8,7},{9,6},{1... | collective-permute-start | bytes 49160 | tf_op jit(solution)/shard_map/ppermute | solution.py:45
  12.9 1.7 %shard_map.198 = (bf16[1152,768]{1,0:T(8,128)(2,1)S(1)}, bf16[1152,256]{1,0:T(8,128)(2,1)S(1)}, s32[9,128]{1,0:T(8,128)S(1)}, s32[9,128]{1,0:T(8,128)S(1)}, bf16...) custom-call(s32[9,128]{1,0:T(8,128)} %refs_0_.1, ...), custom_call_target="tpu_custom_call" | custom-call | bytes 6967296 | tf_op jit(solution)/shard_map/pallas_call | solution.py:530
  14.6 0.0 collective-permute-done.from_low
  14.6 0.0 collective-permute-done.1.from_high
  14.7 1.2 %collective-permute-start.2 = (bf16[96,256]{1,0:T(8,128)(2,1)S(1)}, bf16[96,256]{1,0:T(8,128)(2,1)S(1)}, u32[]{:S(2)}, u32[]{:S(2)}) collective-permute-start(bf16[96,256]{1,0:T(8,128)(2,1)S(1)} %pad_maximum_fusion), channel_id=1, source_target_pairs={{0,1},{1,0},{2,3},{3,2},{4,5},{5,4},{6,7},{7,6},{8,9},{9,8},{10,11... | collective-permute-start | bytes 147464 | tf_op jit(solution)/shard_map/ppermute | solution.py:68
  15.8 1.8 %shard_map.199 = (f32[1152,256]{1,0:T(8,128)S(1)}, bf16[640,1152]{1,0:T(8,128)(2,1)S(1)}, bf16[384,1152]{1,0:T(8,128)(2,1)S(1)}) custom-call(bf16[384,256]{1,0:T(8,128)(2,1)S(1)} %get-tuple-element.88.nodes, bf16[1152,256]{1,0:T(8,128)(2,1)S(1)} %get-tuple-element.90.edges, s32[9,128]{1,0:T(8,128)S(1)} %get-tuple-element.92.senders, ...), custom_call_target="tpu_custom_call" | custom-call | flops 704643072 | bytes 6497280 | tf_op jit(solution)/shard_map/pallas_call | solution.py:530
  17.7 0.0 collective-permute-done.3.straight
  17.7 0.0 collective-permute-done.4.corner_low
  17.7 0.0 collective-permute-done.5.corner_high
  17.7 0.0 collective-permute-done.2.from_core
  17.7 5.6 %shard_map.200 = (bf16[1152,256]{1,0:T(8,128)(2,1)S(1)}, bf16[384,256]{1,0:T(8,128)(2,1)S(1)}, bf16[384,256]{1,0:T(8,128)(2,1)S(1)}, f32[384,256]{1,0:T(8,128)S(...) custom-call(s32[1]{0:T(128)S(6)} %copy.22.count_ref, ...), custom_call_target="tpu_custom_call" | custom-call | flops 2583691264 | bytes 11445252 | tf_op jit(solution)/shard_map/pallas_call | solution.py:530
  23.3 0.1 collective-permute-start.6
  23.4 0.1 collective-permute-start.10
  23.5 3.8 %collective-permute-start.11 = (bf16[96,256]{1,0:T(8,128)(2,1)S(1)}, bf16[96,256]{1,0:T(8,128)(2,1)S(1)}, u32[]{:S(2)}, u32[]{:S(2)}) collective-permute-start(bf16[96,256]{1,0:T(8,128)(2,1)S(1)} %get-tuple-element.123), channel_id=1, source_target_pairs={{0,12},{4,0},{8,4},{12,8},{1,13},{5,1},{9,5},{13,9},{2,14},{6,2},{... | collective-permute-start | bytes 147464 | tf_op jit(solution)/shard_map/ppermute | solution.py:26
  27.3 0.0 collective-permute-done.6.other
  27.3 0.1 shard_map.201
  27.4 0.4 collective-permute-start.7
  27.8 0.0 collective-permute-start.8
  27.8 3.1 %collective-permute-start.9 = (bf16[232,256]{1,0:T(8,128)(2,1)S(1)}, bf16[232,256]{1,0:T(8,128)(2,1)S(1)}, u32[]{:S(2)}, u32[]{:S(2)}) collective-permute-start(bf16[232,256]{1,0:T(8,128)(2,1)S(1)} %get-tuple-element.120), channel_id=1, source_target_pairs={{0,6},{2,4},{4,2},{6,0},{1,7},{3,5},{5,3},{7,1},{8,14},{10,12},{12... | collective-permute-start | bytes 356360 | tf_op jit(solution)/shard_map/ppermute | solution.py:58
  30.9 0.0 collective-permute-done.10.top
  30.9 0.0 collective-permute-done.11.bottom
  31.0 1.5 %collective-permute-done.7.refs_1_ = bf16[232,256]{1,0:T(8,128)(2,1)S(1)} collective-permute-done((bf16[232,256]{1,0:T(8,128)(2,1)S(1)}, bf16[232,256]{1,0:T(8,128)(2,1)S(1)}, u32[]{:S(2)}, u32[]{:S(2)}) %collective-permute-start.7) | collective-permute-done | bytes 118816 | tf_op jit(solution)/shard_map/ppermute | solution.py:58
  32.5 1.4 %collective-permute-done.8.refs_2_ = bf16[232,256]{1,0:T(8,128)(2,1)S(1)} collective-permute-done((bf16[232,256]{1,0:T(8,128)(2,1)S(1)}, bf16[232,256]{1,0:T(8,128)(2,1)S(1)}, u32[]{:S(2)}, u32[]{:S(2)}) %collective-permute-start.8) | collective-permute-done | bytes 118816 | tf_op jit(solution)/shard_map/ppermute | solution.py:58
  33.8 2.4 %collective-permute-done.9.refs_3_ = bf16[232,256]{1,0:T(8,128)(2,1)S(1)} collective-permute-done((bf16[232,256]{1,0:T(8,128)(2,1)S(1)}, bf16[232,256]{1,0:T(8,128)(2,1)S(1)}, u32[]{:S(2)}, u32[]{:S(2)}) %collective-permute-start.9) | collective-permute-done | bytes 118816 | tf_op jit(solution)/shard_map/ppermute | solution.py:58
  36.2 0.1 shard_map.203.own
  36.3 0.1 collective-permute-start.12
  36.4 0.1 collective-permute-start.13
  36.4 1.3 %collective-permute-start.14 = (bf16[96,256]{1,0:T(8,128)(2,1)S(1)}, bf16[96,256]{1,0:T(8,128)(2,1)S(1)}, u32[]{:S(2)}, u32[]{:S(2)}) collective-permute-start(bf16[96,256]{1,0:T(8,128)(2,1)S(1)} %get-tuple-element.130), channel_id=1, source_target_pairs={{0,3},{1,2},{2,1},{3,0},{4,7},{5,6},{6,5},{7,4},{8,11},{9,10},{10,... | collective-permute-start | bytes 147464 | tf_op jit(solution)/shard_map/ppermute | solution.py:35
  37.7 1.3 %shard_map.205 = (bf16[1152,256]{1,0:T(8,128)(2,1)}, f32[384,256]{1,0:T(8,128)S(1)}) custom-call(bf16[1152,256]{1,0:T(8,128)(2,1)S(1)} %get-tuple-element.91.edge_grads, bf16[1152,256]{1,0:T(8,128)(2,1)S(1)} %get-tuple-element.134.pre_grad, bf16[384,256]{1,0:T(8,128)(2,1)S(1)} %get-tuple-element.135.sender_sum, ...), custom_call_target="tpu_custom_call" | custom-call | flops 251658240 | bytes 3342336 | tf_op jit(solution)/shard_map/pallas_call | solution.py:530
  39.1 0.0 collective-permute-done.13.along_core
  39.1 0.9 %collective-permute-done.14.along_chip = bf16[96,256]{1,0:T(8,128)(2,1)S(1)} collective-permute-done((bf16[96,256]{1,0:T(8,128)(2,1)S(1)}, bf16[96,256]{1,0:T(8,128)(2,1)S(1)}, u32[]{:S(2)}, u32[]{:S(2)}) %collective-permute-start.14) | collective-permute-done | bytes 49184 | tf_op jit(solution)/shard_map/ppermute | solution.py:35
  40.0 3.3 %collective-permute-done.12.other = bf16[232,256]{1,0:T(8,128)(2,1)S(1)} collective-permute-done((bf16[232,256]{1,0:T(8,128)(2,1)S(1)}, bf16[232,256]{1,0:T(8,128)(2,1)S(1)}, u32[]{:S(2)}, u32[]{:S(2)}) %collective-permute-start.12) | collective-permute-done | bytes 118816 | tf_op jit(solution)/shard_map/ppermute | solution.py:571
  43.4 0.5 collective-permute-start.17
  43.8 0.0 collective-permute-start.16
  43.8 3.1 %collective-permute-start.15 = (bf16[224,256]{1,0:T(8,128)(2,1)S(1)}, bf16[224,256]{1,0:T(8,128)(2,1)S(1)}, u32[]{:S(2)}, u32[]{:S(2)}) collective-permute-start(bf16[224,256]{1,0:T(8,128)(2,1)S(1)} %get-tuple-element.158.refs_0_), channel_id=1, source_target_pairs={{0,6},{2,4},{4,2},{6,0},{1,7},{3,5},{5,3},{7,1},{8,14},{10,12},{12... | collective-permute-start | bytes 344072 | tf_op jit(solution)/shard_map/ppermute | solution.py:58
  46.9 1.1 %shard_map.206 = bf16[384,256]{1,0:T(8,128)(2,1)} custom-call(s32[8,32]{1,0:T(8,128)S(1)} %get-tuple-element.133.send_list, f32[384,256]{1,0:T(8,128)S(1)} %get-tuple-element.138.local_grad, bf16[64,256]{1,0:T(8,128)(2,1)S(1)} %get-tuple-element.139.center, bf16[96,256]{1,0:T(8,128)(2,1)S(1)} %collective-permute-done.13.along_core, ...), custom_call_target="tpu_custom_call" | custom-call | flops 50331648 | bytes 721920 | tf_op jit(solution)/shard_map/pallas_call | solution.py:530
  48.0 0.5 convert_reduce_fusion
  48.6 0.0 collective-permute-start.18
  48.6 0.9 %collective-permute-done.17.refs_1_ = bf16[224,256]{1,0:T(8,128)(2,1)S(1)} collective-permute-done((bf16[224,256]{1,0:T(8,128)(2,1)S(1)}, bf16[224,256]{1,0:T(8,128)(2,1)S(1)}, u32[]{:S(2)}, u32[]{:S(2)}) %collective-permute-start.17) | collective-permute-done | bytes 114720 | tf_op jit(solution)/shard_map/ppermute | solution.py:58
  49.5 0.0 collective-permute-start.19
  49.5 0.0 collective-permute-done.16.refs_2_
  49.5 0.5 collective-permute-start.20
  50.0 1.1 %collective-permute-done.15.refs_3_ = bf16[224,256]{1,0:T(8,128)(2,1)S(1)} collective-permute-done((bf16[224,256]{1,0:T(8,128)(2,1)S(1)}, bf16[224,256]{1,0:T(8,128)(2,1)S(1)}, u32[]{:S(2)}, u32[]{:S(2)}) %collective-permute-start.15) | collective-permute-done | bytes 114720 | tf_op jit(solution)/shard_map/ppermute | solution.py:58
  51.1 0.0 collective-permute-start.21
  51.1 0.0 collective-permute-done.18.refs_4_
  51.1 0.0 collective-permute-done.19.refs_5_
  51.1 0.0 collective-permute-done.20.refs_6_
  51.1 1.3 %collective-permute-done.21.refs_7_ = bf16[224,256]{1,0:T(8,128)(2,1)S(1)} collective-permute-done((bf16[224,256]{1,0:T(8,128)(2,1)S(1)}, bf16[224,256]{1,0:T(8,128)(2,1)S(1)}, u32[]{:S(2)}, u32[]{:S(2)}) %collective-permute-start.21) | collective-permute-done | bytes 114720 | tf_op jit(solution)/shard_map/ppermute | solution.py:68
  52.4 1.0 %shard_map.207 = (bf16[768,256]{1,0:T(8,128)(2,1)}, bf16[256,256]{1,0:T(8,128)(2,1)}, bf16[512,256]{1,0:T(8,128)(2,1)}, bf16[256,256]{1,0:T(8,128)(2,1)}) custom-call(bf16[224,256]{1,0:T(8,128)(2,1)S(1)} %get-tuple-element.158.refs_0_, bf16[224,256]{1,0:T(8,128)(2,1)S(1)} %collective-permute-done.17.refs_1_, ...), custom_call_target="tpu_custom_call" | custom-call | bytes 1835008 | tf_op jit(solution)/shard_map/pallas_call | solution.py:530
  (5 shorter events, 0.1 us)
Async XLA Ops:
  1.9 12.7 %collective-permute-start = (bf16[64,256]{1,0:T(8,128)(2,1)S(1)}, bf16[64,256]{1,0:T(8,128)(2,1)S(1)}, u32[]{:S(2)}, u32[]{:S(2)}) collective-permute-start(bf16[64,256]{1,0:T(8,128)(2,1)S(1)} %get-tuple-element.94), channel_id=1, source_target_pairs={{0,4},{4,8},{8,12},{12,0},{1,5},{5,9},{9,13},{13,1},{2,6},{6,10},{... | collective-permute-start | bytes 98312 | tf_op jit(solution)/shard_map/ppermute | solution.py:26
  5.0 9.6 %collective-permute-start.1 = (bf16[64,256]{1,0:T(8,128)(2,1)S(1)}, bf16[64,256]{1,0:T(8,128)(2,1)S(1)}, u32[]{:S(2)}, u32[]{:S(2)}) collective-permute-start(bf16[64,256]{1,0:T(8,128)(2,1)S(1)} %get-tuple-element.95), channel_id=1, source_target_pairs={{0,12},{4,0},{8,4},{12,8},{1,13},{5,1},{9,5},{13,9},{2,14},{6,2},{... | collective-permute-start | bytes 98312 | tf_op jit(solution)/shard_map/ppermute | solution.py:26
  7.1 10.6 %collective-permute-start.3 = (bf16[32,256]{1,0:T(8,128)(2,1)S(1)}, bf16[32,256]{1,0:T(8,128)(2,1)S(1)}, u32[]{:S(2)}, u32[]{:S(2)}) collective-permute-start(bf16[32,256]{1,0:T(8,128)(2,1)S(1)} %get-tuple-element.106), channel_id=1, source_target_pairs={{0,3},{1,2},{2,1},{3,0},{4,7},{5,6},{6,5},{7,4},{8,11},{9,10},{10,... | collective-permute-start | bytes 49160 | tf_op jit(solution)/shard_map/ppermute | solution.py:35
  7.8 9.9 %collective-permute-start.4 = (bf16[32,256]{1,0:T(8,128)(2,1)S(1)}, bf16[32,256]{1,0:T(8,128)(2,1)S(1)}, u32[]{:S(2)}, u32[]{:S(2)}) collective-permute-start(bf16[32,256]{1,0:T(8,128)(2,1)S(1)} %get-tuple-element.107), channel_id=1, source_target_pairs={{0,7},{1,6},{2,5},{3,4},{4,11},{5,10},{6,9},{7,8},{8,15},{9,14},{1... | collective-permute-start | bytes 49160 | tf_op jit(solution)/shard_map/ppermute | solution.py:45
  8.2 9.5 %collective-permute-start.5 = (bf16[32,256]{1,0:T(8,128)(2,1)S(1)}, bf16[32,256]{1,0:T(8,128)(2,1)S(1)}, u32[]{:S(2)}, u32[]{:S(2)}) collective-permute-start(bf16[32,256]{1,0:T(8,128)(2,1)S(1)} %get-tuple-element.108), channel_id=1, source_target_pairs={{0,15},{1,14},{2,13},{3,12},{4,3},{5,2},{6,1},{7,0},{8,7},{9,6},{1... | collective-permute-start | bytes 49160 | tf_op jit(solution)/shard_map/ppermute | solution.py:45
  14.7 3.0 %collective-permute-start.2 = (bf16[96,256]{1,0:T(8,128)(2,1)S(1)}, bf16[96,256]{1,0:T(8,128)(2,1)S(1)}, u32[]{:S(2)}, u32[]{:S(2)}) collective-permute-start(bf16[96,256]{1,0:T(8,128)(2,1)S(1)} %pad_maximum_fusion), channel_id=1, source_target_pairs={{0,1},{1,0},{2,3},{3,2},{4,5},{5,4},{6,7},{7,6},{8,9},{9,8},{10,11... | collective-permute-start | bytes 147464 | tf_op jit(solution)/shard_map/ppermute | solution.py:68
  23.3 4.0 %collective-permute-start.6 = (bf16[904,256]{1,0:T(8,128)(2,1)S(1)}, bf16[904,256]{1,0:T(8,128)(2,1)S(1)}, u32[]{:S(2)}, u32[]{:S(2)}) collective-permute-start(bf16[904,256]{1,0:T(8,128)(2,1)S(1)} %get-tuple-element.116), channel_id=1, source_target_pairs={{0,1},{1,0},{2,3},{3,2},{4,5},{5,4},{6,7},{7,6},{8,9},{9,8},{10,11... | collective-permute-start | bytes 1388552 | tf_op jit(solution)/shard_map/ppermute | solution.py:68
  23.4 7.6 %collective-permute-start.10 = (bf16[96,256]{1,0:T(8,128)(2,1)S(1)}, bf16[96,256]{1,0:T(8,128)(2,1)S(1)}, u32[]{:S(2)}, u32[]{:S(2)}) collective-permute-start(bf16[96,256]{1,0:T(8,128)(2,1)S(1)} %get-tuple-element.121), channel_id=1, source_target_pairs={{0,4},{4,8},{8,12},{12,0},{1,5},{5,9},{9,13},{13,1},{2,6},{6,10},{... | collective-permute-start | bytes 147464 | tf_op jit(solution)/shard_map/ppermute | solution.py:26
  23.5 7.5 %collective-permute-start.11 = (bf16[96,256]{1,0:T(8,128)(2,1)S(1)}, bf16[96,256]{1,0:T(8,128)(2,1)S(1)}, u32[]{:S(2)}, u32[]{:S(2)}) collective-permute-start(bf16[96,256]{1,0:T(8,128)(2,1)S(1)} %get-tuple-element.123), channel_id=1, source_target_pairs={{0,12},{4,0},{8,4},{12,8},{1,13},{5,1},{9,5},{13,9},{2,14},{6,2},{... | collective-permute-start | bytes 147464 | tf_op jit(solution)/shard_map/ppermute | solution.py:26
  27.4 5.1 %collective-permute-start.7 = (bf16[232,256]{1,0:T(8,128)(2,1)S(1)}, bf16[232,256]{1,0:T(8,128)(2,1)S(1)}, u32[]{:S(2)}, u32[]{:S(2)}) collective-permute-start(bf16[232,256]{1,0:T(8,128)(2,1)S(1)} %get-tuple-element.118), channel_id=1, source_target_pairs={{0,2},{2,0},{4,6},{6,4},{1,3},{3,1},{5,7},{7,5},{8,10},{10,8},{12,... | collective-permute-start | bytes 356360 | tf_op jit(solution)/shard_map/ppermute | solution.py:58
  27.8 6.0 %collective-permute-start.8 = (bf16[232,256]{1,0:T(8,128)(2,1)S(1)}, bf16[232,256]{1,0:T(8,128)(2,1)S(1)}, u32[]{:S(2)}, u32[]{:S(2)}) collective-permute-start(bf16[232,256]{1,0:T(8,128)(2,1)S(1)} %get-tuple-element.119), channel_id=1, source_target_pairs={{0,4},{2,6},{4,0},{6,2},{1,5},{3,7},{5,1},{7,3},{8,12},{10,14},{12... | collective-permute-start | bytes 356360 | tf_op jit(solution)/shard_map/ppermute | solution.py:58
  27.8 8.4 %collective-permute-start.9 = (bf16[232,256]{1,0:T(8,128)(2,1)S(1)}, bf16[232,256]{1,0:T(8,128)(2,1)S(1)}, u32[]{:S(2)}, u32[]{:S(2)}) collective-permute-start(bf16[232,256]{1,0:T(8,128)(2,1)S(1)} %get-tuple-element.120), channel_id=1, source_target_pairs={{0,6},{2,4},{4,2},{6,0},{1,7},{3,5},{5,3},{7,1},{8,14},{10,12},{12... | collective-permute-start | bytes 356360 | tf_op jit(solution)/shard_map/ppermute | solution.py:58
  36.3 7.1 %collective-permute-start.12 = (bf16[232,256]{1,0:T(8,128)(2,1)S(1)}, bf16[232,256]{1,0:T(8,128)(2,1)S(1)}, u32[]{:S(2)}, u32[]{:S(2)}) collective-permute-start(bf16[232,256]{1,0:T(8,128)(2,1)S(1)} %shard_map.203.own), channel_id=1, source_target_pairs={{0,8},{8,0},{1,9},{9,1},{2,10},{10,2},{3,11},{11,3},{4,12},{12,4},... | collective-permute-start | bytes 356360 | tf_op jit(solution)/shard_map/ppermute | solution.py:571
  36.4 2.7 %collective-permute-start.13 = (bf16[96,256]{1,0:T(8,128)(2,1)S(1)}, bf16[96,256]{1,0:T(8,128)(2,1)S(1)}, u32[]{:S(2)}, u32[]{:S(2)}) collective-permute-start(bf16[96,256]{1,0:T(8,128)(2,1)S(1)} %get-tuple-element.129), channel_id=1, source_target_pairs={{0,1},{1,0},{2,3},{3,2},{4,5},{5,4},{6,7},{7,6},{8,9},{9,8},{10,11... | collective-permute-start | bytes 147464 | tf_op jit(solution)/shard_map/ppermute | solution.py:68
  36.4 3.6 %collective-permute-start.14 = (bf16[96,256]{1,0:T(8,128)(2,1)S(1)}, bf16[96,256]{1,0:T(8,128)(2,1)S(1)}, u32[]{:S(2)}, u32[]{:S(2)}) collective-permute-start(bf16[96,256]{1,0:T(8,128)(2,1)S(1)} %get-tuple-element.130), channel_id=1, source_target_pairs={{0,3},{1,2},{2,1},{3,0},{4,7},{5,6},{6,5},{7,4},{8,11},{9,10},{10,... | collective-permute-start | bytes 147464 | tf_op jit(solution)/shard_map/ppermute | solution.py:35
  43.4 6.1 %collective-permute-start.17 = (bf16[224,256]{1,0:T(8,128)(2,1)S(1)}, bf16[224,256]{1,0:T(8,128)(2,1)S(1)}, u32[]{:S(2)}, u32[]{:S(2)}) collective-permute-start(bf16[224,256]{1,0:T(8,128)(2,1)S(1)} %get-tuple-element.158.refs_0_), channel_id=1, source_target_pairs={{0,2},{2,0},{4,6},{6,4},{1,3},{3,1},{5,7},{7,5},{8,10},{10,8},{12,... | collective-permute-start | bytes 344072 | tf_op jit(solution)/shard_map/ppermute | solution.py:58
  43.8 5.6 %collective-permute-start.16 = (bf16[224,256]{1,0:T(8,128)(2,1)S(1)}, bf16[224,256]{1,0:T(8,128)(2,1)S(1)}, u32[]{:S(2)}, u32[]{:S(2)}) collective-permute-start(bf16[224,256]{1,0:T(8,128)(2,1)S(1)} %get-tuple-element.158.refs_0_), channel_id=1, source_target_pairs={{0,4},{2,6},{4,0},{6,2},{1,5},{3,7},{5,1},{7,3},{8,12},{10,14},{12... | collective-permute-start | bytes 344072 | tf_op jit(solution)/shard_map/ppermute | solution.py:58
  43.8 7.3 %collective-permute-start.15 = (bf16[224,256]{1,0:T(8,128)(2,1)S(1)}, bf16[224,256]{1,0:T(8,128)(2,1)S(1)}, u32[]{:S(2)}, u32[]{:S(2)}) collective-permute-start(bf16[224,256]{1,0:T(8,128)(2,1)S(1)} %get-tuple-element.158.refs_0_), channel_id=1, source_target_pairs={{0,6},{2,4},{4,2},{6,0},{1,7},{3,5},{5,3},{7,1},{8,14},{10,12},{12... | collective-permute-start | bytes 344072 | tf_op jit(solution)/shard_map/ppermute | solution.py:58
  48.6 2.5 %collective-permute-start.18 = (bf16[224,256]{1,0:T(8,128)(2,1)S(1)}, bf16[224,256]{1,0:T(8,128)(2,1)S(1)}, u32[]{:S(2)}, u32[]{:S(2)}) collective-permute-start(bf16[224,256]{1,0:T(8,128)(2,1)S(1)} %get-tuple-element.158.refs_0_), channel_id=1, source_target_pairs={{0,1},{1,0},{2,3},{3,2},{4,5},{5,4},{6,7},{7,6},{8,9},{9,8},{10,11... | collective-permute-start | bytes 344072 | tf_op jit(solution)/shard_map/ppermute | solution.py:68
  49.5 1.7 %collective-permute-start.19 = (bf16[224,256]{1,0:T(8,128)(2,1)S(1)}, bf16[224,256]{1,0:T(8,128)(2,1)S(1)}, u32[]{:S(2)}, u32[]{:S(2)}) collective-permute-start(bf16[224,256]{1,0:T(8,128)(2,1)S(1)} %collective-permute-done.17.refs_1_), channel_id=1, source_target_pairs={{0,1},{1,0},{2,3},{3,2},{4,5},{5,4},{6,7},{7,6},{8,9},{9,8},{10,11... | collective-permute-start | bytes 344072 | tf_op jit(solution)/shard_map/ppermute | solution.py:68
  49.5 1.7 %collective-permute-start.20 = (bf16[224,256]{1,0:T(8,128)(2,1)S(1)}, bf16[224,256]{1,0:T(8,128)(2,1)S(1)}, u32[]{:S(2)}, u32[]{:S(2)}) collective-permute-start(bf16[224,256]{1,0:T(8,128)(2,1)S(1)} %collective-permute-done.16.refs_2_), channel_id=1, source_target_pairs={{0,1},{1,0},{2,3},{3,2},{4,5},{5,4},{6,7},{7,6},{8,9},{9,8},{10,11... | collective-permute-start | bytes 344072 | tf_op jit(solution)/shard_map/ppermute | solution.py:68
  51.1 1.3 %collective-permute-start.21 = (bf16[224,256]{1,0:T(8,128)(2,1)S(1)}, bf16[224,256]{1,0:T(8,128)(2,1)S(1)}, u32[]{:S(2)}, u32[]{:S(2)}) collective-permute-start(bf16[224,256]{1,0:T(8,128)(2,1)S(1)} %collective-permute-done.15.refs_3_), channel_id=1, source_target_pairs={{0,1},{1,0},{2,3},{3,2},{4,5},{5,4},{6,7},{7,6},{8,9},{9,8},{10,11... | collective-permute-start | bytes 344072 | tf_op jit(solution)/shard_map/ppermute | solution.py:68

commit v16 on v14

--- a/solution.py
+++ b/solution.py
@@ -10,25 +10,29 @@
 EPS = 1e-05
 BF16 = jnp.bfloat16
 F32 = jnp.float32
+PACKED = 8
 VMEM_LIMIT = 24 * 1024 * 1024
 
 
 CORE = "core"
 FAR = "far"
-PX = (FAR, "near")
+NEAR = "near"
+PX = (FAR, NEAR)
 PY = ("side", CORE)
-SQUARE = ("near", "side")
-
-
-def passed_along(array, axis, by):
+SQUARE = (NEAR, "side")
+
+
+def other_neighbour(i, size):
+    return (i + 1 if i % 2 else i - 1) % size
+
+
+def in_pair(array, axis):
+    return lax.ppermute(array, axis, [(i, i ^ 1) for i in range(lax.axis_size(axis))])
+
+
+def out_of_pair(array, axis):
     size = lax.axis_size(axis)
-    return lax.ppermute(array, axis, [(i, (i + by) % size) for i in range(size)])
-
-
-def across_chips(array):
-    size = lax.axis_size(PY)
-    pairs = [(i, (i + 1 if i % 2 else i - 1) % size) for i in range(size)]
-    return lax.ppermute(array, PY, pairs)
+    return lax.ppermute(array, axis, [(i, other_neighbour(i, size)) for i in range(size)])
 
 
 def square_members():
@@ -51,7 +55,26 @@
 
 
 def across_cores(array):
-    return lax.ppermute(array, CORE, [(0, 1), (1, 0)])
+    return in_pair(array, CORE)
+
+
+def by_pair(axis, up, down, inner, outer):
+    first = lax.axis_index(axis) == 0
+
+    @pl.when(first)
+    def _():
+        inner[...] = up
+        outer[...] = down
+
+    @pl.when(jnp.logical_not(first))
+    def _():
+        inner[...] = down
+        outer[...] = up
+
+
+def from_pair(axis, inner, outer):
+    first = lax.axis_index(axis) == 0
+    return jnp.where(first, outer, inner), jnp.where(first, inner, outer)
 
 
 def dot(left, right):
@@ -138,14 +161,23 @@
     return copies
 
 
-def send_kernel(nodes_hbm, list_hbm, low, mid, high, nodes, send_list, sems):
+def send_kernel(nodes_hbm, list_hbm, inner, outer, middle, nodes, send_list, sems):
     slots = send_list.shape[1]
     for copy in fetch_all([list_hbm, nodes_hbm], [send_list, nodes], sems):
         copy.wait()
     rows = dot(list_hot(send_list[...], nodes.shape[0]), nodes[...]).astype(BF16)
-    low[...] = rows[: 3 * slots]
-    mid[...] = rows[3 * slots : 5 * slots]
-    high[...] = rows[5 * slots :]
+    by_pair(NEAR, rows[5 * slots :], rows[: 3 * slots], inner, outer)
+    middle[...] = rows[3 * slots : 5 * slots]
+
+
+def corner_kernel(inner, outer, middle, along_core, along_chip, straight):
+    slots = middle.shape[0] // 2
+    low, high = from_pair(NEAR, inner[...], outer[...])
+    up = jnp.concatenate([high[2 * slots :], middle[slots:], low[2 * slots :]], axis=0)
+    down = jnp.concatenate([high[:slots], middle[:slots], low[:slots]], axis=0)
+    by_pair(CORE, up, down, along_core, along_chip)
+    straight[:slots] = high[slots : 2 * slots]
+    straight[slots:] = low[slots : 2 * slots]
 
 
 def index_kernel(sources, *refs):
@@ -204,7 +236,7 @@
 def pack_gains(edge_gain, node_gain):
     edge_high = edge_gain.astype(BF16).astype(F32)
     node_high = node_gain.astype(BF16).astype(F32)
-    row = lax.broadcasted_iota(jnp.int32, (16, edge_gain.shape[1]), 0)
+    row = lax.broadcasted_iota(jnp.int32, (PACKED, edge_gain.shape[1]), 0)
     packed = jnp.where(row == 0, edge_high, 0.0)
     packed = jnp.where(row == 1, edge_gain - edge_high, packed)
     packed = jnp.where(row == 2, node_high, packed)
@@ -224,10 +256,9 @@
     near_rows,
     sender_columns,
     receiver_columns,
-    from_high,
-    from_low,
-    upward,
-    downward,
+    straight,
+    along_core,
+    along_chip,
     w_in,
     w_out,
     gain_edge,
@@ -238,9 +269,9 @@
     sender_out,
     receiver_out,
     node_part_out,
-    top_out,
+    inner_out,
+    outer_out,
     middle_out,
-    bottom_out,
     keep_out,
     away_out,
     gains_out,
@@ -254,17 +285,18 @@
     count, width = nodes.shape
     edge_rows = edges.shape[0]
     live = live_rows(count_ref, tile_rows, edge_rows)
-    slots = from_high.shape[0] // 3
+    slots = straight.shape[0] // 2
+    up, down = from_pair(CORE, along_core[...], along_chip[...])
     halo = jnp.concatenate(
         [
-            downward[:slots],
-            from_high[slots : 2 * slots],
-            upward[:slots],
-            downward[slots : 2 * slots],
-            upward[slots : 2 * slots],
-            downward[2 * slots :],
-            from_low[slots : 2 * slots],
-            upward[2 * slots :],
+            down[:slots],
+            straight[:slots],
+            up[:slots],
+            down[slots : 2 * slots],
+            up[slots : 2 * slots],
+            down[2 * slots :],
+            straight[slots:],
+            up[2 * slots :],
         ],
         axis=0,
     )
@@ -314,9 +346,8 @@
     sender_out[...] = own
     receiver_out[...] = received
     halo_grad = dot_nt(away, w_in[width : 2 * width]).astype(BF16)
-    top_out[...] = halo_grad[: 3 * slots]
+    by_pair(NEAR, halo_grad[: 3 * slots], halo_grad[5 * slots :], inner_out, outer_out)
     middle_out[...] = halo_grad[3 * slots : 5 * slots]
-    bottom_out[...] = halo_grad[5 * slots :]
     edge_sums[:width] = dot_tn(edges[...], pre_grad)
     edge_sums[width : 2 * width] = dot_tn(x, own) + dot_tn(halo, away)
     edge_sums[2 * width : 3 * width] = dot_tn(x, received)
@@ -347,7 +378,7 @@
 
 
 def add_packed(values):
-    packed = 16
+    packed = PACKED
     gains = values[:packed]
     return pack_gains(gains[0:1] + gains[1:2], gains[2:3] + gains[3:4])
 
@@ -356,13 +387,13 @@
     sums_out = refs[-1]
     sums = tree_sum([block[...].astype(F32) for block in refs[:-1]])
     sums_out[...] = sums.astype(BF16)
-    sums_out[:16] = add_packed(sums)
+    sums_out[:PACKED] = add_packed(sums)
 
 
 def join_kernel(own, other, sums_out):
     sums = own[...].astype(F32) + other[...].astype(F32)
     sums_out[...] = sums.astype(BF16)
-    sums_out[:16] = add_packed(sums)
+    sums_out[:PACKED] = add_packed(sums)
 
 
 def whole_kernel(own, other, gains_out, mine):
@@ -414,61 +445,34 @@
     )
 
 
-def turn_kernel(top, middle, bottom, along_core, along_chip, center):
+def turn_kernel(inner, outer, middle, along_core, along_chip, center):
     slots = middle.shape[0] // 2
-
-    def turn(up, down):
-        up[:slots] = top[:slots]
-        up[slots : 2 * slots] = middle[:slots]
-        up[2 * slots :] = bottom[:slots]
-        down[:slots] = top[2 * slots :]
-        down[slots : 2 * slots] = middle[slots:]
-        down[2 * slots :] = bottom[2 * slots :]
-
-    core = lax.axis_index(CORE)
-
-    @pl.when(core == 0)
-    def _():
-        turn(along_core, along_chip)
-
-    @pl.when(core == 1)
-    def _():
-        turn(along_chip, along_core)
-
+    top, bottom = from_pair(NEAR, inner[...], outer[...])
+    up = jnp.concatenate([top[:slots], middle[:slots], bottom[:slots]], axis=0)
+    down = jnp.concatenate([top[2 * slots :], middle[slots:], bottom[2 * slots :]], axis=0)
+    by_pair(CORE, up, down, along_core, along_chip)
     center[:slots] = top[slots : 2 * slots]
     center[slots:] = bottom[slots : 2 * slots]
 
 
-def return_kernel(send_list, local_grad, center, along_core, along_chip, nodes_grad, returned):
+def return_kernel(send_list, local_grad, center, along_core, along_chip, nodes_grad):
     slots = send_list.shape[1]
-
-    def fill(up, down):
-        for k, (source, i) in enumerate(
-            [
-                (up, 0),
-                (center, 0),
-                (down, 0),
-                (up, 1),
-                (down, 1),
-                (up, 2),
-                (center, 1),
-                (down, 2),
-            ]
-        ):
-            returned[k * slots : (k + 1) * slots] = source[i * slots : (i + 1) * slots]
-
-    core = lax.axis_index(CORE)
-
-    @pl.when(core == 0)
-    def _():
-        fill(along_chip, along_core)
-
-    @pl.when(core == 1)
-    def _():
-        fill(along_core, along_chip)
-
+    up, down = from_pair(CORE, along_core[...], along_chip[...])
+    returned = jnp.concatenate(
+        [
+            up[:slots],
+            center[:slots],
+            down[:slots],
+            up[slots : 2 * slots],
+            down[slots : 2 * slots],
+            up[2 * slots :],
+            center[slots:],
+            down[2 * slots :],
+        ],
+        axis=0,
+    )
     hot = list_hot(send_list[...], local_grad.shape[0])
-    nodes_grad[...] = (local_grad[...] + dot_tn(hot, returned[...])).astype(BF16)
+    nodes_grad[...] = (local_grad[...] + dot_tn(hot, returned)).astype(BF16)
 
 
 SMEM = pltpu.SMEM
@@ -564,12 +568,12 @@
     edge_rows = edges.shape[0]
     tile_rows = senders.shape[1]
     square = 2 * width * width
-    low, mid, high, nodes, send_list = call(
+    inner, outer, middle, nodes, send_list = call(
         send_kernel,
         [
+            shaped(3 * slots, width, BF16),
             shaped(3 * slots, width, BF16),
             shaped(2 * slots, width, BF16),
-            shaped(3 * slots, width, BF16),
             like(nodes),
             like(send_list),
         ],
@@ -579,8 +583,8 @@
         spaces=[HBM, HBM],
         scratch=[pltpu.SemaphoreType.DMA((2,))],
     )
-    from_low = passed_along(high, PX, 1)
-    from_high = passed_along(low, PX, -1)
+    inner = in_pair(inner, PX)
+    outer = out_of_pair(outer, PX)
     fetched = [
         senders,
         receivers,
@@ -619,13 +623,21 @@
         node_grads,
         edge_grads,
     ) = fetched
-    from_low, from_high, near_hot = lax.optimization_barrier((from_low, from_high, near_hot))
-    upward = passed_along(
-        jnp.concatenate([from_high[2 * slots :], mid[slots:], from_low[2 * slots :]]), PY, 1
-    )
-    downward = passed_along(
-        jnp.concatenate([from_high[:slots], mid[:slots], from_low[:slots]]), PY, -1
-    )
+    inner, outer, near_hot = lax.optimization_barrier((inner, outer, near_hot))
+    along_core, along_chip, straight = call(
+        corner_kernel,
+        [
+            shaped(3 * slots, width, BF16),
+            shaped(3 * slots, width, BF16),
+            shaped(2 * slots, width, BF16),
+        ],
+        0,
+        inner,
+        outer,
+        middle,
+    )
+    along_chip = out_of_pair(along_chip, PY)
+    along_core = across_cores(along_core)
     pre_local, sender_columns, receiver_columns = call(
         local_kernel,
         [
@@ -643,7 +655,7 @@
     )
     parts = (2 * width, 3 * width // 2)
     halves = sum(parts)
-    pre_grad, sender_sum, receiver_sum, node_part, top, middle, bottom, keep, away, gains = call(
+    pre_grad, sender_sum, receiver_sum, node_part, inner, outer, middle, keep, away, gains = call(
         functools.partial(layer_kernel, tile_rows),
         [
             shaped(edge_rows, width, BF16),
@@ -651,11 +663,11 @@
             shaped(count, width, BF16),
             shaped(count, width, F32),
             shaped(3 * slots, width, BF16),
+            shaped(3 * slots, width, BF16),
             shaped(2 * slots, width, BF16),
-            shaped(3 * slots, width, BF16),
             shaped(halves, width, F32),
-            shaped(halves + 16, width, BF16),
-            shaped(16, width, BF16),
+            shaped(halves + PACKED, width, BF16),
+            shaped(PACKED, width, BF16),
         ],
         square * (6 * edge_rows + 11 * count + 2 * halo_rows)
         + 2 * edge_rows * (4 * count + halo_rows) * width,
@@ -669,10 +681,9 @@
         near_hot,
         sender_columns,
         receiver_columns,
-        from_high,
-        from_low,
-        upward,
-        downward,
+        straight,
+        along_core,
+        along_chip,
         w_edge_in,
         w_edge_out,
         gain_edge,
@@ -693,7 +704,7 @@
     members = square_members()
     own, *blocks = call(
         functools.partial(pair_kernel, parts),
-        [shaped(16 + halves // members, width, BF16)] * members,
+        [shaped(PACKED + halves // members, width, BF16)] * members,
         0,
         keep,
         gains,
@@ -708,16 +719,16 @@
             shaped(2 * slots, width, BF16),
         ],
         10**10,
-        passed_along(top, PX, 1),
+        in_pair(inner, PX),
+        out_of_pair(outer, PX),
         middle,
-        passed_along(bottom, PX, -1),
     )
     *received, along_core, along_chip = lax.optimization_barrier(
         (*received, along_core, along_chip)
     )
     (sums,) = call(sum_kernel, [like(own)], 0, own, *received)
     gains, mine, along_core, along_chip = joined(
-        sums, gains.shape[0], across_cores(along_core), across_chips(along_chip)
+        sums, gains.shape[0], across_cores(along_core), out_of_pair(along_chip, PY)
     )
     blocks = [mine] + [in_square(mine, offset) for offset in range(1, members)]
     gain_edge_grad = (gains[0] + gains[1]).astype(BF16)
@@ -742,7 +753,6 @@
         center,
         along_core,
         along_chip,
-        scratch=[pltpu.VMEM((halo_rows, width), BF16)],
     )
     done = (nodes_grad, edges_grad, gain_edge_grad, gain_node_grad)
     for i in range(members):

time: 50.5 us -> 51.4 us (1.018)
  waiting for transfers between devices: 12.2 us -> 15.3 us
  starting transfers between devices: 21.9 us -> 19.7 us
    ppermute x13, starting transfers between devices: 14 us -> 12 us  [the longest x4 7.99 us: out_of_pair(): lax.ppermute(array, axis, [(i, other_neighbour(i, size)) for i in range(s...]
    ppermute x6, waiting for transfers between devices: 6.84 us -> 8.5 us  [in_square(): lax.ppermute(array, SQUARE, [(i, i ^ offset) for i in range(square_member...]
    ppermute x1, waiting for transfers between devices: 2.76 us -> 3.63 us  [joined(): other = lax.ppermute(sums, FAR, [(i, i ^ distance) for i in range(size)])]
    ppermute x13, waiting for transfers between devices: 2.62 us -> 3.21 us  [the longest x4 1.89 us: out_of_pair(): lax.ppermute(array, axis, [(i, other_neighbour(i, size)) for i in range(s...]
    pallas_call x11 -> x12, Pallas kernels: 14.2 us -> 14.2 us  [call(): pl.pallas_call(body, out_shape=outs, in_specs=[pl.BlockSpec(memory_space=...]
  transfers between devices with their start and end apart: 20 -> 20, of which waited for: 9 -> 11; matrix products, arithmetic and copies ran while one was open for 1% -> 1% of each run, Pallas kernels for 12% -> 12%
where the time goes in v16:
time: 51.4 us; the launch traced here: 51.2 us
  starting transfers between devices  19.7 us (38%)
  waiting for transfers between devices  15.3 us (30%)
  Pallas kernels  14.2 us (28%)
  between operations  1.39 us (3%)
  other arithmetic  0.53 us (1%)
    pallas_call x12, Pallas kernels, call(): pl.pallas_call(body, out_shape=outs, in_specs=[pl.BlockSpec(memory_space=...  14.2 us
    ppermute x6, waiting for transfers between devices, in_square(): lax.ppermute(array, SQUARE, [(i, i ^ offset) for i in range(square_member...  8.5 us
    ppermute x4, starting transfers between devices, out_of_pair(): lax.ppermute(array, axis, [(i, other_neighbour(i, size)) for i in range(s...  7.99 us
    ppermute x6, starting transfers between devices, in_square(): lax.ppermute(array, SQUARE, [(i, i ^ offset) for i in range(square_member...  7.11 us
    ppermute x9, starting transfers between devices, in_pair(): lax.ppermute(array, axis, [(i, i ^ 1) for i in range(lax.axis_size(axis))])  3.97 us
    ppermute x1, waiting for transfers between devices, joined(): other = lax.ppermute(sums, FAR, [(i, i ^ distance) for i in range(size)])  3.63 us
    ppermute x4, waiting for transfers between devices, out_of_pair(): lax.ppermute(array, axis, [(i, other_neighbour(i, size)) for i in range(s...  1.89 us
    ppermute x9, waiting for transfers between devices, in_pair(): lax.ppermute(array, axis, [(i, i ^ 1) for i in range(lax.axis_size(axis))])  1.32 us
  transfers between devices with their start and end apart: 20, of which 11 were waited for; matrix products, arithmetic and copies ran while one was open for 1% of the time, Pallas kernels for 12%

profile of v16, /device:TPU:0, one launch (start us, length us, event | category | flops | bytes accessed | tf_op | source)
XLA Modules:
  0.0 51.2 jit_solution(1837677745851235930)
XLA Ops:
  0.6 1.3 %shard_map.197 = (bf16[96,256]{1,0:T(8,128)(2,1)S(1)}, bf16[96,256]{1,0:T(8,128)(2,1)S(1)}, bf16[64,256]{1,0:T(8,128)(2,1)S(1)}, bf16[384,256]{1,0:T(8,128)(2,1)S(1)}, s32[8,32]{1,0:T(8,128)S(1)}) custom-call(bf16[384,256]{1,0:T(8,128)(2,1)} %nodes_hbm.1, s32[8,32]{1,0:T(8,128)} %list_hbm.1), custom_call_target="tpu_custom_call" | custom-call | flops 50331648 | bytes 526336 | tf_op jit(solution)/shard_map/pallas_call | solution.py:492
  2.0 3.1 %collective-permute-start = (bf16[96,256]{1,0:T(8,128)(2,1)S(1)}, bf16[96,256]{1,0:T(8,128)(2,1)S(1)}, u32[]{:S(2)}, u32[]{:S(2)}) collective-permute-start(bf16[96,256]{1,0:T(8,128)(2,1)S(1)} %get-tuple-element.94), channel_id=1, source_target_pairs={{0,4},{4,0},{8,12},{12,8},{1,5},{5,1},{9,13},{13,9},{2,6},{6,2},{1... | collective-permute-start | bytes 147464 | tf_op jit(solution)/shard_map/ppermute | solution.py:30
  5.0 2.5 %collective-permute-start.1 = (bf16[96,256]{1,0:T(8,128)(2,1)S(1)}, bf16[96,256]{1,0:T(8,128)(2,1)S(1)}, u32[]{:S(2)}, u32[]{:S(2)}) collective-permute-start(bf16[96,256]{1,0:T(8,128)(2,1)S(1)} %get-tuple-element.95), channel_id=1, source_target_pairs={{0,12},{4,8},{8,4},{12,0},{1,13},{5,9},{9,5},{13,1},{2,14},{6,10},... | collective-permute-start | bytes 147464 | tf_op jit(solution)/shard_map/ppermute | solution.py:35
  8.2 1.7 %shard_map.198 = (bf16[1152,768]{1,0:T(8,128)(2,1)S(1)}, bf16[1152,256]{1,0:T(8,128)(2,1)S(1)}, s32[9,128]{1,0:T(8,128)S(1)}, s32[9,128]{1,0:T(8,128)S(1)}, bf16...) custom-call(s32[9,128]{1,0:T(8,128)} %refs_0_.1, ...), custom_call_target="tpu_custom_call" | custom-call | bytes 6967296 | tf_op jit(solution)/shard_map/pallas_call | solution.py:492
  9.9 0.0 collective-permute-done.inner
  9.9 1.0 %collective-permute-done.1.outer = bf16[96,256]{1,0:T(8,128)(2,1)S(1)} collective-permute-done((bf16[96,256]{1,0:T(8,128)(2,1)S(1)}, bf16[96,256]{1,0:T(8,128)(2,1)S(1)}, u32[]{:S(2)}, u32[]{:S(2)}) %collective-permute-start.1) | collective-permute-done | bytes 49184 | tf_op jit(solution)/shard_map/ppermute | solution.py:35
  11.0 0.1 collective-permute-start.2
  11.0 1.6 %collective-permute-start.3 = (bf16[96,256]{1,0:T(8,128)(2,1)S(1)}, bf16[96,256]{1,0:T(8,128)(2,1)S(1)}, u32[]{:S(2)}, u32[]{:S(2)}) collective-permute-start(bf16[96,256]{1,0:T(8,128)(2,1)S(1)} %get-tuple-element.108), channel_id=1, source_target_pairs={{0,3},{1,2},{2,1},{3,0},{4,7},{5,6},{6,5},{7,4},{8,11},{9,10},{10,... | collective-permute-start | bytes 147464 | tf_op jit(solution)/shard_map/ppermute | solution.py:35
  12.6 1.8 %shard_map.199 = (f32[1152,256]{1,0:T(8,128)S(1)}, bf16[640,1152]{1,0:T(8,128)(2,1)S(1)}, bf16[384,1152]{1,0:T(8,128)(2,1)S(1)}) custom-call(bf16[384,256]{1,0:T(8,128)(2,1)S(1)} %get-tuple-element.88.nodes, bf16[1152,256]{1,0:T(8,128)(2,1)S(1)} %get-tuple-element.90.edges, s32[9,128]{1,0:T(8,128)S(1)} %get-tuple-element.92.senders, ...), custom_call_target="tpu_custom_call" | custom-call | flops 704643072 | bytes 6497280 | tf_op jit(solution)/shard_map/pallas_call | solution.py:492
  14.5 0.0 collective-permute-done.2.along_core
  14.5 0.1 collective-permute-done.3.along_chip
  14.6 5.6 %shard_map.201 = (bf16[1152,256]{1,0:T(8,128)(2,1)S(1)}, bf16[384,256]{1,0:T(8,128)(2,1)S(1)}, bf16[384,256]{1,0:T(8,128)(2,1)S(1)}, f32[384,256]{1,0:T(8,128)S(...) custom-call(s32[1]{0:T(128)S(6)} %copy.22.count_ref, ...), custom_call_target="tpu_custom_call" | custom-call | flops 2583691264 | bytes 11412484 | tf_op jit(solution)/shard_map/pallas_call | solution.py:492
  20.2 0.5 %collective-permute-start.4 = (bf16[904,256]{1,0:T(8,128)(2,1)S(1)}, bf16[904,256]{1,0:T(8,128)(2,1)S(1)}, u32[]{:S(2)}, u32[]{:S(2)}) collective-permute-start(bf16[904,256]{1,0:T(8,128)(2,1)S(1)} %get-tuple-element.116), channel_id=1, source_target_pairs={{0,1},{1,0},{2,3},{3,2},{4,5},{5,4},{6,7},{7,6},{8,9},{9,8},{10,11... | collective-permute-start | bytes 1388552 | tf_op jit(solution)/shard_map/ppermute | solution.py:30
  20.7 0.0 collective-permute-start.8
  20.7 2.5 %collective-permute-start.9 = (bf16[96,256]{1,0:T(8,128)(2,1)S(1)}, bf16[96,256]{1,0:T(8,128)(2,1)S(1)}, u32[]{:S(2)}, u32[]{:S(2)}) collective-permute-start(bf16[96,256]{1,0:T(8,128)(2,1)S(1)} %get-tuple-element.122), channel_id=1, source_target_pairs={{0,12},{4,8},{8,4},{12,0},{1,13},{5,9},{9,5},{13,1},{2,14},{6,10},... | collective-permute-start | bytes 147464 | tf_op jit(solution)/shard_map/ppermute | solution.py:35
  23.2 0.0 collective-permute-done.4.other
  23.2 0.1 shard_map.202
  23.3 1.6 %collective-permute-start.5 = (bf16[232,256]{1,0:T(8,128)(2,1)S(1)}, bf16[232,256]{1,0:T(8,128)(2,1)S(1)}, u32[]{:S(2)}, u32[]{:S(2)}) collective-permute-start(bf16[232,256]{1,0:T(8,128)(2,1)S(1)} %get-tuple-element.118), channel_id=1, source_target_pairs={{0,2},{2,0},{4,6},{6,4},{1,3},{3,1},{5,7},{7,5},{8,10},{10,8},{12,... | collective-permute-start | bytes 356360 | tf_op jit(solution)/shard_map/ppermute | solution.py:48
  24.9 1.1 %collective-permute-start.6 = (bf16[232,256]{1,0:T(8,128)(2,1)S(1)}, bf16[232,256]{1,0:T(8,128)(2,1)S(1)}, u32[]{:S(2)}, u32[]{:S(2)}) collective-permute-start(bf16[232,256]{1,0:T(8,128)(2,1)S(1)} %get-tuple-element.119), channel_id=1, source_target_pairs={{0,4},{2,6},{4,0},{6,2},{1,5},{3,7},{5,1},{7,3},{8,12},{10,14},{12... | collective-permute-start | bytes 356360 | tf_op jit(solution)/shard_map/ppermute | solution.py:48
  26.0 0.9 %collective-permute-start.7 = (bf16[232,256]{1,0:T(8,128)(2,1)S(1)}, bf16[232,256]{1,0:T(8,128)(2,1)S(1)}, u32[]{:S(2)}, u32[]{:S(2)}) collective-permute-start(bf16[232,256]{1,0:T(8,128)(2,1)S(1)} %get-tuple-element.120), channel_id=1, source_target_pairs={{0,6},{2,4},{4,2},{6,0},{1,7},{3,5},{5,3},{7,1},{8,14},{10,12},{12... | collective-permute-start | bytes 356360 | tf_op jit(solution)/shard_map/ppermute | solution.py:48
  26.9 0.0 collective-permute-done.8.inner
  26.9 0.0 collective-permute-done.9.outer
  26.9 1.5 %collective-permute-done.5.refs_1_ = bf16[232,256]{1,0:T(8,128)(2,1)S(1)} collective-permute-done((bf16[232,256]{1,0:T(8,128)(2,1)S(1)}, bf16[232,256]{1,0:T(8,128)(2,1)S(1)}, u32[]{:S(2)}, u32[]{:S(2)}) %collective-permute-start.5) | collective-permute-done | bytes 118816 | tf_op jit(solution)/shard_map/ppermute | solution.py:48
  28.4 2.5 %collective-permute-done.6.refs_2_ = bf16[232,256]{1,0:T(8,128)(2,1)S(1)} collective-permute-done((bf16[232,256]{1,0:T(8,128)(2,1)S(1)}, bf16[232,256]{1,0:T(8,128)(2,1)S(1)}, u32[]{:S(2)}, u32[]{:S(2)}) %collective-permute-start.6) | collective-permute-done | bytes 118816 | tf_op jit(solution)/shard_map/ppermute | solution.py:48
  30.9 1.7 %collective-permute-done.7.refs_3_ = bf16[232,256]{1,0:T(8,128)(2,1)S(1)} collective-permute-done((bf16[232,256]{1,0:T(8,128)(2,1)S(1)}, bf16[232,256]{1,0:T(8,128)(2,1)S(1)}, u32[]{:S(2)}, u32[]{:S(2)}) %collective-permute-start.7) | collective-permute-done | bytes 118816 | tf_op jit(solution)/shard_map/ppermute | solution.py:48
  32.6 0.1 shard_map.204.own
  32.7 0.7 %collective-permute-start.10 = (bf16[232,256]{1,0:T(8,128)(2,1)S(1)}, bf16[232,256]{1,0:T(8,128)(2,1)S(1)}, u32[]{:S(2)}, u32[]{:S(2)}) collective-permute-start(bf16[232,256]{1,0:T(8,128)(2,1)S(1)} %shard_map.204.own), channel_id=1, source_target_pairs={{0,8},{8,0},{1,9},{9,1},{2,10},{10,2},{3,11},{11,3},{4,12},{12,4},... | collective-permute-start | bytes 356360 | tf_op jit(solution)/shard_map/ppermute | solution.py:533
  33.4 0.0 collective-permute-start.11
  33.4 1.4 %collective-permute-start.12 = (bf16[96,256]{1,0:T(8,128)(2,1)S(1)}, bf16[96,256]{1,0:T(8,128)(2,1)S(1)}, u32[]{:S(2)}, u32[]{:S(2)}) collective-permute-start(bf16[96,256]{1,0:T(8,128)(2,1)S(1)} %get-tuple-element.130), channel_id=1, source_target_pairs={{0,3},{1,2},{2,1},{3,0},{4,7},{5,6},{6,5},{7,4},{8,11},{9,10},{10,... | collective-permute-start | bytes 147464 | tf_op jit(solution)/shard_map/ppermute | solution.py:35
  34.8 1.3 %shard_map.206 = (bf16[1152,256]{1,0:T(8,128)(2,1)}, f32[384,256]{1,0:T(8,128)S(1)}) custom-call(bf16[1152,256]{1,0:T(8,128)(2,1)S(1)} %get-tuple-element.91.edge_grads, bf16[1152,256]{1,0:T(8,128)(2,1)S(1)} %get-tuple-element.134.pre_grad, bf16[384,256]{1,0:T(8,128)(2,1)S(1)} %get-tuple-element.135.sender_sum, ...), custom_call_target="tpu_custom_call" | custom-call | flops 251658240 | bytes 3342336 | tf_op jit(solution)/shard_map/pallas_call | solution.py:492
  36.1 0.0 collective-permute-done.11.along_core
  36.1 0.7 %collective-permute-done.12.along_chip = bf16[96,256]{1,0:T(8,128)(2,1)S(1)} collective-permute-done((bf16[96,256]{1,0:T(8,128)(2,1)S(1)}, bf16[96,256]{1,0:T(8,128)(2,1)S(1)}, u32[]{:S(2)}, u32[]{:S(2)}) %collective-permute-start.12) | collective-permute-done | bytes 49184 | tf_op jit(solution)/shard_map/ppermute | solution.py:35
  36.9 3.6 %collective-permute-done.10.other = bf16[232,256]{1,0:T(8,128)(2,1)S(1)} collective-permute-done((bf16[232,256]{1,0:T(8,128)(2,1)S(1)}, bf16[232,256]{1,0:T(8,128)(2,1)S(1)}, u32[]{:S(2)}, u32[]{:S(2)}) %collective-permute-start.10) | collective-permute-done | bytes 118816 | tf_op jit(solution)/shard_map/ppermute | solution.py:533
  40.6 0.3 collective-permute-start.15
  40.9 0.0 collective-permute-start.14
  40.9 3.2 %collective-permute-start.13 = (bf16[224,256]{1,0:T(8,128)(2,1)S(1)}, bf16[224,256]{1,0:T(8,128)(2,1)S(1)}, u32[]{:S(2)}, u32[]{:S(2)}) collective-permute-start(bf16[224,256]{1,0:T(8,128)(2,1)S(1)} %get-tuple-element.158.refs_0_), channel_id=1, source_target_pairs={{0,6},{2,4},{4,2},{6,0},{1,7},{3,5},{5,3},{7,1},{8,14},{10,12},{12... | collective-permute-start | bytes 344072 | tf_op jit(solution)/shard_map/ppermute | solution.py:48
  44.1 1.1 %shard_map.207 = bf16[384,256]{1,0:T(8,128)(2,1)} custom-call(s32[8,32]{1,0:T(8,128)S(1)} %get-tuple-element.133.send_list, f32[384,256]{1,0:T(8,128)S(1)} %get-tuple-element.138.local_grad, bf16[64,256]{1,0:T(8,128)(2,1)S(1)} %get-tuple-element.139.center, bf16[96,256]{1,0:T(8,128)(2,1)S(1)} %collective-permute-done.11.along_core, ...), custom_call_target="tpu_custom_call" | custom-call | flops 50331648 | bytes 721920 | tf_op jit(solution)/shard_map/pallas_call | solution.py:492
  45.2 0.5 %convert_reduce_fusion = (bf16[256]{0:T(256)(128)(2,1)}, bf16[256]{0:T(256)(128)(2,1)}) fusion(f32[8,256]{1,0:T(8,128)S(1)} %get-tuple-element.143), kind=kLoop, calls=%fused_computation | loop fusion | flops 1024 | bytes 5120 | tf_op jit(solution)/shard_map/convert_element_type | solution.py:735
  45.8 0.0 collective-permute-start.16
  45.8 0.5 collective-permute-done.15.refs_1_
  46.2 0.1 collective-permute-start.17
  46.3 0.2 collective-permute-done.14.refs_2_
  46.5 0.2 collective-permute-start.18
  46.7 2.1 %collective-permute-done.13.refs_3_ = bf16[224,256]{1,0:T(8,128)(2,1)S(1)} collective-permute-done((bf16[224,256]{1,0:T(8,128)(2,1)S(1)}, bf16[224,256]{1,0:T(8,128)(2,1)S(1)}, u32[]{:S(2)}, u32[]{:S(2)}) %collective-permute-start.13) | collective-permute-done | bytes 114720 | tf_op jit(solution)/shard_map/ppermute | solution.py:48
  48.8 0.0 collective-permute-start.19
  48.8 0.0 collective-permute-done.16.refs_4_
  48.9 0.0 collective-permute-done.17.refs_5_
  48.9 0.0 collective-permute-done.18.refs_6_
  48.9 1.3 %collective-permute-done.19.refs_7_ = bf16[224,256]{1,0:T(8,128)(2,1)S(1)} collective-permute-done((bf16[224,256]{1,0:T(8,128)(2,1)S(1)}, bf16[224,256]{1,0:T(8,128)(2,1)S(1)}, u32[]{:S(2)}, u32[]{:S(2)}) %collective-permute-start.19) | collective-permute-done | bytes 114720 | tf_op jit(solution)/shard_map/ppermute | solution.py:30
  50.2 1.0 %shard_map.208 = (bf16[768,256]{1,0:T(8,128)(2,1)}, bf16[256,256]{1,0:T(8,128)(2,1)}, bf16[512,256]{1,0:T(8,128)(2,1)}, bf16[256,256]{1,0:T(8,128)(2,1)}) custom-call(bf16[224,256]{1,0:T(8,128)(2,1)S(1)} %get-tuple-element.158.refs_0_, bf16[224,256]{1,0:T(8,128)(2,1)S(1)} %collective-permute-done.15.refs_1_, ...), custom_call_target="tpu_custom_call" | custom-call | bytes 1835008 | tf_op jit(solution)/shard_map/pallas_call | solution.py:492
  (3 shorter events, 0.1 us)
Async XLA Ops:
  2.0 8.0 %collective-permute-start = (bf16[96,256]{1,0:T(8,128)(2,1)S(1)}, bf16[96,256]{1,0:T(8,128)(2,1)S(1)}, u32[]{:S(2)}, u32[]{:S(2)}) collective-permute-start(bf16[96,256]{1,0:T(8,128)(2,1)S(1)} %get-tuple-element.94), channel_id=1, source_target_pairs={{0,4},{4,0},{8,12},{12,8},{1,5},{5,1},{9,13},{13,9},{2,6},{6,2},{1... | collective-permute-start | bytes 147464 | tf_op jit(solution)/shard_map/ppermute | solution.py:30
  5.0 5.9 %collective-permute-start.1 = (bf16[96,256]{1,0:T(8,128)(2,1)S(1)}, bf16[96,256]{1,0:T(8,128)(2,1)S(1)}, u32[]{:S(2)}, u32[]{:S(2)}) collective-permute-start(bf16[96,256]{1,0:T(8,128)(2,1)S(1)} %get-tuple-element.95), channel_id=1, source_target_pairs={{0,12},{4,8},{8,4},{12,0},{1,13},{5,9},{9,5},{13,1},{2,14},{6,10},... | collective-permute-start | bytes 147464 | tf_op jit(solution)/shard_map/ppermute | solution.py:35
  11.0 3.5 %collective-permute-start.2 = (bf16[96,256]{1,0:T(8,128)(2,1)S(1)}, bf16[96,256]{1,0:T(8,128)(2,1)S(1)}, u32[]{:S(2)}, u32[]{:S(2)}) collective-permute-start(bf16[96,256]{1,0:T(8,128)(2,1)S(1)} %get-tuple-element.107), channel_id=1, source_target_pairs={{0,1},{1,0},{2,3},{3,2},{4,5},{5,4},{6,7},{7,6},{8,9},{9,8},{10,11... | collective-permute-start | bytes 147464 | tf_op jit(solution)/shard_map/ppermute | solution.py:30
  11.0 3.6 %collective-permute-start.3 = (bf16[96,256]{1,0:T(8,128)(2,1)S(1)}, bf16[96,256]{1,0:T(8,128)(2,1)S(1)}, u32[]{:S(2)}, u32[]{:S(2)}) collective-permute-start(bf16[96,256]{1,0:T(8,128)(2,1)S(1)} %get-tuple-element.108), channel_id=1, source_target_pairs={{0,3},{1,2},{2,1},{3,0},{4,7},{5,6},{6,5},{7,4},{8,11},{9,10},{10,... | collective-permute-start | bytes 147464 | tf_op jit(solution)/shard_map/ppermute | solution.py:35
  20.2 3.0 %collective-permute-start.4 = (bf16[904,256]{1,0:T(8,128)(2,1)S(1)}, bf16[904,256]{1,0:T(8,128)(2,1)S(1)}, u32[]{:S(2)}, u32[]{:S(2)}) collective-permute-start(bf16[904,256]{1,0:T(8,128)(2,1)S(1)} %get-tuple-element.116), channel_id=1, source_target_pairs={{0,1},{1,0},{2,3},{3,2},{4,5},{5,4},{6,7},{7,6},{8,9},{9,8},{10,11... | collective-permute-start | bytes 1388552 | tf_op jit(solution)/shard_map/ppermute | solution.py:30
  20.7 6.2 %collective-permute-start.8 = (bf16[96,256]{1,0:T(8,128)(2,1)S(1)}, bf16[96,256]{1,0:T(8,128)(2,1)S(1)}, u32[]{:S(2)}, u32[]{:S(2)}) collective-permute-start(bf16[96,256]{1,0:T(8,128)(2,1)S(1)} %get-tuple-element.121), channel_id=1, source_target_pairs={{0,4},{4,0},{8,12},{12,8},{1,5},{5,1},{9,13},{13,9},{2,6},{6,2},{1... | collective-permute-start | bytes 147464 | tf_op jit(solution)/shard_map/ppermute | solution.py:30
  20.7 6.2 %collective-permute-start.9 = (bf16[96,256]{1,0:T(8,128)(2,1)S(1)}, bf16[96,256]{1,0:T(8,128)(2,1)S(1)}, u32[]{:S(2)}, u32[]{:S(2)}) collective-permute-start(bf16[96,256]{1,0:T(8,128)(2,1)S(1)} %get-tuple-element.122), channel_id=1, source_target_pairs={{0,12},{4,8},{8,4},{12,0},{1,13},{5,9},{9,5},{13,1},{2,14},{6,10},... | collective-permute-start | bytes 147464 | tf_op jit(solution)/shard_map/ppermute | solution.py:35
  23.3 5.1 %collective-permute-start.5 = (bf16[232,256]{1,0:T(8,128)(2,1)S(1)}, bf16[232,256]{1,0:T(8,128)(2,1)S(1)}, u32[]{:S(2)}, u32[]{:S(2)}) collective-permute-start(bf16[232,256]{1,0:T(8,128)(2,1)S(1)} %get-tuple-element.118), channel_id=1, source_target_pairs={{0,2},{2,0},{4,6},{6,4},{1,3},{3,1},{5,7},{7,5},{8,10},{10,8},{12,... | collective-permute-start | bytes 356360 | tf_op jit(solution)/shard_map/ppermute | solution.py:48
  24.9 6.0 %collective-permute-start.6 = (bf16[232,256]{1,0:T(8,128)(2,1)S(1)}, bf16[232,256]{1,0:T(8,128)(2,1)S(1)}, u32[]{:S(2)}, u32[]{:S(2)}) collective-permute-start(bf16[232,256]{1,0:T(8,128)(2,1)S(1)} %get-tuple-element.119), channel_id=1, source_target_pairs={{0,4},{2,6},{4,0},{6,2},{1,5},{3,7},{5,1},{7,3},{8,12},{10,14},{12... | collective-permute-start | bytes 356360 | tf_op jit(solution)/shard_map/ppermute | solution.py:48
  26.0 6.6 %collective-permute-start.7 = (bf16[232,256]{1,0:T(8,128)(2,1)S(1)}, bf16[232,256]{1,0:T(8,128)(2,1)S(1)}, u32[]{:S(2)}, u32[]{:S(2)}) collective-permute-start(bf16[232,256]{1,0:T(8,128)(2,1)S(1)} %get-tuple-element.120), channel_id=1, source_target_pairs={{0,6},{2,4},{4,2},{6,0},{1,7},{3,5},{5,3},{7,1},{8,14},{10,12},{12... | collective-permute-start | bytes 356360 | tf_op jit(solution)/shard_map/ppermute | solution.py:48
  32.7 7.8 %collective-permute-start.10 = (bf16[232,256]{1,0:T(8,128)(2,1)S(1)}, bf16[232,256]{1,0:T(8,128)(2,1)S(1)}, u32[]{:S(2)}, u32[]{:S(2)}) collective-permute-start(bf16[232,256]{1,0:T(8,128)(2,1)S(1)} %shard_map.204.own), channel_id=1, source_target_pairs={{0,8},{8,0},{1,9},{9,1},{2,10},{10,2},{3,11},{11,3},{4,12},{12,4},... | collective-permute-start | bytes 356360 | tf_op jit(solution)/shard_map/ppermute | solution.py:533
  33.4 2.8 %collective-permute-start.11 = (bf16[96,256]{1,0:T(8,128)(2,1)S(1)}, bf16[96,256]{1,0:T(8,128)(2,1)S(1)}, u32[]{:S(2)}, u32[]{:S(2)}) collective-permute-start(bf16[96,256]{1,0:T(8,128)(2,1)S(1)} %get-tuple-element.129), channel_id=1, source_target_pairs={{0,1},{1,0},{2,3},{3,2},{4,5},{5,4},{6,7},{7,6},{8,9},{9,8},{10,11... | collective-permute-start | bytes 147464 | tf_op jit(solution)/shard_map/ppermute | solution.py:30
  33.4 3.5 %collective-permute-start.12 = (bf16[96,256]{1,0:T(8,128)(2,1)S(1)}, bf16[96,256]{1,0:T(8,128)(2,1)S(1)}, u32[]{:S(2)}, u32[]{:S(2)}) collective-permute-start(bf16[96,256]{1,0:T(8,128)(2,1)S(1)} %get-tuple-element.130), channel_id=1, source_target_pairs={{0,3},{1,2},{2,1},{3,0},{4,7},{5,6},{6,5},{7,4},{8,11},{9,10},{10,... | collective-permute-start | bytes 147464 | tf_op jit(solution)/shard_map/ppermute | solution.py:35
  40.6 5.7 %collective-permute-start.15 = (bf16[224,256]{1,0:T(8,128)(2,1)S(1)}, bf16[224,256]{1,0:T(8,128)(2,1)S(1)}, u32[]{:S(2)}, u32[]{:S(2)}) collective-permute-start(bf16[224,256]{1,0:T(8,128)(2,1)S(1)} %get-tuple-element.158.refs_0_), channel_id=1, source_target_pairs={{0,2},{2,0},{4,6},{6,4},{1,3},{3,1},{5,7},{7,5},{8,10},{10,8},{12,... | collective-permute-start | bytes 344072 | tf_op jit(solution)/shard_map/ppermute | solution.py:48
  40.9 5.6 %collective-permute-start.14 = (bf16[224,256]{1,0:T(8,128)(2,1)S(1)}, bf16[224,256]{1,0:T(8,128)(2,1)S(1)}, u32[]{:S(2)}, u32[]{:S(2)}) collective-permute-start(bf16[224,256]{1,0:T(8,128)(2,1)S(1)} %get-tuple-element.158.refs_0_), channel_id=1, source_target_pairs={{0,4},{2,6},{4,0},{6,2},{1,5},{3,7},{5,1},{7,3},{8,12},{10,14},{12... | collective-permute-start | bytes 344072 | tf_op jit(solution)/shard_map/ppermute | solution.py:48
  40.9 8.0 %collective-permute-start.13 = (bf16[224,256]{1,0:T(8,128)(2,1)S(1)}, bf16[224,256]{1,0:T(8,128)(2,1)S(1)}, u32[]{:S(2)}, u32[]{:S(2)}) collective-permute-start(bf16[224,256]{1,0:T(8,128)(2,1)S(1)} %get-tuple-element.158.refs_0_), channel_id=1, source_target_pairs={{0,6},{2,4},{4,2},{6,0},{1,7},{3,5},{5,3},{7,1},{8,14},{10,12},{12... | collective-permute-start | bytes 344072 | tf_op jit(solution)/shard_map/ppermute | solution.py:48
  45.8 3.1 %collective-permute-start.16 = (bf16[224,256]{1,0:T(8,128)(2,1)S(1)}, bf16[224,256]{1,0:T(8,128)(2,1)S(1)}, u32[]{:S(2)}, u32[]{:S(2)}) collective-permute-start(bf16[224,256]{1,0:T(8,128)(2,1)S(1)} %get-tuple-element.158.refs_0_), channel_id=1, source_target_pairs={{0,1},{1,0},{2,3},{3,2},{4,5},{5,4},{6,7},{7,6},{8,9},{9,8},{10,11... | collective-permute-start | bytes 344072 | tf_op jit(solution)/shard_map/ppermute | solution.py:30
  46.2 2.6 %collective-permute-start.17 = (bf16[224,256]{1,0:T(8,128)(2,1)S(1)}, bf16[224,256]{1,0:T(8,128)(2,1)S(1)}, u32[]{:S(2)}, u32[]{:S(2)}) collective-permute-start(bf16[224,256]{1,0:T(8,128)(2,1)S(1)} %collective-permute-done.15.refs_1_), channel_id=1, source_target_pairs={{0,1},{1,0},{2,3},{3,2},{4,5},{5,4},{6,7},{7,6},{8,9},{9,8},{10,11... | collective-permute-start | bytes 344072 | tf_op jit(solution)/shard_map/ppermute | solution.py:30
  46.5 2.3 %collective-permute-start.18 = (bf16[224,256]{1,0:T(8,128)(2,1)S(1)}, bf16[224,256]{1,0:T(8,128)(2,1)S(1)}, u32[]{:S(2)}, u32[]{:S(2)}) collective-permute-start(bf16[224,256]{1,0:T(8,128)(2,1)S(1)} %collective-permute-done.14.refs_2_), channel_id=1, source_target_pairs={{0,1},{1,0},{2,3},{3,2},{4,5},{5,4},{6,7},{7,6},{8,9},{9,8},{10,11... | collective-permute-start | bytes 344072 | tf_op jit(solution)/shard_map/ppermute | solution.py:30
  48.8 1.3 %collective-permute-start.19 = (bf16[224,256]{1,0:T(8,128)(2,1)S(1)}, bf16[224,256]{1,0:T(8,128)(2,1)S(1)}, u32[]{:S(2)}, u32[]{:S(2)}) collective-permute-start(bf16[224,256]{1,0:T(8,128)(2,1)S(1)} %collective-permute-done.13.refs_3_), channel_id=1, source_target_pairs={{0,1},{1,0},{2,3},{3,2},{4,5},{5,4},{6,7},{7,6},{8,9},{9,8},{10,11... | collective-permute-start | bytes 344072 | tf_op jit(solution)/shard_map/ppermute | solution.py:30

commit v17 on v16

--- a/solution.py
+++ b/solution.py
@@ -480,7 +480,15 @@
 HBM = pltpu.HBM
 
 
-def call(body, outs, flops, *operands, spaces=(), out_space=VMEM, scratch=()):
+def call(body, outs, flops, *operands, spaces=(), out_space=VMEM, scratch=(), after=()):
+    if after:
+        first, rest = len(operands), len(operands) + len(after)
+        inner = body
+
+        def body(*refs):
+            inner(*refs[:first], *refs[rest:])
+
+        operands = operands + tuple(after)
     moved = sum(x.size * x.dtype.itemsize for x in operands)
     moved += sum(x.size * jnp.dtype(x.dtype).itemsize for x in outs)
     spaces = list(spaces) + [VMEM] * (len(operands) - len(spaces))
@@ -711,28 +719,7 @@
         other,
     )
     received = [in_square(block, offset) for offset, block in enumerate(blocks, 1)]
-    along_core, along_chip, center = call(
-        turn_kernel,
-        [
-            shaped(3 * slots, width, BF16),
-            shaped(3 * slots, width, BF16),
-            shaped(2 * slots, width, BF16),
-        ],
-        10**10,
-        in_pair(inner, PX),
-        out_of_pair(outer, PX),
-        middle,
-    )
-    *received, along_core, along_chip = lax.optimization_barrier(
-        (*received, along_core, along_chip)
-    )
     (sums,) = call(sum_kernel, [like(own)], 0, own, *received)
-    gains, mine, along_core, along_chip = joined(
-        sums, gains.shape[0], across_cores(along_core), out_of_pair(along_chip, PY)
-    )
-    blocks = [mine] + [in_square(mine, offset) for offset in range(1, members)]
-    gain_edge_grad = (gains[0] + gains[1]).astype(BF16)
-    gain_node_grad = (gains[2] + gains[3]).astype(BF16)
     edges_grad, local_grad = call(
         finish_kernel,
         [shaped(edge_rows, width, BF16), shaped(count, width, F32)],
@@ -744,6 +731,25 @@
         node_part,
         w_edge_in,
     )
+    along_core, along_chip, center = call(
+        turn_kernel,
+        [
+            shaped(3 * slots, width, BF16),
+            shaped(3 * slots, width, BF16),
+            shaped(2 * slots, width, BF16),
+        ],
+        10**10,
+        in_pair(inner, PX),
+        out_of_pair(outer, PX),
+        middle,
+        after=[sums],
+    )
+    gains, mine, along_core, along_chip = joined(
+        sums, gains.shape[0], across_cores(along_core), out_of_pair(along_chip, PY)
+    )
+    blocks = [mine] + [in_square(mine, offset) for offset in range(1, members)]
+    gain_edge_grad = (gains[0] + gains[1]).astype(BF16)
+    gain_node_grad = (gains[2] + gains[3]).astype(BF16)
     (nodes_grad,) = call(
         return_kernel,
         [shaped(count, width, BF16)],

time: 51.4 us -> 50.6 us (0.984)
  waiting for transfers between devices: 15.3 us -> 13.8 us
  starting transfers between devices: 19.7 us -> 20.5 us
    ppermute x1, waiting for transfers between devices: 3.63 us -> 1.3 us  [joined(): other = lax.ppermute(sums, FAR, [(i, i ^ distance) for i in range(size)])]
    ppermute x6, waiting for transfers between devices: 8.5 us -> 6.51 us  [in_square(): lax.ppermute(array, SQUARE, [(i, i ^ offset) for i in range(square_member...]
    ppermute x9, waiting for transfers between devices: 1.32 us -> 2.77 us  [in_pair(): lax.ppermute(array, axis, [(i, i ^ 1) for i in range(lax.axis_size(axis))])]
    ppermute x4, waiting for transfers between devices: 1.89 us -> 3.24 us  [out_of_pair(): lax.ppermute(array, axis, [(i, other_neighbour(i, size)) for i in range(s...]
    ppermute x1, starting transfers between devices: 0.68 us -> 1.87 us  [joined(): other = lax.ppermute(sums, FAR, [(i, i ^ distance) for i in range(size)])]
    ppermute x4, starting transfers between devices: 7.99 us -> 7.2 us  [out_of_pair(): lax.ppermute(array, axis, [(i, other_neighbour(i, size)) for i in range(s...]
where the time goes in v17:
time: 50.6 us; the launch traced here: 50.4 us
  starting transfers between devices  20.5 us (41%)
  Pallas kernels  14.2 us (28%)
  waiting for transfers between devices  13.8 us (27%)
  between operations  1.4 us (3%)
  other arithmetic  0.53 us (1%)
    pallas_call x12, Pallas kernels, call(): pl.pallas_call(body, out_shape=outs, in_specs=[pl.BlockSpec(memory_space=...  14.2 us
    ppermute x4, starting transfers between devices, out_of_pair(): lax.ppermute(array, axis, [(i, other_neighbour(i, size)) for i in range(s...  7.2 us
    ppermute x6, starting transfers between devices, in_square(): lax.ppermute(array, SQUARE, [(i, i ^ offset) for i in range(square_member...  7.12 us
    ppermute x6, waiting for transfers between devices, in_square(): lax.ppermute(array, SQUARE, [(i, i ^ offset) for i in range(square_member...  6.51 us
    ppermute x9, starting transfers between devices, in_pair(): lax.ppermute(array, axis, [(i, i ^ 1) for i in range(lax.axis_size(axis))])  4.3 us
    ppermute x4, waiting for transfers between devices, out_of_pair(): lax.ppermute(array, axis, [(i, other_neighbour(i, size)) for i in range(s...  3.24 us
    ppermute x9, waiting for transfers between devices, in_pair(): lax.ppermute(array, axis, [(i, i ^ 1) for i in range(lax.axis_size(axis))])  2.77 us
    ppermute x1, starting transfers between devices, joined(): other = lax.ppermute(sums, FAR, [(i, i ^ distance) for i in range(size)])  1.87 us
  transfers between devices with their start and end apart: 20, of which 11 were waited for; matrix products, arithmetic and copies ran while one was open for 1% of the time, Pallas kernels for 12%

profile of v17, /device:TPU:0, one launch (start us, length us, event | category | flops | bytes accessed | tf_op | source)
XLA Modules:
  0.0 50.4 jit_solution(5768632919168169835)
XLA Ops:
  0.6 1.3 %shard_map.197 = (bf16[96,256]{1,0:T(8,128)(2,1)S(1)}, bf16[96,256]{1,0:T(8,128)(2,1)S(1)}, bf16[64,256]{1,0:T(8,128)(2,1)S(1)}, bf16[384,256]{1,0:T(8,128)(2,1)S(1)}, s32[8,32]{1,0:T(8,128)S(1)}) custom-call(bf16[384,256]{1,0:T(8,128)(2,1)} %nodes_hbm.1, s32[8,32]{1,0:T(8,128)} %list_hbm.1), custom_call_target="tpu_custom_call" | custom-call | flops 50331648 | bytes 526336 | tf_op jit(solution)/shard_map/pallas_call | solution.py:500
  2.0 3.1 %collective-permute-start = (bf16[96,256]{1,0:T(8,128)(2,1)S(1)}, bf16[96,256]{1,0:T(8,128)(2,1)S(1)}, u32[]{:S(2)}, u32[]{:S(2)}) collective-permute-start(bf16[96,256]{1,0:T(8,128)(2,1)S(1)} %get-tuple-element.89), channel_id=1, source_target_pairs={{0,4},{4,0},{8,12},{12,8},{1,5},{5,1},{9,13},{13,9},{2,6},{6,2},{1... | collective-permute-start | bytes 147464 | tf_op jit(solution)/shard_map/ppermute | solution.py:30
  5.0 2.5 %collective-permute-start.1 = (bf16[96,256]{1,0:T(8,128)(2,1)S(1)}, bf16[96,256]{1,0:T(8,128)(2,1)S(1)}, u32[]{:S(2)}, u32[]{:S(2)}) collective-permute-start(bf16[96,256]{1,0:T(8,128)(2,1)S(1)} %get-tuple-element.90), channel_id=1, source_target_pairs={{0,12},{4,8},{8,4},{12,0},{1,13},{5,9},{9,5},{13,1},{2,14},{6,10},... | collective-permute-start | bytes 147464 | tf_op jit(solution)/shard_map/ppermute | solution.py:35
  8.2 1.7 %shard_map.198 = (bf16[1152,768]{1,0:T(8,128)(2,1)S(1)}, bf16[1152,256]{1,0:T(8,128)(2,1)S(1)}, s32[9,128]{1,0:T(8,128)S(1)}, s32[9,128]{1,0:T(8,128)S(1)}, bf16...) custom-call(s32[9,128]{1,0:T(8,128)} %refs_0_.1, ...), custom_call_target="tpu_custom_call" | custom-call | bytes 6967296 | tf_op jit(solution)/shard_map/pallas_call | solution.py:500
  9.9 0.0 collective-permute-done.inner
  9.9 1.0 %collective-permute-done.1.outer = bf16[96,256]{1,0:T(8,128)(2,1)S(1)} collective-permute-done((bf16[96,256]{1,0:T(8,128)(2,1)S(1)}, bf16[96,256]{1,0:T(8,128)(2,1)S(1)}, u32[]{:S(2)}, u32[]{:S(2)}) %collective-permute-start.1) | collective-permute-done | bytes 49184 | tf_op jit(solution)/shard_map/ppermute | solution.py:35
  11.0 0.1 collective-permute-start.2
  11.0 1.6 %collective-permute-start.3 = (bf16[96,256]{1,0:T(8,128)(2,1)S(1)}, bf16[96,256]{1,0:T(8,128)(2,1)S(1)}, u32[]{:S(2)}, u32[]{:S(2)}) collective-permute-start(bf16[96,256]{1,0:T(8,128)(2,1)S(1)} %get-tuple-element.103), channel_id=1, source_target_pairs={{0,3},{1,2},{2,1},{3,0},{4,7},{5,6},{6,5},{7,4},{8,11},{9,10},{10,... | collective-permute-start | bytes 147464 | tf_op jit(solution)/shard_map/ppermute | solution.py:35
  12.6 1.8 %shard_map.199 = (f32[1152,256]{1,0:T(8,128)S(1)}, bf16[640,1152]{1,0:T(8,128)(2,1)S(1)}, bf16[384,1152]{1,0:T(8,128)(2,1)S(1)}) custom-call(bf16[384,256]{1,0:T(8,128)(2,1)S(1)} %get-tuple-element.83.nodes, bf16[1152,256]{1,0:T(8,128)(2,1)S(1)} %get-tuple-element.85.edges, s32[9,128]{1,0:T(8,128)S(1)} %get-tuple-element.87.senders, ...), custom_call_target="tpu_custom_call" | custom-call | flops 704643072 | bytes 6497280 | tf_op jit(solution)/shard_map/pallas_call | solution.py:500
  14.5 0.0 collective-permute-done.2.along_core
  14.5 0.1 collective-permute-done.3.along_chip
  14.6 5.6 %shard_map.201 = (bf16[1152,256]{1,0:T(8,128)(2,1)S(1)}, bf16[384,256]{1,0:T(8,128)(2,1)S(1)}, bf16[384,256]{1,0:T(8,128)(2,1)S(1)}, f32[384,256]{1,0:T(8,128)S(...) custom-call(s32[1]{0:T(128)S(6)} %copy.22.count_ref, ...), custom_call_target="tpu_custom_call" | custom-call | flops 2583691264 | bytes 11412484 | tf_op jit(solution)/shard_map/pallas_call | solution.py:500
  20.2 0.5 %collective-permute-start.4 = (bf16[904,256]{1,0:T(8,128)(2,1)S(1)}, bf16[904,256]{1,0:T(8,128)(2,1)S(1)}, u32[]{:S(2)}, u32[]{:S(2)}) collective-permute-start(bf16[904,256]{1,0:T(8,128)(2,1)S(1)} %get-tuple-element.111), channel_id=1, source_target_pairs={{0,1},{1,0},{2,3},{3,2},{4,5},{5,4},{6,7},{7,6},{8,9},{9,8},{10,11... | collective-permute-start | bytes 1388552 | tf_op jit(solution)/shard_map/ppermute | solution.py:30
  20.7 1.4 %collective-permute-done.4.other = bf16[904,256]{1,0:T(8,128)(2,1)S(1)} collective-permute-done((bf16[904,256]{1,0:T(8,128)(2,1)S(1)}, bf16[904,256]{1,0:T(8,128)(2,1)S(1)}, u32[]{:S(2)}, u32[]{:S(2)}) %collective-permute-start.4) | collective-permute-done | bytes 462880 | tf_op jit(solution)/shard_map/ppermute | solution.py:30
  22.2 0.1 shard_map.202
  22.3 1.6 %collective-permute-start.5 = (bf16[232,256]{1,0:T(8,128)(2,1)S(1)}, bf16[232,256]{1,0:T(8,128)(2,1)S(1)}, u32[]{:S(2)}, u32[]{:S(2)}) collective-permute-start(bf16[232,256]{1,0:T(8,128)(2,1)S(1)} %get-tuple-element.113), channel_id=1, source_target_pairs={{0,2},{2,0},{4,6},{6,4},{1,3},{3,1},{5,7},{7,5},{8,10},{10,8},{12,... | collective-permute-start | bytes 356360 | tf_op jit(solution)/shard_map/ppermute | solution.py:48
  23.9 0.0 collective-permute-start.6
  23.9 2.0 %collective-permute-start.7 = (bf16[232,256]{1,0:T(8,128)(2,1)S(1)}, bf16[232,256]{1,0:T(8,128)(2,1)S(1)}, u32[]{:S(2)}, u32[]{:S(2)}) collective-permute-start(bf16[232,256]{1,0:T(8,128)(2,1)S(1)} %get-tuple-element.115), channel_id=1, source_target_pairs={{0,6},{2,4},{4,2},{6,0},{1,7},{3,5},{5,3},{7,1},{8,14},{10,12},{12... | collective-permute-start | bytes 356360 | tf_op jit(solution)/shard_map/ppermute | solution.py:48
  25.9 0.0 collective-permute-start.9
  25.9 2.5 %collective-permute-start.10 = (bf16[96,256]{1,0:T(8,128)(2,1)S(1)}, bf16[96,256]{1,0:T(8,128)(2,1)S(1)}, u32[]{:S(2)}, u32[]{:S(2)}) collective-permute-start(bf16[96,256]{1,0:T(8,128)(2,1)S(1)} %get-tuple-element.117), channel_id=1, source_target_pairs={{0,12},{4,8},{8,4},{12,0},{1,13},{5,9},{9,5},{13,1},{2,14},{6,10},... | collective-permute-start | bytes 147464 | tf_op jit(solution)/shard_map/ppermute | solution.py:35
  28.4 0.0 collective-permute-done.5.refs_1_
  28.4 1.6 %collective-permute-done.6.refs_2_ = bf16[232,256]{1,0:T(8,128)(2,1)S(1)} collective-permute-done((bf16[232,256]{1,0:T(8,128)(2,1)S(1)}, bf16[232,256]{1,0:T(8,128)(2,1)S(1)}, u32[]{:S(2)}, u32[]{:S(2)}) %collective-permute-start.6) | collective-permute-done | bytes 118816 | tf_op jit(solution)/shard_map/ppermute | solution.py:48
  30.0 2.2 %collective-permute-done.7.refs_3_ = bf16[232,256]{1,0:T(8,128)(2,1)S(1)} collective-permute-done((bf16[232,256]{1,0:T(8,128)(2,1)S(1)}, bf16[232,256]{1,0:T(8,128)(2,1)S(1)}, u32[]{:S(2)}, u32[]{:S(2)}) %collective-permute-start.7) | collective-permute-done | bytes 118816 | tf_op jit(solution)/shard_map/ppermute | solution.py:48
  32.1 0.1 shard_map.203.refs_3_.own
  32.2 1.9 %collective-permute-start.8 = (bf16[232,256]{1,0:T(8,128)(2,1)S(1)}, bf16[232,256]{1,0:T(8,128)(2,1)S(1)}, u32[]{:S(2)}, u32[]{:S(2)}) collective-permute-start(bf16[232,256]{1,0:T(8,128)(2,1)S(1)} %shard_map.203.refs_3_.own), channel_id=1, source_target_pairs={{0,8},{8,0},{1,9},{9,1},{2,10},{10,2},{3,11},{11,3},{4,12},{12,4},... | collective-permute-start | bytes 356360 | tf_op jit(solution)/shard_map/ppermute | solution.py:541
  34.1 0.0 collective-permute-done.9.refs_0_
  34.1 0.5 collective-permute-done.10.refs_1_
  34.6 0.1 collective-permute-start.11
  34.7 0.6 %collective-permute-start.12 = (bf16[96,256]{1,0:T(8,128)(2,1)S(1)}, bf16[96,256]{1,0:T(8,128)(2,1)S(1)}, u32[]{:S(2)}, u32[]{:S(2)}) collective-permute-start(bf16[96,256]{1,0:T(8,128)(2,1)S(1)} %get-tuple-element.120), channel_id=1, source_target_pairs={{0,3},{1,2},{2,1},{3,0},{4,7},{5,6},{6,5},{7,4},{8,11},{9,10},{10,... | collective-permute-start | bytes 147464 | tf_op jit(solution)/shard_map/ppermute | solution.py:35
  35.3 1.3 %shard_map.206 = (bf16[1152,256]{1,0:T(8,128)(2,1)}, f32[384,256]{1,0:T(8,128)S(1)}) custom-call(bf16[1152,256]{1,0:T(8,128)(2,1)S(1)} %get-tuple-element.86.edge_grads, bf16[1152,256]{1,0:T(8,128)(2,1)S(1)} %get-tuple-element.124.pre_grad, bf16[384,256]{1,0:T(8,128)(2,1)S(1)} %get-tuple-element.125.sender_sum, ...), custom_call_target="tpu_custom_call" | custom-call | flops 251658240 | bytes 3342336 | tf_op jit(solution)/shard_map/pallas_call | solution.py:500
  36.7 0.0 collective-permute-done.11.along_core
  36.7 1.6 %collective-permute-done.12.along_chip = bf16[96,256]{1,0:T(8,128)(2,1)S(1)} collective-permute-done((bf16[96,256]{1,0:T(8,128)(2,1)S(1)}, bf16[96,256]{1,0:T(8,128)(2,1)S(1)}, u32[]{:S(2)}, u32[]{:S(2)}) %collective-permute-start.12) | collective-permute-done | bytes 49184 | tf_op jit(solution)/shard_map/ppermute | solution.py:35
  38.3 1.3 %collective-permute-done.8.other = bf16[232,256]{1,0:T(8,128)(2,1)S(1)} collective-permute-done((bf16[232,256]{1,0:T(8,128)(2,1)S(1)}, bf16[232,256]{1,0:T(8,128)(2,1)S(1)}, u32[]{:S(2)}, u32[]{:S(2)}) %collective-permute-start.8) | collective-permute-done | bytes 118816 | tf_op jit(solution)/shard_map/ppermute | solution.py:541
  39.6 1.5 %collective-permute-start.15 = (bf16[224,256]{1,0:T(8,128)(2,1)S(1)}, bf16[224,256]{1,0:T(8,128)(2,1)S(1)}, u32[]{:S(2)}, u32[]{:S(2)}) collective-permute-start(bf16[224,256]{1,0:T(8,128)(2,1)S(1)} %get-tuple-element.148.refs_0_), channel_id=1, source_target_pairs={{0,2},{2,0},{4,6},{6,4},{1,3},{3,1},{5,7},{7,5},{8,10},{10,8},{12,... | collective-permute-start | bytes 344072 | tf_op jit(solution)/shard_map/ppermute | solution.py:48
  41.1 0.0 collective-permute-start.14
  41.1 2.0 %collective-permute-start.13 = (bf16[224,256]{1,0:T(8,128)(2,1)S(1)}, bf16[224,256]{1,0:T(8,128)(2,1)S(1)}, u32[]{:S(2)}, u32[]{:S(2)}) collective-permute-start(bf16[224,256]{1,0:T(8,128)(2,1)S(1)} %get-tuple-element.148.refs_0_), channel_id=1, source_target_pairs={{0,6},{2,4},{4,2},{6,0},{1,7},{3,5},{5,3},{7,1},{8,14},{10,12},{12... | collective-permute-start | bytes 344072 | tf_op jit(solution)/shard_map/ppermute | solution.py:48
  43.2 1.1 %shard_map.207 = bf16[384,256]{1,0:T(8,128)(2,1)} custom-call(s32[8,32]{1,0:T(8,128)S(1)} %get-tuple-element.123.send_list, f32[384,256]{1,0:T(8,128)S(1)} %get-tuple-element.128.local_grad, bf16[64,256]{1,0:T(8,128)(2,1)S(1)} %get-tuple-element.129.center, bf16[96,256]{1,0:T(8,128)(2,1)S(1)} %collective-permute-done.11.along_core, ...), custom_call_target="tpu_custom_call" | custom-call | flops 50331648 | bytes 721920 | tf_op jit(solution)/shard_map/pallas_call | solution.py:500
  44.3 0.5 %convert_reduce_fusion = (bf16[256]{0:T(256)(128)(2,1)}, bf16[256]{0:T(256)(128)(2,1)}) fusion(f32[8,256]{1,0:T(8,128)S(1)} %get-tuple-element.133), kind=kLoop, calls=%fused_computation | loop fusion | flops 1024 | bytes 5120 | tf_op jit(solution)/shard_map/convert_element_type | solution.py:752
  44.8 0.0 collective-permute-start.16
  44.8 0.0 collective-permute-done.15.refs_1_
  44.8 0.5 %collective-permute-start.17 = (bf16[224,256]{1,0:T(8,128)(2,1)S(1)}, bf16[224,256]{1,0:T(8,128)(2,1)S(1)}, u32[]{:S(2)}, u32[]{:S(2)}) collective-permute-start(bf16[224,256]{1,0:T(8,128)(2,1)S(1)} %collective-permute-done.15.refs_1_), channel_id=1, source_target_pairs={{0,1},{1,0},{2,3},{3,2},{4,5},{5,4},{6,7},{7,6},{8,9},{9,8},{10,11... | collective-permute-start | bytes 344072 | tf_op jit(solution)/shard_map/ppermute | solution.py:30
  45.3 0.9 %collective-permute-done.14.refs_2_ = bf16[224,256]{1,0:T(8,128)(2,1)S(1)} collective-permute-done((bf16[224,256]{1,0:T(8,128)(2,1)S(1)}, bf16[224,256]{1,0:T(8,128)(2,1)S(1)}, u32[]{:S(2)}, u32[]{:S(2)}) %collective-permute-start.14) | collective-permute-done | bytes 114720 | tf_op jit(solution)/shard_map/ppermute | solution.py:48
  46.3 0.0 collective-permute-start.18
  46.3 1.8 %collective-permute-done.13.refs_3_ = bf16[224,256]{1,0:T(8,128)(2,1)S(1)} collective-permute-done((bf16[224,256]{1,0:T(8,128)(2,1)S(1)}, bf16[224,256]{1,0:T(8,128)(2,1)S(1)}, u32[]{:S(2)}, u32[]{:S(2)}) %collective-permute-start.13) | collective-permute-done | bytes 114720 | tf_op jit(solution)/shard_map/ppermute | solution.py:48
  48.1 0.0 collective-permute-start.19
  48.1 0.0 collective-permute-done.16.refs_4_
  48.1 0.0 collective-permute-done.17.refs_5_
  48.1 0.0 collective-permute-done.18.refs_6_
  48.1 1.3 %collective-permute-done.19.refs_7_ = bf16[224,256]{1,0:T(8,128)(2,1)S(1)} collective-permute-done((bf16[224,256]{1,0:T(8,128)(2,1)S(1)}, bf16[224,256]{1,0:T(8,128)(2,1)S(1)}, u32[]{:S(2)}, u32[]{:S(2)}) %collective-permute-start.19) | collective-permute-done | bytes 114720 | tf_op jit(solution)/shard_map/ppermute | solution.py:30
  49.4 1.0 %shard_map.208 = (bf16[768,256]{1,0:T(8,128)(2,1)}, bf16[256,256]{1,0:T(8,128)(2,1)}, bf16[512,256]{1,0:T(8,128)(2,1)}, bf16[256,256]{1,0:T(8,128)(2,1)}) custom-call(bf16[224,256]{1,0:T(8,128)(2,1)S(1)} %get-tuple-element.148.refs_0_, bf16[224,256]{1,0:T(8,128)(2,1)S(1)} %collective-permute-done.15.refs_1_, ...), custom_call_target="tpu_custom_call" | custom-call | bytes 1835008 | tf_op jit(solution)/shard_map/pallas_call | solution.py:500
  (3 shorter events, 0.1 us)
Async XLA Ops:
  2.0 8.0 %collective-permute-start = (bf16[96,256]{1,0:T(8,128)(2,1)S(1)}, bf16[96,256]{1,0:T(8,128)(2,1)S(1)}, u32[]{:S(2)}, u32[]{:S(2)}) collective-permute-start(bf16[96,256]{1,0:T(8,128)(2,1)S(1)} %get-tuple-element.89), channel_id=1, source_target_pairs={{0,4},{4,0},{8,12},{12,8},{1,5},{5,1},{9,13},{13,9},{2,6},{6,2},{1... | collective-permute-start | bytes 147464 | tf_op jit(solution)/shard_map/ppermute | solution.py:30
  5.0 5.9 %collective-permute-start.1 = (bf16[96,256]{1,0:T(8,128)(2,1)S(1)}, bf16[96,256]{1,0:T(8,128)(2,1)S(1)}, u32[]{:S(2)}, u32[]{:S(2)}) collective-permute-start(bf16[96,256]{1,0:T(8,128)(2,1)S(1)} %get-tuple-element.90), channel_id=1, source_target_pairs={{0,12},{4,8},{8,4},{12,0},{1,13},{5,9},{9,5},{13,1},{2,14},{6,10},... | collective-permute-start | bytes 147464 | tf_op jit(solution)/shard_map/ppermute | solution.py:35
  11.0 3.5 %collective-permute-start.2 = (bf16[96,256]{1,0:T(8,128)(2,1)S(1)}, bf16[96,256]{1,0:T(8,128)(2,1)S(1)}, u32[]{:S(2)}, u32[]{:S(2)}) collective-permute-start(bf16[96,256]{1,0:T(8,128)(2,1)S(1)} %get-tuple-element.102), channel_id=1, source_target_pairs={{0,1},{1,0},{2,3},{3,2},{4,5},{5,4},{6,7},{7,6},{8,9},{9,8},{10,11... | collective-permute-start | bytes 147464 | tf_op jit(solution)/shard_map/ppermute | solution.py:30
  11.0 3.6 %collective-permute-start.3 = (bf16[96,256]{1,0:T(8,128)(2,1)S(1)}, bf16[96,256]{1,0:T(8,128)(2,1)S(1)}, u32[]{:S(2)}, u32[]{:S(2)}) collective-permute-start(bf16[96,256]{1,0:T(8,128)(2,1)S(1)} %get-tuple-element.103), channel_id=1, source_target_pairs={{0,3},{1,2},{2,1},{3,0},{4,7},{5,6},{6,5},{7,4},{8,11},{9,10},{10,... | collective-permute-start | bytes 147464 | tf_op jit(solution)/shard_map/ppermute | solution.py:35
  20.2 2.0 %collective-permute-start.4 = (bf16[904,256]{1,0:T(8,128)(2,1)S(1)}, bf16[904,256]{1,0:T(8,128)(2,1)S(1)}, u32[]{:S(2)}, u32[]{:S(2)}) collective-permute-start(bf16[904,256]{1,0:T(8,128)(2,1)S(1)} %get-tuple-element.111), channel_id=1, source_target_pairs={{0,1},{1,0},{2,3},{3,2},{4,5},{5,4},{6,7},{7,6},{8,9},{9,8},{10,11... | collective-permute-start | bytes 1388552 | tf_op jit(solution)/shard_map/ppermute | solution.py:30
  22.3 6.1 %collective-permute-start.5 = (bf16[232,256]{1,0:T(8,128)(2,1)S(1)}, bf16[232,256]{1,0:T(8,128)(2,1)S(1)}, u32[]{:S(2)}, u32[]{:S(2)}) collective-permute-start(bf16[232,256]{1,0:T(8,128)(2,1)S(1)} %get-tuple-element.113), channel_id=1, source_target_pairs={{0,2},{2,0},{4,6},{6,4},{1,3},{3,1},{5,7},{7,5},{8,10},{10,8},{12,... | collective-permute-start | bytes 356360 | tf_op jit(solution)/shard_map/ppermute | solution.py:48
  23.9 6.1 %collective-permute-start.6 = (bf16[232,256]{1,0:T(8,128)(2,1)S(1)}, bf16[232,256]{1,0:T(8,128)(2,1)S(1)}, u32[]{:S(2)}, u32[]{:S(2)}) collective-permute-start(bf16[232,256]{1,0:T(8,128)(2,1)S(1)} %get-tuple-element.114), channel_id=1, source_target_pairs={{0,4},{2,6},{4,0},{6,2},{1,5},{3,7},{5,1},{7,3},{8,12},{10,14},{12... | collective-permute-start | bytes 356360 | tf_op jit(solution)/shard_map/ppermute | solution.py:48
  23.9 8.3 %collective-permute-start.7 = (bf16[232,256]{1,0:T(8,128)(2,1)S(1)}, bf16[232,256]{1,0:T(8,128)(2,1)S(1)}, u32[]{:S(2)}, u32[]{:S(2)}) collective-permute-start(bf16[232,256]{1,0:T(8,128)(2,1)S(1)} %get-tuple-element.115), channel_id=1, source_target_pairs={{0,6},{2,4},{4,2},{6,0},{1,7},{3,5},{5,3},{7,1},{8,14},{10,12},{12... | collective-permute-start | bytes 356360 | tf_op jit(solution)/shard_map/ppermute | solution.py:48
  25.9 8.2 %collective-permute-start.9 = (bf16[96,256]{1,0:T(8,128)(2,1)S(1)}, bf16[96,256]{1,0:T(8,128)(2,1)S(1)}, u32[]{:S(2)}, u32[]{:S(2)}) collective-permute-start(bf16[96,256]{1,0:T(8,128)(2,1)S(1)} %get-tuple-element.116), channel_id=1, source_target_pairs={{0,4},{4,0},{8,12},{12,8},{1,5},{5,1},{9,13},{13,9},{2,6},{6,2},{1... | collective-permute-start | bytes 147464 | tf_op jit(solution)/shard_map/ppermute | solution.py:30
  25.9 8.7 %collective-permute-start.10 = (bf16[96,256]{1,0:T(8,128)(2,1)S(1)}, bf16[96,256]{1,0:T(8,128)(2,1)S(1)}, u32[]{:S(2)}, u32[]{:S(2)}) collective-permute-start(bf16[96,256]{1,0:T(8,128)(2,1)S(1)} %get-tuple-element.117), channel_id=1, source_target_pairs={{0,12},{4,8},{8,4},{12,0},{1,13},{5,9},{9,5},{13,1},{2,14},{6,10},... | collective-permute-start | bytes 147464 | tf_op jit(solution)/shard_map/ppermute | solution.py:35
  32.2 7.4 %collective-permute-start.8 = (bf16[232,256]{1,0:T(8,128)(2,1)S(1)}, bf16[232,256]{1,0:T(8,128)(2,1)S(1)}, u32[]{:S(2)}, u32[]{:S(2)}) collective-permute-start(bf16[232,256]{1,0:T(8,128)(2,1)S(1)} %shard_map.203.refs_3_.own), channel_id=1, source_target_pairs={{0,8},{8,0},{1,9},{9,1},{2,10},{10,2},{3,11},{11,3},{4,12},{12,4},... | collective-permute-start | bytes 356360 | tf_op jit(solution)/shard_map/ppermute | solution.py:541
  34.6 2.1 %collective-permute-start.11 = (bf16[96,256]{1,0:T(8,128)(2,1)S(1)}, bf16[96,256]{1,0:T(8,128)(2,1)S(1)}, u32[]{:S(2)}, u32[]{:S(2)}) collective-permute-start(bf16[96,256]{1,0:T(8,128)(2,1)S(1)} %get-tuple-element.119), channel_id=1, source_target_pairs={{0,1},{1,0},{2,3},{3,2},{4,5},{5,4},{6,7},{7,6},{8,9},{9,8},{10,11... | collective-permute-start | bytes 147464 | tf_op jit(solution)/shard_map/ppermute | solution.py:30
  34.7 3.6 %collective-permute-start.12 = (bf16[96,256]{1,0:T(8,128)(2,1)S(1)}, bf16[96,256]{1,0:T(8,128)(2,1)S(1)}, u32[]{:S(2)}, u32[]{:S(2)}) collective-permute-start(bf16[96,256]{1,0:T(8,128)(2,1)S(1)} %get-tuple-element.120), channel_id=1, source_target_pairs={{0,3},{1,2},{2,1},{3,0},{4,7},{5,6},{6,5},{7,4},{8,11},{9,10},{10,... | collective-permute-start | bytes 147464 | tf_op jit(solution)/shard_map/ppermute | solution.py:35
  39.6 5.2 %collective-permute-start.15 = (bf16[224,256]{1,0:T(8,128)(2,1)S(1)}, bf16[224,256]{1,0:T(8,128)(2,1)S(1)}, u32[]{:S(2)}, u32[]{:S(2)}) collective-permute-start(bf16[224,256]{1,0:T(8,128)(2,1)S(1)} %get-tuple-element.148.refs_0_), channel_id=1, source_target_pairs={{0,2},{2,0},{4,6},{6,4},{1,3},{3,1},{5,7},{7,5},{8,10},{10,8},{12,... | collective-permute-start | bytes 344072 | tf_op jit(solution)/shard_map/ppermute | solution.py:48
  41.1 5.1 %collective-permute-start.14 = (bf16[224,256]{1,0:T(8,128)(2,1)S(1)}, bf16[224,256]{1,0:T(8,128)(2,1)S(1)}, u32[]{:S(2)}, u32[]{:S(2)}) collective-permute-start(bf16[224,256]{1,0:T(8,128)(2,1)S(1)} %get-tuple-element.148.refs_0_), channel_id=1, source_target_pairs={{0,4},{2,6},{4,0},{6,2},{1,5},{3,7},{5,1},{7,3},{8,12},{10,14},{12... | collective-permute-start | bytes 344072 | tf_op jit(solution)/shard_map/ppermute | solution.py:48
  41.1 6.9 %collective-permute-start.13 = (bf16[224,256]{1,0:T(8,128)(2,1)S(1)}, bf16[224,256]{1,0:T(8,128)(2,1)S(1)}, u32[]{:S(2)}, u32[]{:S(2)}) collective-permute-start(bf16[224,256]{1,0:T(8,128)(2,1)S(1)} %get-tuple-element.148.refs_0_), channel_id=1, source_target_pairs={{0,6},{2,4},{4,2},{6,0},{1,7},{3,5},{5,3},{7,1},{8,14},{10,12},{12... | collective-permute-start | bytes 344072 | tf_op jit(solution)/shard_map/ppermute | solution.py:48
  44.8 3.3 %collective-permute-start.16 = (bf16[224,256]{1,0:T(8,128)(2,1)S(1)}, bf16[224,256]{1,0:T(8,128)(2,1)S(1)}, u32[]{:S(2)}, u32[]{:S(2)}) collective-permute-start(bf16[224,256]{1,0:T(8,128)(2,1)S(1)} %get-tuple-element.148.refs_0_), channel_id=1, source_target_pairs={{0,1},{1,0},{2,3},{3,2},{4,5},{5,4},{6,7},{7,6},{8,9},{9,8},{10,11... | collective-permute-start | bytes 344072 | tf_op jit(solution)/shard_map/ppermute | solution.py:30
  44.8 3.3 %collective-permute-start.17 = (bf16[224,256]{1,0:T(8,128)(2,1)S(1)}, bf16[224,256]{1,0:T(8,128)(2,1)S(1)}, u32[]{:S(2)}, u32[]{:S(2)}) collective-permute-start(bf16[224,256]{1,0:T(8,128)(2,1)S(1)} %collective-permute-done.15.refs_1_), channel_id=1, source_target_pairs={{0,1},{1,0},{2,3},{3,2},{4,5},{5,4},{6,7},{7,6},{8,9},{9,8},{10,11... | collective-permute-start | bytes 344072 | tf_op jit(solution)/shard_map/ppermute | solution.py:30
  46.3 1.8 %collective-permute-start.18 = (bf16[224,256]{1,0:T(8,128)(2,1)S(1)}, bf16[224,256]{1,0:T(8,128)(2,1)S(1)}, u32[]{:S(2)}, u32[]{:S(2)}) collective-permute-start(bf16[224,256]{1,0:T(8,128)(2,1)S(1)} %collective-permute-done.14.refs_2_), channel_id=1, source_target_pairs={{0,1},{1,0},{2,3},{3,2},{4,5},{5,4},{6,7},{7,6},{8,9},{9,8},{10,11... | collective-permute-start | bytes 344072 | tf_op jit(solution)/shard_map/ppermute | solution.py:30
  48.1 1.3 %collective-permute-start.19 = (bf16[224,256]{1,0:T(8,128)(2,1)S(1)}, bf16[224,256]{1,0:T(8,128)(2,1)S(1)}, u32[]{:S(2)}, u32[]{:S(2)}) collective-permute-start(bf16[224,256]{1,0:T(8,128)(2,1)S(1)} %collective-permute-done.13.refs_3_), channel_id=1, source_target_pairs={{0,1},{1,0},{2,3},{3,2},{4,5},{5,4},{6,7},{7,6},{8,9},{9,8},{10,11... | collective-permute-start | bytes 344072 | tf_op jit(solution)/shard_map/ppermute | solution.py:30

commit v18 on v17

--- a/solution.py
+++ b/solution.py
@@ -161,7 +161,7 @@
     return copies
 
 
-def send_kernel(nodes_hbm, list_hbm, inner, outer, middle, nodes, send_list, sems):
+def send_kernel(nodes_hbm, list_hbm, outer, inner, middle, nodes, send_list, sems):
     slots = send_list.shape[1]
     for copy in fetch_all([list_hbm, nodes_hbm], [send_list, nodes], sems):
         copy.wait()
@@ -170,7 +170,7 @@
     middle[...] = rows[3 * slots : 5 * slots]
 
 
-def corner_kernel(inner, outer, middle, along_core, along_chip, straight):
+def corner_kernel(outer, inner, middle, along_core, along_chip, straight):
     slots = middle.shape[0] // 2
     low, high = from_pair(NEAR, inner[...], outer[...])
     up = jnp.concatenate([high[2 * slots :], middle[slots:], low[2 * slots :]], axis=0)
@@ -366,7 +366,7 @@
     both = gains[...].astype(F32) + other[rows : rows + packed].astype(F32)
     summed = pack_gains(both[0:1] + both[1:2], both[2:3] + both[3:4])
     me = place_in_square()
-    for offset, out in enumerate(outs):
+    for offset, out in enumerate(reversed(outs)):
         owner = me ^ offset
         out[:packed] = summed
         first, at = 0, packed
@@ -381,6 +381,10 @@
     packed = PACKED
     gains = values[:packed]
     return pack_gains(gains[0:1] + gains[1:2], gains[2:3] + gains[3:4])
+
+
+def copy_kernel(source, target):
+    target[...] = source[...]
 
 
 def sum_kernel(*refs):
@@ -576,7 +580,7 @@
     edge_rows = edges.shape[0]
     tile_rows = senders.shape[1]
     square = 2 * width * width
-    inner, outer, middle, nodes, send_list = call(
+    outer, inner, middle, nodes, send_list = call(
         send_kernel,
         [
             shaped(3 * slots, width, BF16),
@@ -591,8 +595,8 @@
         spaces=[HBM, HBM],
         scratch=[pltpu.SemaphoreType.DMA((2,))],
     )
+    outer = out_of_pair(outer, PX)
     inner = in_pair(inner, PX)
-    outer = out_of_pair(outer, PX)
     fetched = [
         senders,
         receivers,
@@ -631,7 +635,7 @@
         node_grads,
         edge_grads,
     ) = fetched
-    inner, outer, near_hot = lax.optimization_barrier((inner, outer, near_hot))
+    outer, inner, near_hot = lax.optimization_barrier((outer, inner, near_hot))
     along_core, along_chip, straight = call(
         corner_kernel,
         [
@@ -640,8 +644,8 @@
             shaped(2 * slots, width, BF16),
         ],
         0,
+        outer,
         inner,
-        outer,
         middle,
     )
     along_chip = out_of_pair(along_chip, PY)
@@ -710,7 +714,7 @@
     )
     other = across_cores(away)
     members = square_members()
-    own, *blocks = call(
+    *blocks, own = call(
         functools.partial(pair_kernel, parts),
         [shaped(PACKED + halves // members, width, BF16)] * members,
         0,
@@ -718,8 +722,11 @@
         gains,
         other,
     )
-    received = [in_square(block, offset) for offset, block in enumerate(blocks, 1)]
-    (sums,) = call(sum_kernel, [like(own)], 0, own, *received)
+    received = [in_square(block, members - 1 - i) for i, block in enumerate(blocks)]
+    outer = out_of_pair(outer, PX)
+    (inner,) = call(copy_kernel, [like(inner)], 10**9, in_pair(inner, PX))
+    *received, inner = lax.optimization_barrier((*received, inner))
+    (sums,) = call(sum_kernel, [like(own)], 0, *received, own)
     edges_grad, local_grad = call(
         finish_kernel,
         [shaped(edge_rows, width, BF16), shaped(count, width, F32)],
@@ -739,8 +746,8 @@
             shaped(2 * slots, width, BF16),
         ],
         10**10,
-        in_pair(inner, PX),
-        out_of_pair(outer, PX),
+        inner,
+        outer,
         middle,
         after=[sums],
     )

time: 50.6 us -> 51.4 us (1.016)
  waiting for transfers between devices: 13.8 us -> 16.8 us
  starting transfers between devices: 20.5 us -> 18.3 us
    ppermute x9, starting transfers between devices: 4.3 us -> 1.71 us  [in_pair(): lax.ppermute(array, axis, [(i, i ^ 1) for i in range(lax.axis_size(axis))])]
    ppermute x4, starting transfers between devices: 7.2 us -> 9.38 us  [out_of_pair(): lax.ppermute(array, axis, [(i, other_neighbour(i, size)) for i in range(s...]
    ppermute x1, waiting for transfers between devices: 1.3 us -> 3.46 us  [joined(): other = lax.ppermute(sums, FAR, [(i, i ^ distance) for i in range(size)])]
    ppermute x1, starting transfers between devices: 1.87 us -> 0.07 us  [joined(): other = lax.ppermute(sums, FAR, [(i, i ^ distance) for i in range(size)])]
    ppermute x4, waiting for transfers between devices: 3.24 us -> 1.54 us  [out_of_pair(): lax.ppermute(array, axis, [(i, other_neighbour(i, size)) for i in range(s...]
    ppermute x6, waiting for transfers between devices: 6.51 us -> 7.89 us  [in_square(): lax.ppermute(array, SQUARE, [(i, i ^ offset) for i in range(square_member...]
    ppermute x9, waiting for transfers between devices: 2.77 us -> 3.92 us  [in_pair(): lax.ppermute(array, axis, [(i, i ^ 1) for i in range(lax.axis_size(axis))])]
    pallas_call x12 -> x13, Pallas kernels: 14.2 us -> 14.2 us  [call(): pl.pallas_call(body, out_shape=outs, in_specs=[pl.BlockSpec(memory_space=...]
where the time goes in v18:
time: 51.4 us; the launch traced here: 51.2 us
  starting transfers between devices  18.3 us (36%)
  waiting for transfers between devices  16.8 us (33%)
  Pallas kernels  14.2 us (28%)
  between operations  1.41 us (3%)
  other arithmetic  0.53 us (1%)
    pallas_call x13, Pallas kernels, call(): pl.pallas_call(body, out_shape=outs, in_specs=[pl.BlockSpec(memory_space=...  14.2 us
    ppermute x4, starting transfers between devices, out_of_pair(): lax.ppermute(array, axis, [(i, other_neighbour(i, size)) for i in range(s...  9.38 us
    ppermute x6, waiting for transfers between devices, in_square(): lax.ppermute(array, SQUARE, [(i, i ^ offset) for i in range(square_member...  7.89 us
    ppermute x6, starting transfers between devices, in_square(): lax.ppermute(array, SQUARE, [(i, i ^ offset) for i in range(square_member...  7.12 us
    ppermute x9, waiting for transfers between devices, in_pair(): lax.ppermute(array, axis, [(i, i ^ 1) for i in range(lax.axis_size(axis))])  3.92 us
    ppermute x1, waiting for transfers between devices, joined(): other = lax.ppermute(sums, FAR, [(i, i ^ distance) for i in range(size)])  3.46 us
    ppermute x9, starting transfers between devices, in_pair(): lax.ppermute(array, axis, [(i, i ^ 1) for i in range(lax.axis_size(axis))])  1.71 us
    ppermute x4, waiting for transfers between devices, out_of_pair(): lax.ppermute(array, axis, [(i, other_neighbour(i, size)) for i in range(s...  1.54 us
  transfers between devices with their start and end apart: 20, of which 11 were waited for; matrix products, arithmetic and copies ran while one was open for 1% of the time, Pallas kernels for 12%

profile of v18, /device:TPU:0, one launch (start us, length us, event | category | flops | bytes accessed | tf_op | source)
XLA Modules:
  0.0 51.2 jit_solution(272925749303626695)
XLA Ops:
  0.6 1.3 %shard_map.197 = (bf16[96,256]{1,0:T(8,128)(2,1)S(1)}, bf16[96,256]{1,0:T(8,128)(2,1)S(1)}, bf16[64,256]{1,0:T(8,128)(2,1)S(1)}, bf16[384,256]{1,0:T(8,128)(2,1)S(1)}, s32[8,32]{1,0:T(8,128)S(1)}) custom-call(bf16[384,256]{1,0:T(8,128)(2,1)} %nodes_hbm.1, s32[8,32]{1,0:T(8,128)} %list_hbm.1), custom_call_target="tpu_custom_call" | custom-call | flops 50331648 | bytes 526336 | tf_op jit(solution)/shard_map/pallas_call | solution.py:504
  2.0 5.1 %collective-permute-start = (bf16[96,256]{1,0:T(8,128)(2,1)S(1)}, bf16[96,256]{1,0:T(8,128)(2,1)S(1)}, u32[]{:S(2)}, u32[]{:S(2)}) collective-permute-start(bf16[96,256]{1,0:T(8,128)(2,1)S(1)} %get-tuple-element.93), channel_id=1, source_target_pairs={{0,12},{4,8},{8,4},{12,0},{1,13},{5,9},{9,5},{13,1},{2,14},{6,10},... | collective-permute-start | bytes 147464 | tf_op jit(solution)/shard_map/ppermute | solution.py:35
  7.1 0.0 collective-permute-start.1
  7.7 1.7 %shard_map.198 = (bf16[1152,768]{1,0:T(8,128)(2,1)S(1)}, bf16[1152,256]{1,0:T(8,128)(2,1)S(1)}, s32[9,128]{1,0:T(8,128)S(1)}, s32[9,128]{1,0:T(8,128)S(1)}, bf16...) custom-call(s32[9,128]{1,0:T(8,128)} %refs_0_.1, ...), custom_call_target="tpu_custom_call" | custom-call | bytes 6967296 | tf_op jit(solution)/shard_map/pallas_call | solution.py:504
  9.5 0.0 collective-permute-done.outer
  9.5 1.7 %collective-permute-done.1.inner = bf16[96,256]{1,0:T(8,128)(2,1)S(1)} collective-permute-done((bf16[96,256]{1,0:T(8,128)(2,1)S(1)}, bf16[96,256]{1,0:T(8,128)(2,1)S(1)}, u32[]{:S(2)}, u32[]{:S(2)}) %collective-permute-start.1) | collective-permute-done | bytes 49184 | tf_op jit(solution)/shard_map/ppermute | solution.py:30
  11.2 0.1 collective-permute-start.2
  11.3 1.6 %collective-permute-start.3 = (bf16[96,256]{1,0:T(8,128)(2,1)S(1)}, bf16[96,256]{1,0:T(8,128)(2,1)S(1)}, u32[]{:S(2)}, u32[]{:S(2)}) collective-permute-start(bf16[96,256]{1,0:T(8,128)(2,1)S(1)} %get-tuple-element.107), channel_id=1, source_target_pairs={{0,3},{1,2},{2,1},{3,0},{4,7},{5,6},{6,5},{7,4},{8,11},{9,10},{10,... | collective-permute-start | bytes 147464 | tf_op jit(solution)/shard_map/ppermute | solution.py:35
  12.9 1.8 %shard_map.199 = (f32[1152,256]{1,0:T(8,128)S(1)}, bf16[640,1152]{1,0:T(8,128)(2,1)S(1)}, bf16[384,1152]{1,0:T(8,128)(2,1)S(1)}) custom-call(bf16[384,256]{1,0:T(8,128)(2,1)S(1)} %get-tuple-element.87.nodes, bf16[1152,256]{1,0:T(8,128)(2,1)S(1)} %get-tuple-element.89.edges, s32[9,128]{1,0:T(8,128)S(1)} %get-tuple-element.91.senders, ...), custom_call_target="tpu_custom_call" | custom-call | flops 704643072 | bytes 6497280 | tf_op jit(solution)/shard_map/pallas_call | solution.py:504
  14.7 0.0 collective-permute-done.2.along_core
  14.7 0.1 collective-permute-done.3.along_chip
  14.8 5.6 %shard_map.201 = (bf16[1152,256]{1,0:T(8,128)(2,1)S(1)}, bf16[384,256]{1,0:T(8,128)(2,1)S(1)}, bf16[384,256]{1,0:T(8,128)(2,1)S(1)}, f32[384,256]{1,0:T(8,128)S(...) custom-call(s32[1]{0:T(128)S(6)} %copy.22.count_ref, ...), custom_call_target="tpu_custom_call" | custom-call | flops 2583691264 | bytes 11412484 | tf_op jit(solution)/shard_map/pallas_call | solution.py:504
  20.4 0.5 %collective-permute-start.4 = (bf16[904,256]{1,0:T(8,128)(2,1)S(1)}, bf16[904,256]{1,0:T(8,128)(2,1)S(1)}, u32[]{:S(2)}, u32[]{:S(2)}) collective-permute-start(bf16[904,256]{1,0:T(8,128)(2,1)S(1)} %get-tuple-element.115), channel_id=1, source_target_pairs={{0,1},{1,0},{2,3},{3,2},{4,5},{5,4},{6,7},{7,6},{8,9},{9,8},{10,11... | collective-permute-start | bytes 1388552 | tf_op jit(solution)/shard_map/ppermute | solution.py:30
  20.9 0.5 %collective-permute-start.8 = (bf16[96,256]{1,0:T(8,128)(2,1)S(1)}, bf16[96,256]{1,0:T(8,128)(2,1)S(1)}, u32[]{:S(2)}, u32[]{:S(2)}) collective-permute-start(bf16[96,256]{1,0:T(8,128)(2,1)S(1)} %get-tuple-element.119), channel_id=1, source_target_pairs={{0,4},{4,0},{8,12},{12,8},{1,5},{5,1},{9,13},{13,9},{2,6},{6,2},{1... | collective-permute-start | bytes 147464 | tf_op jit(solution)/shard_map/ppermute | solution.py:30
  21.5 0.9 %collective-permute-done.4.other = bf16[904,256]{1,0:T(8,128)(2,1)S(1)} collective-permute-done((bf16[904,256]{1,0:T(8,128)(2,1)S(1)}, bf16[904,256]{1,0:T(8,128)(2,1)S(1)}, u32[]{:S(2)}, u32[]{:S(2)}) %collective-permute-start.4) | collective-permute-done | bytes 462880 | tf_op jit(solution)/shard_map/ppermute | solution.py:30
  22.4 0.1 shard_map.202
  22.5 1.6 %collective-permute-start.5 = (bf16[232,256]{1,0:T(8,128)(2,1)S(1)}, bf16[232,256]{1,0:T(8,128)(2,1)S(1)}, u32[]{:S(2)}, u32[]{:S(2)}) collective-permute-start(bf16[232,256]{1,0:T(8,128)(2,1)S(1)} %get-tuple-element.116), channel_id=1, source_target_pairs={{0,6},{2,4},{4,2},{6,0},{1,7},{3,5},{5,3},{7,1},{8,14},{10,12},{12... | collective-permute-start | bytes 356360 | tf_op jit(solution)/shard_map/ppermute | solution.py:48
  24.1 1.5 %collective-permute-start.6 = (bf16[232,256]{1,0:T(8,128)(2,1)S(1)}, bf16[232,256]{1,0:T(8,128)(2,1)S(1)}, u32[]{:S(2)}, u32[]{:S(2)}) collective-permute-start(bf16[232,256]{1,0:T(8,128)(2,1)S(1)} %get-tuple-element.117), channel_id=1, source_target_pairs={{0,4},{2,6},{4,0},{6,2},{1,5},{3,7},{5,1},{7,3},{8,12},{10,14},{12... | collective-permute-start | bytes 356360 | tf_op jit(solution)/shard_map/ppermute | solution.py:48
  25.6 0.5 %collective-permute-start.7 = (bf16[232,256]{1,0:T(8,128)(2,1)S(1)}, bf16[232,256]{1,0:T(8,128)(2,1)S(1)}, u32[]{:S(2)}, u32[]{:S(2)}) collective-permute-start(bf16[232,256]{1,0:T(8,128)(2,1)S(1)} %get-tuple-element.118), channel_id=1, source_target_pairs={{0,2},{2,0},{4,6},{6,4},{1,3},{3,1},{5,7},{7,5},{8,10},{10,8},{12,... | collective-permute-start | bytes 356360 | tf_op jit(solution)/shard_map/ppermute | solution.py:48
  26.1 1.8 %collective-permute-start.10 = (bf16[96,256]{1,0:T(8,128)(2,1)S(1)}, bf16[96,256]{1,0:T(8,128)(2,1)S(1)}, u32[]{:S(2)}, u32[]{:S(2)}) collective-permute-start(bf16[96,256]{1,0:T(8,128)(2,1)S(1)} %get-tuple-element.125), channel_id=1, source_target_pairs={{0,12},{4,8},{8,4},{12,0},{1,13},{5,9},{9,5},{13,1},{2,14},{6,10},... | collective-permute-start | bytes 147464 | tf_op jit(solution)/shard_map/ppermute | solution.py:35
  27.9 0.0 collective-permute-done.8.source
  27.9 1.6 %collective-permute-done.5.refs_0_ = bf16[232,256]{1,0:T(8,128)(2,1)S(1)} collective-permute-done((bf16[232,256]{1,0:T(8,128)(2,1)S(1)}, bf16[232,256]{1,0:T(8,128)(2,1)S(1)}, u32[]{:S(2)}, u32[]{:S(2)}) %collective-permute-start.5) | collective-permute-done | bytes 118816 | tf_op jit(solution)/shard_map/ppermute | solution.py:48
  29.6 3.1 %collective-permute-done.6.refs_1_ = bf16[232,256]{1,0:T(8,128)(2,1)S(1)} collective-permute-done((bf16[232,256]{1,0:T(8,128)(2,1)S(1)}, bf16[232,256]{1,0:T(8,128)(2,1)S(1)}, u32[]{:S(2)}, u32[]{:S(2)}) %collective-permute-start.6) | collective-permute-done | bytes 118816 | tf_op jit(solution)/shard_map/ppermute | solution.py:48
  32.6 0.0 collective-permute-done.7.refs_2_
  32.6 0.1 shard_map.204.refs_3_.own
  32.7 0.1 collective-permute-start.9
  32.8 0.0 collective-permute-done.10.refs_1_
  32.8 0.1 collective-permute-start.11
  32.9 0.8 %collective-permute-start.12 = (bf16[96,256]{1,0:T(8,128)(2,1)S(1)}, bf16[96,256]{1,0:T(8,128)(2,1)S(1)}, u32[]{:S(2)}, u32[]{:S(2)}) collective-permute-start(bf16[96,256]{1,0:T(8,128)(2,1)S(1)} %get-tuple-element.128), channel_id=1, source_target_pairs={{0,3},{1,2},{2,1},{3,0},{4,7},{5,6},{6,5},{7,4},{8,11},{9,10},{10,... | collective-permute-start | bytes 147464 | tf_op jit(solution)/shard_map/ppermute | solution.py:35
  33.7 1.3 %shard_map.207 = (bf16[1152,256]{1,0:T(8,128)(2,1)}, f32[384,256]{1,0:T(8,128)S(1)}) custom-call(bf16[1152,256]{1,0:T(8,128)(2,1)S(1)} %get-tuple-element.90.edge_grads, bf16[1152,256]{1,0:T(8,128)(2,1)S(1)} %get-tuple-element.132.pre_grad, bf16[384,256]{1,0:T(8,128)(2,1)S(1)} %get-tuple-element.133.sender_sum, ...), custom_call_target="tpu_custom_call" | custom-call | flops 251658240 | bytes 3342336 | tf_op jit(solution)/shard_map/pallas_call | solution.py:504
  35.1 0.0 collective-permute-done.11.along_core
  35.1 1.4 %collective-permute-done.12.along_chip = bf16[96,256]{1,0:T(8,128)(2,1)S(1)} collective-permute-done((bf16[96,256]{1,0:T(8,128)(2,1)S(1)}, bf16[96,256]{1,0:T(8,128)(2,1)S(1)}, u32[]{:S(2)}, u32[]{:S(2)}) %collective-permute-start.12) | collective-permute-done | bytes 49184 | tf_op jit(solution)/shard_map/ppermute | solution.py:35
  36.5 3.5 %collective-permute-done.9.other = bf16[232,256]{1,0:T(8,128)(2,1)S(1)} collective-permute-done((bf16[232,256]{1,0:T(8,128)(2,1)S(1)}, bf16[232,256]{1,0:T(8,128)(2,1)S(1)}, u32[]{:S(2)}, u32[]{:S(2)}) %collective-permute-start.9) | collective-permute-done | bytes 118816 | tf_op jit(solution)/shard_map/ppermute | solution.py:545
  40.0 1.9 %collective-permute-start.15 = (bf16[224,256]{1,0:T(8,128)(2,1)S(1)}, bf16[224,256]{1,0:T(8,128)(2,1)S(1)}, u32[]{:S(2)}, u32[]{:S(2)}) collective-permute-start(bf16[224,256]{1,0:T(8,128)(2,1)S(1)} %get-tuple-element.156.refs_0_), channel_id=1, source_target_pairs={{0,2},{2,0},{4,6},{6,4},{1,3},{3,1},{5,7},{7,5},{8,10},{10,8},{12,... | collective-permute-start | bytes 344072 | tf_op jit(solution)/shard_map/ppermute | solution.py:48
  41.8 0.0 collective-permute-start.14
  41.8 1.7 %collective-permute-start.13 = (bf16[224,256]{1,0:T(8,128)(2,1)S(1)}, bf16[224,256]{1,0:T(8,128)(2,1)S(1)}, u32[]{:S(2)}, u32[]{:S(2)}) collective-permute-start(bf16[224,256]{1,0:T(8,128)(2,1)S(1)} %get-tuple-element.156.refs_0_), channel_id=1, source_target_pairs={{0,6},{2,4},{4,2},{6,0},{1,7},{3,5},{5,3},{7,1},{8,14},{10,12},{12... | collective-permute-start | bytes 344072 | tf_op jit(solution)/shard_map/ppermute | solution.py:48
  43.5 1.1 %shard_map.208 = bf16[384,256]{1,0:T(8,128)(2,1)} custom-call(s32[8,32]{1,0:T(8,128)S(1)} %get-tuple-element.131.send_list, f32[384,256]{1,0:T(8,128)S(1)} %get-tuple-element.136.local_grad, bf16[64,256]{1,0:T(8,128)(2,1)S(1)} %get-tuple-element.137.center, bf16[96,256]{1,0:T(8,128)(2,1)S(1)} %collective-permute-done.11.along_core, ...), custom_call_target="tpu_custom_call" | custom-call | flops 50331648 | bytes 721920 | tf_op jit(solution)/shard_map/pallas_call | solution.py:504
  44.7 0.5 %convert_reduce_fusion = (bf16[256]{0:T(256)(128)(2,1)}, bf16[256]{0:T(256)(128)(2,1)}) fusion(f32[8,256]{1,0:T(8,128)S(1)} %get-tuple-element.141), kind=kLoop, calls=%fused_computation | loop fusion | flops 1024 | bytes 5120 | tf_op jit(solution)/shard_map/convert_element_type | solution.py:759
  45.2 0.0 collective-permute-start.16
  45.2 0.0 collective-permute-done.15.refs_1_
  45.2 0.5 collective-permute-start.17
  45.7 2.2 %collective-permute-done.14.refs_2_ = bf16[224,256]{1,0:T(8,128)(2,1)S(1)} collective-permute-done((bf16[224,256]{1,0:T(8,128)(2,1)S(1)}, bf16[224,256]{1,0:T(8,128)(2,1)S(1)}, u32[]{:S(2)}, u32[]{:S(2)}) %collective-permute-start.14) | collective-permute-done | bytes 114720 | tf_op jit(solution)/shard_map/ppermute | solution.py:48
  47.9 0.0 collective-permute-start.18
  47.9 1.0 %collective-permute-done.13.refs_3_ = bf16[224,256]{1,0:T(8,128)(2,1)S(1)} collective-permute-done((bf16[224,256]{1,0:T(8,128)(2,1)S(1)}, bf16[224,256]{1,0:T(8,128)(2,1)S(1)}, u32[]{:S(2)}, u32[]{:S(2)}) %collective-permute-start.13) | collective-permute-done | bytes 114720 | tf_op jit(solution)/shard_map/ppermute | solution.py:48
  48.9 0.0 collective-permute-start.19
  48.9 0.0 collective-permute-done.16.refs_4_
  48.9 0.0 collective-permute-done.17.refs_5_
  48.9 0.3 collective-permute-done.18.refs_6_
  49.2 1.0 %collective-permute-done.19.refs_7_ = bf16[224,256]{1,0:T(8,128)(2,1)S(1)} collective-permute-done((bf16[224,256]{1,0:T(8,128)(2,1)S(1)}, bf16[224,256]{1,0:T(8,128)(2,1)S(1)}, u32[]{:S(2)}, u32[]{:S(2)}) %collective-permute-start.19) | collective-permute-done | bytes 114720 | tf_op jit(solution)/shard_map/ppermute | solution.py:30
  50.2 1.0 %shard_map.209 = (bf16[768,256]{1,0:T(8,128)(2,1)}, bf16[256,256]{1,0:T(8,128)(2,1)}, bf16[512,256]{1,0:T(8,128)(2,1)}, bf16[256,256]{1,0:T(8,128)(2,1)}) custom-call(bf16[224,256]{1,0:T(8,128)(2,1)S(1)} %get-tuple-element.156.refs_0_, bf16[224,256]{1,0:T(8,128)(2,1)S(1)} %collective-permute-done.15.refs_1_, ...), custom_call_target="tpu_custom_call" | custom-call | bytes 1835008 | tf_op jit(solution)/shard_map/pallas_call | solution.py:504
  (4 shorter events, 0.1 us)
Async XLA Ops:
  2.0 7.5 %collective-permute-start = (bf16[96,256]{1,0:T(8,128)(2,1)S(1)}, bf16[96,256]{1,0:T(8,128)(2,1)S(1)}, u32[]{:S(2)}, u32[]{:S(2)}) collective-permute-start(bf16[96,256]{1,0:T(8,128)(2,1)S(1)} %get-tuple-element.93), channel_id=1, source_target_pairs={{0,12},{4,8},{8,4},{12,0},{1,13},{5,9},{9,5},{13,1},{2,14},{6,10},... | collective-permute-start | bytes 147464 | tf_op jit(solution)/shard_map/ppermute | solution.py:35
  7.1 4.1 %collective-permute-start.1 = (bf16[96,256]{1,0:T(8,128)(2,1)S(1)}, bf16[96,256]{1,0:T(8,128)(2,1)S(1)}, u32[]{:S(2)}, u32[]{:S(2)}) collective-permute-start(bf16[96,256]{1,0:T(8,128)(2,1)S(1)} %get-tuple-element.94), channel_id=1, source_target_pairs={{0,4},{4,0},{8,12},{12,8},{1,5},{5,1},{9,13},{13,9},{2,6},{6,2},{1... | collective-permute-start | bytes 147464 | tf_op jit(solution)/shard_map/ppermute | solution.py:30
  11.2 3.5 %collective-permute-start.2 = (bf16[96,256]{1,0:T(8,128)(2,1)S(1)}, bf16[96,256]{1,0:T(8,128)(2,1)S(1)}, u32[]{:S(2)}, u32[]{:S(2)}) collective-permute-start(bf16[96,256]{1,0:T(8,128)(2,1)S(1)} %get-tuple-element.106), channel_id=1, source_target_pairs={{0,1},{1,0},{2,3},{3,2},{4,5},{5,4},{6,7},{7,6},{8,9},{9,8},{10,11... | collective-permute-start | bytes 147464 | tf_op jit(solution)/shard_map/ppermute | solution.py:30
  11.3 3.6 %collective-permute-start.3 = (bf16[96,256]{1,0:T(8,128)(2,1)S(1)}, bf16[96,256]{1,0:T(8,128)(2,1)S(1)}, u32[]{:S(2)}, u32[]{:S(2)}) collective-permute-start(bf16[96,256]{1,0:T(8,128)(2,1)S(1)} %get-tuple-element.107), channel_id=1, source_target_pairs={{0,3},{1,2},{2,1},{3,0},{4,7},{5,6},{6,5},{7,4},{8,11},{9,10},{10,... | collective-permute-start | bytes 147464 | tf_op jit(solution)/shard_map/ppermute | solution.py:35
  20.4 2.0 %collective-permute-start.4 = (bf16[904,256]{1,0:T(8,128)(2,1)S(1)}, bf16[904,256]{1,0:T(8,128)(2,1)S(1)}, u32[]{:S(2)}, u32[]{:S(2)}) collective-permute-start(bf16[904,256]{1,0:T(8,128)(2,1)S(1)} %get-tuple-element.115), channel_id=1, source_target_pairs={{0,1},{1,0},{2,3},{3,2},{4,5},{5,4},{6,7},{7,6},{8,9},{9,8},{10,11... | collective-permute-start | bytes 1388552 | tf_op jit(solution)/shard_map/ppermute | solution.py:30
  20.9 7.0 %collective-permute-start.8 = (bf16[96,256]{1,0:T(8,128)(2,1)S(1)}, bf16[96,256]{1,0:T(8,128)(2,1)S(1)}, u32[]{:S(2)}, u32[]{:S(2)}) collective-permute-start(bf16[96,256]{1,0:T(8,128)(2,1)S(1)} %get-tuple-element.119), channel_id=1, source_target_pairs={{0,4},{4,0},{8,12},{12,8},{1,5},{5,1},{9,13},{13,9},{2,6},{6,2},{1... | collective-permute-start | bytes 147464 | tf_op jit(solution)/shard_map/ppermute | solution.py:30
  22.5 7.0 %collective-permute-start.5 = (bf16[232,256]{1,0:T(8,128)(2,1)S(1)}, bf16[232,256]{1,0:T(8,128)(2,1)S(1)}, u32[]{:S(2)}, u32[]{:S(2)}) collective-permute-start(bf16[232,256]{1,0:T(8,128)(2,1)S(1)} %get-tuple-element.116), channel_id=1, source_target_pairs={{0,6},{2,4},{4,2},{6,0},{1,7},{3,5},{5,3},{7,1},{8,14},{10,12},{12... | collective-permute-start | bytes 356360 | tf_op jit(solution)/shard_map/ppermute | solution.py:48
  24.1 8.5 %collective-permute-start.6 = (bf16[232,256]{1,0:T(8,128)(2,1)S(1)}, bf16[232,256]{1,0:T(8,128)(2,1)S(1)}, u32[]{:S(2)}, u32[]{:S(2)}) collective-permute-start(bf16[232,256]{1,0:T(8,128)(2,1)S(1)} %get-tuple-element.117), channel_id=1, source_target_pairs={{0,4},{2,6},{4,0},{6,2},{1,5},{3,7},{5,1},{7,3},{8,12},{10,14},{12... | collective-permute-start | bytes 356360 | tf_op jit(solution)/shard_map/ppermute | solution.py:48
  25.6 7.1 %collective-permute-start.7 = (bf16[232,256]{1,0:T(8,128)(2,1)S(1)}, bf16[232,256]{1,0:T(8,128)(2,1)S(1)}, u32[]{:S(2)}, u32[]{:S(2)}) collective-permute-start(bf16[232,256]{1,0:T(8,128)(2,1)S(1)} %get-tuple-element.118), channel_id=1, source_target_pairs={{0,2},{2,0},{4,6},{6,4},{1,3},{3,1},{5,7},{7,5},{8,10},{10,8},{12,... | collective-permute-start | bytes 356360 | tf_op jit(solution)/shard_map/ppermute | solution.py:48
  26.1 6.7 %collective-permute-start.10 = (bf16[96,256]{1,0:T(8,128)(2,1)S(1)}, bf16[96,256]{1,0:T(8,128)(2,1)S(1)}, u32[]{:S(2)}, u32[]{:S(2)}) collective-permute-start(bf16[96,256]{1,0:T(8,128)(2,1)S(1)} %get-tuple-element.125), channel_id=1, source_target_pairs={{0,12},{4,8},{8,4},{12,0},{1,13},{5,9},{9,5},{13,1},{2,14},{6,10},... | collective-permute-start | bytes 147464 | tf_op jit(solution)/shard_map/ppermute | solution.py:35
  32.7 7.2 %collective-permute-start.9 = (bf16[232,256]{1,0:T(8,128)(2,1)S(1)}, bf16[232,256]{1,0:T(8,128)(2,1)S(1)}, u32[]{:S(2)}, u32[]{:S(2)}) collective-permute-start(bf16[232,256]{1,0:T(8,128)(2,1)S(1)} %shard_map.204.refs_3_.own), channel_id=1, source_target_pairs={{0,8},{8,0},{1,9},{9,1},{2,10},{10,2},{3,11},{11,3},{4,12},{12,4},... | collective-permute-start | bytes 356360 | tf_op jit(solution)/shard_map/ppermute | solution.py:545
  32.8 2.3 %collective-permute-start.11 = (bf16[96,256]{1,0:T(8,128)(2,1)S(1)}, bf16[96,256]{1,0:T(8,128)(2,1)S(1)}, u32[]{:S(2)}, u32[]{:S(2)}) collective-permute-start(bf16[96,256]{1,0:T(8,128)(2,1)S(1)} %get-tuple-element.127), channel_id=1, source_target_pairs={{0,1},{1,0},{2,3},{3,2},{4,5},{5,4},{6,7},{7,6},{8,9},{9,8},{10,11... | collective-permute-start | bytes 147464 | tf_op jit(solution)/shard_map/ppermute | solution.py:30
  32.9 3.6 %collective-permute-start.12 = (bf16[96,256]{1,0:T(8,128)(2,1)S(1)}, bf16[96,256]{1,0:T(8,128)(2,1)S(1)}, u32[]{:S(2)}, u32[]{:S(2)}) collective-permute-start(bf16[96,256]{1,0:T(8,128)(2,1)S(1)} %get-tuple-element.128), channel_id=1, source_target_pairs={{0,3},{1,2},{2,1},{3,0},{4,7},{5,6},{6,5},{7,4},{8,11},{9,10},{10,... | collective-permute-start | bytes 147464 | tf_op jit(solution)/shard_map/ppermute | solution.py:35
  40.0 5.2 %collective-permute-start.15 = (bf16[224,256]{1,0:T(8,128)(2,1)S(1)}, bf16[224,256]{1,0:T(8,128)(2,1)S(1)}, u32[]{:S(2)}, u32[]{:S(2)}) collective-permute-start(bf16[224,256]{1,0:T(8,128)(2,1)S(1)} %get-tuple-element.156.refs_0_), channel_id=1, source_target_pairs={{0,2},{2,0},{4,6},{6,4},{1,3},{3,1},{5,7},{7,5},{8,10},{10,8},{12,... | collective-permute-start | bytes 344072 | tf_op jit(solution)/shard_map/ppermute | solution.py:48
  41.8 6.0 %collective-permute-start.14 = (bf16[224,256]{1,0:T(8,128)(2,1)S(1)}, bf16[224,256]{1,0:T(8,128)(2,1)S(1)}, u32[]{:S(2)}, u32[]{:S(2)}) collective-permute-start(bf16[224,256]{1,0:T(8,128)(2,1)S(1)} %get-tuple-element.156.refs_0_), channel_id=1, source_target_pairs={{0,4},{2,6},{4,0},{6,2},{1,5},{3,7},{5,1},{7,3},{8,12},{10,14},{12... | collective-permute-start | bytes 344072 | tf_op jit(solution)/shard_map/ppermute | solution.py:48
  41.8 7.0 %collective-permute-start.13 = (bf16[224,256]{1,0:T(8,128)(2,1)S(1)}, bf16[224,256]{1,0:T(8,128)(2,1)S(1)}, u32[]{:S(2)}, u32[]{:S(2)}) collective-permute-start(bf16[224,256]{1,0:T(8,128)(2,1)S(1)} %get-tuple-element.156.refs_0_), channel_id=1, source_target_pairs={{0,6},{2,4},{4,2},{6,0},{1,7},{3,5},{5,3},{7,1},{8,14},{10,12},{12... | collective-permute-start | bytes 344072 | tf_op jit(solution)/shard_map/ppermute | solution.py:48
  45.2 3.7 %collective-permute-start.16 = (bf16[224,256]{1,0:T(8,128)(2,1)S(1)}, bf16[224,256]{1,0:T(8,128)(2,1)S(1)}, u32[]{:S(2)}, u32[]{:S(2)}) collective-permute-start(bf16[224,256]{1,0:T(8,128)(2,1)S(1)} %get-tuple-element.156.refs_0_), channel_id=1, source_target_pairs={{0,1},{1,0},{2,3},{3,2},{4,5},{5,4},{6,7},{7,6},{8,9},{9,8},{10,11... | collective-permute-start | bytes 344072 | tf_op jit(solution)/shard_map/ppermute | solution.py:30
  45.2 3.7 %collective-permute-start.17 = (bf16[224,256]{1,0:T(8,128)(2,1)S(1)}, bf16[224,256]{1,0:T(8,128)(2,1)S(1)}, u32[]{:S(2)}, u32[]{:S(2)}) collective-permute-start(bf16[224,256]{1,0:T(8,128)(2,1)S(1)} %collective-permute-done.15.refs_1_), channel_id=1, source_target_pairs={{0,1},{1,0},{2,3},{3,2},{4,5},{5,4},{6,7},{7,6},{8,9},{9,8},{10,11... | collective-permute-start | bytes 344072 | tf_op jit(solution)/shard_map/ppermute | solution.py:30
  47.9 1.3 %collective-permute-start.18 = (bf16[224,256]{1,0:T(8,128)(2,1)S(1)}, bf16[224,256]{1,0:T(8,128)(2,1)S(1)}, u32[]{:S(2)}, u32[]{:S(2)}) collective-permute-start(bf16[224,256]{1,0:T(8,128)(2,1)S(1)} %collective-permute-done.14.refs_2_), channel_id=1, source_target_pairs={{0,1},{1,0},{2,3},{3,2},{4,5},{5,4},{6,7},{7,6},{8,9},{9,8},{10,11... | collective-permute-start | bytes 344072 | tf_op jit(solution)/shard_map/ppermute | solution.py:30
  48.9 1.3 %collective-permute-start.19 = (bf16[224,256]{1,0:T(8,128)(2,1)S(1)}, bf16[224,256]{1,0:T(8,128)(2,1)S(1)}, u32[]{:S(2)}, u32[]{:S(2)}) collective-permute-start(bf16[224,256]{1,0:T(8,128)(2,1)S(1)} %collective-permute-done.13.refs_3_), channel_id=1, source_target_pairs={{0,1},{1,0},{2,3},{3,2},{4,5},{5,4},{6,7},{7,6},{8,9},{9,8},{10,11... | collective-permute-start | bytes 344072 | tf_op jit(solution)/shard_map/ppermute | solution.py:30

commit v19 on v18

--- a/solution.py
+++ b/solution.py
@@ -161,16 +161,18 @@
     return copies
 
 
-def send_kernel(nodes_hbm, list_hbm, outer, inner, middle, nodes, send_list, sems):
+def send_kernel(nodes_hbm, list_hbm, inner, outer, middle, nodes, send_list, sems):
     slots = send_list.shape[1]
-    for copy in fetch_all([list_hbm, nodes_hbm], [send_list, nodes], sems):
-        copy.wait()
-    rows = dot(list_hot(send_list[...], nodes.shape[0]), nodes[...]).astype(BF16)
+    list_copy, nodes_copy = fetch_all([list_hbm, nodes_hbm], [send_list, nodes], sems)
+    list_copy.wait()
+    hot = list_hot(send_list[...], nodes.shape[0])
+    nodes_copy.wait()
+    rows = dot(hot, nodes[...]).astype(BF16)
     by_pair(NEAR, rows[5 * slots :], rows[: 3 * slots], inner, outer)
     middle[...] = rows[3 * slots : 5 * slots]
 
 
-def corner_kernel(outer, inner, middle, along_core, along_chip, straight):
+def corner_kernel(inner, outer, middle, along_core, along_chip, straight):
     slots = middle.shape[0] // 2
     low, high = from_pair(NEAR, inner[...], outer[...])
     up = jnp.concatenate([high[2 * slots :], middle[slots:], low[2 * slots :]], axis=0)
@@ -415,22 +417,23 @@
     members = len(blocks) // 2
     core = lax.axis_index(CORE)
     me = place_in_square()
-    for position, block in enumerate(blocks):
-        half = core if position < members else 1 - core
-        owner = me ^ (position % members)
-        at = 0
-        for part, whole in zip(parts, wholes):
-            step = part // members
+    copies = []
+    at = 0
+    for i, (part, whole) in enumerate(zip(parts, wholes)):
+        step = part // members
+        for position, block in enumerate(blocks):
+            half = core if position < members else 1 - core
+            owner = me ^ (position % members)
             row = pl.multiple_of(half * part + owner * step, 16)
             whole[pl.ds(row, step), :] = block[at : at + step]
-            at += step
-    copies = []
-    for i, whole in enumerate(wholes):
+        at += step
         cut = outs[2 * i].shape[0]
-        copies.append(pltpu.make_async_copy(whole.at[:cut], outs[2 * i], sems.at[2 * i]))
-        copies.append(pltpu.make_async_copy(whole.at[cut:], outs[2 * i + 1], sems.at[2 * i + 1]))
-    for copy in copies:
-        copy.start()
+        copies += [
+            pltpu.make_async_copy(whole.at[:cut], outs[2 * i], sems.at[2 * i]),
+            pltpu.make_async_copy(whole.at[cut:], outs[2 * i + 1], sems.at[2 * i + 1]),
+        ]
+        for copy in copies[-2:]:
+            copy.start()
     for copy in copies:
         copy.wait()
 
@@ -580,7 +583,7 @@
     edge_rows = edges.shape[0]
     tile_rows = senders.shape[1]
     square = 2 * width * width
-    outer, inner, middle, nodes, send_list = call(
+    inner, outer, middle, nodes, send_list = call(
         send_kernel,
         [
             shaped(3 * slots, width, BF16),
@@ -595,8 +598,8 @@
         spaces=[HBM, HBM],
         scratch=[pltpu.SemaphoreType.DMA((2,))],
     )
+    inner = in_pair(inner, PX)
     outer = out_of_pair(outer, PX)
-    inner = in_pair(inner, PX)
     fetched = [
         senders,
         receivers,
@@ -635,7 +638,7 @@
         node_grads,
         edge_grads,
     ) = fetched
-    outer, inner, near_hot = lax.optimization_barrier((outer, inner, near_hot))
+    inner, outer, near_hot = lax.optimization_barrier((inner, outer, near_hot))
     along_core, along_chip, straight = call(
         corner_kernel,
         [
@@ -644,8 +647,8 @@
             shaped(2 * slots, width, BF16),
         ],
         0,
+        inner,
         outer,
-        inner,
         middle,
     )
     along_chip = out_of_pair(along_chip, PY)

time: 51.4 us -> 51 us (level)
  waiting for transfers between devices: 16.8 us -> 14.6 us
  starting transfers between devices: 18.3 us -> 20.2 us
    ppermute x9, starting transfers between devices: 1.71 us -> 4.27 us  [in_pair(): lax.ppermute(array, axis, [(i, i ^ 1) for i in range(lax.axis_size(axis))])]
    ppermute x4, starting transfers between devices: 9.38 us -> 7.51 us  [out_of_pair(): lax.ppermute(array, axis, [(i, other_neighbour(i, size)) for i in range(s...]
    ppermute x6, waiting for transfers between devices: 7.89 us -> 6.38 us  [in_square(): lax.ppermute(array, SQUARE, [(i, i ^ offset) for i in range(square_member...]
    ppermute x1, starting transfers between devices: 0.07 us -> 1.31 us  [joined(): other = lax.ppermute(sums, FAR, [(i, i ^ distance) for i in range(size)])]
    ppermute x9, waiting for transfers between devices: 3.92 us -> 2.77 us  [in_pair(): lax.ppermute(array, axis, [(i, i ^ 1) for i in range(lax.axis_size(axis))])]
    ppermute x4, waiting for transfers between devices: 1.54 us -> 2.43 us  [out_of_pair(): lax.ppermute(array, axis, [(i, other_neighbour(i, size)) for i in range(s...]
where the time goes in v19:
time: 51 us; the launch traced here: 50.7 us
  starting transfers between devices  20.2 us (40%)
  waiting for transfers between devices  14.6 us (29%)
  Pallas kernels  14 us (27%)
  between operations  1.39 us (3%)
  other arithmetic  0.53 us (1%)
    pallas_call x13, Pallas kernels, call(): pl.pallas_call(body, out_shape=outs, in_specs=[pl.BlockSpec(memory_space=...  14 us
    ppermute x4, starting transfers between devices, out_of_pair(): lax.ppermute(array, axis, [(i, other_neighbour(i, size)) for i in range(s...  7.51 us
    ppermute x6, starting transfers between devices, in_square(): lax.ppermute(array, SQUARE, [(i, i ^ offset) for i in range(square_member...  7.12 us
    ppermute x6, waiting for transfers between devices, in_square(): lax.ppermute(array, SQUARE, [(i, i ^ offset) for i in range(square_member...  6.38 us
    ppermute x9, starting transfers between devices, in_pair(): lax.ppermute(array, axis, [(i, i ^ 1) for i in range(lax.axis_size(axis))])  4.27 us
    ppermute x1, waiting for transfers between devices, joined(): other = lax.ppermute(sums, FAR, [(i, i ^ distance) for i in range(size)])  2.98 us
    ppermute x9, waiting for transfers between devices, in_pair(): lax.ppermute(array, axis, [(i, i ^ 1) for i in range(lax.axis_size(axis))])  2.77 us
    ppermute x4, waiting for transfers between devices, out_of_pair(): lax.ppermute(array, axis, [(i, other_neighbour(i, size)) for i in range(s...  2.43 us
  transfers between devices with their start and end apart: 20, of which 11 were waited for; matrix products, arithmetic and copies ran while one was open for 1% of the time, Pallas kernels for 12%

profile of v19, /device:TPU:0, one launch (start us, length us, event | category | flops | bytes accessed | tf_op | source)
XLA Modules:
  0.0 50.7 jit_solution(2743664562260804448)
XLA Ops:
  0.6 1.2 %shard_map.197 = (bf16[96,256]{1,0:T(8,128)(2,1)S(1)}, bf16[96,256]{1,0:T(8,128)(2,1)S(1)}, bf16[64,256]{1,0:T(8,128)(2,1)S(1)}, bf16[384,256]{1,0:T(8,128)(2,1)S(1)}, s32[8,32]{1,0:T(8,128)S(1)}) custom-call(bf16[384,256]{1,0:T(8,128)(2,1)} %nodes_hbm.1, s32[8,32]{1,0:T(8,128)} %list_hbm.1), custom_call_target="tpu_custom_call" | custom-call | flops 50331648 | bytes 526336 | tf_op jit(solution)/shard_map/pallas_call | solution.py:507
  1.8 3.1 %collective-permute-start = (bf16[96,256]{1,0:T(8,128)(2,1)S(1)}, bf16[96,256]{1,0:T(8,128)(2,1)S(1)}, u32[]{:S(2)}, u32[]{:S(2)}) collective-permute-start(bf16[96,256]{1,0:T(8,128)(2,1)S(1)} %get-tuple-element.93), channel_id=1, source_target_pairs={{0,4},{4,0},{8,12},{12,8},{1,5},{5,1},{9,13},{13,9},{2,6},{6,2},{1... | collective-permute-start | bytes 147464 | tf_op jit(solution)/shard_map/ppermute | solution.py:30
  4.9 2.5 %collective-permute-start.1 = (bf16[96,256]{1,0:T(8,128)(2,1)S(1)}, bf16[96,256]{1,0:T(8,128)(2,1)S(1)}, u32[]{:S(2)}, u32[]{:S(2)}) collective-permute-start(bf16[96,256]{1,0:T(8,128)(2,1)S(1)} %get-tuple-element.94), channel_id=1, source_target_pairs={{0,12},{4,8},{8,4},{12,0},{1,13},{5,9},{9,5},{13,1},{2,14},{6,10},... | collective-permute-start | bytes 147464 | tf_op jit(solution)/shard_map/ppermute | solution.py:35
  8.0 1.7 %shard_map.198 = (bf16[1152,768]{1,0:T(8,128)(2,1)S(1)}, bf16[1152,256]{1,0:T(8,128)(2,1)S(1)}, s32[9,128]{1,0:T(8,128)S(1)}, s32[9,128]{1,0:T(8,128)S(1)}, bf16...) custom-call(s32[9,128]{1,0:T(8,128)} %refs_0_.1, ...), custom_call_target="tpu_custom_call" | custom-call | bytes 6967296 | tf_op jit(solution)/shard_map/pallas_call | solution.py:507
  9.8 0.0 collective-permute-done.inner
  9.8 1.0 %collective-permute-done.1.outer = bf16[96,256]{1,0:T(8,128)(2,1)S(1)} collective-permute-done((bf16[96,256]{1,0:T(8,128)(2,1)S(1)}, bf16[96,256]{1,0:T(8,128)(2,1)S(1)}, u32[]{:S(2)}, u32[]{:S(2)}) %collective-permute-start.1) | collective-permute-done | bytes 49184 | tf_op jit(solution)/shard_map/ppermute | solution.py:35
  10.8 0.1 collective-permute-start.2
  10.9 1.6 %collective-permute-start.3 = (bf16[96,256]{1,0:T(8,128)(2,1)S(1)}, bf16[96,256]{1,0:T(8,128)(2,1)S(1)}, u32[]{:S(2)}, u32[]{:S(2)}) collective-permute-start(bf16[96,256]{1,0:T(8,128)(2,1)S(1)} %get-tuple-element.107), channel_id=1, source_target_pairs={{0,3},{1,2},{2,1},{3,0},{4,7},{5,6},{6,5},{7,4},{8,11},{9,10},{10,... | collective-permute-start | bytes 147464 | tf_op jit(solution)/shard_map/ppermute | solution.py:35
  12.5 1.8 %shard_map.199 = (f32[1152,256]{1,0:T(8,128)S(1)}, bf16[640,1152]{1,0:T(8,128)(2,1)S(1)}, bf16[384,1152]{1,0:T(8,128)(2,1)S(1)}) custom-call(bf16[384,256]{1,0:T(8,128)(2,1)S(1)} %get-tuple-element.87.nodes, bf16[1152,256]{1,0:T(8,128)(2,1)S(1)} %get-tuple-element.89.edges, s32[9,128]{1,0:T(8,128)S(1)} %get-tuple-element.91.senders, ...), custom_call_target="tpu_custom_call" | custom-call | flops 704643072 | bytes 6497280 | tf_op jit(solution)/shard_map/pallas_call | solution.py:507
  14.4 0.0 collective-permute-done.2.along_core
  14.4 0.1 collective-permute-done.3.along_chip
  14.5 5.6 %shard_map.201 = (bf16[1152,256]{1,0:T(8,128)(2,1)S(1)}, bf16[384,256]{1,0:T(8,128)(2,1)S(1)}, bf16[384,256]{1,0:T(8,128)(2,1)S(1)}, f32[384,256]{1,0:T(8,128)S(...) custom-call(s32[1]{0:T(128)S(6)} %copy.22.count_ref, ...), custom_call_target="tpu_custom_call" | custom-call | flops 2583691264 | bytes 11412484 | tf_op jit(solution)/shard_map/pallas_call | solution.py:507
  20.1 0.5 %collective-permute-start.4 = (bf16[904,256]{1,0:T(8,128)(2,1)S(1)}, bf16[904,256]{1,0:T(8,128)(2,1)S(1)}, u32[]{:S(2)}, u32[]{:S(2)}) collective-permute-start(bf16[904,256]{1,0:T(8,128)(2,1)S(1)} %get-tuple-element.115), channel_id=1, source_target_pairs={{0,1},{1,0},{2,3},{3,2},{4,5},{5,4},{6,7},{7,6},{8,9},{9,8},{10,11... | collective-permute-start | bytes 1388552 | tf_op jit(solution)/shard_map/ppermute | solution.py:30
  20.6 0.0 collective-permute-start.8
  20.6 1.4 %collective-permute-done.4.other = bf16[904,256]{1,0:T(8,128)(2,1)S(1)} collective-permute-done((bf16[904,256]{1,0:T(8,128)(2,1)S(1)}, bf16[904,256]{1,0:T(8,128)(2,1)S(1)}, u32[]{:S(2)}, u32[]{:S(2)}) %collective-permute-start.4) | collective-permute-done | bytes 462880 | tf_op jit(solution)/shard_map/ppermute | solution.py:30
  22.0 0.1 shard_map.202
  22.2 1.6 %collective-permute-start.5 = (bf16[232,256]{1,0:T(8,128)(2,1)S(1)}, bf16[232,256]{1,0:T(8,128)(2,1)S(1)}, u32[]{:S(2)}, u32[]{:S(2)}) collective-permute-start(bf16[232,256]{1,0:T(8,128)(2,1)S(1)} %get-tuple-element.116), channel_id=1, source_target_pairs={{0,6},{2,4},{4,2},{6,0},{1,7},{3,5},{5,3},{7,1},{8,14},{10,12},{12... | collective-permute-start | bytes 356360 | tf_op jit(solution)/shard_map/ppermute | solution.py:48
  23.8 1.5 %collective-permute-start.6 = (bf16[232,256]{1,0:T(8,128)(2,1)S(1)}, bf16[232,256]{1,0:T(8,128)(2,1)S(1)}, u32[]{:S(2)}, u32[]{:S(2)}) collective-permute-start(bf16[232,256]{1,0:T(8,128)(2,1)S(1)} %get-tuple-element.117), channel_id=1, source_target_pairs={{0,4},{2,6},{4,0},{6,2},{1,5},{3,7},{5,1},{7,3},{8,12},{10,14},{12... | collective-permute-start | bytes 356360 | tf_op jit(solution)/shard_map/ppermute | solution.py:48
  25.2 0.5 %collective-permute-start.7 = (bf16[232,256]{1,0:T(8,128)(2,1)S(1)}, bf16[232,256]{1,0:T(8,128)(2,1)S(1)}, u32[]{:S(2)}, u32[]{:S(2)}) collective-permute-start(bf16[232,256]{1,0:T(8,128)(2,1)S(1)} %get-tuple-element.118), channel_id=1, source_target_pairs={{0,2},{2,0},{4,6},{6,4},{1,3},{3,1},{5,7},{7,5},{8,10},{10,8},{12,... | collective-permute-start | bytes 356360 | tf_op jit(solution)/shard_map/ppermute | solution.py:48
  25.7 2.5 %collective-permute-start.10 = (bf16[96,256]{1,0:T(8,128)(2,1)S(1)}, bf16[96,256]{1,0:T(8,128)(2,1)S(1)}, u32[]{:S(2)}, u32[]{:S(2)}) collective-permute-start(bf16[96,256]{1,0:T(8,128)(2,1)S(1)} %get-tuple-element.125), channel_id=1, source_target_pairs={{0,12},{4,8},{8,4},{12,0},{1,13},{5,9},{9,5},{13,1},{2,14},{6,10},... | collective-permute-start | bytes 147464 | tf_op jit(solution)/shard_map/ppermute | solution.py:35
  28.2 0.0 collective-permute-done.8.source
  28.2 1.0 %collective-permute-done.5.refs_0_ = bf16[232,256]{1,0:T(8,128)(2,1)S(1)} collective-permute-done((bf16[232,256]{1,0:T(8,128)(2,1)S(1)}, bf16[232,256]{1,0:T(8,128)(2,1)S(1)}, u32[]{:S(2)}, u32[]{:S(2)}) %collective-permute-start.5) | collective-permute-done | bytes 118816 | tf_op jit(solution)/shard_map/ppermute | solution.py:48
  29.2 2.4 %collective-permute-done.6.refs_1_ = bf16[232,256]{1,0:T(8,128)(2,1)S(1)} collective-permute-done((bf16[232,256]{1,0:T(8,128)(2,1)S(1)}, bf16[232,256]{1,0:T(8,128)(2,1)S(1)}, u32[]{:S(2)}, u32[]{:S(2)}) %collective-permute-start.6) | collective-permute-done | bytes 118816 | tf_op jit(solution)/shard_map/ppermute | solution.py:48
  31.6 0.0 collective-permute-done.7.refs_2_
  31.6 0.1 shard_map.204.refs_3_.own
  31.7 1.3 %collective-permute-start.9 = (bf16[232,256]{1,0:T(8,128)(2,1)S(1)}, bf16[232,256]{1,0:T(8,128)(2,1)S(1)}, u32[]{:S(2)}, u32[]{:S(2)}) collective-permute-start(bf16[232,256]{1,0:T(8,128)(2,1)S(1)} %shard_map.204.refs_3_.own), channel_id=1, source_target_pairs={{0,8},{8,0},{1,9},{9,1},{2,10},{10,2},{3,11},{11,3},{4,12},{12,4},... | collective-permute-start | bytes 356360 | tf_op jit(solution)/shard_map/ppermute | solution.py:548
  33.0 0.0 collective-permute-done.10.refs_1_
  33.0 0.1 collective-permute-start.11
  33.1 0.9 %collective-permute-start.12 = (bf16[96,256]{1,0:T(8,128)(2,1)S(1)}, bf16[96,256]{1,0:T(8,128)(2,1)S(1)}, u32[]{:S(2)}, u32[]{:S(2)}) collective-permute-start(bf16[96,256]{1,0:T(8,128)(2,1)S(1)} %get-tuple-element.128), channel_id=1, source_target_pairs={{0,3},{1,2},{2,1},{3,0},{4,7},{5,6},{6,5},{7,4},{8,11},{9,10},{10,... | collective-permute-start | bytes 147464 | tf_op jit(solution)/shard_map/ppermute | solution.py:35
  34.1 1.3 %shard_map.207 = (bf16[1152,256]{1,0:T(8,128)(2,1)}, f32[384,256]{1,0:T(8,128)S(1)}) custom-call(bf16[1152,256]{1,0:T(8,128)(2,1)S(1)} %get-tuple-element.90.edge_grads, bf16[1152,256]{1,0:T(8,128)(2,1)S(1)} %get-tuple-element.132.pre_grad, bf16[384,256]{1,0:T(8,128)(2,1)S(1)} %get-tuple-element.133.sender_sum, ...), custom_call_target="tpu_custom_call" | custom-call | flops 251658240 | bytes 3342336 | tf_op jit(solution)/shard_map/pallas_call | solution.py:507
  35.4 0.0 collective-permute-done.11.along_core
  35.4 1.3 %collective-permute-done.12.along_chip = bf16[96,256]{1,0:T(8,128)(2,1)S(1)} collective-permute-done((bf16[96,256]{1,0:T(8,128)(2,1)S(1)}, bf16[96,256]{1,0:T(8,128)(2,1)S(1)}, u32[]{:S(2)}, u32[]{:S(2)}) %collective-permute-start.12) | collective-permute-done | bytes 49184 | tf_op jit(solution)/shard_map/ppermute | solution.py:35
  36.7 3.0 %collective-permute-done.9.other = bf16[232,256]{1,0:T(8,128)(2,1)S(1)} collective-permute-done((bf16[232,256]{1,0:T(8,128)(2,1)S(1)}, bf16[232,256]{1,0:T(8,128)(2,1)S(1)}, u32[]{:S(2)}, u32[]{:S(2)}) %collective-permute-start.9) | collective-permute-done | bytes 118816 | tf_op jit(solution)/shard_map/ppermute | solution.py:548
  39.7 1.6 %collective-permute-start.15 = (bf16[224,256]{1,0:T(8,128)(2,1)S(1)}, bf16[224,256]{1,0:T(8,128)(2,1)S(1)}, u32[]{:S(2)}, u32[]{:S(2)}) collective-permute-start(bf16[224,256]{1,0:T(8,128)(2,1)S(1)} %get-tuple-element.156.refs_0_), channel_id=1, source_target_pairs={{0,2},{2,0},{4,6},{6,4},{1,3},{3,1},{5,7},{7,5},{8,10},{10,8},{12,... | collective-permute-start | bytes 344072 | tf_op jit(solution)/shard_map/ppermute | solution.py:48
  41.4 0.0 collective-permute-start.14
  41.4 1.9 %collective-permute-start.13 = (bf16[224,256]{1,0:T(8,128)(2,1)S(1)}, bf16[224,256]{1,0:T(8,128)(2,1)S(1)}, u32[]{:S(2)}, u32[]{:S(2)}) collective-permute-start(bf16[224,256]{1,0:T(8,128)(2,1)S(1)} %get-tuple-element.156.refs_0_), channel_id=1, source_target_pairs={{0,6},{2,4},{4,2},{6,0},{1,7},{3,5},{5,3},{7,1},{8,14},{10,12},{12... | collective-permute-start | bytes 344072 | tf_op jit(solution)/shard_map/ppermute | solution.py:48
  43.3 1.1 %shard_map.208 = bf16[384,256]{1,0:T(8,128)(2,1)} custom-call(s32[8,32]{1,0:T(8,128)S(1)} %get-tuple-element.131.send_list, f32[384,256]{1,0:T(8,128)S(1)} %get-tuple-element.136.local_grad, bf16[64,256]{1,0:T(8,128)(2,1)S(1)} %get-tuple-element.137.center, bf16[96,256]{1,0:T(8,128)(2,1)S(1)} %collective-permute-done.11.along_core, ...), custom_call_target="tpu_custom_call" | custom-call | flops 50331648 | bytes 721920 | tf_op jit(solution)/shard_map/pallas_call | solution.py:507
  44.4 0.5 %convert_reduce_fusion = (bf16[256]{0:T(256)(128)(2,1)}, bf16[256]{0:T(256)(128)(2,1)}) fusion(f32[8,256]{1,0:T(8,128)S(1)} %get-tuple-element.141), kind=kLoop, calls=%fused_computation | loop fusion | flops 1024 | bytes 5120 | tf_op jit(solution)/shard_map/convert_element_type | solution.py:762
  44.9 0.0 collective-permute-start.16
  44.9 0.0 collective-permute-done.15.refs_1_
  44.9 0.5 %collective-permute-start.17 = (bf16[224,256]{1,0:T(8,128)(2,1)S(1)}, bf16[224,256]{1,0:T(8,128)(2,1)S(1)}, u32[]{:S(2)}, u32[]{:S(2)}) collective-permute-start(bf16[224,256]{1,0:T(8,128)(2,1)S(1)} %collective-permute-done.15.refs_1_), channel_id=1, source_target_pairs={{0,1},{1,0},{2,3},{3,2},{4,5},{5,4},{6,7},{7,6},{8,9},{9,8},{10,11... | collective-permute-start | bytes 344072 | tf_op jit(solution)/shard_map/ppermute | solution.py:30
  45.4 1.9 %collective-permute-done.14.refs_2_ = bf16[224,256]{1,0:T(8,128)(2,1)S(1)} collective-permute-done((bf16[224,256]{1,0:T(8,128)(2,1)S(1)}, bf16[224,256]{1,0:T(8,128)(2,1)S(1)}, u32[]{:S(2)}, u32[]{:S(2)}) %collective-permute-start.14) | collective-permute-done | bytes 114720 | tf_op jit(solution)/shard_map/ppermute | solution.py:48
  47.4 0.0 collective-permute-start.18
  47.4 1.0 %collective-permute-done.13.refs_3_ = bf16[224,256]{1,0:T(8,128)(2,1)S(1)} collective-permute-done((bf16[224,256]{1,0:T(8,128)(2,1)S(1)}, bf16[224,256]{1,0:T(8,128)(2,1)S(1)}, u32[]{:S(2)}, u32[]{:S(2)}) %collective-permute-start.13) | collective-permute-done | bytes 114720 | tf_op jit(solution)/shard_map/ppermute | solution.py:48
  48.4 0.0 collective-permute-start.19
  48.4 0.0 collective-permute-done.16.refs_4_
  48.4 0.0 collective-permute-done.17.refs_5_
  48.4 0.3 collective-permute-done.18.refs_6_
  48.7 1.0 %collective-permute-done.19.refs_7_ = bf16[224,256]{1,0:T(8,128)(2,1)S(1)} collective-permute-done((bf16[224,256]{1,0:T(8,128)(2,1)S(1)}, bf16[224,256]{1,0:T(8,128)(2,1)S(1)}, u32[]{:S(2)}, u32[]{:S(2)}) %collective-permute-start.19) | collective-permute-done | bytes 114720 | tf_op jit(solution)/shard_map/ppermute | solution.py:30
  49.7 1.0 %shard_map.209 = (bf16[768,256]{1,0:T(8,128)(2,1)}, bf16[256,256]{1,0:T(8,128)(2,1)}, bf16[512,256]{1,0:T(8,128)(2,1)}, bf16[256,256]{1,0:T(8,128)(2,1)}) custom-call(bf16[224,256]{1,0:T(8,128)(2,1)S(1)} %get-tuple-element.156.refs_0_, bf16[224,256]{1,0:T(8,128)(2,1)S(1)} %collective-permute-done.15.refs_1_, ...), custom_call_target="tpu_custom_call" | custom-call | bytes 1835008 | tf_op jit(solution)/shard_map/pallas_call | solution.py:507
  (4 shorter events, 0.1 us)
Async XLA Ops:
  1.8 8.0 %collective-permute-start = (bf16[96,256]{1,0:T(8,128)(2,1)S(1)}, bf16[96,256]{1,0:T(8,128)(2,1)S(1)}, u32[]{:S(2)}, u32[]{:S(2)}) collective-permute-start(bf16[96,256]{1,0:T(8,128)(2,1)S(1)} %get-tuple-element.93), channel_id=1, source_target_pairs={{0,4},{4,0},{8,12},{12,8},{1,5},{5,1},{9,13},{13,9},{2,6},{6,2},{1... | collective-permute-start | bytes 147464 | tf_op jit(solution)/shard_map/ppermute | solution.py:30
  4.9 5.9 %collective-permute-start.1 = (bf16[96,256]{1,0:T(8,128)(2,1)S(1)}, bf16[96,256]{1,0:T(8,128)(2,1)S(1)}, u32[]{:S(2)}, u32[]{:S(2)}) collective-permute-start(bf16[96,256]{1,0:T(8,128)(2,1)S(1)} %get-tuple-element.94), channel_id=1, source_target_pairs={{0,12},{4,8},{8,4},{12,0},{1,13},{5,9},{9,5},{13,1},{2,14},{6,10},... | collective-permute-start | bytes 147464 | tf_op jit(solution)/shard_map/ppermute | solution.py:35
  10.8 3.5 %collective-permute-start.2 = (bf16[96,256]{1,0:T(8,128)(2,1)S(1)}, bf16[96,256]{1,0:T(8,128)(2,1)S(1)}, u32[]{:S(2)}, u32[]{:S(2)}) collective-permute-start(bf16[96,256]{1,0:T(8,128)(2,1)S(1)} %get-tuple-element.106), channel_id=1, source_target_pairs={{0,1},{1,0},{2,3},{3,2},{4,5},{5,4},{6,7},{7,6},{8,9},{9,8},{10,11... | collective-permute-start | bytes 147464 | tf_op jit(solution)/shard_map/ppermute | solution.py:30
  10.9 3.6 %collective-permute-start.3 = (bf16[96,256]{1,0:T(8,128)(2,1)S(1)}, bf16[96,256]{1,0:T(8,128)(2,1)S(1)}, u32[]{:S(2)}, u32[]{:S(2)}) collective-permute-start(bf16[96,256]{1,0:T(8,128)(2,1)S(1)} %get-tuple-element.107), channel_id=1, source_target_pairs={{0,3},{1,2},{2,1},{3,0},{4,7},{5,6},{6,5},{7,4},{8,11},{9,10},{10,... | collective-permute-start | bytes 147464 | tf_op jit(solution)/shard_map/ppermute | solution.py:35
  20.1 2.0 %collective-permute-start.4 = (bf16[904,256]{1,0:T(8,128)(2,1)S(1)}, bf16[904,256]{1,0:T(8,128)(2,1)S(1)}, u32[]{:S(2)}, u32[]{:S(2)}) collective-permute-start(bf16[904,256]{1,0:T(8,128)(2,1)S(1)} %get-tuple-element.115), channel_id=1, source_target_pairs={{0,1},{1,0},{2,3},{3,2},{4,5},{5,4},{6,7},{7,6},{8,9},{9,8},{10,11... | collective-permute-start | bytes 1388552 | tf_op jit(solution)/shard_map/ppermute | solution.py:30
  20.6 7.6 %collective-permute-start.8 = (bf16[96,256]{1,0:T(8,128)(2,1)S(1)}, bf16[96,256]{1,0:T(8,128)(2,1)S(1)}, u32[]{:S(2)}, u32[]{:S(2)}) collective-permute-start(bf16[96,256]{1,0:T(8,128)(2,1)S(1)} %get-tuple-element.119), channel_id=1, source_target_pairs={{0,4},{4,0},{8,12},{12,8},{1,5},{5,1},{9,13},{13,9},{2,6},{6,2},{1... | collective-permute-start | bytes 147464 | tf_op jit(solution)/shard_map/ppermute | solution.py:30
  22.2 7.0 %collective-permute-start.5 = (bf16[232,256]{1,0:T(8,128)(2,1)S(1)}, bf16[232,256]{1,0:T(8,128)(2,1)S(1)}, u32[]{:S(2)}, u32[]{:S(2)}) collective-permute-start(bf16[232,256]{1,0:T(8,128)(2,1)S(1)} %get-tuple-element.116), channel_id=1, source_target_pairs={{0,6},{2,4},{4,2},{6,0},{1,7},{3,5},{5,3},{7,1},{8,14},{10,12},{12... | collective-permute-start | bytes 356360 | tf_op jit(solution)/shard_map/ppermute | solution.py:48
  23.8 7.9 %collective-permute-start.6 = (bf16[232,256]{1,0:T(8,128)(2,1)S(1)}, bf16[232,256]{1,0:T(8,128)(2,1)S(1)}, u32[]{:S(2)}, u32[]{:S(2)}) collective-permute-start(bf16[232,256]{1,0:T(8,128)(2,1)S(1)} %get-tuple-element.117), channel_id=1, source_target_pairs={{0,4},{2,6},{4,0},{6,2},{1,5},{3,7},{5,1},{7,3},{8,12},{10,14},{12... | collective-permute-start | bytes 356360 | tf_op jit(solution)/shard_map/ppermute | solution.py:48
  25.2 6.4 %collective-permute-start.7 = (bf16[232,256]{1,0:T(8,128)(2,1)S(1)}, bf16[232,256]{1,0:T(8,128)(2,1)S(1)}, u32[]{:S(2)}, u32[]{:S(2)}) collective-permute-start(bf16[232,256]{1,0:T(8,128)(2,1)S(1)} %get-tuple-element.118), channel_id=1, source_target_pairs={{0,2},{2,0},{4,6},{6,4},{1,3},{3,1},{5,7},{7,5},{8,10},{10,8},{12,... | collective-permute-start | bytes 356360 | tf_op jit(solution)/shard_map/ppermute | solution.py:48
  25.7 7.3 %collective-permute-start.10 = (bf16[96,256]{1,0:T(8,128)(2,1)S(1)}, bf16[96,256]{1,0:T(8,128)(2,1)S(1)}, u32[]{:S(2)}, u32[]{:S(2)}) collective-permute-start(bf16[96,256]{1,0:T(8,128)(2,1)S(1)} %get-tuple-element.125), channel_id=1, source_target_pairs={{0,12},{4,8},{8,4},{12,0},{1,13},{5,9},{9,5},{13,1},{2,14},{6,10},... | collective-permute-start | bytes 147464 | tf_op jit(solution)/shard_map/ppermute | solution.py:35
  31.7 8.0 %collective-permute-start.9 = (bf16[232,256]{1,0:T(8,128)(2,1)S(1)}, bf16[232,256]{1,0:T(8,128)(2,1)S(1)}, u32[]{:S(2)}, u32[]{:S(2)}) collective-permute-start(bf16[232,256]{1,0:T(8,128)(2,1)S(1)} %shard_map.204.refs_3_.own), channel_id=1, source_target_pairs={{0,8},{8,0},{1,9},{9,1},{2,10},{10,2},{3,11},{11,3},{4,12},{12,4},... | collective-permute-start | bytes 356360 | tf_op jit(solution)/shard_map/ppermute | solution.py:548
  33.0 2.4 %collective-permute-start.11 = (bf16[96,256]{1,0:T(8,128)(2,1)S(1)}, bf16[96,256]{1,0:T(8,128)(2,1)S(1)}, u32[]{:S(2)}, u32[]{:S(2)}) collective-permute-start(bf16[96,256]{1,0:T(8,128)(2,1)S(1)} %get-tuple-element.127), channel_id=1, source_target_pairs={{0,1},{1,0},{2,3},{3,2},{4,5},{5,4},{6,7},{7,6},{8,9},{9,8},{10,11... | collective-permute-start | bytes 147464 | tf_op jit(solution)/shard_map/ppermute | solution.py:30
  33.1 3.6 %collective-permute-start.12 = (bf16[96,256]{1,0:T(8,128)(2,1)S(1)}, bf16[96,256]{1,0:T(8,128)(2,1)S(1)}, u32[]{:S(2)}, u32[]{:S(2)}) collective-permute-start(bf16[96,256]{1,0:T(8,128)(2,1)S(1)} %get-tuple-element.128), channel_id=1, source_target_pairs={{0,3},{1,2},{2,1},{3,0},{4,7},{5,6},{6,5},{7,4},{8,11},{9,10},{10,... | collective-permute-start | bytes 147464 | tf_op jit(solution)/shard_map/ppermute | solution.py:35
  39.7 5.2 %collective-permute-start.15 = (bf16[224,256]{1,0:T(8,128)(2,1)S(1)}, bf16[224,256]{1,0:T(8,128)(2,1)S(1)}, u32[]{:S(2)}, u32[]{:S(2)}) collective-permute-start(bf16[224,256]{1,0:T(8,128)(2,1)S(1)} %get-tuple-element.156.refs_0_), channel_id=1, source_target_pairs={{0,2},{2,0},{4,6},{6,4},{1,3},{3,1},{5,7},{7,5},{8,10},{10,8},{12,... | collective-permute-start | bytes 344072 | tf_op jit(solution)/shard_map/ppermute | solution.py:48
  41.4 6.0 %collective-permute-start.14 = (bf16[224,256]{1,0:T(8,128)(2,1)S(1)}, bf16[224,256]{1,0:T(8,128)(2,1)S(1)}, u32[]{:S(2)}, u32[]{:S(2)}) collective-permute-start(bf16[224,256]{1,0:T(8,128)(2,1)S(1)} %get-tuple-element.156.refs_0_), channel_id=1, source_target_pairs={{0,4},{2,6},{4,0},{6,2},{1,5},{3,7},{5,1},{7,3},{8,12},{10,14},{12... | collective-permute-start | bytes 344072 | tf_op jit(solution)/shard_map/ppermute | solution.py:48
  41.4 7.0 %collective-permute-start.13 = (bf16[224,256]{1,0:T(8,128)(2,1)S(1)}, bf16[224,256]{1,0:T(8,128)(2,1)S(1)}, u32[]{:S(2)}, u32[]{:S(2)}) collective-permute-start(bf16[224,256]{1,0:T(8,128)(2,1)S(1)} %get-tuple-element.156.refs_0_), channel_id=1, source_target_pairs={{0,6},{2,4},{4,2},{6,0},{1,7},{3,5},{5,3},{7,1},{8,14},{10,12},{12... | collective-permute-start | bytes 344072 | tf_op jit(solution)/shard_map/ppermute | solution.py:48
  44.9 3.5 %collective-permute-start.16 = (bf16[224,256]{1,0:T(8,128)(2,1)S(1)}, bf16[224,256]{1,0:T(8,128)(2,1)S(1)}, u32[]{:S(2)}, u32[]{:S(2)}) collective-permute-start(bf16[224,256]{1,0:T(8,128)(2,1)S(1)} %get-tuple-element.156.refs_0_), channel_id=1, source_target_pairs={{0,1},{1,0},{2,3},{3,2},{4,5},{5,4},{6,7},{7,6},{8,9},{9,8},{10,11... | collective-permute-start | bytes 344072 | tf_op jit(solution)/shard_map/ppermute | solution.py:30
  44.9 3.5 %collective-permute-start.17 = (bf16[224,256]{1,0:T(8,128)(2,1)S(1)}, bf16[224,256]{1,0:T(8,128)(2,1)S(1)}, u32[]{:S(2)}, u32[]{:S(2)}) collective-permute-start(bf16[224,256]{1,0:T(8,128)(2,1)S(1)} %collective-permute-done.15.refs_1_), channel_id=1, source_target_pairs={{0,1},{1,0},{2,3},{3,2},{4,5},{5,4},{6,7},{7,6},{8,9},{9,8},{10,11... | collective-permute-start | bytes 344072 | tf_op jit(solution)/shard_map/ppermute | solution.py:30
  47.4 1.3 %collective-permute-start.18 = (bf16[224,256]{1,0:T(8,128)(2,1)S(1)}, bf16[224,256]{1,0:T(8,128)(2,1)S(1)}, u32[]{:S(2)}, u32[]{:S(2)}) collective-permute-start(bf16[224,256]{1,0:T(8,128)(2,1)S(1)} %collective-permute-done.14.refs_2_), channel_id=1, source_target_pairs={{0,1},{1,0},{2,3},{3,2},{4,5},{5,4},{6,7},{7,6},{8,9},{9,8},{10,11... | collective-permute-start | bytes 344072 | tf_op jit(solution)/shard_map/ppermute | solution.py:30
  48.4 1.3 %collective-permute-start.19 = (bf16[224,256]{1,0:T(8,128)(2,1)S(1)}, bf16[224,256]{1,0:T(8,128)(2,1)S(1)}, u32[]{:S(2)}, u32[]{:S(2)}) collective-permute-start(bf16[224,256]{1,0:T(8,128)(2,1)S(1)} %collective-permute-done.13.refs_3_), channel_id=1, source_target_pairs={{0,1},{1,0},{2,3},{3,2},{4,5},{5,4},{6,7},{7,6},{8,9},{9,8},{10,11... | collective-permute-start | bytes 344072 | tf_op jit(solution)/shard_map/ppermute | solution.py:30

commit v20 on v19

--- a/solution.py
+++ b/solution.py
@@ -361,7 +361,7 @@
     gains_out[...] = gains
 
 
-def pair_kernel(parts, keep, gains, other, *outs):
+def pair_kernel(parts, keep, gains, other, inner, *outs):
     rows = keep.shape[0]
     packed = gains.shape[0]
     members = len(outs)
@@ -370,8 +370,12 @@
     me = place_in_square()
     for offset, out in enumerate(reversed(outs)):
         owner = me ^ offset
-        out[:packed] = summed
-        first, at = 0, packed
+        at = 0
+        if offset == lax.axis_size(SQUARE[1]):
+            at = inner.shape[0]
+            out[:at] = inner[...]
+        out[at : at + packed] = summed
+        first, at = 0, at + packed
         for part in parts:
             step = part // members
             source = pl.ds(pl.multiple_of(first + owner * step, 16), step)
@@ -385,13 +389,10 @@
     return pack_gains(gains[0:1] + gains[1:2], gains[2:3] + gains[3:4])
 
 
-def copy_kernel(source, target):
-    target[...] = source[...]
-
-
 def sum_kernel(*refs):
     sums_out = refs[-1]
-    sums = tree_sum([block[...].astype(F32) for block in refs[:-1]])
+    rows = sums_out.shape[0]
+    sums = tree_sum([block[block.shape[0] - rows :].astype(F32) for block in refs[:-1]])
     sums_out[...] = sums.astype(BF16)
     sums_out[:PACKED] = add_packed(sums)
 
@@ -454,7 +455,7 @@
 
 def turn_kernel(inner, outer, middle, along_core, along_chip, center):
     slots = middle.shape[0] // 2
-    top, bottom = from_pair(NEAR, inner[...], outer[...])
+    top, bottom = from_pair(NEAR, inner[: outer.shape[0]], outer[...])
     up = jnp.concatenate([top[:slots], middle[:slots], bottom[:slots]], axis=0)
     down = jnp.concatenate([top[2 * slots :], middle[slots:], bottom[2 * slots :]], axis=0)
     by_pair(CORE, up, down, along_core, along_chip)
@@ -717,18 +718,23 @@
     )
     other = across_cores(away)
     members = square_members()
+    block_rows = PACKED + halves // members
+    paired = lax.axis_size(SQUARE[1])
     *blocks, own = call(
         functools.partial(pair_kernel, parts),
-        [shaped(PACKED + halves // members, width, BF16)] * members,
+        [
+            shaped(block_rows + (3 * slots if offset == paired else 0), width, BF16)
+            for offset in reversed(range(members))
+        ],
         0,
         keep,
         gains,
         other,
+        inner,
     )
     received = [in_square(block, members - 1 - i) for i, block in enumerate(blocks)]
+    inner = received[members - 1 - paired]
     outer = out_of_pair(outer, PX)
-    (inner,) = call(copy_kernel, [like(inner)], 10**9, in_pair(inner, PX))
-    *received, inner = lax.optimization_barrier((*received, inner))
     (sums,) = call(sum_kernel, [like(own)], 0, *received, own)
     edges_grad, local_grad = call(
         finish_kernel,

time: 51 us -> 51.4 us (level)
  waiting for transfers between devices: 14.6 us -> 15.6 us
  starting transfers between devices: 20.2 us -> 19.6 us
    ppermute x6, waiting for transfers between devices: 6.38 us -> 7.44 us  [in_square(): lax.ppermute(array, SQUARE, [(i, i ^ offset) for i in range(square_member...]
    ppermute x9 -> x8, starting transfers between devices: 4.27 us -> 3.85 us  [in_pair(): lax.ppermute(array, axis, [(i, i ^ 1) for i in range(lax.axis_size(axis))])]
    pallas_call x13 -> x12, Pallas kernels: 14 us -> 14.1 us  [call(): pl.pallas_call(body, out_shape=outs, in_specs=[pl.BlockSpec(memory_space=...]
    ppermute x9 -> x8, waiting for transfers between devices: 2.77 us -> 2.77 us  [in_pair(): lax.ppermute(array, axis, [(i, i ^ 1) for i in range(lax.axis_size(axis))])]
  transfers between devices with their start and end apart: 20 -> 19, of which waited for: 11 -> 11; matrix products, arithmetic and copies ran while one was open for 1% -> 1% of each run, Pallas kernels for 12% -> 12%
where the time goes in v20:
time: 51.4 us; the launch traced here: 51.2 us
  starting transfers between devices  19.6 us (38%)
  waiting for transfers between devices  15.6 us (30%)
  Pallas kernels  14.1 us (27%)
  between operations  1.4 us (3%)
  other arithmetic  0.53 us (1%)
    pallas_call x12, Pallas kernels, call(): pl.pallas_call(body, out_shape=outs, in_specs=[pl.BlockSpec(memory_space=...  14.1 us
    ppermute x6, waiting for transfers between devices, in_square(): lax.ppermute(array, SQUARE, [(i, i ^ offset) for i in range(square_member...  7.44 us
    ppermute x4, starting transfers between devices, out_of_pair(): lax.ppermute(array, axis, [(i, other_neighbour(i, size)) for i in range(s...  7.2 us
    ppermute x6, starting transfers between devices, in_square(): lax.ppermute(array, SQUARE, [(i, i ^ offset) for i in range(square_member...  7.11 us
    ppermute x8, starting transfers between devices, in_pair(): lax.ppermute(array, axis, [(i, i ^ 1) for i in range(lax.axis_size(axis))])  3.85 us
    ppermute x8, waiting for transfers between devices, in_pair(): lax.ppermute(array, axis, [(i, i ^ 1) for i in range(lax.axis_size(axis))])  2.77 us
    ppermute x4, waiting for transfers between devices, out_of_pair(): lax.ppermute(array, axis, [(i, other_neighbour(i, size)) for i in range(s...  2.73 us
    ppermute x1, waiting for transfers between devices, joined(): other = lax.ppermute(sums, FAR, [(i, i ^ distance) for i in range(size)])  2.69 us
  transfers between devices with their start and end apart: 19, of which 11 were waited for; matrix products, arithmetic and copies ran while one was open for 1% of the time, Pallas kernels for 12%

profile of v20, /device:TPU:0, one launch (start us, length us, event | category | flops | bytes accessed | tf_op | source)
XLA Modules:
  0.0 51.2 jit_solution(16391493484010262113)
XLA Ops:
  0.6 1.2 %shard_map.197 = (bf16[96,256]{1,0:T(8,128)(2,1)S(1)}, bf16[96,256]{1,0:T(8,128)(2,1)S(1)}, bf16[64,256]{1,0:T(8,128)(2,1)S(1)}, bf16[384,256]{1,0:T(8,128)(2,1)S(1)}, s32[8,32]{1,0:T(8,128)S(1)}) custom-call(bf16[384,256]{1,0:T(8,128)(2,1)} %nodes_hbm.1, s32[8,32]{1,0:T(8,128)} %list_hbm.1), custom_call_target="tpu_custom_call" | custom-call | flops 50331648 | bytes 526336 | tf_op jit(solution)/shard_map/pallas_call | solution.py:508
  1.8 3.1 %collective-permute-start = (bf16[96,256]{1,0:T(8,128)(2,1)S(1)}, bf16[96,256]{1,0:T(8,128)(2,1)S(1)}, u32[]{:S(2)}, u32[]{:S(2)}) collective-permute-start(bf16[96,256]{1,0:T(8,128)(2,1)S(1)} %get-tuple-element.89), channel_id=1, source_target_pairs={{0,4},{4,0},{8,12},{12,8},{1,5},{5,1},{9,13},{13,9},{2,6},{6,2},{1... | collective-permute-start | bytes 147464 | tf_op jit(solution)/shard_map/ppermute | solution.py:30
  4.9 2.5 %collective-permute-start.1 = (bf16[96,256]{1,0:T(8,128)(2,1)S(1)}, bf16[96,256]{1,0:T(8,128)(2,1)S(1)}, u32[]{:S(2)}, u32[]{:S(2)}) collective-permute-start(bf16[96,256]{1,0:T(8,128)(2,1)S(1)} %get-tuple-element.90), channel_id=1, source_target_pairs={{0,12},{4,8},{8,4},{12,0},{1,13},{5,9},{9,5},{13,1},{2,14},{6,10},... | collective-permute-start | bytes 147464 | tf_op jit(solution)/shard_map/ppermute | solution.py:35
  8.0 1.7 %shard_map.198 = (bf16[1152,768]{1,0:T(8,128)(2,1)S(1)}, bf16[1152,256]{1,0:T(8,128)(2,1)S(1)}, s32[9,128]{1,0:T(8,128)S(1)}, s32[9,128]{1,0:T(8,128)S(1)}, bf16...) custom-call(s32[9,128]{1,0:T(8,128)} %refs_0_.1, ...), custom_call_target="tpu_custom_call" | custom-call | bytes 6967296 | tf_op jit(solution)/shard_map/pallas_call | solution.py:508
  9.8 0.0 collective-permute-done.inner
  9.8 1.0 %collective-permute-done.1.outer = bf16[96,256]{1,0:T(8,128)(2,1)S(1)} collective-permute-done((bf16[96,256]{1,0:T(8,128)(2,1)S(1)}, bf16[96,256]{1,0:T(8,128)(2,1)S(1)}, u32[]{:S(2)}, u32[]{:S(2)}) %collective-permute-start.1) | collective-permute-done | bytes 49184 | tf_op jit(solution)/shard_map/ppermute | solution.py:35
  10.8 0.1 collective-permute-start.2
  10.9 1.6 %collective-permute-start.3 = (bf16[96,256]{1,0:T(8,128)(2,1)S(1)}, bf16[96,256]{1,0:T(8,128)(2,1)S(1)}, u32[]{:S(2)}, u32[]{:S(2)}) collective-permute-start(bf16[96,256]{1,0:T(8,128)(2,1)S(1)} %get-tuple-element.103), channel_id=1, source_target_pairs={{0,3},{1,2},{2,1},{3,0},{4,7},{5,6},{6,5},{7,4},{8,11},{9,10},{10,... | collective-permute-start | bytes 147464 | tf_op jit(solution)/shard_map/ppermute | solution.py:35
  12.5 1.8 %shard_map.199 = (f32[1152,256]{1,0:T(8,128)S(1)}, bf16[640,1152]{1,0:T(8,128)(2,1)S(1)}, bf16[384,1152]{1,0:T(8,128)(2,1)S(1)}) custom-call(bf16[384,256]{1,0:T(8,128)(2,1)S(1)} %get-tuple-element.83.nodes, bf16[1152,256]{1,0:T(8,128)(2,1)S(1)} %get-tuple-element.85.edges, s32[9,128]{1,0:T(8,128)S(1)} %get-tuple-element.87.senders, ...), custom_call_target="tpu_custom_call" | custom-call | flops 704643072 | bytes 6497280 | tf_op jit(solution)/shard_map/pallas_call | solution.py:508
  14.4 0.0 collective-permute-done.2.along_core
  14.4 0.1 collective-permute-done.3.along_chip
  14.5 5.6 %shard_map.201 = (bf16[1152,256]{1,0:T(8,128)(2,1)S(1)}, bf16[384,256]{1,0:T(8,128)(2,1)S(1)}, bf16[384,256]{1,0:T(8,128)(2,1)S(1)}, f32[384,256]{1,0:T(8,128)S(...) custom-call(s32[1]{0:T(128)S(6)} %copy.22.count_ref, ...), custom_call_target="tpu_custom_call" | custom-call | flops 2583691264 | bytes 11412484 | tf_op jit(solution)/shard_map/pallas_call | solution.py:508
  20.1 0.5 %collective-permute-start.4 = (bf16[904,256]{1,0:T(8,128)(2,1)S(1)}, bf16[904,256]{1,0:T(8,128)(2,1)S(1)}, u32[]{:S(2)}, u32[]{:S(2)}) collective-permute-start(bf16[904,256]{1,0:T(8,128)(2,1)S(1)} %get-tuple-element.111), channel_id=1, source_target_pairs={{0,1},{1,0},{2,3},{3,2},{4,5},{5,4},{6,7},{7,6},{8,9},{9,8},{10,11... | collective-permute-start | bytes 1388552 | tf_op jit(solution)/shard_map/ppermute | solution.py:30
  20.6 1.4 %collective-permute-done.4.other = bf16[904,256]{1,0:T(8,128)(2,1)S(1)} collective-permute-done((bf16[904,256]{1,0:T(8,128)(2,1)S(1)}, bf16[904,256]{1,0:T(8,128)(2,1)S(1)}, u32[]{:S(2)}, u32[]{:S(2)}) %collective-permute-start.4) | collective-permute-done | bytes 462880 | tf_op jit(solution)/shard_map/ppermute | solution.py:30
  22.1 0.1 shard_map.202
  22.2 0.1 collective-permute-start.6
  22.3 3.0 %collective-permute-start.5 = (bf16[232,256]{1,0:T(8,128)(2,1)S(1)}, bf16[232,256]{1,0:T(8,128)(2,1)S(1)}, u32[]{:S(2)}, u32[]{:S(2)}) collective-permute-start(bf16[232,256]{1,0:T(8,128)(2,1)S(1)} %get-tuple-element.113), channel_id=1, source_target_pairs={{0,6},{2,4},{4,2},{6,0},{1,7},{3,5},{5,3},{7,1},{8,14},{10,12},{12... | collective-permute-start | bytes 356360 | tf_op jit(solution)/shard_map/ppermute | solution.py:48
  25.2 0.5 %collective-permute-start.7 = (bf16[232,256]{1,0:T(8,128)(2,1)S(1)}, bf16[232,256]{1,0:T(8,128)(2,1)S(1)}, u32[]{:S(2)}, u32[]{:S(2)}) collective-permute-start(bf16[232,256]{1,0:T(8,128)(2,1)S(1)} %get-tuple-element.115), channel_id=1, source_target_pairs={{0,2},{2,0},{4,6},{6,4},{1,3},{3,1},{5,7},{7,5},{8,10},{10,8},{12,... | collective-permute-start | bytes 356360 | tf_op jit(solution)/shard_map/ppermute | solution.py:48
  25.7 2.5 %collective-permute-start.9 = (bf16[96,256]{1,0:T(8,128)(2,1)S(1)}, bf16[96,256]{1,0:T(8,128)(2,1)S(1)}, u32[]{:S(2)}, u32[]{:S(2)}) collective-permute-start(bf16[96,256]{1,0:T(8,128)(2,1)S(1)} %get-tuple-element.117), channel_id=1, source_target_pairs={{0,12},{4,8},{8,4},{12,0},{1,13},{5,9},{9,5},{13,1},{2,14},{6,10},... | collective-permute-start | bytes 147464 | tf_op jit(solution)/shard_map/ppermute | solution.py:35
  28.2 4.2 %collective-permute-done.5.refs_0_ = bf16[232,256]{1,0:T(8,128)(2,1)S(1)} collective-permute-done((bf16[232,256]{1,0:T(8,128)(2,1)S(1)}, bf16[232,256]{1,0:T(8,128)(2,1)S(1)}, u32[]{:S(2)}, u32[]{:S(2)}) %collective-permute-start.5) | collective-permute-done | bytes 118816 | tf_op jit(solution)/shard_map/ppermute | solution.py:48
  32.4 0.3 collective-permute-done.7.refs_2_
  32.7 0.0 collective-permute-done.6.refs_1_.refs_0_
  32.7 0.1 shard_map.203.refs_3_.own
  32.8 1.4 %collective-permute-start.8 = (bf16[232,256]{1,0:T(8,128)(2,1)S(1)}, bf16[232,256]{1,0:T(8,128)(2,1)S(1)}, u32[]{:S(2)}, u32[]{:S(2)}) collective-permute-start(bf16[232,256]{1,0:T(8,128)(2,1)S(1)} %shard_map.203.refs_3_.own), channel_id=1, source_target_pairs={{0,8},{8,0},{1,9},{9,1},{2,10},{10,2},{3,11},{11,3},{4,12},{12,4},... | collective-permute-start | bytes 356360 | tf_op jit(solution)/shard_map/ppermute | solution.py:549
  34.2 0.0 collective-permute-done.9.refs_1_
  34.2 0.1 collective-permute-start.10
  34.3 0.6 %collective-permute-start.11 = (bf16[96,256]{1,0:T(8,128)(2,1)S(1)}, bf16[96,256]{1,0:T(8,128)(2,1)S(1)}, u32[]{:S(2)}, u32[]{:S(2)}) collective-permute-start(bf16[96,256]{1,0:T(8,128)(2,1)S(1)} %get-tuple-element.120), channel_id=1, source_target_pairs={{0,3},{1,2},{2,1},{3,0},{4,7},{5,6},{6,5},{7,4},{8,11},{9,10},{10,... | collective-permute-start | bytes 147464 | tf_op jit(solution)/shard_map/ppermute | solution.py:35
  35.0 1.3 %shard_map.206 = (bf16[1152,256]{1,0:T(8,128)(2,1)}, f32[384,256]{1,0:T(8,128)S(1)}) custom-call(bf16[1152,256]{1,0:T(8,128)(2,1)S(1)} %get-tuple-element.86.edge_grads, bf16[1152,256]{1,0:T(8,128)(2,1)S(1)} %get-tuple-element.124.pre_grad, bf16[384,256]{1,0:T(8,128)(2,1)S(1)} %get-tuple-element.125.sender_sum, ...), custom_call_target="tpu_custom_call" | custom-call | flops 251658240 | bytes 3342336 | tf_op jit(solution)/shard_map/pallas_call | solution.py:508
  36.3 0.0 collective-permute-done.10.along_core
  36.3 1.6 %collective-permute-done.11.along_chip = bf16[96,256]{1,0:T(8,128)(2,1)S(1)} collective-permute-done((bf16[96,256]{1,0:T(8,128)(2,1)S(1)}, bf16[96,256]{1,0:T(8,128)(2,1)S(1)}, u32[]{:S(2)}, u32[]{:S(2)}) %collective-permute-start.11) | collective-permute-done | bytes 49184 | tf_op jit(solution)/shard_map/ppermute | solution.py:35
  37.9 2.7 %collective-permute-done.8.other = bf16[232,256]{1,0:T(8,128)(2,1)S(1)} collective-permute-done((bf16[232,256]{1,0:T(8,128)(2,1)S(1)}, bf16[232,256]{1,0:T(8,128)(2,1)S(1)}, u32[]{:S(2)}, u32[]{:S(2)}) %collective-permute-start.8) | collective-permute-done | bytes 118816 | tf_op jit(solution)/shard_map/ppermute | solution.py:549
  40.6 0.6 %collective-permute-start.14 = (bf16[224,256]{1,0:T(8,128)(2,1)S(1)}, bf16[224,256]{1,0:T(8,128)(2,1)S(1)}, u32[]{:S(2)}, u32[]{:S(2)}) collective-permute-start(bf16[224,256]{1,0:T(8,128)(2,1)S(1)} %get-tuple-element.148.refs_0_), channel_id=1, source_target_pairs={{0,2},{2,0},{4,6},{6,4},{1,3},{3,1},{5,7},{7,5},{8,10},{10,8},{12,... | collective-permute-start | bytes 344072 | tf_op jit(solution)/shard_map/ppermute | solution.py:48
  41.2 0.0 collective-permute-start.13
  41.2 3.0 %collective-permute-start.12 = (bf16[224,256]{1,0:T(8,128)(2,1)S(1)}, bf16[224,256]{1,0:T(8,128)(2,1)S(1)}, u32[]{:S(2)}, u32[]{:S(2)}) collective-permute-start(bf16[224,256]{1,0:T(8,128)(2,1)S(1)} %get-tuple-element.148.refs_0_), channel_id=1, source_target_pairs={{0,6},{2,4},{4,2},{6,0},{1,7},{3,5},{5,3},{7,1},{8,14},{10,12},{12... | collective-permute-start | bytes 344072 | tf_op jit(solution)/shard_map/ppermute | solution.py:48
  44.2 1.1 %shard_map.207 = bf16[384,256]{1,0:T(8,128)(2,1)} custom-call(s32[8,32]{1,0:T(8,128)S(1)} %get-tuple-element.123.send_list, f32[384,256]{1,0:T(8,128)S(1)} %get-tuple-element.128.local_grad, bf16[64,256]{1,0:T(8,128)(2,1)S(1)} %get-tuple-element.129.center, bf16[96,256]{1,0:T(8,128)(2,1)S(1)} %collective-permute-done.10.along_core, ...), custom_call_target="tpu_custom_call" | custom-call | flops 50331648 | bytes 721920 | tf_op jit(solution)/shard_map/pallas_call | solution.py:508
  45.3 0.5 %convert_reduce_fusion = (bf16[256]{0:T(256)(128)(2,1)}, bf16[256]{0:T(256)(128)(2,1)}) fusion(f32[8,256]{1,0:T(8,128)S(1)} %get-tuple-element.133), kind=kLoop, calls=%fused_computation | loop fusion | flops 1024 | bytes 5120 | tf_op jit(solution)/shard_map/convert_element_type | solution.py:768
  45.8 0.0 collective-permute-start.15
  45.8 0.5 collective-permute-done.14.refs_1_
  46.3 0.0 collective-permute-start.16
  46.4 0.4 collective-permute-done.13.refs_2_
  46.8 0.1 collective-permute-start.17
  46.8 2.1 %collective-permute-done.12.refs_3_ = bf16[224,256]{1,0:T(8,128)(2,1)S(1)} collective-permute-done((bf16[224,256]{1,0:T(8,128)(2,1)S(1)}, bf16[224,256]{1,0:T(8,128)(2,1)S(1)}, u32[]{:S(2)}, u32[]{:S(2)}) %collective-permute-start.12) | collective-permute-done | bytes 114720 | tf_op jit(solution)/shard_map/ppermute | solution.py:48
  48.9 0.0 collective-permute-start.18
  48.9 0.0 collective-permute-done.15.refs_4_
  48.9 0.0 collective-permute-done.16.refs_5_
  48.9 0.0 collective-permute-done.17.refs_6_
  48.9 1.3 %collective-permute-done.18.refs_7_ = bf16[224,256]{1,0:T(8,128)(2,1)S(1)} collective-permute-done((bf16[224,256]{1,0:T(8,128)(2,1)S(1)}, bf16[224,256]{1,0:T(8,128)(2,1)S(1)}, u32[]{:S(2)}, u32[]{:S(2)}) %collective-permute-start.18) | collective-permute-done | bytes 114720 | tf_op jit(solution)/shard_map/ppermute | solution.py:30
  50.2 1.0 %shard_map.208 = (bf16[768,256]{1,0:T(8,128)(2,1)}, bf16[256,256]{1,0:T(8,128)(2,1)}, bf16[512,256]{1,0:T(8,128)(2,1)}, bf16[256,256]{1,0:T(8,128)(2,1)}) custom-call(bf16[224,256]{1,0:T(8,128)(2,1)S(1)} %get-tuple-element.148.refs_0_, bf16[224,256]{1,0:T(8,128)(2,1)S(1)} %collective-permute-done.14.refs_1_, ...), custom_call_target="tpu_custom_call" | custom-call | bytes 1835008 | tf_op jit(solution)/shard_map/pallas_call | solution.py:508
  (3 shorter events, 0.1 us)
Async XLA Ops:
  1.8 8.0 %collective-permute-start = (bf16[96,256]{1,0:T(8,128)(2,1)S(1)}, bf16[96,256]{1,0:T(8,128)(2,1)S(1)}, u32[]{:S(2)}, u32[]{:S(2)}) collective-permute-start(bf16[96,256]{1,0:T(8,128)(2,1)S(1)} %get-tuple-element.89), channel_id=1, source_target_pairs={{0,4},{4,0},{8,12},{12,8},{1,5},{5,1},{9,13},{13,9},{2,6},{6,2},{1... | collective-permute-start | bytes 147464 | tf_op jit(solution)/shard_map/ppermute | solution.py:30
  4.9 5.9 %collective-permute-start.1 = (bf16[96,256]{1,0:T(8,128)(2,1)S(1)}, bf16[96,256]{1,0:T(8,128)(2,1)S(1)}, u32[]{:S(2)}, u32[]{:S(2)}) collective-permute-start(bf16[96,256]{1,0:T(8,128)(2,1)S(1)} %get-tuple-element.90), channel_id=1, source_target_pairs={{0,12},{4,8},{8,4},{12,0},{1,13},{5,9},{9,5},{13,1},{2,14},{6,10},... | collective-permute-start | bytes 147464 | tf_op jit(solution)/shard_map/ppermute | solution.py:35
  10.8 3.5 %collective-permute-start.2 = (bf16[96,256]{1,0:T(8,128)(2,1)S(1)}, bf16[96,256]{1,0:T(8,128)(2,1)S(1)}, u32[]{:S(2)}, u32[]{:S(2)}) collective-permute-start(bf16[96,256]{1,0:T(8,128)(2,1)S(1)} %get-tuple-element.102), channel_id=1, source_target_pairs={{0,1},{1,0},{2,3},{3,2},{4,5},{5,4},{6,7},{7,6},{8,9},{9,8},{10,11... | collective-permute-start | bytes 147464 | tf_op jit(solution)/shard_map/ppermute | solution.py:30
  10.9 3.6 %collective-permute-start.3 = (bf16[96,256]{1,0:T(8,128)(2,1)S(1)}, bf16[96,256]{1,0:T(8,128)(2,1)S(1)}, u32[]{:S(2)}, u32[]{:S(2)}) collective-permute-start(bf16[96,256]{1,0:T(8,128)(2,1)S(1)} %get-tuple-element.103), channel_id=1, source_target_pairs={{0,3},{1,2},{2,1},{3,0},{4,7},{5,6},{6,5},{7,4},{8,11},{9,10},{10,... | collective-permute-start | bytes 147464 | tf_op jit(solution)/shard_map/ppermute | solution.py:35
  20.1 2.0 %collective-permute-start.4 = (bf16[904,256]{1,0:T(8,128)(2,1)S(1)}, bf16[904,256]{1,0:T(8,128)(2,1)S(1)}, u32[]{:S(2)}, u32[]{:S(2)}) collective-permute-start(bf16[904,256]{1,0:T(8,128)(2,1)S(1)} %get-tuple-element.111), channel_id=1, source_target_pairs={{0,1},{1,0},{2,3},{3,2},{4,5},{5,4},{6,7},{7,6},{8,9},{9,8},{10,11... | collective-permute-start | bytes 1388552 | tf_op jit(solution)/shard_map/ppermute | solution.py:30
  22.2 10.5 %collective-permute-start.6 = (bf16[328,256]{1,0:T(8,128)(2,1)S(1)}, bf16[328,256]{1,0:T(8,128)(2,1)S(1)}, u32[]{:S(2)}, u32[]{:S(2)}) collective-permute-start(bf16[328,256]{1,0:T(8,128)(2,1)S(1)} %get-tuple-element.114), channel_id=1, source_target_pairs={{0,4},{2,6},{4,0},{6,2},{1,5},{3,7},{5,1},{7,3},{8,12},{10,14},{12... | collective-permute-start | bytes 503816 | tf_op jit(solution)/shard_map/ppermute | solution.py:48
  22.3 10.1 %collective-permute-start.5 = (bf16[232,256]{1,0:T(8,128)(2,1)S(1)}, bf16[232,256]{1,0:T(8,128)(2,1)S(1)}, u32[]{:S(2)}, u32[]{:S(2)}) collective-permute-start(bf16[232,256]{1,0:T(8,128)(2,1)S(1)} %get-tuple-element.113), channel_id=1, source_target_pairs={{0,6},{2,4},{4,2},{6,0},{1,7},{3,5},{5,3},{7,1},{8,14},{10,12},{12... | collective-permute-start | bytes 356360 | tf_op jit(solution)/shard_map/ppermute | solution.py:48
  25.2 7.5 %collective-permute-start.7 = (bf16[232,256]{1,0:T(8,128)(2,1)S(1)}, bf16[232,256]{1,0:T(8,128)(2,1)S(1)}, u32[]{:S(2)}, u32[]{:S(2)}) collective-permute-start(bf16[232,256]{1,0:T(8,128)(2,1)S(1)} %get-tuple-element.115), channel_id=1, source_target_pairs={{0,2},{2,0},{4,6},{6,4},{1,3},{3,1},{5,7},{7,5},{8,10},{10,8},{12,... | collective-permute-start | bytes 356360 | tf_op jit(solution)/shard_map/ppermute | solution.py:48
  25.7 8.5 %collective-permute-start.9 = (bf16[96,256]{1,0:T(8,128)(2,1)S(1)}, bf16[96,256]{1,0:T(8,128)(2,1)S(1)}, u32[]{:S(2)}, u32[]{:S(2)}) collective-permute-start(bf16[96,256]{1,0:T(8,128)(2,1)S(1)} %get-tuple-element.117), channel_id=1, source_target_pairs={{0,12},{4,8},{8,4},{12,0},{1,13},{5,9},{9,5},{13,1},{2,14},{6,10},... | collective-permute-start | bytes 147464 | tf_op jit(solution)/shard_map/ppermute | solution.py:35
  32.8 7.8 %collective-permute-start.8 = (bf16[232,256]{1,0:T(8,128)(2,1)S(1)}, bf16[232,256]{1,0:T(8,128)(2,1)S(1)}, u32[]{:S(2)}, u32[]{:S(2)}) collective-permute-start(bf16[232,256]{1,0:T(8,128)(2,1)S(1)} %shard_map.203.refs_3_.own), channel_id=1, source_target_pairs={{0,8},{8,0},{1,9},{9,1},{2,10},{10,2},{3,11},{11,3},{4,12},{12,4},... | collective-permute-start | bytes 356360 | tf_op jit(solution)/shard_map/ppermute | solution.py:549
  34.2 2.1 %collective-permute-start.10 = (bf16[96,256]{1,0:T(8,128)(2,1)S(1)}, bf16[96,256]{1,0:T(8,128)(2,1)S(1)}, u32[]{:S(2)}, u32[]{:S(2)}) collective-permute-start(bf16[96,256]{1,0:T(8,128)(2,1)S(1)} %get-tuple-element.119), channel_id=1, source_target_pairs={{0,1},{1,0},{2,3},{3,2},{4,5},{5,4},{6,7},{7,6},{8,9},{9,8},{10,11... | collective-permute-start | bytes 147464 | tf_op jit(solution)/shard_map/ppermute | solution.py:30
  34.3 3.6 %collective-permute-start.11 = (bf16[96,256]{1,0:T(8,128)(2,1)S(1)}, bf16[96,256]{1,0:T(8,128)(2,1)S(1)}, u32[]{:S(2)}, u32[]{:S(2)}) collective-permute-start(bf16[96,256]{1,0:T(8,128)(2,1)S(1)} %get-tuple-element.120), channel_id=1, source_target_pairs={{0,3},{1,2},{2,1},{3,0},{4,7},{5,6},{6,5},{7,4},{8,11},{9,10},{10,... | collective-permute-start | bytes 147464 | tf_op jit(solution)/shard_map/ppermute | solution.py:35
  40.6 5.7 %collective-permute-start.14 = (bf16[224,256]{1,0:T(8,128)(2,1)S(1)}, bf16[224,256]{1,0:T(8,128)(2,1)S(1)}, u32[]{:S(2)}, u32[]{:S(2)}) collective-permute-start(bf16[224,256]{1,0:T(8,128)(2,1)S(1)} %get-tuple-element.148.refs_0_), channel_id=1, source_target_pairs={{0,2},{2,0},{4,6},{6,4},{1,3},{3,1},{5,7},{7,5},{8,10},{10,8},{12,... | collective-permute-start | bytes 344072 | tf_op jit(solution)/shard_map/ppermute | solution.py:48
  41.2 5.5 %collective-permute-start.13 = (bf16[224,256]{1,0:T(8,128)(2,1)S(1)}, bf16[224,256]{1,0:T(8,128)(2,1)S(1)}, u32[]{:S(2)}, u32[]{:S(2)}) collective-permute-start(bf16[224,256]{1,0:T(8,128)(2,1)S(1)} %get-tuple-element.148.refs_0_), channel_id=1, source_target_pairs={{0,4},{2,6},{4,0},{6,2},{1,5},{3,7},{5,1},{7,3},{8,12},{10,14},{12... | collective-permute-start | bytes 344072 | tf_op jit(solution)/shard_map/ppermute | solution.py:48
  41.2 7.7 %collective-permute-start.12 = (bf16[224,256]{1,0:T(8,128)(2,1)S(1)}, bf16[224,256]{1,0:T(8,128)(2,1)S(1)}, u32[]{:S(2)}, u32[]{:S(2)}) collective-permute-start(bf16[224,256]{1,0:T(8,128)(2,1)S(1)} %get-tuple-element.148.refs_0_), channel_id=1, source_target_pairs={{0,6},{2,4},{4,2},{6,0},{1,7},{3,5},{5,3},{7,1},{8,14},{10,12},{12... | collective-permute-start | bytes 344072 | tf_op jit(solution)/shard_map/ppermute | solution.py:48
  45.8 3.1 %collective-permute-start.15 = (bf16[224,256]{1,0:T(8,128)(2,1)S(1)}, bf16[224,256]{1,0:T(8,128)(2,1)S(1)}, u32[]{:S(2)}, u32[]{:S(2)}) collective-permute-start(bf16[224,256]{1,0:T(8,128)(2,1)S(1)} %get-tuple-element.148.refs_0_), channel_id=1, source_target_pairs={{0,1},{1,0},{2,3},{3,2},{4,5},{5,4},{6,7},{7,6},{8,9},{9,8},{10,11... | collective-permute-start | bytes 344072 | tf_op jit(solution)/shard_map/ppermute | solution.py:30
  46.3 2.6 %collective-permute-start.16 = (bf16[224,256]{1,0:T(8,128)(2,1)S(1)}, bf16[224,256]{1,0:T(8,128)(2,1)S(1)}, u32[]{:S(2)}, u32[]{:S(2)}) collective-permute-start(bf16[224,256]{1,0:T(8,128)(2,1)S(1)} %collective-permute-done.14.refs_1_), channel_id=1, source_target_pairs={{0,1},{1,0},{2,3},{3,2},{4,5},{5,4},{6,7},{7,6},{8,9},{9,8},{10,11... | collective-permute-start | bytes 344072 | tf_op jit(solution)/shard_map/ppermute | solution.py:30
  46.8 2.2 %collective-permute-start.17 = (bf16[224,256]{1,0:T(8,128)(2,1)S(1)}, bf16[224,256]{1,0:T(8,128)(2,1)S(1)}, u32[]{:S(2)}, u32[]{:S(2)}) collective-permute-start(bf16[224,256]{1,0:T(8,128)(2,1)S(1)} %collective-permute-done.13.refs_2_), channel_id=1, source_target_pairs={{0,1},{1,0},{2,3},{3,2},{4,5},{5,4},{6,7},{7,6},{8,9},{9,8},{10,11... | collective-permute-start | bytes 344072 | tf_op jit(solution)/shard_map/ppermute | solution.py:30
  48.9 1.3 %collective-permute-start.18 = (bf16[224,256]{1,0:T(8,128)(2,1)S(1)}, bf16[224,256]{1,0:T(8,128)(2,1)S(1)}, u32[]{:S(2)}, u32[]{:S(2)}) collective-permute-start(bf16[224,256]{1,0:T(8,128)(2,1)S(1)} %collective-permute-done.12.refs_3_), channel_id=1, source_target_pairs={{0,1},{1,0},{2,3},{3,2},{4,5},{5,4},{6,7},{7,6},{8,9},{9,8},{10,11... | collective-permute-start | bytes 344072 | tf_op jit(solution)/shard_map/ppermute | solution.py:30

commit v21 on v19

--- a/solution.py
+++ b/solution.py
@@ -385,10 +385,6 @@
     return pack_gains(gains[0:1] + gains[1:2], gains[2:3] + gains[3:4])
 
 
-def copy_kernel(source, target):
-    target[...] = source[...]
-
-
 def sum_kernel(*refs):
     sums_out = refs[-1]
     sums = tree_sum([block[...].astype(F32) for block in refs[:-1]])
@@ -726,9 +722,6 @@
         other,
     )
     received = [in_square(block, members - 1 - i) for i, block in enumerate(blocks)]
-    outer = out_of_pair(outer, PX)
-    (inner,) = call(copy_kernel, [like(inner)], 10**9, in_pair(inner, PX))
-    *received, inner = lax.optimization_barrier((*received, inner))
     (sums,) = call(sum_kernel, [like(own)], 0, *received, own)
     edges_grad, local_grad = call(
         finish_kernel,
@@ -749,8 +742,8 @@
             shaped(2 * slots, width, BF16),
         ],
         10**10,
-        inner,
-        outer,
+        in_pair(inner, PX),
+        out_of_pair(outer, PX),
         middle,
         after=[sums],
     )

time: 51 us -> 51 us (level)
    ppermute x1, waiting for transfers between devices: 2.98 us -> 2.44 us  [joined(): other = lax.ppermute(sums, FAR, [(i, i ^ distance) for i in range(size)])]
    pallas_call x13 -> x12, Pallas kernels: 14 us -> 14 us  [call(): pl.pallas_call(body, out_shape=outs, in_specs=[pl.BlockSpec(memory_space=...]
  transfers between devices with their start and end apart: 20 -> 20, of which waited for: 11 -> 12; matrix products, arithmetic and copies ran while one was open for 1% -> 1% of each run, Pallas kernels for 12% -> 12%
where the time goes in v21:
time: 51 us; the launch traced here: 50.7 us
  starting transfers between devices  20.3 us (40%)
  waiting for transfers between devices  14.5 us (28%)
  Pallas kernels  14 us (27%)
  between operations  1.39 us (3%)
  other arithmetic  0.53 us (1%)
    pallas_call x12, Pallas kernels, call(): pl.pallas_call(body, out_shape=outs, in_specs=[pl.BlockSpec(memory_space=...  14 us
    ppermute x4, starting transfers between devices, out_of_pair(): lax.ppermute(array, axis, [(i, other_neighbour(i, size)) for i in range(s...  7.76 us
    ppermute x6, starting transfers between devices, in_square(): lax.ppermute(array, SQUARE, [(i, i ^ offset) for i in range(square_member...  7.12 us
    ppermute x6, waiting for transfers between devices, in_square(): lax.ppermute(array, SQUARE, [(i, i ^ offset) for i in range(square_member...  6.4 us
    ppermute x9, starting transfers between devices, in_pair(): lax.ppermute(array, axis, [(i, i ^ 1) for i in range(lax.axis_size(axis))])  4.38 us
    ppermute x4, waiting for transfers between devices, out_of_pair(): lax.ppermute(array, axis, [(i, other_neighbour(i, size)) for i in range(s...  2.89 us
    ppermute x9, waiting for transfers between devices, in_pair(): lax.ppermute(array, axis, [(i, i ^ 1) for i in range(lax.axis_size(axis))])  2.78 us
    ppermute x1, waiting for transfers between devices, joined(): other = lax.ppermute(sums, FAR, [(i, i ^ distance) for i in range(size)])  2.44 us
  transfers between devices with their start and end apart: 20, of which 12 were waited for; matrix products, arithmetic and copies ran while one was open for 1% of the time, Pallas kernels for 12%

profile of v21, /device:TPU:0, one launch (start us, length us, event | category | flops | bytes accessed | tf_op | source)
XLA Modules:
  0.0 50.7 jit_solution(3512031321602444100)
XLA Ops:
  0.6 1.2 %shard_map.197 = (bf16[96,256]{1,0:T(8,128)(2,1)S(1)}, bf16[96,256]{1,0:T(8,128)(2,1)S(1)}, bf16[64,256]{1,0:T(8,128)(2,1)S(1)}, bf16[384,256]{1,0:T(8,128)(2,1)S(1)}, s32[8,32]{1,0:T(8,128)S(1)}) custom-call(bf16[384,256]{1,0:T(8,128)(2,1)} %nodes_hbm.1, s32[8,32]{1,0:T(8,128)} %list_hbm.1), custom_call_target="tpu_custom_call" | custom-call | flops 50331648 | bytes 526336 | tf_op jit(solution)/shard_map/pallas_call | solution.py:503
  1.8 3.1 %collective-permute-start = (bf16[96,256]{1,0:T(8,128)(2,1)S(1)}, bf16[96,256]{1,0:T(8,128)(2,1)S(1)}, u32[]{:S(2)}, u32[]{:S(2)}) collective-permute-start(bf16[96,256]{1,0:T(8,128)(2,1)S(1)} %get-tuple-element.89), channel_id=1, source_target_pairs={{0,4},{4,0},{8,12},{12,8},{1,5},{5,1},{9,13},{13,9},{2,6},{6,2},{1... | collective-permute-start | bytes 147464 | tf_op jit(solution)/shard_map/ppermute | solution.py:30
  4.9 2.5 %collective-permute-start.1 = (bf16[96,256]{1,0:T(8,128)(2,1)S(1)}, bf16[96,256]{1,0:T(8,128)(2,1)S(1)}, u32[]{:S(2)}, u32[]{:S(2)}) collective-permute-start(bf16[96,256]{1,0:T(8,128)(2,1)S(1)} %get-tuple-element.90), channel_id=1, source_target_pairs={{0,12},{4,8},{8,4},{12,0},{1,13},{5,9},{9,5},{13,1},{2,14},{6,10},... | collective-permute-start | bytes 147464 | tf_op jit(solution)/shard_map/ppermute | solution.py:35
  8.0 1.7 %shard_map.198 = (bf16[1152,768]{1,0:T(8,128)(2,1)S(1)}, bf16[1152,256]{1,0:T(8,128)(2,1)S(1)}, s32[9,128]{1,0:T(8,128)S(1)}, s32[9,128]{1,0:T(8,128)S(1)}, bf16...) custom-call(s32[9,128]{1,0:T(8,128)} %refs_0_.1, ...), custom_call_target="tpu_custom_call" | custom-call | bytes 6967296 | tf_op jit(solution)/shard_map/pallas_call | solution.py:503
  9.8 0.0 collective-permute-done.inner
  9.8 1.0 %collective-permute-done.1.outer = bf16[96,256]{1,0:T(8,128)(2,1)S(1)} collective-permute-done((bf16[96,256]{1,0:T(8,128)(2,1)S(1)}, bf16[96,256]{1,0:T(8,128)(2,1)S(1)}, u32[]{:S(2)}, u32[]{:S(2)}) %collective-permute-start.1) | collective-permute-done | bytes 49184 | tf_op jit(solution)/shard_map/ppermute | solution.py:35
  10.8 0.1 collective-permute-start.2
  10.9 1.6 %collective-permute-start.3 = (bf16[96,256]{1,0:T(8,128)(2,1)S(1)}, bf16[96,256]{1,0:T(8,128)(2,1)S(1)}, u32[]{:S(2)}, u32[]{:S(2)}) collective-permute-start(bf16[96,256]{1,0:T(8,128)(2,1)S(1)} %get-tuple-element.103), channel_id=1, source_target_pairs={{0,3},{1,2},{2,1},{3,0},{4,7},{5,6},{6,5},{7,4},{8,11},{9,10},{10,... | collective-permute-start | bytes 147464 | tf_op jit(solution)/shard_map/ppermute | solution.py:35
  12.5 1.8 %shard_map.199 = (f32[1152,256]{1,0:T(8,128)S(1)}, bf16[640,1152]{1,0:T(8,128)(2,1)S(1)}, bf16[384,1152]{1,0:T(8,128)(2,1)S(1)}) custom-call(bf16[384,256]{1,0:T(8,128)(2,1)S(1)} %get-tuple-element.83.nodes, bf16[1152,256]{1,0:T(8,128)(2,1)S(1)} %get-tuple-element.85.edges, s32[9,128]{1,0:T(8,128)S(1)} %get-tuple-element.87.senders, ...), custom_call_target="tpu_custom_call" | custom-call | flops 704643072 | bytes 6497280 | tf_op jit(solution)/shard_map/pallas_call | solution.py:503
  14.4 0.0 collective-permute-done.2.along_core
  14.4 0.1 collective-permute-done.3.along_chip
  14.5 5.6 %shard_map.201 = (bf16[1152,256]{1,0:T(8,128)(2,1)S(1)}, bf16[384,256]{1,0:T(8,128)(2,1)S(1)}, bf16[384,256]{1,0:T(8,128)(2,1)S(1)}, f32[384,256]{1,0:T(8,128)S(...) custom-call(s32[1]{0:T(128)S(6)} %copy.22.count_ref, ...), custom_call_target="tpu_custom_call" | custom-call | flops 2583691264 | bytes 11412484 | tf_op jit(solution)/shard_map/pallas_call | solution.py:503
  20.1 0.5 %collective-permute-start.4 = (bf16[904,256]{1,0:T(8,128)(2,1)S(1)}, bf16[904,256]{1,0:T(8,128)(2,1)S(1)}, u32[]{:S(2)}, u32[]{:S(2)}) collective-permute-start(bf16[904,256]{1,0:T(8,128)(2,1)S(1)} %get-tuple-element.111), channel_id=1, source_target_pairs={{0,1},{1,0},{2,3},{3,2},{4,5},{5,4},{6,7},{7,6},{8,9},{9,8},{10,11... | collective-permute-start | bytes 1388552 | tf_op jit(solution)/shard_map/ppermute | solution.py:30
  20.6 1.4 %collective-permute-done.4.other = bf16[904,256]{1,0:T(8,128)(2,1)S(1)} collective-permute-done((bf16[904,256]{1,0:T(8,128)(2,1)S(1)}, bf16[904,256]{1,0:T(8,128)(2,1)S(1)}, u32[]{:S(2)}, u32[]{:S(2)}) %collective-permute-start.4) | collective-permute-done | bytes 462880 | tf_op jit(solution)/shard_map/ppermute | solution.py:30
  22.0 0.1 shard_map.202
  22.2 0.7 %collective-permute-start.5 = (bf16[232,256]{1,0:T(8,128)(2,1)S(1)}, bf16[232,256]{1,0:T(8,128)(2,1)S(1)}, u32[]{:S(2)}, u32[]{:S(2)}) collective-permute-start(bf16[232,256]{1,0:T(8,128)(2,1)S(1)} %get-tuple-element.112), channel_id=1, source_target_pairs={{0,6},{2,4},{4,2},{6,0},{1,7},{3,5},{5,3},{7,1},{8,14},{10,12},{12... | collective-permute-start | bytes 356360 | tf_op jit(solution)/shard_map/ppermute | solution.py:48
  22.9 2.3 %collective-permute-start.6 = (bf16[232,256]{1,0:T(8,128)(2,1)S(1)}, bf16[232,256]{1,0:T(8,128)(2,1)S(1)}, u32[]{:S(2)}, u32[]{:S(2)}) collective-permute-start(bf16[232,256]{1,0:T(8,128)(2,1)S(1)} %get-tuple-element.113), channel_id=1, source_target_pairs={{0,4},{2,6},{4,0},{6,2},{1,5},{3,7},{5,1},{7,3},{8,12},{10,14},{12... | collective-permute-start | bytes 356360 | tf_op jit(solution)/shard_map/ppermute | solution.py:48
  25.2 0.5 %collective-permute-start.7 = (bf16[232,256]{1,0:T(8,128)(2,1)S(1)}, bf16[232,256]{1,0:T(8,128)(2,1)S(1)}, u32[]{:S(2)}, u32[]{:S(2)}) collective-permute-start(bf16[232,256]{1,0:T(8,128)(2,1)S(1)} %get-tuple-element.114), channel_id=1, source_target_pairs={{0,2},{2,0},{4,6},{6,4},{1,3},{3,1},{5,7},{7,5},{8,10},{10,8},{12,... | collective-permute-start | bytes 356360 | tf_op jit(solution)/shard_map/ppermute | solution.py:48
  25.7 0.1 collective-permute-start.9
  25.9 2.5 %collective-permute-start.10 = (bf16[96,256]{1,0:T(8,128)(2,1)S(1)}, bf16[96,256]{1,0:T(8,128)(2,1)S(1)}, u32[]{:S(2)}, u32[]{:S(2)}) collective-permute-start(bf16[96,256]{1,0:T(8,128)(2,1)S(1)} %get-tuple-element.117), channel_id=1, source_target_pairs={{0,12},{4,8},{8,4},{12,0},{1,13},{5,9},{9,5},{13,1},{2,14},{6,10},... | collective-permute-start | bytes 147464 | tf_op jit(solution)/shard_map/ppermute | solution.py:35
  28.3 0.9 %collective-permute-done.5.refs_0_ = bf16[232,256]{1,0:T(8,128)(2,1)S(1)} collective-permute-done((bf16[232,256]{1,0:T(8,128)(2,1)S(1)}, bf16[232,256]{1,0:T(8,128)(2,1)S(1)}, u32[]{:S(2)}, u32[]{:S(2)}) %collective-permute-start.5) | collective-permute-done | bytes 118816 | tf_op jit(solution)/shard_map/ppermute | solution.py:48
  29.2 2.6 %collective-permute-done.6.refs_1_ = bf16[232,256]{1,0:T(8,128)(2,1)S(1)} collective-permute-done((bf16[232,256]{1,0:T(8,128)(2,1)S(1)}, bf16[232,256]{1,0:T(8,128)(2,1)S(1)}, u32[]{:S(2)}, u32[]{:S(2)}) %collective-permute-start.6) | collective-permute-done | bytes 118816 | tf_op jit(solution)/shard_map/ppermute | solution.py:48
  31.8 0.0 collective-permute-done.7.refs_2_
  31.8 0.1 shard_map.203.refs_3_.own
  31.8 1.0 %collective-permute-start.8 = (bf16[232,256]{1,0:T(8,128)(2,1)S(1)}, bf16[232,256]{1,0:T(8,128)(2,1)S(1)}, u32[]{:S(2)}, u32[]{:S(2)}) collective-permute-start(bf16[232,256]{1,0:T(8,128)(2,1)S(1)} %shard_map.203.refs_3_.own), channel_id=1, source_target_pairs={{0,8},{8,0},{1,9},{9,1},{2,10},{10,2},{3,11},{11,3},{4,12},{12,4},... | collective-permute-start | bytes 356360 | tf_op jit(solution)/shard_map/ppermute | solution.py:544
  32.8 0.0 collective-permute-done.9.refs_0_
  32.8 0.7 %collective-permute-done.10.refs_1_ = bf16[96,256]{1,0:T(8,128)(2,1)S(1)} collective-permute-done((bf16[96,256]{1,0:T(8,128)(2,1)S(1)}, bf16[96,256]{1,0:T(8,128)(2,1)S(1)}, u32[]{:S(2)}, u32[]{:S(2)}) %collective-permute-start.10) | collective-permute-done | bytes 49184 | tf_op jit(solution)/shard_map/ppermute | solution.py:35
  33.6 0.1 collective-permute-start.11
  33.7 1.2 %collective-permute-start.12 = (bf16[96,256]{1,0:T(8,128)(2,1)S(1)}, bf16[96,256]{1,0:T(8,128)(2,1)S(1)}, u32[]{:S(2)}, u32[]{:S(2)}) collective-permute-start(bf16[96,256]{1,0:T(8,128)(2,1)S(1)} %get-tuple-element.120), channel_id=1, source_target_pairs={{0,3},{1,2},{2,1},{3,0},{4,7},{5,6},{6,5},{7,4},{8,11},{9,10},{10,... | collective-permute-start | bytes 147464 | tf_op jit(solution)/shard_map/ppermute | solution.py:35
  34.9 1.3 %shard_map.206 = (bf16[1152,256]{1,0:T(8,128)(2,1)}, f32[384,256]{1,0:T(8,128)S(1)}) custom-call(bf16[1152,256]{1,0:T(8,128)(2,1)S(1)} %get-tuple-element.86.edge_grads, bf16[1152,256]{1,0:T(8,128)(2,1)S(1)} %get-tuple-element.124.pre_grad, bf16[384,256]{1,0:T(8,128)(2,1)S(1)} %get-tuple-element.125.sender_sum, ...), custom_call_target="tpu_custom_call" | custom-call | flops 251658240 | bytes 3342336 | tf_op jit(solution)/shard_map/pallas_call | solution.py:503
  36.2 0.0 collective-permute-done.11.along_core
  36.2 1.0 %collective-permute-done.12.along_chip = bf16[96,256]{1,0:T(8,128)(2,1)S(1)} collective-permute-done((bf16[96,256]{1,0:T(8,128)(2,1)S(1)}, bf16[96,256]{1,0:T(8,128)(2,1)S(1)}, u32[]{:S(2)}, u32[]{:S(2)}) %collective-permute-start.12) | collective-permute-done | bytes 49184 | tf_op jit(solution)/shard_map/ppermute | solution.py:35
  37.2 2.4 %collective-permute-done.8.other = bf16[232,256]{1,0:T(8,128)(2,1)S(1)} collective-permute-done((bf16[232,256]{1,0:T(8,128)(2,1)S(1)}, bf16[232,256]{1,0:T(8,128)(2,1)S(1)}, u32[]{:S(2)}, u32[]{:S(2)}) %collective-permute-start.8) | collective-permute-done | bytes 118816 | tf_op jit(solution)/shard_map/ppermute | solution.py:544
  39.7 1.6 %collective-permute-start.15 = (bf16[224,256]{1,0:T(8,128)(2,1)S(1)}, bf16[224,256]{1,0:T(8,128)(2,1)S(1)}, u32[]{:S(2)}, u32[]{:S(2)}) collective-permute-start(bf16[224,256]{1,0:T(8,128)(2,1)S(1)} %get-tuple-element.148.refs_0_), channel_id=1, source_target_pairs={{0,2},{2,0},{4,6},{6,4},{1,3},{3,1},{5,7},{7,5},{8,10},{10,8},{12,... | collective-permute-start | bytes 344072 | tf_op jit(solution)/shard_map/ppermute | solution.py:48
  41.4 0.0 collective-permute-start.14
  41.4 1.9 %collective-permute-start.13 = (bf16[224,256]{1,0:T(8,128)(2,1)S(1)}, bf16[224,256]{1,0:T(8,128)(2,1)S(1)}, u32[]{:S(2)}, u32[]{:S(2)}) collective-permute-start(bf16[224,256]{1,0:T(8,128)(2,1)S(1)} %get-tuple-element.148.refs_0_), channel_id=1, source_target_pairs={{0,6},{2,4},{4,2},{6,0},{1,7},{3,5},{5,3},{7,1},{8,14},{10,12},{12... | collective-permute-start | bytes 344072 | tf_op jit(solution)/shard_map/ppermute | solution.py:48
  43.3 1.1 %shard_map.207 = bf16[384,256]{1,0:T(8,128)(2,1)} custom-call(s32[8,32]{1,0:T(8,128)S(1)} %get-tuple-element.123.send_list, f32[384,256]{1,0:T(8,128)S(1)} %get-tuple-element.128.local_grad, bf16[64,256]{1,0:T(8,128)(2,1)S(1)} %get-tuple-element.129.center, bf16[96,256]{1,0:T(8,128)(2,1)S(1)} %collective-permute-done.11.along_core, ...), custom_call_target="tpu_custom_call" | custom-call | flops 50331648 | bytes 721920 | tf_op jit(solution)/shard_map/pallas_call | solution.py:503
  44.4 0.5 %convert_reduce_fusion = (bf16[256]{0:T(256)(128)(2,1)}, bf16[256]{0:T(256)(128)(2,1)}) fusion(f32[8,256]{1,0:T(8,128)S(1)} %get-tuple-element.133), kind=kLoop, calls=%fused_computation | loop fusion | flops 1024 | bytes 5120 | tf_op jit(solution)/shard_map/convert_element_type | solution.py:755
  44.9 0.0 collective-permute-start.16
  44.9 0.0 collective-permute-done.15.refs_1_
  44.9 0.5 %collective-permute-start.17 = (bf16[224,256]{1,0:T(8,128)(2,1)S(1)}, bf16[224,256]{1,0:T(8,128)(2,1)S(1)}, u32[]{:S(2)}, u32[]{:S(2)}) collective-permute-start(bf16[224,256]{1,0:T(8,128)(2,1)S(1)} %collective-permute-done.15.refs_1_), channel_id=1, source_target_pairs={{0,1},{1,0},{2,3},{3,2},{4,5},{5,4},{6,7},{7,6},{8,9},{9,8},{10,11... | collective-permute-start | bytes 344072 | tf_op jit(solution)/shard_map/ppermute | solution.py:30
  45.4 1.9 %collective-permute-done.14.refs_2_ = bf16[224,256]{1,0:T(8,128)(2,1)S(1)} collective-permute-done((bf16[224,256]{1,0:T(8,128)(2,1)S(1)}, bf16[224,256]{1,0:T(8,128)(2,1)S(1)}, u32[]{:S(2)}, u32[]{:S(2)}) %collective-permute-start.14) | collective-permute-done | bytes 114720 | tf_op jit(solution)/shard_map/ppermute | solution.py:48
  47.4 0.0 collective-permute-start.18
  47.4 1.0 %collective-permute-done.13.refs_3_ = bf16[224,256]{1,0:T(8,128)(2,1)S(1)} collective-permute-done((bf16[224,256]{1,0:T(8,128)(2,1)S(1)}, bf16[224,256]{1,0:T(8,128)(2,1)S(1)}, u32[]{:S(2)}, u32[]{:S(2)}) %collective-permute-start.13) | collective-permute-done | bytes 114720 | tf_op jit(solution)/shard_map/ppermute | solution.py:48
  48.4 0.0 collective-permute-start.19
  48.4 0.0 collective-permute-done.16.refs_4_
  48.4 0.0 collective-permute-done.17.refs_5_
  48.4 0.3 collective-permute-done.18.refs_6_
  48.7 1.0 %collective-permute-done.19.refs_7_ = bf16[224,256]{1,0:T(8,128)(2,1)S(1)} collective-permute-done((bf16[224,256]{1,0:T(8,128)(2,1)S(1)}, bf16[224,256]{1,0:T(8,128)(2,1)S(1)}, u32[]{:S(2)}, u32[]{:S(2)}) %collective-permute-start.19) | collective-permute-done | bytes 114720 | tf_op jit(solution)/shard_map/ppermute | solution.py:30
  49.7 1.0 %shard_map.208 = (bf16[768,256]{1,0:T(8,128)(2,1)}, bf16[256,256]{1,0:T(8,128)(2,1)}, bf16[512,256]{1,0:T(8,128)(2,1)}, bf16[256,256]{1,0:T(8,128)(2,1)}) custom-call(bf16[224,256]{1,0:T(8,128)(2,1)S(1)} %get-tuple-element.148.refs_0_, bf16[224,256]{1,0:T(8,128)(2,1)S(1)} %collective-permute-done.15.refs_1_, ...), custom_call_target="tpu_custom_call" | custom-call | bytes 1835008 | tf_op jit(solution)/shard_map/pallas_call | solution.py:503
  (3 shorter events, 0.1 us)
Async XLA Ops:
  1.8 8.0 %collective-permute-start = (bf16[96,256]{1,0:T(8,128)(2,1)S(1)}, bf16[96,256]{1,0:T(8,128)(2,1)S(1)}, u32[]{:S(2)}, u32[]{:S(2)}) collective-permute-start(bf16[96,256]{1,0:T(8,128)(2,1)S(1)} %get-tuple-element.89), channel_id=1, source_target_pairs={{0,4},{4,0},{8,12},{12,8},{1,5},{5,1},{9,13},{13,9},{2,6},{6,2},{1... | collective-permute-start | bytes 147464 | tf_op jit(solution)/shard_map/ppermute | solution.py:30
  4.9 5.9 %collective-permute-start.1 = (bf16[96,256]{1,0:T(8,128)(2,1)S(1)}, bf16[96,256]{1,0:T(8,128)(2,1)S(1)}, u32[]{:S(2)}, u32[]{:S(2)}) collective-permute-start(bf16[96,256]{1,0:T(8,128)(2,1)S(1)} %get-tuple-element.90), channel_id=1, source_target_pairs={{0,12},{4,8},{8,4},{12,0},{1,13},{5,9},{9,5},{13,1},{2,14},{6,10},... | collective-permute-start | bytes 147464 | tf_op jit(solution)/shard_map/ppermute | solution.py:35
  10.8 3.5 %collective-permute-start.2 = (bf16[96,256]{1,0:T(8,128)(2,1)S(1)}, bf16[96,256]{1,0:T(8,128)(2,1)S(1)}, u32[]{:S(2)}, u32[]{:S(2)}) collective-permute-start(bf16[96,256]{1,0:T(8,128)(2,1)S(1)} %get-tuple-element.102), channel_id=1, source_target_pairs={{0,1},{1,0},{2,3},{3,2},{4,5},{5,4},{6,7},{7,6},{8,9},{9,8},{10,11... | collective-permute-start | bytes 147464 | tf_op jit(solution)/shard_map/ppermute | solution.py:30
  10.9 3.6 %collective-permute-start.3 = (bf16[96,256]{1,0:T(8,128)(2,1)S(1)}, bf16[96,256]{1,0:T(8,128)(2,1)S(1)}, u32[]{:S(2)}, u32[]{:S(2)}) collective-permute-start(bf16[96,256]{1,0:T(8,128)(2,1)S(1)} %get-tuple-element.103), channel_id=1, source_target_pairs={{0,3},{1,2},{2,1},{3,0},{4,7},{5,6},{6,5},{7,4},{8,11},{9,10},{10,... | collective-permute-start | bytes 147464 | tf_op jit(solution)/shard_map/ppermute | solution.py:35
  20.1 2.0 %collective-permute-start.4 = (bf16[904,256]{1,0:T(8,128)(2,1)S(1)}, bf16[904,256]{1,0:T(8,128)(2,1)S(1)}, u32[]{:S(2)}, u32[]{:S(2)}) collective-permute-start(bf16[904,256]{1,0:T(8,128)(2,1)S(1)} %get-tuple-element.111), channel_id=1, source_target_pairs={{0,1},{1,0},{2,3},{3,2},{4,5},{5,4},{6,7},{7,6},{8,9},{9,8},{10,11... | collective-permute-start | bytes 1388552 | tf_op jit(solution)/shard_map/ppermute | solution.py:30
  22.2 7.0 %collective-permute-start.5 = (bf16[232,256]{1,0:T(8,128)(2,1)S(1)}, bf16[232,256]{1,0:T(8,128)(2,1)S(1)}, u32[]{:S(2)}, u32[]{:S(2)}) collective-permute-start(bf16[232,256]{1,0:T(8,128)(2,1)S(1)} %get-tuple-element.112), channel_id=1, source_target_pairs={{0,6},{2,4},{4,2},{6,0},{1,7},{3,5},{5,3},{7,1},{8,14},{10,12},{12... | collective-permute-start | bytes 356360 | tf_op jit(solution)/shard_map/ppermute | solution.py:48
  22.9 8.8 %collective-permute-start.6 = (bf16[232,256]{1,0:T(8,128)(2,1)S(1)}, bf16[232,256]{1,0:T(8,128)(2,1)S(1)}, u32[]{:S(2)}, u32[]{:S(2)}) collective-permute-start(bf16[232,256]{1,0:T(8,128)(2,1)S(1)} %get-tuple-element.113), channel_id=1, source_target_pairs={{0,4},{2,6},{4,0},{6,2},{1,5},{3,7},{5,1},{7,3},{8,12},{10,14},{12... | collective-permute-start | bytes 356360 | tf_op jit(solution)/shard_map/ppermute | solution.py:48
  25.2 6.5 %collective-permute-start.7 = (bf16[232,256]{1,0:T(8,128)(2,1)S(1)}, bf16[232,256]{1,0:T(8,128)(2,1)S(1)}, u32[]{:S(2)}, u32[]{:S(2)}) collective-permute-start(bf16[232,256]{1,0:T(8,128)(2,1)S(1)} %get-tuple-element.114), channel_id=1, source_target_pairs={{0,2},{2,0},{4,6},{6,4},{1,3},{3,1},{5,7},{7,5},{8,10},{10,8},{12,... | collective-permute-start | bytes 356360 | tf_op jit(solution)/shard_map/ppermute | solution.py:48
  25.7 7.1 %collective-permute-start.9 = (bf16[96,256]{1,0:T(8,128)(2,1)S(1)}, bf16[96,256]{1,0:T(8,128)(2,1)S(1)}, u32[]{:S(2)}, u32[]{:S(2)}) collective-permute-start(bf16[96,256]{1,0:T(8,128)(2,1)S(1)} %get-tuple-element.116), channel_id=1, source_target_pairs={{0,4},{4,0},{8,12},{12,8},{1,5},{5,1},{9,13},{13,9},{2,6},{6,2},{1... | collective-permute-start | bytes 147464 | tf_op jit(solution)/shard_map/ppermute | solution.py:30
  25.9 7.7 %collective-permute-start.10 = (bf16[96,256]{1,0:T(8,128)(2,1)S(1)}, bf16[96,256]{1,0:T(8,128)(2,1)S(1)}, u32[]{:S(2)}, u32[]{:S(2)}) collective-permute-start(bf16[96,256]{1,0:T(8,128)(2,1)S(1)} %get-tuple-element.117), channel_id=1, source_target_pairs={{0,12},{4,8},{8,4},{12,0},{1,13},{5,9},{9,5},{13,1},{2,14},{6,10},... | collective-permute-start | bytes 147464 | tf_op jit(solution)/shard_map/ppermute | solution.py:35
  31.8 7.9 %collective-permute-start.8 = (bf16[232,256]{1,0:T(8,128)(2,1)S(1)}, bf16[232,256]{1,0:T(8,128)(2,1)S(1)}, u32[]{:S(2)}, u32[]{:S(2)}) collective-permute-start(bf16[232,256]{1,0:T(8,128)(2,1)S(1)} %shard_map.203.refs_3_.own), channel_id=1, source_target_pairs={{0,8},{8,0},{1,9},{9,1},{2,10},{10,2},{3,11},{11,3},{4,12},{12,4},... | collective-permute-start | bytes 356360 | tf_op jit(solution)/shard_map/ppermute | solution.py:544
  33.6 2.6 %collective-permute-start.11 = (bf16[96,256]{1,0:T(8,128)(2,1)S(1)}, bf16[96,256]{1,0:T(8,128)(2,1)S(1)}, u32[]{:S(2)}, u32[]{:S(2)}) collective-permute-start(bf16[96,256]{1,0:T(8,128)(2,1)S(1)} %get-tuple-element.119), channel_id=1, source_target_pairs={{0,1},{1,0},{2,3},{3,2},{4,5},{5,4},{6,7},{7,6},{8,9},{9,8},{10,11... | collective-permute-start | bytes 147464 | tf_op jit(solution)/shard_map/ppermute | solution.py:30
  33.7 3.6 %collective-permute-start.12 = (bf16[96,256]{1,0:T(8,128)(2,1)S(1)}, bf16[96,256]{1,0:T(8,128)(2,1)S(1)}, u32[]{:S(2)}, u32[]{:S(2)}) collective-permute-start(bf16[96,256]{1,0:T(8,128)(2,1)S(1)} %get-tuple-element.120), channel_id=1, source_target_pairs={{0,3},{1,2},{2,1},{3,0},{4,7},{5,6},{6,5},{7,4},{8,11},{9,10},{10,... | collective-permute-start | bytes 147464 | tf_op jit(solution)/shard_map/ppermute | solution.py:35
  39.7 5.2 %collective-permute-start.15 = (bf16[224,256]{1,0:T(8,128)(2,1)S(1)}, bf16[224,256]{1,0:T(8,128)(2,1)S(1)}, u32[]{:S(2)}, u32[]{:S(2)}) collective-permute-start(bf16[224,256]{1,0:T(8,128)(2,1)S(1)} %get-tuple-element.148.refs_0_), channel_id=1, source_target_pairs={{0,2},{2,0},{4,6},{6,4},{1,3},{3,1},{5,7},{7,5},{8,10},{10,8},{12,... | collective-permute-start | bytes 344072 | tf_op jit(solution)/shard_map/ppermute | solution.py:48
  41.4 6.0 %collective-permute-start.14 = (bf16[224,256]{1,0:T(8,128)(2,1)S(1)}, bf16[224,256]{1,0:T(8,128)(2,1)S(1)}, u32[]{:S(2)}, u32[]{:S(2)}) collective-permute-start(bf16[224,256]{1,0:T(8,128)(2,1)S(1)} %get-tuple-element.148.refs_0_), channel_id=1, source_target_pairs={{0,4},{2,6},{4,0},{6,2},{1,5},{3,7},{5,1},{7,3},{8,12},{10,14},{12... | collective-permute-start | bytes 344072 | tf_op jit(solution)/shard_map/ppermute | solution.py:48
  41.4 7.0 %collective-permute-start.13 = (bf16[224,256]{1,0:T(8,128)(2,1)S(1)}, bf16[224,256]{1,0:T(8,128)(2,1)S(1)}, u32[]{:S(2)}, u32[]{:S(2)}) collective-permute-start(bf16[224,256]{1,0:T(8,128)(2,1)S(1)} %get-tuple-element.148.refs_0_), channel_id=1, source_target_pairs={{0,6},{2,4},{4,2},{6,0},{1,7},{3,5},{5,3},{7,1},{8,14},{10,12},{12... | collective-permute-start | bytes 344072 | tf_op jit(solution)/shard_map/ppermute | solution.py:48
  44.9 3.5 %collective-permute-start.16 = (bf16[224,256]{1,0:T(8,128)(2,1)S(1)}, bf16[224,256]{1,0:T(8,128)(2,1)S(1)}, u32[]{:S(2)}, u32[]{:S(2)}) collective-permute-start(bf16[224,256]{1,0:T(8,128)(2,1)S(1)} %get-tuple-element.148.refs_0_), channel_id=1, source_target_pairs={{0,1},{1,0},{2,3},{3,2},{4,5},{5,4},{6,7},{7,6},{8,9},{9,8},{10,11... | collective-permute-start | bytes 344072 | tf_op jit(solution)/shard_map/ppermute | solution.py:30
  44.9 3.5 %collective-permute-start.17 = (bf16[224,256]{1,0:T(8,128)(2,1)S(1)}, bf16[224,256]{1,0:T(8,128)(2,1)S(1)}, u32[]{:S(2)}, u32[]{:S(2)}) collective-permute-start(bf16[224,256]{1,0:T(8,128)(2,1)S(1)} %collective-permute-done.15.refs_1_), channel_id=1, source_target_pairs={{0,1},{1,0},{2,3},{3,2},{4,5},{5,4},{6,7},{7,6},{8,9},{9,8},{10,11... | collective-permute-start | bytes 344072 | tf_op jit(solution)/shard_map/ppermute | solution.py:30
  47.4 1.3 %collective-permute-start.18 = (bf16[224,256]{1,0:T(8,128)(2,1)S(1)}, bf16[224,256]{1,0:T(8,128)(2,1)S(1)}, u32[]{:S(2)}, u32[]{:S(2)}) collective-permute-start(bf16[224,256]{1,0:T(8,128)(2,1)S(1)} %collective-permute-done.14.refs_2_), channel_id=1, source_target_pairs={{0,1},{1,0},{2,3},{3,2},{4,5},{5,4},{6,7},{7,6},{8,9},{9,8},{10,11... | collective-permute-start | bytes 344072 | tf_op jit(solution)/shard_map/ppermute | solution.py:30
  48.4 1.3 %collective-permute-start.19 = (bf16[224,256]{1,0:T(8,128)(2,1)S(1)}, bf16[224,256]{1,0:T(8,128)(2,1)S(1)}, u32[]{:S(2)}, u32[]{:S(2)}) collective-permute-start(bf16[224,256]{1,0:T(8,128)(2,1)S(1)} %collective-permute-done.13.refs_3_), channel_id=1, source_target_pairs={{0,1},{1,0},{2,3},{3,2},{4,5},{5,4},{6,7},{7,6},{8,9},{9,8},{10,11... | collective-permute-start | bytes 344072 | tf_op jit(solution)/shard_map/ppermute | solution.py:30
